TPU v7x, 32 devices: a whole 2x2x4 slice. The times are simulated.
32 devices in a mesh: dp: 2 (over x), tile: 16 (over z, y, core).
Axes of the slice: x: 2, y: 2, z: 4, core: 2. Of those that a mesh axis runs over, the one named last changes fastest.
Arguments:
- features: bfloat16 [8, 2, 2048, 1024], P('dp', None, 'tile'), may hold values from -6 to 6
- proj_weight: bfloat16 [2, 1024, 256], replicated, may hold values from -0.1875 to 0.1875
- conv_weight: bfloat16 [2, 3, 3, 256, 256], replicated, may hold values from -0.125 to 0.125
- saved: bfloat16 [8, 2, 128, 16, 256], P('dp', None, 'tile'), may hold values from -6 to 6
- cotangent: bfloat16 [8, 256, 32, 256], P('dp', 'tile'), may hold values from -6 to 6
Outputs:
- feature_grad: bfloat16 [8, 2, 2048, 1024], P('dp', None, 'tile')
- head_grad: float32 [6656, 256], P(('dp', 'tile'))
All inputs are finite; a program needn't handle non-finite values.
Results may differ from a plain program's by a relative error of at most 0.0057.
Values may be sent and summed in bfloat16 or wider, within the bound.
No kernel may reach another device: no remote copies, remote signals or barrier semaphores. Data moves between devices by JAX's collectives and lax.ppermute only.
A program may use at most 128 MiB of HBM per device.

v0:
```python
import math

import jax
import jax.numpy as jnp
from jax import lax
from jax.sharding import PartitionSpec as P

COL_BITS = 3
TILE_COLS = 8


def from_partner(block, axis, apart):
    count = lax.axis_size(axis)
    route = []
    for low in range(count):
        high = low | 1 << apart
        if high != low and high < count:
            route += [(low, high), (high, low)]
    return lax.ppermute(block, axis, route)


def from_behind(block, axis, distance):
    devices = range(lax.axis_size(axis))
    route = [(i - distance, i) for i in devices if i - distance in devices]
    return lax.ppermute(block, axis, route)


def pool(values_in, along_dim, lo_edge, hi_edge):
    cell_count = (values_in.shape[along_dim] - 2) // 2
    even_part = lax.slice_in_dim(values_in, 1, 2 * cell_count + 1, 2, along_dim)
    odd_part = lax.slice_in_dim(values_in, 2, 2 * cell_count + 2, 2, along_dim)
    before = lax.slice_in_dim(values_in, 0, 2 * cell_count, 2, along_dim)
    after = lax.slice_in_dim(values_in, 3, 2 * cell_count + 2, 2, along_dim)
    target_shape = [1] * values_in.ndim
    target_shape[along_dim] = cell_count
    iota_pos = lax.broadcasted_iota(jnp.int32, tuple(target_shape), along_dim)
    at_first = jnp.logical_and(iota_pos == 0, lo_edge)
    at_last = jnp.logical_and(iota_pos == cell_count - 1, hi_edge)
    result = 0.75 * (even_part + odd_part) + 0.25 * (before + after)
    result = result + 0.25 * jnp.where(at_first, even_part, jnp.zeros_like(even_part))
    result = result + 0.25 * jnp.where(at_last, odd_part, jnp.zeros_like(odd_part))
    return result


def column_of(code):
    column = code
    for step_bit in range(1, COL_BITS):
        column = jnp.bitwise_xor(column, jnp.right_shift(code, step_bit))
    return column


def trade(outgoing, bit_index):
    return from_partner(outgoing, "tile", bit_index)


def widen(field_in, col_pos, gray_pos):
    width = field_in.shape[2]
    left_edge = field_in[:, :, :1]
    right_edge = field_in[:, :, width - 1 :]
    left_rim = jnp.zeros_like(left_edge)
    right_rim = jnp.zeros_like(right_edge)
    for bit_index in range(COL_BITS):
        partner_col = column_of(jnp.bitwise_xor(gray_pos, 1 << bit_index))
        to_left = partner_col == col_pos - 1
        to_right = partner_col == col_pos + 1
        outgoing = jnp.where(
            to_left, left_edge, jnp.where(to_right, right_edge, jnp.zeros_like(left_edge))
        )
        incoming = trade(outgoing, bit_index)
        left_rim = jnp.where(to_left, incoming, left_rim)
        right_rim = jnp.where(to_right, incoming, right_rim)
    side = jnp.concatenate([left_rim, field_in, right_rim], axis=2)
    upper = from_behind(side[:, side.shape[1] - 1 :], "tile", TILE_COLS)
    lower = from_behind(side[:, :1], "tile", -TILE_COLS)
    return jnp.concatenate([upper, side, lower], axis=1)


def regroup(grouped, gray_pos, sender):
    full_shape = grouped.shape
    for bit_index in range(COL_BITS):
        half_size = 1 << bit_index
        split_view = grouped.reshape(
            full_shape[0],
            full_shape[1],
            TILE_COLS // (2 * half_size),
            2,
            half_size,
            full_shape[3],
            full_shape[4],
            full_shape[5],
        )
        lower_half = split_view[:, :, :, 0]
        upper_half = split_view[:, :, :, 1]
        mine_low = gray_pos // half_size % 2 == 0
        outgoing = jnp.where(mine_low, upper_half, lower_half)
        kept_half = jnp.where(mine_low, lower_half, upper_half)
        incoming = sender(outgoing, bit_index)
        new_lower = jnp.where(mine_low, kept_half, incoming)
        new_upper = jnp.where(mine_low, incoming, kept_half)
        grouped = jnp.stack([new_lower, new_upper], axis=3).reshape(full_shape)
    order = [column ^ column >> 1 for column in range(TILE_COLS)]
    grouped = jnp.take(grouped, jnp.array(order, jnp.int32), axis=2)
    ordered = grouped.transpose(0, 1, 3, 2, 4, 5)
    return ordered.reshape(
        full_shape[0], full_shape[1], full_shape[3] * full_shape[2] * full_shape[4], full_shape[5]
    )


def send_each(outgoing, bit_index):
    return from_partner(outgoing, "tile", bit_index)


def project(token_grad, weights, feats):
    feat_grad = jnp.einsum(
        "iknc,kdc->iknd", token_grad, weights, preferred_element_type=jnp.float32
    )
    proj_term = jnp.einsum("iknd,iknc->kdc", feats, token_grad, preferred_element_type=jnp.float32)
    return (feat_grad.astype(jnp.bfloat16), proj_term.reshape(-1, token_grad.shape[3]))


def per_device(features, proj_weight, conv_weight, saved, cotangent):
    position = lax.axis_index("tile")
    gray_pos = position % TILE_COLS
    col_pos = column_of(gray_pos)
    row_pos = position // TILE_COLS
    row_count = lax.axis_size("tile") // TILE_COLS
    image_count = features.shape[0]
    depth_count = features.shape[1]
    tok_dev = features.shape[2]
    tile_height = saved.shape[2]
    tile_width = saved.shape[3]
    channels = saved.shape[4]
    padded_grad = widen(cotangent, col_pos, gray_pos).astype(jnp.float32)
    row_pooled = pool(padded_grad, 1, row_pos == 0, row_pos == row_count - 1)
    pooled = pool(row_pooled, 2, col_pos == 0, col_pos == TILE_COLS - 1).astype(jnp.bfloat16)
    dpad = widen(pooled, col_pos, gray_pos)
    shifted = [
        dpad[
            :,
            2 - kernel_row : 2 - kernel_row + tile_height,
            2 - kernel_col : 2 - kernel_col + tile_width,
        ]
        for kernel_row in range(3)
        for kernel_col in range(3)
    ]
    patches = jnp.stack(shifted, axis=3).reshape(
        image_count, tile_height, tile_width, 3, 3, channels
    )
    input_grad = jnp.einsum(
        "ihwuvo,kuvco->ikhwc", patches, conv_weight, preferred_element_type=jnp.float32
    ).astype(jnp.bfloat16)
    conv_term = jnp.einsum(
        "ikhwc,ihwuvo->kuvco", saved, patches, preferred_element_type=jnp.float32
    ).reshape(-1, channels)
    grouped = input_grad.reshape(
        image_count, depth_count, TILE_COLS, tile_height // TILE_COLS, tile_width, channels
    )
    grad_parts = []
    term_parts = []
    for depth_index in range(depth_count):
        token_grad = regroup(grouped[:, depth_index : depth_index + 1], gray_pos, send_each)
        feat_part, term_part = project(
            token_grad,
            proj_weight[depth_index : depth_index + 1],
            features[:, depth_index : depth_index + 1],
        )
        grad_parts.append(feat_part)
        term_parts.append(term_part)
    feature_grad = jnp.concatenate(grad_parts, axis=1)
    proj_term = jnp.concatenate(term_parts, axis=0)
    scale = 1.0 / math.sqrt(image_count * lax.axis_size("dp") * tok_dev * lax.axis_size("tile"))
    head_terms = jnp.concatenate([proj_term, conv_term], axis=0) * scale
    head_grad = lax.psum_scatter(head_terms, ("dp", "tile"), scatter_dimension=0, tiled=True)
    return (feature_grad, head_grad)


def solution(mesh):
    in_specs = (
        P("dp", None, "tile", None),
        P(),
        P(),
        P("dp", None, "tile", None, None),
        P("dp", "tile", None, None),
    )
    out_specs = (P("dp", None, "tile", None), P(("dp", "tile"), None))
    return jax.shard_map(
        per_device, mesh=mesh, in_specs=in_specs, out_specs=out_specs, check_vma=False
    )
```

profile of v0, /device:TPU:0, one launch (start us, length us, event | category | flops | bytes accessed | tf_op | source)
XLA Modules:
  0.0 256.7 jit_solution(1790466661318459788)
XLA Ops:
  7.2 0.0 reduce-scatter.2.cloned.1.call-start
  7.3 2.1 broadcast_select_fusion.3
  9.4 3.0 %collective-permute-start = (bf16[4,16,1,256]{3,2,1,0:T(2,128)(2,1)}, bf16[4,16,1,256]{3,2,1,0:T(2,128)(2,1)S(1)}, u32[]{:S(2)}, u32[]{:S(2)}) collective-permute-start(bf16[4,16,1,256]{3,2,1,0:T(2,128)(2,1)} %get-tuple-element.11), channel_id=1, source_target_pairs={{0,4},{4,0},{1,5},{5,1},{2,6},{6,2},{3,7},{7,3},{8,12},{12,8},{9,1... | collective-permute-start | bytes 98312 | tf_op jit(solution)/shard_map/ppermute | solution.py:19
  12.4 1.5 collective-permute-start.1
  14.0 0.9 collective-permute-done
  14.9 2.1 collective-permute-done.1
  17.0 1.1 broadcast_select_fusion.10
  18.1 0.9 pad_maximum_fusion.12
  19.0 4.5 %collective-permute-start.3 = (bf16[4,1,34,256]{3,2,1,0:T(8,128)(2,1)S(1)}, bf16[4,1,34,256]{3,2,1,0:T(8,128)(2,1)S(1)}, u32[]{:S(2)}, u32[]{:S(2)}) collective-permute-start(bf16[4,1,34,256]{3,2,1,0:T(8,128)(2,1)S(1)} %get-tuple-element.7), channel_id=1, source_target_pairs={{0,8},{1,9},{2,10},{3,11},{4,12},{5,13},{6,14},{7,15},{16,24},{17,... | collective-permute-start | bytes 208904 | tf_op jit(solution)/shard_map/ppermute | solution.py:25
  23.5 1.3 collective-permute-start.4
  24.8 0.7 collective-permute-done.3
  25.6 6.0 %collective-permute-done.4 = bf16[4,1,34,256]{3,2,1,0:T(8,128)(2,1)S(1)} collective-permute-done((bf16[4,1,34,256]{3,2,1,0:T(8,128)(2,1)S(1)}, bf16[4,1,34,256]{3,2,1,0:T(8,128)(2,1)S(1)}, u32[]{:S(2)}, u32[]{:S(2)}) %collective-permute-start.4) | collective-permute-done | bytes 69664 | tf_op jit(solution)/shard_map/ppermute | solution.py:25
  31.5 0.6 maximum_convert_fusion
  32.1 1.5 multiply_add_fusion
  33.7 3.8 %slice.142 = f32[4,8,16,256]{3,2,1,0:T(8,128)S(1)} slice(f32[4,8,34,256]{3,2,1,0:T(8,128)} %multiply_add_fusion), slice={[0:4:1], [0:8:1], [1:33:2], [0:256:1]} | slice | bytes 1048576 | tf_op jit(solution)/shard_map/slice | solution.py:30
  37.5 5.1 %slice.143 = f32[4,8,16,256]{3,2,1,0:T(8,128)} slice(f32[4,8,34,256]{3,2,1,0:T(8,128)} %multiply_add_fusion), slice={[0:4:1], [0:8:1], [2:34:2], [0:256:1]} | slice | bytes 1048576 | tf_op jit(solution)/shard_map/slice | solution.py:31
  42.6 5.0 %slice.144 = f32[4,8,16,256]{3,2,1,0:T(8,128)} slice(f32[4,8,34,256]{3,2,1,0:T(8,128)} %multiply_add_fusion), slice={[0:4:1], [0:8:1], [0:32:2], [0:256:1]} | slice | bytes 1048576 | tf_op jit(solution)/shard_map/slice | solution.py:32
  47.7 5.1 %slice.145 = f32[4,8,16,256]{3,2,1,0:T(8,128)} slice(f32[4,8,34,256]{3,2,1,0:T(8,128)} %multiply_add_fusion), slice={[0:4:1], [0:8:1], [3:34:2], [0:256:1]} | slice | bytes 1048576 | tf_op jit(solution)/shard_map/slice | solution.py:33
  52.8 1.7 add_convert_fusion
  54.5 0.1 broadcast_select_fusion.21
  54.6 0.1 collective-permute-start.5
  54.7 1.6 collective-permute-start.6
  56.3 2.3 collective-permute-done.5
  58.6 0.1 collective-permute-done.6
  58.7 0.1 broadcast_select_fusion.28
  58.8 1.3 collective-permute-start.8
  60.1 5.4 %collective-permute-start.9 = (bf16[4,1,18,256]{3,2,1,0:T(8,128)(2,1)S(1)}, bf16[4,1,18,256]{3,2,1,0:T(8,128)(2,1)S(1)}, u32[]{:S(2)}, u32[]{:S(2)}) collective-permute-start(bf16[4,1,18,256]{3,2,1,0:T(8,128)(2,1)S(1)} %get-tuple-element.28), channel_id=1, source_target_pairs={{0,8},{1,9},{2,10},{3,11},{4,12},{5,13},{6,14},{7,15},{16,24},{17,... | collective-permute-start | bytes 110600 | tf_op jit(solution)/shard_map/ppermute | solution.py:25
  65.7 1.6 collective-permute-done.9
  67.3 0.3 maximum_maximum_fusion
  67.7 0.1 fusion.36
  67.8 0.1 fusion.35
  67.9 0.1 fusion.33
  68.1 0.1 fusion.31
  68.2 0.1 fusion.29
  68.2 0.1 fusion.28
  68.4 0.2 copy.37
  68.6 1.4 fusion.15
  70.1 0.1 collective-permute-start.10
  70.2 1.5 fusion.4
  71.7 2.6 %copy.62 = f32[2,3,3,256,256]{4,3,2,1,0:T(8,128)} copy(f32[2,3,3,256,256]{4,3,1,0,2:T(8,128)S(1)} %fusion.4) | data formatting | bytes 9437184 | tf_op jit(solution)/shard_map/ikhwc,ihwuvo->kuvco/transpose | solution.py:152
  74.2 0.6 collective-permute-start.13
  74.9 1.6 collective-permute-start.11
  76.5 0.9 collective-permute-start.14
  77.4 3.8 %collective-permute-done.11 = bf16[4,1,2,2,1,16,256]{6,5,2,0,3,4,1:T(8,128)(2,1)S(1)} collective-permute-done((bf16[4,1,2,2,1,16,256]{6,5,2,0,3,4,1:T(8,128)(2,1)S(1)}, bf16[4,1,2,2,1,16,256]{6,5,2,0,3,4,1:T(8,128)(2,1)S(1)}, u32[]{:S(2)}, u32[]{:S(2)}) %collective-permute-start.11) | collective-permute-done | bytes 131104 | tf_op jit(solution)/shard_map/ppermute | solution.py:19
  81.4 2.0 collective-permute-start.12
  83.5 0.7 select_bitcast_fusion
  84.3 1.7 collective-permute-start.15
  85.9 0.7 collective-permute-done.12
  86.8 0.6 gather_fusion
  87.4 0.7 copy-done.2
  88.1 1.7 convolution_bitcast_fusion.1
  89.8 1.4 copy.63
  91.1 1.0 fusion.45
  92.2 0.6 gather_fusion.1
  92.8 0.7 copy-done.4
  93.5 1.7 convolution_bitcast_fusion
  95.2 1.3 copy.64
  96.5 4.9 %maximum_multiply_fusion = f32[6656,256]{1,0:T(8,128)} fusion(f32[4608,256]{1,0:T(8,128)} %bitcast.282, f32[1024,256]{1,0:T(8,128)} %copy.64, f32[1024,256]{1,0:T(8,128)} %copy.63), kind=kLoop, calls=%fused_computation.2 | loop fusion | flops 5111808 | bytes 13631488 | tf_op jit(solution)/shard_map/mul | solution.py:172
  101.5 0.9 copy-done.3
  102.4 1.5 fusion.7
  103.9 1.5 fusion.8
  105.4 0.2 pad_maximum_fusion
  105.6 1.5 copy.65
  107.1 142.7 %reduce-scatter.2.cloned.1.call-done = f32[208,256]{1,0:T(8,128)} async-done(((f32[6656,256]{1,0:T(8,128)}), f32[208,256]{1,0:T(8,128)}) %reduce-scatter.2.cloned.1.call-update) | async-done | bytes 213008 | tf_op jit(solution)/shard_map/reduce_scatter | solution.py:173
  (52 shorter events, 0.7 us)
Async XLA Ops:
  7.2 61.4 %copy-start = (bf16[2,3,3,256,256]{4,3,2,1,0:T(8,128)(2,1)S(1)}, bf16[2,3,3,256,256]{4,3,2,1,0:T(8,128)(2,1)}, u32[]{:S(2)}) copy-start(bf16[2,3,3,256,256]{4,3,2,1,0:T(8,128)(2,1)} %param.11) | copy-start | bytes 7077892
  7.2 24.3 %copy-start.1 = (bf16[4,16,32,256]{3,2,1,0:T(8,128)(2,1)S(1)}, bf16[4,16,32,256]{3,2,1,0:T(8,128)(2,1)}, u32[]{:S(2)}) copy-start(bf16[4,16,32,256]{3,2,1,0:T(8,128)(2,1)} %param.13) | copy-start | bytes 3145732
  7.2 242.7 %reduce-scatter.2.cloned.1.call-start = ((), (), s32[]{:S(2)}) async-start(), calls=%async_computation.1 | async-start | bytes 7028736 | tf_op jit(solution)/shard_map/reduce_scatter | solution.py:173
  9.4 5.5 %collective-permute-start = (bf16[4,16,1,256]{3,2,1,0:T(2,128)(2,1)}, bf16[4,16,1,256]{3,2,1,0:T(2,128)(2,1)S(1)}, u32[]{:S(2)}, u32[]{:S(2)}) collective-permute-start(bf16[4,16,1,256]{3,2,1,0:T(2,128)(2,1)} %get-tuple-element.11), channel_id=1, source_target_pairs={{0,4},{4,0},{1,5},{5,1},{2,6},{6,2},{3,7},{7,3},{8,12},{12,8},{9,1... | collective-permute-start | bytes 98312 | tf_op jit(solution)/shard_map/ppermute | solution.py:19
  12.4 4.6 %collective-permute-start.1 = (bf16[4,16,1,256]{3,2,1,0:T(2,128)(2,1)}, bf16[4,16,1,256]{3,2,1,0:T(2,128)(2,1)}, u32[]{:S(2)}, u32[]{:S(2)}) collective-permute-start(bf16[4,16,1,256]{3,2,1,0:T(2,128)(2,1)} %get-tuple-element.10), channel_id=1, source_target_pairs={{0,2},{2,0},{1,3},{3,1},{4,6},{6,4},{5,7},{7,5},{8,10},{10,8},{9,1... | collective-permute-start | bytes 98312 | tf_op jit(solution)/shard_map/ppermute | solution.py:19
  13.9 3.1 %collective-permute-start.2 = (bf16[4,16,1,256]{3,2,1,0:T(2,128)(2,1)S(1)}, bf16[4,16,1,256]{3,2,1,0:T(2,128)(2,1)}, u32[]{:S(2)}, u32[]{:S(2)}) collective-permute-start(bf16[4,16,1,256]{3,2,1,0:T(2,128)(2,1)S(1)} %get-tuple-element.9), channel_id=1, source_target_pairs={{0,1},{1,0},{2,3},{3,2},{4,5},{5,4},{6,7},{7,6},{8,9},{9,8},{10,11... | collective-permute-start | bytes 98312 | tf_op jit(solution)/shard_map/ppermute | solution.py:19
  19.0 6.5 %collective-permute-start.3 = (bf16[4,1,34,256]{3,2,1,0:T(8,128)(2,1)S(1)}, bf16[4,1,34,256]{3,2,1,0:T(8,128)(2,1)S(1)}, u32[]{:S(2)}, u32[]{:S(2)}) collective-permute-start(bf16[4,1,34,256]{3,2,1,0:T(8,128)(2,1)S(1)} %get-tuple-element.7), channel_id=1, source_target_pairs={{0,8},{1,9},{2,10},{3,11},{4,12},{5,13},{6,14},{7,15},{16,24},{17,... | collective-permute-start | bytes 208904 | tf_op jit(solution)/shard_map/ppermute | solution.py:25
  23.5 8.0 %collective-permute-start.4 = (bf16[4,1,34,256]{3,2,1,0:T(8,128)(2,1)S(1)}, bf16[4,1,34,256]{3,2,1,0:T(8,128)(2,1)S(1)}, u32[]{:S(2)}, u32[]{:S(2)}) collective-permute-start(bf16[4,1,34,256]{3,2,1,0:T(8,128)(2,1)S(1)} %get-tuple-element.8), channel_id=1, source_target_pairs={{8,0},{9,1},{10,2},{11,3},{12,4},{13,5},{14,6},{15,7},{24,16},{25,... | collective-permute-start | bytes 208904 | tf_op jit(solution)/shard_map/ppermute | solution.py:25
  42.6 23.0 %copy-start.8 = (s32[8]{0:T(128)S(1)}, s32[8]{0:T(128)}, u32[]{:S(2)}) copy-start(s32[8]{0:T(128)} %constant.140) | copy-start | bytes 100
  54.6 4.0 %collective-permute-start.5 = (bf16[4,8,1,256]{3,2,1,0:T(2,128)(2,1)S(1)}, bf16[4,8,1,256]{3,2,1,0:T(2,128)(2,1)S(1)}, u32[]{:S(2)}, u32[]{:S(2)}) collective-permute-start(bf16[4,8,1,256]{3,2,1,0:T(2,128)(2,1)S(1)} %get-tuple-element.31), channel_id=1, source_target_pairs={{0,4},{4,0},{1,5},{5,1},{2,6},{6,2},{3,7},{7,3},{8,12},{12,8},{9,1... | collective-permute-start | bytes 49160 | tf_op jit(solution)/shard_map/ppermute | solution.py:19
  54.7 4.0 %collective-permute-start.6 = (bf16[4,8,1,256]{3,2,1,0:T(2,128)(2,1)S(1)}, bf16[4,8,1,256]{3,2,1,0:T(2,128)(2,1)S(1)}, u32[]{:S(2)}, u32[]{:S(2)}) collective-permute-start(bf16[4,8,1,256]{3,2,1,0:T(2,128)(2,1)S(1)} %get-tuple-element.32), channel_id=1, source_target_pairs={{0,2},{2,0},{1,3},{3,1},{4,6},{6,4},{5,7},{7,5},{8,10},{10,8},{9,1... | collective-permute-start | bytes 49160 | tf_op jit(solution)/shard_map/ppermute | solution.py:19
  56.3 2.4 collective-permute-start.7
  58.8 6.9 %collective-permute-start.8 = (bf16[4,1,18,256]{3,2,1,0:T(8,128)(2,1)S(1)}, bf16[4,1,18,256]{3,2,1,0:T(8,128)(2,1)S(1)}, u32[]{:S(2)}, u32[]{:S(2)}) collective-permute-start(bf16[4,1,18,256]{3,2,1,0:T(8,128)(2,1)S(1)} %get-tuple-element.29), channel_id=1, source_target_pairs={{8,0},{9,1},{10,2},{11,3},{12,4},{13,5},{14,6},{15,7},{24,16},{25,... | collective-permute-start | bytes 110600 | tf_op jit(solution)/shard_map/ppermute | solution.py:25
  60.1 7.2 %collective-permute-start.9 = (bf16[4,1,18,256]{3,2,1,0:T(8,128)(2,1)S(1)}, bf16[4,1,18,256]{3,2,1,0:T(8,128)(2,1)S(1)}, u32[]{:S(2)}, u32[]{:S(2)}) collective-permute-start(bf16[4,1,18,256]{3,2,1,0:T(8,128)(2,1)S(1)} %get-tuple-element.28), channel_id=1, source_target_pairs={{0,8},{1,9},{2,10},{3,11},{4,12},{5,13},{6,14},{7,15},{16,24},{17,... | collective-permute-start | bytes 110600 | tf_op jit(solution)/shard_map/ppermute | solution.py:25
  68.6 1.6 copy-start.7
  70.1 4.7 %collective-permute-start.10 = (bf16[4,1,4,1,1,16,256]{6,5,2,0,4,3,1:T(8,128)(2,1)S(1)}, bf16[4,1,4,1,1,16,256]{6,5,2,0,4,3,1:T(8,128)(2,1)S(1)}, u32[]{:S(2)}, u32[]{:S(2)}) collective-permute-start(bf16[4,1,4,1,1,16,256]{6,5,2,0,4,3,1:T(8,128)(2,1)S(1)} %select_bitcast_fusion.5), channel_id=1, source_target_pairs={{0,1},{1,0},{2,3},{3,2},{4,5},{5,4},{6,7},{7,6},{8,9},{9,8},{10,11... | collective-permute-start | bytes 393224 | tf_op jit(solution)/shard_map/ppermute | solution.py:19
  74.2 2.2 collective-permute-start.13
  74.9 6.4 %collective-permute-start.11 = (bf16[4,1,2,2,1,16,256]{6,5,2,0,3,4,1:T(8,128)(2,1)S(1)}, bf16[4,1,2,2,1,16,256]{6,5,2,0,3,4,1:T(8,128)(2,1)S(1)}, u32[]{:S(2)}, u32[]{:S(2)}) collective-permute-start(bf16[4,1,2,2,1,16,256]{6,5,2,0,3,4,1:T(8,128)(2,1)S(1)} %select_bitcast_fusion.4), channel_id=1, source_target_pairs={{0,2},{2,0},{1,3},{3,1},{4,6},{6,4},{5,7},{7,5},{8,10},{10,8},{9,1... | collective-permute-start | bytes 393224 | tf_op jit(solution)/shard_map/ppermute | solution.py:19
  76.5 6.9 %collective-permute-start.14 = (bf16[4,1,2,2,1,16,256]{6,5,2,0,3,4,1:T(8,128)(2,1)S(1)}, bf16[4,1,2,2,1,16,256]{6,5,2,0,3,4,1:T(8,128)(2,1)S(1)}, u32[]{:S(2)}, u32[]{:S(2)}) collective-permute-start(bf16[4,1,2,2,1,16,256]{6,5,2,0,3,4,1:T(8,128)(2,1)S(1)} %fusion.38), channel_id=1, source_target_pairs={{0,2},{2,0},{1,3},{3,1},{4,6},{6,4},{5,7},{7,5},{8,10},{10,8},{9,1... | collective-permute-start | bytes 393224 | tf_op jit(solution)/shard_map/ppermute | solution.py:19
  81.4 5.3 %collective-permute-start.12 = (bf16[4,1,1,4,1,16,256]{6,5,3,0,4,2,1:T(8,128)(2,1)S(1)}, bf16[4,1,1,4,1,16,256]{6,5,3,0,4,2,1:T(8,128)(2,1)S(1)}, u32[]{:S(2)}, u32[]{:S(2)}) collective-permute-start(bf16[4,1,1,4,1,16,256]{6,5,3,0,4,2,1:T(8,128)(2,1)S(1)} %select_bitcast_fusion.3), channel_id=1, source_target_pairs={{0,4},{4,0},{1,5},{5,1},{2,6},{6,2},{3,7},{7,3},{8,12},{12,8},{9,1... | collective-permute-start | bytes 393224 | tf_op jit(solution)/shard_map/ppermute | solution.py:19
  83.5 3.2 %copy-start.6 = (bf16[4,1,2,2,2,1,16,256]{7,6,4,3,0,2,5,1:T(8,128)(2,1)}, bf16[4,1,2,2,2,1,16,256]{7,6,4,3,0,2,5,1:T(8,128)(2,1)S(1)}, u32[]{:S(2)}) copy-start(bf16[4,1,2,2,2,1,16,256]{7,6,4,3,0,2,5,1:T(8,128)(2,1)S(1)} %copy.53) | copy-start | bytes 786436
  84.3 6.9 %collective-permute-start.15 = (bf16[4,1,1,4,1,16,256]{6,5,3,0,4,2,1:T(8,128)(2,1)}, bf16[4,1,1,4,1,16,256]{6,5,3,0,4,2,1:T(8,128)(2,1)S(1)}, u32[]{:S(2)}, u32[]{:S(2)}) collective-permute-start(bf16[4,1,1,4,1,16,256]{6,5,3,0,4,2,1:T(8,128)(2,1)} %select_bitcast_fusion), channel_id=1, source_target_pairs={{0,4},{4,0},{1,5},{5,1},{2,6},{6,2},{3,7},{7,3},{8,12},{12,8},{9,1... | collective-permute-start | bytes 393224 | tf_op jit(solution)/shard_map/ppermute | solution.py:19
  87.4 0.7 copy-start.2
  92.8 0.7 copy-start.4
  101.4 0.9 copy-start.3
  101.4 2.5 copy-start.5
Sparse Core Ops, SparseCore 0:
  101.6 148.2 reduce-scatter.1
where the time goes:
time: 258 us; the launch traced here: 257 us
  waiting for transfers between devices  161 us (62%)
  local copies, waits for them, and re-layouts  30 us (12%)
  starting transfers between devices  25.6 us (10%)
  other arithmetic  16 us (6%)
  between operations  14.6 us (6%)
  matrix products  9.3 us (4%)
    reduce_scatter x1, waiting for transfers between devices, per_device(): lax.psum_scatter(head_terms, ('dp', 'tile'), scatter_dimension=0, tiled=T...  143 us
    ppermute x12, starting transfers between devices, from_partner(): return lax.ppermute(block, axis, route)  13 us
    ppermute x4, starting transfers between devices, from_behind(): return lax.ppermute(block, axis, route)  12.5 us
    ppermute x12, waiting for transfers between devices, from_partner(): return lax.ppermute(block, axis, route)  10 us
    ppermute x4, waiting for transfers between devices, from_behind(): return lax.ppermute(block, axis, route)  8.31 us
  transfers between devices with their start and end apart: 17, of which 10 were waited for; matrix products, arithmetic and copies ran while one was open for 5% of the time, Pallas kernels for 0%

commit v1 on v0

v1 whole, which is shorter than its diff:
```python
import functools
import math

import jax
import jax.numpy as jnp
from jax import lax
from jax.experimental import pallas as pl
from jax.experimental.pallas import tpu as pltpu
from jax.sharding import PartitionSpec as P

TILE_COLS = 8
HALO = 4
LEFT = 8
BF16 = jnp.bfloat16
F32 = jnp.float32


def gray_of(column):
    return column ^ column >> 1


def paired(count, first):
    pairs = []
    for low in range(first, count - 1, 2):
        pairs += [(low, low + 1), (low + 1, low)]
    return pairs


def tile_route(row_pairs, col_pairs, rows):
    row_moves = row_pairs if row_pairs is not None else [(r, r) for r in range(rows)]
    col_moves = col_pairs if col_pairs is not None else [(c, c) for c in range(TILE_COLS)]
    return [
        (r0 * TILE_COLS + gray_of(c0), r1 * TILE_COLS + gray_of(c1))
        for r0, r1 in row_moves
        for c0, c1 in col_moves
    ]


def pool_conv_kernel(
    has_second, flags, cot, row_a, row_b, col_a, col_b, aa, ab, ba, bb, weight, saved, ig, early, late,
    rows_ref, cells_ref, patch_ref, acc_ref,
):
    images, height2, width2, channels = cot.shape
    height, width = height2 // 2, width2 // 2
    depths = weight.shape[0]
    row_odd, col_odd = flags[0] == 1, flags[1] == 1
    top, bottom, left, right = flags[2] == 1, flags[3] == 1, flags[4] == 1, flags[5] == 1
    zero = jnp.zeros((), F32)

    def mix(odd, when_odd, when_even):
        if when_even is None:
            return jnp.where(odd, when_odd, zero)
        if when_odd is None:
            return jnp.where(odd, zero, when_even)
        return jnp.where(odd, when_odd, when_even)

    def load(ref, *at):
        return ref[at].astype(F32)

    def pool_rows(line, up, down):
        first, last = line(0), line(height2 - 1)
        above = jnp.where(top, first, up[1])
        below = jnp.where(bottom, last, down[0])
        out = [jnp.where(top, zero, up[0] + 0.25 * first)]
        for j in range(height):
            before = above if j == 0 else line(2 * j - 1)
            after = below if j == height - 1 else line(2 * j + 2)
            out.append(0.75 * (line(2 * j) + line(2 * j + 1)) + 0.25 * (before + after))
        out.append(jnp.where(bottom, zero, down[1] + 0.25 * last))
        return out

    def per_image(i, carry):
        def ends(first_ref, second_ref):
            up = [mix(row_odd, load(first_ref, i, n), load(second_ref, i, n) if has_second else None) for n in range(2)]
            down = [mix(row_odd, load(second_ref, i, n) if has_second else None, load(first_ref, i, n)) for n in range(2)]
            return up, down

        def corner(first_ref, second_ref, n, is_left):
            one, two = load(first_ref, i, n), load(second_ref, i, n)
            return jnp.where(col_odd, one, two) if is_left else jnp.where(col_odd, two, one)

        def put(d, at, value):
            for h in range(channels // 128):
                rows_ref[h, d, at : at + value.shape[0], :] = value[:, h * 128 : (h + 1) * 128]

        up, down = ends(row_a, row_b)
        centre = pool_rows(lambda r: load(cot, i, r), up, down)
        for d, value in enumerate(centre):
            put(d, LEFT, value)
        for is_left in (True, False):
            def line(r):
                one, two = load(col_a, i, r), load(col_b, i, r)
                return jnp.where(col_odd, one, two) if is_left else jnp.where(col_odd, two, one)

            firsts = [corner(aa, ab, n, is_left) for n in range(2)]
            seconds = [corner(ba, bb, n, is_left) for n in range(2)] if has_second else [None, None]
            side_up = [mix(row_odd, firsts[n], seconds[n]) for n in range(2)]
            side_down = [mix(row_odd, seconds[n], firsts[n]) for n in range(2)]
            for d, value in enumerate(pool_rows(line, side_up, side_down)):
                if is_left:
                    value = jnp.where(left, jnp.broadcast_to(centre[d][0:1], value.shape), value)
                    put(d, LEFT - HALO, value)
                else:
                    value = jnp.where(right, jnp.broadcast_to(centre[d][width2 - 1 : width2], value.shape), value)
                    put(d, LEFT + width2, value)
        cells = width + 8
        column = lax.broadcasted_iota(jnp.int32, (cells, channels), 0)
        outside = jnp.logical_or(
            jnp.logical_and(column == 0, left), jnp.logical_and(column == width + 1, right)
        )
        for d in range(height + 2):
            taps = [
                jnp.concatenate(
                    [rows_ref[h, d, pl.ds(LEFT - 3 + n, cells, stride=2), :] for h in range(channels // 128)],
                    axis=1,
                )
                for n in range(4)
            ]
            pooled = 0.75 * (taps[1] + taps[2]) + 0.25 * (taps[0] + taps[3])
            cells_ref[d] = jnp.where(outside, 0.0, pooled)
        for d in range(height + 2):
            for v in range(3):
                block = cells_ref[d, pl.ds(2 - v, width), :].astype(BF16)
                for u in range(3):
                    h = d - 2 + u
                    if 0 <= h < height:
                        at = pl.multiple_of((i * height + h) * width, width)
                        patch_ref[pl.ds(at, width), pl.ds((u * 3 + v) * channels, channels)] = block
        return carry

    rows_ref[...] = jnp.zeros_like(rows_ref)
    lax.fori_loop(0, images, per_image, 0)
    for k in range(depths):
        for n in range(9):
            part = lax.dot_general(
                patch_ref[:, pl.ds(n * channels, channels)],
                weight[k, n // 3, n % 3],
                (((1,), (1,)), ((), ())),
                preferred_element_type=F32,
            )
            if n == 0:
                acc_ref[...] = part
            else:
                acc_ref[...] += part
        for i in range(images):
            for h in range(height):
                at = (i * height + h) * width
                ig[h, i, k] = acc_ref[at : at + width, :].astype(BF16)
    split = late.shape[0]
    for k in range(depths):
        flat = saved[:, k].reshape(images * height * width, channels)
        flat_t = flat.T
        for n in range(9):
            part = jnp.dot(
                flat_t, patch_ref[:, pl.ds(n * channels, channels)], preferred_element_type=F32
            ).astype(BF16)
            at = (k * 9 + n) * channels
            if at < split:
                late[at : at + channels, :] = part
            else:
                early[at - split : at - split + channels, :] = part


def proj_term_kernel(came, feats, conv_late, out, tokens):
    groups, images, depths, width, channels = came.shape
    for k in range(depths):
        for i in range(images):
            for c in range(groups):
                at = (i * groups + c) * width
                tokens[k, at : at + width, :] = came[gray_of(c), i, k]
    dim = feats.shape[3]
    for k in range(depths):
        flat = feats[:, k].reshape(images * feats.shape[2], dim)
        part = lax.dot_general(
            flat, tokens[k], (((0,), (0,)), ((), ())), preferred_element_type=F32
        )
        out[k * dim : (k + 1) * dim, :] = part.astype(BF16)
    out[depths * dim :, :] = conv_late[...]


def feat_grad_kernel(tokens, weight, out):
    images, depths, count, dim = out.shape
    for k in range(depths):
        part = lax.dot_general(
            tokens[k], weight[k], (((1,), (1,)), ((), ())), preferred_element_type=F32
        )
        out[:, k] = part.astype(BF16).reshape(images, count, dim)


def vmem_call(kernel, out_shape, operands, scratch=(), scalars=0, flops=0, limit=48):
    whole = pl.BlockSpec(memory_space=pltpu.VMEM)
    moved = sum(a.size * a.dtype.itemsize for a in operands)
    moved += sum(math.prod(s.shape) * s.dtype.itemsize for s in jax.tree.leaves(out_shape))
    return pl.pallas_call(
        kernel,
        out_shape=out_shape,
        in_specs=[pl.BlockSpec(memory_space=pltpu.SMEM)] * scalars + [whole] * (len(operands) - scalars),
        out_specs=jax.tree.map(lambda _: whole, out_shape),
        scratch_shapes=list(scratch),
        compiler_params=pltpu.CompilerParams(vmem_limit_bytes=limit << 20),
        cost_estimate=pl.CostEstimate(flops=flops, bytes_accessed=moved, transcendentals=0),
    )(*operands)


def halved(block, index, bit):
    count = lax.axis_size("tile")
    rows, channels = block.shape[1:]
    pairs = block.reshape(block.shape[0] // 2, 2, rows, channels)
    mine = index >> bit & 1
    sent = lax.dynamic_index_in_dim(pairs, 1 - mine, 1, keepdims=False)
    kept = lax.dynamic_index_in_dim(pairs, mine, 1, keepdims=False)
    came = lax.ppermute(sent, "tile", [(t, t ^ 1 << bit) for t in range(count)])
    return kept.astype(F32) + came.astype(F32)


def scatter_sum(terms, index):
    count = lax.axis_size("tile")
    block = terms.reshape(count, terms.shape[0] // count, terms.shape[1])
    bits = count.bit_length() - 1
    for bit in range(bits):
        total = halved(block, index, bit)
        block = total.astype(BF16)
    return total[0]


def per_device(features, proj_weight, conv_weight, saved, cotangent):
    position = lax.axis_index("tile")
    tile_count = lax.axis_size("tile")
    rows = tile_count // TILE_COLS
    gray = position % TILE_COLS
    col = gray ^ gray >> 1 ^ gray >> 2
    row = position // TILE_COLS
    images, height2, width2, channels = cotangent.shape
    depths, dim = proj_weight.shape[:2]
    height, width = height2 // 2, width2 // 2
    patches = images * height * width
    row_odd, col_odd = row % 2 == 1, col % 2 == 1

    cot = cotangent
    wide = cot.astype(F32)
    to_below = jnp.stack(
        [0.25 * wide[:, -3] + 0.75 * (wide[:, -2] + wide[:, -1]), wide[:, -1]], axis=1
    ).astype(BF16)
    to_above = jnp.stack(
        [wide[:, 0], 0.75 * (wide[:, 0] + wide[:, 1]) + 0.25 * wide[:, 2]], axis=1
    ).astype(BF16)
    has_second = rows > 2

    def swap(block, row_pairs, col_pairs):
        return lax.ppermute(block, "tile", tile_route(row_pairs, col_pairs, rows))

    row_first, row_second = paired(rows, 0), paired(rows, 1)
    col_first, col_second = paired(TILE_COLS, 0), paired(TILE_COLS, 1)
    row_out = jnp.where(row_odd, to_above, to_below)
    row_a = swap(row_out, row_first, None)

    def edge(block, odd):
        return jnp.where(odd, block[:, :, :HALO], block[:, :, width2 - HALO :])

    col_b = swap(edge(cot, jnp.logical_not(col_odd)), None, col_second)
    col_a = swap(edge(cot, col_odd), None, col_first)
    ab = swap(edge(row_out, jnp.logical_not(col_odd)), row_first, col_second)
    aa = swap(edge(row_out, col_odd), row_first, col_first)
    if has_second:
        row_out = jnp.where(row_odd, to_below, to_above)
        row_b = swap(row_out, row_second, None)
        bb = swap(edge(row_out, jnp.logical_not(col_odd)), row_second, col_second)
        ba = swap(edge(row_out, col_odd), row_second, col_first)
    else:
        row_b, ba, bb = row_a, aa, ab
    flags = jnp.stack(
        [row % 2, col % 2, row == 0, row == rows - 1, col == 0, col == TILE_COLS - 1]
    ).astype(jnp.int32)
    head_rows = depths * (dim + 9 * channels)
    conv_late = head_rows // 2 - depths * dim
    conv_early = head_rows // 2
    sds = jax.ShapeDtypeStruct
    conv_flops = 2 * patches * depths * 9 * channels * channels
    ig, early, late = vmem_call(
        functools.partial(pool_conv_kernel, has_second),
        (
            sds((height, images, depths, width, channels), BF16),
            sds((conv_early, channels), BF16),
            sds((conv_late, channels), BF16),
        ),
        (flags, cot, row_a, row_b, col_a, col_b, aa, ab, ba, bb, conv_weight, saved),
        scratch=(
            pltpu.VMEM((channels // 128, height + 2, LEFT + width2 + 16, 128), F32),
            pltpu.VMEM((height + 2, width + 8, channels), F32),
            pltpu.VMEM((patches, 9 * channels), BF16),
            pltpu.VMEM((patches, channels), F32),
        ),
        scalars=1,
        flops=2 * conv_flops,
    )
    groups = [[g * TILE_COLS + t for t in range(TILE_COLS)] for g in range(rows)]
    came = lax.all_to_all(ig, "tile", 0, 0, axis_index_groups=groups, tiled=True)
    early_sum = scatter_sum(early, position)
    tokens = features.shape[2]
    proj_flops = 2 * images * tokens * depths * dim * channels
    terms, token_grad = vmem_call(
        proj_term_kernel,
        (sds((head_rows // 2, channels), BF16), sds((depths, images * tokens, channels), BF16)),
        (came, features, late),
        flops=proj_flops,
    )
    feature_grad = vmem_call(
        feat_grad_kernel,
        sds((images, depths, tokens, dim), BF16),
        (token_grad, proj_weight),
        flops=proj_flops,
    )
    late_sum = scatter_sum(terms, position)
    first = lax.axis_index("dp") == 0
    sent = jnp.where(first, early_sum, late_sum).astype(BF16)
    kept = jnp.where(first, late_sum, early_sum)
    other = lax.ppermute(sent, "dp", [(0, 1), (1, 0)])
    scale = 1.0 / math.sqrt(images * lax.axis_size("dp") * tokens * tile_count)
    head_grad = (kept + other.astype(F32)) * scale
    return feature_grad, head_grad


def solution(mesh):
    in_specs = (
        P("dp", None, "tile", None),
        P(),
        P(),
        P("dp", None, "tile", None, None),
        P("dp", "tile", None, None),
    )
    out_specs = (P("dp", None, "tile", None), P(("dp", "tile"), None))
    return jax.shard_map(
        per_device, mesh=mesh, in_specs=in_specs, out_specs=out_specs, check_vma=False
    )
```

time: 258 us -> 87.3 us (0.34)
  waiting for transfers between devices: 161 us -> 33.4 us
  local copies, waits for them, and re-layouts: 30 us -> 7.42 us
  between operations: 14.6 us -> 0.9 us
  matrix products: 9.3 us -> 0 us
  Pallas kernels: 0 us -> 8.18 us
  other arithmetic: 16 us -> 9.29 us
    reduce_scatter x1 -> x0, waiting for transfers between devices: 143 us -> none  [per_device(): lax.psum_scatter(head_terms, ('dp', 'tile'), scatter_dimension=0, tiled=T...]
    slice x5 -> x1, local copies, waits for them, and re-layouts: 19.2 us -> 0.01 us  [per_device(): wide[:, -1]]
    dot_general x6 -> x0, matrix products: 9.3 us -> none  [the longest x2 3.38 us: project(): jnp.einsum('iknd,iknc->kdc', feats, token_grad, preferred_element_type=jn...]
    ppermute x16 -> x14, waiting for transfers between devices: 18.3 us -> 27.2 us  [the longest x8 24.1 us: halved(): came = lax.ppermute(sent, 'tile', [(t, t ^ 1 << bit) for t in range(count)])]
    pallas_call x0 -> x3, Pallas kernels: none -> 8.18 us  [vmem_call(): pl.pallas_call(kernel, out_shape=out_shape, in_specs=[pl.BlockSpec(memory...]
    all_to_all x0 -> x1, starting transfers between devices: none -> 7.55 us  [per_device(): lax.all_to_all(ig, 'tile', 0, 0, axis_index_groups=groups, tiled=True)]
    all_to_all x0 -> x1, waiting for transfers between devices: none -> 6.21 us  [per_device(): lax.all_to_all(ig, 'tile', 0, 0, axis_index_groups=groups, tiled=True)]
    ppermute x16 -> x14, starting transfers between devices: 25.6 us -> 20 us  [the longest x8 10 us: halved(): came = lax.ppermute(sent, 'tile', [(t, t ^ 1 << bit) for t in range(count)])]
  transfers between devices with their start and end apart: 17 -> 15, of which waited for: 10 -> 8; matrix products, arithmetic and copies ran while one was open for 5% -> 9% of each run, Pallas kernels for 0% -> 3%
where the time goes in v1:
time: 87.3 us; the launch traced here: 86.8 us
  waiting for transfers between devices  33.4 us (38%)
  starting transfers between devices  27.6 us (32%)
  other arithmetic  9.29 us (11%)
  Pallas kernels  8.18 us (9%)
  local copies, waits for them, and re-layouts  7.42 us (8%)
  between operations  0.9 us (1%)
    ppermute x8, waiting for transfers between devices, halved(): came = lax.ppermute(sent, 'tile', [(t, t ^ 1 << bit) for t in range(count)])  24.1 us
    ppermute x8, starting transfers between devices, halved(): came = lax.ppermute(sent, 'tile', [(t, t ^ 1 << bit) for t in range(count)])  10 us
    ppermute x5, starting transfers between devices, swap(): return lax.ppermute(block, 'tile', tile_route(row_pairs, col_pairs, rows))  8.46 us
    pallas_call x3, Pallas kernels, vmem_call(): pl.pallas_call(kernel, out_shape=out_shape, in_specs=[pl.BlockSpec(memory...  8.18 us
    all_to_all x1, starting transfers between devices, per_device(): lax.all_to_all(ig, 'tile', 0, 0, axis_index_groups=groups, tiled=True)  7.55 us
    all_to_all x1, waiting for transfers between devices, per_device(): lax.all_to_all(ig, 'tile', 0, 0, axis_index_groups=groups, tiled=True)  6.21 us
    unnamed x22, local copies, waits for them, and re-layouts  4.22 us
    convert_element_type x6, other arithmetic, scatter_sum(): block = total.astype(BF16)  4.07 us
  transfers between devices with their start and end apart: 15, of which 8 were waited for; matrix products, arithmetic and copies ran while one was open for 9% of the time, Pallas kernels for 3%

profile of v1, /device:TPU:0, one launch (start us, length us, event | category | flops | bytes accessed | tf_op | source)
XLA Modules:
  0.0 86.8 jit_solution(7720864687159857291)
XLA Ops:
  0.6 0.0 copy-start.1
  0.7 2.9 %convert_element_type.106 = f32[4,16,32,256]{3,2,1,0:T(8,128)} convert(bf16[4,16,32,256]{3,2,1,0:T(8,128)(2,1)} %cot.1) | non-fusion elementwise | flops 524288 | bytes 3145728 | tf_op jit(solution)/shard_map/convert_element_type | solution.py:240
  3.6 0.0 copy-done.1
  3.6 1.3 %fusion.9 = (bf16[4,1,32,256]{3,2,1,0:T(8,128)(2,1)S(1)}, bf16[4,1,32,256]{3,2,1,0:T(8,128)(2,1)S(1)}) fusion(f32[4,16,32,256]{3,2,1,0:T(8,128)} %convert_element_type.106), kind=kLoop, calls=%fused_computation.26 | loop fusion | flops 327680 | bytes 917504 | tf_op jit(solution)/shard_map/convert.10
  4.9 4.1 %collective-permute-start = (bf16[4,2,32,256]{3,2,1,0:T(8,128)(2,1)S(1)}, bf16[4,2,32,256]{3,2,1,0:T(8,128)(2,1)S(1)}, u32[]{:S(2)}, u32[]{:S(2)}) collective-permute-start(bf16[4,2,32,256]{3,2,1,0:T(8,128)(2,1)S(1)} %maximum_select_fusion), channel_id=1, source_target_pairs={{0,8},{1,9},{3,11},{2,10},{6,14},{7,15},{5,13},{4,12},{8,0},{9,1},... | collective-permute-start | bytes 393224 | tf_op jit(solution)/shard_map/ppermute | solution.py:250
  9.0 0.1 broadcast_select_fusion
  9.2 0.1 collective-permute-start.1
  9.3 0.7 collective-permute-start.2
  10.0 3.0 %collective-permute-start.3 = (bf16[4,2,4,256]{3,2,1,0:T(4,128)(2,1)S(1)}, bf16[4,2,4,256]{3,2,1,0:T(4,128)(2,1)S(1)}, u32[]{:S(2)}, u32[]{:S(2)}) collective-permute-start(bf16[4,2,4,256]{3,2,1,0:T(4,128)(2,1)S(1)} %get-tuple-element.19), channel_id=1, source_target_pairs={{0,9},{1,8},{3,10},{2,11},{6,15},{7,14},{5,12},{4,13},{8,1},{9,0},... | collective-permute-start | bytes 49160 | tf_op jit(solution)/shard_map/ppermute | solution.py:250
  13.0 0.7 collective-permute-start.4
  13.6 0.1 stack.53.flags
  13.7 1.1 %collective-permute-done.3.aa.ba = bf16[4,2,4,256]{3,2,1,0:T(4,128)(2,1)S(1)} collective-permute-done((bf16[4,2,4,256]{3,2,1,0:T(4,128)(2,1)S(1)}, bf16[4,2,4,256]{3,2,1,0:T(4,128)(2,1)S(1)}, u32[]{:S(2)}, u32[]{:S(2)}) %collective-permute-start.3) | collective-permute-done | bytes 16416 | tf_op jit(solution)/shard_map/ppermute | solution.py:250
  14.9 0.0 collective-permute-done.4.ab.bb
  14.9 0.8 collective-permute-done.row_a.row_b
  15.7 0.0 collective-permute-done.1.col_a
  15.7 0.0 collective-permute-done.2.col_b
  15.7 0.0 copy-done.10
  15.7 5.3 %shard_map.68 = (bf16[8,4,2,16,256]{4,3,2,1,0:T(8,128)(2,1)S(1)}, bf16[3328,256]{1,0:T(8,128)(2,1)S(1)}, bf16[1280,256]{1,0:T(8,128)(2,1)S(1)}) custom-call(s32[6]{0:T(128)S(1)} %stack.53.flags, bf16[4,16,32,256]{3,2,1,0:T(8,128)(2,1)S(1)} %copy-done.1, bf16[4,2,32,256]{3,2,1,0:T(8,128)(2,1)S(1)} %collective-permute-done.row_a.row_b, ...), custom_call_target="tpu_custom_call" | custom-call | flops 2415919104 | bytes 7405592 | tf_op jit(solution)/shard_map/pallas_call | solution.py:194
  21.0 0.0 copy-start.2
  21.1 1.2 %copy-done.2 = bf16[3328,256]{1,0:T(8,128)(2,1)} copy-done((bf16[3328,256]{1,0:T(8,128)(2,1)}, bf16[3328,256]{1,0:T(8,128)(2,1)S(1)}, u32[]{:S(2)}) %copy-start.2) | copy-done | bytes 1703960
  22.3 0.8 copy-done.9
  23.1 7.5 %all-to-all-start = ((bf16[8,4,2,16,256]{4,3,2,1,0:T(8,128)(2,1)}), bf16[8,4,2,16,256]{4,3,2,1,0:T(8,128)(2,1)S(1)}, u32[]{:S(2)}, u32[]{:S(2)}) async-start(bf16[8,4,2,16,256]{4,3,2,1,0:T(8,128)(2,1)} %copy-done.9), calls=%async_computation | async-start | bytes 1048576 | tf_op jit(solution)/shard_map/all_to_all | solution.py:297
  30.6 2.1 %dynamic-slice_bitcast_fusion = bf16[8,208,256]{2,1,0:T(8,128)(2,1)} fusion(bf16[8,2,208,256]{3,2,1,0:T(8,128)(2,1)} %bitcast.54, s32[]{:T(128)S(6)} %select_n.127), kind=kLoop, calls=%fused_computation.8 | loop fusion | bytes 1703940 | tf_op jit(solution)/shard_map/jit(dynamic_index_in_dim)/squeeze | solution.py:210
  32.7 0.5 collective-permute-start.9
  33.2 6.2 %all-to-all-done.came = bf16[8,4,2,16,256]{4,3,2,1,0:T(8,128)(2,1)S(1)} async-done(((bf16[8,4,2,16,256]{4,3,2,1,0:T(8,128)(2,1)}), bf16[8,4,2,16,256]{4,3,2,1,0:T(8,128)(2,1)S(1)}, u32[]{:S(2)}, u32[]{:S(2)}) %all-to-all-start) | async-done | bytes 524320 | tf_op jit(solution)/shard_map/all_to_all | solution.py:297
  39.5 0.0 copy-done
  39.5 0.8 shard_map.69
  40.3 0.0 copy-start.4
  40.3 0.0 copy-start.7
  40.3 0.0 copy-start.3
  40.3 1.2 %copy-done.4 = bf16[3328,256]{1,0:T(8,128)(2,1)} copy-done((bf16[3328,256]{1,0:T(8,128)(2,1)}, bf16[3328,256]{1,0:T(8,128)(2,1)S(1)}, u32[]{:S(2)}) %copy-start.4) | copy-done | bytes 1703960
  41.5 0.1 dynamic-slice_bitcast_fusion.1
  41.5 0.1 copy-done.7
  41.6 0.0 collective-permute-start.5
  41.6 0.0 collective-permute-done.9
  41.6 0.9 %copy-done.3 = bf16[3328,256]{1,0:T(8,128)(2,1)S(1)} copy-done((bf16[3328,256]{1,0:T(8,128)(2,1)S(1)}, bf16[3328,256]{1,0:T(8,128)(2,1)}, u32[]{:S(2)}) %copy-start.3) | copy-done | bytes 1703960
  42.5 1.4 %fusion = bf16[8,208,256]{2,1,0:T(8,128)(2,1)S(1)} fusion(bf16[8,208,256]{2,1,0:T(8,128)(2,1)} %collective-permute-done.9, bf16[8,2,208,256]{3,2,1,0:T(8,128)(2,1)S(1)} %bitcast.55, s32[]{:T(128)S(6)} %select_n.126), kind=kLoop, calls=%fused_computation.1 | loop fusion | flops 1703936 | bytes 2555908 | tf_op jit(solution)/shard_map/convert_element_type | solution.py:222
  44.0 1.5 %collective-permute-start.10 = (bf16[4,208,256]{2,1,0:T(8,128)(2,1)S(1)}, bf16[4,208,256]{2,1,0:T(8,128)(2,1)S(1)}, u32[]{:S(2)}, u32[]{:S(2)}) collective-permute-start(bf16[4,208,256]{2,1,0:T(8,128)(2,1)S(1)} %dynamic-slice_bitcast_fusion.2), channel_id=1, source_target_pairs={{0,2},{1,3},{2,0},{3,1},{4,6},{5,7},{6,4},{7,5},{8,10},{9,11},{10,... | collective-permute-start | bytes 1277960 | tf_op jit(solution)/shard_map/ppermute | solution.py:212
  45.5 0.0 collective-permute-done.5
  45.5 0.0 copy-done.5
  45.5 1.4 %fusion.1 = bf16[8,208,256]{2,1,0:T(8,128)(2,1)S(1)} fusion(bf16[8,208,256]{2,1,0:T(8,128)(2,1)} %collective-permute-done.5, bf16[8,2,208,256]{3,2,1,0:T(8,128)(2,1)S(1)} %bitcast.57, s32[]{:T(128)S(6)} %select_n.126), kind=kLoop, calls=%fused_computation.3 | loop fusion | flops 1703936 | bytes 2555908 | tf_op jit(solution)/shard_map/convert_element_type | solution.py:222
  46.9 0.8 dynamic-slice_bitcast_fusion.3
  47.7 0.6 collective-permute-start.6
  48.2 8.5 %collective-permute-done.10 = bf16[4,208,256]{2,1,0:T(8,128)(2,1)S(1)} collective-permute-done((bf16[4,208,256]{2,1,0:T(8,128)(2,1)S(1)}, bf16[4,208,256]{2,1,0:T(8,128)(2,1)S(1)}, u32[]{:S(2)}, u32[]{:S(2)}) %collective-permute-start.10) | collective-permute-done | bytes 426016 | tf_op jit(solution)/shard_map/ppermute | solution.py:212
  56.7 0.1 fusion.2
  56.9 0.0 copy-start.6
  56.9 1.5 %collective-permute-start.11 = (bf16[2,208,256]{2,1,0:T(8,128)(2,1)S(1)}, bf16[2,208,256]{2,1,0:T(8,128)(2,1)S(1)}, u32[]{:S(2)}, u32[]{:S(2)}) collective-permute-start(bf16[2,208,256]{2,1,0:T(8,128)(2,1)S(1)} %dynamic-slice_bitcast_fusion.4), channel_id=1, source_target_pairs={{0,4},{1,5},{2,6},{3,7},{4,0},{5,1},{6,2},{7,3},{8,12},{9,13},{10,... | collective-permute-start | bytes 638984 | tf_op jit(solution)/shard_map/ppermute | solution.py:212
  58.4 6.3 %collective-permute-done.6 = bf16[4,208,256]{2,1,0:T(8,128)(2,1)} collective-permute-done((bf16[4,208,256]{2,1,0:T(8,128)(2,1)}, bf16[4,208,256]{2,1,0:T(8,128)(2,1)}, u32[]{:S(2)}, u32[]{:S(2)}) %collective-permute-start.6) | collective-permute-done | bytes 426016 | tf_op jit(solution)/shard_map/ppermute | solution.py:212
  64.8 1.1 %fusion.3 = bf16[4,208,256]{2,1,0:T(8,128)(2,1)S(1)} fusion(bf16[4,208,256]{2,1,0:T(8,128)(2,1)} %collective-permute-done.6, bf16[4,2,208,256]{3,2,1,0:T(8,128)(2,1)S(1)} %bitcast.61, s32[]{:T(128)S(6)} %select_n.128), kind=kLoop, calls=%fused_computation.7 | loop fusion | flops 851968 | bytes 1277956 | tf_op jit(solution)/shard_map/convert_element_type | solution.py:222
  65.9 1.5 %collective-permute-start.7 = (bf16[2,208,256]{2,1,0:T(8,128)(2,1)S(1)}, bf16[2,208,256]{2,1,0:T(8,128)(2,1)S(1)}, u32[]{:S(2)}, u32[]{:S(2)}) collective-permute-start(bf16[2,208,256]{2,1,0:T(8,128)(2,1)S(1)} %dynamic-slice_bitcast_fusion.5), channel_id=1, source_target_pairs={{0,4},{1,5},{2,6},{3,7},{4,0},{5,1},{6,2},{7,3},{8,12},{9,13},{10,... | collective-permute-start | bytes 638984 | tf_op jit(solution)/shard_map/ppermute | solution.py:212
  67.4 0.0 collective-permute-done.11
  67.4 0.1 fusion.4
  67.5 2.7 %collective-permute-start.12 = (bf16[1,208,256]{2,1,0:T(8,128)(2,1)S(1)}, bf16[1,208,256]{2,1,0:T(8,128)(2,1)S(1)}, u32[]{:S(2)}, u32[]{:S(2)}) collective-permute-start(bf16[1,208,256]{2,1,0:T(8,128)(2,1)S(1)} %constant_dynamic-slice_fusion), channel_id=1, source_target_pairs={{0,8},{1,9},{2,10},{3,11},{4,12},{5,13},{6,14},{7,15},{8,0},{9,1},... | collective-permute-start | bytes 319496 | tf_op jit(solution)/shard_map/ppermute | solution.py:212
  70.2 4.1 %collective-permute-done.7 = bf16[2,208,256]{2,1,0:T(8,128)(2,1)S(1)} collective-permute-done((bf16[2,208,256]{2,1,0:T(8,128)(2,1)S(1)}, bf16[2,208,256]{2,1,0:T(8,128)(2,1)S(1)}, u32[]{:S(2)}, u32[]{:S(2)}) %collective-permute-start.7) | collective-permute-done | bytes 213024 | tf_op jit(solution)/shard_map/ppermute | solution.py:212
  74.3 0.1 fusion.5
  74.4 1.7 %collective-permute-start.8 = (bf16[1,208,256]{2,1,0:T(8,128)(2,1)S(1)}, bf16[1,208,256]{2,1,0:T(8,128)(2,1)S(1)}, u32[]{:S(2)}, u32[]{:S(2)}) collective-permute-start(bf16[1,208,256]{2,1,0:T(8,128)(2,1)S(1)} %constant_dynamic-slice_fusion.1), channel_id=1, source_target_pairs={{0,8},{1,9},{2,10},{3,11},{4,12},{5,13},{6,14},{7,15},{8,0},{9,1},... | collective-permute-start | bytes 319496 | tf_op jit(solution)/shard_map/ppermute | solution.py:212
  76.1 0.0 collective-permute-done.12
  76.1 5.1 %collective-permute-done.8 = bf16[1,208,256]{2,1,0:T(8,128)(2,1)S(1)} collective-permute-done((bf16[1,208,256]{2,1,0:T(8,128)(2,1)S(1)}, bf16[1,208,256]{2,1,0:T(8,128)(2,1)S(1)}, u32[]{:S(2)}, u32[]{:S(2)}) %collective-permute-start.8) | collective-permute-done | bytes 106528 | tf_op jit(solution)/shard_map/ppermute | solution.py:212
  81.2 0.1 fusion.13
  81.3 1.6 %collective-permute-start.13 = (bf16[208,256]{1,0:T(8,128)(2,1)S(1)}, bf16[208,256]{1,0:T(8,128)(2,1)S(1)}, u32[]{:S(2)}, u32[]{:S(2)}) collective-permute-start(bf16[208,256]{1,0:T(8,128)(2,1)S(1)} %fusion.13), channel_id=1, source_target_pairs={{0,16},{16,0},{1,17},{17,1},{2,18},{18,2},{3,19},{19,3},{4,20},{20... | collective-permute-start | bytes 319496 | tf_op jit(solution)/shard_map/ppermute | solution.py:317
  82.8 0.0 copy-done.8
  82.8 2.1 %shard_map.70 = bf16[4,2,128,1024]{3,2,1,0:T(8,128)(2,1)} custom-call(bf16[2,512,256]{2,1,0:T(8,128)(2,1)S(1)} %copy-done.8, bf16[2,1024,256]{2,1,0:T(8,128)(2,1)S(1)} %copy-done.6), custom_call_target="tpu_custom_call" | custom-call | flops 536870912 | bytes 3670016 | tf_op jit(solution)/shard_map/pallas_call | solution.py:194
  84.9 1.1 %collective-permute-done.13 = bf16[208,256]{1,0:T(8,128)(2,1)S(1)} collective-permute-done((bf16[208,256]{1,0:T(8,128)(2,1)S(1)}, bf16[208,256]{1,0:T(8,128)(2,1)S(1)}, u32[]{:S(2)}, u32[]{:S(2)}) %collective-permute-start.13) | collective-permute-done | bytes 106528 | tf_op jit(solution)/shard_map/ppermute | solution.py:317
  86.0 0.8 fusion.6
  (14 shorter events, 0.2 us)
Async XLA Ops:
  0.6 2.9 %copy-start.1 = (bf16[4,16,32,256]{3,2,1,0:T(8,128)(2,1)S(1)}, bf16[4,16,32,256]{3,2,1,0:T(8,128)(2,1)}, u32[]{:S(2)}) copy-start(bf16[4,16,32,256]{3,2,1,0:T(8,128)(2,1)} %cot.1) | copy-start | bytes 3145732
  3.6 12.1 %copy-start.10 = (bf16[4,2,8,16,256]{4,3,2,1,0:T(8,128)(2,1)S(1)}, bf16[4,2,8,16,256]{4,3,2,1,0:T(8,128)(2,1)}, u32[]{:S(2)}) copy-start(bf16[4,2,8,16,256]{4,3,2,1,0:T(8,128)(2,1)} %saved.1) | copy-start | bytes 1572868
  4.9 10.8 %collective-permute-start = (bf16[4,2,32,256]{3,2,1,0:T(8,128)(2,1)S(1)}, bf16[4,2,32,256]{3,2,1,0:T(8,128)(2,1)S(1)}, u32[]{:S(2)}, u32[]{:S(2)}) collective-permute-start(bf16[4,2,32,256]{3,2,1,0:T(8,128)(2,1)S(1)} %maximum_select_fusion), channel_id=1, source_target_pairs={{0,8},{1,9},{3,11},{2,10},{6,14},{7,15},{5,13},{4,12},{8,0},{9,1},... | collective-permute-start | bytes 393224 | tf_op jit(solution)/shard_map/ppermute | solution.py:250
  9.2 6.5 %collective-permute-start.1 = (bf16[4,16,4,256]{3,2,1,0:T(4,128)(2,1)S(1)}, bf16[4,16,4,256]{3,2,1,0:T(4,128)(2,1)S(1)}, u32[]{:S(2)}, u32[]{:S(2)}) collective-permute-start(bf16[4,16,4,256]{3,2,1,0:T(4,128)(2,1)S(1)} %get-tuple-element.15), channel_id=1, source_target_pairs={{0,1},{1,0},{3,2},{2,3},{6,7},{7,6},{5,4},{4,5},{8,9},{9,8},{11,10... | collective-permute-start | bytes 393224 | tf_op jit(solution)/shard_map/ppermute | solution.py:250
  9.3 6.4 %collective-permute-start.2 = (bf16[4,16,4,256]{3,2,1,0:T(4,128)(2,1)S(1)}, bf16[4,16,4,256]{3,2,1,0:T(4,128)(2,1)S(1)}, u32[]{:S(2)}, u32[]{:S(2)}) collective-permute-start(bf16[4,16,4,256]{3,2,1,0:T(4,128)(2,1)S(1)} %get-tuple-element.14), channel_id=1, source_target_pairs={{1,3},{3,1},{2,6},{6,2},{7,5},{5,7},{9,11},{11,9},{10,14},{14,10},... | collective-permute-start | bytes 393224 | tf_op jit(solution)/shard_map/ppermute | solution.py:250
  10.0 4.9 %collective-permute-start.3 = (bf16[4,2,4,256]{3,2,1,0:T(4,128)(2,1)S(1)}, bf16[4,2,4,256]{3,2,1,0:T(4,128)(2,1)S(1)}, u32[]{:S(2)}, u32[]{:S(2)}) collective-permute-start(bf16[4,2,4,256]{3,2,1,0:T(4,128)(2,1)S(1)} %get-tuple-element.19), channel_id=1, source_target_pairs={{0,9},{1,8},{3,10},{2,11},{6,15},{7,14},{5,12},{4,13},{8,1},{9,0},... | collective-permute-start | bytes 49160 | tf_op jit(solution)/shard_map/ppermute | solution.py:250
  13.0 1.9 %collective-permute-start.4 = (bf16[4,2,4,256]{3,2,1,0:T(4,128)(2,1)S(1)}, bf16[4,2,4,256]{3,2,1,0:T(4,128)(2,1)S(1)}, u32[]{:S(2)}, u32[]{:S(2)}) collective-permute-start(bf16[4,2,4,256]{3,2,1,0:T(4,128)(2,1)S(1)} %get-tuple-element.18), channel_id=1, source_target_pairs={{1,11},{3,9},{2,14},{6,10},{7,13},{5,15},{9,3},{11,1},{10,6},{14,2... | collective-permute-start | bytes 49160 | tf_op jit(solution)/shard_map/ppermute | solution.py:250
  21.0 1.2 %copy-start.2 = (bf16[3328,256]{1,0:T(8,128)(2,1)}, bf16[3328,256]{1,0:T(8,128)(2,1)S(1)}, u32[]{:S(2)}) copy-start(bf16[3328,256]{1,0:T(8,128)(2,1)S(1)} %get-tuple-element.11) | copy-start | bytes 5111812
  22.3 0.8 copy-start.9
  23.1 16.4 %copy-start = (bf16[4,2,128,1024]{3,2,1,0:T(8,128)(2,1)S(1)}, bf16[4,2,128,1024]{3,2,1,0:T(8,128)(2,1)}, u32[]{:S(2)}) copy-start(bf16[4,2,128,1024]{3,2,1,0:T(8,128)(2,1)} %feats.1) | copy-start | bytes 6291460
  23.1 16.4 %all-to-all-start = ((bf16[8,4,2,16,256]{4,3,2,1,0:T(8,128)(2,1)}), bf16[8,4,2,16,256]{4,3,2,1,0:T(8,128)(2,1)S(1)}, u32[]{:S(2)}, u32[]{:S(2)}) async-start(bf16[8,4,2,16,256]{4,3,2,1,0:T(8,128)(2,1)} %copy-done.9), calls=%async_computation | async-start | bytes 1048576 | tf_op jit(solution)/shard_map/all_to_all | solution.py:297
  32.7 8.9 %collective-permute-start.9 = (bf16[8,208,256]{2,1,0:T(8,128)(2,1)}, bf16[8,208,256]{2,1,0:T(8,128)(2,1)}, u32[]{:S(2)}, u32[]{:S(2)}) collective-permute-start(bf16[8,208,256]{2,1,0:T(8,128)(2,1)} %dynamic-slice_bitcast_fusion), channel_id=1, source_target_pairs={{0,1},{1,0},{2,3},{3,2},{4,5},{5,4},{6,7},{7,6},{8,9},{9,8},{10,11... | collective-permute-start | bytes 2555912 | tf_op jit(solution)/shard_map/ppermute | solution.py:212
  40.3 1.2 %copy-start.4 = (bf16[3328,256]{1,0:T(8,128)(2,1)}, bf16[3328,256]{1,0:T(8,128)(2,1)S(1)}, u32[]{:S(2)}) copy-start(bf16[3328,256]{1,0:T(8,128)(2,1)S(1)} %get-tuple-element.10) | copy-start | bytes 5111812
  40.3 1.4 %copy-start.7 = (bf16[2,512,256]{2,1,0:T(8,128)(2,1)}, bf16[2,512,256]{2,1,0:T(8,128)(2,1)S(1)}, u32[]{:S(2)}) copy-start(bf16[2,512,256]{2,1,0:T(8,128)(2,1)S(1)} %get-tuple-element.9.tokens) | copy-start | bytes 1572868
  40.3 2.3 %copy-start.3 = (bf16[3328,256]{1,0:T(8,128)(2,1)S(1)}, bf16[3328,256]{1,0:T(8,128)(2,1)}, u32[]{:S(2)}) copy-start(bf16[3328,256]{1,0:T(8,128)(2,1)} %copy-done.2) | copy-start | bytes 5111812
  41.6 3.8 %collective-permute-start.5 = (bf16[8,208,256]{2,1,0:T(8,128)(2,1)S(1)}, bf16[8,208,256]{2,1,0:T(8,128)(2,1)}, u32[]{:S(2)}, u32[]{:S(2)}) collective-permute-start(bf16[8,208,256]{2,1,0:T(8,128)(2,1)S(1)} %dynamic-slice_bitcast_fusion.1), channel_id=1, source_target_pairs={{0,1},{1,0},{2,3},{3,2},{4,5},{5,4},{6,7},{7,6},{8,9},{9,8},{10,11... | collective-permute-start | bytes 2555912 | tf_op jit(solution)/shard_map/ppermute | solution.py:212
  41.6 3.8 %copy-start.5 = (bf16[3328,256]{1,0:T(8,128)(2,1)S(1)}, bf16[3328,256]{1,0:T(8,128)(2,1)}, u32[]{:S(2)}) copy-start(bf16[3328,256]{1,0:T(8,128)(2,1)} %copy-done.4) | copy-start | bytes 5111812
  44.0 12.8 %collective-permute-start.10 = (bf16[4,208,256]{2,1,0:T(8,128)(2,1)S(1)}, bf16[4,208,256]{2,1,0:T(8,128)(2,1)S(1)}, u32[]{:S(2)}, u32[]{:S(2)}) collective-permute-start(bf16[4,208,256]{2,1,0:T(8,128)(2,1)S(1)} %dynamic-slice_bitcast_fusion.2), channel_id=1, source_target_pairs={{0,2},{1,3},{2,0},{3,1},{4,6},{5,7},{6,4},{7,5},{8,10},{9,11},{10,... | collective-permute-start | bytes 1277960 | tf_op jit(solution)/shard_map/ppermute | solution.py:212
  47.7 17.1 %collective-permute-start.6 = (bf16[4,208,256]{2,1,0:T(8,128)(2,1)}, bf16[4,208,256]{2,1,0:T(8,128)(2,1)}, u32[]{:S(2)}, u32[]{:S(2)}) collective-permute-start(bf16[4,208,256]{2,1,0:T(8,128)(2,1)} %dynamic-slice_bitcast_fusion.3), channel_id=1, source_target_pairs={{0,2},{1,3},{2,0},{3,1},{4,6},{5,7},{6,4},{7,5},{8,10},{9,11},{10,... | collective-permute-start | bytes 1277960 | tf_op jit(solution)/shard_map/ppermute | solution.py:212
  56.9 25.9 %copy-start.6 = (bf16[2,1024,256]{2,1,0:T(8,128)(2,1)S(1)}, bf16[2,1024,256]{2,1,0:T(8,128)(2,1)}, u32[]{:S(2)}) copy-start(bf16[2,1024,256]{2,1,0:T(8,128)(2,1)} %weight.3) | copy-start | bytes 3145732
  56.9 25.9 %copy-start.8 = (bf16[2,512,256]{2,1,0:T(8,128)(2,1)S(1)}, bf16[2,512,256]{2,1,0:T(8,128)(2,1)}, u32[]{:S(2)}) copy-start(bf16[2,512,256]{2,1,0:T(8,128)(2,1)} %copy-done.7) | copy-start | bytes 1572868
  56.9 10.5 %collective-permute-start.11 = (bf16[2,208,256]{2,1,0:T(8,128)(2,1)S(1)}, bf16[2,208,256]{2,1,0:T(8,128)(2,1)S(1)}, u32[]{:S(2)}, u32[]{:S(2)}) collective-permute-start(bf16[2,208,256]{2,1,0:T(8,128)(2,1)S(1)} %dynamic-slice_bitcast_fusion.4), channel_id=1, source_target_pairs={{0,4},{1,5},{2,6},{3,7},{4,0},{5,1},{6,2},{7,3},{8,12},{9,13},{10,... | collective-permute-start | bytes 638984 | tf_op jit(solution)/shard_map/ppermute | solution.py:212
  65.9 8.4 %collective-permute-start.7 = (bf16[2,208,256]{2,1,0:T(8,128)(2,1)S(1)}, bf16[2,208,256]{2,1,0:T(8,128)(2,1)S(1)}, u32[]{:S(2)}, u32[]{:S(2)}) collective-permute-start(bf16[2,208,256]{2,1,0:T(8,128)(2,1)S(1)} %dynamic-slice_bitcast_fusion.5), channel_id=1, source_target_pairs={{0,4},{1,5},{2,6},{3,7},{4,0},{5,1},{6,2},{7,3},{8,12},{9,13},{10,... | collective-permute-start | bytes 638984 | tf_op jit(solution)/shard_map/ppermute | solution.py:212
  67.5 8.6 %collective-permute-start.12 = (bf16[1,208,256]{2,1,0:T(8,128)(2,1)S(1)}, bf16[1,208,256]{2,1,0:T(8,128)(2,1)S(1)}, u32[]{:S(2)}, u32[]{:S(2)}) collective-permute-start(bf16[1,208,256]{2,1,0:T(8,128)(2,1)S(1)} %constant_dynamic-slice_fusion), channel_id=1, source_target_pairs={{0,8},{1,9},{2,10},{3,11},{4,12},{5,13},{6,14},{7,15},{8,0},{9,1},... | collective-permute-start | bytes 319496 | tf_op jit(solution)/shard_map/ppermute | solution.py:212
  74.4 6.8 %collective-permute-start.8 = (bf16[1,208,256]{2,1,0:T(8,128)(2,1)S(1)}, bf16[1,208,256]{2,1,0:T(8,128)(2,1)S(1)}, u32[]{:S(2)}, u32[]{:S(2)}) collective-permute-start(bf16[1,208,256]{2,1,0:T(8,128)(2,1)S(1)} %constant_dynamic-slice_fusion.1), channel_id=1, source_target_pairs={{0,8},{1,9},{2,10},{3,11},{4,12},{5,13},{6,14},{7,15},{8,0},{9,1},... | collective-permute-start | bytes 319496 | tf_op jit(solution)/shard_map/ppermute | solution.py:212
  81.3 4.8 %collective-permute-start.13 = (bf16[208,256]{1,0:T(8,128)(2,1)S(1)}, bf16[208,256]{1,0:T(8,128)(2,1)S(1)}, u32[]{:S(2)}, u32[]{:S(2)}) collective-permute-start(bf16[208,256]{1,0:T(8,128)(2,1)S(1)} %fusion.13), channel_id=1, source_target_pairs={{0,16},{16,0},{1,17},{17,1},{2,18},{18,2},{3,19},{19,3},{4,20},{20... | collective-permute-start | bytes 319496 | tf_op jit(solution)/shard_map/ppermute | solution.py:317

commit v2 on v1

--- a/solution.py
+++ b/solution.py
@@ -37,9 +37,11 @@
 
 
 def pool_conv_kernel(
-    has_second, flags, cot, row_a, row_b, col_a, col_b, aa, ab, ba, bb, weight, saved, ig, early, late,
-    rows_ref, cells_ref, patch_ref, acc_ref,
+    has_second, flags, cot, row_a, row_b, col_a, col_b, aa, ab, ba, bb, weight, saved,
+    *outs_and_scratch,
 ):
+    igs, (split_refs, late) = outs_and_scratch[:TILE_COLS], (outs_and_scratch[TILE_COLS:-6], outs_and_scratch[-6])
+    rows_ref, cells_ref, patch_ref, acc_ref, full_ref = outs_and_scratch[-5:]
     images, height2, width2, channels = cot.shape
     height, width = height2 // 2, width2 // 2
     depths = weight.shape[0]
@@ -130,6 +132,7 @@
 
     rows_ref[...] = jnp.zeros_like(rows_ref)
     lax.fori_loop(0, images, per_image, 0)
+    gray = flags[6]
     for k in range(depths):
         for n in range(9):
             part = lax.dot_general(
@@ -143,9 +146,9 @@
             else:
                 acc_ref[...] += part
         for i in range(images):
-            for h in range(height):
-                at = (i * height + h) * width
-                ig[h, i, k] = acc_ref[at : at + width, :].astype(BF16)
+            for apart in range(height):
+                at = pl.multiple_of((i * height + (gray ^ apart)) * width, width)
+                igs[apart][i, k] = acc_ref[pl.ds(at, width), :].astype(BF16)
     split = late.shape[0]
     for k in range(depths):
         flat = saved[:, k].reshape(images * height * width, channels)
@@ -158,24 +161,65 @@
             if at < split:
                 late[at : at + channels, :] = part
             else:
-                early[at - split : at - split + channels, :] = part
-
-
-def proj_term_kernel(came, feats, conv_late, out, tokens):
-    groups, images, depths, width, channels = came.shape
-    for k in range(depths):
-        for i in range(images):
-            for c in range(groups):
-                at = (i * groups + c) * width
-                tokens[k, at : at + width, :] = came[gray_of(c), i, k]
+                full_ref[at - split : at - split + channels, :] = part
+    deal(full_ref, split_refs, flags[7])
+
+
+def deal(full_ref, split_refs, mine):
+    if len(split_refs) == 1:
+        split_refs[0][...] = full_ref[...]
+        return
+    kept, sent = split_refs
+    count, rows = kept.shape[:2]
+    for j in range(count):
+        kept[j] = full_ref[pl.ds(pl.multiple_of((2 * j + mine) * rows, 16), rows), :]
+        sent[j] = full_ref[pl.ds(pl.multiple_of((2 * j + 1 - mine) * rows, 16), rows), :]
+
+
+def pack_kernel(has_second, flags, cot, *outs):
+    width2 = cot.shape[2]
+    row_odd, col_odd = flags[0] == 1, flags[1] == 1
+
+    def line(r):
+        return cot[:, r].astype(F32)
+
+    end = cot.shape[1] - 1
+    below = [0.25 * line(end - 2) + 0.75 * (line(end - 1) + line(end)), line(end)]
+    above = [line(0), 0.75 * (line(0) + line(1)) + 0.25 * line(2)]
+    for second in range(2 if has_second else 1):
+        flip = second == 1
+        for n in range(2):
+            value = jnp.where(row_odd, below[n], above[n]) if flip else jnp.where(row_odd, above[n], below[n])
+            low, high = value[:, :HALO], value[:, width2 - HALO :]
+            outs[3 * second][:, n] = value.astype(BF16)
+            outs[3 * second + 1][:, n] = jnp.where(col_odd, low, high).astype(BF16)
+            outs[3 * second + 2][:, n] = jnp.where(col_odd, high, low).astype(BF16)
+    low, high = cot[:, :, :HALO].astype(F32), cot[:, :, width2 - HALO :].astype(F32)
+    outs[-2][...] = jnp.where(col_odd, low, high).astype(BF16)
+    outs[-1][...] = jnp.where(col_odd, high, low).astype(BF16)
+
+
+def proj_term_kernel(flags, *refs):
+    came, (feats, conv_late) = refs[:TILE_COLS], refs[TILE_COLS : TILE_COLS + 2]
+    split_refs, tokens, full_ref = refs[TILE_COLS + 2 : -2], refs[-2], refs[-1]
+    images, depths, width, channels = came[0].shape
+    gray = flags[6]
+    for apart in range(TILE_COLS):
+        sender = gray ^ apart
+        column = sender ^ sender >> 1 ^ sender >> 2
+        for k in range(depths):
+            for i in range(images):
+                at = pl.multiple_of((i * TILE_COLS + column) * width, width)
+                tokens[k, pl.ds(at, width), :] = came[apart][i, k]
     dim = feats.shape[3]
     for k in range(depths):
         flat = feats[:, k].reshape(images * feats.shape[2], dim)
         part = lax.dot_general(
             flat, tokens[k], (((0,), (0,)), ((), ())), preferred_element_type=F32
         )
-        out[k * dim : (k + 1) * dim, :] = part.astype(BF16)
-    out[depths * dim :, :] = conv_late[...]
+        full_ref[k * dim : (k + 1) * dim, :] = part.astype(BF16)
+    full_ref[depths * dim :, :] = conv_late[...]
+    deal(full_ref, split_refs, flags[7])
 
 
 def feat_grad_kernel(tokens, weight, out):
@@ -187,7 +231,50 @@
         out[:, k] = part.astype(BF16).reshape(images, count, dim)
 
 
-def vmem_call(kernel, out_shape, operands, scratch=(), scalars=0, flops=0, limit=48):
+def round_kernel(parts, bits_at, bits, by_columns, flags, *refs):
+    ins, outs = refs[:parts], refs[parts:]
+    span = 1 << bits
+    mine, dp = 0, flags[8]
+    for b in range(bits):
+        mine = mine + flags[9 + bits_at + b] * (1 << b)
+    count = outs[0].shape[0]
+    width = outs[0].shape[2]
+    for n, out in enumerate(outs):
+        across, apart = n // span, n % span
+        for q in range(count):
+            block = q * span + (mine ^ apart)
+            if by_columns:
+                columns = pl.ds(pl.multiple_of((dp ^ across) * width, width), width)
+            else:
+                columns = slice(None)
+            total = ins[0][block, :, columns].astype(F32)
+            for other in ins[1:]:
+                total = total + other[block, :, columns].astype(F32)
+            out[q] = total.astype(out.dtype)
+
+
+def last_kernel(parts, flags, *refs):
+    early, late, (sent, kept) = refs[:parts], refs[parts : 2 * parts], refs[2 * parts :]
+    first = flags[8] == 0
+    sums = []
+    for group in (early, late):
+        total = group[0][0].astype(F32)
+        for other in group[1:]:
+            total = total + other[0].astype(F32)
+        sums.append(total)
+    sent[...] = jnp.where(first, sums[0], sums[1]).astype(BF16)
+    kept[...] = jnp.where(first, sums[1], sums[0])
+
+
+def join_kernel(scale, flags, kept, came, out):
+    width = kept.shape[1]
+    at = pl.multiple_of(flags[8] * width, width)
+    out[:, pl.ds(at, width)] = kept[...] * scale
+    at = pl.multiple_of((1 - flags[8]) * width, width)
+    out[:, pl.ds(at, width)] = came[...].astype(F32) * scale
+
+
+def vmem_call(kernel, out_shape, operands, scratch=(), scalars=1, flops=0, limit=16):
     whole = pl.BlockSpec(memory_space=pltpu.VMEM)
     moved = sum(a.size * a.dtype.itemsize for a in operands)
     moved += sum(math.prod(s.shape) * s.dtype.itemsize for s in jax.tree.leaves(out_shape))
@@ -202,25 +289,50 @@
     )(*operands)
 
 
-def halved(block, index, bit):
-    count = lax.axis_size("tile")
-    rows, channels = block.shape[1:]
-    pairs = block.reshape(block.shape[0] // 2, 2, rows, channels)
-    mine = index >> bit & 1
-    sent = lax.dynamic_index_in_dim(pairs, 1 - mine, 1, keepdims=False)
-    kept = lax.dynamic_index_in_dim(pairs, mine, 1, keepdims=False)
-    came = lax.ppermute(sent, "tile", [(t, t ^ 1 << bit) for t in range(count)])
-    return kept.astype(F32) + came.astype(F32)
-
-
-def scatter_sum(terms, index):
-    count = lax.axis_size("tile")
-    block = terms.reshape(count, terms.shape[0] // count, terms.shape[1])
-    bits = count.bit_length() - 1
-    for bit in range(bits):
-        total = halved(block, index, bit)
-        block = total.astype(BF16)
-    return total[0]
+def sds(*shape, dtype=BF16):
+    return jax.ShapeDtypeStruct(shape, dtype)
+
+
+def xor_move(block, apart, across):
+    tiles = lax.axis_size("tile")
+    if not across:
+        return lax.ppermute(block, "tile", [(t, t ^ apart) for t in range(tiles)])
+    if not apart:
+        return lax.ppermute(block, "dp", [(0, 1), (1, 0)])
+    route = [(d * tiles + t, (1 - d) * tiles + (t ^ apart)) for d in range(2) for t in range(tiles)]
+    return lax.ppermute(block, ("dp", "tile"), route)
+
+
+def scatter_sum(dealt, flags, core):
+    tiles = lax.axis_size("tile")
+    if len(dealt) == 1:
+        pairs = dealt[0].reshape(tiles // 2, 2, dealt[0].shape[0] // tiles, dealt[0].shape[1])
+        kept = lax.dynamic_index_in_dim(pairs, core, 1, keepdims=False)
+        sent = lax.dynamic_index_in_dim(pairs, 1 - core, 1, keepdims=False)
+    else:
+        kept, sent = dealt
+    parts = [kept, xor_move(sent, 1, False)]
+    total_bits = tiles.bit_length() - 1
+    at = 1
+    while at < total_bits:
+        by_columns = at == 1
+        bits = 1 if by_columns else min(2, total_bits - at)
+        span = 1 << bits
+        count, rows, channels = parts[0].shape
+        if by_columns:
+            channels //= 2
+        outs = [
+            sds(count // span, rows, channels, dtype=F32 if n == 0 else BF16)
+            for n in range(span * (2 if by_columns else 1))
+        ]
+        pieces = vmem_call(
+            functools.partial(round_kernel, len(parts), at, bits, by_columns), outs, [flags] + parts
+        )
+        parts = [pieces[0]] + [
+            xor_move(pieces[n], (n % span) << at, n >= span) for n in range(1, len(pieces))
+        ]
+        at += bits
+    return parts
 
 
 def per_device(features, proj_weight, conv_weight, saved, cotangent):
@@ -234,89 +346,88 @@
     depths, dim = proj_weight.shape[:2]
     height, width = height2 // 2, width2 // 2
     patches = images * height * width
-    row_odd, col_odd = row % 2 == 1, col % 2 == 1
-
-    cot = cotangent
-    wide = cot.astype(F32)
-    to_below = jnp.stack(
-        [0.25 * wide[:, -3] + 0.75 * (wide[:, -2] + wide[:, -1]), wide[:, -1]], axis=1
-    ).astype(BF16)
-    to_above = jnp.stack(
-        [wide[:, 0], 0.75 * (wide[:, 0] + wide[:, 1]) + 0.25 * wide[:, 2]], axis=1
-    ).astype(BF16)
     has_second = rows > 2
+    bits = tile_count.bit_length() - 1
+    flags = jnp.stack(
+        [row % 2, col % 2, row == 0, row == rows - 1, col == 0, col == TILE_COLS - 1, gray, position % 2]
+        + [lax.axis_index("dp")]
+        + [position >> b & 1 for b in range(bits)]
+    ).astype(jnp.int32)
 
     def swap(block, row_pairs, col_pairs):
         return lax.ppermute(block, "tile", tile_route(row_pairs, col_pairs, rows))
 
     row_first, row_second = paired(rows, 0), paired(rows, 1)
     col_first, col_second = paired(TILE_COLS, 0), paired(TILE_COLS, 1)
-    row_out = jnp.where(row_odd, to_above, to_below)
-    row_a = swap(row_out, row_first, None)
-
-    def edge(block, odd):
-        return jnp.where(odd, block[:, :, :HALO], block[:, :, width2 - HALO :])
-
-    col_b = swap(edge(cot, jnp.logical_not(col_odd)), None, col_second)
-    col_a = swap(edge(cot, col_odd), None, col_first)
-    ab = swap(edge(row_out, jnp.logical_not(col_odd)), row_first, col_second)
-    aa = swap(edge(row_out, col_odd), row_first, col_first)
+    strip = [sds(images, 2, width2, channels)] + [sds(images, 2, HALO, channels)] * 2
+    edges = vmem_call(
+        functools.partial(pack_kernel, has_second),
+        strip * (2 if has_second else 1) + [sds(images, height2, HALO, channels)] * 2,
+        (flags, cotangent),
+    )
+    row_a = swap(edges[0], row_first, None)
+    col_b = swap(edges[-1], None, col_second)
+    col_a = swap(edges[-2], None, col_first)
+    ab = swap(edges[2], row_first, col_second)
+    aa = swap(edges[1], row_first, col_first)
     if has_second:
-        row_out = jnp.where(row_odd, to_below, to_above)
-        row_b = swap(row_out, row_second, None)
-        bb = swap(edge(row_out, jnp.logical_not(col_odd)), row_second, col_second)
-        ba = swap(edge(row_out, col_odd), row_second, col_first)
+        row_b = swap(edges[3], row_second, None)
+        bb = swap(edges[5], row_second, col_second)
+        ba = swap(edges[4], row_second, col_first)
     else:
         row_b, ba, bb = row_a, aa, ab
-    flags = jnp.stack(
-        [row % 2, col % 2, row == 0, row == rows - 1, col == 0, col == TILE_COLS - 1]
-    ).astype(jnp.int32)
-    head_rows = depths * (dim + 9 * channels)
-    conv_late = head_rows // 2 - depths * dim
-    conv_early = head_rows // 2
-    sds = jax.ShapeDtypeStruct
+    half_rows = depths * (dim + 9 * channels) // 2
+    conv_late = half_rows - depths * dim
+    block_rows = half_rows // tile_count
+    if block_rows % 16:
+        dealt = [sds(half_rows, channels)]
+    else:
+        dealt = [sds(tile_count // 2, block_rows, channels)] * 2
     conv_flops = 2 * patches * depths * 9 * channels * channels
-    ig, early, late = vmem_call(
+    outs = vmem_call(
         functools.partial(pool_conv_kernel, has_second),
-        (
-            sds((height, images, depths, width, channels), BF16),
-            sds((conv_early, channels), BF16),
-            sds((conv_late, channels), BF16),
-        ),
-        (flags, cot, row_a, row_b, col_a, col_b, aa, ab, ba, bb, conv_weight, saved),
+        [sds(images, depths, width, channels)] * height + dealt + [sds(conv_late, channels)],
+        (flags, cotangent, row_a, row_b, col_a, col_b, aa, ab, ba, bb, conv_weight, saved),
         scratch=(
             pltpu.VMEM((channels // 128, height + 2, LEFT + width2 + 16, 128), F32),
             pltpu.VMEM((height + 2, width + 8, channels), F32),
             pltpu.VMEM((patches, 9 * channels), BF16),
             pltpu.VMEM((patches, channels), F32),
+            pltpu.VMEM((half_rows, channels), BF16),
         ),
-        scalars=1,
         flops=2 * conv_flops,
     )
-    groups = [[g * TILE_COLS + t for t in range(TILE_COLS)] for g in range(rows)]
-    came = lax.all_to_all(ig, "tile", 0, 0, axis_index_groups=groups, tiled=True)
-    early_sum = scatter_sum(early, position)
+    igs, early, late = outs[:height], outs[height:-1], outs[-1]
+    came = [igs[0]] + [xor_move(igs[apart], apart, False) for apart in range(1, height)]
+    early_parts = scatter_sum(early, flags, position % 2)
     tokens = features.shape[2]
     proj_flops = 2 * images * tokens * depths * dim * channels
-    terms, token_grad = vmem_call(
+    *terms, token_grad = vmem_call(
         proj_term_kernel,
-        (sds((head_rows // 2, channels), BF16), sds((depths, images * tokens, channels), BF16)),
-        (came, features, late),
+        dealt + [sds(depths, images * tokens, channels)],
+        [flags] + came + [features, late],
+        scratch=(pltpu.VMEM((half_rows, channels), BF16),),
         flops=proj_flops,
     )
     feature_grad = vmem_call(
         feat_grad_kernel,
-        sds((images, depths, tokens, dim), BF16),
+        sds(images, depths, tokens, dim),
         (token_grad, proj_weight),
+        scalars=0,
         flops=proj_flops,
     )
-    late_sum = scatter_sum(terms, position)
-    first = lax.axis_index("dp") == 0
-    sent = jnp.where(first, early_sum, late_sum).astype(BF16)
-    kept = jnp.where(first, late_sum, early_sum)
-    other = lax.ppermute(sent, "dp", [(0, 1), (1, 0)])
+    late_parts = scatter_sum(terms, flags, position % 2)
+    half = sds(block_rows, channels // 2)
+    sent, kept = vmem_call(
+        functools.partial(last_kernel, len(early_parts)),
+        [half, sds(block_rows, channels // 2, dtype=F32)],
+        [flags] + early_parts + late_parts,
+    )
+    other = xor_move(sent, 0, True)
     scale = 1.0 / math.sqrt(images * lax.axis_size("dp") * tokens * tile_count)
-    head_grad = (kept + other.astype(F32)) * scale
+    head_grad = vmem_call(
+        functools.partial(join_kernel, scale), sds(block_rows, channels, dtype=F32), (flags, kept, other)
+    )
     return feature_grad, head_grad
 
 

time: 87.3 us -> 78.2 us (0.90)
  waiting for transfers between devices: 33.4 us -> 22.5 us
  starting transfers between devices: 27.6 us -> 37.3 us
  other arithmetic: 9.29 us -> 0 us
  Pallas kernels: 8.18 us -> 13.3 us
  local copies, waits for them, and re-layouts: 7.42 us -> 4.03 us
    ppermute x9 -> x22, starting transfers between devices: 11.6 us -> 28.8 us  [the longest x17 20.5 us: xor_move(): return lax.ppermute(block, 'tile', [(t, t ^ apart) for t in range(tiles)])]
    all_to_all x1 -> x0, starting transfers between devices: 7.55 us -> none  [per_device(): lax.all_to_all(ig, 'tile', 0, 0, axis_index_groups=groups, tiled=True)]
    convert_element_type x8 -> x0, other arithmetic: 7.01 us -> none  [the longest x6 4.07 us: scatter_sum(): block = total.astype(BF16)]
    all_to_all x1 -> x0, waiting for transfers between devices: 6.21 us -> none  [per_device(): lax.all_to_all(ig, 'tile', 0, 0, axis_index_groups=groups, tiled=True)]
    pallas_call x3 -> x10, Pallas kernels: 8.18 us -> 13.3 us  [vmem_call(): pl.pallas_call(kernel, out_shape=out_shape, in_specs=[pl.BlockSpec(memory...]
    ppermute x9 -> x22, waiting for transfers between devices: 25.2 us -> 20.3 us  [the longest x17 13.5 us: xor_move(): return lax.ppermute(block, 'tile', [(t, t ^ apart) for t in range(tiles)])]
    squeeze x8 -> x0, local copies, waits for them, and re-layouts: 3.1 us -> none  [halved(): sent = lax.dynamic_index_in_dim(pairs, 1 - mine, 1, keepdims=False)]
    another operation x1 -> x0, other arithmetic: 1.32 us -> none
  transfers between devices with their start and end apart: 15 -> 27, of which waited for: 8 -> 14; matrix products, arithmetic and copies ran while one was open for 9% -> 0% of each run, Pallas kernels for 3% -> 8%
where the time goes in v2:
time: 78.2 us; the launch traced here: 77.9 us
  starting transfers between devices  37.3 us (48%)
  waiting for transfers between devices  22.5 us (29%)
  Pallas kernels  13.3 us (17%)
  local copies, waits for them, and re-layouts  4.03 us (5%)
  between operations  0.8 us (1%)
    ppermute x17, starting transfers between devices, xor_move(): return lax.ppermute(block, 'tile', [(t, t ^ apart) for t in range(tiles)])  20.5 us
    ppermute x17, waiting for transfers between devices, xor_move(): return lax.ppermute(block, 'tile', [(t, t ^ apart) for t in range(tiles)])  13.5 us
    pallas_call x10, Pallas kernels, vmem_call(): pl.pallas_call(kernel, out_shape=out_shape, in_specs=[pl.BlockSpec(memory...  13.3 us
    ppermute x5, starting transfers between devices, swap(): return lax.ppermute(block, 'tile', tile_route(row_pairs, col_pairs, rows))  8.53 us
    ppermute x2, waiting for transfers between devices, xor_move(): return lax.ppermute(block, ('dp', 'tile'), route)  6.13 us
    ppermute x3, starting transfers between devices, xor_move(): return lax.ppermute(block, 'dp', [(0, 1), (1, 0)])  4.55 us
    unnamed x10, local copies, waits for them, and re-layouts  3.94 us
    ppermute x2, starting transfers between devices, xor_move(): return lax.ppermute(block, ('dp', 'tile'), route)  3.74 us
  transfers between devices with their start and end apart: 27, of which 14 were waited for; matrix products, arithmetic and copies ran while one was open for 0% of the time, Pallas kernels for 8%

profile of v2, /device:TPU:0, one launch (start us, length us, event | category | flops | bytes accessed | tf_op | source)
XLA Modules:
  0.0 77.9 jit_solution(11740407968243932116)
XLA Ops:
  0.7 0.1 stack.71.flags
  0.8 0.0 copy-start.2
  0.8 1.2 %copy-done.2 = bf16[4,16,32,256]{3,2,1,0:T(8,128)(2,1)S(1)} copy-done((bf16[4,16,32,256]{3,2,1,0:T(8,128)(2,1)S(1)}, bf16[4,16,32,256]{3,2,1,0:T(8,128)(2,1)}, u32[]{:S(2)}) %copy-start.2) | copy-done | bytes 1048600
  2.0 0.8 %shard_map.68 = (bf16[4,2,32,256]{3,2,1,0:T(8,128)(2,1)S(1)}, bf16[4,2,4,256]{3,2,1,0:T(4,128)(2,1)S(1)}, bf16[4,2,4,256]{3,2,1,0:T(4,128)(2,1)S(1)}, bf16[4,16,...) custom-call(s32[13]{0:T(128)S(1)} %stack.71.flags, bf16[4,16,32,256]{3,2,1,0:T(8,128)(2,1)S(1)} %copy-done.2), custom_call_target="tpu_custom_call" | custom-call | bytes 1474612 | tf_op jit(solution)/shard_map/pallas_call | solution.py:281
  2.8 4.1 %collective-permute-start = (bf16[4,2,32,256]{3,2,1,0:T(8,128)(2,1)S(1)}, bf16[4,2,32,256]{3,2,1,0:T(8,128)(2,1)S(1)}, u32[]{:S(2)}, u32[]{:S(2)}) collective-permute-start(bf16[4,2,32,256]{3,2,1,0:T(8,128)(2,1)S(1)} %get-tuple-element.39), channel_id=1, source_target_pairs={{0,8},{1,9},{3,11},{2,10},{6,14},{7,15},{5,13},{4,12},{8,0},{9,1},... | collective-permute-start | bytes 393224 | tf_op jit(solution)/shard_map/ppermute | solution.py:358
  6.9 0.0 collective-permute-start.1
  6.9 0.7 collective-permute-start.2
  7.6 3.0 %collective-permute-start.3 = (bf16[4,2,4,256]{3,2,1,0:T(4,128)(2,1)S(1)}, bf16[4,2,4,256]{3,2,1,0:T(4,128)(2,1)S(1)}, u32[]{:S(2)}, u32[]{:S(2)}) collective-permute-start(bf16[4,2,4,256]{3,2,1,0:T(4,128)(2,1)S(1)} %get-tuple-element.42), channel_id=1, source_target_pairs={{0,9},{1,8},{3,10},{2,11},{6,15},{7,14},{5,12},{4,13},{8,1},{9,0},... | collective-permute-start | bytes 49160 | tf_op jit(solution)/shard_map/ppermute | solution.py:358
  10.6 0.8 %collective-permute-start.4 = (bf16[4,2,4,256]{3,2,1,0:T(4,128)(2,1)S(1)}, bf16[4,2,4,256]{3,2,1,0:T(4,128)(2,1)S(1)}, u32[]{:S(2)}, u32[]{:S(2)}) collective-permute-start(bf16[4,2,4,256]{3,2,1,0:T(4,128)(2,1)S(1)} %get-tuple-element.43), channel_id=1, source_target_pairs={{1,11},{3,9},{2,14},{6,10},{7,13},{5,15},{9,3},{11,1},{10,6},{14,2... | collective-permute-start | bytes 49160 | tf_op jit(solution)/shard_map/ppermute | solution.py:358
  11.4 1.4 %collective-permute-done.3.aa.ba = bf16[4,2,4,256]{3,2,1,0:T(4,128)(2,1)S(1)} collective-permute-done((bf16[4,2,4,256]{3,2,1,0:T(4,128)(2,1)S(1)}, bf16[4,2,4,256]{3,2,1,0:T(4,128)(2,1)S(1)}, u32[]{:S(2)}, u32[]{:S(2)}) %collective-permute-start.3) | collective-permute-done | bytes 16416 | tf_op jit(solution)/shard_map/ppermute | solution.py:358
  12.7 0.0 collective-permute-done.4.ab.bb
  12.7 0.8 %collective-permute-done.row_a.row_b = bf16[4,2,32,256]{3,2,1,0:T(8,128)(2,1)S(1)} collective-permute-done((bf16[4,2,32,256]{3,2,1,0:T(8,128)(2,1)S(1)}, bf16[4,2,32,256]{3,2,1,0:T(8,128)(2,1)S(1)}, u32[]{:S(2)}, u32[]{:S(2)}) %collective-permute-start) | collective-permute-done | bytes 131104 | tf_op jit(solution)/shard_map/ppermute | solution.py:358
  13.6 0.0 collective-permute-done.1.col_a
  13.6 0.0 collective-permute-done.2.col_b
  13.6 1.7 %copy-done.3 = bf16[2,3,3,256,256]{4,3,2,1,0:T(8,128)(2,1)S(1)} copy-done((bf16[2,3,3,256,256]{4,3,2,1,0:T(8,128)(2,1)S(1)}, bf16[2,3,3,256,256]{4,3,2,1,0:T(8,128)(2,1)}, u32[]{:S(2)}) %copy-start.3) | copy-done | bytes 2359320
  15.3 1.0 %copy-done.4 = bf16[4,2,8,16,256]{4,3,2,1,0:T(8,128)(2,1)S(1)} copy-done((bf16[4,2,8,16,256]{4,3,2,1,0:T(8,128)(2,1)S(1)}, bf16[4,2,8,16,256]{4,3,2,1,0:T(8,128)(2,1)}, u32[]{:S(2)}) %copy-start.4) | copy-done | bytes 524312
  16.3 4.4 %shard_map.69 = (bf16[4,2,16,256]{3,2,1,0:T(8,128)(2,1)S(1)}, bf16[4,2,16,256]{3,2,1,0:T(8,128)(2,1)S(1)}, bf16[4,2,16,256]{3,2,1,0:T(8,128)(2,1)S(1)}, bf16[4,2...) custom-call(s32[13]{0:T(128)S(1)} %stack.71.flags, ...), custom_call_target="tpu_custom_call" | custom-call | flops 2415919104 | bytes 7405620 | tf_op jit(solution)/shard_map/pallas_call | solution.py:281
  20.7 3.8 %collective-permute-start.12 = (bf16[8,208,256]{2,1,0:T(8,128)(2,1)S(1)}, bf16[8,208,256]{2,1,0:T(8,128)(2,1)S(1)}, u32[]{:S(2)}, u32[]{:S(2)}) collective-permute-start(bf16[8,208,256]{2,1,0:T(8,128)(2,1)S(1)} %get-tuple-element.55), channel_id=1, source_target_pairs={{0,1},{1,0},{2,3},{3,2},{4,5},{5,4},{6,7},{7,6},{8,9},{9,8},{10,11... | collective-permute-start | bytes 2555912 | tf_op jit(solution)/shard_map/ppermute | solution.py:299
  24.5 0.1 collective-permute-start.5
  24.6 2.7 %collective-permute-start.6 = (bf16[4,2,16,256]{3,2,1,0:T(8,128)(2,1)S(1)}, bf16[4,2,16,256]{3,2,1,0:T(8,128)(2,1)S(1)}, u32[]{:S(2)}, u32[]{:S(2)}) collective-permute-start(bf16[4,2,16,256]{3,2,1,0:T(8,128)(2,1)S(1)} %get-tuple-element.46), channel_id=1, source_target_pairs={{0,2},{1,3},{2,0},{3,1},{4,6},{5,7},{6,4},{7,5},{8,10},{9,11},{10,... | collective-permute-start | bytes 196616 | tf_op jit(solution)/shard_map/ppermute | solution.py:299
  27.3 0.0 collective-permute-start.7
  27.3 0.4 collective-permute-start.8
  27.7 0.0 collective-permute-done.5.refs_1_
  27.7 1.1 %collective-permute-start.9 = (bf16[4,2,16,256]{3,2,1,0:T(8,128)(2,1)S(1)}, bf16[4,2,16,256]{3,2,1,0:T(8,128)(2,1)S(1)}, u32[]{:S(2)}, u32[]{:S(2)}) collective-permute-start(bf16[4,2,16,256]{3,2,1,0:T(8,128)(2,1)S(1)} %get-tuple-element.49), channel_id=1, source_target_pairs={{0,5},{1,4},{2,7},{3,6},{4,1},{5,0},{6,3},{7,2},{8,13},{9,12},{10,... | collective-permute-start | bytes 196616 | tf_op jit(solution)/shard_map/ppermute | solution.py:299
  28.8 0.8 %collective-permute-done.6.refs_2_ = bf16[4,2,16,256]{3,2,1,0:T(8,128)(2,1)S(1)} collective-permute-done((bf16[4,2,16,256]{3,2,1,0:T(8,128)(2,1)S(1)}, bf16[4,2,16,256]{3,2,1,0:T(8,128)(2,1)S(1)}, u32[]{:S(2)}, u32[]{:S(2)}) %collective-permute-start.6) | collective-permute-done | bytes 65568 | tf_op jit(solution)/shard_map/ppermute | solution.py:299
  29.6 1.0 %collective-permute-start.10 = (bf16[4,2,16,256]{3,2,1,0:T(8,128)(2,1)S(1)}, bf16[4,2,16,256]{3,2,1,0:T(8,128)(2,1)S(1)}, u32[]{:S(2)}, u32[]{:S(2)}) collective-permute-start(bf16[4,2,16,256]{3,2,1,0:T(8,128)(2,1)S(1)} %get-tuple-element.50), channel_id=1, source_target_pairs={{0,6},{1,7},{2,4},{3,5},{4,2},{5,3},{6,0},{7,1},{8,14},{9,15},{10,... | collective-permute-start | bytes 196616 | tf_op jit(solution)/shard_map/ppermute | solution.py:299
  30.5 1.1 %collective-permute-done.7.refs_3_ = bf16[4,2,16,256]{3,2,1,0:T(8,128)(2,1)S(1)} collective-permute-done((bf16[4,2,16,256]{3,2,1,0:T(8,128)(2,1)S(1)}, bf16[4,2,16,256]{3,2,1,0:T(8,128)(2,1)S(1)}, u32[]{:S(2)}, u32[]{:S(2)}) %collective-permute-start.7) | collective-permute-done | bytes 65568 | tf_op jit(solution)/shard_map/ppermute | solution.py:299
  31.6 0.0 collective-permute-start.11
  31.7 0.4 collective-permute-done.8.refs_4_
  32.1 0.0 collective-permute-done.9.refs_5_
  32.1 3.6 %collective-permute-done.10.refs_6_ = bf16[4,2,16,256]{3,2,1,0:T(8,128)(2,1)S(1)} collective-permute-done((bf16[4,2,16,256]{3,2,1,0:T(8,128)(2,1)S(1)}, bf16[4,2,16,256]{3,2,1,0:T(8,128)(2,1)S(1)}, u32[]{:S(2)}, u32[]{:S(2)}) %collective-permute-start.10) | collective-permute-done | bytes 65568 | tf_op jit(solution)/shard_map/ppermute | solution.py:299
  35.7 1.2 %collective-permute-done.11.refs_7_ = bf16[4,2,16,256]{3,2,1,0:T(8,128)(2,1)S(1)} collective-permute-done((bf16[4,2,16,256]{3,2,1,0:T(8,128)(2,1)S(1)}, bf16[4,2,16,256]{3,2,1,0:T(8,128)(2,1)S(1)}, u32[]{:S(2)}, u32[]{:S(2)}) %collective-permute-start.11) | collective-permute-done | bytes 65568 | tf_op jit(solution)/shard_map/ppermute | solution.py:299
  36.9 1.5 %shard_map.70 = (bf16[8,208,256]{2,1,0:T(8,128)(2,1)S(1)}, bf16[8,208,256]{2,1,0:T(8,128)(2,1)S(1)}, bf16[2,512,256]{2,1,0:T(8,128)(2,1)S(1)}) custom-call(s32[13]{0:T(128)S(1)} %stack.71.flags, bf16[4,2,16,256]{3,2,1,0:T(8,128)(2,1)S(1)} %get-tuple-element.44.refs_0_, bf16[4,2,16,256]{3,2,1,0:T(8,128)(2,1)S(1)} %collective-permute-done.5.refs_1_, ...), custom_call_target="tpu_custom_call" | custom-call | flops 536870912 | bytes 5505076 | tf_op jit(solution)/shard_map/pallas_call | solution.py:281
  38.4 0.2 collective-permute-start.19
  38.6 0.0 collective-permute-done.12.refs_1_
  38.6 0.7 shard_map.72
  39.3 1.1 %collective-permute-start.13 = (bf16[4,208,128]{2,1,0:T(8,128)(2,1)S(1)}, bf16[4,208,128]{2,1,0:T(8,128)(2,1)S(1)}, u32[]{:S(2)}, u32[]{:S(2)}) collective-permute-start(bf16[4,208,128]{2,1,0:T(8,128)(2,1)S(1)} %get-tuple-element.57), channel_id=1, source_target_pairs={{0,2},{1,3},{2,0},{3,1},{4,6},{5,7},{6,4},{7,5},{8,10},{9,11},{10,... | collective-permute-start | bytes 638984 | tf_op jit(solution)/shard_map/ppermute | solution.py:299
  40.4 1.5 %collective-permute-start.14 = (bf16[4,208,128]{2,1,0:T(8,128)(2,1)S(1)}, bf16[4,208,128]{2,1,0:T(8,128)(2,1)S(1)}, u32[]{:S(2)}, u32[]{:S(2)}) collective-permute-start(bf16[4,208,128]{2,1,0:T(8,128)(2,1)S(1)} %get-tuple-element.58), channel_id=1, source_target_pairs={{0,16},{16,0},{1,17},{17,1},{2,18},{18,2},{3,19},{19,3},{4,20},{20... | collective-permute-start | bytes 638984 | tf_op jit(solution)/shard_map/ppermute | solution.py:301
  41.9 1.0 %collective-permute-start.15 = (bf16[4,208,128]{2,1,0:T(8,128)(2,1)S(1)}, bf16[4,208,128]{2,1,0:T(8,128)(2,1)S(1)}, u32[]{:S(2)}, u32[]{:S(2)}) collective-permute-start(bf16[4,208,128]{2,1,0:T(8,128)(2,1)S(1)} %get-tuple-element.59), channel_id=1, source_target_pairs={{0,18},{1,19},{2,16},{3,17},{4,22},{5,23},{6,20},{7,21},{8,26},{9,... | collective-permute-start | bytes 638984 | tf_op jit(solution)/shard_map/ppermute | solution.py:303
  42.9 0.7 shard_map.74
  43.6 1.1 %collective-permute-start.20 = (bf16[4,208,128]{2,1,0:T(8,128)(2,1)S(1)}, bf16[4,208,128]{2,1,0:T(8,128)(2,1)S(1)}, u32[]{:S(2)}, u32[]{:S(2)}) collective-permute-start(bf16[4,208,128]{2,1,0:T(8,128)(2,1)S(1)} %get-tuple-element.67), channel_id=1, source_target_pairs={{0,2},{1,3},{2,0},{3,1},{4,6},{5,7},{6,4},{7,5},{8,10},{9,11},{10,... | collective-permute-start | bytes 638984 | tf_op jit(solution)/shard_map/ppermute | solution.py:299
  44.7 1.5 %collective-permute-start.21 = (bf16[4,208,128]{2,1,0:T(8,128)(2,1)S(1)}, bf16[4,208,128]{2,1,0:T(8,128)(2,1)S(1)}, u32[]{:S(2)}, u32[]{:S(2)}) collective-permute-start(bf16[4,208,128]{2,1,0:T(8,128)(2,1)S(1)} %get-tuple-element.68), channel_id=1, source_target_pairs={{0,16},{16,0},{1,17},{17,1},{2,18},{18,2},{3,19},{19,3},{4,20},{20... | collective-permute-start | bytes 638984 | tf_op jit(solution)/shard_map/ppermute | solution.py:301
  46.2 1.5 %collective-permute-done.13.refs_1_ = bf16[4,208,128]{2,1,0:T(8,128)(2,1)S(1)} collective-permute-done((bf16[4,208,128]{2,1,0:T(8,128)(2,1)S(1)}, bf16[4,208,128]{2,1,0:T(8,128)(2,1)S(1)}, u32[]{:S(2)}, u32[]{:S(2)}) %collective-permute-start.13) | collective-permute-done | bytes 213024 | tf_op jit(solution)/shard_map/ppermute | solution.py:299
  47.7 2.8 %collective-permute-start.22 = (bf16[4,208,128]{2,1,0:T(8,128)(2,1)S(1)}, bf16[4,208,128]{2,1,0:T(8,128)(2,1)S(1)}, u32[]{:S(2)}, u32[]{:S(2)}) collective-permute-start(bf16[4,208,128]{2,1,0:T(8,128)(2,1)S(1)} %get-tuple-element.69), channel_id=1, source_target_pairs={{0,18},{1,19},{2,16},{3,17},{4,22},{5,23},{6,20},{7,21},{8,26},{9,... | collective-permute-start | bytes 638984 | tf_op jit(solution)/shard_map/ppermute | solution.py:303
  50.5 0.0 collective-permute-done.14.refs_2_
  50.5 3.1 %collective-permute-done.15.refs_3_ = bf16[4,208,128]{2,1,0:T(8,128)(2,1)S(1)} collective-permute-done((bf16[4,208,128]{2,1,0:T(8,128)(2,1)S(1)}, bf16[4,208,128]{2,1,0:T(8,128)(2,1)S(1)}, u32[]{:S(2)}, u32[]{:S(2)}) %collective-permute-start.15) | collective-permute-done | bytes 213024 | tf_op jit(solution)/shard_map/ppermute | solution.py:303
  53.6 0.6 shard_map.73
  54.2 1.1 %collective-permute-start.16 = (bf16[1,208,128]{2,1,0:T(8,128)(2,1)S(1)}, bf16[1,208,128]{2,1,0:T(8,128)(2,1)S(1)}, u32[]{:S(2)}, u32[]{:S(2)}) collective-permute-start(bf16[1,208,128]{2,1,0:T(8,128)(2,1)S(1)} %get-tuple-element.61), channel_id=1, source_target_pairs={{0,4},{1,5},{2,6},{3,7},{4,0},{5,1},{6,2},{7,3},{8,12},{9,13},{10,... | collective-permute-start | bytes 159752 | tf_op jit(solution)/shard_map/ppermute | solution.py:299
  55.4 2.3 %collective-permute-start.17 = (bf16[1,208,128]{2,1,0:T(8,128)(2,1)S(1)}, bf16[1,208,128]{2,1,0:T(8,128)(2,1)S(1)}, u32[]{:S(2)}, u32[]{:S(2)}) collective-permute-start(bf16[1,208,128]{2,1,0:T(8,128)(2,1)S(1)} %get-tuple-element.62), channel_id=1, source_target_pairs={{0,8},{1,9},{2,10},{3,11},{4,12},{5,13},{6,14},{7,15},{8,0},{9,1},... | collective-permute-start | bytes 159752 | tf_op jit(solution)/shard_map/ppermute | solution.py:299
  57.7 0.0 collective-permute-done.20.refs_1_
  57.7 1.2 %collective-permute-start.18 = (bf16[1,208,128]{2,1,0:T(8,128)(2,1)S(1)}, bf16[1,208,128]{2,1,0:T(8,128)(2,1)S(1)}, u32[]{:S(2)}, u32[]{:S(2)}) collective-permute-start(bf16[1,208,128]{2,1,0:T(8,128)(2,1)S(1)} %get-tuple-element.63), channel_id=1, source_target_pairs={{0,12},{1,13},{2,14},{3,15},{4,8},{5,9},{6,10},{7,11},{8,4},{9,5},... | collective-permute-start | bytes 159752 | tf_op jit(solution)/shard_map/ppermute | solution.py:299
  58.8 3.0 %collective-permute-done.22.refs_3_ = bf16[4,208,128]{2,1,0:T(8,128)(2,1)S(1)} collective-permute-done((bf16[4,208,128]{2,1,0:T(8,128)(2,1)S(1)}, bf16[4,208,128]{2,1,0:T(8,128)(2,1)S(1)}, u32[]{:S(2)}, u32[]{:S(2)}) %collective-permute-start.22) | collective-permute-done | bytes 213024 | tf_op jit(solution)/shard_map/ppermute | solution.py:303
  61.9 0.6 shard_map.75
  62.5 1.3 %collective-permute-start.23 = (bf16[1,208,128]{2,1,0:T(8,128)(2,1)S(1)}, bf16[1,208,128]{2,1,0:T(8,128)(2,1)S(1)}, u32[]{:S(2)}, u32[]{:S(2)}) collective-permute-start(bf16[1,208,128]{2,1,0:T(8,128)(2,1)S(1)} %get-tuple-element.71), channel_id=1, source_target_pairs={{0,4},{1,5},{2,6},{3,7},{4,0},{5,1},{6,2},{7,3},{8,12},{9,13},{10,... | collective-permute-start | bytes 159752 | tf_op jit(solution)/shard_map/ppermute | solution.py:299
  63.8 2.1 %collective-permute-start.24 = (bf16[1,208,128]{2,1,0:T(8,128)(2,1)S(1)}, bf16[1,208,128]{2,1,0:T(8,128)(2,1)S(1)}, u32[]{:S(2)}, u32[]{:S(2)}) collective-permute-start(bf16[1,208,128]{2,1,0:T(8,128)(2,1)S(1)} %get-tuple-element.72), channel_id=1, source_target_pairs={{0,8},{1,9},{2,10},{3,11},{4,12},{5,13},{6,14},{7,15},{8,0},{9,1},... | collective-permute-start | bytes 159752 | tf_op jit(solution)/shard_map/ppermute | solution.py:299
  65.9 1.1 %collective-permute-start.25 = (bf16[1,208,128]{2,1,0:T(8,128)(2,1)S(1)}, bf16[1,208,128]{2,1,0:T(8,128)(2,1)S(1)}, u32[]{:S(2)}, u32[]{:S(2)}) collective-permute-start(bf16[1,208,128]{2,1,0:T(8,128)(2,1)S(1)} %get-tuple-element.73), channel_id=1, source_target_pairs={{0,12},{1,13},{2,14},{3,15},{4,8},{5,9},{6,10},{7,11},{8,4},{9,5},... | collective-permute-start | bytes 159752 | tf_op jit(solution)/shard_map/ppermute | solution.py:299
  67.0 0.3 collective-permute-done.23.refs_5_
  67.3 2.8 %collective-permute-done.24.refs_6_ = bf16[1,208,128]{2,1,0:T(8,128)(2,1)S(1)} collective-permute-done((bf16[1,208,128]{2,1,0:T(8,128)(2,1)S(1)}, bf16[1,208,128]{2,1,0:T(8,128)(2,1)S(1)}, u32[]{:S(2)}, u32[]{:S(2)}) %collective-permute-start.24) | collective-permute-done | bytes 53280 | tf_op jit(solution)/shard_map/ppermute | solution.py:299
  70.1 1.7 %collective-permute-done.25.refs_7_ = bf16[1,208,128]{2,1,0:T(8,128)(2,1)S(1)} collective-permute-done((bf16[1,208,128]{2,1,0:T(8,128)(2,1)S(1)}, bf16[1,208,128]{2,1,0:T(8,128)(2,1)S(1)}, u32[]{:S(2)}, u32[]{:S(2)}) %collective-permute-start.25) | collective-permute-done | bytes 53280 | tf_op jit(solution)/shard_map/ppermute | solution.py:299
  71.8 0.6 shard_map.76
  72.5 1.6 %collective-permute-start.26 = (bf16[208,128]{1,0:T(8,128)(2,1)S(1)}, bf16[208,128]{1,0:T(8,128)(2,1)S(1)}, u32[]{:S(2)}, u32[]{:S(2)}) collective-permute-start(bf16[208,128]{1,0:T(8,128)(2,1)S(1)} %get-tuple-element.75), channel_id=1, source_target_pairs={{0,16},{16,0},{1,17},{17,1},{2,18},{18,2},{3,19},{19,3},{4,20},{20... | collective-permute-start | bytes 159752 | tf_op jit(solution)/shard_map/ppermute | solution.py:301
  74.0 2.1 %shard_map.71 = bf16[4,2,128,1024]{3,2,1,0:T(8,128)(2,1)} custom-call(bf16[2,512,256]{2,1,0:T(8,128)(2,1)S(1)} %get-tuple-element.53.tokens, bf16[2,1024,256]{2,1,0:T(8,128)(2,1)S(1)} %copy-done.1), custom_call_target="tpu_custom_call" | custom-call | flops 536870912 | bytes 3670016 | tf_op jit(solution)/shard_map/pallas_call | solution.py:281
  76.1 0.6 collective-permute-done.26.came
  76.7 1.2 %shard_map.77 = f32[208,256]{1,0:T(8,128)} custom-call(s32[13]{0:T(128)S(1)} %stack.71.flags, f32[208,128]{1,0:T(8,128)S(1)} %get-tuple-element.74.kept, bf16[208,128]{1,0:T(8,128)(2,1)S(1)} %collective-permute-done.26.came), custom_call_target="tpu_custom_call" | custom-call | bytes 372788 | tf_op jit(solution)/shard_map/pallas_call | solution.py:281
  (11 shorter events, 0.0 us)
Async XLA Ops:
  0.8 1.2 %copy-start.2 = (bf16[4,16,32,256]{3,2,1,0:T(8,128)(2,1)S(1)}, bf16[4,16,32,256]{3,2,1,0:T(8,128)(2,1)}, u32[]{:S(2)}) copy-start(bf16[4,16,32,256]{3,2,1,0:T(8,128)(2,1)} %cot.3) | copy-start | bytes 3145732
  2.8 10.8 %collective-permute-start = (bf16[4,2,32,256]{3,2,1,0:T(8,128)(2,1)S(1)}, bf16[4,2,32,256]{3,2,1,0:T(8,128)(2,1)S(1)}, u32[]{:S(2)}, u32[]{:S(2)}) collective-permute-start(bf16[4,2,32,256]{3,2,1,0:T(8,128)(2,1)S(1)} %get-tuple-element.39), channel_id=1, source_target_pairs={{0,8},{1,9},{3,11},{2,10},{6,14},{7,15},{5,13},{4,12},{8,0},{9,1},... | collective-permute-start | bytes 393224 | tf_op jit(solution)/shard_map/ppermute | solution.py:358
  6.9 6.7 %collective-permute-start.1 = (bf16[4,16,4,256]{3,2,1,0:T(4,128)(2,1)S(1)}, bf16[4,16,4,256]{3,2,1,0:T(4,128)(2,1)S(1)}, u32[]{:S(2)}, u32[]{:S(2)}) collective-permute-start(bf16[4,16,4,256]{3,2,1,0:T(4,128)(2,1)S(1)} %get-tuple-element.40), channel_id=1, source_target_pairs={{0,1},{1,0},{3,2},{2,3},{6,7},{7,6},{5,4},{4,5},{8,9},{9,8},{11,10... | collective-permute-start | bytes 393224 | tf_op jit(solution)/shard_map/ppermute | solution.py:358
  6.9 6.7 %collective-permute-start.2 = (bf16[4,16,4,256]{3,2,1,0:T(4,128)(2,1)S(1)}, bf16[4,16,4,256]{3,2,1,0:T(4,128)(2,1)S(1)}, u32[]{:S(2)}, u32[]{:S(2)}) collective-permute-start(bf16[4,16,4,256]{3,2,1,0:T(4,128)(2,1)S(1)} %get-tuple-element.41), channel_id=1, source_target_pairs={{1,3},{3,1},{2,6},{6,2},{7,5},{5,7},{9,11},{11,9},{10,14},{14,10},... | collective-permute-start | bytes 393224 | tf_op jit(solution)/shard_map/ppermute | solution.py:358
  7.6 5.2 %collective-permute-start.3 = (bf16[4,2,4,256]{3,2,1,0:T(4,128)(2,1)S(1)}, bf16[4,2,4,256]{3,2,1,0:T(4,128)(2,1)S(1)}, u32[]{:S(2)}, u32[]{:S(2)}) collective-permute-start(bf16[4,2,4,256]{3,2,1,0:T(4,128)(2,1)S(1)} %get-tuple-element.42), channel_id=1, source_target_pairs={{0,9},{1,8},{3,10},{2,11},{6,15},{7,14},{5,12},{4,13},{8,1},{9,0},... | collective-permute-start | bytes 49160 | tf_op jit(solution)/shard_map/ppermute | solution.py:358
  10.6 26.3 %copy-start = (bf16[4,2,128,1024]{3,2,1,0:T(8,128)(2,1)S(1)}, bf16[4,2,128,1024]{3,2,1,0:T(8,128)(2,1)}, u32[]{:S(2)}) copy-start(bf16[4,2,128,1024]{3,2,1,0:T(8,128)(2,1)} %refs_8_.1) | copy-start | bytes 6291460
  10.6 2.2 %collective-permute-start.4 = (bf16[4,2,4,256]{3,2,1,0:T(4,128)(2,1)S(1)}, bf16[4,2,4,256]{3,2,1,0:T(4,128)(2,1)S(1)}, u32[]{:S(2)}, u32[]{:S(2)}) collective-permute-start(bf16[4,2,4,256]{3,2,1,0:T(4,128)(2,1)S(1)} %get-tuple-element.43), channel_id=1, source_target_pairs={{1,11},{3,9},{2,14},{6,10},{7,13},{5,15},{9,3},{11,1},{10,6},{14,2... | collective-permute-start | bytes 49160 | tf_op jit(solution)/shard_map/ppermute | solution.py:358
  13.6 1.7 %copy-start.3 = (bf16[2,3,3,256,256]{4,3,2,1,0:T(8,128)(2,1)S(1)}, bf16[2,3,3,256,256]{4,3,2,1,0:T(8,128)(2,1)}, u32[]{:S(2)}) copy-start(bf16[2,3,3,256,256]{4,3,2,1,0:T(8,128)(2,1)} %weight.2) | copy-start | bytes 7077892
  15.2 1.0 %copy-start.4 = (bf16[4,2,8,16,256]{4,3,2,1,0:T(8,128)(2,1)S(1)}, bf16[4,2,8,16,256]{4,3,2,1,0:T(8,128)(2,1)}, u32[]{:S(2)}) copy-start(bf16[4,2,8,16,256]{4,3,2,1,0:T(8,128)(2,1)} %saved.1) | copy-start | bytes 1572868
  20.7 17.9 %collective-permute-start.12 = (bf16[8,208,256]{2,1,0:T(8,128)(2,1)S(1)}, bf16[8,208,256]{2,1,0:T(8,128)(2,1)S(1)}, u32[]{:S(2)}, u32[]{:S(2)}) collective-permute-start(bf16[8,208,256]{2,1,0:T(8,128)(2,1)S(1)} %get-tuple-element.55), channel_id=1, source_target_pairs={{0,1},{1,0},{2,3},{3,2},{4,5},{5,4},{6,7},{7,6},{8,9},{9,8},{10,11... | collective-permute-start | bytes 2555912 | tf_op jit(solution)/shard_map/ppermute | solution.py:299
  24.5 3.2 %collective-permute-start.5 = (bf16[4,2,16,256]{3,2,1,0:T(8,128)(2,1)S(1)}, bf16[4,2,16,256]{3,2,1,0:T(8,128)(2,1)S(1)}, u32[]{:S(2)}, u32[]{:S(2)}) collective-permute-start(bf16[4,2,16,256]{3,2,1,0:T(8,128)(2,1)S(1)} %get-tuple-element.45), channel_id=1, source_target_pairs={{0,1},{1,0},{2,3},{3,2},{4,5},{5,4},{6,7},{7,6},{8,9},{9,8},{10,11... | collective-permute-start | bytes 196616 | tf_op jit(solution)/shard_map/ppermute | solution.py:299
  24.6 5.0 %collective-permute-start.6 = (bf16[4,2,16,256]{3,2,1,0:T(8,128)(2,1)S(1)}, bf16[4,2,16,256]{3,2,1,0:T(8,128)(2,1)S(1)}, u32[]{:S(2)}, u32[]{:S(2)}) collective-permute-start(bf16[4,2,16,256]{3,2,1,0:T(8,128)(2,1)S(1)} %get-tuple-element.46), channel_id=1, source_target_pairs={{0,2},{1,3},{2,0},{3,1},{4,6},{5,7},{6,4},{7,5},{8,10},{9,11},{10,... | collective-permute-start | bytes 196616 | tf_op jit(solution)/shard_map/ppermute | solution.py:299
  27.3 4.4 %collective-permute-start.7 = (bf16[4,2,16,256]{3,2,1,0:T(8,128)(2,1)S(1)}, bf16[4,2,16,256]{3,2,1,0:T(8,128)(2,1)S(1)}, u32[]{:S(2)}, u32[]{:S(2)}) collective-permute-start(bf16[4,2,16,256]{3,2,1,0:T(8,128)(2,1)S(1)} %get-tuple-element.47), channel_id=1, source_target_pairs={{0,3},{1,2},{2,1},{3,0},{4,7},{5,6},{6,5},{7,4},{8,11},{9,10},{10,... | collective-permute-start | bytes 196616 | tf_op jit(solution)/shard_map/ppermute | solution.py:299
  27.3 4.8 %collective-permute-start.8 = (bf16[4,2,16,256]{3,2,1,0:T(8,128)(2,1)S(1)}, bf16[4,2,16,256]{3,2,1,0:T(8,128)(2,1)S(1)}, u32[]{:S(2)}, u32[]{:S(2)}) collective-permute-start(bf16[4,2,16,256]{3,2,1,0:T(8,128)(2,1)S(1)} %get-tuple-element.48), channel_id=1, source_target_pairs={{0,4},{1,5},{2,6},{3,7},{4,0},{5,1},{6,2},{7,3},{8,12},{9,13},{10,... | collective-permute-start | bytes 196616 | tf_op jit(solution)/shard_map/ppermute | solution.py:299
  27.7 4.4 %collective-permute-start.9 = (bf16[4,2,16,256]{3,2,1,0:T(8,128)(2,1)S(1)}, bf16[4,2,16,256]{3,2,1,0:T(8,128)(2,1)S(1)}, u32[]{:S(2)}, u32[]{:S(2)}) collective-permute-start(bf16[4,2,16,256]{3,2,1,0:T(8,128)(2,1)S(1)} %get-tuple-element.49), channel_id=1, source_target_pairs={{0,5},{1,4},{2,7},{3,6},{4,1},{5,0},{6,3},{7,2},{8,13},{9,12},{10,... | collective-permute-start | bytes 196616 | tf_op jit(solution)/shard_map/ppermute | solution.py:299
  29.6 6.1 %collective-permute-start.10 = (bf16[4,2,16,256]{3,2,1,0:T(8,128)(2,1)S(1)}, bf16[4,2,16,256]{3,2,1,0:T(8,128)(2,1)S(1)}, u32[]{:S(2)}, u32[]{:S(2)}) collective-permute-start(bf16[4,2,16,256]{3,2,1,0:T(8,128)(2,1)S(1)} %get-tuple-element.50), channel_id=1, source_target_pairs={{0,6},{1,7},{2,4},{3,5},{4,2},{5,3},{6,0},{7,1},{8,14},{9,15},{10,... | collective-permute-start | bytes 196616 | tf_op jit(solution)/shard_map/ppermute | solution.py:299
  31.6 5.3 %collective-permute-start.11 = (bf16[4,2,16,256]{3,2,1,0:T(8,128)(2,1)S(1)}, bf16[4,2,16,256]{3,2,1,0:T(8,128)(2,1)S(1)}, u32[]{:S(2)}, u32[]{:S(2)}) collective-permute-start(bf16[4,2,16,256]{3,2,1,0:T(8,128)(2,1)S(1)} %get-tuple-element.51), channel_id=1, source_target_pairs={{0,7},{1,6},{2,5},{3,4},{4,3},{5,2},{6,1},{7,0},{8,15},{9,14},{10,... | collective-permute-start | bytes 196616 | tf_op jit(solution)/shard_map/ppermute | solution.py:299
  38.4 4.5 %collective-permute-start.19 = (bf16[8,208,256]{2,1,0:T(8,128)(2,1)S(1)}, bf16[8,208,256]{2,1,0:T(8,128)(2,1)S(1)}, u32[]{:S(2)}, u32[]{:S(2)}) collective-permute-start(bf16[8,208,256]{2,1,0:T(8,128)(2,1)S(1)} %get-tuple-element.65), channel_id=1, source_target_pairs={{0,1},{1,0},{2,3},{3,2},{4,5},{5,4},{6,7},{7,6},{8,9},{9,8},{10,11... | collective-permute-start | bytes 2555912 | tf_op jit(solution)/shard_map/ppermute | solution.py:299
  39.3 8.4 %collective-permute-start.13 = (bf16[4,208,128]{2,1,0:T(8,128)(2,1)S(1)}, bf16[4,208,128]{2,1,0:T(8,128)(2,1)S(1)}, u32[]{:S(2)}, u32[]{:S(2)}) collective-permute-start(bf16[4,208,128]{2,1,0:T(8,128)(2,1)S(1)} %get-tuple-element.57), channel_id=1, source_target_pairs={{0,2},{1,3},{2,0},{3,1},{4,6},{5,7},{6,4},{7,5},{8,10},{9,11},{10,... | collective-permute-start | bytes 638984 | tf_op jit(solution)/shard_map/ppermute | solution.py:299
  40.4 10.0 %collective-permute-start.14 = (bf16[4,208,128]{2,1,0:T(8,128)(2,1)S(1)}, bf16[4,208,128]{2,1,0:T(8,128)(2,1)S(1)}, u32[]{:S(2)}, u32[]{:S(2)}) collective-permute-start(bf16[4,208,128]{2,1,0:T(8,128)(2,1)S(1)} %get-tuple-element.58), channel_id=1, source_target_pairs={{0,16},{16,0},{1,17},{17,1},{2,18},{18,2},{3,19},{19,3},{4,20},{20... | collective-permute-start | bytes 638984 | tf_op jit(solution)/shard_map/ppermute | solution.py:301
  41.9 11.7 %collective-permute-start.15 = (bf16[4,208,128]{2,1,0:T(8,128)(2,1)S(1)}, bf16[4,208,128]{2,1,0:T(8,128)(2,1)S(1)}, u32[]{:S(2)}, u32[]{:S(2)}) collective-permute-start(bf16[4,208,128]{2,1,0:T(8,128)(2,1)S(1)} %get-tuple-element.59), channel_id=1, source_target_pairs={{0,18},{1,19},{2,16},{3,17},{4,22},{5,23},{6,20},{7,21},{8,26},{9,... | collective-permute-start | bytes 638984 | tf_op jit(solution)/shard_map/ppermute | solution.py:303
  42.9 31.1 %copy-start.1 = (bf16[2,1024,256]{2,1,0:T(8,128)(2,1)S(1)}, bf16[2,1024,256]{2,1,0:T(8,128)(2,1)}, u32[]{:S(2)}) copy-start(bf16[2,1024,256]{2,1,0:T(8,128)(2,1)} %weight.3) | copy-start | bytes 3145732
  43.6 14.0 %collective-permute-start.20 = (bf16[4,208,128]{2,1,0:T(8,128)(2,1)S(1)}, bf16[4,208,128]{2,1,0:T(8,128)(2,1)S(1)}, u32[]{:S(2)}, u32[]{:S(2)}) collective-permute-start(bf16[4,208,128]{2,1,0:T(8,128)(2,1)S(1)} %get-tuple-element.67), channel_id=1, source_target_pairs={{0,2},{1,3},{2,0},{3,1},{4,6},{5,7},{6,4},{7,5},{8,10},{9,11},{10,... | collective-permute-start | bytes 638984 | tf_op jit(solution)/shard_map/ppermute | solution.py:299
  44.7 14.1 %collective-permute-start.21 = (bf16[4,208,128]{2,1,0:T(8,128)(2,1)S(1)}, bf16[4,208,128]{2,1,0:T(8,128)(2,1)S(1)}, u32[]{:S(2)}, u32[]{:S(2)}) collective-permute-start(bf16[4,208,128]{2,1,0:T(8,128)(2,1)S(1)} %get-tuple-element.68), channel_id=1, source_target_pairs={{0,16},{16,0},{1,17},{17,1},{2,18},{18,2},{3,19},{19,3},{4,20},{20... | collective-permute-start | bytes 638984 | tf_op jit(solution)/shard_map/ppermute | solution.py:301
  47.7 14.1 %collective-permute-start.22 = (bf16[4,208,128]{2,1,0:T(8,128)(2,1)S(1)}, bf16[4,208,128]{2,1,0:T(8,128)(2,1)S(1)}, u32[]{:S(2)}, u32[]{:S(2)}) collective-permute-start(bf16[4,208,128]{2,1,0:T(8,128)(2,1)S(1)} %get-tuple-element.69), channel_id=1, source_target_pairs={{0,18},{1,19},{2,16},{3,17},{4,22},{5,23},{6,20},{7,21},{8,26},{9,... | collective-permute-start | bytes 638984 | tf_op jit(solution)/shard_map/ppermute | solution.py:303
  54.2 11.7 %collective-permute-start.16 = (bf16[1,208,128]{2,1,0:T(8,128)(2,1)S(1)}, bf16[1,208,128]{2,1,0:T(8,128)(2,1)S(1)}, u32[]{:S(2)}, u32[]{:S(2)}) collective-permute-start(bf16[1,208,128]{2,1,0:T(8,128)(2,1)S(1)} %get-tuple-element.61), channel_id=1, source_target_pairs={{0,4},{1,5},{2,6},{3,7},{4,0},{5,1},{6,2},{7,3},{8,12},{9,13},{10,... | collective-permute-start | bytes 159752 | tf_op jit(solution)/shard_map/ppermute | solution.py:299
  55.4 11.6 %collective-permute-start.17 = (bf16[1,208,128]{2,1,0:T(8,128)(2,1)S(1)}, bf16[1,208,128]{2,1,0:T(8,128)(2,1)S(1)}, u32[]{:S(2)}, u32[]{:S(2)}) collective-permute-start(bf16[1,208,128]{2,1,0:T(8,128)(2,1)S(1)} %get-tuple-element.62), channel_id=1, source_target_pairs={{0,8},{1,9},{2,10},{3,11},{4,12},{5,13},{6,14},{7,15},{8,0},{9,1},... | collective-permute-start | bytes 159752 | tf_op jit(solution)/shard_map/ppermute | solution.py:299
  57.7 9.3 %collective-permute-start.18 = (bf16[1,208,128]{2,1,0:T(8,128)(2,1)S(1)}, bf16[1,208,128]{2,1,0:T(8,128)(2,1)S(1)}, u32[]{:S(2)}, u32[]{:S(2)}) collective-permute-start(bf16[1,208,128]{2,1,0:T(8,128)(2,1)S(1)} %get-tuple-element.63), channel_id=1, source_target_pairs={{0,12},{1,13},{2,14},{3,15},{4,8},{5,9},{6,10},{7,11},{8,4},{9,5},... | collective-permute-start | bytes 159752 | tf_op jit(solution)/shard_map/ppermute | solution.py:299
  62.5 4.8 %collective-permute-start.23 = (bf16[1,208,128]{2,1,0:T(8,128)(2,1)S(1)}, bf16[1,208,128]{2,1,0:T(8,128)(2,1)S(1)}, u32[]{:S(2)}, u32[]{:S(2)}) collective-permute-start(bf16[1,208,128]{2,1,0:T(8,128)(2,1)S(1)} %get-tuple-element.71), channel_id=1, source_target_pairs={{0,4},{1,5},{2,6},{3,7},{4,0},{5,1},{6,2},{7,3},{8,12},{9,13},{10,... | collective-permute-start | bytes 159752 | tf_op jit(solution)/shard_map/ppermute | solution.py:299
  63.8 6.3 %collective-permute-start.24 = (bf16[1,208,128]{2,1,0:T(8,128)(2,1)S(1)}, bf16[1,208,128]{2,1,0:T(8,128)(2,1)S(1)}, u32[]{:S(2)}, u32[]{:S(2)}) collective-permute-start(bf16[1,208,128]{2,1,0:T(8,128)(2,1)S(1)} %get-tuple-element.72), channel_id=1, source_target_pairs={{0,8},{1,9},{2,10},{3,11},{4,12},{5,13},{6,14},{7,15},{8,0},{9,1},... | collective-permute-start | bytes 159752 | tf_op jit(solution)/shard_map/ppermute | solution.py:299
  65.9 5.9 %collective-permute-start.25 = (bf16[1,208,128]{2,1,0:T(8,128)(2,1)S(1)}, bf16[1,208,128]{2,1,0:T(8,128)(2,1)S(1)}, u32[]{:S(2)}, u32[]{:S(2)}) collective-permute-start(bf16[1,208,128]{2,1,0:T(8,128)(2,1)S(1)} %get-tuple-element.73), channel_id=1, source_target_pairs={{0,12},{1,13},{2,14},{3,15},{4,8},{5,9},{6,10},{7,11},{8,4},{9,5},... | collective-permute-start | bytes 159752 | tf_op jit(solution)/shard_map/ppermute | solution.py:299
  72.5 4.2 %collective-permute-start.26 = (bf16[208,128]{1,0:T(8,128)(2,1)S(1)}, bf16[208,128]{1,0:T(8,128)(2,1)S(1)}, u32[]{:S(2)}, u32[]{:S(2)}) collective-permute-start(bf16[208,128]{1,0:T(8,128)(2,1)S(1)} %get-tuple-element.75), channel_id=1, source_target_pairs={{0,16},{16,0},{1,17},{17,1},{2,18},{18,2},{3,19},{19,3},{4,20},{20... | collective-permute-start | bytes 159752 | tf_op jit(solution)/shard_map/ppermute | solution.py:301

commit v3 on v2

--- a/solution.py
+++ b/solution.py
@@ -37,14 +37,17 @@
 
 
 def pool_conv_kernel(
-    has_second, flags, cot, row_a, row_b, col_a, col_b, aa, ab, ba, bb, weight, saved,
+    has_second, flags, cot, row_a, row_b, col_a, col_b, aa, ab, ba, bb, weight,
     *outs_and_scratch,
 ):
-    igs, (split_refs, late) = outs_and_scratch[:TILE_COLS], (outs_and_scratch[TILE_COLS:-6], outs_and_scratch[-6])
-    rows_ref, cells_ref, patch_ref, acc_ref, full_ref = outs_and_scratch[-5:]
+    igs, patch_ref = outs_and_scratch[:TILE_COLS], outs_and_scratch[TILE_COLS]
+    rows_ref, cells_ref, acc_ref, weight_ref, sems = outs_and_scratch[TILE_COLS + 1 :]
     images, height2, width2, channels = cot.shape
     height, width = height2 // 2, width2 // 2
     depths = weight.shape[0]
+    copies = [pltpu.make_async_copy(weight.at[k], weight_ref.at[k], sems.at[k]) for k in range(depths)]
+    for copy in copies:
+        copy.start()
     row_odd, col_odd = flags[0] == 1, flags[1] == 1
     top, bottom, left, right = flags[2] == 1, flags[3] == 1, flags[4] == 1, flags[5] == 1
     zero = jnp.zeros((), F32)
@@ -134,10 +137,11 @@
     lax.fori_loop(0, images, per_image, 0)
     gray = flags[6]
     for k in range(depths):
+        copies[k].wait()
         for n in range(9):
             part = lax.dot_general(
                 patch_ref[:, pl.ds(n * channels, channels)],
-                weight[k, n // 3, n % 3],
+                weight_ref[k, n // 3, n % 3],
                 (((1,), (1,)), ((), ())),
                 preferred_element_type=F32,
             )
@@ -149,13 +153,16 @@
             for apart in range(height):
                 at = pl.multiple_of((i * height + (gray ^ apart)) * width, width)
                 igs[apart][i, k] = acc_ref[pl.ds(at, width), :].astype(BF16)
+
+
+def conv_term_kernel(flags, patches, saved_t, *refs):
+    split_refs, late, full_ref = refs[:-2], refs[-2], refs[-1]
+    depths, channels = saved_t.shape[:2]
     split = late.shape[0]
     for k in range(depths):
-        flat = saved[:, k].reshape(images * height * width, channels)
-        flat_t = flat.T
         for n in range(9):
             part = jnp.dot(
-                flat_t, patch_ref[:, pl.ds(n * channels, channels)], preferred_element_type=F32
+                saved_t[k], patches[:, pl.ds(n * channels, channels)], preferred_element_type=F32
             ).astype(BF16)
             at = (k * 9 + n) * channels
             if at < split:
@@ -163,6 +170,12 @@
             else:
                 full_ref[at - split : at - split + channels, :] = part
     deal(full_ref, split_refs, flags[7])
+
+
+def turn_kernel(value, out):
+    depths, channels, count = out.shape
+    for k in range(depths):
+        out[k] = value[:, k].reshape(count, channels).T
 
 
 def deal(full_ref, split_refs, mine):
@@ -190,17 +203,24 @@
         flip = second == 1
         for n in range(2):
             value = jnp.where(row_odd, below[n], above[n]) if flip else jnp.where(row_odd, above[n], below[n])
-            low, high = value[:, :HALO], value[:, width2 - HALO :]
-            outs[3 * second][:, n] = value.astype(BF16)
-            outs[3 * second + 1][:, n] = jnp.where(col_odd, low, high).astype(BF16)
-            outs[3 * second + 2][:, n] = jnp.where(col_odd, high, low).astype(BF16)
+            outs[second][:, n] = value.astype(BF16)
     low, high = cot[:, :, :HALO].astype(F32), cot[:, :, width2 - HALO :].astype(F32)
     outs[-2][...] = jnp.where(col_odd, low, high).astype(BF16)
     outs[-1][...] = jnp.where(col_odd, high, low).astype(BF16)
 
 
+def corner_kernel(flags, *refs):
+    col_odd = flags[1] == 1
+    for n in range(len(refs) // 3):
+        rows, first, second = refs[n], refs[len(refs) // 3 + 2 * n], refs[len(refs) // 3 + 2 * n + 1]
+        low = rows[:, :, :HALO].astype(F32)
+        high = rows[:, :, rows.shape[2] - HALO :].astype(F32)
+        first[...] = jnp.where(col_odd, low, high).astype(BF16)
+        second[...] = jnp.where(col_odd, high, low).astype(BF16)
+
+
 def proj_term_kernel(flags, *refs):
-    came, (feats, conv_late) = refs[:TILE_COLS], refs[TILE_COLS : TILE_COLS + 2]
+    came, (feats_t, conv_late) = refs[:TILE_COLS], refs[TILE_COLS : TILE_COLS + 2]
     split_refs, tokens, full_ref = refs[TILE_COLS + 2 : -2], refs[-2], refs[-1]
     images, depths, width, channels = came[0].shape
     gray = flags[6]
@@ -211,12 +231,9 @@
             for i in range(images):
                 at = pl.multiple_of((i * TILE_COLS + column) * width, width)
                 tokens[k, pl.ds(at, width), :] = came[apart][i, k]
-    dim = feats.shape[3]
+    dim = feats_t.shape[1]
     for k in range(depths):
-        flat = feats[:, k].reshape(images * feats.shape[2], dim)
-        part = lax.dot_general(
-            flat, tokens[k], (((0,), (0,)), ((), ())), preferred_element_type=F32
-        )
+        part = jnp.dot(feats_t[k], tokens[k], preferred_element_type=F32)
         full_ref[k * dim : (k + 1) * dim, :] = part.astype(BF16)
     full_ref[depths * dim :, :] = conv_late[...]
     deal(full_ref, split_refs, flags[7])
@@ -253,8 +270,8 @@
             out[q] = total.astype(out.dtype)
 
 
-def last_kernel(parts, flags, *refs):
-    early, late, (sent, kept) = refs[:parts], refs[parts : 2 * parts], refs[2 * parts :]
+def last_kernel(early_parts, late_parts, flags, *refs):
+    early, late, (sent, kept) = refs[:early_parts], refs[early_parts:-2], refs[-2:]
     first = flags[8] == 0
     sums = []
     for group in (early, late):
@@ -274,19 +291,28 @@
     out[:, pl.ds(at, width)] = came[...].astype(F32) * scale
 
 
-def vmem_call(kernel, out_shape, operands, scratch=(), scalars=1, flops=0, limit=16):
+def vmem_call(kernel, out_shape, operands, scratch=(), scalars=1, flops=0, limit=16, hbm=(), after=()):
     whole = pl.BlockSpec(memory_space=pltpu.VMEM)
+    specs = [pl.BlockSpec(memory_space=pltpu.SMEM)] * scalars + [whole] * (len(operands) - scalars)
+    for n in hbm:
+        specs[n] = pl.BlockSpec(memory_space=pltpu.HBM)
+    specs += [pl.BlockSpec(memory_space=pl.ANY)] * len(after)
+    count = len(operands)
+
+    def run(*refs):
+        kernel(*refs[:count], *refs[count + len(after) :])
+
     moved = sum(a.size * a.dtype.itemsize for a in operands)
     moved += sum(math.prod(s.shape) * s.dtype.itemsize for s in jax.tree.leaves(out_shape))
     return pl.pallas_call(
-        kernel,
+        run,
         out_shape=out_shape,
-        in_specs=[pl.BlockSpec(memory_space=pltpu.SMEM)] * scalars + [whole] * (len(operands) - scalars),
+        in_specs=specs,
         out_specs=jax.tree.map(lambda _: whole, out_shape),
         scratch_shapes=list(scratch),
         compiler_params=pltpu.CompilerParams(vmem_limit_bytes=limit << 20),
         cost_estimate=pl.CostEstimate(flops=flops, bytes_accessed=moved, transcendentals=0),
-    )(*operands)
+    )(*operands, *after)
 
 
 def sds(*shape, dtype=BF16):
@@ -303,36 +329,36 @@
     return lax.ppermute(block, ("dp", "tile"), route)
 
 
-def scatter_sum(dealt, flags, core):
-    tiles = lax.axis_size("tile")
+def core_sum(dealt, core):
     if len(dealt) == 1:
+        tiles = lax.axis_size("tile")
         pairs = dealt[0].reshape(tiles // 2, 2, dealt[0].shape[0] // tiles, dealt[0].shape[1])
         kept = lax.dynamic_index_in_dim(pairs, core, 1, keepdims=False)
         sent = lax.dynamic_index_in_dim(pairs, 1 - core, 1, keepdims=False)
     else:
         kept, sent = dealt
-    parts = [kept, xor_move(sent, 1, False)]
-    total_bits = tiles.bit_length() - 1
-    at = 1
-    while at < total_bits:
-        by_columns = at == 1
-        bits = 1 if by_columns else min(2, total_bits - at)
-        span = 1 << bits
-        count, rows, channels = parts[0].shape
-        if by_columns:
-            channels //= 2
-        outs = [
-            sds(count // span, rows, channels, dtype=F32 if n == 0 else BF16)
-            for n in range(span * (2 if by_columns else 1))
-        ]
-        pieces = vmem_call(
-            functools.partial(round_kernel, len(parts), at, bits, by_columns), outs, [flags] + parts
-        )
-        parts = [pieces[0]] + [
-            xor_move(pieces[n], (n % span) << at, n >= span) for n in range(1, len(pieces))
-        ]
-        at += bits
-    return parts
+    return [kept, xor_move(sent, 1, False)]
+
+
+def deal_round(parts, flags, at, bits, by_columns):
+    span = 1 << bits
+    count, rows, channels = parts[0].shape
+    if by_columns:
+        channels //= 2
+    outs = [
+        sds(count // span, rows, channels, dtype=F32 if n == 0 else BF16)
+        for n in range(span * (2 if by_columns else 1))
+    ]
+    return vmem_call(
+        functools.partial(round_kernel, len(parts), at, bits, by_columns), outs, [flags] + parts
+    )
+
+
+def send_round(pieces, at, bits):
+    span = 1 << bits
+    return [pieces[0]] + [
+        xor_move(pieces[n], (n % span) << at, n >= span) for n in range(1, len(pieces))
+    ]
 
 
 def per_device(features, proj_weight, conv_weight, saved, cotangent):
@@ -359,23 +385,26 @@
 
     row_first, row_second = paired(rows, 0), paired(rows, 1)
     col_first, col_second = paired(TILE_COLS, 0), paired(TILE_COLS, 1)
-    strip = [sds(images, 2, width2, channels)] + [sds(images, 2, HALO, channels)] * 2
+    sides = 2 if has_second else 1
     edges = vmem_call(
         functools.partial(pack_kernel, has_second),
-        strip * (2 if has_second else 1) + [sds(images, height2, HALO, channels)] * 2,
+        [sds(images, 2, width2, channels)] * sides + [sds(images, height2, HALO, channels)] * 2,
         (flags, cotangent),
     )
     row_a = swap(edges[0], row_first, None)
     col_b = swap(edges[-1], None, col_second)
     col_a = swap(edges[-2], None, col_first)
-    ab = swap(edges[2], row_first, col_second)
-    aa = swap(edges[1], row_first, col_first)
+    row_b = swap(edges[1], row_second, None) if has_second else row_a
+    came_rows = [row_a, row_b][:sides]
+    corners = vmem_call(corner_kernel, [sds(images, 2, HALO, channels)] * (2 * sides), [flags] + came_rows)
+    aa, ab = swap(corners[0], None, col_first), swap(corners[1], None, col_second)
     if has_second:
-        row_b = swap(edges[3], row_second, None)
-        bb = swap(edges[5], row_second, col_second)
-        ba = swap(edges[4], row_second, col_first)
+        ba, bb = swap(corners[2], None, col_first), swap(corners[3], None, col_second)
     else:
-        row_b, ba, bb = row_a, aa, ab
+        ba, bb = aa, ab
+    tokens = features.shape[2]
+    saved_t = vmem_call(turn_kernel, sds(depths, channels, patches), (saved,), scalars=0)
+    feats_t = vmem_call(turn_kernel, sds(depths, dim, images * tokens), (features,), scalars=0)
     half_rows = depths * (dim + 9 * channels) // 2
     conv_late = half_rows - depths * dim
     block_rows = half_rows // tile_count
@@ -386,29 +415,41 @@
     conv_flops = 2 * patches * depths * 9 * channels * channels
     outs = vmem_call(
         functools.partial(pool_conv_kernel, has_second),
-        [sds(images, depths, width, channels)] * height + dealt + [sds(conv_late, channels)],
-        (flags, cotangent, row_a, row_b, col_a, col_b, aa, ab, ba, bb, conv_weight, saved),
+        [sds(images, depths, width, channels)] * height + [sds(patches, 9 * channels)],
+        (flags, cotangent, row_a, row_b, col_a, col_b, aa, ab, ba, bb, conv_weight),
         scratch=(
             pltpu.VMEM((channels // 128, height + 2, LEFT + width2 + 16, 128), F32),
             pltpu.VMEM((height + 2, width + 8, channels), F32),
-            pltpu.VMEM((patches, 9 * channels), BF16),
             pltpu.VMEM((patches, channels), F32),
-            pltpu.VMEM((half_rows, channels), BF16),
+            pltpu.VMEM(conv_weight.shape, BF16),
+            pltpu.SemaphoreType.DMA((depths,)),
         ),
-        flops=2 * conv_flops,
-    )
-    igs, early, late = outs[:height], outs[height:-1], outs[-1]
+        flops=conv_flops,
+        hbm=(10,),
+    )
+    igs, windows = outs[:height], outs[height]
     came = [igs[0]] + [xor_move(igs[apart], apart, False) for apart in range(1, height)]
-    early_parts = scatter_sum(early, flags, position % 2)
-    tokens = features.shape[2]
+    *early, conv_top = vmem_call(
+        conv_term_kernel,
+        dealt + [sds(conv_late, channels)],
+        (flags, windows, saved_t),
+        scratch=(pltpu.VMEM((half_rows, channels), BF16),),
+        flops=conv_flops,
+    )
+    early_parts = core_sum(early, position % 2)
+    early_pieces = deal_round(early_parts, flags, 1, 0, True)
     proj_flops = 2 * images * tokens * depths * dim * channels
     *terms, token_grad = vmem_call(
         proj_term_kernel,
         dealt + [sds(depths, images * tokens, channels)],
-        [flags] + came + [features, late],
+        [flags] + came + [feats_t, conv_top],
         scratch=(pltpu.VMEM((half_rows, channels), BF16),),
         flops=proj_flops,
-    )
+        after=(early_pieces[0],),
+    )
+    early_parts = send_round(early_pieces, 1, 0)
+    for bit in range(1, bits):
+        early_parts = send_round(deal_round(early_parts, flags, bit, 1, False), bit, 1)
     feature_grad = vmem_call(
         feat_grad_kernel,
         sds(images, depths, tokens, dim),
@@ -416,10 +457,15 @@
         scalars=0,
         flops=proj_flops,
     )
-    late_parts = scatter_sum(terms, flags, position % 2)
+    late_parts = core_sum(terms, position % 2)
+    at = 1
+    while at < bits:
+        step = 1 if at == 1 else min(2, bits - at)
+        late_parts = send_round(deal_round(late_parts, flags, at, step, at == 1), at, step)
+        at += step
     half = sds(block_rows, channels // 2)
     sent, kept = vmem_call(
-        functools.partial(last_kernel, len(early_parts)),
+        functools.partial(last_kernel, len(early_parts), len(late_parts)),
         [half, sds(block_rows, channels // 2, dtype=F32)],
         [flags] + early_parts + late_parts,
     )

time: 78.2 us -> 88.6 us (1.13)
  waiting for transfers between devices: 22.5 us -> 33.8 us
  starting transfers between devices: 37.3 us -> 31.4 us
  Pallas kernels: 13.3 us -> 18.3 us
    ppermute x3, waiting for transfers between devices: 0.59 us -> 11.2 us  [xor_move(): return lax.ppermute(block, 'dp', [(0, 1), (1, 0)])]
    ppermute x2 -> x1, waiting for transfers between devices: 6.13 us -> 0.01 us  [xor_move(): return lax.ppermute(block, ('dp', 'tile'), route)]
    pallas_call x10 -> x16, Pallas kernels: 13.3 us -> 18.3 us  [vmem_call(): pl.pallas_call(run, out_shape=out_shape, in_specs=specs, out_specs=jax.tr...]
    ppermute x2 -> x1, starting transfers between devices: 3.74 us -> 0.25 us  [xor_move(): return lax.ppermute(block, ('dp', 'tile'), route)]
    ppermute x5, waiting for transfers between devices: 2.21 us -> 5.65 us  [swap(): return lax.ppermute(block, 'tile', tile_route(row_pairs, col_pairs, rows))]
    ppermute x17 -> x16, waiting for transfers between devices: 13.5 us -> 16.9 us  [xor_move(): return lax.ppermute(block, 'tile', [(t, t ^ apart) for t in range(tiles)])]
    ppermute x5, starting transfers between devices: 8.53 us -> 5.49 us  [swap(): return lax.ppermute(block, 'tile', tile_route(row_pairs, col_pairs, rows))]
    ppermute x17 -> x16, starting transfers between devices: 20.5 us -> 21.1 us  [xor_move(): return lax.ppermute(block, 'tile', [(t, t ^ apart) for t in range(tiles)])]
  transfers between devices with their start and end apart: 27 -> 25, of which waited for: 14 -> 10; matrix products, arithmetic and copies ran while one was open for 0% -> 0% of each run, Pallas kernels for 8% -> 8%
where the time goes in v3:
time: 88.6 us; the launch traced here: 88.4 us
  waiting for transfers between devices  33.8 us (38%)
  starting transfers between devices  31.4 us (35%)
  Pallas kernels  18.3 us (21%)
  local copies, waits for them, and re-layouts  4.03 us (5%)
  between operations  0.94 us (1%)
    ppermute x16, starting transfers between devices, xor_move(): return lax.ppermute(block, 'tile', [(t, t ^ apart) for t in range(tiles)])  21.1 us
    pallas_call x16, Pallas kernels, vmem_call(): pl.pallas_call(run, out_shape=out_shape, in_specs=specs, out_specs=jax.tr...  18.3 us
    ppermute x16, waiting for transfers between devices, xor_move(): return lax.ppermute(block, 'tile', [(t, t ^ apart) for t in range(tiles)])  16.9 us
    ppermute x3, waiting for transfers between devices, xor_move(): return lax.ppermute(block, 'dp', [(0, 1), (1, 0)])  11.2 us
    ppermute x5, waiting for transfers between devices, swap(): return lax.ppermute(block, 'tile', tile_route(row_pairs, col_pairs, rows))  5.65 us
    ppermute x5, starting transfers between devices, swap(): return lax.ppermute(block, 'tile', tile_route(row_pairs, col_pairs, rows))  5.49 us
    ppermute x3, starting transfers between devices, xor_move(): return lax.ppermute(block, 'dp', [(0, 1), (1, 0)])  4.57 us
    unnamed x12, local copies, waits for them, and re-layouts  3.94 us
  transfers between devices with their start and end apart: 25, of which 10 were waited for; matrix products, arithmetic and copies ran while one was open for 0% of the time, Pallas kernels for 8%

profile of v3, /device:TPU:0, one launch (start us, length us, event | category | flops | bytes accessed | tf_op | source)
XLA Modules:
  0.0 88.4 jit_solution(3570543417693877490)
XLA Ops:
  0.7 0.1 stack.71.refs_0_
  0.8 0.0 copy-start.2
  0.8 1.2 %copy-done.2 = bf16[4,16,32,256]{3,2,1,0:T(8,128)(2,1)S(1)} copy-done((bf16[4,16,32,256]{3,2,1,0:T(8,128)(2,1)S(1)}, bf16[4,16,32,256]{3,2,1,0:T(8,128)(2,1)}, u32[]{:S(2)}) %copy-start.2) | copy-done | bytes 1048600
  2.0 0.8 shard_map.68
  2.8 4.1 %collective-permute-start = (bf16[4,2,32,256]{3,2,1,0:T(8,128)(2,1)S(1)}, bf16[4,2,32,256]{3,2,1,0:T(8,128)(2,1)S(1)}, u32[]{:S(2)}, u32[]{:S(2)}) collective-permute-start(bf16[4,2,32,256]{3,2,1,0:T(8,128)(2,1)S(1)} %get-tuple-element.40), channel_id=1, source_target_pairs={{0,8},{1,9},{3,11},{2,10},{6,14},{7,15},{5,13},{4,12},{8,0},{9,1},... | collective-permute-start | bytes 393224 | tf_op jit(solution)/shard_map/ppermute | solution.py:384
  6.9 0.7 collective-permute-start.2
  7.6 5.6 %collective-permute-done.refs_1_.refs_2_.refs_3_ = bf16[4,2,32,256]{3,2,1,0:T(8,128)(2,1)S(1)} collective-permute-done((bf16[4,2,32,256]{3,2,1,0:T(8,128)(2,1)S(1)}, bf16[4,2,32,256]{3,2,1,0:T(8,128)(2,1)S(1)}, u32[]{:S(2)}, u32[]{:S(2)}) %collective-permute-start) | collective-permute-done | bytes 131104 | tf_op jit(solution)/shard_map/ppermute | solution.py:384
  13.2 0.6 shard_map.69
  13.8 0.1 collective-permute-start.3
  13.9 0.7 collective-permute-start.4
  14.5 0.0 copy-start.4
  14.5 1.0 %copy-done.4 = bf16[4,2,8,16,256]{4,3,2,1,0:T(8,128)(2,1)S(1)} copy-done((bf16[4,2,8,16,256]{4,3,2,1,0:T(8,128)(2,1)S(1)}, bf16[4,2,8,16,256]{4,3,2,1,0:T(8,128)(2,1)}, u32[]{:S(2)}) %copy-start.4) | copy-done | bytes 524312
  15.6 0.2 shard_map.72.refs_2_
  15.8 0.0 collective-permute-done.2.refs_5_
  15.8 0.0 copy-start.5
  15.8 1.7 %copy-done.5 = bf16[2,3,3,256,256]{4,3,2,1,0:T(8,128)(2,1)S(1)} copy-done((bf16[2,3,3,256,256]{4,3,2,1,0:T(8,128)(2,1)S(1)}, bf16[2,3,3,256,256]{4,3,2,1,0:T(8,128)(2,1)}, u32[]{:S(2)}) %copy-start.5) | copy-done | bytes 2359320
  17.5 4.9 %shard_map.70 = (bf16[4,2,16,256]{3,2,1,0:T(8,128)(2,1)S(1)}, bf16[4,2,16,256]{3,2,1,0:T(8,128)(2,1)S(1)}, bf16[4,2,16,256]{3,2,1,0:T(8,128)(2,1)S(1)}, bf16[4,2...) custom-call(s32[13]{0:T(128)S(1)} %stack.71.refs_0_, ...), custom_call_target="tpu_custom_call" | custom-call | flops 1207959552 | bytes 6881332 | tf_op jit(solution)/shard_map/pallas_call | solution.py:307
  22.4 0.0 copy-start
  22.4 2.0 %shard_map.73 = (bf16[8,208,256]{2,1,0:T(8,128)(2,1)S(1)}, bf16[8,208,256]{2,1,0:T(8,128)(2,1)S(1)}, bf16[1280,256]{1,0:T(8,128)(2,1)S(1)}) custom-call(s32[13]{0:T(128)S(1)} %stack.71.refs_0_, bf16[512,2304]{1,0:T(8,128)(2,1)S(1)} %get-tuple-element.53.refs_1_, bf16[2,256,512]{2,1,0:T(8,128)(2,1)S(1)} %shard_map.72.refs_2_), custom_call_target="tpu_custom_call" | custom-call | flops 1207959552 | bytes 5242932 | tf_op jit(solution)/shard_map/pallas_call | solution.py:307
  24.5 3.2 %collective-permute-start.12 = (bf16[8,208,256]{2,1,0:T(8,128)(2,1)S(1)}, bf16[8,208,256]{2,1,0:T(8,128)(2,1)S(1)}, u32[]{:S(2)}, u32[]{:S(2)}) collective-permute-start(bf16[8,208,256]{2,1,0:T(8,128)(2,1)S(1)} %get-tuple-element.56), channel_id=1, source_target_pairs={{0,1},{1,0},{2,3},{3,2},{4,5},{5,4},{6,7},{7,6},{8,9},{9,8},{10,11... | collective-permute-start | bytes 2555912 | tf_op jit(solution)/shard_map/ppermute | solution.py:325
  27.7 2.4 %collective-permute-start.10 = (bf16[4,2,16,256]{3,2,1,0:T(8,128)(2,1)S(1)}, bf16[4,2,16,256]{3,2,1,0:T(8,128)(2,1)S(1)}, u32[]{:S(2)}, u32[]{:S(2)}) collective-permute-start(bf16[4,2,16,256]{3,2,1,0:T(8,128)(2,1)S(1)} %get-tuple-element.51), channel_id=1, source_target_pairs={{0,6},{1,7},{2,4},{3,5},{4,2},{5,3},{6,0},{7,1},{8,14},{9,15},{10,... | collective-permute-start | bytes 196616 | tf_op jit(solution)/shard_map/ppermute | solution.py:325
  30.0 0.1 collective-permute-start.11
  30.1 0.6 collective-permute-start.5
  30.7 2.3 %collective-permute-start.6 = (bf16[4,2,16,256]{3,2,1,0:T(8,128)(2,1)S(1)}, bf16[4,2,16,256]{3,2,1,0:T(8,128)(2,1)S(1)}, u32[]{:S(2)}, u32[]{:S(2)}) collective-permute-start(bf16[4,2,16,256]{3,2,1,0:T(8,128)(2,1)S(1)} %get-tuple-element.47), channel_id=1, source_target_pairs={{0,2},{1,3},{2,0},{3,1},{4,6},{5,7},{6,4},{7,5},{8,10},{9,11},{10,... | collective-permute-start | bytes 196616 | tf_op jit(solution)/shard_map/ppermute | solution.py:325
  33.0 0.0 collective-permute-done.10.refs_7_
  33.0 1.6 %collective-permute-start.7 = (bf16[4,2,16,256]{3,2,1,0:T(8,128)(2,1)S(1)}, bf16[4,2,16,256]{3,2,1,0:T(8,128)(2,1)S(1)}, u32[]{:S(2)}, u32[]{:S(2)}) collective-permute-start(bf16[4,2,16,256]{3,2,1,0:T(8,128)(2,1)S(1)} %get-tuple-element.48), channel_id=1, source_target_pairs={{0,3},{1,2},{2,1},{3,0},{4,7},{5,6},{6,5},{7,4},{8,11},{9,10},{10,... | collective-permute-start | bytes 196616 | tf_op jit(solution)/shard_map/ppermute | solution.py:325
  34.6 0.5 collective-permute-done.11.refs_8_
  35.1 1.4 %collective-permute-start.8 = (bf16[4,2,16,256]{3,2,1,0:T(8,128)(2,1)S(1)}, bf16[4,2,16,256]{3,2,1,0:T(8,128)(2,1)S(1)}, u32[]{:S(2)}, u32[]{:S(2)}) collective-permute-start(bf16[4,2,16,256]{3,2,1,0:T(8,128)(2,1)S(1)} %get-tuple-element.49), channel_id=1, source_target_pairs={{0,4},{1,5},{2,6},{3,7},{4,0},{5,1},{6,2},{7,3},{8,12},{9,13},{10,... | collective-permute-start | bytes 196616 | tf_op jit(solution)/shard_map/ppermute | solution.py:325
  36.5 0.8 collective-permute-start.9
  37.2 0.6 shard_map.71.refs_9_
  37.8 0.7 shard_map.74
  38.6 0.0 collective-permute-done.6.refs_3_
  38.6 0.0 collective-permute-done.7.refs_4_
  38.6 1.4 %collective-permute-done.8.refs_5_ = bf16[4,2,16,256]{3,2,1,0:T(8,128)(2,1)S(1)} collective-permute-done((bf16[4,2,16,256]{3,2,1,0:T(8,128)(2,1)S(1)}, bf16[4,2,16,256]{3,2,1,0:T(8,128)(2,1)S(1)}, u32[]{:S(2)}, u32[]{:S(2)}) %collective-permute-start.8) | collective-permute-done | bytes 65568 | tf_op jit(solution)/shard_map/ppermute | solution.py:325
  40.0 1.1 %collective-permute-done.9.refs_6_ = bf16[4,2,16,256]{3,2,1,0:T(8,128)(2,1)S(1)} collective-permute-done((bf16[4,2,16,256]{3,2,1,0:T(8,128)(2,1)S(1)}, bf16[4,2,16,256]{3,2,1,0:T(8,128)(2,1)S(1)}, u32[]{:S(2)}, u32[]{:S(2)}) %collective-permute-start.9) | collective-permute-done | bytes 65568 | tf_op jit(solution)/shard_map/ppermute | solution.py:325
  41.1 1.4 %shard_map.75 = (bf16[8,208,256]{2,1,0:T(8,128)(2,1)S(1)}, bf16[8,208,256]{2,1,0:T(8,128)(2,1)S(1)}, bf16[2,512,256]{2,1,0:T(8,128)(2,1)S(1)}) custom-call(s32[13]{0:T(128)S(1)} %stack.71.refs_0_, bf16[4,2,16,256]{3,2,1,0:T(8,128)(2,1)S(1)} %get-tuple-element.45.refs_1_, bf16[4,2,16,256]{3,2,1,0:T(8,128)(2,1)S(1)} %collective-permute-done.5.refs_2_, ...), custom_call_target="tpu_custom_call" | custom-call | flops 536870912 | bytes 5505076 | tf_op jit(solution)/shard_map/pallas_call | solution.py:307
  42.5 0.2 collective-permute-start.17
  42.7 1.5 %collective-permute-start.13 = (bf16[8,208,128]{2,1,0:T(8,128)(2,1)S(1)}, bf16[8,208,128]{2,1,0:T(8,128)(2,1)S(1)}, u32[]{:S(2)}, u32[]{:S(2)}) collective-permute-start(bf16[8,208,128]{2,1,0:T(8,128)(2,1)S(1)} %get-tuple-element.59), channel_id=1, source_target_pairs={{0,16},{16,0},{1,17},{17,1},{2,18},{18,2},{3,19},{19,3},{4,20},{20... | collective-permute-start | bytes 1277960 | tf_op jit(solution)/shard_map/ppermute | solution.py:327
  44.2 10.6 %collective-permute-done.13.refs_2_ = bf16[8,208,128]{2,1,0:T(8,128)(2,1)S(1)} collective-permute-done((bf16[8,208,128]{2,1,0:T(8,128)(2,1)S(1)}, bf16[8,208,128]{2,1,0:T(8,128)(2,1)S(1)}, u32[]{:S(2)}, u32[]{:S(2)}) %collective-permute-start.13) | collective-permute-done | bytes 426016 | tf_op jit(solution)/shard_map/ppermute | solution.py:327
  54.8 0.6 shard_map.77
  55.5 0.0 copy-start.1
  55.5 0.4 collective-permute-start.14
  55.9 0.0 collective-permute-done.17.refs_2_
  55.9 0.7 shard_map.80
  56.6 1.8 %collective-permute-start.18 = (bf16[4,208,128]{2,1,0:T(8,128)(2,1)S(1)}, bf16[4,208,128]{2,1,0:T(8,128)(2,1)S(1)}, u32[]{:S(2)}, u32[]{:S(2)}) collective-permute-start(bf16[4,208,128]{2,1,0:T(8,128)(2,1)S(1)} %get-tuple-element.69), channel_id=1, source_target_pairs={{0,2},{1,3},{2,0},{3,1},{4,6},{5,7},{6,4},{7,5},{8,10},{9,11},{10,... | collective-permute-start | bytes 638984 | tf_op jit(solution)/shard_map/ppermute | solution.py:325
  58.4 1.5 %collective-permute-start.19 = (bf16[4,208,128]{2,1,0:T(8,128)(2,1)S(1)}, bf16[4,208,128]{2,1,0:T(8,128)(2,1)S(1)}, u32[]{:S(2)}, u32[]{:S(2)}) collective-permute-start(bf16[4,208,128]{2,1,0:T(8,128)(2,1)S(1)} %get-tuple-element.70), channel_id=1, source_target_pairs={{0,16},{16,0},{1,17},{17,1},{2,18},{18,2},{3,19},{19,3},{4,20},{20... | collective-permute-start | bytes 638984 | tf_op jit(solution)/shard_map/ppermute | solution.py:327
  59.9 0.3 collective-permute-start.20
  60.1 5.0 %collective-permute-done.14.refs_2_ = bf16[4,208,128]{2,1,0:T(8,128)(2,1)S(1)} collective-permute-done((bf16[4,208,128]{2,1,0:T(8,128)(2,1)S(1)}, bf16[4,208,128]{2,1,0:T(8,128)(2,1)S(1)}, u32[]{:S(2)}, u32[]{:S(2)}) %collective-permute-start.14) | collective-permute-done | bytes 213024 | tf_op jit(solution)/shard_map/ppermute | solution.py:325
  65.2 0.6 shard_map.78
  65.8 0.1 collective-permute-start.15
  65.8 5.3 %collective-permute-done.15.refs_2_ = bf16[2,208,128]{2,1,0:T(8,128)(2,1)S(1)} collective-permute-done((bf16[2,208,128]{2,1,0:T(8,128)(2,1)S(1)}, bf16[2,208,128]{2,1,0:T(8,128)(2,1)S(1)}, u32[]{:S(2)}, u32[]{:S(2)}) %collective-permute-start.15) | collective-permute-done | bytes 106528 | tf_op jit(solution)/shard_map/ppermute | solution.py:325
  71.1 0.6 shard_map.79
  71.7 1.7 %collective-permute-start.16 = (bf16[1,208,128]{2,1,0:T(8,128)(2,1)S(1)}, bf16[1,208,128]{2,1,0:T(8,128)(2,1)S(1)}, u32[]{:S(2)}, u32[]{:S(2)}) collective-permute-start(bf16[1,208,128]{2,1,0:T(8,128)(2,1)S(1)} %get-tuple-element.65), channel_id=1, source_target_pairs={{0,8},{1,9},{2,10},{3,11},{4,12},{5,13},{6,14},{7,15},{8,0},{9,1},... | collective-permute-start | bytes 159752 | tf_op jit(solution)/shard_map/ppermute | solution.py:325
  73.4 0.7 shard_map.81
  74.0 2.3 %collective-permute-start.21 = (bf16[1,208,128]{2,1,0:T(8,128)(2,1)S(1)}, bf16[1,208,128]{2,1,0:T(8,128)(2,1)S(1)}, u32[]{:S(2)}, u32[]{:S(2)}) collective-permute-start(bf16[1,208,128]{2,1,0:T(8,128)(2,1)S(1)} %get-tuple-element.73), channel_id=1, source_target_pairs={{0,4},{1,5},{2,6},{3,7},{4,0},{5,1},{6,2},{7,3},{8,12},{9,13},{10,... | collective-permute-start | bytes 159752 | tf_op jit(solution)/shard_map/ppermute | solution.py:325
  76.3 0.0 collective-permute-start.22
  76.3 2.4 %collective-permute-start.23 = (bf16[1,208,128]{2,1,0:T(8,128)(2,1)S(1)}, bf16[1,208,128]{2,1,0:T(8,128)(2,1)S(1)}, u32[]{:S(2)}, u32[]{:S(2)}) collective-permute-start(bf16[1,208,128]{2,1,0:T(8,128)(2,1)S(1)} %get-tuple-element.75), channel_id=1, source_target_pairs={{0,12},{1,13},{2,14},{3,15},{4,8},{5,9},{6,10},{7,11},{8,4},{9,5},... | collective-permute-start | bytes 159752 | tf_op jit(solution)/shard_map/ppermute | solution.py:325
  78.7 2.7 %collective-permute-done.22.refs_5_ = bf16[1,208,128]{2,1,0:T(8,128)(2,1)S(1)} collective-permute-done((bf16[1,208,128]{2,1,0:T(8,128)(2,1)S(1)}, bf16[1,208,128]{2,1,0:T(8,128)(2,1)S(1)}, u32[]{:S(2)}, u32[]{:S(2)}) %collective-permute-start.22) | collective-permute-done | bytes 53280 | tf_op jit(solution)/shard_map/ppermute | solution.py:325
  81.4 0.9 %collective-permute-done.23.refs_6_ = bf16[1,208,128]{2,1,0:T(8,128)(2,1)S(1)} collective-permute-done((bf16[1,208,128]{2,1,0:T(8,128)(2,1)S(1)}, bf16[1,208,128]{2,1,0:T(8,128)(2,1)S(1)}, u32[]{:S(2)}, u32[]{:S(2)}) %collective-permute-start.23) | collective-permute-done | bytes 53280 | tf_op jit(solution)/shard_map/ppermute | solution.py:325
  82.3 0.6 shard_map.82
  82.9 1.6 %collective-permute-start.24 = (bf16[208,128]{1,0:T(8,128)(2,1)S(1)}, bf16[208,128]{1,0:T(8,128)(2,1)S(1)}, u32[]{:S(2)}, u32[]{:S(2)}) collective-permute-start(bf16[208,128]{1,0:T(8,128)(2,1)S(1)} %get-tuple-element.77), channel_id=1, source_target_pairs={{0,16},{16,0},{1,17},{17,1},{2,18},{18,2},{3,19},{19,3},{4,20},{20... | collective-permute-start | bytes 159752 | tf_op jit(solution)/shard_map/ppermute | solution.py:327
  84.5 2.1 %shard_map.76 = bf16[4,2,128,1024]{3,2,1,0:T(8,128)(2,1)} custom-call(bf16[2,512,256]{2,1,0:T(8,128)(2,1)S(1)} %get-tuple-element.58.refs_0_, bf16[2,1024,256]{2,1,0:T(8,128)(2,1)S(1)} %copy-done.1), custom_call_target="tpu_custom_call" | custom-call | flops 536870912 | bytes 3670016 | tf_op jit(solution)/shard_map/pallas_call | solution.py:307
  86.6 0.6 collective-permute-done.24.refs_2_
  87.1 1.2 %shard_map.83 = f32[208,256]{1,0:T(8,128)} custom-call(s32[13]{0:T(128)S(1)} %stack.71.refs_0_, f32[208,128]{1,0:T(8,128)S(1)} %get-tuple-element.76.refs_1_, bf16[208,128]{1,0:T(8,128)(2,1)S(1)} %collective-permute-done.24.refs_2_), custom_call_target="tpu_custom_call" | custom-call | bytes 372788 | tf_op jit(solution)/shard_map/pallas_call | solution.py:307
  (15 shorter events, 0.0 us)
Async XLA Ops:
  0.8 1.2 %copy-start.2 = (bf16[4,16,32,256]{3,2,1,0:T(8,128)(2,1)S(1)}, bf16[4,16,32,256]{3,2,1,0:T(8,128)(2,1)}, u32[]{:S(2)}) copy-start(bf16[4,16,32,256]{3,2,1,0:T(8,128)(2,1)} %refs_1_.4) | copy-start | bytes 3145732
  2.0 13.8 %copy-start.3 = (bf16[4,16,32,256]{3,2,1,0:T(8,128)(2,1)S(1)}, bf16[4,16,32,256]{3,2,1,0:T(8,128)(2,1)}, u32[]{:S(2)}) copy-start(bf16[4,16,32,256]{3,2,1,0:T(8,128)(2,1)} %refs_1_.4) | copy-start | bytes 3145732
  2.8 10.4 %collective-permute-start = (bf16[4,2,32,256]{3,2,1,0:T(8,128)(2,1)S(1)}, bf16[4,2,32,256]{3,2,1,0:T(8,128)(2,1)S(1)}, u32[]{:S(2)}, u32[]{:S(2)}) collective-permute-start(bf16[4,2,32,256]{3,2,1,0:T(8,128)(2,1)S(1)} %get-tuple-element.40), channel_id=1, source_target_pairs={{0,8},{1,9},{3,11},{2,10},{6,14},{7,15},{5,13},{4,12},{8,0},{9,1},... | collective-permute-start | bytes 393224 | tf_op jit(solution)/shard_map/ppermute | solution.py:384
  6.9 8.9 %collective-permute-start.1 = (bf16[4,16,4,256]{3,2,1,0:T(4,128)(2,1)S(1)}, bf16[4,16,4,256]{3,2,1,0:T(4,128)(2,1)S(1)}, u32[]{:S(2)}, u32[]{:S(2)}) collective-permute-start(bf16[4,16,4,256]{3,2,1,0:T(4,128)(2,1)S(1)} %get-tuple-element.41), channel_id=1, source_target_pairs={{0,1},{1,0},{3,2},{2,3},{6,7},{7,6},{5,4},{4,5},{8,9},{9,8},{11,10... | collective-permute-start | bytes 393224 | tf_op jit(solution)/shard_map/ppermute | solution.py:384
  6.9 8.9 %collective-permute-start.2 = (bf16[4,16,4,256]{3,2,1,0:T(4,128)(2,1)S(1)}, bf16[4,16,4,256]{3,2,1,0:T(4,128)(2,1)S(1)}, u32[]{:S(2)}, u32[]{:S(2)}) collective-permute-start(bf16[4,16,4,256]{3,2,1,0:T(4,128)(2,1)S(1)} %get-tuple-element.42), channel_id=1, source_target_pairs={{1,3},{3,1},{2,6},{6,2},{7,5},{5,7},{9,11},{11,9},{10,14},{14,10},... | collective-permute-start | bytes 393224 | tf_op jit(solution)/shard_map/ppermute | solution.py:384
  13.8 2.0 %collective-permute-start.3 = (bf16[4,2,4,256]{3,2,1,0:T(4,128)(2,1)S(1)}, bf16[4,2,4,256]{3,2,1,0:T(4,128)(2,1)S(1)}, u32[]{:S(2)}, u32[]{:S(2)}) collective-permute-start(bf16[4,2,4,256]{3,2,1,0:T(4,128)(2,1)S(1)} %get-tuple-element.43), channel_id=1, source_target_pairs={{0,1},{1,0},{3,2},{2,3},{6,7},{7,6},{5,4},{4,5},{8,9},{9,8},{11,10... | collective-permute-start | bytes 49160 | tf_op jit(solution)/shard_map/ppermute | solution.py:384
  13.9 1.9 %collective-permute-start.4 = (bf16[4,2,4,256]{3,2,1,0:T(4,128)(2,1)S(1)}, bf16[4,2,4,256]{3,2,1,0:T(4,128)(2,1)S(1)}, u32[]{:S(2)}, u32[]{:S(2)}) collective-permute-start(bf16[4,2,4,256]{3,2,1,0:T(4,128)(2,1)S(1)} %get-tuple-element.44), channel_id=1, source_target_pairs={{1,3},{3,1},{2,6},{6,2},{7,5},{5,7},{9,11},{11,9},{10,14},{14,10},... | collective-permute-start | bytes 49160 | tf_op jit(solution)/shard_map/ppermute | solution.py:384
  14.5 1.0 %copy-start.4 = (bf16[4,2,8,16,256]{4,3,2,1,0:T(8,128)(2,1)S(1)}, bf16[4,2,8,16,256]{4,3,2,1,0:T(8,128)(2,1)}, u32[]{:S(2)}) copy-start(bf16[4,2,8,16,256]{4,3,2,1,0:T(8,128)(2,1)} %refs_0_.3) | copy-start | bytes 1572868
  15.8 1.7 %copy-start.5 = (bf16[2,3,3,256,256]{4,3,2,1,0:T(8,128)(2,1)S(1)}, bf16[2,3,3,256,256]{4,3,2,1,0:T(8,128)(2,1)}, u32[]{:S(2)}) copy-start(bf16[2,3,3,256,256]{4,3,2,1,0:T(8,128)(2,1)} %refs_10_.1) | copy-start | bytes 7077892
  22.4 14.8 %copy-start = (bf16[4,2,128,1024]{3,2,1,0:T(8,128)(2,1)S(1)}, bf16[4,2,128,1024]{3,2,1,0:T(8,128)(2,1)}, u32[]{:S(2)}) copy-start(bf16[4,2,128,1024]{3,2,1,0:T(8,128)(2,1)} %refs_0_.2) | copy-start | bytes 6291460
  24.5 12.0 %collective-permute-start.12 = (bf16[8,208,256]{2,1,0:T(8,128)(2,1)S(1)}, bf16[8,208,256]{2,1,0:T(8,128)(2,1)S(1)}, u32[]{:S(2)}, u32[]{:S(2)}) collective-permute-start(bf16[8,208,256]{2,1,0:T(8,128)(2,1)S(1)} %get-tuple-element.56), channel_id=1, source_target_pairs={{0,1},{1,0},{2,3},{3,2},{4,5},{5,4},{6,7},{7,6},{8,9},{9,8},{10,11... | collective-permute-start | bytes 2555912 | tf_op jit(solution)/shard_map/ppermute | solution.py:325
  27.7 5.4 %collective-permute-start.10 = (bf16[4,2,16,256]{3,2,1,0:T(8,128)(2,1)S(1)}, bf16[4,2,16,256]{3,2,1,0:T(8,128)(2,1)S(1)}, u32[]{:S(2)}, u32[]{:S(2)}) collective-permute-start(bf16[4,2,16,256]{3,2,1,0:T(8,128)(2,1)S(1)} %get-tuple-element.51), channel_id=1, source_target_pairs={{0,6},{1,7},{2,4},{3,5},{4,2},{5,3},{6,0},{7,1},{8,14},{9,15},{10,... | collective-permute-start | bytes 196616 | tf_op jit(solution)/shard_map/ppermute | solution.py:325
  30.0 5.0 %collective-permute-start.11 = (bf16[4,2,16,256]{3,2,1,0:T(8,128)(2,1)S(1)}, bf16[4,2,16,256]{3,2,1,0:T(8,128)(2,1)S(1)}, u32[]{:S(2)}, u32[]{:S(2)}) collective-permute-start(bf16[4,2,16,256]{3,2,1,0:T(8,128)(2,1)S(1)} %get-tuple-element.52), channel_id=1, source_target_pairs={{0,7},{1,6},{2,5},{3,4},{4,3},{5,2},{6,1},{7,0},{8,15},{9,14},{10,... | collective-permute-start | bytes 196616 | tf_op jit(solution)/shard_map/ppermute | solution.py:325
  30.1 8.5 %collective-permute-start.5 = (bf16[4,2,16,256]{3,2,1,0:T(8,128)(2,1)S(1)}, bf16[4,2,16,256]{3,2,1,0:T(8,128)(2,1)S(1)}, u32[]{:S(2)}, u32[]{:S(2)}) collective-permute-start(bf16[4,2,16,256]{3,2,1,0:T(8,128)(2,1)S(1)} %get-tuple-element.46), channel_id=1, source_target_pairs={{0,1},{1,0},{2,3},{3,2},{4,5},{5,4},{6,7},{7,6},{8,9},{9,8},{10,11... | collective-permute-start | bytes 196616 | tf_op jit(solution)/shard_map/ppermute | solution.py:325
  30.7 7.9 %collective-permute-start.6 = (bf16[4,2,16,256]{3,2,1,0:T(8,128)(2,1)S(1)}, bf16[4,2,16,256]{3,2,1,0:T(8,128)(2,1)S(1)}, u32[]{:S(2)}, u32[]{:S(2)}) collective-permute-start(bf16[4,2,16,256]{3,2,1,0:T(8,128)(2,1)S(1)} %get-tuple-element.47), channel_id=1, source_target_pairs={{0,2},{1,3},{2,0},{3,1},{4,6},{5,7},{6,4},{7,5},{8,10},{9,11},{10,... | collective-permute-start | bytes 196616 | tf_op jit(solution)/shard_map/ppermute | solution.py:325
  33.0 5.6 %collective-permute-start.7 = (bf16[4,2,16,256]{3,2,1,0:T(8,128)(2,1)S(1)}, bf16[4,2,16,256]{3,2,1,0:T(8,128)(2,1)S(1)}, u32[]{:S(2)}, u32[]{:S(2)}) collective-permute-start(bf16[4,2,16,256]{3,2,1,0:T(8,128)(2,1)S(1)} %get-tuple-element.48), channel_id=1, source_target_pairs={{0,3},{1,2},{2,1},{3,0},{4,7},{5,6},{6,5},{7,4},{8,11},{9,10},{10,... | collective-permute-start | bytes 196616 | tf_op jit(solution)/shard_map/ppermute | solution.py:325
  35.1 5.0 %collective-permute-start.8 = (bf16[4,2,16,256]{3,2,1,0:T(8,128)(2,1)S(1)}, bf16[4,2,16,256]{3,2,1,0:T(8,128)(2,1)S(1)}, u32[]{:S(2)}, u32[]{:S(2)}) collective-permute-start(bf16[4,2,16,256]{3,2,1,0:T(8,128)(2,1)S(1)} %get-tuple-element.49), channel_id=1, source_target_pairs={{0,4},{1,5},{2,6},{3,7},{4,0},{5,1},{6,2},{7,3},{8,12},{9,13},{10,... | collective-permute-start | bytes 196616 | tf_op jit(solution)/shard_map/ppermute | solution.py:325
  36.5 4.6 %collective-permute-start.9 = (bf16[4,2,16,256]{3,2,1,0:T(8,128)(2,1)S(1)}, bf16[4,2,16,256]{3,2,1,0:T(8,128)(2,1)S(1)}, u32[]{:S(2)}, u32[]{:S(2)}) collective-permute-start(bf16[4,2,16,256]{3,2,1,0:T(8,128)(2,1)S(1)} %get-tuple-element.50), channel_id=1, source_target_pairs={{0,5},{1,4},{2,7},{3,6},{4,1},{5,0},{6,3},{7,2},{8,13},{9,12},{10,... | collective-permute-start | bytes 196616 | tf_op jit(solution)/shard_map/ppermute | solution.py:325
  42.5 13.3 %collective-permute-start.17 = (bf16[8,208,256]{2,1,0:T(8,128)(2,1)S(1)}, bf16[8,208,256]{2,1,0:T(8,128)(2,1)S(1)}, u32[]{:S(2)}, u32[]{:S(2)}) collective-permute-start(bf16[8,208,256]{2,1,0:T(8,128)(2,1)S(1)} %get-tuple-element.67), channel_id=1, source_target_pairs={{0,1},{1,0},{2,3},{3,2},{4,5},{5,4},{6,7},{7,6},{8,9},{9,8},{10,11... | collective-permute-start | bytes 2555912 | tf_op jit(solution)/shard_map/ppermute | solution.py:325
  42.7 12.1 %collective-permute-start.13 = (bf16[8,208,128]{2,1,0:T(8,128)(2,1)S(1)}, bf16[8,208,128]{2,1,0:T(8,128)(2,1)S(1)}, u32[]{:S(2)}, u32[]{:S(2)}) collective-permute-start(bf16[8,208,128]{2,1,0:T(8,128)(2,1)S(1)} %get-tuple-element.59), channel_id=1, source_target_pairs={{0,16},{16,0},{1,17},{17,1},{2,18},{18,2},{3,19},{19,3},{4,20},{20... | collective-permute-start | bytes 1277960 | tf_op jit(solution)/shard_map/ppermute | solution.py:327
  55.5 29.0 %copy-start.1 = (bf16[2,1024,256]{2,1,0:T(8,128)(2,1)S(1)}, bf16[2,1024,256]{2,1,0:T(8,128)(2,1)}, u32[]{:S(2)}) copy-start(bf16[2,1024,256]{2,1,0:T(8,128)(2,1)} %refs_1_.5) | copy-start | bytes 3145732
  55.5 9.7 %collective-permute-start.14 = (bf16[4,208,128]{2,1,0:T(8,128)(2,1)S(1)}, bf16[4,208,128]{2,1,0:T(8,128)(2,1)S(1)}, u32[]{:S(2)}, u32[]{:S(2)}) collective-permute-start(bf16[4,208,128]{2,1,0:T(8,128)(2,1)S(1)} %get-tuple-element.61), channel_id=1, source_target_pairs={{0,2},{1,3},{2,0},{3,1},{4,6},{5,7},{6,4},{7,5},{8,10},{9,11},{10,... | collective-permute-start | bytes 638984 | tf_op jit(solution)/shard_map/ppermute | solution.py:325
  56.6 16.7 %collective-permute-start.18 = (bf16[4,208,128]{2,1,0:T(8,128)(2,1)S(1)}, bf16[4,208,128]{2,1,0:T(8,128)(2,1)S(1)}, u32[]{:S(2)}, u32[]{:S(2)}) collective-permute-start(bf16[4,208,128]{2,1,0:T(8,128)(2,1)S(1)} %get-tuple-element.69), channel_id=1, source_target_pairs={{0,2},{1,3},{2,0},{3,1},{4,6},{5,7},{6,4},{7,5},{8,10},{9,11},{10,... | collective-permute-start | bytes 638984 | tf_op jit(solution)/shard_map/ppermute | solution.py:325
  58.4 14.9 %collective-permute-start.19 = (bf16[4,208,128]{2,1,0:T(8,128)(2,1)S(1)}, bf16[4,208,128]{2,1,0:T(8,128)(2,1)S(1)}, u32[]{:S(2)}, u32[]{:S(2)}) collective-permute-start(bf16[4,208,128]{2,1,0:T(8,128)(2,1)S(1)} %get-tuple-element.70), channel_id=1, source_target_pairs={{0,16},{16,0},{1,17},{17,1},{2,18},{18,2},{3,19},{19,3},{4,20},{20... | collective-permute-start | bytes 638984 | tf_op jit(solution)/shard_map/ppermute | solution.py:327
  59.9 13.5 %collective-permute-start.20 = (bf16[4,208,128]{2,1,0:T(8,128)(2,1)S(1)}, bf16[4,208,128]{2,1,0:T(8,128)(2,1)S(1)}, u32[]{:S(2)}, u32[]{:S(2)}) collective-permute-start(bf16[4,208,128]{2,1,0:T(8,128)(2,1)S(1)} %get-tuple-element.71), channel_id=1, source_target_pairs={{0,18},{1,19},{2,16},{3,17},{4,22},{5,23},{6,20},{7,21},{8,26},{9,... | collective-permute-start | bytes 638984 | tf_op jit(solution)/shard_map/ppermute | solution.py:329
  65.8 5.3 %collective-permute-start.15 = (bf16[2,208,128]{2,1,0:T(8,128)(2,1)S(1)}, bf16[2,208,128]{2,1,0:T(8,128)(2,1)S(1)}, u32[]{:S(2)}, u32[]{:S(2)}) collective-permute-start(bf16[2,208,128]{2,1,0:T(8,128)(2,1)S(1)} %get-tuple-element.63), channel_id=1, source_target_pairs={{0,4},{1,5},{2,6},{3,7},{4,0},{5,1},{6,2},{7,3},{8,12},{9,13},{10,... | collective-permute-start | bytes 319496 | tf_op jit(solution)/shard_map/ppermute | solution.py:325
  71.7 7.1 %collective-permute-start.16 = (bf16[1,208,128]{2,1,0:T(8,128)(2,1)S(1)}, bf16[1,208,128]{2,1,0:T(8,128)(2,1)S(1)}, u32[]{:S(2)}, u32[]{:S(2)}) collective-permute-start(bf16[1,208,128]{2,1,0:T(8,128)(2,1)S(1)} %get-tuple-element.65), channel_id=1, source_target_pairs={{0,8},{1,9},{2,10},{3,11},{4,12},{5,13},{6,14},{7,15},{8,0},{9,1},... | collective-permute-start | bytes 159752 | tf_op jit(solution)/shard_map/ppermute | solution.py:325
  74.0 4.7 %collective-permute-start.21 = (bf16[1,208,128]{2,1,0:T(8,128)(2,1)S(1)}, bf16[1,208,128]{2,1,0:T(8,128)(2,1)S(1)}, u32[]{:S(2)}, u32[]{:S(2)}) collective-permute-start(bf16[1,208,128]{2,1,0:T(8,128)(2,1)S(1)} %get-tuple-element.73), channel_id=1, source_target_pairs={{0,4},{1,5},{2,6},{3,7},{4,0},{5,1},{6,2},{7,3},{8,12},{9,13},{10,... | collective-permute-start | bytes 159752 | tf_op jit(solution)/shard_map/ppermute | solution.py:325
  76.3 5.1 %collective-permute-start.22 = (bf16[1,208,128]{2,1,0:T(8,128)(2,1)S(1)}, bf16[1,208,128]{2,1,0:T(8,128)(2,1)S(1)}, u32[]{:S(2)}, u32[]{:S(2)}) collective-permute-start(bf16[1,208,128]{2,1,0:T(8,128)(2,1)S(1)} %get-tuple-element.74), channel_id=1, source_target_pairs={{0,8},{1,9},{2,10},{3,11},{4,12},{5,13},{6,14},{7,15},{8,0},{9,1},... | collective-permute-start | bytes 159752 | tf_op jit(solution)/shard_map/ppermute | solution.py:325
  76.3 6.0 %collective-permute-start.23 = (bf16[1,208,128]{2,1,0:T(8,128)(2,1)S(1)}, bf16[1,208,128]{2,1,0:T(8,128)(2,1)S(1)}, u32[]{:S(2)}, u32[]{:S(2)}) collective-permute-start(bf16[1,208,128]{2,1,0:T(8,128)(2,1)S(1)} %get-tuple-element.75), channel_id=1, source_target_pairs={{0,12},{1,13},{2,14},{3,15},{4,8},{5,9},{6,10},{7,11},{8,4},{9,5},... | collective-permute-start | bytes 159752 | tf_op jit(solution)/shard_map/ppermute | solution.py:325
  82.9 4.2 %collective-permute-start.24 = (bf16[208,128]{1,0:T(8,128)(2,1)S(1)}, bf16[208,128]{1,0:T(8,128)(2,1)S(1)}, u32[]{:S(2)}, u32[]{:S(2)}) collective-permute-start(bf16[208,128]{1,0:T(8,128)(2,1)S(1)} %get-tuple-element.77), channel_id=1, source_target_pairs={{0,16},{16,0},{1,17},{17,1},{2,18},{18,2},{3,19},{19,3},{4,20},{20... | collective-permute-start | bytes 159752 | tf_op jit(solution)/shard_map/ppermute | solution.py:327

commit v4 on v3

v4 whole, which is shorter than its diff:
```python
import functools
import math

import jax
import jax.numpy as jnp
from jax import lax
from jax.experimental import pallas as pl
from jax.experimental.pallas import tpu as pltpu
from jax.sharding import PartitionSpec as P

TILE_COLS = 8
HALO = 4
LEFT = 8
BF16 = jnp.bfloat16
F32 = jnp.float32
ROW_ODD, COL_ODD, TOP, BOTTOM, LEFT_END, RIGHT_END, CORE, DP, BITS = range(9)


def gray_of(column):
    return column ^ column >> 1


def column_of(code):
    return code ^ code >> 1 ^ code >> 2


def paired(count, first):
    pairs = []
    for low in range(first, count - 1, 2):
        pairs += [(low, low + 1), (low + 1, low)]
    return pairs


def tile_route(row_pairs, col_pairs, rows):
    row_moves = row_pairs if row_pairs is not None else [(r, r) for r in range(rows)]
    col_moves = col_pairs if col_pairs is not None else [(c, c) for c in range(TILE_COLS)]
    return [
        (r0 * TILE_COLS + gray_of(c0), r1 * TILE_COLS + gray_of(c1))
        for r0, r1 in row_moves
        for c0, c1 in col_moves
    ]


def nt_dot(left, right):
    return lax.dot_general(left, right, (((1,), (1,)), ((), ())), preferred_element_type=F32)


def column_pack_kernel(flags, cot, held, first, second, sems):
    col_odd = flags[COL_ODD] == 1
    images, _, width2, _ = cot.shape
    copies = [pltpu.make_async_copy(cot.at[i], held.at[i], sems.at[i]) for i in range(images)]
    for copy in copies:
        copy.start()
    for i in range(images):
        copies[i].wait()
        low, high = held[i, :, :HALO].astype(F32), held[i, :, width2 - HALO :].astype(F32)
        first[i] = jnp.where(col_odd, low, high).astype(BF16)
        second[i] = jnp.where(col_odd, high, low).astype(BF16)


def pool_columns(flags, held, col_a, col_b, wide, i, lines):
    width2, channels = held.shape[2:]
    width = width2 // 2
    col_odd, left, right = flags[COL_ODD] == 1, flags[LEFT_END] == 1, flags[RIGHT_END] == 1
    side = lax.broadcasted_iota(jnp.int32, (2, channels), 0)
    outside = jnp.logical_or(jnp.logical_and(side == 0, left), jnp.logical_and(side == 1, right))
    cells, beside = [], []
    for at, r in enumerate(lines):
        centre = held[i, r].astype(F32)
        one, two = col_a[i, r].astype(F32), col_b[i, r].astype(F32)
        before = jnp.where(left, jnp.broadcast_to(centre[:1], one.shape), jnp.where(col_odd, one, two))
        after = jnp.where(
            right, jnp.broadcast_to(centre[width2 - 1 :], one.shape), jnp.where(col_odd, two, one)
        )
        for h in range(channels // 128):
            lanes = slice(h * 128, (h + 1) * 128)
            wide[h, at, LEFT - HALO : LEFT, :] = before[:, lanes]
            wide[h, at, LEFT : LEFT + width2, :] = centre[:, lanes]
            wide[h, at, LEFT + width2 : LEFT + width2 + HALO, :] = after[:, lanes]
    for at in range(len(lines)):
        def taps(start, size, stride):
            got = [
                jnp.concatenate(
                    [wide[h, at, pl.ds(start + n, size, stride=stride), :] for h in range(channels // 128)], axis=1
                )
                for n in range(4)
            ]
            return 0.75 * (got[1] + got[2]) + 0.25 * (got[0] + got[3])

        cells.append(taps(LEFT - 1, width, 2))
        beside.append(jnp.where(outside, 0.0, taps(LEFT - 3, 2, 2 * width + 2)))
    return cells, beside


def place(cells, beside, pooled, window, at):
    width = cells.shape[0]
    pooled[LEFT : LEFT + width, :] = cells
    pooled[LEFT - 1 : LEFT, :] = beside[:1]
    pooled[LEFT + width : LEFT + width + 1, :] = beside[1:]
    for v in range(3):
        window[v, pl.ds(at, width), :] = pooled[pl.ds(LEFT + 1 - v, width), :].astype(BF16)


def row_pack_kernel(has_second, flags, held, col_a, col_b, *refs):
    outs, (cells_out, beside_out, wide, ends) = refs[: 2 if has_second else 1], refs[-4:]
    images, height2, width2, channels = held.shape
    width = width2 // 2
    row_odd = flags[ROW_ODD] == 1
    lines = [0, 1, 2, height2 - 3, height2 - 2, height2 - 1]
    for i in range(images):
        cells, beside = pool_columns(flags, held, col_a, col_b, wide, i, lines)
        for n in range(6):
            cells_out[i, n] = cells[n]
            beside_out[i, n] = beside[n]
        for group, is_end in ((cells, False), (beside, True)):
            above = [group[0], 0.75 * (group[0] + group[1]) + 0.25 * group[2]]
            below = [0.25 * group[3] + 0.75 * (group[4] + group[5]), group[5]]
            for second in range(len(outs)):
                for n in range(2):
                    odd, even = (below[n], above[n]) if second else (above[n], below[n])
                    value = jnp.where(row_odd, odd, even)
                    if is_end:
                        ends[second, (2 * i + n) * 2 : (2 * i + n) * 2 + 2, :] = value
                    else:
                        at = (2 * i + n) * width
                        outs[second][at : at + width, :] = value.astype(BF16)
    for second in range(len(outs)):
        outs[second][2 * images * width :, :] = ends[second].astype(BF16)


def main_kernel(
    flags, held, col_a, col_b, weight, saved, feats,
    window, acc, weight_out, saved_t, feats_t,
    wide, pooled, saved_in, feats_in, saved_flat, sems,
):
    images, height2, width2, channels = held.shape
    height, width = height2 // 2, width2 // 2
    depths = weight.shape[0]
    copies = [pltpu.make_async_copy(weight.at[k], weight_out.at[k], sems.at[k]) for k in range(depths)]
    copies.append(pltpu.make_async_copy(saved, saved_in, sems.at[depths]))
    copies.append(pltpu.make_async_copy(feats, feats_in, sems.at[depths + 1]))
    for copy in copies:
        copy.start()
    pooled[...] = jnp.zeros_like(pooled)

    def per_image(i, carry):
        cells, beside = pool_columns(flags, held, col_a, col_b, wide, i, range(1, height2 - 1))
        for p in range(1, height - 1):
            at = 2 * p - 2
            both = [
                0.75 * (group[at + 1] + group[at + 2]) + 0.25 * (group[at] + group[at + 3])
                for group in (cells, beside)
            ]
            where = pl.multiple_of((p - 1) * images * width + i * width, width)
            place(both[0], both[1], pooled.at[p], window, where)
        return carry

    lax.fori_loop(0, images, per_image, 0)
    line = images * width
    inner = (height - 2) * line
    for k in range(depths):
        copies[k].wait()
        for u in range(3):
            part = nt_dot(window[0], weight_out[k, u, 0])
            part = part + nt_dot(window[1], weight_out[k, u, 1])
            part = part + nt_dot(window[2], weight_out[k, u, 2])
            if u == 0:
                acc[k, :inner, :] = part
                acc[k, inner:, :] = jnp.zeros((2 * line, channels), F32)
            else:
                acc[k, u * line : u * line + inner, :] += part
    copies[depths].wait()
    for k in range(depths):
        for h in range(height):
            for i in range(images):
                at = (h * images + i) * width
                saved_flat[at : at + width, :] = saved_in[i, k, h]
        saved_t[k] = saved_flat[...].T
    copies[depths + 1].wait()
    for k in range(depths):
        feats_t[k] = feats_in[:, k].reshape(feats_t.shape[2], feats_t.shape[1]).T


def edge_kernel(has_second, flags, *refs):
    sides = 2 if has_second else 1
    rows, (cells, beside, inner, acc, weight) = refs[:sides], refs[sides : sides + 5]
    grads, window, pooled, ends, total = refs[sides + 5 :]
    images, width = cells.shape[0], cells.shape[2]
    depths, count = acc.shape[:2]
    line = images * width
    height = count // line
    row_odd, top, bottom = flags[ROW_ODD] == 1, flags[TOP] == 1, flags[BOTTOM] == 1
    for n in range(sides):
        ends[n] = rows[n][2 * line :, :].astype(F32)
    pooled[...] = jnp.zeros_like(pooled)
    for i in range(images):
        for_rows = []
        for is_end, own in ((False, cells), (True, beside)):
            def came(from_above, n):
                def of(ref_at):
                    if is_end:
                        at = (2 * i + n) * 2
                        return ends[ref_at, at : at + 2, :]
                    at = (2 * i + n) * width
                    return rows[ref_at][at : at + width, :].astype(F32)

                first = of(0)
                second = of(1) if has_second else jnp.zeros_like(first)
                return jnp.where(row_odd, first, second) if from_above else jnp.where(row_odd, second, first)

            edge = [own[i, n] for n in range(6)]
            zero = jnp.zeros_like(edge[0])
            for_rows.append(
                [
                    jnp.where(top, zero, came(True, 0) + 0.25 * edge[0]),
                    0.75 * (edge[0] + edge[1]) + 0.25 * (jnp.where(top, edge[0], came(True, 1)) + edge[2]),
                    0.75 * (edge[4] + edge[5]) + 0.25 * (jnp.where(bottom, edge[5], came(False, 0)) + edge[3]),
                    jnp.where(bottom, zero, came(False, 1) + 0.25 * edge[5]),
                ]
            )
        for n, p in enumerate((0, 1, height, height + 1)):
            place(for_rows[0][n], for_rows[1][n], pooled.at[n], window, p * line + i * width)
    for v in range(3):
        window[v, 2 * line : height * line, :] = inner[v]
    low, high = slice(0, 2 * line), slice(height * line, (height + 2) * line)
    for k in range(depths):
        total[...] = acc[k]
        for v in range(3):
            total[(height - 2) * line :, :] += nt_dot(window[v, high, :], weight[k, 0, v])
            total[: 2 * line, :] += nt_dot(window[v, low, :], weight[k, 2, v])
            middle = jnp.concatenate(
                [window[v, line : 2 * line, :], window[v, height * line : (height + 1) * line, :]], axis=0
            )
            part = nt_dot(middle, weight[k, 1, v])
            total[:line, :] += part[:line]
            total[(height - 1) * line :, :] += part[line:]
        for h in range(height):
            grads[h, k] = total[h * line : (h + 1) * line, :].astype(BF16)


def deal(full, split_refs, core):
    if len(split_refs) == 1:
        split_refs[0][...] = full[...]
        return
    kept, sent = split_refs
    count, rows = kept.shape[:2]
    for j in range(count):
        kept[j] = full[pl.ds(pl.multiple_of((2 * j + core) * rows, 16), rows), :]
        sent[j] = full[pl.ds(pl.multiple_of((2 * j + 1 - core) * rows, 16), rows), :]


def conv_term_kernel(flags, window, saved_t, *refs):
    split_refs, top, full = refs[:-2], refs[-2], refs[-1]
    depths, channels, count = saved_t.shape
    line = (window.shape[1] - count) // 2
    split = top.shape[0]
    for k in range(depths):
        for n in range(9):
            start = (2 - n // 3) * line
            part = jnp.dot(
                saved_t[k], window[n % 3, start : start + count, :], preferred_element_type=F32
            ).astype(BF16)
            at = (k * 9 + n) * channels
            if at < split:
                top[at : at + channels, :] = part
            else:
                full[at - split : at - split + channels, :] = part
    deal(full, split_refs, flags[CORE])


def proj_term_kernel(images, flags, came, feats_t, conv_top, *refs):
    split_refs, tokens, full = refs[:-2], refs[-2], refs[-1]
    groups, depths, line, channels = came.shape
    dim = feats_t.shape[1]
    width = line // images
    per_image = groups * width
    for k in range(depths):
        for g in range(groups):
            for i in range(images):
                at = i * per_image + column_of(g) * width
                tokens[k, at : at + width, :] = came[g, k, i * width : (i + 1) * width, :]
    for k in range(depths):
        part = jnp.dot(feats_t[k], tokens[k], preferred_element_type=F32)
        full[k * dim : (k + 1) * dim, :] = part.astype(BF16)
    full[depths * dim :, :] = conv_top[...]
    deal(full, split_refs, flags[CORE])


def feat_grad_kernel(tokens, weight, out):
    images, depths, count, dim = out.shape
    for k in range(depths):
        out[:, k] = nt_dot(tokens[k], weight[k]).astype(BF16).reshape(images, count, dim)


def round_kernel(parts, bits_at, bits, by_columns, flags, *refs):
    ins, outs = refs[:parts], refs[parts:]
    span = 1 << bits
    mine, dp = 0, flags[DP]
    for b in range(bits):
        mine = mine + flags[BITS + bits_at + b] * (1 << b)
    count, _, width = outs[0].shape
    for n, out in enumerate(outs):
        across, apart = n // span, n % span
        for q in range(count):
            block = q * span + (mine ^ apart)
            if by_columns:
                columns = pl.ds(pl.multiple_of((dp ^ across) * width, width), width)
            else:
                columns = slice(None)
            total = ins[0][block, :, columns].astype(F32)
            for other in ins[1:]:
                total = total + other[block, :, columns].astype(F32)
            out[q] = total.astype(out.dtype)


def last_kernel(early_parts, flags, *refs):
    early, late, (sent, kept) = refs[:early_parts], refs[early_parts:-2], refs[-2:]
    first = flags[DP] == 0
    sums = []
    for group in (early, late):
        total = group[0][0].astype(F32)
        for other in group[1:]:
            total = total + other[0].astype(F32)
        sums.append(total)
    sent[...] = jnp.where(first, sums[0], sums[1]).astype(BF16)
    kept[...] = jnp.where(first, sums[1], sums[0])


def join_kernel(scale, flags, kept, came, out):
    width = kept.shape[1]
    at = pl.multiple_of(flags[DP] * width, width)
    out[:, pl.ds(at, width)] = kept[...] * scale
    at = pl.multiple_of((1 - flags[DP]) * width, width)
    out[:, pl.ds(at, width)] = came[...].astype(F32) * scale


def vmem_call(kernel, out_shape, operands, scratch=(), scalars=1, flops=0, limit=16, hbm=(), after=()):
    whole = pl.BlockSpec(memory_space=pltpu.VMEM)
    specs = [pl.BlockSpec(memory_space=pltpu.SMEM)] * scalars + [whole] * (len(operands) - scalars)
    for n in hbm:
        specs[n] = pl.BlockSpec(memory_space=pltpu.HBM)
    specs += [pl.BlockSpec(memory_space=pl.ANY)] * len(after)
    count = len(operands)

    def run(*refs):
        kernel(*refs[:count], *refs[count + len(after) :])

    moved = sum(a.size * a.dtype.itemsize for a in operands)
    moved += sum(math.prod(s.shape) * s.dtype.itemsize for s in jax.tree.leaves(out_shape))
    return pl.pallas_call(
        run,
        out_shape=out_shape,
        in_specs=specs,
        out_specs=jax.tree.map(lambda _: whole, out_shape),
        scratch_shapes=list(scratch),
        compiler_params=pltpu.CompilerParams(vmem_limit_bytes=limit << 20),
        cost_estimate=pl.CostEstimate(flops=flops, bytes_accessed=moved, transcendentals=0),
    )(*operands, *after)


def sds(*shape, dtype=BF16):
    return jax.ShapeDtypeStruct(shape, dtype)


def xor_move(block, apart, across):
    tiles = lax.axis_size("tile")
    if not across:
        return lax.ppermute(block, "tile", [(t, t ^ apart) for t in range(tiles)])
    if not apart:
        return lax.ppermute(block, "dp", [(0, 1), (1, 0)])
    route = [(d * tiles + t, (1 - d) * tiles + (t ^ apart)) for d in range(2) for t in range(tiles)]
    return lax.ppermute(block, ("dp", "tile"), route)


def core_sum(dealt, core):
    if len(dealt) == 1:
        tiles = lax.axis_size("tile")
        pairs = dealt[0].reshape(tiles // 2, 2, dealt[0].shape[0] // tiles, dealt[0].shape[1])
        kept = lax.dynamic_index_in_dim(pairs, core, 1, keepdims=False)
        sent = lax.dynamic_index_in_dim(pairs, 1 - core, 1, keepdims=False)
    else:
        kept, sent = dealt
    return [kept, xor_move(sent, 1, False)]


def deal_round(parts, flags, at, bits, by_columns, after=()):
    span = 1 << bits
    count, rows, channels = parts[0].shape
    if by_columns:
        channels //= 2
    outs = [
        sds(count // span, rows, channels, dtype=F32 if n == 0 else BF16)
        for n in range(span * (2 if by_columns else 1))
    ]
    return vmem_call(
        functools.partial(round_kernel, len(parts), at, bits, by_columns), outs, [flags] + parts, after=after
    )


def send_round(pieces, at, bits):
    span = 1 << bits
    return [pieces[0]] + [
        xor_move(pieces[n], (n % span) << at, n >= span) for n in range(1, len(pieces))
    ]


def per_device(features, proj_weight, conv_weight, saved, cotangent):
    position = lax.axis_index("tile")
    tile_count = lax.axis_size("tile")
    rows = tile_count // TILE_COLS
    gray = position % TILE_COLS
    col, row = column_of(gray), position // TILE_COLS
    images, height2, width2, channels = cotangent.shape
    depths, dim = proj_weight.shape[:2]
    height, width = height2 // 2, width2 // 2
    patches = images * height * width
    line = images * width
    tokens = features.shape[2]
    has_second = rows > 2
    sides = 2 if has_second else 1
    bits = tile_count.bit_length() - 1
    flags = jnp.stack(
        [row % 2, col % 2, row == 0, row == rows - 1, col == 0, col == TILE_COLS - 1]
        + [position % 2, lax.axis_index("dp")]
        + [position >> b & 1 for b in range(bits)]
    ).astype(jnp.int32)

    def swap(block, row_pairs, col_pairs):
        return lax.ppermute(block, "tile", tile_route(row_pairs, col_pairs, rows))

    held, to_first, to_second = vmem_call(
        column_pack_kernel,
        [sds(*cotangent.shape)] + [sds(images, height2, HALO, channels)] * 2,
        (flags, cotangent),
        scratch=(pltpu.SemaphoreType.DMA((images,)),),
        hbm=(1,),
    )
    col_b = swap(to_second, None, paired(TILE_COLS, 1))
    col_a = swap(to_first, None, paired(TILE_COLS, 0))
    halves = channels // 128
    *row_out, cells, beside = vmem_call(
        functools.partial(row_pack_kernel, has_second),
        [sds(2 * images * (width + 2), channels)] * sides
        + [sds(images, 6, width, channels, dtype=F32), sds(images, 6, 2, channels, dtype=F32)],
        (flags, held, col_a, col_b),
        scratch=(
            pltpu.VMEM((halves, 6, LEFT + width2 + 8, 128), F32),
            pltpu.VMEM((sides, 4 * images, channels), F32),
        ),
    )
    came_rows = [swap(row_out[n], paired(rows, n), None) for n in range(sides)]
    conv_flops = 2 * patches * depths * 9 * channels * channels
    inner, acc, weight, saved_t, feats_t = vmem_call(
        main_kernel,
        [
            sds(3, (height - 2) * line, channels),
            sds(depths, patches, channels, dtype=F32),
            sds(*conv_weight.shape),
            sds(depths, channels, patches),
            sds(depths, dim, images * tokens),
        ],
        (flags, held, col_a, col_b, conv_weight, saved, features),
        scratch=(
            pltpu.VMEM((halves, height2 - 2, LEFT + width2 + 8, 128), F32),
            pltpu.VMEM((height, LEFT + width + 8, channels), F32),
            pltpu.VMEM(saved.shape, BF16),
            pltpu.VMEM(features.shape, BF16),
            pltpu.VMEM((patches, channels), BF16),
            pltpu.SemaphoreType.DMA((depths + 2,)),
        ),
        flops=conv_flops,
        hbm=(4, 5, 6),
        after=(row_out[0],),
    )
    grads, window = vmem_call(
        functools.partial(edge_kernel, has_second),
        [sds(height, depths, line, channels), sds(3, (height + 2) * line, channels)],
        [flags] + came_rows + [cells, beside, inner, acc, weight],
        scratch=(
            pltpu.VMEM((4, LEFT + width + 8, channels), F32),
            pltpu.VMEM((sides, 4 * images, channels), F32),
            pltpu.VMEM((patches, channels), F32),
        ),
        flops=conv_flops // 4,
    )
    groups = [[g * TILE_COLS + t for t in range(TILE_COLS)] for g in range(rows)]
    came = lax.all_to_all(grads, "tile", 0, 0, axis_index_groups=groups, tiled=True)

    half_rows = depths * (dim + 9 * channels) // 2
    conv_late = half_rows - depths * dim
    block_rows = half_rows // tile_count
    if block_rows % 16:
        dealt = [sds(half_rows, channels)]
    else:
        dealt = [sds(tile_count // 2, block_rows, channels)] * 2
    full = pltpu.VMEM((half_rows, channels), BF16)
    *early, conv_top = vmem_call(
        conv_term_kernel,
        dealt + [sds(conv_late, channels)],
        (flags, window, saved_t),
        scratch=(full,),
        flops=conv_flops,
    )
    early_pieces = deal_round(core_sum(early, position % 2), flags, 1, 0, True)
    early_parts = send_round(early_pieces, 1, 0)
    proj_flops = 2 * images * tokens * depths * dim * channels
    *terms, token_grad = vmem_call(
        functools.partial(proj_term_kernel, images),
        dealt + [sds(depths, images * tokens, channels)],
        (flags, came, feats_t, conv_top),
        scratch=(full,),
        flops=proj_flops,
        after=(early_pieces[0],),
    )
    early_pieces = deal_round(early_parts, flags, 1, 1, False, after=(token_grad,))
    early_parts = send_round(early_pieces, 1, 1)
    late_pieces = deal_round(core_sum(terms, position % 2), flags, 1, 1, True, after=(early_pieces[0],))
    late_parts = send_round(late_pieces, 1, 1)
    feature_grad = vmem_call(
        feat_grad_kernel,
        sds(images, depths, tokens, dim),
        (token_grad, proj_weight),
        scalars=0,
        flops=proj_flops,
        after=(late_pieces[0],),
    )
    before = feature_grad
    for bit in range(2, bits):
        early_pieces = deal_round(early_parts, flags, bit, 1, False, after=(before,))
        early_parts = send_round(early_pieces, bit, 1)
        before = early_pieces[0]
    at = 2
    while at < bits:
        step = min(2, bits - at)
        late_pieces = deal_round(late_parts, flags, at, step, False, after=(before,))
        late_parts = send_round(late_pieces, at, step)
        before = late_pieces[0]
        at += step
    half = sds(block_rows, channels // 2)
    sent, kept = vmem_call(
        functools.partial(last_kernel, len(early_parts)),
        [half, sds(block_rows, channels // 2, dtype=F32)],
        [flags] + early_parts + late_parts,
    )
    other = xor_move(sent, 0, True)
    scale = 1.0 / math.sqrt(images * lax.axis_size("dp") * tokens * tile_count)
    head_grad = vmem_call(
        functools.partial(join_kernel, scale), sds(block_rows, channels, dtype=F32), (flags, kept, other)
    )
    return feature_grad, head_grad


def solution(mesh):
    in_specs = (
        P("dp", None, "tile", None),
        P(),
        P(),
        P("dp", None, "tile", None, None),
        P("dp", "tile", None, None),
    )
    out_specs = (P("dp", None, "tile", None), P(("dp", "tile"), None))
    return jax.shard_map(
        per_device, mesh=mesh, in_specs=in_specs, out_specs=out_specs, check_vma=False
    )
```

time: 88.6 us -> 89 us (level)
  waiting for transfers between devices: 33.8 us -> 24.2 us
  local copies, waits for them, and re-layouts: 4.03 us -> 11.6 us
  Pallas kernels: 18.3 us -> 20.3 us
    ppermute x16 -> x9, starting transfers between devices: 21.1 us -> 10.8 us  [xor_move(): return lax.ppermute(block, 'tile', [(t, t ^ apart) for t in range(tiles)])]
    all_to_all x0 -> x1, starting transfers between devices: none -> 9.33 us  [per_device(): lax.all_to_all(grads, 'tile', 0, 0, axis_index_groups=groups, tiled=True)]
    unnamed x12 -> x32, local copies, waits for them, and re-layouts: 3.94 us -> 11.5 us
    ppermute x16 -> x9, waiting for transfers between devices: 16.9 us -> 10.8 us  [xor_move(): return lax.ppermute(block, 'tile', [(t, t ^ apart) for t in range(tiles)])]
    ppermute x5 -> x3, waiting for transfers between devices: 5.65 us -> 0.33 us  [swap(): return lax.ppermute(block, 'tile', tile_route(row_pairs, col_pairs, rows))]
    pallas_call x16 -> x15, Pallas kernels: 18.3 us -> 20.3 us  [vmem_call(): pl.pallas_call(run, out_shape=out_shape, in_specs=specs, out_specs=jax.tr...]
    ppermute x3, waiting for transfers between devices: 11.2 us -> 13 us  [xor_move(): return lax.ppermute(block, 'dp', [(0, 1), (1, 0)])]
    ppermute x1, starting transfers between devices: 0.25 us -> 1.87 us  [xor_move(): return lax.ppermute(block, ('dp', 'tile'), route)]
  transfers between devices with their start and end apart: 25 -> 17, of which waited for: 10 -> 8; matrix products, arithmetic and copies ran while one was open for 0% -> 0% of each run, Pallas kernels for 8% -> 15%
where the time goes in v4:
time: 89 us; the launch traced here: 88.6 us
  starting transfers between devices  31.7 us (36%)
  waiting for transfers between devices  24.2 us (27%)
  Pallas kernels  20.3 us (23%)
  local copies, waits for them, and re-layouts  11.6 us (13%)
    pallas_call x15, Pallas kernels, vmem_call(): pl.pallas_call(run, out_shape=out_shape, in_specs=specs, out_specs=jax.tr...  20.3 us
    ppermute x3, waiting for transfers between devices, xor_move(): return lax.ppermute(block, 'dp', [(0, 1), (1, 0)])  13 us
    unnamed x32, local copies, waits for them, and re-layouts  11.5 us
    ppermute x9, waiting for transfers between devices, xor_move(): return lax.ppermute(block, 'tile', [(t, t ^ apart) for t in range(tiles)])  10.8 us
    ppermute x9, starting transfers between devices, xor_move(): return lax.ppermute(block, 'tile', [(t, t ^ apart) for t in range(tiles)])  10.8 us
    all_to_all x1, starting transfers between devices, per_device(): lax.all_to_all(grads, 'tile', 0, 0, axis_index_groups=groups, tiled=True)  9.33 us
    ppermute x3, starting transfers between devices, swap(): return lax.ppermute(block, 'tile', tile_route(row_pairs, col_pairs, rows))  5.18 us
    ppermute x3, starting transfers between devices, xor_move(): return lax.ppermute(block, 'dp', [(0, 1), (1, 0)])  4.52 us
  transfers between devices with their start and end apart: 17, of which 8 were waited for; matrix products, arithmetic and copies ran while one was open for 0% of the time, Pallas kernels for 15%

profile of v4, /device:TPU:0, one launch (start us, length us, event | category | flops | bytes accessed | tf_op | source)
XLA Modules:
  0.0 88.6 jit_solution(7280092077354766685)
XLA Ops:
  0.7 0.1 stack.67.refs_0_
  0.8 0.0 copy-start.5
  0.8 1.3 %copy-done.5 = bf16[4,16,32,256]{3,2,1,0:T(8,128)(2,1)S(1)} copy-done((bf16[4,16,32,256]{3,2,1,0:T(8,128)(2,1)S(1)}, bf16[4,16,32,256]{3,2,1,0:T(8,128)(2,1)}, u32[]{:S(2)}) %copy-start.5) | copy-done | bytes 1048600
  2.2 0.8 shard_map.68
  3.0 0.5 collective-permute-start
  3.5 0.7 collective-permute-start.1
  4.2 0.3 collective-permute-done.refs_2_
  4.5 0.0 collective-permute-done.1.refs_3_
  4.5 0.8 shard_map.69
  5.3 4.0 %collective-permute-start.2 = (bf16[144,256]{1,0:T(8,128)(2,1)S(1)}, bf16[144,256]{1,0:T(8,128)(2,1)S(1)}, u32[]{:S(2)}, u32[]{:S(2)}) collective-permute-start(bf16[144,256]{1,0:T(8,128)(2,1)S(1)} %get-tuple-element.42.refs_7_), channel_id=1, source_target_pairs={{0,8},{1,9},{3,11},{2,10},{6,14},{7,15},{5,13},{4,12},{8,0},{9,1},... | collective-permute-start | bytes 221192 | tf_op jit(solution)/shard_map/ppermute | solution.py:429
  9.3 0.0 copy-done.1
  9.3 1.6 %copy-done.2 = bf16[4,2,128,1024]{3,2,1,0:T(8,128)(2,1)S(1)} copy-done((bf16[4,2,128,1024]{3,2,1,0:T(8,128)(2,1)S(1)}, bf16[4,2,128,1024]{3,2,1,0:T(8,128)(2,1)}, u32[]{:S(2)}) %copy-start.2) | copy-done | bytes 2097176
  10.9 1.0 %copy-done.9 = bf16[4,2,8,16,256]{4,3,2,1,0:T(8,128)(2,1)S(1)} copy-done((bf16[4,2,8,16,256]{4,3,2,1,0:T(8,128)(2,1)S(1)}, bf16[4,2,8,16,256]{4,3,2,1,0:T(8,128)(2,1)}, u32[]{:S(2)}) %copy-start.9) | copy-done | bytes 524312
  12.0 5.1 %shard_map.70 = (bf16[3,384,256]{2,1,0:T(8,128)(2,1)S(1)}, f32[2,512,256]{2,1,0:T(8,128)S(1)}, bf16[2,3,3,256,256]{4,3,2,1,0:T(8,128)(2,1)S(1)}, bf16[2,256,512]...) custom-call(s32[12]{0:T(128)S(1)} %stack.67.refs_0_, bf16[4,16,32,256]{3,2,1,0:T(8,128)(2,1)S(1)} %get-tuple-element.39.refs_1_, ...), custom_call_target="tpu_custom_call" | custom-call | flops 1207959552 | bytes 12910640 | tf_op jit(solution)/shard_map/pallas_call | solution.py:350
  17.1 0.0 copy-start.3
  17.1 0.0 collective-permute-done.2.refs_1_
  17.1 2.3 %shard_map.71 = (bf16[8,2,64,256]{3,2,1,0:T(8,128)(2,1)}, bf16[3,640,256]{2,1,0:T(8,128)(2,1)S(1)}) custom-call(s32[12]{0:T(128)S(1)} %stack.67.refs_0_, bf16[144,256]{1,0:T(8,128)(2,1)S(1)} %collective-permute-done.2.refs_1_, f32[4,6,16,256]{3,2,1,0:T(8,128)S(1)} %get-tuple-element.43.refs_2_, f32[4,6,2,256]{3,2,1,0:T(2,128)S(1)} %get-tuple-element.44.refs_3_, ...), custom_call_target="tpu_custom_call" | custom-call | flops 301989888 | bytes 6021168 | tf_op jit(solution)/shard_map/pallas_call | solution.py:350
  19.4 1.0 %copy-done.10 = bf16[3,640,256]{2,1,0:T(8,128)(2,1)} copy-done((bf16[3,640,256]{2,1,0:T(8,128)(2,1)}, bf16[3,640,256]{2,1,0:T(8,128)(2,1)S(1)}, u32[]{:S(2)}) %copy-start.10) | copy-done | bytes 983064
  20.4 9.3 %all-to-all-start = ((bf16[8,2,64,256]{3,2,1,0:T(8,128)(2,1)}), bf16[8,2,64,256]{3,2,1,0:T(8,128)(2,1)S(1)}, u32[]{:S(2)}, u32[]{:S(2)}) async-start(bf16[8,2,64,256]{3,2,1,0:T(8,128)(2,1)} %get-tuple-element.48), calls=%async_computation | async-start | bytes 1048576 | tf_op jit(solution)/shard_map/all_to_all | solution.py:487
  29.8 1.2 %copy-done.11 = bf16[3,640,256]{2,1,0:T(8,128)(2,1)S(1)} copy-done((bf16[3,640,256]{2,1,0:T(8,128)(2,1)S(1)}, bf16[3,640,256]{2,1,0:T(8,128)(2,1)}, u32[]{:S(2)}) %copy-start.11) | copy-done | bytes 983064
  31.0 1.0 %copy-done.13 = bf16[2,256,512]{2,1,0:T(8,128)(2,1)S(1)} copy-done((bf16[2,256,512]{2,1,0:T(8,128)(2,1)S(1)}, bf16[2,256,512]{2,1,0:T(8,128)(2,1)}, u32[]{:S(2)}) %copy-start.13) | copy-done | bytes 524312
  32.0 2.0 %shard_map.72 = (bf16[8,208,256]{2,1,0:T(8,128)(2,1)S(1)}, bf16[8,208,256]{2,1,0:T(8,128)(2,1)S(1)}, bf16[1280,256]{1,0:T(8,128)(2,1)S(1)}) custom-call(s32[12]{0:T(128)S(1)} %stack.67.refs_0_, bf16[3,640,256]{2,1,0:T(8,128)(2,1)S(1)} %copy-done.11, bf16[2,256,512]{2,1,0:T(8,128)(2,1)S(1)} %copy-done.13), custom_call_target="tpu_custom_call" | custom-call | flops 1207959552 | bytes 3866672 | tf_op jit(solution)/shard_map/pallas_call | solution.py:350
  34.1 0.8 copy-done.7
  34.9 0.5 collective-permute-start.3
  35.4 2.0 %collective-permute-done.3.refs_2_ = bf16[8,208,256]{2,1,0:T(8,128)(2,1)S(1)} collective-permute-done((bf16[8,208,256]{2,1,0:T(8,128)(2,1)S(1)}, bf16[8,208,256]{2,1,0:T(8,128)(2,1)S(1)}, u32[]{:S(2)}, u32[]{:S(2)}) %collective-permute-start.3) | collective-permute-done | bytes 852000 | tf_op jit(solution)/shard_map/ppermute | solution.py:368
  37.4 0.7 shard_map.73
  38.1 0.7 copy-done.14
  38.9 0.0 all-to-all-done.refs_1_
  38.9 1.1 %copy-done.8 = bf16[1280,256]{1,0:T(8,128)(2,1)S(1)} copy-done((bf16[1280,256]{1,0:T(8,128)(2,1)S(1)}, bf16[1280,256]{1,0:T(8,128)(2,1)}, u32[]{:S(2)}) %copy-start.8) | copy-done | bytes 655384
  40.0 1.4 %shard_map.74 = (bf16[8,208,256]{2,1,0:T(8,128)(2,1)S(1)}, bf16[8,208,256]{2,1,0:T(8,128)(2,1)S(1)}, bf16[2,512,256]{2,1,0:T(8,128)(2,1)S(1)}) custom-call(s32[12]{0:T(128)S(1)} %stack.67.refs_0_, bf16[8,2,64,256]{3,2,1,0:T(8,128)(2,1)S(1)} %all-to-all-done.refs_1_, bf16[2,1024,512]{2,1,0:T(8,128)(2,1)S(1)} %copy-done.4, bf16[1280,256]{1,0:T(8,128)(2,1)S(1)} %copy-done.8, ...), custom_call_target="tpu_custom_call" | custom-call | flops 536870912 | bytes 5505072 | tf_op jit(solution)/shard_map/pallas_call | solution.py:350
  41.4 0.0 copy-start.6
  41.4 0.4 collective-permute-start.4
  41.8 1.5 %collective-permute-start.5 = (bf16[8,208,128]{2,1,0:T(8,128)(2,1)S(1)}, bf16[8,208,128]{2,1,0:T(8,128)(2,1)S(1)}, u32[]{:S(2)}, u32[]{:S(2)}) collective-permute-start(bf16[8,208,128]{2,1,0:T(8,128)(2,1)S(1)} %copy-done.15), channel_id=1, source_target_pairs={{0,16},{16,0},{1,17},{17,1},{2,18},{18,2},{3,19},{19,3},{4,20},{20... | collective-permute-start | bytes 1277960 | tf_op jit(solution)/shard_map/ppermute | solution.py:370
  43.3 10.4 %collective-permute-done.5.refs_2_ = bf16[8,208,128]{2,1,0:T(8,128)(2,1)S(1)} collective-permute-done((bf16[8,208,128]{2,1,0:T(8,128)(2,1)S(1)}, bf16[8,208,128]{2,1,0:T(8,128)(2,1)S(1)}, u32[]{:S(2)}, u32[]{:S(2)}) %collective-permute-start.5) | collective-permute-done | bytes 426016 | tf_op jit(solution)/shard_map/ppermute | solution.py:370
  53.7 0.6 shard_map.75
  54.3 2.0 %collective-permute-start.6 = (bf16[4,208,128]{2,1,0:T(8,128)(2,1)S(1)}, bf16[4,208,128]{2,1,0:T(8,128)(2,1)S(1)}, u32[]{:S(2)}, u32[]{:S(2)}) collective-permute-start(bf16[4,208,128]{2,1,0:T(8,128)(2,1)S(1)} %get-tuple-element.62), channel_id=1, source_target_pairs={{0,2},{1,3},{2,0},{3,1},{4,6},{5,7},{6,4},{7,5},{8,10},{9,11},{10,... | collective-permute-start | bytes 638984 | tf_op jit(solution)/shard_map/ppermute | solution.py:368
  56.3 0.0 collective-permute-done.4.refs_2_
  56.3 0.7 shard_map.76
  57.0 0.2 collective-permute-start.9
  57.2 1.5 %collective-permute-start.10 = (bf16[4,208,128]{2,1,0:T(8,128)(2,1)S(1)}, bf16[4,208,128]{2,1,0:T(8,128)(2,1)S(1)}, u32[]{:S(2)}, u32[]{:S(2)}) collective-permute-start(bf16[4,208,128]{2,1,0:T(8,128)(2,1)S(1)} %get-tuple-element.68), channel_id=1, source_target_pairs={{0,16},{16,0},{1,17},{17,1},{2,18},{18,2},{3,19},{19,3},{4,20},{20... | collective-permute-start | bytes 638984 | tf_op jit(solution)/shard_map/ppermute | solution.py:370
  58.7 1.9 %collective-permute-start.11 = (bf16[4,208,128]{2,1,0:T(8,128)(2,1)S(1)}, bf16[4,208,128]{2,1,0:T(8,128)(2,1)S(1)}, u32[]{:S(2)}, u32[]{:S(2)}) collective-permute-start(bf16[4,208,128]{2,1,0:T(8,128)(2,1)S(1)} %get-tuple-element.69), channel_id=1, source_target_pairs={{0,18},{1,19},{2,16},{3,17},{4,22},{5,23},{6,20},{7,21},{8,26},{9,... | collective-permute-start | bytes 638984 | tf_op jit(solution)/shard_map/ppermute | solution.py:372
  60.6 2.1 %shard_map.77.refs_3_ = bf16[4,2,128,1024]{3,2,1,0:T(8,128)(2,1)} custom-call(bf16[2,512,256]{2,1,0:T(8,128)(2,1)S(1)} %get-tuple-element.56.refs_3_.refs_0_, bf16[2,1024,256]{2,1,0:T(8,128)(2,1)S(1)} %copy-done.6, f32[4,208,128]{2,1,0:T(8,128)S(1)} %get-tuple-element.61.refs_2_.refs_1_), custom_call_target="tpu_custom_call" | custom-call | flops 536870912 | bytes 3670016 | tf_op jit(solution)/shard_map/pallas_call | solution.py:350
  62.6 0.1 collective-permute-done.6.refs_2_
  62.7 1.6 %copy-done = bf16[4,2,128,1024]{3,2,1,0:T(8,128)(2,1)S(1)} copy-done((bf16[4,2,128,1024]{3,2,1,0:T(8,128)(2,1)S(1)}, bf16[4,2,128,1024]{3,2,1,0:T(8,128)(2,1)}, u32[]{:S(2)}) %copy-start) | copy-done | bytes 2097176
  64.3 0.6 shard_map.78
  64.9 2.1 %collective-permute-start.7 = (bf16[2,208,128]{2,1,0:T(8,128)(2,1)S(1)}, bf16[2,208,128]{2,1,0:T(8,128)(2,1)S(1)}, u32[]{:S(2)}, u32[]{:S(2)}) collective-permute-start(bf16[2,208,128]{2,1,0:T(8,128)(2,1)S(1)} %get-tuple-element.64), channel_id=1, source_target_pairs={{0,4},{1,5},{2,6},{3,7},{4,0},{5,1},{6,2},{7,3},{8,12},{9,13},{10,... | collective-permute-start | bytes 319496 | tf_op jit(solution)/shard_map/ppermute | solution.py:368
  67.0 2.8 %collective-permute-done.7.refs_2_ = bf16[2,208,128]{2,1,0:T(8,128)(2,1)S(1)} collective-permute-done((bf16[2,208,128]{2,1,0:T(8,128)(2,1)S(1)}, bf16[2,208,128]{2,1,0:T(8,128)(2,1)S(1)}, u32[]{:S(2)}, u32[]{:S(2)}) %collective-permute-start.7) | collective-permute-done | bytes 106528 | tf_op jit(solution)/shard_map/ppermute | solution.py:368
  69.8 0.6 shard_map.79
  70.4 0.3 collective-permute-start.8
  70.7 0.0 collective-permute-done.9.refs_2_
  70.7 0.0 collective-permute-done.10.refs_3_
  70.7 0.0 collective-permute-done.11.refs_4_
  70.7 0.7 shard_map.80
  71.4 2.4 %collective-permute-start.12 = (bf16[1,208,128]{2,1,0:T(8,128)(2,1)S(1)}, bf16[1,208,128]{2,1,0:T(8,128)(2,1)S(1)}, u32[]{:S(2)}, u32[]{:S(2)}) collective-permute-start(bf16[1,208,128]{2,1,0:T(8,128)(2,1)S(1)} %get-tuple-element.71), channel_id=1, source_target_pairs={{0,4},{1,5},{2,6},{3,7},{4,0},{5,1},{6,2},{7,3},{8,12},{9,13},{10,... | collective-permute-start | bytes 159752 | tf_op jit(solution)/shard_map/ppermute | solution.py:368
  73.7 2.9 %collective-permute-start.13 = (bf16[1,208,128]{2,1,0:T(8,128)(2,1)S(1)}, bf16[1,208,128]{2,1,0:T(8,128)(2,1)S(1)}, u32[]{:S(2)}, u32[]{:S(2)}) collective-permute-start(bf16[1,208,128]{2,1,0:T(8,128)(2,1)S(1)} %get-tuple-element.72), channel_id=1, source_target_pairs={{0,8},{1,9},{2,10},{3,11},{4,12},{5,13},{6,14},{7,15},{8,0},{9,1},... | collective-permute-start | bytes 159752 | tf_op jit(solution)/shard_map/ppermute | solution.py:368
  76.6 0.0 collective-permute-start.14
  76.6 0.0 collective-permute-done.8.refs_2_
  76.6 0.0 collective-permute-done.12.refs_4_
  76.6 2.7 %collective-permute-done.13.refs_5_ = bf16[1,208,128]{2,1,0:T(8,128)(2,1)S(1)} collective-permute-done((bf16[1,208,128]{2,1,0:T(8,128)(2,1)S(1)}, bf16[1,208,128]{2,1,0:T(8,128)(2,1)S(1)}, u32[]{:S(2)}, u32[]{:S(2)}) %collective-permute-start.13) | collective-permute-done | bytes 53280 | tf_op jit(solution)/shard_map/ppermute | solution.py:368
  79.3 3.2 %collective-permute-done.14.refs_6_ = bf16[1,208,128]{2,1,0:T(8,128)(2,1)S(1)} collective-permute-done((bf16[1,208,128]{2,1,0:T(8,128)(2,1)S(1)}, bf16[1,208,128]{2,1,0:T(8,128)(2,1)S(1)}, u32[]{:S(2)}, u32[]{:S(2)}) %collective-permute-start.14) | collective-permute-done | bytes 53280 | tf_op jit(solution)/shard_map/ppermute | solution.py:368
  82.5 0.6 shard_map.81
  83.1 1.5 %collective-permute-start.15 = (bf16[208,128]{1,0:T(8,128)(2,1)S(1)}, bf16[208,128]{1,0:T(8,128)(2,1)S(1)}, u32[]{:S(2)}, u32[]{:S(2)}) collective-permute-start(bf16[208,128]{1,0:T(8,128)(2,1)S(1)} %get-tuple-element.75), channel_id=1, source_target_pairs={{0,16},{16,0},{1,17},{17,1},{2,18},{18,2},{3,19},{19,3},{4,20},{20... | collective-permute-start | bytes 159752 | tf_op jit(solution)/shard_map/ppermute | solution.py:370
  84.7 2.7 %collective-permute-done.15.refs_2_ = bf16[208,128]{1,0:T(8,128)(2,1)S(1)} collective-permute-done((bf16[208,128]{1,0:T(8,128)(2,1)S(1)}, bf16[208,128]{1,0:T(8,128)(2,1)S(1)}, u32[]{:S(2)}, u32[]{:S(2)}) %collective-permute-start.15) | collective-permute-done | bytes 53280 | tf_op jit(solution)/shard_map/ppermute | solution.py:370
  87.3 1.2 %shard_map.82 = f32[208,256]{1,0:T(8,128)} custom-call(s32[12]{0:T(128)S(1)} %stack.67.refs_0_, f32[208,128]{1,0:T(8,128)S(1)} %get-tuple-element.74.refs_1_, bf16[208,128]{1,0:T(8,128)(2,1)S(1)} %collective-permute-done.15.refs_2_), custom_call_target="tpu_custom_call" | custom-call | bytes 372784 | tf_op jit(solution)/shard_map/pallas_call | solution.py:350
  (18 shorter events, 0.0 us)
Async XLA Ops:
  0.6 8.7 %copy-start.1 = (bf16[2,3,3,256,256]{4,3,2,1,0:T(8,128)(2,1)S(1)}, bf16[2,3,3,256,256]{4,3,2,1,0:T(8,128)(2,1)}, u32[]{:S(2)}) copy-start(bf16[2,3,3,256,256]{4,3,2,1,0:T(8,128)(2,1)} %refs_4_.1) | copy-start | bytes 7077892
  0.8 1.4 %copy-start.5 = (bf16[4,16,32,256]{3,2,1,0:T(8,128)(2,1)S(1)}, bf16[4,16,32,256]{3,2,1,0:T(8,128)(2,1)}, u32[]{:S(2)}) copy-start(bf16[4,16,32,256]{3,2,1,0:T(8,128)(2,1)} %refs_1_.2) | copy-start | bytes 3145732
  3.0 1.5 %collective-permute-start = (bf16[4,16,4,256]{3,2,1,0:T(4,128)(2,1)S(1)}, bf16[4,16,4,256]{3,2,1,0:T(4,128)(2,1)S(1)}, u32[]{:S(2)}, u32[]{:S(2)}) collective-permute-start(bf16[4,16,4,256]{3,2,1,0:T(4,128)(2,1)S(1)} %get-tuple-element.40), channel_id=1, source_target_pairs={{0,1},{1,0},{3,2},{2,3},{6,7},{7,6},{5,4},{4,5},{8,9},{9,8},{11,10... | collective-permute-start | bytes 393224 | tf_op jit(solution)/shard_map/ppermute | solution.py:429
  3.5 1.0 %collective-permute-start.1 = (bf16[4,16,4,256]{3,2,1,0:T(4,128)(2,1)S(1)}, bf16[4,16,4,256]{3,2,1,0:T(4,128)(2,1)S(1)}, u32[]{:S(2)}, u32[]{:S(2)}) collective-permute-start(bf16[4,16,4,256]{3,2,1,0:T(4,128)(2,1)S(1)} %get-tuple-element.41), channel_id=1, source_target_pairs={{1,3},{3,1},{2,6},{6,2},{7,5},{5,7},{9,11},{11,9},{10,14},{14,10},... | collective-permute-start | bytes 393224 | tf_op jit(solution)/shard_map/ppermute | solution.py:429
  5.3 11.8 %collective-permute-start.2 = (bf16[144,256]{1,0:T(8,128)(2,1)S(1)}, bf16[144,256]{1,0:T(8,128)(2,1)S(1)}, u32[]{:S(2)}, u32[]{:S(2)}) collective-permute-start(bf16[144,256]{1,0:T(8,128)(2,1)S(1)} %get-tuple-element.42.refs_7_), channel_id=1, source_target_pairs={{0,8},{1,9},{3,11},{2,10},{6,14},{7,15},{5,13},{4,12},{8,0},{9,1},... | collective-permute-start | bytes 221192 | tf_op jit(solution)/shard_map/ppermute | solution.py:429
  9.3 1.6 %copy-start.2 = (bf16[4,2,128,1024]{3,2,1,0:T(8,128)(2,1)S(1)}, bf16[4,2,128,1024]{3,2,1,0:T(8,128)(2,1)}, u32[]{:S(2)}) copy-start(bf16[4,2,128,1024]{3,2,1,0:T(8,128)(2,1)} %refs_6_.1) | copy-start | bytes 6291460
  10.9 1.0 %copy-start.9 = (bf16[4,2,8,16,256]{4,3,2,1,0:T(8,128)(2,1)S(1)}, bf16[4,2,8,16,256]{4,3,2,1,0:T(8,128)(2,1)}, u32[]{:S(2)}) copy-start(bf16[4,2,8,16,256]{4,3,2,1,0:T(8,128)(2,1)} %refs_5_.1) | copy-start | bytes 1572868
  17.1 2.4 %copy-start.3 = (bf16[2,1024,512]{2,1,0:T(8,128)(2,1)}, bf16[2,1024,512]{2,1,0:T(8,128)(2,1)S(1)}, u32[]{:S(2)}) copy-start(bf16[2,1024,512]{2,1,0:T(8,128)(2,1)S(1)} %get-tuple-element.49.refs_2_) | copy-start | bytes 6291460
  17.1 2.4 %copy-start.12 = (bf16[2,256,512]{2,1,0:T(8,128)(2,1)}, bf16[2,256,512]{2,1,0:T(8,128)(2,1)S(1)}, u32[]{:S(2)}) copy-start(bf16[2,256,512]{2,1,0:T(8,128)(2,1)S(1)} %get-tuple-element.51.refs_2_) | copy-start | bytes 1572868
  19.4 1.0 %copy-start.10 = (bf16[3,640,256]{2,1,0:T(8,128)(2,1)}, bf16[3,640,256]{2,1,0:T(8,128)(2,1)S(1)}, u32[]{:S(2)}) copy-start(bf16[3,640,256]{2,1,0:T(8,128)(2,1)S(1)} %get-tuple-element.50.refs_1_) | copy-start | bytes 2949124
  20.4 18.5 %all-to-all-start = ((bf16[8,2,64,256]{3,2,1,0:T(8,128)(2,1)}), bf16[8,2,64,256]{3,2,1,0:T(8,128)(2,1)S(1)}, u32[]{:S(2)}, u32[]{:S(2)}) async-start(bf16[8,2,64,256]{3,2,1,0:T(8,128)(2,1)} %get-tuple-element.48), calls=%async_computation | async-start | bytes 1048576 | tf_op jit(solution)/shard_map/all_to_all | solution.py:487
  29.8 1.2 %copy-start.11 = (bf16[3,640,256]{2,1,0:T(8,128)(2,1)S(1)}, bf16[3,640,256]{2,1,0:T(8,128)(2,1)}, u32[]{:S(2)}) copy-start(bf16[3,640,256]{2,1,0:T(8,128)(2,1)} %copy-done.10) | copy-start | bytes 2949124
  31.0 1.0 %copy-start.13 = (bf16[2,256,512]{2,1,0:T(8,128)(2,1)S(1)}, bf16[2,256,512]{2,1,0:T(8,128)(2,1)}, u32[]{:S(2)}) copy-start(bf16[2,256,512]{2,1,0:T(8,128)(2,1)} %copy-done.12) | copy-start | bytes 1572868
  32.0 6.9 %copy-start.4 = (bf16[2,1024,512]{2,1,0:T(8,128)(2,1)S(1)}, bf16[2,1024,512]{2,1,0:T(8,128)(2,1)}, u32[]{:S(2)}) copy-start(bf16[2,1024,512]{2,1,0:T(8,128)(2,1)} %copy-done.3) | copy-start | bytes 6291460
  34.0 0.8 copy-start.7
  34.9 2.5 %collective-permute-start.3 = (bf16[8,208,256]{2,1,0:T(8,128)(2,1)S(1)}, bf16[8,208,256]{2,1,0:T(8,128)(2,1)S(1)}, u32[]{:S(2)}, u32[]{:S(2)}) collective-permute-start(bf16[8,208,256]{2,1,0:T(8,128)(2,1)S(1)} %get-tuple-element.54), channel_id=1, source_target_pairs={{0,1},{1,0},{2,3},{3,2},{4,5},{5,4},{6,7},{7,6},{8,9},{9,8},{10,11... | collective-permute-start | bytes 2555912 | tf_op jit(solution)/shard_map/ppermute | solution.py:368
  38.1 0.8 copy-start.14
  38.9 1.1 %copy-start.8 = (bf16[1280,256]{1,0:T(8,128)(2,1)S(1)}, bf16[1280,256]{1,0:T(8,128)(2,1)}, u32[]{:S(2)}) copy-start(bf16[1280,256]{1,0:T(8,128)(2,1)} %copy-done.7) | copy-start | bytes 1966084
  40.0 1.8 %copy-start.15 = (bf16[8,208,128]{2,1,0:T(8,128)(2,1)S(1)}, bf16[8,208,128]{2,1,0:T(8,128)(2,1)}, u32[]{:S(2)}) copy-start(bf16[8,208,128]{2,1,0:T(8,128)(2,1)} %copy-done.14) | copy-start | bytes 1277956
  41.4 19.2 %copy-start.6 = (bf16[2,1024,256]{2,1,0:T(8,128)(2,1)S(1)}, bf16[2,1024,256]{2,1,0:T(8,128)(2,1)}, u32[]{:S(2)}) copy-start(bf16[2,1024,256]{2,1,0:T(8,128)(2,1)} %refs_1_.3) | copy-start | bytes 3145732
  41.4 14.9 %collective-permute-start.4 = (bf16[8,208,256]{2,1,0:T(8,128)(2,1)S(1)}, bf16[8,208,256]{2,1,0:T(8,128)(2,1)S(1)}, u32[]{:S(2)}, u32[]{:S(2)}) collective-permute-start(bf16[8,208,256]{2,1,0:T(8,128)(2,1)S(1)} %get-tuple-element.58), channel_id=1, source_target_pairs={{0,1},{1,0},{2,3},{3,2},{4,5},{5,4},{6,7},{7,6},{8,9},{9,8},{10,11... | collective-permute-start | bytes 2555912 | tf_op jit(solution)/shard_map/ppermute | solution.py:368
  41.8 11.9 %collective-permute-start.5 = (bf16[8,208,128]{2,1,0:T(8,128)(2,1)S(1)}, bf16[8,208,128]{2,1,0:T(8,128)(2,1)S(1)}, u32[]{:S(2)}, u32[]{:S(2)}) collective-permute-start(bf16[8,208,128]{2,1,0:T(8,128)(2,1)S(1)} %copy-done.15), channel_id=1, source_target_pairs={{0,16},{16,0},{1,17},{17,1},{2,18},{18,2},{3,19},{19,3},{4,20},{20... | collective-permute-start | bytes 1277960 | tf_op jit(solution)/shard_map/ppermute | solution.py:370
  54.3 8.4 %collective-permute-start.6 = (bf16[4,208,128]{2,1,0:T(8,128)(2,1)S(1)}, bf16[4,208,128]{2,1,0:T(8,128)(2,1)S(1)}, u32[]{:S(2)}, u32[]{:S(2)}) collective-permute-start(bf16[4,208,128]{2,1,0:T(8,128)(2,1)S(1)} %get-tuple-element.62), channel_id=1, source_target_pairs={{0,2},{1,3},{2,0},{3,1},{4,6},{5,7},{6,4},{7,5},{8,10},{9,11},{10,... | collective-permute-start | bytes 638984 | tf_op jit(solution)/shard_map/ppermute | solution.py:368
  57.0 13.7 %collective-permute-start.9 = (bf16[4,208,128]{2,1,0:T(8,128)(2,1)S(1)}, bf16[4,208,128]{2,1,0:T(8,128)(2,1)S(1)}, u32[]{:S(2)}, u32[]{:S(2)}) collective-permute-start(bf16[4,208,128]{2,1,0:T(8,128)(2,1)S(1)} %get-tuple-element.67), channel_id=1, source_target_pairs={{0,2},{1,3},{2,0},{3,1},{4,6},{5,7},{6,4},{7,5},{8,10},{9,11},{10,... | collective-permute-start | bytes 638984 | tf_op jit(solution)/shard_map/ppermute | solution.py:368
  57.2 13.5 %collective-permute-start.10 = (bf16[4,208,128]{2,1,0:T(8,128)(2,1)S(1)}, bf16[4,208,128]{2,1,0:T(8,128)(2,1)S(1)}, u32[]{:S(2)}, u32[]{:S(2)}) collective-permute-start(bf16[4,208,128]{2,1,0:T(8,128)(2,1)S(1)} %get-tuple-element.68), channel_id=1, source_target_pairs={{0,16},{16,0},{1,17},{17,1},{2,18},{18,2},{3,19},{19,3},{4,20},{20... | collective-permute-start | bytes 638984 | tf_op jit(solution)/shard_map/ppermute | solution.py:370
  58.7 12.0 %collective-permute-start.11 = (bf16[4,208,128]{2,1,0:T(8,128)(2,1)S(1)}, bf16[4,208,128]{2,1,0:T(8,128)(2,1)S(1)}, u32[]{:S(2)}, u32[]{:S(2)}) collective-permute-start(bf16[4,208,128]{2,1,0:T(8,128)(2,1)S(1)} %get-tuple-element.69), channel_id=1, source_target_pairs={{0,18},{1,19},{2,16},{3,17},{4,22},{5,23},{6,20},{7,21},{8,26},{9,... | collective-permute-start | bytes 638984 | tf_op jit(solution)/shard_map/ppermute | solution.py:372
  62.7 1.6 %copy-start = (bf16[4,2,128,1024]{3,2,1,0:T(8,128)(2,1)S(1)}, bf16[4,2,128,1024]{3,2,1,0:T(8,128)(2,1)}, u32[]{:S(2)}) copy-start(bf16[4,2,128,1024]{3,2,1,0:T(8,128)(2,1)} %shard_map.77.refs_3_) | copy-start | bytes 6291460
  64.9 4.9 %collective-permute-start.7 = (bf16[2,208,128]{2,1,0:T(8,128)(2,1)S(1)}, bf16[2,208,128]{2,1,0:T(8,128)(2,1)S(1)}, u32[]{:S(2)}, u32[]{:S(2)}) collective-permute-start(bf16[2,208,128]{2,1,0:T(8,128)(2,1)S(1)} %get-tuple-element.64), channel_id=1, source_target_pairs={{0,4},{1,5},{2,6},{3,7},{4,0},{5,1},{6,2},{7,3},{8,12},{9,13},{10,... | collective-permute-start | bytes 319496 | tf_op jit(solution)/shard_map/ppermute | solution.py:368
  70.4 6.2 %collective-permute-start.8 = (bf16[1,208,128]{2,1,0:T(8,128)(2,1)S(1)}, bf16[1,208,128]{2,1,0:T(8,128)(2,1)S(1)}, u32[]{:S(2)}, u32[]{:S(2)}) collective-permute-start(bf16[1,208,128]{2,1,0:T(8,128)(2,1)S(1)} %get-tuple-element.66), channel_id=1, source_target_pairs={{0,8},{1,9},{2,10},{3,11},{4,12},{5,13},{6,14},{7,15},{8,0},{9,1},... | collective-permute-start | bytes 159752 | tf_op jit(solution)/shard_map/ppermute | solution.py:368
  71.4 5.3 %collective-permute-start.12 = (bf16[1,208,128]{2,1,0:T(8,128)(2,1)S(1)}, bf16[1,208,128]{2,1,0:T(8,128)(2,1)S(1)}, u32[]{:S(2)}, u32[]{:S(2)}) collective-permute-start(bf16[1,208,128]{2,1,0:T(8,128)(2,1)S(1)} %get-tuple-element.71), channel_id=1, source_target_pairs={{0,4},{1,5},{2,6},{3,7},{4,0},{5,1},{6,2},{7,3},{8,12},{9,13},{10,... | collective-permute-start | bytes 159752 | tf_op jit(solution)/shard_map/ppermute | solution.py:368
  73.7 5.6 %collective-permute-start.13 = (bf16[1,208,128]{2,1,0:T(8,128)(2,1)S(1)}, bf16[1,208,128]{2,1,0:T(8,128)(2,1)S(1)}, u32[]{:S(2)}, u32[]{:S(2)}) collective-permute-start(bf16[1,208,128]{2,1,0:T(8,128)(2,1)S(1)} %get-tuple-element.72), channel_id=1, source_target_pairs={{0,8},{1,9},{2,10},{3,11},{4,12},{5,13},{6,14},{7,15},{8,0},{9,1},... | collective-permute-start | bytes 159752 | tf_op jit(solution)/shard_map/ppermute | solution.py:368
  76.6 5.9 %collective-permute-start.14 = (bf16[1,208,128]{2,1,0:T(8,128)(2,1)S(1)}, bf16[1,208,128]{2,1,0:T(8,128)(2,1)S(1)}, u32[]{:S(2)}, u32[]{:S(2)}) collective-permute-start(bf16[1,208,128]{2,1,0:T(8,128)(2,1)S(1)} %get-tuple-element.73), channel_id=1, source_target_pairs={{0,12},{1,13},{2,14},{3,15},{4,8},{5,9},{6,10},{7,11},{8,4},{9,5},... | collective-permute-start | bytes 159752 | tf_op jit(solution)/shard_map/ppermute | solution.py:368
  83.1 4.2 %collective-permute-start.15 = (bf16[208,128]{1,0:T(8,128)(2,1)S(1)}, bf16[208,128]{1,0:T(8,128)(2,1)S(1)}, u32[]{:S(2)}, u32[]{:S(2)}) collective-permute-start(bf16[208,128]{1,0:T(8,128)(2,1)S(1)} %get-tuple-element.75), channel_id=1, source_target_pairs={{0,16},{16,0},{1,17},{17,1},{2,18},{18,2},{3,19},{19,3},{4,20},{20... | collective-permute-start | bytes 159752 | tf_op jit(solution)/shard_map/ppermute | solution.py:370

commit v5 on v4

--- a/solution.py
+++ b/solution.py
@@ -13,7 +13,8 @@
 LEFT = 8
 BF16 = jnp.bfloat16
 F32 = jnp.float32
-ROW_ODD, COL_ODD, TOP, BOTTOM, LEFT_END, RIGHT_END, CORE, DP, BITS = range(9)
+ROW_ODD, COL_ODD, TOP, BOTTOM, LEFT_END, RIGHT_END, CORE, DP, GRAY, BITS = range(10)
+CHIPS = TILE_COLS // 2
 
 
 def gray_of(column):
@@ -45,50 +46,46 @@
     return lax.dot_general(left, right, (((1,), (1,)), ((), ())), preferred_element_type=F32)
 
 
-def column_pack_kernel(flags, cot, held, first, second, sems):
-    col_odd = flags[COL_ODD] == 1
-    images, _, width2, _ = cot.shape
-    copies = [pltpu.make_async_copy(cot.at[i], held.at[i], sems.at[i]) for i in range(images)]
-    for copy in copies:
-        copy.start()
-    for i in range(images):
-        copies[i].wait()
-        low, high = held[i, :, :HALO].astype(F32), held[i, :, width2 - HALO :].astype(F32)
-        first[i] = jnp.where(col_odd, low, high).astype(BF16)
-        second[i] = jnp.where(col_odd, high, low).astype(BF16)
-
-
-def pool_columns(flags, held, col_a, col_b, wide, i, lines):
-    width2, channels = held.shape[2:]
+def centre_kernel(cot, pooled, wide):
+    images, height2, width2, channels = cot.shape
     width = width2 // 2
+    wide[...] = jnp.zeros_like(wide)
+
+    def per_image(i, carry):
+        for r in range(height2):
+            value = cot[i, r].astype(F32)
+            for h in range(channels // 128):
+                wide[h, r, LEFT : LEFT + width2, :] = value[:, h * 128 : (h + 1) * 128]
+        for r in range(height2):
+            for h in range(channels // 128):
+                taps = [wide[h, r, pl.ds(LEFT - 1 + n, width, stride=2), :] for n in range(4)]
+                pooled[i, r, :, h * 128 : (h + 1) * 128] = 0.75 * (taps[1] + taps[2]) + 0.25 * (taps[0] + taps[3])
+        return carry
+
+    lax.fori_loop(0, images, per_image, 0)
+
+
+def pool_columns(flags, cot, centre, col_a, col_b, i, lines):
+    width2 = cot.shape[2]
+    width, channels = centre.shape[2:]
     col_odd, left, right = flags[COL_ODD] == 1, flags[LEFT_END] == 1, flags[RIGHT_END] == 1
-    side = lax.broadcasted_iota(jnp.int32, (2, channels), 0)
-    outside = jnp.logical_or(jnp.logical_and(side == 0, left), jnp.logical_and(side == 1, right))
+    cell = lax.broadcasted_iota(jnp.int32, (width, channels), 0)
+    is_first, is_last = cell == 0, cell == width - 1
     cells, beside = [], []
-    for at, r in enumerate(lines):
-        centre = held[i, r].astype(F32)
+    for r in lines:
+        own_first, own_last = cot[i, r, 0:1].astype(F32), cot[i, r, width2 - 1 : width2].astype(F32)
         one, two = col_a[i, r].astype(F32), col_b[i, r].astype(F32)
-        before = jnp.where(left, jnp.broadcast_to(centre[:1], one.shape), jnp.where(col_odd, one, two))
-        after = jnp.where(
-            right, jnp.broadcast_to(centre[width2 - 1 :], one.shape), jnp.where(col_odd, two, one)
+        before, after = jnp.where(col_odd, one, two), jnp.where(col_odd, two, one)
+        near_before = jnp.where(left, own_first, before[3:4])
+        near_after = jnp.where(right, own_last, after[0:1])
+        cells.append(
+            centre[i, r] + 0.25 * (jnp.where(is_first, near_before, 0.0) + jnp.where(is_last, near_after, 0.0))
         )
-        for h in range(channels // 128):
-            lanes = slice(h * 128, (h + 1) * 128)
-            wide[h, at, LEFT - HALO : LEFT, :] = before[:, lanes]
-            wide[h, at, LEFT : LEFT + width2, :] = centre[:, lanes]
-            wide[h, at, LEFT + width2 : LEFT + width2 + HALO, :] = after[:, lanes]
-    for at in range(len(lines)):
-        def taps(start, size, stride):
-            got = [
-                jnp.concatenate(
-                    [wide[h, at, pl.ds(start + n, size, stride=stride), :] for h in range(channels // 128)], axis=1
-                )
-                for n in range(4)
-            ]
-            return 0.75 * (got[1] + got[2]) + 0.25 * (got[0] + got[3])
-
-        cells.append(taps(LEFT - 1, width, 2))
-        beside.append(jnp.where(outside, 0.0, taps(LEFT - 3, 2, 2 * width + 2)))
+        first = 0.75 * (before[2:3] + before[3:4]) + 0.25 * (before[1:2] + own_first)
+        last = 0.75 * (after[0:1] + after[1:2]) + 0.25 * (own_last + after[2:3])
+        beside.append(
+            jnp.concatenate([jnp.where(left, 0.0, first), jnp.where(right, 0.0, last)], axis=0)
+        )
     return cells, beside
 
 
@@ -101,14 +98,13 @@
         window[v, pl.ds(at, width), :] = pooled[pl.ds(LEFT + 1 - v, width), :].astype(BF16)
 
 
-def row_pack_kernel(has_second, flags, held, col_a, col_b, *refs):
-    outs, (cells_out, beside_out, wide, ends) = refs[: 2 if has_second else 1], refs[-4:]
-    images, height2, width2, channels = held.shape
-    width = width2 // 2
+def row_pack_kernel(has_second, flags, cot, centre, col_a, col_b, *refs):
+    outs, (cells_out, beside_out, ends) = refs[: 2 if has_second else 1], refs[-3:]
+    images, height2, width, _ = centre.shape
     row_odd = flags[ROW_ODD] == 1
     lines = [0, 1, 2, height2 - 3, height2 - 2, height2 - 1]
     for i in range(images):
-        cells, beside = pool_columns(flags, held, col_a, col_b, wide, i, lines)
+        cells, beside = pool_columns(flags, cot, centre, col_a, col_b, i, lines)
         for n in range(6):
             cells_out[i, n] = cells[n]
             beside_out[i, n] = beside[n]
@@ -128,63 +124,43 @@
         outs[second][2 * images * width :, :] = ends[second].astype(BF16)
 
 
-def main_kernel(
-    flags, held, col_a, col_b, weight, saved, feats,
-    window, acc, weight_out, saved_t, feats_t,
-    wide, pooled, saved_in, feats_in, saved_flat, sems,
-):
-    images, height2, width2, channels = held.shape
-    height, width = height2 // 2, width2 // 2
-    depths = weight.shape[0]
-    copies = [pltpu.make_async_copy(weight.at[k], weight_out.at[k], sems.at[k]) for k in range(depths)]
-    copies.append(pltpu.make_async_copy(saved, saved_in, sems.at[depths]))
-    copies.append(pltpu.make_async_copy(feats, feats_in, sems.at[depths + 1]))
-    for copy in copies:
-        copy.start()
+def main_kernel(flags, cot, centre, col_a, col_b, weight, window, acc, pooled):
+    images, height2, width, channels = centre.shape
+    height, depths = height2 // 2, weight.shape[0]
     pooled[...] = jnp.zeros_like(pooled)
 
     def per_image(i, carry):
-        cells, beside = pool_columns(flags, held, col_a, col_b, wide, i, range(1, height2 - 1))
+        cells, beside = pool_columns(flags, cot, centre, col_a, col_b, i, range(1, height2 - 1))
         for p in range(1, height - 1):
             at = 2 * p - 2
             both = [
                 0.75 * (group[at + 1] + group[at + 2]) + 0.25 * (group[at] + group[at + 3])
                 for group in (cells, beside)
             ]
-            where = pl.multiple_of((p - 1) * images * width + i * width, width)
+            where = pl.multiple_of((p + 1) * images * width + i * width, width)
             place(both[0], both[1], pooled.at[p], window, where)
         return carry
 
     lax.fori_loop(0, images, per_image, 0)
     line = images * width
     inner = (height - 2) * line
+    rows = slice(2 * line, 2 * line + inner)
     for k in range(depths):
-        copies[k].wait()
         for u in range(3):
-            part = nt_dot(window[0], weight_out[k, u, 0])
-            part = part + nt_dot(window[1], weight_out[k, u, 1])
-            part = part + nt_dot(window[2], weight_out[k, u, 2])
+            part = nt_dot(window[0, rows, :], weight[k, u, 0])
+            part = part + nt_dot(window[1, rows, :], weight[k, u, 1])
+            part = part + nt_dot(window[2, rows, :], weight[k, u, 2])
             if u == 0:
                 acc[k, :inner, :] = part
                 acc[k, inner:, :] = jnp.zeros((2 * line, channels), F32)
             else:
                 acc[k, u * line : u * line + inner, :] += part
-    copies[depths].wait()
-    for k in range(depths):
-        for h in range(height):
-            for i in range(images):
-                at = (h * images + i) * width
-                saved_flat[at : at + width, :] = saved_in[i, k, h]
-        saved_t[k] = saved_flat[...].T
-    copies[depths + 1].wait()
-    for k in range(depths):
-        feats_t[k] = feats_in[:, k].reshape(feats_t.shape[2], feats_t.shape[1]).T
 
 
 def edge_kernel(has_second, flags, *refs):
     sides = 2 if has_second else 1
-    rows, (cells, beside, inner, acc, weight) = refs[:sides], refs[sides : sides + 5]
-    grads, window, pooled, ends, total = refs[sides + 5 :]
+    rows, (cells, beside, _, acc, weight) = refs[:sides], refs[sides : sides + 5]
+    *grads, window, pooled, ends, total = refs[sides + 5 :]
     images, width = cells.shape[0], cells.shape[2]
     depths, count = acc.shape[:2]
     line = images * width
@@ -220,8 +196,6 @@
             )
         for n, p in enumerate((0, 1, height, height + 1)):
             place(for_rows[0][n], for_rows[1][n], pooled.at[n], window, p * line + i * width)
-    for v in range(3):
-        window[v, 2 * line : height * line, :] = inner[v]
     low, high = slice(0, 2 * line), slice(height * line, (height + 2) * line)
     for k in range(depths):
         total[...] = acc[k]
@@ -234,8 +208,9 @@
             part = nt_dot(middle, weight[k, 1, v])
             total[:line, :] += part[:line]
             total[(height - 1) * line :, :] += part[line:]
-        for h in range(height):
-            grads[h, k] = total[h * line : (h + 1) * line, :].astype(BF16)
+        for apart in range(2 * CHIPS):
+            at = pl.multiple_of((flags[GRAY] ^ apart) * line, line)
+            grads[apart // 2][apart % 2, k] = total[pl.ds(at, line), :].astype(BF16)
 
 
 def deal(full, split_refs, core):
@@ -249,16 +224,22 @@
         sent[j] = full[pl.ds(pl.multiple_of((2 * j + 1 - core) * rows, 16), rows), :]
 
 
-def conv_term_kernel(flags, window, saved_t, *refs):
-    split_refs, top, full = refs[:-2], refs[-2], refs[-1]
-    depths, channels, count = saved_t.shape
-    line = (window.shape[1] - count) // 2
+def conv_term_kernel(flags, window, saved, *refs):
+    split_refs, top, full, flat = refs[:-3], refs[-3], refs[-2], refs[-1]
+    images, depths, height, width, channels = saved.shape
+    line = images * width
+    count = height * line
     split = top.shape[0]
     for k in range(depths):
+        for h in range(height):
+            for i in range(images):
+                at = (h * images + i) * width
+                flat[at : at + width, :] = saved[i, k, h]
+        flat_t = flat[...].T
         for n in range(9):
             start = (2 - n // 3) * line
             part = jnp.dot(
-                saved_t[k], window[n % 3, start : start + count, :], preferred_element_type=F32
+                flat_t, window[n % 3, start : start + count, :], preferred_element_type=F32
             ).astype(BF16)
             at = (k * 9 + n) * channels
             if at < split:
@@ -268,25 +249,37 @@
     deal(full, split_refs, flags[CORE])
 
 
-def proj_term_kernel(images, flags, came, feats_t, conv_top, *refs):
-    split_refs, tokens, full = refs[:-2], refs[-2], refs[-1]
-    groups, depths, line, channels = came.shape
-    dim = feats_t.shape[1]
+def pass_on_kernel(*refs):
+    for n, piece in enumerate(refs[:-1]):
+        refs[-1][n] = piece[1]
+
+
+def proj_term_kernel(flags, *refs):
+    came, (passed, feats, conv_top) = refs[:CHIPS], refs[CHIPS : CHIPS + 3]
+    split_refs, tokens, full = refs[CHIPS + 3 : -2], refs[-2], refs[-1]
+    images, depths, _, dim = feats.shape
+    line = passed.shape[2]
     width = line // images
-    per_image = groups * width
+    for apart in range(2 * CHIPS):
+        column = column_of(flags[GRAY] ^ apart)
+        for k in range(depths):
+            for i in range(images):
+                at = pl.multiple_of((i * TILE_COLS + column) * width, width)
+                rows = slice(i * width, (i + 1) * width)
+                piece = passed[apart // 2, k, rows, :] if apart % 2 else came[apart // 2][0, k, rows, :]
+                tokens[k, pl.ds(at, width), :] = piece
     for k in range(depths):
-        for g in range(groups):
-            for i in range(images):
-                at = i * per_image + column_of(g) * width
-                tokens[k, at : at + width, :] = came[g, k, i * width : (i + 1) * width, :]
-    for k in range(depths):
-        part = jnp.dot(feats_t[k], tokens[k], preferred_element_type=F32)
+        flat = feats[:, k].reshape(tokens.shape[1], dim)
+        part = lax.dot_general(
+            flat, tokens[k], (((0,), (0,)), ((), ())), preferred_element_type=F32
+        )
         full[k * dim : (k + 1) * dim, :] = part.astype(BF16)
     full[depths * dim :, :] = conv_top[...]
     deal(full, split_refs, flags[CORE])
 
 
-def feat_grad_kernel(tokens, weight, out):
+def feat_grad_kernel(tokens, weight, out, done):
+    done[...] = jnp.zeros_like(done)
     images, depths, count, dim = out.shape
     for k in range(depths):
         out[:, k] = nt_dot(tokens[k], weight[k]).astype(BF16).reshape(images, count, dim)
@@ -334,11 +327,9 @@
     out[:, pl.ds(at, width)] = came[...].astype(F32) * scale
 
 
-def vmem_call(kernel, out_shape, operands, scratch=(), scalars=1, flops=0, limit=16, hbm=(), after=()):
+def vmem_call(kernel, out_shape, operands, scratch=(), scalars=1, flops=0, limit=16, after=(), aliases=()):
     whole = pl.BlockSpec(memory_space=pltpu.VMEM)
     specs = [pl.BlockSpec(memory_space=pltpu.SMEM)] * scalars + [whole] * (len(operands) - scalars)
-    for n in hbm:
-        specs[n] = pl.BlockSpec(memory_space=pltpu.HBM)
     specs += [pl.BlockSpec(memory_space=pl.ANY)] * len(after)
     count = len(operands)
 
@@ -353,6 +344,7 @@
         in_specs=specs,
         out_specs=jax.tree.map(lambda _: whole, out_shape),
         scratch_shapes=list(scratch),
+        input_output_aliases=dict(aliases),
         compiler_params=pltpu.CompilerParams(vmem_limit_bytes=limit << 20),
         cost_estimate=pl.CostEstimate(flops=flops, bytes_accessed=moved, transcendentals=0),
     )(*operands, *after)
@@ -421,70 +413,56 @@
     bits = tile_count.bit_length() - 1
     flags = jnp.stack(
         [row % 2, col % 2, row == 0, row == rows - 1, col == 0, col == TILE_COLS - 1]
-        + [position % 2, lax.axis_index("dp")]
+        + [position % 2, lax.axis_index("dp"), gray]
         + [position >> b & 1 for b in range(bits)]
     ).astype(jnp.int32)
 
     def swap(block, row_pairs, col_pairs):
         return lax.ppermute(block, "tile", tile_route(row_pairs, col_pairs, rows))
 
-    held, to_first, to_second = vmem_call(
-        column_pack_kernel,
-        [sds(*cotangent.shape)] + [sds(images, height2, HALO, channels)] * 2,
-        (flags, cotangent),
-        scratch=(pltpu.SemaphoreType.DMA((images,)),),
-        hbm=(1,),
-    )
-    col_b = swap(to_second, None, paired(TILE_COLS, 1))
-    col_a = swap(to_first, None, paired(TILE_COLS, 0))
-    halves = channels // 128
+    low, high = cotangent[:, :, :HALO], cotangent[:, :, width2 - HALO :]
+    around = paired(TILE_COLS, 1) + [(0, TILE_COLS - 1), (TILE_COLS - 1, 0)]
+    col_b = swap(jnp.where(col % 2 == 1, high, low), None, around)
+    col_a = swap(jnp.where(col % 2 == 1, low, high), None, paired(TILE_COLS, 0))
+    centre = vmem_call(
+        centre_kernel,
+        sds(images, height2, width, channels, dtype=F32),
+        (cotangent,),
+        scratch=(pltpu.VMEM((channels // 128, height2, LEFT + width2 + 8, 128), F32),),
+        scalars=0,
+    )
     *row_out, cells, beside = vmem_call(
         functools.partial(row_pack_kernel, has_second),
         [sds(2 * images * (width + 2), channels)] * sides
         + [sds(images, 6, width, channels, dtype=F32), sds(images, 6, 2, channels, dtype=F32)],
-        (flags, held, col_a, col_b),
-        scratch=(
-            pltpu.VMEM((halves, 6, LEFT + width2 + 8, 128), F32),
-            pltpu.VMEM((sides, 4 * images, channels), F32),
-        ),
+        (flags, cotangent, centre, col_a, col_b),
+        scratch=(pltpu.VMEM((sides, 4 * images, channels), F32),),
     )
     came_rows = [swap(row_out[n], paired(rows, n), None) for n in range(sides)]
     conv_flops = 2 * patches * depths * 9 * channels * channels
-    inner, acc, weight, saved_t, feats_t = vmem_call(
+    window, acc = vmem_call(
         main_kernel,
-        [
-            sds(3, (height - 2) * line, channels),
-            sds(depths, patches, channels, dtype=F32),
-            sds(*conv_weight.shape),
-            sds(depths, channels, patches),
-            sds(depths, dim, images * tokens),
-        ],
-        (flags, held, col_a, col_b, conv_weight, saved, features),
-        scratch=(
-            pltpu.VMEM((halves, height2 - 2, LEFT + width2 + 8, 128), F32),
-            pltpu.VMEM((height, LEFT + width + 8, channels), F32),
-            pltpu.VMEM(saved.shape, BF16),
-            pltpu.VMEM(features.shape, BF16),
-            pltpu.VMEM((patches, channels), BF16),
-            pltpu.SemaphoreType.DMA((depths + 2,)),
-        ),
+        [sds(3, (height + 2) * line, channels), sds(depths, patches, channels, dtype=F32)],
+        (flags, cotangent, centre, col_a, col_b, conv_weight),
+        scratch=(pltpu.VMEM((height, LEFT + width + 8, channels), F32),),
         flops=conv_flops,
-        hbm=(4, 5, 6),
         after=(row_out[0],),
     )
-    grads, window = vmem_call(
+    *grads, window = vmem_call(
         functools.partial(edge_kernel, has_second),
-        [sds(height, depths, line, channels), sds(3, (height + 2) * line, channels)],
-        [flags] + came_rows + [cells, beside, inner, acc, weight],
+        [sds(2, depths, line, channels)] * CHIPS + [sds(3, (height + 2) * line, channels)],
+        [flags] + came_rows + [cells, beside, window, acc, conv_weight],
         scratch=(
             pltpu.VMEM((4, LEFT + width + 8, channels), F32),
             pltpu.VMEM((sides, 4 * images, channels), F32),
             pltpu.VMEM((patches, channels), F32),
         ),
         flops=conv_flops // 4,
-    )
-    groups = [[g * TILE_COLS + t for t in range(TILE_COLS)] for g in range(rows)]
-    came = lax.all_to_all(grads, "tile", 0, 0, axis_index_groups=groups, tiled=True)
+        aliases={sides + 3: CHIPS},
+    )
+    came = [grads[0]] + [xor_move(grads[chip], 2 * chip, False) for chip in range(1, CHIPS)]
+    to_pass = vmem_call(pass_on_kernel, sds(CHIPS, depths, line, channels), came, scalars=0)
+    passed = xor_move(to_pass, 1, False)
 
     half_rows = depths * (dim + 9 * channels) // 2
     conv_late = half_rows - depths * dim
@@ -497,45 +475,42 @@
     *early, conv_top = vmem_call(
         conv_term_kernel,
         dealt + [sds(conv_late, channels)],
-        (flags, window, saved_t),
-        scratch=(full,),
+        (flags, window, saved),
+        scratch=(full, pltpu.VMEM((patches, channels), BF16)),
         flops=conv_flops,
-    )
-    early_pieces = deal_round(core_sum(early, position % 2), flags, 1, 0, True)
-    early_parts = send_round(early_pieces, 1, 0)
+        after=(to_pass,),
+    )
+    early_parts = core_sum(early, position % 2)
     proj_flops = 2 * images * tokens * depths * dim * channels
     *terms, token_grad = vmem_call(
-        functools.partial(proj_term_kernel, images),
+        proj_term_kernel,
         dealt + [sds(depths, images * tokens, channels)],
-        (flags, came, feats_t, conv_top),
+        [flags] + came + [passed, features, conv_top],
         scratch=(full,),
         flops=proj_flops,
-        after=(early_pieces[0],),
-    )
-    early_pieces = deal_round(early_parts, flags, 1, 1, False, after=(token_grad,))
-    early_parts = send_round(early_pieces, 1, 1)
-    late_pieces = deal_round(core_sum(terms, position % 2), flags, 1, 1, True, after=(early_pieces[0],))
-    late_parts = send_round(late_pieces, 1, 1)
-    feature_grad = vmem_call(
+    )
+    early_pieces = deal_round(early_parts, flags, 1, 0, True, after=(token_grad,))
+    early_parts = send_round(early_pieces, 1, 0)
+    feature_grad, done = vmem_call(
         feat_grad_kernel,
-        sds(images, depths, tokens, dim),
+        [sds(images, depths, tokens, dim), sds(8, 128, dtype=F32)],
         (token_grad, proj_weight),
         scalars=0,
         flops=proj_flops,
-        after=(late_pieces[0],),
-    )
-    before = feature_grad
-    for bit in range(2, bits):
-        early_pieces = deal_round(early_parts, flags, bit, 1, False, after=(before,))
-        early_parts = send_round(early_pieces, bit, 1)
-        before = early_pieces[0]
-    at = 2
+        after=(early_pieces[0],),
+    )
+    late_parts = core_sum(terms, position % 2)
+    at, before = 1, done
     while at < bits:
-        step = min(2, bits - at)
-        late_pieces = deal_round(late_parts, flags, at, step, False, after=(before,))
-        late_parts = send_round(late_pieces, at, step)
+        late_step = 1 if at == 1 else min(2, bits - at)
+        late_pieces = deal_round(late_parts, flags, at, late_step, at == 1, after=(before,))
+        late_parts = send_round(late_pieces, at, late_step)
         before = late_pieces[0]
-        at += step
+        for bit in range(at, at + late_step):
+            early_pieces = deal_round(early_parts, flags, bit, 1, False, after=(before,))
+            early_parts = send_round(early_pieces, bit, 1)
+            before = early_pieces[0]
+        at += late_step
     half = sds(block_rows, channels // 2)
     sent, kept = vmem_call(
         functools.partial(last_kernel, len(early_parts)),

time: 89 us -> 78.2 us (0.88)
  local copies, waits for them, and re-layouts: 11.6 us -> 3.52 us
  starting transfers between devices: 31.7 us -> 25.9 us
  waiting for transfers between devices: 24.2 us -> 28.4 us
  Pallas kernels: 20.3 us -> 17.4 us
  other arithmetic: 0 us -> 1.87 us
    all_to_all x1 -> x0, starting transfers between devices: 9.33 us -> none  [per_device(): lax.all_to_all(grads, 'tile', 0, 0, axis_index_groups=groups, tiled=True)]
    unnamed x32 -> x16, local copies, waits for them, and re-layouts: 11.5 us -> 3.44 us
    ppermute x1, waiting for transfers between devices: 0.01 us -> 4.36 us  [xor_move(): return lax.ppermute(block, ('dp', 'tile'), route)]
    ppermute x9 -> x13, starting transfers between devices: 10.8 us -> 14 us  [xor_move(): return lax.ppermute(block, 'tile', [(t, t ^ apart) for t in range(tiles)])]
    pallas_call x15 -> x16, Pallas kernels: 20.3 us -> 17.4 us  [vmem_call(): pl.pallas_call(run, out_shape=out_shape, in_specs=specs, out_specs=jax.tr...]
    ppermute x3, waiting for transfers between devices: 13 us -> 10.5 us  [xor_move(): return lax.ppermute(block, 'dp', [(0, 1), (1, 0)])]
    select_n x0 -> x1, other arithmetic: none -> 1.87 us  [per_device(): col_b = swap(jnp.where(col % 2 == 1, high, low), None, around)]
    ppermute x3, waiting for transfers between devices: 0.33 us -> 1.6 us  [swap(): return lax.ppermute(block, 'tile', tile_route(row_pairs, col_pairs, rows))]
  transfers between devices with their start and end apart: 17 -> 20, of which waited for: 8 -> 13; matrix products, arithmetic and copies ran while one was open for 0% -> 0% of each run, Pallas kernels for 15% -> 13%
where the time goes in v5:
time: 78.2 us; the launch traced here: 78 us
  waiting for transfers between devices  28.4 us (36%)
  starting transfers between devices  25.9 us (33%)
  Pallas kernels  17.4 us (22%)
  local copies, waits for them, and re-layouts  3.52 us (5%)
  other arithmetic  1.87 us (2%)
  between operations  0.81 us (1%)
    pallas_call x16, Pallas kernels, vmem_call(): pl.pallas_call(run, out_shape=out_shape, in_specs=specs, out_specs=jax.tr...  17.4 us
    ppermute x13, starting transfers between devices, xor_move(): return lax.ppermute(block, 'tile', [(t, t ^ apart) for t in range(tiles)])  14 us
    ppermute x13, waiting for transfers between devices, xor_move(): return lax.ppermute(block, 'tile', [(t, t ^ apart) for t in range(tiles)])  12 us
    ppermute x3, waiting for transfers between devices, xor_move(): return lax.ppermute(block, 'dp', [(0, 1), (1, 0)])  10.5 us
    ppermute x3, starting transfers between devices, swap(): return lax.ppermute(block, 'tile', tile_route(row_pairs, col_pairs, rows))  6.13 us
    ppermute x1, waiting for transfers between devices, xor_move(): return lax.ppermute(block, ('dp', 'tile'), route)  4.36 us
    ppermute x3, starting transfers between devices, xor_move(): return lax.ppermute(block, 'dp', [(0, 1), (1, 0)])  3.65 us
    unnamed x16, local copies, waits for them, and re-layouts  3.44 us
  transfers between devices with their start and end apart: 20, of which 13 were waited for; matrix products, arithmetic and copies ran while one was open for 0% of the time, Pallas kernels for 13%

profile of v5, /device:TPU:0, one launch (start us, length us, event | category | flops | bytes accessed | tf_op | source)
XLA Modules:
  0.0 78.0 jit_solution(8176707247473702825)
XLA Ops:
  0.7 1.9 %broadcast_select_fusion = (bf16[4,16,4,256]{3,2,1,0:T(4,128)(2,1)}, bf16[4,16,4,256]{3,2,1,0:T(4,128)(2,1)}) fusion(pred[]{:T(512)S(6)} %eq.27, bf16[4,16,32,256]{3,2,1,0:T(8,128)(2,1)} %refs_1_.4), kind=kLoop, calls=%fused_computation | loop fusion | flops 131072 | bytes 524289 | tf_op jit(solution)/shard_map/jit(_where)/select_n | solution.py:425
  2.5 0.5 collective-permute-start
  3.0 2.6 %collective-permute-start.1 = (bf16[4,16,4,256]{3,2,1,0:T(4,128)(2,1)}, bf16[4,16,4,256]{3,2,1,0:T(4,128)(2,1)}, u32[]{:S(2)}, u32[]{:S(2)}) collective-permute-start(bf16[4,16,4,256]{3,2,1,0:T(4,128)(2,1)} %get-tuple-element.74), channel_id=1, source_target_pairs={{1,3},{3,1},{2,6},{6,2},{7,5},{5,7},{0,4},{4,0},{9,11},{11,9},{10,... | collective-permute-start | bytes 393224 | tf_op jit(solution)/shard_map/ppermute | solution.py:421
  5.6 1.2 %copy-done = bf16[4,16,32,256]{3,2,1,0:T(8,128)(2,1)S(1)} copy-done((bf16[4,16,32,256]{3,2,1,0:T(8,128)(2,1)S(1)}, bf16[4,16,32,256]{3,2,1,0:T(8,128)(2,1)}, u32[]{:S(2)}) %copy-start) | copy-done | bytes 1048600
  6.8 0.4 shard_map.68.refs_2_
  7.2 0.0 copy-start.3
  7.2 1.0 %copy-done.3 = f32[4,16,16,256]{3,2,1,0:T(8,128)} copy-done((f32[4,16,16,256]{3,2,1,0:T(8,128)}, f32[4,16,16,256]{3,2,1,0:T(8,128)S(1)}, u32[]{:S(2)}) %copy-start.3) | copy-done | bytes 1048600
  8.2 0.1 stack.71.refs_0_
  8.3 0.0 collective-permute-done.refs_3_
  8.3 0.5 collective-permute-done.1.refs_4_
  8.8 0.0 copy-done.1
  8.8 1.2 %copy-done.4 = f32[4,16,16,256]{3,2,1,0:T(8,128)S(1)} copy-done((f32[4,16,16,256]{3,2,1,0:T(8,128)S(1)}, f32[4,16,16,256]{3,2,1,0:T(8,128)}, u32[]{:S(2)}) %copy-start.4) | copy-done | bytes 1048600
  10.1 1.2 %shard_map.69 = (bf16[144,256]{1,0:T(8,128)(2,1)S(1)}, f32[4,6,16,256]{3,2,1,0:T(8,128)S(1)}, f32[4,6,2,256]{3,2,1,0:T(2,128)S(1)}) custom-call(s32[13]{0:T(128)S(1)} %stack.71.refs_0_, bf16[4,16,32,256]{3,2,1,0:T(8,128)(2,1)S(1)} %copy-done.1, f32[4,16,16,256]{3,2,1,0:T(8,128)S(1)} %copy-done.4, bf16[4,16,4,256]{3,2,1,0:T(4,128)(2,1)S(1)} %collective-permute-done.refs_3_, ...), custom_call_target="tpu_custom_call" | custom-call | bytes 2875444 | tf_op jit(solution)/shard_map/pallas_call | solution.py:341
  11.2 3.1 %collective-permute-start.2 = (bf16[144,256]{1,0:T(8,128)(2,1)S(1)}, bf16[144,256]{1,0:T(8,128)(2,1)S(1)}, u32[]{:S(2)}, u32[]{:S(2)}) collective-permute-start(bf16[144,256]{1,0:T(8,128)(2,1)S(1)} %get-tuple-element.38.refs_6_), channel_id=1, source_target_pairs={{0,8},{1,9},{3,11},{2,10},{6,14},{7,15},{5,13},{4,12},{8,0},{9,1},... | collective-permute-start | bytes 221192 | tf_op jit(solution)/shard_map/ppermute | solution.py:421
  14.3 2.8 %shard_map.70 = (bf16[3,640,256]{2,1,0:T(8,128)(2,1)S(1)}, f32[2,512,256]{2,1,0:T(8,128)S(1)}) custom-call(s32[13]{0:T(128)S(1)} %stack.71.refs_0_, bf16[4,16,32,256]{3,2,1,0:T(8,128)(2,1)S(1)} %copy-done.1, f32[4,16,16,256]{3,2,1,0:T(8,128)S(1)} %copy-done.4, bf16[4,16,4,256]{3,2,1,0:T(4,128)(2,1)S(1)} %collective-permute-done.refs_3_, ...), custom_call_target="tpu_custom_call" | custom-call | flops 1207959552 | bytes 6750260 | tf_op jit(solution)/shard_map/pallas_call | solution.py:341
  17.2 1.1 %collective-permute-done.2.refs_1_ = bf16[144,256]{1,0:T(8,128)(2,1)S(1)} collective-permute-done((bf16[144,256]{1,0:T(8,128)(2,1)S(1)}, bf16[144,256]{1,0:T(8,128)(2,1)S(1)}, u32[]{:S(2)}, u32[]{:S(2)}) %collective-permute-start.2) | collective-permute-done | bytes 73760 | tf_op jit(solution)/shard_map/ppermute | solution.py:421
  18.2 1.6 %shard_map.71 = (bf16[2,2,64,256]{3,2,1,0:T(8,128)(2,1)S(1)}, bf16[2,2,64,256]{3,2,1,0:T(8,128)(2,1)S(1)}, bf16[2,2,64,256]{3,2,1,0:T(8,128)(2,1)S(1)}, bf16[2,2...) custom-call(s32[13]{0:T(128)S(1)} %stack.71.refs_0_, ...), custom_call_target="tpu_custom_call", output_to_operand_aliasing={{4}: (4, {})} | custom-call | flops 301989888 | bytes 6414388 | tf_op jit(solution)/shard_map/pallas_call | solution.py:341
  19.9 1.6 %collective-permute-start.3 = (bf16[2,2,64,256]{3,2,1,0:T(8,128)(2,1)S(1)}, bf16[2,2,64,256]{3,2,1,0:T(8,128)(2,1)S(1)}, u32[]{:S(2)}, u32[]{:S(2)}) collective-permute-start(bf16[2,2,64,256]{3,2,1,0:T(8,128)(2,1)S(1)} %get-tuple-element.44), channel_id=1, source_target_pairs={{0,2},{1,3},{2,0},{3,1},{4,6},{5,7},{6,4},{7,5},{8,10},{9,11},{10,... | collective-permute-start | bytes 393224 | tf_op jit(solution)/shard_map/ppermute | solution.py:360
  21.5 0.5 collective-permute-start.4
  22.0 1.4 %collective-permute-start.5 = (bf16[2,2,64,256]{3,2,1,0:T(8,128)(2,1)S(1)}, bf16[2,2,64,256]{3,2,1,0:T(8,128)(2,1)S(1)}, u32[]{:S(2)}, u32[]{:S(2)}) collective-permute-start(bf16[2,2,64,256]{3,2,1,0:T(8,128)(2,1)S(1)} %get-tuple-element.46), channel_id=1, source_target_pairs={{0,6},{1,7},{2,4},{3,5},{4,2},{5,3},{6,0},{7,1},{8,14},{9,15},{10,... | collective-permute-start | bytes 393224 | tf_op jit(solution)/shard_map/ppermute | solution.py:360
  23.4 2.7 %collective-permute-done.3.refs_1_.refs_2_ = bf16[2,2,64,256]{3,2,1,0:T(8,128)(2,1)S(1)} collective-permute-done((bf16[2,2,64,256]{3,2,1,0:T(8,128)(2,1)S(1)}, bf16[2,2,64,256]{3,2,1,0:T(8,128)(2,1)S(1)}, u32[]{:S(2)}, u32[]{:S(2)}) %collective-permute-start.3) | collective-permute-done | bytes 131104 | tf_op jit(solution)/shard_map/ppermute | solution.py:360
  26.1 0.3 collective-permute-done.4.refs_2_.refs_3_
  26.4 2.1 %collective-permute-done.5.refs_3_.refs_4_ = bf16[2,2,64,256]{3,2,1,0:T(8,128)(2,1)S(1)} collective-permute-done((bf16[2,2,64,256]{3,2,1,0:T(8,128)(2,1)S(1)}, bf16[2,2,64,256]{3,2,1,0:T(8,128)(2,1)S(1)}, u32[]{:S(2)}, u32[]{:S(2)}) %collective-permute-start.5) | collective-permute-done | bytes 131104 | tf_op jit(solution)/shard_map/ppermute | solution.py:360
  28.5 0.0 copy-start.5
  28.5 2.1 %shard_map.73 = (bf16[8,208,256]{2,1,0:T(8,128)(2,1)S(1)}, bf16[8,208,256]{2,1,0:T(8,128)(2,1)S(1)}, bf16[1280,256]{1,0:T(8,128)(2,1)S(1)}) custom-call(s32[13]{0:T(128)S(1)} %stack.71.refs_0_, bf16[3,640,256]{2,1,0:T(8,128)(2,1)S(1)} %get-tuple-element.47.refs_1_, bf16[4,2,8,16,256]{4,3,2,1,0:T(8,128)(2,1)S(1)} %copy-done.7, ...), custom_call_target="tpu_custom_call" | custom-call | flops 1207959552 | bytes 3866676 | tf_op jit(solution)/shard_map/pallas_call | solution.py:341
  30.6 0.1 collective-permute-start.7
  30.7 0.5 collective-permute-start.6
  31.2 2.2 %collective-permute-done.6.refs_5_ = bf16[4,2,64,256]{3,2,1,0:T(8,128)(2,1)S(1)} collective-permute-done((bf16[4,2,64,256]{3,2,1,0:T(8,128)(2,1)S(1)}, bf16[4,2,64,256]{3,2,1,0:T(8,128)(2,1)S(1)}, u32[]{:S(2)}, u32[]{:S(2)}) %collective-permute-start.6) | collective-permute-done | bytes 262176 | tf_op jit(solution)/shard_map/ppermute | solution.py:360
  33.4 0.0 copy-done.5
  33.4 1.5 %shard_map.74 = (bf16[8,208,256]{2,1,0:T(8,128)(2,1)S(1)}, bf16[8,208,256]{2,1,0:T(8,128)(2,1)S(1)}, bf16[2,512,256]{2,1,0:T(8,128)(2,1)S(1)}) custom-call(s32[13]{0:T(128)S(1)} %stack.71.refs_0_, bf16[2,2,64,256]{3,2,1,0:T(8,128)(2,1)S(1)} %get-tuple-element.43.refs_0_.refs_1_, bf16[2,2,64,256]{3,2,1,0:T(8,128)(2,1)S(1)} %collective-permute-done.3.refs_1_.refs_2_, ...), custom_call_target="tpu_custom_call" | custom-call | flops 536870912 | bytes 5767220 | tf_op jit(solution)/shard_map/pallas_call | solution.py:341
  34.9 0.2 collective-permute-start.9
  35.1 0.0 collective-permute-done.7.refs_2_
  35.1 0.7 shard_map.75
  35.9 1.6 %collective-permute-start.8 = (bf16[8,208,128]{2,1,0:T(8,128)(2,1)S(1)}, bf16[8,208,128]{2,1,0:T(8,128)(2,1)S(1)}, u32[]{:S(2)}, u32[]{:S(2)}) collective-permute-start(bf16[8,208,128]{2,1,0:T(8,128)(2,1)S(1)} %get-tuple-element.54), channel_id=1, source_target_pairs={{0,16},{16,0},{1,17},{17,1},{2,18},{18,2},{3,19},{19,3},{4,20},{20... | collective-permute-start | bytes 1277960 | tf_op jit(solution)/shard_map/ppermute | solution.py:362
  37.4 2.1 %shard_map.76 = (bf16[4,2,128,1024]{3,2,1,0:T(8,128)(2,1)}, f32[8,128]{1,0:T(8,128)S(1)}) custom-call(bf16[2,512,256]{2,1,0:T(8,128)(2,1)S(1)} %get-tuple-element.49.refs_3_.refs_0_, bf16[2,1024,256]{2,1,0:T(8,128)(2,1)S(1)} %copy-done.6, f32[8,208,128]{2,1,0:T(8,128)S(1)} %get-tuple-element.52.refs_2_.refs_1_), custom_call_target="tpu_custom_call" | custom-call | flops 536870912 | bytes 3674112 | tf_op jit(solution)/shard_map/pallas_call | solution.py:341
  39.5 0.0 collective-permute-done.9.refs_2_
  39.5 0.7 shard_map.77
  40.2 0.9 %collective-permute-start.11 = (bf16[4,208,128]{2,1,0:T(8,128)(2,1)S(1)}, bf16[4,208,128]{2,1,0:T(8,128)(2,1)S(1)}, u32[]{:S(2)}, u32[]{:S(2)}) collective-permute-start(bf16[4,208,128]{2,1,0:T(8,128)(2,1)S(1)} %get-tuple-element.61), channel_id=1, source_target_pairs={{0,2},{1,3},{2,0},{3,1},{4,6},{5,7},{6,4},{7,5},{8,10},{9,11},{10,... | collective-permute-start | bytes 638984 | tf_op jit(solution)/shard_map/ppermute | solution.py:360
  41.1 0.5 collective-permute-start.12
  41.7 2.1 %collective-permute-start.13 = (bf16[4,208,128]{2,1,0:T(8,128)(2,1)S(1)}, bf16[4,208,128]{2,1,0:T(8,128)(2,1)S(1)}, u32[]{:S(2)}, u32[]{:S(2)}) collective-permute-start(bf16[4,208,128]{2,1,0:T(8,128)(2,1)S(1)} %get-tuple-element.63), channel_id=1, source_target_pairs={{0,18},{1,19},{2,16},{3,17},{4,22},{5,23},{6,20},{7,21},{8,26},{9,... | collective-permute-start | bytes 638984 | tf_op jit(solution)/shard_map/ppermute | solution.py:364
  43.8 4.8 %collective-permute-done.8.refs_2_ = bf16[8,208,128]{2,1,0:T(8,128)(2,1)S(1)} collective-permute-done((bf16[8,208,128]{2,1,0:T(8,128)(2,1)S(1)}, bf16[8,208,128]{2,1,0:T(8,128)(2,1)S(1)}, u32[]{:S(2)}, u32[]{:S(2)}) %collective-permute-start.8) | collective-permute-done | bytes 426016 | tf_op jit(solution)/shard_map/ppermute | solution.py:362
  48.6 0.6 shard_map.78
  49.2 0.9 %collective-permute-start.10 = (bf16[4,208,128]{2,1,0:T(8,128)(2,1)S(1)}, bf16[4,208,128]{2,1,0:T(8,128)(2,1)S(1)}, u32[]{:S(2)}, u32[]{:S(2)}) collective-permute-start(bf16[4,208,128]{2,1,0:T(8,128)(2,1)S(1)} %get-tuple-element.60), channel_id=1, source_target_pairs={{0,2},{1,3},{2,0},{3,1},{4,6},{5,7},{6,4},{7,5},{8,10},{9,11},{10,... | collective-permute-start | bytes 638984 | tf_op jit(solution)/shard_map/ppermute | solution.py:360
  50.1 0.0 collective-permute-done.11.refs_2_
  50.1 3.0 %collective-permute-done.12.refs_3_ = bf16[4,208,128]{2,1,0:T(8,128)(2,1)S(1)} collective-permute-done((bf16[4,208,128]{2,1,0:T(8,128)(2,1)S(1)}, bf16[4,208,128]{2,1,0:T(8,128)(2,1)S(1)}, u32[]{:S(2)}, u32[]{:S(2)}) %collective-permute-start.12) | collective-permute-done | bytes 213024 | tf_op jit(solution)/shard_map/ppermute | solution.py:362
  53.1 4.4 %collective-permute-done.13.refs_4_ = bf16[4,208,128]{2,1,0:T(8,128)(2,1)S(1)} collective-permute-done((bf16[4,208,128]{2,1,0:T(8,128)(2,1)S(1)}, bf16[4,208,128]{2,1,0:T(8,128)(2,1)S(1)}, u32[]{:S(2)}, u32[]{:S(2)}) %collective-permute-start.13) | collective-permute-done | bytes 213024 | tf_op jit(solution)/shard_map/ppermute | solution.py:364
  57.5 0.7 shard_map.79
  58.2 1.8 %collective-permute-done.10.refs_2_ = bf16[4,208,128]{2,1,0:T(8,128)(2,1)S(1)} collective-permute-done((bf16[4,208,128]{2,1,0:T(8,128)(2,1)S(1)}, bf16[4,208,128]{2,1,0:T(8,128)(2,1)S(1)}, u32[]{:S(2)}, u32[]{:S(2)}) %collective-permute-start.10) | collective-permute-done | bytes 213024 | tf_op jit(solution)/shard_map/ppermute | solution.py:360
  60.0 0.6 shard_map.80
  60.6 0.9 %collective-permute-start.14 = (bf16[2,208,128]{2,1,0:T(8,128)(2,1)S(1)}, bf16[2,208,128]{2,1,0:T(8,128)(2,1)S(1)}, u32[]{:S(2)}, u32[]{:S(2)}) collective-permute-start(bf16[2,208,128]{2,1,0:T(8,128)(2,1)S(1)} %get-tuple-element.66), channel_id=1, source_target_pairs={{0,4},{1,5},{2,6},{3,7},{4,0},{5,1},{6,2},{7,3},{8,12},{9,13},{10,... | collective-permute-start | bytes 319496 | tf_op jit(solution)/shard_map/ppermute | solution.py:360
  61.5 1.2 %collective-permute-start.16 = (bf16[1,208,128]{2,1,0:T(8,128)(2,1)S(1)}, bf16[1,208,128]{2,1,0:T(8,128)(2,1)S(1)}, u32[]{:S(2)}, u32[]{:S(2)}) collective-permute-start(bf16[1,208,128]{2,1,0:T(8,128)(2,1)S(1)} %get-tuple-element.69), channel_id=1, source_target_pairs={{0,4},{1,5},{2,6},{3,7},{4,0},{5,1},{6,2},{7,3},{8,12},{9,13},{10,... | collective-permute-start | bytes 159752 | tf_op jit(solution)/shard_map/ppermute | solution.py:360
  62.7 2.7 %collective-permute-start.17 = (bf16[1,208,128]{2,1,0:T(8,128)(2,1)S(1)}, bf16[1,208,128]{2,1,0:T(8,128)(2,1)S(1)}, u32[]{:S(2)}, u32[]{:S(2)}) collective-permute-start(bf16[1,208,128]{2,1,0:T(8,128)(2,1)S(1)} %get-tuple-element.70), channel_id=1, source_target_pairs={{0,8},{1,9},{2,10},{3,11},{4,12},{5,13},{6,14},{7,15},{8,0},{9,1},... | collective-permute-start | bytes 159752 | tf_op jit(solution)/shard_map/ppermute | solution.py:360
  65.3 0.9 %collective-permute-start.18 = (bf16[1,208,128]{2,1,0:T(8,128)(2,1)S(1)}, bf16[1,208,128]{2,1,0:T(8,128)(2,1)S(1)}, u32[]{:S(2)}, u32[]{:S(2)}) collective-permute-start(bf16[1,208,128]{2,1,0:T(8,128)(2,1)S(1)} %get-tuple-element.71), channel_id=1, source_target_pairs={{0,12},{1,13},{2,14},{3,15},{4,8},{5,9},{6,10},{7,11},{8,4},{9,5},... | collective-permute-start | bytes 159752 | tf_op jit(solution)/shard_map/ppermute | solution.py:360
  66.2 0.0 collective-permute-done.14.refs_2_
  66.3 0.6 shard_map.81
  66.8 2.3 %collective-permute-start.15 = (bf16[1,208,128]{2,1,0:T(8,128)(2,1)S(1)}, bf16[1,208,128]{2,1,0:T(8,128)(2,1)S(1)}, u32[]{:S(2)}, u32[]{:S(2)}) collective-permute-start(bf16[1,208,128]{2,1,0:T(8,128)(2,1)S(1)} %get-tuple-element.68), channel_id=1, source_target_pairs={{0,8},{1,9},{2,10},{3,11},{4,12},{5,13},{6,14},{7,15},{8,0},{9,1},... | collective-permute-start | bytes 159752 | tf_op jit(solution)/shard_map/ppermute | solution.py:360
  69.1 0.0 collective-permute-done.16.refs_4_
  69.1 0.0 collective-permute-done.17.refs_5_
  69.1 2.2 %collective-permute-done.18.refs_6_ = bf16[1,208,128]{2,1,0:T(8,128)(2,1)S(1)} collective-permute-done((bf16[1,208,128]{2,1,0:T(8,128)(2,1)S(1)}, bf16[1,208,128]{2,1,0:T(8,128)(2,1)S(1)}, u32[]{:S(2)}, u32[]{:S(2)}) %collective-permute-start.18) | collective-permute-done | bytes 53280 | tf_op jit(solution)/shard_map/ppermute | solution.py:360
  71.3 0.6 collective-permute-done.15.refs_2_
  71.9 0.6 shard_map.82
  72.5 1.5 %collective-permute-start.19 = (bf16[208,128]{1,0:T(8,128)(2,1)S(1)}, bf16[208,128]{1,0:T(8,128)(2,1)S(1)}, u32[]{:S(2)}, u32[]{:S(2)}) collective-permute-start(bf16[208,128]{1,0:T(8,128)(2,1)S(1)} %get-tuple-element.73), channel_id=1, source_target_pairs={{0,16},{16,0},{1,17},{17,1},{2,18},{18,2},{3,19},{19,3},{4,20},{20... | collective-permute-start | bytes 159752 | tf_op jit(solution)/shard_map/ppermute | solution.py:362
  74.1 2.7 %collective-permute-done.19.refs_2_ = bf16[208,128]{1,0:T(8,128)(2,1)S(1)} collective-permute-done((bf16[208,128]{1,0:T(8,128)(2,1)S(1)}, bf16[208,128]{1,0:T(8,128)(2,1)S(1)}, u32[]{:S(2)}, u32[]{:S(2)}) %collective-permute-start.19) | collective-permute-done | bytes 53280 | tf_op jit(solution)/shard_map/ppermute | solution.py:362
  76.7 1.2 %shard_map.83 = f32[208,256]{1,0:T(8,128)} custom-call(s32[13]{0:T(128)S(1)} %stack.71.refs_0_, f32[208,128]{1,0:T(8,128)S(1)} %get-tuple-element.72.refs_1_, bf16[208,128]{1,0:T(8,128)(2,1)S(1)} %collective-permute-done.19.refs_2_), custom_call_target="tpu_custom_call" | custom-call | bytes 372788 | tf_op jit(solution)/shard_map/pallas_call | solution.py:341
  (10 shorter events, 0.0 us)
Async XLA Ops:
  2.5 5.8 %collective-permute-start = (bf16[4,16,4,256]{3,2,1,0:T(4,128)(2,1)}, bf16[4,16,4,256]{3,2,1,0:T(4,128)(2,1)S(1)}, u32[]{:S(2)}, u32[]{:S(2)}) collective-permute-start(bf16[4,16,4,256]{3,2,1,0:T(4,128)(2,1)} %get-tuple-element.75), channel_id=1, source_target_pairs={{0,1},{1,0},{3,2},{2,3},{6,7},{7,6},{5,4},{4,5},{8,9},{9,8},{11,10... | collective-permute-start | bytes 393224 | tf_op jit(solution)/shard_map/ppermute | solution.py:421
  3.0 5.8 %collective-permute-start.1 = (bf16[4,16,4,256]{3,2,1,0:T(4,128)(2,1)}, bf16[4,16,4,256]{3,2,1,0:T(4,128)(2,1)}, u32[]{:S(2)}, u32[]{:S(2)}) collective-permute-start(bf16[4,16,4,256]{3,2,1,0:T(4,128)(2,1)} %get-tuple-element.74), channel_id=1, source_target_pairs={{1,3},{3,1},{2,6},{6,2},{7,5},{5,7},{0,4},{4,0},{9,11},{11,9},{10,... | collective-permute-start | bytes 393224 | tf_op jit(solution)/shard_map/ppermute | solution.py:421
  5.6 1.2 %copy-start = (bf16[4,16,32,256]{3,2,1,0:T(8,128)(2,1)S(1)}, bf16[4,16,32,256]{3,2,1,0:T(8,128)(2,1)}, u32[]{:S(2)}) copy-start(bf16[4,16,32,256]{3,2,1,0:T(8,128)(2,1)} %refs_1_.4) | copy-start | bytes 3145732
  6.8 2.0 %copy-start.1 = (bf16[4,16,32,256]{3,2,1,0:T(8,128)(2,1)S(1)}, bf16[4,16,32,256]{3,2,1,0:T(8,128)(2,1)}, u32[]{:S(2)}) copy-start(bf16[4,16,32,256]{3,2,1,0:T(8,128)(2,1)} %refs_1_.4) | copy-start | bytes 3145732
  6.8 7.5 %copy-start.2 = (bf16[2,3,3,256,256]{4,3,2,1,0:T(8,128)(2,1)S(1)}, bf16[2,3,3,256,256]{4,3,2,1,0:T(8,128)(2,1)}, u32[]{:S(2)}) copy-start(bf16[2,3,3,256,256]{4,3,2,1,0:T(8,128)(2,1)} %refs_6_.2) | copy-start | bytes 7077892
  7.2 1.0 %copy-start.3 = (f32[4,16,16,256]{3,2,1,0:T(8,128)}, f32[4,16,16,256]{3,2,1,0:T(8,128)S(1)}, u32[]{:S(2)}) copy-start(f32[4,16,16,256]{3,2,1,0:T(8,128)S(1)} %shard_map.68.refs_2_) | copy-start | bytes 3145732
  8.8 1.2 %copy-start.4 = (f32[4,16,16,256]{3,2,1,0:T(8,128)S(1)}, f32[4,16,16,256]{3,2,1,0:T(8,128)}, u32[]{:S(2)}) copy-start(f32[4,16,16,256]{3,2,1,0:T(8,128)} %copy-done.3) | copy-start | bytes 3145732
  11.2 7.0 %collective-permute-start.2 = (bf16[144,256]{1,0:T(8,128)(2,1)S(1)}, bf16[144,256]{1,0:T(8,128)(2,1)S(1)}, u32[]{:S(2)}, u32[]{:S(2)}) collective-permute-start(bf16[144,256]{1,0:T(8,128)(2,1)S(1)} %get-tuple-element.38.refs_6_), channel_id=1, source_target_pairs={{0,8},{1,9},{3,11},{2,10},{6,14},{7,15},{5,13},{4,12},{8,0},{9,1},... | collective-permute-start | bytes 221192 | tf_op jit(solution)/shard_map/ppermute | solution.py:421
  18.2 10.3 %copy-start.7 = (bf16[4,2,8,16,256]{4,3,2,1,0:T(8,128)(2,1)S(1)}, bf16[4,2,8,16,256]{4,3,2,1,0:T(8,128)(2,1)}, u32[]{:S(2)}) copy-start(bf16[4,2,8,16,256]{4,3,2,1,0:T(8,128)(2,1)} %refs_2_.1) | copy-start | bytes 1572868
  19.9 6.3 %collective-permute-start.3 = (bf16[2,2,64,256]{3,2,1,0:T(8,128)(2,1)S(1)}, bf16[2,2,64,256]{3,2,1,0:T(8,128)(2,1)S(1)}, u32[]{:S(2)}, u32[]{:S(2)}) collective-permute-start(bf16[2,2,64,256]{3,2,1,0:T(8,128)(2,1)S(1)} %get-tuple-element.44), channel_id=1, source_target_pairs={{0,2},{1,3},{2,0},{3,1},{4,6},{5,7},{6,4},{7,5},{8,10},{9,11},{10,... | collective-permute-start | bytes 393224 | tf_op jit(solution)/shard_map/ppermute | solution.py:360
  21.5 5.0 %collective-permute-start.4 = (bf16[2,2,64,256]{3,2,1,0:T(8,128)(2,1)S(1)}, bf16[2,2,64,256]{3,2,1,0:T(8,128)(2,1)S(1)}, u32[]{:S(2)}, u32[]{:S(2)}) collective-permute-start(bf16[2,2,64,256]{3,2,1,0:T(8,128)(2,1)S(1)} %get-tuple-element.45), channel_id=1, source_target_pairs={{0,4},{1,5},{2,6},{3,7},{4,0},{5,1},{6,2},{7,3},{8,12},{9,13},{10,... | collective-permute-start | bytes 393224 | tf_op jit(solution)/shard_map/ppermute | solution.py:360
  22.0 6.5 %collective-permute-start.5 = (bf16[2,2,64,256]{3,2,1,0:T(8,128)(2,1)S(1)}, bf16[2,2,64,256]{3,2,1,0:T(8,128)(2,1)S(1)}, u32[]{:S(2)}, u32[]{:S(2)}) collective-permute-start(bf16[2,2,64,256]{3,2,1,0:T(8,128)(2,1)S(1)} %get-tuple-element.46), channel_id=1, source_target_pairs={{0,6},{1,7},{2,4},{3,5},{4,2},{5,3},{6,0},{7,1},{8,14},{9,15},{10,... | collective-permute-start | bytes 393224 | tf_op jit(solution)/shard_map/ppermute | solution.py:360
  28.5 4.9 %copy-start.5 = (bf16[4,2,128,1024]{3,2,1,0:T(8,128)(2,1)S(1)}, bf16[4,2,128,1024]{3,2,1,0:T(8,128)(2,1)}, u32[]{:S(2)}) copy-start(bf16[4,2,128,1024]{3,2,1,0:T(8,128)(2,1)} %refs_6_.3) | copy-start | bytes 6291460
  30.6 4.5 %collective-permute-start.7 = (bf16[8,208,256]{2,1,0:T(8,128)(2,1)S(1)}, bf16[8,208,256]{2,1,0:T(8,128)(2,1)S(1)}, u32[]{:S(2)}, u32[]{:S(2)}) collective-permute-start(bf16[8,208,256]{2,1,0:T(8,128)(2,1)S(1)} %get-tuple-element.51), channel_id=1, source_target_pairs={{0,1},{1,0},{2,3},{3,2},{4,5},{5,4},{6,7},{7,6},{8,9},{9,8},{10,11... | collective-permute-start | bytes 2555912 | tf_op jit(solution)/shard_map/ppermute | solution.py:360
  30.7 2.7 %collective-permute-start.6 = (bf16[4,2,64,256]{3,2,1,0:T(8,128)(2,1)S(1)}, bf16[4,2,64,256]{3,2,1,0:T(8,128)(2,1)S(1)}, u32[]{:S(2)}, u32[]{:S(2)}) collective-permute-start(bf16[4,2,64,256]{3,2,1,0:T(8,128)(2,1)S(1)} %shard_map.72.refs_3_), channel_id=1, source_target_pairs={{0,1},{1,0},{2,3},{3,2},{4,5},{5,4},{6,7},{7,6},{8,9},{9,8},{10,11... | collective-permute-start | bytes 786440 | tf_op jit(solution)/shard_map/ppermute | solution.py:360
  33.4 4.0 %copy-start.6 = (bf16[2,1024,256]{2,1,0:T(8,128)(2,1)S(1)}, bf16[2,1024,256]{2,1,0:T(8,128)(2,1)}, u32[]{:S(2)}) copy-start(bf16[2,1024,256]{2,1,0:T(8,128)(2,1)} %refs_1_.5) | copy-start | bytes 3145732
  34.9 4.6 %collective-permute-start.9 = (bf16[8,208,256]{2,1,0:T(8,128)(2,1)S(1)}, bf16[8,208,256]{2,1,0:T(8,128)(2,1)S(1)}, u32[]{:S(2)}, u32[]{:S(2)}) collective-permute-start(bf16[8,208,256]{2,1,0:T(8,128)(2,1)S(1)} %get-tuple-element.56), channel_id=1, source_target_pairs={{0,1},{1,0},{2,3},{3,2},{4,5},{5,4},{6,7},{7,6},{8,9},{9,8},{10,11... | collective-permute-start | bytes 2555912 | tf_op jit(solution)/shard_map/ppermute | solution.py:360
  35.9 12.7 %collective-permute-start.8 = (bf16[8,208,128]{2,1,0:T(8,128)(2,1)S(1)}, bf16[8,208,128]{2,1,0:T(8,128)(2,1)S(1)}, u32[]{:S(2)}, u32[]{:S(2)}) collective-permute-start(bf16[8,208,128]{2,1,0:T(8,128)(2,1)S(1)} %get-tuple-element.54), channel_id=1, source_target_pairs={{0,16},{16,0},{1,17},{17,1},{2,18},{18,2},{3,19},{19,3},{4,20},{20... | collective-permute-start | bytes 1277960 | tf_op jit(solution)/shard_map/ppermute | solution.py:362
  40.2 9.8 %collective-permute-start.11 = (bf16[4,208,128]{2,1,0:T(8,128)(2,1)S(1)}, bf16[4,208,128]{2,1,0:T(8,128)(2,1)S(1)}, u32[]{:S(2)}, u32[]{:S(2)}) collective-permute-start(bf16[4,208,128]{2,1,0:T(8,128)(2,1)S(1)} %get-tuple-element.61), channel_id=1, source_target_pairs={{0,2},{1,3},{2,0},{3,1},{4,6},{5,7},{6,4},{7,5},{8,10},{9,11},{10,... | collective-permute-start | bytes 638984 | tf_op jit(solution)/shard_map/ppermute | solution.py:360
  41.1 12.0 %collective-permute-start.12 = (bf16[4,208,128]{2,1,0:T(8,128)(2,1)S(1)}, bf16[4,208,128]{2,1,0:T(8,128)(2,1)S(1)}, u32[]{:S(2)}, u32[]{:S(2)}) collective-permute-start(bf16[4,208,128]{2,1,0:T(8,128)(2,1)S(1)} %get-tuple-element.62), channel_id=1, source_target_pairs={{0,16},{16,0},{1,17},{17,1},{2,18},{18,2},{3,19},{19,3},{4,20},{20... | collective-permute-start | bytes 638984 | tf_op jit(solution)/shard_map/ppermute | solution.py:362
  41.7 15.8 %collective-permute-start.13 = (bf16[4,208,128]{2,1,0:T(8,128)(2,1)S(1)}, bf16[4,208,128]{2,1,0:T(8,128)(2,1)S(1)}, u32[]{:S(2)}, u32[]{:S(2)}) collective-permute-start(bf16[4,208,128]{2,1,0:T(8,128)(2,1)S(1)} %get-tuple-element.63), channel_id=1, source_target_pairs={{0,18},{1,19},{2,16},{3,17},{4,22},{5,23},{6,20},{7,21},{8,26},{9,... | collective-permute-start | bytes 638984 | tf_op jit(solution)/shard_map/ppermute | solution.py:364
  49.2 10.8 %collective-permute-start.10 = (bf16[4,208,128]{2,1,0:T(8,128)(2,1)S(1)}, bf16[4,208,128]{2,1,0:T(8,128)(2,1)S(1)}, u32[]{:S(2)}, u32[]{:S(2)}) collective-permute-start(bf16[4,208,128]{2,1,0:T(8,128)(2,1)S(1)} %get-tuple-element.60), channel_id=1, source_target_pairs={{0,2},{1,3},{2,0},{3,1},{4,6},{5,7},{6,4},{7,5},{8,10},{9,11},{10,... | collective-permute-start | bytes 638984 | tf_op jit(solution)/shard_map/ppermute | solution.py:360
  60.6 5.7 %collective-permute-start.14 = (bf16[2,208,128]{2,1,0:T(8,128)(2,1)S(1)}, bf16[2,208,128]{2,1,0:T(8,128)(2,1)S(1)}, u32[]{:S(2)}, u32[]{:S(2)}) collective-permute-start(bf16[2,208,128]{2,1,0:T(8,128)(2,1)S(1)} %get-tuple-element.66), channel_id=1, source_target_pairs={{0,4},{1,5},{2,6},{3,7},{4,0},{5,1},{6,2},{7,3},{8,12},{9,13},{10,... | collective-permute-start | bytes 319496 | tf_op jit(solution)/shard_map/ppermute | solution.py:360
  61.5 7.6 %collective-permute-start.16 = (bf16[1,208,128]{2,1,0:T(8,128)(2,1)S(1)}, bf16[1,208,128]{2,1,0:T(8,128)(2,1)S(1)}, u32[]{:S(2)}, u32[]{:S(2)}) collective-permute-start(bf16[1,208,128]{2,1,0:T(8,128)(2,1)S(1)} %get-tuple-element.69), channel_id=1, source_target_pairs={{0,4},{1,5},{2,6},{3,7},{4,0},{5,1},{6,2},{7,3},{8,12},{9,13},{10,... | collective-permute-start | bytes 159752 | tf_op jit(solution)/shard_map/ppermute | solution.py:360
  62.7 6.4 %collective-permute-start.17 = (bf16[1,208,128]{2,1,0:T(8,128)(2,1)S(1)}, bf16[1,208,128]{2,1,0:T(8,128)(2,1)S(1)}, u32[]{:S(2)}, u32[]{:S(2)}) collective-permute-start(bf16[1,208,128]{2,1,0:T(8,128)(2,1)S(1)} %get-tuple-element.70), channel_id=1, source_target_pairs={{0,8},{1,9},{2,10},{3,11},{4,12},{5,13},{6,14},{7,15},{8,0},{9,1},... | collective-permute-start | bytes 159752 | tf_op jit(solution)/shard_map/ppermute | solution.py:360
  65.3 5.9 %collective-permute-start.18 = (bf16[1,208,128]{2,1,0:T(8,128)(2,1)S(1)}, bf16[1,208,128]{2,1,0:T(8,128)(2,1)S(1)}, u32[]{:S(2)}, u32[]{:S(2)}) collective-permute-start(bf16[1,208,128]{2,1,0:T(8,128)(2,1)S(1)} %get-tuple-element.71), channel_id=1, source_target_pairs={{0,12},{1,13},{2,14},{3,15},{4,8},{5,9},{6,10},{7,11},{8,4},{9,5},... | collective-permute-start | bytes 159752 | tf_op jit(solution)/shard_map/ppermute | solution.py:360
  66.8 5.1 %collective-permute-start.15 = (bf16[1,208,128]{2,1,0:T(8,128)(2,1)S(1)}, bf16[1,208,128]{2,1,0:T(8,128)(2,1)S(1)}, u32[]{:S(2)}, u32[]{:S(2)}) collective-permute-start(bf16[1,208,128]{2,1,0:T(8,128)(2,1)S(1)} %get-tuple-element.68), channel_id=1, source_target_pairs={{0,8},{1,9},{2,10},{3,11},{4,12},{5,13},{6,14},{7,15},{8,0},{9,1},... | collective-permute-start | bytes 159752 | tf_op jit(solution)/shard_map/ppermute | solution.py:360
  72.5 4.2 %collective-permute-start.19 = (bf16[208,128]{1,0:T(8,128)(2,1)S(1)}, bf16[208,128]{1,0:T(8,128)(2,1)S(1)}, u32[]{:S(2)}, u32[]{:S(2)}) collective-permute-start(bf16[208,128]{1,0:T(8,128)(2,1)S(1)} %get-tuple-element.73), channel_id=1, source_target_pairs={{0,16},{16,0},{1,17},{17,1},{2,18},{18,2},{3,19},{19,3},{4,20},{20... | collective-permute-start | bytes 159752 | tf_op jit(solution)/shard_map/ppermute | solution.py:362

commit v6 on v5

--- a/solution.py
+++ b/solution.py
@@ -46,7 +46,7 @@
     return lax.dot_general(left, right, (((1,), (1,)), ((), ())), preferred_element_type=F32)
 
 
-def centre_kernel(cot, pooled, wide):
+def centre_kernel(cot, pooled, own, wide):
     images, height2, width2, channels = cot.shape
     width = width2 // 2
     wide[...] = jnp.zeros_like(wide)
@@ -56,6 +56,8 @@
             value = cot[i, r].astype(F32)
             for h in range(channels // 128):
                 wide[h, r, LEFT : LEFT + width2, :] = value[:, h * 128 : (h + 1) * 128]
+            own[i, r, 0:1, :] = value[:1]
+            own[i, r, 1:2, :] = value[width2 - 1 :]
         for r in range(height2):
             for h in range(channels // 128):
                 taps = [wide[h, r, pl.ds(LEFT - 1 + n, width, stride=2), :] for n in range(4)]
@@ -65,15 +67,14 @@
     lax.fori_loop(0, images, per_image, 0)
 
 
-def pool_columns(flags, cot, centre, col_a, col_b, i, lines):
-    width2 = cot.shape[2]
+def pool_columns(flags, centre, own, col_a, col_b, i, lines):
     width, channels = centre.shape[2:]
     col_odd, left, right = flags[COL_ODD] == 1, flags[LEFT_END] == 1, flags[RIGHT_END] == 1
     cell = lax.broadcasted_iota(jnp.int32, (width, channels), 0)
     is_first, is_last = cell == 0, cell == width - 1
     cells, beside = [], []
     for r in lines:
-        own_first, own_last = cot[i, r, 0:1].astype(F32), cot[i, r, width2 - 1 : width2].astype(F32)
+        own_first, own_last = own[i, r, 0:1, :], own[i, r, 1:2, :]
         one, two = col_a[i, r].astype(F32), col_b[i, r].astype(F32)
         before, after = jnp.where(col_odd, one, two), jnp.where(col_odd, two, one)
         near_before = jnp.where(left, own_first, before[3:4])
@@ -98,13 +99,13 @@
         window[v, pl.ds(at, width), :] = pooled[pl.ds(LEFT + 1 - v, width), :].astype(BF16)
 
 
-def row_pack_kernel(has_second, flags, cot, centre, col_a, col_b, *refs):
+def row_pack_kernel(has_second, flags, centre, own, col_a, col_b, *refs):
     outs, (cells_out, beside_out, ends) = refs[: 2 if has_second else 1], refs[-3:]
     images, height2, width, _ = centre.shape
     row_odd = flags[ROW_ODD] == 1
     lines = [0, 1, 2, height2 - 3, height2 - 2, height2 - 1]
     for i in range(images):
-        cells, beside = pool_columns(flags, cot, centre, col_a, col_b, i, lines)
+        cells, beside = pool_columns(flags, centre, own, col_a, col_b, i, lines)
         for n in range(6):
             cells_out[i, n] = cells[n]
             beside_out[i, n] = beside[n]
@@ -124,13 +125,13 @@
         outs[second][2 * images * width :, :] = ends[second].astype(BF16)
 
 
-def main_kernel(flags, cot, centre, col_a, col_b, weight, window, acc, pooled):
+def main_kernel(flags, centre, own, col_a, col_b, weight, window, acc, pooled):
     images, height2, width, channels = centre.shape
     height, depths = height2 // 2, weight.shape[0]
     pooled[...] = jnp.zeros_like(pooled)
 
     def per_image(i, carry):
-        cells, beside = pool_columns(flags, cot, centre, col_a, col_b, i, range(1, height2 - 1))
+        cells, beside = pool_columns(flags, centre, own, col_a, col_b, i, range(1, height2 - 1))
         for p in range(1, height - 1):
             at = 2 * p - 2
             both = [
@@ -217,11 +218,12 @@
     if len(split_refs) == 1:
         split_refs[0][...] = full[...]
         return
-    kept, sent = split_refs
+    kept, *sent = split_refs
     count, rows = kept.shape[:2]
+    size = sent[0].shape[0]
     for j in range(count):
         kept[j] = full[pl.ds(pl.multiple_of((2 * j + core) * rows, 16), rows), :]
-        sent[j] = full[pl.ds(pl.multiple_of((2 * j + 1 - core) * rows, 16), rows), :]
+        sent[j // size][j % size] = full[pl.ds(pl.multiple_of((2 * j + 1 - core) * rows, 16), rows), :]
 
 
 def conv_term_kernel(flags, window, saved, *refs):
@@ -278,53 +280,66 @@
     deal(full, split_refs, flags[CORE])
 
 
-def feat_grad_kernel(tokens, weight, out, done):
-    done[...] = jnp.zeros_like(done)
+def feat_grad_kernel(tokens, weight, out):
     images, depths, count, dim = out.shape
     for k in range(depths):
         out[:, k] = nt_dot(tokens[k], weight[k]).astype(BF16).reshape(images, count, dim)
 
 
-def round_kernel(parts, bits_at, bits, by_columns, flags, *refs):
-    ins, outs = refs[:parts], refs[parts:]
-    span = 1 << bits
-    mine, dp = 0, flags[DP]
-    for b in range(bits):
-        mine = mine + flags[BITS + bits_at + b] * (1 << b)
-    count, _, width = outs[0].shape
-    for n, out in enumerate(outs):
-        across, apart = n // span, n % span
-        for q in range(count):
-            block = q * span + (mine ^ apart)
+def take(part, block, at, columns=None):
+    size = part[0].shape[0]
+    return part[block // size][block % size + at, :, slice(None) if columns is None else columns].astype(F32)
+
+
+def round_kernel(jobs, flags, *refs):
+    ins, outs, dp = list(refs[: sum(sum(job[0]) for job in jobs)]), refs, flags[DP]
+    outs = list(refs[len(ins) :])
+    for sizes, at, bits, by_columns, cut in jobs:
+        parts = []
+        for size in sizes:
+            parts.append(ins[:size])
+            del ins[:size]
+        span = 1 << bits
+        mine = 0
+        for b in range(bits):
+            mine = mine + flags[BITS + at + b] * (1 << b)
+        for n in range(span * (2 if by_columns else 1)):
+            across, apart = n // span, n % span
+            pieces = outs[: cut if n else 1]
+            del outs[: len(pieces)]
+            count, _, width = pieces[0].shape
+            columns = None
             if by_columns:
                 columns = pl.ds(pl.multiple_of((dp ^ across) * width, width), width)
-            else:
-                columns = slice(None)
-            total = ins[0][block, :, columns].astype(F32)
-            for other in ins[1:]:
-                total = total + other[block, :, columns].astype(F32)
-            out[q] = total.astype(out.dtype)
+            for q in range(count):
+                total = take(parts[0], q * span, mine ^ apart, columns)
+                for other in parts[1:]:
+                    total = total + take(other, q * span, mine ^ apart, columns)
+                for p, piece in enumerate(pieces):
+                    piece[q] = total[:, p * width : (p + 1) * width].astype(piece.dtype)
 
 
 def last_kernel(early_parts, flags, *refs):
-    early, late, (sent, kept) = refs[:early_parts], refs[early_parts:-2], refs[-2:]
+    ins, (sent, kept) = list(refs[:-2]), refs[-2:]
     first = flags[DP] == 0
     sums = []
-    for group in (early, late):
-        total = group[0][0].astype(F32)
-        for other in group[1:]:
-            total = total + other[0].astype(F32)
+    for sizes in (early_parts, (1,) * (len(ins) - sum(early_parts))):
+        total = 0.0
+        for size in sizes:
+            total = total + take(ins[:size], 0, 0)
+            del ins[:size]
         sums.append(total)
-    sent[...] = jnp.where(first, sums[0], sums[1]).astype(BF16)
-    kept[...] = jnp.where(first, sums[1], sums[0])
+    wide = jnp.concatenate([sums[1], sums[1]], axis=1)
+    sent[...] = jnp.where(first, sums[0], wide).astype(BF16)
+    kept[...] = jnp.where(first, wide, sums[0])
 
 
 def join_kernel(scale, flags, kept, came, out):
-    width = kept.shape[1]
-    at = pl.multiple_of(flags[DP] * width, width)
-    out[:, pl.ds(at, width)] = kept[...] * scale
-    at = pl.multiple_of((1 - flags[DP]) * width, width)
-    out[:, pl.ds(at, width)] = came[...].astype(F32) * scale
+    half = kept.shape[1] // 2
+    first = flags[DP] == 0
+    mine, other = kept[...], came[...].astype(F32)
+    beside = jnp.concatenate([mine[:, :half], other[:, :half]], axis=1)
+    out[...] = jnp.where(first, beside, mine + other) * scale
 
 
 def vmem_call(kernel, out_shape, operands, scratch=(), scalars=1, flops=0, limit=16, after=(), aliases=()):
@@ -364,36 +379,41 @@
     return lax.ppermute(block, ("dp", "tile"), route)
 
 
-def core_sum(dealt, core):
+def core_sum(dealt, core, pieces=1):
     if len(dealt) == 1:
         tiles = lax.axis_size("tile")
         pairs = dealt[0].reshape(tiles // 2, 2, dealt[0].shape[0] // tiles, dealt[0].shape[1])
         kept = lax.dynamic_index_in_dim(pairs, core, 1, keepdims=False)
         sent = lax.dynamic_index_in_dim(pairs, 1 - core, 1, keepdims=False)
+        size = sent.shape[0] // pieces
+        sent = [sent[n * size : (n + 1) * size] for n in range(pieces)]
     else:
-        kept, sent = dealt
-    return [kept, xor_move(sent, 1, False)]
-
-
-def deal_round(parts, flags, at, bits, by_columns, after=()):
-    span = 1 << bits
-    count, rows, channels = parts[0].shape
-    if by_columns:
-        channels //= 2
-    outs = [
-        sds(count // span, rows, channels, dtype=F32 if n == 0 else BF16)
-        for n in range(span * (2 if by_columns else 1))
-    ]
-    return vmem_call(
-        functools.partial(round_kernel, len(parts), at, bits, by_columns), outs, [flags] + parts, after=after
-    )
-
-
-def send_round(pieces, at, bits):
-    span = 1 << bits
-    return [pieces[0]] + [
-        xor_move(pieces[n], (n % span) << at, n >= span) for n in range(1, len(pieces))
-    ]
+        kept, *sent = dealt
+    return [[kept], [xor_move(piece, 1, False) for piece in sent]]
+
+
+def deal_rounds(jobs, flags, after=()):
+    outs, plans, operands = [], [], [flags]
+    for parts, at, bits, by_columns, cut in jobs:
+        span = 1 << bits
+        count, rows, channels = parts[0][0].shape
+        channels = channels // 2 if by_columns else channels
+        for n in range(span * (2 if by_columns else 1)):
+            if n == 0:
+                outs.append(sds(count // span, rows, channels, dtype=F32))
+            else:
+                outs += [sds(count // span, rows, channels // cut)] * cut
+        plans.append((tuple(len(part) for part in parts), at, bits, by_columns, cut))
+        operands += [piece for part in parts for piece in part]
+    pieces = list(vmem_call(functools.partial(round_kernel, plans), outs, operands, after=after))
+    token, sums = pieces[0], []
+    for _, at, bits, by_columns, cut in plans:
+        span = 1 << bits
+        parts = [[pieces.pop(0)]]
+        for n in range(1, span * (2 if by_columns else 1)):
+            parts.append([xor_move(pieces.pop(0), (n % span) << at, n >= span) for _ in range(cut)])
+        sums.append(parts)
+    return sums, token
 
 
 def per_device(features, proj_weight, conv_weight, saved, cotangent):
@@ -424,9 +444,9 @@
     around = paired(TILE_COLS, 1) + [(0, TILE_COLS - 1), (TILE_COLS - 1, 0)]
     col_b = swap(jnp.where(col % 2 == 1, high, low), None, around)
     col_a = swap(jnp.where(col % 2 == 1, low, high), None, paired(TILE_COLS, 0))
-    centre = vmem_call(
+    centre, own = vmem_call(
         centre_kernel,
-        sds(images, height2, width, channels, dtype=F32),
+        [sds(images, height2, width, channels, dtype=F32), sds(images, height2, 2, channels, dtype=F32)],
         (cotangent,),
         scratch=(pltpu.VMEM((channels // 128, height2, LEFT + width2 + 8, 128), F32),),
         scalars=0,
@@ -435,7 +455,7 @@
         functools.partial(row_pack_kernel, has_second),
         [sds(2 * images * (width + 2), channels)] * sides
         + [sds(images, 6, width, channels, dtype=F32), sds(images, 6, 2, channels, dtype=F32)],
-        (flags, cotangent, centre, col_a, col_b),
+        (flags, centre, own, col_a, col_b),
         scratch=(pltpu.VMEM((sides, 4 * images, channels), F32),),
     )
     came_rows = [swap(row_out[n], paired(rows, n), None) for n in range(sides)]
@@ -443,7 +463,7 @@
     window, acc = vmem_call(
         main_kernel,
         [sds(3, (height + 2) * line, channels), sds(depths, patches, channels, dtype=F32)],
-        (flags, cotangent, centre, col_a, col_b, conv_weight),
+        (flags, centre, own, col_a, col_b, conv_weight),
         scratch=(pltpu.VMEM((height, LEFT + width + 8, channels), F32),),
         flops=conv_flops,
         after=(row_out[0],),
@@ -467,10 +487,12 @@
     half_rows = depths * (dim + 9 * channels) // 2
     conv_late = half_rows - depths * dim
     block_rows = half_rows // tile_count
+    pieces = 4
     if block_rows % 16:
         dealt = [sds(half_rows, channels)]
     else:
-        dealt = [sds(tile_count // 2, block_rows, channels)] * 2
+        dealt = [sds(tile_count // 2, block_rows, channels)]
+        dealt += [sds(tile_count // 2 // pieces, block_rows, channels)] * pieces
     full = pltpu.VMEM((half_rows, channels), BF16)
     *early, conv_top = vmem_call(
         conv_term_kernel,
@@ -478,9 +500,8 @@
         (flags, window, saved),
         scratch=(full, pltpu.VMEM((patches, channels), BF16)),
         flops=conv_flops,
-        after=(to_pass,),
-    )
-    early_parts = core_sum(early, position % 2)
+    )
+    (early_parts,), before = deal_rounds([(core_sum(early, position % 2, pieces), 1, 1, False, 1)], flags)
     proj_flops = 2 * images * tokens * depths * dim * channels
     *terms, token_grad = vmem_call(
         proj_term_kernel,
@@ -488,34 +509,32 @@
         [flags] + came + [passed, features, conv_top],
         scratch=(full,),
         flops=proj_flops,
-    )
-    early_pieces = deal_round(early_parts, flags, 1, 0, True, after=(token_grad,))
-    early_parts = send_round(early_pieces, 1, 0)
-    feature_grad, done = vmem_call(
+        after=(before,),
+    )
+    (late_parts,), before = deal_rounds(
+        [(core_sum(terms, position % 2, pieces), 1, 1, True, 1)], flags, after=(token_grad,)
+    )
+    at = 2
+    while at < bits:
+        step = min(2, bits - at)
+        if step == 2:
+            (early_parts,), before = deal_rounds([(early_parts, at, 1, False, 1)], flags, after=(before,))
+        (late_parts, early_parts), before = deal_rounds(
+            [(late_parts, at, step, False, 1), (early_parts, at + step - 1, 1, False, 1)], flags, after=(before,)
+        )
+        at += step
+    feature_grad = vmem_call(
         feat_grad_kernel,
-        [sds(images, depths, tokens, dim), sds(8, 128, dtype=F32)],
+        sds(images, depths, tokens, dim),
         (token_grad, proj_weight),
         scalars=0,
         flops=proj_flops,
-        after=(early_pieces[0],),
-    )
-    late_parts = core_sum(terms, position % 2)
-    at, before = 1, done
-    while at < bits:
-        late_step = 1 if at == 1 else min(2, bits - at)
-        late_pieces = deal_round(late_parts, flags, at, late_step, at == 1, after=(before,))
-        late_parts = send_round(late_pieces, at, late_step)
-        before = late_pieces[0]
-        for bit in range(at, at + late_step):
-            early_pieces = deal_round(early_parts, flags, bit, 1, False, after=(before,))
-            early_parts = send_round(early_pieces, bit, 1)
-            before = early_pieces[0]
-        at += late_step
-    half = sds(block_rows, channels // 2)
+        after=(before,),
+    )
     sent, kept = vmem_call(
-        functools.partial(last_kernel, len(early_parts)),
-        [half, sds(block_rows, channels // 2, dtype=F32)],
-        [flags] + early_parts + late_parts,
+        functools.partial(last_kernel, tuple(len(part) for part in early_parts)),
+        [sds(block_rows, channels), sds(block_rows, channels, dtype=F32)],
+        [flags] + [piece for part in early_parts + late_parts for piece in part],
     )
     other = xor_move(sent, 0, True)
     scale = 1.0 / math.sqrt(images * lax.axis_size("dp") * tokens * tile_count)

time: 78.2 us -> 69.1 us (0.88)
  waiting for transfers between devices: 28.4 us -> 20.6 us
  Pallas kernels: 17.4 us -> 16.3 us
    ppermute x3 -> x2, waiting for transfers between devices: 10.5 us -> 1.24 us  [xor_move(): return lax.ppermute(block, 'dp', [(0, 1), (1, 0)])]
    ppermute x13 -> x19, waiting for transfers between devices: 12 us -> 18.7 us  [xor_move(): return lax.ppermute(block, 'tile', [(t, t ^ apart) for t in range(tiles)])]
    ppermute x1, waiting for transfers between devices: 4.36 us -> 0.01 us  [xor_move(): return lax.ppermute(block, ('dp', 'tile'), route)]
    ppermute x13 -> x19, starting transfers between devices: 14 us -> 16 us  [xor_move(): return lax.ppermute(block, 'tile', [(t, t ^ apart) for t in range(tiles)])]
    ppermute x1, starting transfers between devices: 2.14 us -> 1.01 us  [xor_move(): return lax.ppermute(block, ('dp', 'tile'), route)]
    pallas_call x16 -> x14, Pallas kernels: 17.4 us -> 16.3 us  [vmem_call(): pl.pallas_call(run, out_shape=out_shape, in_specs=specs, out_specs=jax.tr...]
    ppermute x3, waiting for transfers between devices: 1.6 us -> 0.71 us  [swap(): return lax.ppermute(block, 'tile', tile_route(row_pairs, col_pairs, rows))]
    unnamed x16 -> x14, local copies, waits for them, and re-layouts: 3.44 us -> 2.8 us
  transfers between devices with their start and end apart: 20 -> 25, of which waited for: 13 -> 12; matrix products, arithmetic and copies ran while one was open for 0% -> 0% of each run, Pallas kernels for 13% -> 16%
where the time goes in v6:
time: 69.1 us; the launch traced here: 68.9 us
  starting transfers between devices  26.2 us (38%)
  waiting for transfers between devices  20.6 us (30%)
  Pallas kernels  16.3 us (24%)
  local copies, waits for them, and re-layouts  2.89 us (4%)
  other arithmetic  2.02 us (3%)
  between operations  0.85 us (1%)
    ppermute x19, waiting for transfers between devices, xor_move(): return lax.ppermute(block, 'tile', [(t, t ^ apart) for t in range(tiles)])  18.7 us
    pallas_call x14, Pallas kernels, vmem_call(): pl.pallas_call(run, out_shape=out_shape, in_specs=specs, out_specs=jax.tr...  16.3 us
    ppermute x19, starting transfers between devices, xor_move(): return lax.ppermute(block, 'tile', [(t, t ^ apart) for t in range(tiles)])  16 us
    ppermute x3, starting transfers between devices, swap(): return lax.ppermute(block, 'tile', tile_route(row_pairs, col_pairs, rows))  6.13 us
    ppermute x2, starting transfers between devices, xor_move(): return lax.ppermute(block, 'dp', [(0, 1), (1, 0)])  3.04 us
    unnamed x14, local copies, waits for them, and re-layouts  2.8 us
    select_n x1, other arithmetic, per_device(): col_b = swap(jnp.where(col % 2 == 1, high, low), None, around)  2.02 us
  transfers between devices with their start and end apart: 25, of which 12 were waited for; matrix products, arithmetic and copies ran while one was open for 0% of the time, Pallas kernels for 16%

profile of v6, /device:TPU:0, one launch (start us, length us, event | category | flops | bytes accessed | tf_op | source)
XLA Modules:
  0.0 68.9 jit_solution(2974472278310231478)
XLA Ops:
  0.7 2.0 %broadcast_select_fusion = (bf16[4,16,4,256]{3,2,1,0:T(4,128)(2,1)}, bf16[4,16,4,256]{3,2,1,0:T(4,128)(2,1)}) fusion(pred[]{:T(512)S(6)} %eq.27, bf16[4,16,32,256]{3,2,1,0:T(8,128)(2,1)} %refs_0_.1), kind=kLoop, calls=%fused_computation | loop fusion | flops 131072 | bytes 524289 | tf_op jit(solution)/shard_map/jit(_where)/select_n | solution.py:445
  2.7 3.0 %collective-permute-start.1 = (bf16[4,16,4,256]{3,2,1,0:T(4,128)(2,1)}, bf16[4,16,4,256]{3,2,1,0:T(4,128)(2,1)S(1)}, u32[]{:S(2)}, u32[]{:S(2)}) collective-permute-start(bf16[4,16,4,256]{3,2,1,0:T(4,128)(2,1)} %get-tuple-element.82), channel_id=1, source_target_pairs={{1,3},{3,1},{2,6},{6,2},{7,5},{5,7},{0,4},{4,0},{9,11},{11,9},{10,... | collective-permute-start | bytes 393224 | tf_op jit(solution)/shard_map/ppermute | solution.py:441
  5.7 0.0 collective-permute-start
  5.7 1.2 %copy-done.2 = bf16[4,16,32,256]{3,2,1,0:T(8,128)(2,1)S(1)} copy-done((bf16[4,16,32,256]{3,2,1,0:T(8,128)(2,1)S(1)}, bf16[4,16,32,256]{3,2,1,0:T(8,128)(2,1)}, u32[]{:S(2)}) %copy-start.2) | copy-done | bytes 1048600
  7.0 0.5 shard_map.68
  7.4 0.0 copy-start.4
  7.4 0.6 copy-done.4
  8.1 0.1 stack.71.refs_0_
  8.2 0.7 %collective-permute-done.1.refs_4_ = bf16[4,16,4,256]{3,2,1,0:T(4,128)(2,1)S(1)} collective-permute-done((bf16[4,16,4,256]{3,2,1,0:T(4,128)(2,1)}, bf16[4,16,4,256]{3,2,1,0:T(4,128)(2,1)S(1)}, u32[]{:S(2)}, u32[]{:S(2)}) %collective-permute-start.1) | collective-permute-done | bytes 131104 | tf_op jit(solution)/shard_map/ppermute | solution.py:441
  8.9 0.0 collective-permute-done.refs_3_
  8.9 0.9 %copy-done.5 = f32[4,16,2,256]{3,2,1,0:T(2,128)S(1)} copy-done((f32[4,16,2,256]{3,2,1,0:T(2,128)S(1)}, f32[4,16,2,256]{3,2,1,0:T(2,128)}, u32[]{:S(2)}) %copy-start.5) | copy-done | bytes 131096
  9.8 1.1 %shard_map.69 = (bf16[144,256]{1,0:T(8,128)(2,1)S(1)}, f32[4,6,16,256]{3,2,1,0:T(8,128)S(1)}, f32[4,6,2,256]{3,2,1,0:T(2,128)S(1)}) custom-call(s32[13]{0:T(128)S(1)} %stack.71.refs_0_, f32[4,16,16,256]{3,2,1,0:T(8,128)S(1)} %get-tuple-element.42.refs_1_, f32[4,16,2,256]{3,2,1,0:T(2,128)S(1)} %copy-done.5, ...), custom_call_target="tpu_custom_call" | custom-call | bytes 1957940 | tf_op jit(solution)/shard_map/pallas_call | solution.py:356
  10.9 3.1 %collective-permute-start.2 = (bf16[144,256]{1,0:T(8,128)(2,1)S(1)}, bf16[144,256]{1,0:T(8,128)(2,1)S(1)}, u32[]{:S(2)}, u32[]{:S(2)}) collective-permute-start(bf16[144,256]{1,0:T(8,128)(2,1)S(1)} %get-tuple-element.44.refs_6_), channel_id=1, source_target_pairs={{0,8},{1,9},{3,11},{2,10},{6,14},{7,15},{5,13},{4,12},{8,0},{9,1},... | collective-permute-start | bytes 221192 | tf_op jit(solution)/shard_map/ppermute | solution.py:441
  14.0 2.8 %shard_map.70 = (bf16[3,640,256]{2,1,0:T(8,128)(2,1)S(1)}, f32[2,512,256]{2,1,0:T(8,128)S(1)}) custom-call(s32[13]{0:T(128)S(1)} %stack.71.refs_0_, f32[4,16,16,256]{3,2,1,0:T(8,128)S(1)} %get-tuple-element.42.refs_1_, f32[4,16,2,256]{3,2,1,0:T(2,128)S(1)} %copy-done.5, bf16[4,16,4,256]{3,2,1,0:T(4,128)(2,1)} %collective-permute-done.refs_3_, ...), custom_call_target="tpu_custom_call" | custom-call | flops 1207959552 | bytes 5832756 | tf_op jit(solution)/shard_map/pallas_call | solution.py:356
  16.8 0.0 collective-permute-done.2.refs_1_
  16.8 0.0 copy-start.6
  16.8 1.6 %shard_map.71 = (bf16[2,2,64,256]{3,2,1,0:T(8,128)(2,1)S(1)}, bf16[2,2,64,256]{3,2,1,0:T(8,128)(2,1)S(1)}, bf16[2,2,64,256]{3,2,1,0:T(8,128)(2,1)S(1)}, bf16[2,2...) custom-call(s32[13]{0:T(128)S(1)} %stack.71.refs_0_, ...), custom_call_target="tpu_custom_call", output_to_operand_aliasing={{4}: (4, {})} | custom-call | flops 301989888 | bytes 6414388 | tf_op jit(solution)/shard_map/pallas_call | solution.py:356
  18.5 1.6 %collective-permute-start.3 = (bf16[2,2,64,256]{3,2,1,0:T(8,128)(2,1)S(1)}, bf16[2,2,64,256]{3,2,1,0:T(8,128)(2,1)S(1)}, u32[]{:S(2)}, u32[]{:S(2)}) collective-permute-start(bf16[2,2,64,256]{3,2,1,0:T(8,128)(2,1)S(1)} %get-tuple-element.50), channel_id=1, source_target_pairs={{0,2},{1,3},{2,0},{3,1},{4,6},{5,7},{6,4},{7,5},{8,10},{9,11},{10,... | collective-permute-start | bytes 393224 | tf_op jit(solution)/shard_map/ppermute | solution.py:375
  20.0 1.6 %collective-permute-start.4 = (bf16[2,2,64,256]{3,2,1,0:T(8,128)(2,1)S(1)}, bf16[2,2,64,256]{3,2,1,0:T(8,128)(2,1)S(1)}, u32[]{:S(2)}, u32[]{:S(2)}) collective-permute-start(bf16[2,2,64,256]{3,2,1,0:T(8,128)(2,1)S(1)} %get-tuple-element.51), channel_id=1, source_target_pairs={{0,4},{1,5},{2,6},{3,7},{4,0},{5,1},{6,2},{7,3},{8,12},{9,13},{10,... | collective-permute-start | bytes 393224 | tf_op jit(solution)/shard_map/ppermute | solution.py:375
  21.6 0.4 collective-permute-start.5
  22.0 2.1 %shard_map.73 = (bf16[8,208,256]{2,1,0:T(8,128)(2,1)S(1)}, bf16[2,208,256]{2,1,0:T(8,128)(2,1)S(1)}, bf16[2,208,256]{2,1,0:T(8,128)(2,1)S(1)}, bf16[2,208,256]{2...) custom-call(s32[13]{0:T(128)S(1)} %stack.71.refs_0_, ...), custom_call_target="tpu_custom_call" | custom-call | flops 1207959552 | bytes 3866676 | tf_op jit(solution)/shard_map/pallas_call | solution.py:356
  24.1 0.0 copy-start.1
  24.1 0.1 collective-permute-start.7
  24.2 0.5 collective-permute-start.8
  24.7 0.0 collective-permute-done.3.refs_1_.refs_2_
  24.7 0.1 collective-permute-start.9
  24.8 0.9 %collective-permute-done.4.refs_2_.refs_3_ = bf16[2,2,64,256]{3,2,1,0:T(8,128)(2,1)S(1)} collective-permute-done((bf16[2,2,64,256]{3,2,1,0:T(8,128)(2,1)S(1)}, bf16[2,2,64,256]{3,2,1,0:T(8,128)(2,1)S(1)}, u32[]{:S(2)}, u32[]{:S(2)}) %collective-permute-start.4) | collective-permute-done | bytes 131104 | tf_op jit(solution)/shard_map/ppermute | solution.py:375
  25.7 0.0 collective-permute-start.10
  25.7 1.8 %collective-permute-done.5.refs_3_.refs_4_ = bf16[2,2,64,256]{3,2,1,0:T(8,128)(2,1)S(1)} collective-permute-done((bf16[2,2,64,256]{3,2,1,0:T(8,128)(2,1)S(1)}, bf16[2,2,64,256]{3,2,1,0:T(8,128)(2,1)S(1)}, u32[]{:S(2)}, u32[]{:S(2)}) %collective-permute-start.5) | collective-permute-done | bytes 131104 | tf_op jit(solution)/shard_map/ppermute | solution.py:375
  27.5 0.1 collective-permute-start.6
  27.6 0.0 collective-permute-done.7.refs_2_
  27.6 0.0 collective-permute-done.8.refs_3_
  27.6 0.7 %shard_map.74 = (f32[4,208,256]{2,1,0:T(8,128)S(1)}, bf16[4,208,256]{2,1,0:T(8,128)(2,1)S(1)}) custom-call(s32[13]{0:T(128)S(1)} %stack.71.refs_0_, bf16[8,208,256]{2,1,0:T(8,128)(2,1)S(1)} %get-tuple-element.55.refs_1_, bf16[2,208,256]{2,1,0:T(8,128)(2,1)S(1)} %collective-permute-done.7.refs_2_, bf16[2,208,256]{2,1,0:T(8,128)(2,1)S(1)} %collective-permute-done.8.refs_3_, ...), custom_call_target="tpu_custom_call" | custom-call | bytes 2981940 | tf_op jit(solution)/shard_map/pallas_call | solution.py:356
  28.4 1.1 %collective-permute-start.18 = (bf16[4,208,256]{2,1,0:T(8,128)(2,1)S(1)}, bf16[4,208,256]{2,1,0:T(8,128)(2,1)S(1)}, u32[]{:S(2)}, u32[]{:S(2)}) collective-permute-start(bf16[4,208,256]{2,1,0:T(8,128)(2,1)S(1)} %get-tuple-element.71), channel_id=1, source_target_pairs={{0,2},{1,3},{2,0},{3,1},{4,6},{5,7},{6,4},{7,5},{8,10},{9,11},{10,... | collective-permute-start | bytes 1277960 | tf_op jit(solution)/shard_map/ppermute | solution.py:375
  29.5 0.0 collective-permute-done.6.refs_5_
  29.5 1.5 %shard_map.75 = (bf16[8,208,256]{2,1,0:T(8,128)(2,1)S(1)}, bf16[2,208,256]{2,1,0:T(8,128)(2,1)S(1)}, bf16[2,208,256]{2,1,0:T(8,128)(2,1)S(1)}, bf16[2,208,256]{2...) custom-call(s32[13]{0:T(128)S(1)} %stack.71.refs_0_, ...), custom_call_target="tpu_custom_call" | custom-call | flops 536870912 | bytes 5767220 | tf_op jit(solution)/shard_map/pallas_call | solution.py:356
  31.0 0.3 collective-permute-start.11
  31.2 0.3 collective-permute-start.12
  31.5 0.2 collective-permute-start.13
  31.7 0.3 collective-permute-start.14
  32.0 0.4 collective-permute-done.11.refs_2_
  32.5 0.3 collective-permute-done.12.refs_3_
  32.8 0.3 collective-permute-done.13.refs_4_
  33.1 0.3 collective-permute-done.14.refs_5_
  33.4 0.7 %shard_map.76 = (f32[4,208,128]{2,1,0:T(8,128)S(1)}, bf16[4,208,128]{2,1,0:T(8,128)(2,1)S(1)}, bf16[4,208,128]{2,1,0:T(8,128)(2,1)S(1)}, bf16[4,208,128]{2,1,0:T(8,128)(2,1)S(1)}) custom-call(s32[13]{0:T(128)S(1)} %stack.71.refs_0_, bf16[8,208,256]{2,1,0:T(8,128)(2,1)S(1)} %get-tuple-element.62.refs_1_, ...), custom_call_target="tpu_custom_call" | custom-call | bytes 2768948 | tf_op jit(solution)/shard_map/pallas_call | solution.py:356
  34.1 1.1 %collective-permute-start.15 = (bf16[4,208,128]{2,1,0:T(8,128)(2,1)S(1)}, bf16[4,208,128]{2,1,0:T(8,128)(2,1)S(1)}, u32[]{:S(2)}, u32[]{:S(2)}) collective-permute-start(bf16[4,208,128]{2,1,0:T(8,128)(2,1)S(1)} %get-tuple-element.68), channel_id=1, source_target_pairs={{0,2},{1,3},{2,0},{3,1},{4,6},{5,7},{6,4},{7,5},{8,10},{9,11},{10,... | collective-permute-start | bytes 638984 | tf_op jit(solution)/shard_map/ppermute | solution.py:375
  35.2 1.5 %collective-permute-start.16 = (bf16[4,208,128]{2,1,0:T(8,128)(2,1)S(1)}, bf16[4,208,128]{2,1,0:T(8,128)(2,1)S(1)}, u32[]{:S(2)}, u32[]{:S(2)}) collective-permute-start(bf16[4,208,128]{2,1,0:T(8,128)(2,1)S(1)} %get-tuple-element.69), channel_id=1, source_target_pairs={{0,16},{16,0},{1,17},{17,1},{2,18},{18,2},{3,19},{19,3},{4,20},{20... | collective-permute-start | bytes 638984 | tf_op jit(solution)/shard_map/ppermute | solution.py:377
  36.7 1.0 %collective-permute-start.17 = (bf16[4,208,128]{2,1,0:T(8,128)(2,1)S(1)}, bf16[4,208,128]{2,1,0:T(8,128)(2,1)S(1)}, u32[]{:S(2)}, u32[]{:S(2)}) collective-permute-start(bf16[4,208,128]{2,1,0:T(8,128)(2,1)S(1)} %get-tuple-element.70), channel_id=1, source_target_pairs={{0,18},{1,19},{2,16},{3,17},{4,22},{5,23},{6,20},{7,21},{8,26},{9,... | collective-permute-start | bytes 638984 | tf_op jit(solution)/shard_map/ppermute | solution.py:379
  37.7 3.3 %collective-permute-done.18.refs_2_ = bf16[4,208,256]{2,1,0:T(8,128)(2,1)S(1)} collective-permute-done((bf16[4,208,256]{2,1,0:T(8,128)(2,1)S(1)}, bf16[4,208,256]{2,1,0:T(8,128)(2,1)S(1)}, u32[]{:S(2)}, u32[]{:S(2)}) %collective-permute-start.18) | collective-permute-done | bytes 426016 | tf_op jit(solution)/shard_map/ppermute | solution.py:375
  41.0 0.6 shard_map.77
  41.7 0.9 %collective-permute-start.19 = (bf16[2,208,256]{2,1,0:T(8,128)(2,1)S(1)}, bf16[2,208,256]{2,1,0:T(8,128)(2,1)S(1)}, u32[]{:S(2)}, u32[]{:S(2)}) collective-permute-start(bf16[2,208,256]{2,1,0:T(8,128)(2,1)S(1)} %get-tuple-element.73), channel_id=1, source_target_pairs={{0,4},{1,5},{2,6},{3,7},{4,0},{5,1},{6,2},{7,3},{8,12},{9,13},{10,... | collective-permute-start | bytes 638984 | tf_op jit(solution)/shard_map/ppermute | solution.py:375
  42.6 7.1 %collective-permute-done.15.refs_2_ = bf16[4,208,128]{2,1,0:T(8,128)(2,1)S(1)} collective-permute-done((bf16[4,208,128]{2,1,0:T(8,128)(2,1)S(1)}, bf16[4,208,128]{2,1,0:T(8,128)(2,1)S(1)}, u32[]{:S(2)}, u32[]{:S(2)}) %collective-permute-start.15) | collective-permute-done | bytes 213024 | tf_op jit(solution)/shard_map/ppermute | solution.py:375
  49.8 0.7 %shard_map.78 = (f32[1,208,128]{2,1,0:T(8,128)S(1)}, bf16[1,208,128]{2,1,0:T(8,128)(2,1)S(1)}, bf16[1,208,128]{2,1,0:T(8,128)(2,1)S(1)}, bf16[1,208,128]{2,1,0:T...) custom-call(s32[13]{0:T(128)S(1)} %stack.71.refs_0_, ...), custom_call_target="tpu_custom_call" | custom-call | bytes 2289716 | tf_op jit(solution)/shard_map/pallas_call | solution.py:356
  50.5 3.2 %collective-permute-start.20 = (bf16[1,208,256]{2,1,0:T(8,128)(2,1)S(1)}, bf16[1,208,256]{2,1,0:T(8,128)(2,1)S(1)}, u32[]{:S(2)}, u32[]{:S(2)}) collective-permute-start(bf16[1,208,256]{2,1,0:T(8,128)(2,1)S(1)} %get-tuple-element.76), channel_id=1, source_target_pairs={{0,8},{1,9},{2,10},{3,11},{4,12},{5,13},{6,14},{7,15},{8,0},{9,1},... | collective-permute-start | bytes 319496 | tf_op jit(solution)/shard_map/ppermute | solution.py:375
  53.6 0.5 collective-permute-start.21
  54.1 0.2 collective-permute-start.22
  54.3 3.7 %collective-permute-start.23 = (bf16[1,208,128]{2,1,0:T(8,128)(2,1)S(1)}, bf16[1,208,128]{2,1,0:T(8,128)(2,1)S(1)}, u32[]{:S(2)}, u32[]{:S(2)}) collective-permute-start(bf16[1,208,128]{2,1,0:T(8,128)(2,1)S(1)} %get-tuple-element.79), channel_id=1, source_target_pairs={{0,12},{1,13},{2,14},{3,15},{4,8},{5,9},{6,10},{7,11},{8,4},{9,5},... | collective-permute-start | bytes 159752 | tf_op jit(solution)/shard_map/ppermute | solution.py:375
  58.0 0.4 collective-permute-done.21.refs_4_
  58.4 3.7 %collective-permute-done.22.refs_5_ = bf16[1,208,128]{2,1,0:T(8,128)(2,1)S(1)} collective-permute-done((bf16[1,208,128]{2,1,0:T(8,128)(2,1)S(1)}, bf16[1,208,128]{2,1,0:T(8,128)(2,1)S(1)}, u32[]{:S(2)}, u32[]{:S(2)}) %collective-permute-start.22) | collective-permute-done | bytes 53280 | tf_op jit(solution)/shard_map/ppermute | solution.py:375
  62.1 0.6 shard_map.80
  62.7 1.6 %collective-permute-start.24 = (bf16[208,256]{1,0:T(8,128)(2,1)S(1)}, bf16[208,256]{1,0:T(8,128)(2,1)S(1)}, u32[]{:S(2)}, u32[]{:S(2)}) collective-permute-start(bf16[208,256]{1,0:T(8,128)(2,1)S(1)} %get-tuple-element.81), channel_id=1, source_target_pairs={{0,16},{16,0},{1,17},{17,1},{2,18},{18,2},{3,19},{19,3},{4,20},{20... | collective-permute-start | bytes 319496 | tf_op jit(solution)/shard_map/ppermute | solution.py:377
  64.3 2.1 %shard_map.79 = bf16[4,2,128,1024]{3,2,1,0:T(8,128)(2,1)} custom-call(bf16[2,512,256]{2,1,0:T(8,128)(2,1)S(1)} %get-tuple-element.61.refs_6_.refs_0_, bf16[2,1024,256]{2,1,0:T(8,128)(2,1)S(1)} %copy-done.3, f32[1,208,128]{2,1,0:T(8,128)S(1)} %get-tuple-element.74.refs_2_.refs_3_), custom_call_target="tpu_custom_call" | custom-call | flops 536870912 | bytes 3670016 | tf_op jit(solution)/shard_map/pallas_call | solution.py:356
  66.4 1.2 %collective-permute-done.24.refs_2_ = bf16[208,256]{1,0:T(8,128)(2,1)S(1)} collective-permute-done((bf16[208,256]{1,0:T(8,128)(2,1)S(1)}, bf16[208,256]{1,0:T(8,128)(2,1)S(1)}, u32[]{:S(2)}, u32[]{:S(2)}) %collective-permute-start.24) | collective-permute-done | bytes 106528 | tf_op jit(solution)/shard_map/ppermute | solution.py:377
  67.6 1.3 %shard_map.81 = f32[208,256]{1,0:T(8,128)} custom-call(s32[13]{0:T(128)S(1)} %stack.71.refs_0_, f32[208,256]{1,0:T(8,128)S(1)} %get-tuple-element.80.refs_1_, bf16[208,256]{1,0:T(8,128)(2,1)S(1)} %collective-permute-done.24.refs_2_), custom_call_target="tpu_custom_call" | custom-call | bytes 532532 | tf_op jit(solution)/shard_map/pallas_call | solution.py:356
  (16 shorter events, 0.1 us)
Async XLA Ops:
  0.6 13.4 %copy-start = (bf16[2,3,3,256,256]{4,3,2,1,0:T(8,128)(2,1)S(1)}, bf16[2,3,3,256,256]{4,3,2,1,0:T(8,128)(2,1)}, u32[]{:S(2)}) copy-start(bf16[2,3,3,256,256]{4,3,2,1,0:T(8,128)(2,1)} %refs_6_.2) | copy-start | bytes 7077892
  2.7 6.2 %collective-permute-start.1 = (bf16[4,16,4,256]{3,2,1,0:T(4,128)(2,1)}, bf16[4,16,4,256]{3,2,1,0:T(4,128)(2,1)S(1)}, u32[]{:S(2)}, u32[]{:S(2)}) collective-permute-start(bf16[4,16,4,256]{3,2,1,0:T(4,128)(2,1)} %get-tuple-element.82), channel_id=1, source_target_pairs={{1,3},{3,1},{2,6},{6,2},{7,5},{5,7},{0,4},{4,0},{9,11},{11,9},{10,... | collective-permute-start | bytes 393224 | tf_op jit(solution)/shard_map/ppermute | solution.py:441
  5.7 3.2 %collective-permute-start = (bf16[4,16,4,256]{3,2,1,0:T(4,128)(2,1)}, bf16[4,16,4,256]{3,2,1,0:T(4,128)(2,1)}, u32[]{:S(2)}, u32[]{:S(2)}) collective-permute-start(bf16[4,16,4,256]{3,2,1,0:T(4,128)(2,1)} %get-tuple-element.83), channel_id=1, source_target_pairs={{0,1},{1,0},{3,2},{2,3},{6,7},{7,6},{5,4},{4,5},{8,9},{9,8},{11,10... | collective-permute-start | bytes 393224 | tf_op jit(solution)/shard_map/ppermute | solution.py:441
  5.7 1.2 %copy-start.2 = (bf16[4,16,32,256]{3,2,1,0:T(8,128)(2,1)S(1)}, bf16[4,16,32,256]{3,2,1,0:T(8,128)(2,1)}, u32[]{:S(2)}) copy-start(bf16[4,16,32,256]{3,2,1,0:T(8,128)(2,1)} %refs_0_.1) | copy-start | bytes 3145732
  7.4 0.7 copy-start.4
  8.9 0.9 %copy-start.5 = (f32[4,16,2,256]{3,2,1,0:T(2,128)S(1)}, f32[4,16,2,256]{3,2,1,0:T(2,128)}, u32[]{:S(2)}) copy-start(f32[4,16,2,256]{3,2,1,0:T(2,128)} %copy-done.4) | copy-start | bytes 393220
  10.9 5.9 %collective-permute-start.2 = (bf16[144,256]{1,0:T(8,128)(2,1)S(1)}, bf16[144,256]{1,0:T(8,128)(2,1)S(1)}, u32[]{:S(2)}, u32[]{:S(2)}) collective-permute-start(bf16[144,256]{1,0:T(8,128)(2,1)S(1)} %get-tuple-element.44.refs_6_), channel_id=1, source_target_pairs={{0,8},{1,9},{3,11},{2,10},{6,14},{7,15},{5,13},{4,12},{8,0},{9,1},... | collective-permute-start | bytes 221192 | tf_op jit(solution)/shard_map/ppermute | solution.py:441
  16.8 5.2 %copy-start.6 = (bf16[4,2,8,16,256]{4,3,2,1,0:T(8,128)(2,1)S(1)}, bf16[4,2,8,16,256]{4,3,2,1,0:T(8,128)(2,1)}, u32[]{:S(2)}) copy-start(bf16[4,2,8,16,256]{4,3,2,1,0:T(8,128)(2,1)} %refs_2_.1) | copy-start | bytes 1572868
  18.5 6.2 %collective-permute-start.3 = (bf16[2,2,64,256]{3,2,1,0:T(8,128)(2,1)S(1)}, bf16[2,2,64,256]{3,2,1,0:T(8,128)(2,1)S(1)}, u32[]{:S(2)}, u32[]{:S(2)}) collective-permute-start(bf16[2,2,64,256]{3,2,1,0:T(8,128)(2,1)S(1)} %get-tuple-element.50), channel_id=1, source_target_pairs={{0,2},{1,3},{2,0},{3,1},{4,6},{5,7},{6,4},{7,5},{8,10},{9,11},{10,... | collective-permute-start | bytes 393224 | tf_op jit(solution)/shard_map/ppermute | solution.py:375
  20.0 5.6 %collective-permute-start.4 = (bf16[2,2,64,256]{3,2,1,0:T(8,128)(2,1)S(1)}, bf16[2,2,64,256]{3,2,1,0:T(8,128)(2,1)S(1)}, u32[]{:S(2)}, u32[]{:S(2)}) collective-permute-start(bf16[2,2,64,256]{3,2,1,0:T(8,128)(2,1)S(1)} %get-tuple-element.51), channel_id=1, source_target_pairs={{0,4},{1,5},{2,6},{3,7},{4,0},{5,1},{6,2},{7,3},{8,12},{9,13},{10,... | collective-permute-start | bytes 393224 | tf_op jit(solution)/shard_map/ppermute | solution.py:375
  21.6 5.9 %collective-permute-start.5 = (bf16[2,2,64,256]{3,2,1,0:T(8,128)(2,1)S(1)}, bf16[2,2,64,256]{3,2,1,0:T(8,128)(2,1)S(1)}, u32[]{:S(2)}, u32[]{:S(2)}) collective-permute-start(bf16[2,2,64,256]{3,2,1,0:T(8,128)(2,1)S(1)} %get-tuple-element.52), channel_id=1, source_target_pairs={{0,6},{1,7},{2,4},{3,5},{4,2},{5,3},{6,0},{7,1},{8,14},{9,15},{10,... | collective-permute-start | bytes 393224 | tf_op jit(solution)/shard_map/ppermute | solution.py:375
  24.1 5.4 %copy-start.1 = (bf16[4,2,128,1024]{3,2,1,0:T(8,128)(2,1)S(1)}, bf16[4,2,128,1024]{3,2,1,0:T(8,128)(2,1)}, u32[]{:S(2)}) copy-start(bf16[4,2,128,1024]{3,2,1,0:T(8,128)(2,1)} %refs_6_.3) | copy-start | bytes 6291460
  24.1 3.5 %collective-permute-start.7 = (bf16[2,208,256]{2,1,0:T(8,128)(2,1)S(1)}, bf16[2,208,256]{2,1,0:T(8,128)(2,1)S(1)}, u32[]{:S(2)}, u32[]{:S(2)}) collective-permute-start(bf16[2,208,256]{2,1,0:T(8,128)(2,1)S(1)} %get-tuple-element.56), channel_id=1, source_target_pairs={{0,1},{1,0},{2,3},{3,2},{4,5},{5,4},{6,7},{7,6},{8,9},{9,8},{10,11... | collective-permute-start | bytes 638984 | tf_op jit(solution)/shard_map/ppermute | solution.py:375
  24.2 3.4 %collective-permute-start.8 = (bf16[2,208,256]{2,1,0:T(8,128)(2,1)S(1)}, bf16[2,208,256]{2,1,0:T(8,128)(2,1)S(1)}, u32[]{:S(2)}, u32[]{:S(2)}) collective-permute-start(bf16[2,208,256]{2,1,0:T(8,128)(2,1)S(1)} %get-tuple-element.57), channel_id=1, source_target_pairs={{0,1},{1,0},{2,3},{3,2},{4,5},{5,4},{6,7},{7,6},{8,9},{9,8},{10,11... | collective-permute-start | bytes 638984 | tf_op jit(solution)/shard_map/ppermute | solution.py:375
  24.7 2.9 %collective-permute-start.9 = (bf16[2,208,256]{2,1,0:T(8,128)(2,1)S(1)}, bf16[2,208,256]{2,1,0:T(8,128)(2,1)S(1)}, u32[]{:S(2)}, u32[]{:S(2)}) collective-permute-start(bf16[2,208,256]{2,1,0:T(8,128)(2,1)S(1)} %get-tuple-element.58), channel_id=1, source_target_pairs={{0,1},{1,0},{2,3},{3,2},{4,5},{5,4},{6,7},{7,6},{8,9},{9,8},{10,11... | collective-permute-start | bytes 638984 | tf_op jit(solution)/shard_map/ppermute | solution.py:375
  25.7 2.0 %collective-permute-start.10 = (bf16[2,208,256]{2,1,0:T(8,128)(2,1)S(1)}, bf16[2,208,256]{2,1,0:T(8,128)(2,1)S(1)}, u32[]{:S(2)}, u32[]{:S(2)}) collective-permute-start(bf16[2,208,256]{2,1,0:T(8,128)(2,1)S(1)} %get-tuple-element.59), channel_id=1, source_target_pairs={{0,1},{1,0},{2,3},{3,2},{4,5},{5,4},{6,7},{7,6},{8,9},{9,8},{10,11... | collective-permute-start | bytes 638984 | tf_op jit(solution)/shard_map/ppermute | solution.py:375
  27.5 2.0 %collective-permute-start.6 = (bf16[4,2,64,256]{3,2,1,0:T(8,128)(2,1)S(1)}, bf16[4,2,64,256]{3,2,1,0:T(8,128)(2,1)S(1)}, u32[]{:S(2)}, u32[]{:S(2)}) collective-permute-start(bf16[4,2,64,256]{3,2,1,0:T(8,128)(2,1)S(1)} %shard_map.72), channel_id=1, source_target_pairs={{0,1},{1,0},{2,3},{3,2},{4,5},{5,4},{6,7},{7,6},{8,9},{9,8},{10,11... | collective-permute-start | bytes 786440 | tf_op jit(solution)/shard_map/ppermute | solution.py:375
  28.4 12.7 %collective-permute-start.18 = (bf16[4,208,256]{2,1,0:T(8,128)(2,1)S(1)}, bf16[4,208,256]{2,1,0:T(8,128)(2,1)S(1)}, u32[]{:S(2)}, u32[]{:S(2)}) collective-permute-start(bf16[4,208,256]{2,1,0:T(8,128)(2,1)S(1)} %get-tuple-element.71), channel_id=1, source_target_pairs={{0,2},{1,3},{2,0},{3,1},{4,6},{5,7},{6,4},{7,5},{8,10},{9,11},{10,... | collective-permute-start | bytes 1277960 | tf_op jit(solution)/shard_map/ppermute | solution.py:375
  31.0 1.5 %collective-permute-start.11 = (bf16[2,208,256]{2,1,0:T(8,128)(2,1)S(1)}, bf16[2,208,256]{2,1,0:T(8,128)(2,1)S(1)}, u32[]{:S(2)}, u32[]{:S(2)}) collective-permute-start(bf16[2,208,256]{2,1,0:T(8,128)(2,1)S(1)} %get-tuple-element.63), channel_id=1, source_target_pairs={{0,1},{1,0},{2,3},{3,2},{4,5},{5,4},{6,7},{7,6},{8,9},{9,8},{10,11... | collective-permute-start | bytes 638984 | tf_op jit(solution)/shard_map/ppermute | solution.py:375
  31.2 1.6 %collective-permute-start.12 = (bf16[2,208,256]{2,1,0:T(8,128)(2,1)S(1)}, bf16[2,208,256]{2,1,0:T(8,128)(2,1)S(1)}, u32[]{:S(2)}, u32[]{:S(2)}) collective-permute-start(bf16[2,208,256]{2,1,0:T(8,128)(2,1)S(1)} %get-tuple-element.64), channel_id=1, source_target_pairs={{0,1},{1,0},{2,3},{3,2},{4,5},{5,4},{6,7},{7,6},{8,9},{9,8},{10,11... | collective-permute-start | bytes 638984 | tf_op jit(solution)/shard_map/ppermute | solution.py:375
  31.5 1.6 %collective-permute-start.13 = (bf16[2,208,256]{2,1,0:T(8,128)(2,1)S(1)}, bf16[2,208,256]{2,1,0:T(8,128)(2,1)S(1)}, u32[]{:S(2)}, u32[]{:S(2)}) collective-permute-start(bf16[2,208,256]{2,1,0:T(8,128)(2,1)S(1)} %get-tuple-element.65), channel_id=1, source_target_pairs={{0,1},{1,0},{2,3},{3,2},{4,5},{5,4},{6,7},{7,6},{8,9},{9,8},{10,11... | collective-permute-start | bytes 638984 | tf_op jit(solution)/shard_map/ppermute | solution.py:375
  31.7 1.7 %collective-permute-start.14 = (bf16[2,208,256]{2,1,0:T(8,128)(2,1)S(1)}, bf16[2,208,256]{2,1,0:T(8,128)(2,1)S(1)}, u32[]{:S(2)}, u32[]{:S(2)}) collective-permute-start(bf16[2,208,256]{2,1,0:T(8,128)(2,1)S(1)} %get-tuple-element.66), channel_id=1, source_target_pairs={{0,1},{1,0},{2,3},{3,2},{4,5},{5,4},{6,7},{7,6},{8,9},{9,8},{10,11... | collective-permute-start | bytes 638984 | tf_op jit(solution)/shard_map/ppermute | solution.py:375
  34.1 15.6 %collective-permute-start.15 = (bf16[4,208,128]{2,1,0:T(8,128)(2,1)S(1)}, bf16[4,208,128]{2,1,0:T(8,128)(2,1)S(1)}, u32[]{:S(2)}, u32[]{:S(2)}) collective-permute-start(bf16[4,208,128]{2,1,0:T(8,128)(2,1)S(1)} %get-tuple-element.68), channel_id=1, source_target_pairs={{0,2},{1,3},{2,0},{3,1},{4,6},{5,7},{6,4},{7,5},{8,10},{9,11},{10,... | collective-permute-start | bytes 638984 | tf_op jit(solution)/shard_map/ppermute | solution.py:375
  35.2 14.6 %collective-permute-start.16 = (bf16[4,208,128]{2,1,0:T(8,128)(2,1)S(1)}, bf16[4,208,128]{2,1,0:T(8,128)(2,1)S(1)}, u32[]{:S(2)}, u32[]{:S(2)}) collective-permute-start(bf16[4,208,128]{2,1,0:T(8,128)(2,1)S(1)} %get-tuple-element.69), channel_id=1, source_target_pairs={{0,16},{16,0},{1,17},{17,1},{2,18},{18,2},{3,19},{19,3},{4,20},{20... | collective-permute-start | bytes 638984 | tf_op jit(solution)/shard_map/ppermute | solution.py:377
  36.7 13.1 %collective-permute-start.17 = (bf16[4,208,128]{2,1,0:T(8,128)(2,1)S(1)}, bf16[4,208,128]{2,1,0:T(8,128)(2,1)S(1)}, u32[]{:S(2)}, u32[]{:S(2)}) collective-permute-start(bf16[4,208,128]{2,1,0:T(8,128)(2,1)S(1)} %get-tuple-element.70), channel_id=1, source_target_pairs={{0,18},{1,19},{2,16},{3,17},{4,22},{5,23},{6,20},{7,21},{8,26},{9,... | collective-permute-start | bytes 638984 | tf_op jit(solution)/shard_map/ppermute | solution.py:379
  41.0 23.2 %copy-start.3 = (bf16[2,1024,256]{2,1,0:T(8,128)(2,1)S(1)}, bf16[2,1024,256]{2,1,0:T(8,128)(2,1)}, u32[]{:S(2)}) copy-start(bf16[2,1024,256]{2,1,0:T(8,128)(2,1)} %refs_1_.1) | copy-start | bytes 3145732
  41.7 8.1 %collective-permute-start.19 = (bf16[2,208,256]{2,1,0:T(8,128)(2,1)S(1)}, bf16[2,208,256]{2,1,0:T(8,128)(2,1)S(1)}, u32[]{:S(2)}, u32[]{:S(2)}) collective-permute-start(bf16[2,208,256]{2,1,0:T(8,128)(2,1)S(1)} %get-tuple-element.73), channel_id=1, source_target_pairs={{0,4},{1,5},{2,6},{3,7},{4,0},{5,1},{6,2},{7,3},{8,12},{9,13},{10,... | collective-permute-start | bytes 638984 | tf_op jit(solution)/shard_map/ppermute | solution.py:375
  50.5 11.7 %collective-permute-start.20 = (bf16[1,208,256]{2,1,0:T(8,128)(2,1)S(1)}, bf16[1,208,256]{2,1,0:T(8,128)(2,1)S(1)}, u32[]{:S(2)}, u32[]{:S(2)}) collective-permute-start(bf16[1,208,256]{2,1,0:T(8,128)(2,1)S(1)} %get-tuple-element.76), channel_id=1, source_target_pairs={{0,8},{1,9},{2,10},{3,11},{4,12},{5,13},{6,14},{7,15},{8,0},{9,1},... | collective-permute-start | bytes 319496 | tf_op jit(solution)/shard_map/ppermute | solution.py:375
  53.6 4.8 %collective-permute-start.21 = (bf16[1,208,128]{2,1,0:T(8,128)(2,1)S(1)}, bf16[1,208,128]{2,1,0:T(8,128)(2,1)S(1)}, u32[]{:S(2)}, u32[]{:S(2)}) collective-permute-start(bf16[1,208,128]{2,1,0:T(8,128)(2,1)S(1)} %get-tuple-element.77), channel_id=1, source_target_pairs={{0,4},{1,5},{2,6},{3,7},{4,0},{5,1},{6,2},{7,3},{8,12},{9,13},{10,... | collective-permute-start | bytes 159752 | tf_op jit(solution)/shard_map/ppermute | solution.py:375
  54.1 8.0 %collective-permute-start.22 = (bf16[1,208,128]{2,1,0:T(8,128)(2,1)S(1)}, bf16[1,208,128]{2,1,0:T(8,128)(2,1)S(1)}, u32[]{:S(2)}, u32[]{:S(2)}) collective-permute-start(bf16[1,208,128]{2,1,0:T(8,128)(2,1)S(1)} %get-tuple-element.78), channel_id=1, source_target_pairs={{0,8},{1,9},{2,10},{3,11},{4,12},{5,13},{6,14},{7,15},{8,0},{9,1},... | collective-permute-start | bytes 159752 | tf_op jit(solution)/shard_map/ppermute | solution.py:375
  54.3 7.8 %collective-permute-start.23 = (bf16[1,208,128]{2,1,0:T(8,128)(2,1)S(1)}, bf16[1,208,128]{2,1,0:T(8,128)(2,1)S(1)}, u32[]{:S(2)}, u32[]{:S(2)}) collective-permute-start(bf16[1,208,128]{2,1,0:T(8,128)(2,1)S(1)} %get-tuple-element.79), channel_id=1, source_target_pairs={{0,12},{1,13},{2,14},{3,15},{4,8},{5,9},{6,10},{7,11},{8,4},{9,5},... | collective-permute-start | bytes 159752 | tf_op jit(solution)/shard_map/ppermute | solution.py:375
  62.7 4.9 %collective-permute-start.24 = (bf16[208,256]{1,0:T(8,128)(2,1)S(1)}, bf16[208,256]{1,0:T(8,128)(2,1)S(1)}, u32[]{:S(2)}, u32[]{:S(2)}) collective-permute-start(bf16[208,256]{1,0:T(8,128)(2,1)S(1)} %get-tuple-element.81), channel_id=1, source_target_pairs={{0,16},{16,0},{1,17},{17,1},{2,18},{18,2},{3,19},{19,3},{4,20},{20... | collective-permute-start | bytes 319496 | tf_op jit(solution)/shard_map/ppermute | solution.py:377

commit v7 on v6

--- a/solution.py
+++ b/solution.py
@@ -46,7 +46,7 @@
     return lax.dot_general(left, right, (((1,), (1,)), ((), ())), preferred_element_type=F32)
 
 
-def centre_kernel(cot, pooled, own, wide):
+def centre_kernel(cot, pooled, wide):
     images, height2, width2, channels = cot.shape
     width = width2 // 2
     wide[...] = jnp.zeros_like(wide)
@@ -56,31 +56,31 @@
             value = cot[i, r].astype(F32)
             for h in range(channels // 128):
                 wide[h, r, LEFT : LEFT + width2, :] = value[:, h * 128 : (h + 1) * 128]
-            own[i, r, 0:1, :] = value[:1]
-            own[i, r, 1:2, :] = value[width2 - 1 :]
+            pooled[i, r, width : width + 1, :] = value[:1]
+            pooled[i, r, width + 1 : width + 2, :] = value[width2 - 1 :]
         for r in range(height2):
             for h in range(channels // 128):
                 taps = [wide[h, r, pl.ds(LEFT - 1 + n, width, stride=2), :] for n in range(4)]
-                pooled[i, r, :, h * 128 : (h + 1) * 128] = 0.75 * (taps[1] + taps[2]) + 0.25 * (taps[0] + taps[3])
+                pooled[i, r, :width, h * 128 : (h + 1) * 128] = 0.75 * (taps[1] + taps[2]) + 0.25 * (taps[0] + taps[3])
         return carry
 
     lax.fori_loop(0, images, per_image, 0)
 
 
-def pool_columns(flags, centre, own, col_a, col_b, i, lines):
-    width, channels = centre.shape[2:]
+def pool_columns(flags, centre, col_a, col_b, i, lines):
+    width, channels = centre.shape[2] - 8, centre.shape[3]
     col_odd, left, right = flags[COL_ODD] == 1, flags[LEFT_END] == 1, flags[RIGHT_END] == 1
     cell = lax.broadcasted_iota(jnp.int32, (width, channels), 0)
     is_first, is_last = cell == 0, cell == width - 1
     cells, beside = [], []
     for r in lines:
-        own_first, own_last = own[i, r, 0:1, :], own[i, r, 1:2, :]
+        own_first, own_last = centre[i, r, width : width + 1, :], centre[i, r, width + 1 : width + 2, :]
         one, two = col_a[i, r].astype(F32), col_b[i, r].astype(F32)
         before, after = jnp.where(col_odd, one, two), jnp.where(col_odd, two, one)
         near_before = jnp.where(left, own_first, before[3:4])
         near_after = jnp.where(right, own_last, after[0:1])
         cells.append(
-            centre[i, r] + 0.25 * (jnp.where(is_first, near_before, 0.0) + jnp.where(is_last, near_after, 0.0))
+            centre[i, r, :width, :] + 0.25 * (jnp.where(is_first, near_before, 0.0) + jnp.where(is_last, near_after, 0.0))
         )
         first = 0.75 * (before[2:3] + before[3:4]) + 0.25 * (before[1:2] + own_first)
         last = 0.75 * (after[0:1] + after[1:2]) + 0.25 * (own_last + after[2:3])
@@ -99,13 +99,13 @@
         window[v, pl.ds(at, width), :] = pooled[pl.ds(LEFT + 1 - v, width), :].astype(BF16)
 
 
-def row_pack_kernel(has_second, flags, centre, own, col_a, col_b, *refs):
+def row_pack_kernel(has_second, flags, centre, col_a, col_b, *refs):
     outs, (cells_out, beside_out, ends) = refs[: 2 if has_second else 1], refs[-3:]
-    images, height2, width, _ = centre.shape
+    images, height2, width = centre.shape[0], centre.shape[1], centre.shape[2] - 8
     row_odd = flags[ROW_ODD] == 1
     lines = [0, 1, 2, height2 - 3, height2 - 2, height2 - 1]
     for i in range(images):
-        cells, beside = pool_columns(flags, centre, own, col_a, col_b, i, lines)
+        cells, beside = pool_columns(flags, centre, col_a, col_b, i, lines)
         for n in range(6):
             cells_out[i, n] = cells[n]
             beside_out[i, n] = beside[n]
@@ -125,13 +125,13 @@
         outs[second][2 * images * width :, :] = ends[second].astype(BF16)
 
 
-def main_kernel(flags, centre, own, col_a, col_b, weight, window, acc, pooled):
-    images, height2, width, channels = centre.shape
+def main_kernel(flags, centre, col_a, col_b, weight, window, acc, pooled):
+    images, height2, width, channels = centre.shape[0], centre.shape[1], centre.shape[2] - 8, centre.shape[3]
     height, depths = height2 // 2, weight.shape[0]
     pooled[...] = jnp.zeros_like(pooled)
 
     def per_image(i, carry):
-        cells, beside = pool_columns(flags, centre, own, col_a, col_b, i, range(1, height2 - 1))
+        cells, beside = pool_columns(flags, centre, col_a, col_b, i, range(1, height2 - 1))
         for p in range(1, height - 1):
             at = 2 * p - 2
             both = [
@@ -214,7 +214,7 @@
             grads[apart // 2][apart % 2, k] = total[pl.ds(at, line), :].astype(BF16)
 
 
-def deal(full, split_refs, core):
+def deal(full, split_refs, core, turned):
     if len(split_refs) == 1:
         split_refs[0][...] = full[...]
         return
@@ -222,8 +222,9 @@
     count, rows = kept.shape[:2]
     size = sent[0].shape[0]
     for j in range(count):
-        kept[j] = full[pl.ds(pl.multiple_of((2 * j + core) * rows, 16), rows), :]
-        sent[j // size][j % size] = full[pl.ds(pl.multiple_of((2 * j + 1 - core) * rows, 16), rows), :]
+        p = j >> 1 | (j & 1) * (count >> 1) if turned else j
+        kept[p] = full[pl.ds(pl.multiple_of((2 * j + core) * rows, 16), rows), :]
+        sent[p // size][p % size] = full[pl.ds(pl.multiple_of((2 * j + 1 - core) * rows, 16), rows), :]
 
 
 def conv_term_kernel(flags, window, saved, *refs):
@@ -248,7 +249,7 @@
                 top[at : at + channels, :] = part
             else:
                 full[at - split : at - split + channels, :] = part
-    deal(full, split_refs, flags[CORE])
+    deal(full, split_refs, flags[CORE], True)
 
 
 def pass_on_kernel(*refs):
@@ -277,7 +278,7 @@
         )
         full[k * dim : (k + 1) * dim, :] = part.astype(BF16)
     full[depths * dim :, :] = conv_top[...]
-    deal(full, split_refs, flags[CORE])
+    deal(full, split_refs, flags[CORE], False)
 
 
 def feat_grad_kernel(tokens, weight, out):
@@ -294,7 +295,7 @@
 def round_kernel(jobs, flags, *refs):
     ins, outs, dp = list(refs[: sum(sum(job[0]) for job in jobs)]), refs, flags[DP]
     outs = list(refs[len(ins) :])
-    for sizes, at, bits, by_columns, cut in jobs:
+    for sizes, at, bits, by_columns, heights in jobs:
         parts = []
         for size in sizes:
             parts.append(ins[:size])
@@ -305,7 +306,7 @@
             mine = mine + flags[BITS + at + b] * (1 << b)
         for n in range(span * (2 if by_columns else 1)):
             across, apart = n // span, n % span
-            pieces = outs[: cut if n else 1]
+            pieces = outs[: len(heights) if n else 1]
             del outs[: len(pieces)]
             count, _, width = pieces[0].shape
             columns = None
@@ -315,8 +316,10 @@
                 total = take(parts[0], q * span, mine ^ apart, columns)
                 for other in parts[1:]:
                     total = total + take(other, q * span, mine ^ apart, columns)
-                for p, piece in enumerate(pieces):
-                    piece[q] = total[:, p * width : (p + 1) * width].astype(piece.dtype)
+                start = 0
+                for piece in pieces:
+                    piece[q] = total[start : start + piece.shape[1]].astype(piece.dtype)
+                    start += piece.shape[1]
 
 
 def last_kernel(early_parts, flags, *refs):
@@ -326,7 +329,8 @@
     for sizes in (early_parts, (1,) * (len(ins) - sum(early_parts))):
         total = 0.0
         for size in sizes:
-            total = total + take(ins[:size], 0, 0)
+            rows = [piece[0].astype(F32) for piece in ins[:size]]
+            total = total + (jnp.concatenate(rows, axis=0) if size > 1 else rows[0])
             del ins[:size]
         sums.append(total)
     wide = jnp.concatenate([sums[1], sums[1]], axis=1)
@@ -379,10 +383,13 @@
     return lax.ppermute(block, ("dp", "tile"), route)
 
 
-def core_sum(dealt, core, pieces=1):
+def core_sum(dealt, core, pieces, turned):
     if len(dealt) == 1:
         tiles = lax.axis_size("tile")
-        pairs = dealt[0].reshape(tiles // 2, 2, dealt[0].shape[0] // tiles, dealt[0].shape[1])
+        rows, channels = dealt[0].shape[0] // tiles, dealt[0].shape[1]
+        pairs = dealt[0].reshape(tiles // 2, 2, rows, channels)
+        if turned:
+            pairs = pairs.reshape(tiles // 4, 2, 2, rows, channels).swapaxes(0, 1).reshape(pairs.shape)
         kept = lax.dynamic_index_in_dim(pairs, core, 1, keepdims=False)
         sent = lax.dynamic_index_in_dim(pairs, 1 - core, 1, keepdims=False)
         size = sent.shape[0] // pieces
@@ -398,20 +405,24 @@
         span = 1 << bits
         count, rows, channels = parts[0][0].shape
         channels = channels // 2 if by_columns else channels
+        tiles = rows // 16
+        heights = [rows]
+        if rows % 16 == 0 and cut > 1:
+            heights = [16 * (tiles * (n + 1) // cut - tiles * n // cut) for n in range(cut)]
         for n in range(span * (2 if by_columns else 1)):
             if n == 0:
                 outs.append(sds(count // span, rows, channels, dtype=F32))
             else:
-                outs += [sds(count // span, rows, channels // cut)] * cut
-        plans.append((tuple(len(part) for part in parts), at, bits, by_columns, cut))
+                outs += [sds(count // span, height, channels) for height in heights]
+        plans.append((tuple(len(part) for part in parts), at, bits, by_columns, tuple(heights)))
         operands += [piece for part in parts for piece in part]
     pieces = list(vmem_call(functools.partial(round_kernel, plans), outs, operands, after=after))
     token, sums = pieces[0], []
-    for _, at, bits, by_columns, cut in plans:
+    for _, at, bits, by_columns, heights in plans:
         span = 1 << bits
         parts = [[pieces.pop(0)]]
         for n in range(1, span * (2 if by_columns else 1)):
-            parts.append([xor_move(pieces.pop(0), (n % span) << at, n >= span) for _ in range(cut)])
+            parts.append([xor_move(pieces.pop(0), (n % span) << at, n >= span) for _ in heights])
         sums.append(parts)
     return sums, token
 
@@ -444,9 +455,9 @@
     around = paired(TILE_COLS, 1) + [(0, TILE_COLS - 1), (TILE_COLS - 1, 0)]
     col_b = swap(jnp.where(col % 2 == 1, high, low), None, around)
     col_a = swap(jnp.where(col % 2 == 1, low, high), None, paired(TILE_COLS, 0))
-    centre, own = vmem_call(
+    centre = vmem_call(
         centre_kernel,
-        [sds(images, height2, width, channels, dtype=F32), sds(images, height2, 2, channels, dtype=F32)],
+        sds(images, height2, width + 8, channels, dtype=F32),
         (cotangent,),
         scratch=(pltpu.VMEM((channels // 128, height2, LEFT + width2 + 8, 128), F32),),
         scalars=0,
@@ -455,7 +466,7 @@
         functools.partial(row_pack_kernel, has_second),
         [sds(2 * images * (width + 2), channels)] * sides
         + [sds(images, 6, width, channels, dtype=F32), sds(images, 6, 2, channels, dtype=F32)],
-        (flags, centre, own, col_a, col_b),
+        (flags, centre, col_a, col_b),
         scratch=(pltpu.VMEM((sides, 4 * images, channels), F32),),
     )
     came_rows = [swap(row_out[n], paired(rows, n), None) for n in range(sides)]
@@ -463,7 +474,7 @@
     window, acc = vmem_call(
         main_kernel,
         [sds(3, (height + 2) * line, channels), sds(depths, patches, channels, dtype=F32)],
-        (flags, centre, own, col_a, col_b, conv_weight),
+        (flags, centre, col_a, col_b, conv_weight),
         scratch=(pltpu.VMEM((height, LEFT + width + 8, channels), F32),),
         flops=conv_flops,
         after=(row_out[0],),
@@ -501,7 +512,7 @@
         scratch=(full, pltpu.VMEM((patches, channels), BF16)),
         flops=conv_flops,
     )
-    (early_parts,), before = deal_rounds([(core_sum(early, position % 2, pieces), 1, 1, False, 1)], flags)
+    (early_parts,), before = deal_rounds([(core_sum(early, position % 2, pieces, True), 2, 1, False, 1)], flags)
     proj_flops = 2 * images * tokens * depths * dim * channels
     *terms, token_grad = vmem_call(
         proj_term_kernel,
@@ -512,17 +523,20 @@
         after=(before,),
     )
     (late_parts,), before = deal_rounds(
-        [(core_sum(terms, position % 2, pieces), 1, 1, True, 1)], flags, after=(token_grad,)
-    )
-    at = 2
+        [(core_sum(terms, position % 2, pieces, False), 1, 1, True, 1)], flags, after=(token_grad,)
+    )
+    at, early_bits = 2, list(range(3, bits)) + [1]
     while at < bits:
         step = min(2, bits - at)
-        if step == 2:
-            (early_parts,), before = deal_rounds([(early_parts, at, 1, False, 1)], flags, after=(before,))
-        (late_parts, early_parts), before = deal_rounds(
-            [(late_parts, at, step, False, 1), (early_parts, at + step - 1, 1, False, 1)], flags, after=(before,)
+        if len(early_bits) > 1:
+            (early_parts,), before = deal_rounds([(early_parts, early_bits.pop(0), 1, False, 1)], flags, after=(before,))
+        (late_parts,), before = deal_rounds([(late_parts, at, step, False, 1)], flags, after=(before,))
+        at += step
+    while early_bits:
+        bit = early_bits.pop(0)
+        (early_parts,), before = deal_rounds(
+            [(early_parts, bit, 1, False, 3 if bit == 1 else 1)], flags, after=(before,)
         )
-        at += step
     feature_grad = vmem_call(
         feat_grad_kernel,
         sds(images, depths, tokens, dim),

time: 69.1 us -> 68.7 us (level)
  starting transfers between devices: 26.2 us -> 28 us
  waiting for transfers between devices: 20.6 us -> 19.3 us
  other arithmetic: 2.02 us -> 1.19 us
    ppermute x19 -> x21, waiting for transfers between devices: 18.7 us -> 13.2 us  [xor_move(): return lax.ppermute(block, 'tile', [(t, t ^ apart) for t in range(tiles)])]
    ppermute x1, waiting for transfers between devices: 0.01 us -> 3.45 us  [xor_move(): return lax.ppermute(block, ('dp', 'tile'), route)]
    ppermute x19 -> x21, starting transfers between devices: 16 us -> 18.3 us  [xor_move(): return lax.ppermute(block, 'tile', [(t, t ^ apart) for t in range(tiles)])]
    select_n x1, other arithmetic: 2.02 us -> 1.19 us  [per_device(): col_b = swap(jnp.where(col % 2 == 1, high, low), None, around)]
    pallas_call x14 -> x15, Pallas kernels: 16.3 us -> 16.1 us  [vmem_call(): pl.pallas_call(run, out_shape=out_shape, in_specs=specs, out_specs=jax.tr...]
    unnamed x14 -> x12, local copies, waits for them, and re-layouts: 2.8 us -> 2.91 us
  transfers between devices with their start and end apart: 25 -> 27, of which waited for: 12 -> 14; matrix products, arithmetic and copies ran while one was open for 0% -> 0% of each run, Pallas kernels for 16% -> 17%
where the time goes in v7:
time: 68.7 us; the launch traced here: 68.5 us
  starting transfers between devices  28 us (41%)
  waiting for transfers between devices  19.3 us (28%)
  Pallas kernels  16.1 us (23%)
  local copies, waits for them, and re-layouts  3 us (4%)
  other arithmetic  1.19 us (2%)
  between operations  0.89 us (1%)
    ppermute x21, starting transfers between devices, xor_move(): return lax.ppermute(block, 'tile', [(t, t ^ apart) for t in range(tiles)])  18.3 us
    pallas_call x15, Pallas kernels, vmem_call(): pl.pallas_call(run, out_shape=out_shape, in_specs=specs, out_specs=jax.tr...  16.1 us
    ppermute x21, waiting for transfers between devices, xor_move(): return lax.ppermute(block, 'tile', [(t, t ^ apart) for t in range(tiles)])  13.2 us
    ppermute x3, starting transfers between devices, swap(): return lax.ppermute(block, 'tile', tile_route(row_pairs, col_pairs, rows))  6.19 us
    ppermute x1, waiting for transfers between devices, xor_move(): return lax.ppermute(block, ('dp', 'tile'), route)  3.45 us
    ppermute x2, starting transfers between devices, xor_move(): return lax.ppermute(block, 'dp', [(0, 1), (1, 0)])  3.06 us
    unnamed x12, local copies, waits for them, and re-layouts  2.91 us
    ppermute x2, waiting for transfers between devices, xor_move(): return lax.ppermute(block, 'dp', [(0, 1), (1, 0)])  1.55 us
  transfers between devices with their start and end apart: 27, of which 14 were waited for; matrix products, arithmetic and copies ran while one was open for 0% of the time, Pallas kernels for 17%

profile of v7, /device:TPU:0, one launch (start us, length us, event | category | flops | bytes accessed | tf_op | source)
XLA Modules:
  0.0 68.5 jit_solution(5663900497881549848)
XLA Ops:
  0.7 1.2 %broadcast_select_fusion = (bf16[4,16,4,256]{3,2,1,0:T(4,128)(2,1)S(1)}, bf16[4,16,4,256]{3,2,1,0:T(4,128)(2,1)S(1)}) fusion(pred[]{:T(512)S(6)} %eq.27, bf16[4,16,32,256]{3,2,1,0:T(8,128)(2,1)} %refs_0_.1), kind=kLoop, calls=%fused_computation | loop fusion | flops 131072 | bytes 524289 | tf_op jit(solution)/shard_map/jit(_where)/select_n | solution.py:456
  1.9 3.1 %collective-permute-start.1 = (bf16[4,16,4,256]{3,2,1,0:T(4,128)(2,1)S(1)}, bf16[4,16,4,256]{3,2,1,0:T(4,128)(2,1)S(1)}, u32[]{:S(2)}, u32[]{:S(2)}) collective-permute-start(bf16[4,16,4,256]{3,2,1,0:T(4,128)(2,1)S(1)} %get-tuple-element.82), channel_id=1, source_target_pairs={{1,3},{3,1},{2,6},{6,2},{7,5},{5,7},{0,4},{4,0},{9,11},{11,9},{10,... | collective-permute-start | bytes 393224 | tf_op jit(solution)/shard_map/ppermute | solution.py:452
  4.9 0.0 collective-permute-start
  4.9 1.2 %copy-done.3 = bf16[4,16,32,256]{3,2,1,0:T(8,128)(2,1)S(1)} copy-done((bf16[4,16,32,256]{3,2,1,0:T(8,128)(2,1)S(1)}, bf16[4,16,32,256]{3,2,1,0:T(8,128)(2,1)}, u32[]{:S(2)}) %copy-start.3) | copy-done | bytes 1048600
  6.2 0.5 shard_map.68.refs_1_
  6.7 0.1 stack.71.refs_0_
  6.8 1.1 %collective-permute-done.1.refs_3_ = bf16[4,16,4,256]{3,2,1,0:T(4,128)(2,1)S(1)} collective-permute-done((bf16[4,16,4,256]{3,2,1,0:T(4,128)(2,1)S(1)}, bf16[4,16,4,256]{3,2,1,0:T(4,128)(2,1)S(1)}, u32[]{:S(2)}, u32[]{:S(2)}) %collective-permute-start.1) | collective-permute-done | bytes 131104 | tf_op jit(solution)/shard_map/ppermute | solution.py:452
  7.9 0.0 collective-permute-done.refs_2_
  7.9 0.8 %shard_map.69 = (bf16[144,256]{1,0:T(8,128)(2,1)S(1)}, f32[4,6,16,256]{3,2,1,0:T(8,128)S(1)}, f32[4,6,2,256]{3,2,1,0:T(2,128)S(1)}) custom-call(s32[13]{0:T(128)S(1)} %stack.71.refs_0_, f32[4,16,24,256]{3,2,1,0:T(8,128)S(1)} %shard_map.68.refs_1_, bf16[4,16,4,256]{3,2,1,0:T(4,128)(2,1)S(1)} %collective-permute-done.refs_2_, ...), custom_call_target="tpu_custom_call" | custom-call | bytes 2351156 | tf_op jit(solution)/shard_map/pallas_call | solution.py:360
  8.7 3.1 %collective-permute-start.2 = (bf16[144,256]{1,0:T(8,128)(2,1)S(1)}, bf16[144,256]{1,0:T(8,128)(2,1)S(1)}, u32[]{:S(2)}, u32[]{:S(2)}) collective-permute-start(bf16[144,256]{1,0:T(8,128)(2,1)S(1)} %get-tuple-element.42.refs_5_), channel_id=1, source_target_pairs={{0,8},{1,9},{3,11},{2,10},{6,14},{7,15},{5,13},{4,12},{8,0},{9,1},... | collective-permute-start | bytes 221192 | tf_op jit(solution)/shard_map/ppermute | solution.py:452
  11.8 1.7 %copy-done = bf16[2,3,3,256,256]{4,3,2,1,0:T(8,128)(2,1)S(1)} copy-done((bf16[2,3,3,256,256]{4,3,2,1,0:T(8,128)(2,1)S(1)}, bf16[2,3,3,256,256]{4,3,2,1,0:T(8,128)(2,1)}, u32[]{:S(2)}) %copy-start) | copy-done | bytes 2359320
  13.4 2.4 %shard_map.70 = (bf16[3,640,256]{2,1,0:T(8,128)(2,1)S(1)}, f32[2,512,256]{2,1,0:T(8,128)S(1)}) custom-call(s32[13]{0:T(128)S(1)} %stack.71.refs_0_, f32[4,16,24,256]{3,2,1,0:T(8,128)S(1)} %shard_map.68.refs_1_, bf16[4,16,4,256]{3,2,1,0:T(4,128)(2,1)S(1)} %collective-permute-done.refs_2_, bf16[4,16,4,256]{3,2,1,0:T(4,128)(2,1)S(1)} %collective-permute-done.1.refs_3_, ...), custom_call_target="tpu_custom_call" | custom-call | flops 1207959552 | bytes 6225972 | tf_op jit(solution)/shard_map/pallas_call | solution.py:360
  15.8 0.0 copy-start.5
  15.9 1.6 %shard_map.71 = (bf16[2,2,64,256]{3,2,1,0:T(8,128)(2,1)S(1)}, bf16[2,2,64,256]{3,2,1,0:T(8,128)(2,1)S(1)}, bf16[2,2,64,256]{3,2,1,0:T(8,128)(2,1)S(1)}, bf16[2,2...) custom-call(s32[13]{0:T(128)S(1)} %stack.71.refs_0_, ...), custom_call_target="tpu_custom_call", output_to_operand_aliasing={{4}: (4, {})} | custom-call | flops 301989888 | bytes 6414388 | tf_op jit(solution)/shard_map/pallas_call | solution.py:360
  17.5 1.6 %collective-permute-start.3 = (bf16[2,2,64,256]{3,2,1,0:T(8,128)(2,1)S(1)}, bf16[2,2,64,256]{3,2,1,0:T(8,128)(2,1)S(1)}, u32[]{:S(2)}, u32[]{:S(2)}) collective-permute-start(bf16[2,2,64,256]{3,2,1,0:T(8,128)(2,1)S(1)} %get-tuple-element.48), channel_id=1, source_target_pairs={{0,2},{1,3},{2,0},{3,1},{4,6},{5,7},{6,4},{7,5},{8,10},{9,11},{10,... | collective-permute-start | bytes 393224 | tf_op jit(solution)/shard_map/ppermute | solution.py:379
  19.1 1.6 %collective-permute-start.4 = (bf16[2,2,64,256]{3,2,1,0:T(8,128)(2,1)S(1)}, bf16[2,2,64,256]{3,2,1,0:T(8,128)(2,1)S(1)}, u32[]{:S(2)}, u32[]{:S(2)}) collective-permute-start(bf16[2,2,64,256]{3,2,1,0:T(8,128)(2,1)S(1)} %get-tuple-element.49), channel_id=1, source_target_pairs={{0,4},{1,5},{2,6},{3,7},{4,0},{5,1},{6,2},{7,3},{8,12},{9,13},{10,... | collective-permute-start | bytes 393224 | tf_op jit(solution)/shard_map/ppermute | solution.py:379
  20.7 0.4 collective-permute-start.5
  21.1 2.1 %shard_map.73 = (bf16[8,208,256]{2,1,0:T(8,128)(2,1)S(1)}, bf16[2,208,256]{2,1,0:T(8,128)(2,1)S(1)}, bf16[2,208,256]{2,1,0:T(8,128)(2,1)S(1)}, bf16[2,208,256]{2...) custom-call(s32[13]{0:T(128)S(1)} %stack.71.refs_0_, ...), custom_call_target="tpu_custom_call" | custom-call | flops 1207959552 | bytes 3866676 | tf_op jit(solution)/shard_map/pallas_call | solution.py:360
  23.1 0.0 copy-start.2
  23.2 0.1 collective-permute-start.7
  23.2 0.5 collective-permute-start.8
  23.7 0.0 collective-permute-done.3.refs_1_.refs_2_
  23.7 0.1 collective-permute-start.9
  23.8 0.5 collective-permute-done.4.refs_2_.refs_3_
  24.4 0.0 collective-permute-start.10
  24.4 2.2 %collective-permute-done.5.refs_3_.refs_4_ = bf16[2,2,64,256]{3,2,1,0:T(8,128)(2,1)S(1)} collective-permute-done((bf16[2,2,64,256]{3,2,1,0:T(8,128)(2,1)S(1)}, bf16[2,2,64,256]{3,2,1,0:T(8,128)(2,1)S(1)}, u32[]{:S(2)}, u32[]{:S(2)}) %collective-permute-start.5) | collective-permute-done | bytes 131104 | tf_op jit(solution)/shard_map/ppermute | solution.py:379
  26.5 0.1 collective-permute-start.6
  26.6 0.0 collective-permute-done.8.refs_3_
  26.7 0.7 %shard_map.74 = (f32[4,208,256]{2,1,0:T(8,128)S(1)}, bf16[4,208,256]{2,1,0:T(8,128)(2,1)S(1)}) custom-call(s32[13]{0:T(128)S(1)} %stack.71.refs_0_, bf16[8,208,256]{2,1,0:T(8,128)(2,1)S(1)} %get-tuple-element.53.refs_1_, bf16[2,208,256]{2,1,0:T(8,128)(2,1)S(1)} %collective-permute-done.7.refs_2_, bf16[2,208,256]{2,1,0:T(8,128)(2,1)S(1)} %collective-permute-done.8.refs_3_, ...), custom_call_target="tpu_custom_call" | custom-call | bytes 2981940 | tf_op jit(solution)/shard_map/pallas_call | solution.py:360
  27.4 0.8 %collective-permute-start.11 = (bf16[4,208,256]{2,1,0:T(8,128)(2,1)S(1)}, bf16[4,208,256]{2,1,0:T(8,128)(2,1)S(1)}, u32[]{:S(2)}, u32[]{:S(2)}) collective-permute-start(bf16[4,208,256]{2,1,0:T(8,128)(2,1)S(1)} %get-tuple-element.60), channel_id=1, source_target_pairs={{0,4},{1,5},{2,6},{3,7},{4,0},{5,1},{6,2},{7,3},{8,12},{9,13},{10,... | collective-permute-start | bytes 1277960 | tf_op jit(solution)/shard_map/ppermute | solution.py:379
  28.2 1.5 %shard_map.75 = (bf16[8,208,256]{2,1,0:T(8,128)(2,1)S(1)}, bf16[2,208,256]{2,1,0:T(8,128)(2,1)S(1)}, bf16[2,208,256]{2,1,0:T(8,128)(2,1)S(1)}, bf16[2,208,256]{2...) custom-call(s32[13]{0:T(128)S(1)} %stack.71.refs_0_, ...), custom_call_target="tpu_custom_call" | custom-call | flops 536870912 | bytes 5767220 | tf_op jit(solution)/shard_map/pallas_call | solution.py:360
  29.7 0.3 collective-permute-start.12
  30.0 0.3 collective-permute-start.13
  30.3 0.2 collective-permute-start.14
  30.5 0.3 collective-permute-start.15
  30.8 0.4 collective-permute-done.12.refs_2_
  31.2 0.3 collective-permute-done.13.refs_3_
  31.5 0.3 collective-permute-done.14.refs_4_
  31.8 0.3 collective-permute-done.15.refs_5_
  32.1 0.7 %shard_map.76 = (f32[4,208,128]{2,1,0:T(8,128)S(1)}, bf16[4,208,128]{2,1,0:T(8,128)(2,1)S(1)}, bf16[4,208,128]{2,1,0:T(8,128)(2,1)S(1)}, bf16[4,208,128]{2,1,0:T(8,128)(2,1)S(1)}) custom-call(s32[13]{0:T(128)S(1)} %stack.71.refs_0_, bf16[8,208,256]{2,1,0:T(8,128)(2,1)S(1)} %get-tuple-element.61.refs_1_, ...), custom_call_target="tpu_custom_call" | custom-call | bytes 2768948 | tf_op jit(solution)/shard_map/pallas_call | solution.py:360
  32.9 1.6 %collective-permute-start.17 = (bf16[4,208,128]{2,1,0:T(8,128)(2,1)S(1)}, bf16[4,208,128]{2,1,0:T(8,128)(2,1)S(1)}, u32[]{:S(2)}, u32[]{:S(2)}) collective-permute-start(bf16[4,208,128]{2,1,0:T(8,128)(2,1)S(1)} %get-tuple-element.69), channel_id=1, source_target_pairs={{0,2},{1,3},{2,0},{3,1},{4,6},{5,7},{6,4},{7,5},{8,10},{9,11},{10,... | collective-permute-start | bytes 638984 | tf_op jit(solution)/shard_map/ppermute | solution.py:379
  34.5 1.5 %collective-permute-start.18 = (bf16[4,208,128]{2,1,0:T(8,128)(2,1)S(1)}, bf16[4,208,128]{2,1,0:T(8,128)(2,1)S(1)}, u32[]{:S(2)}, u32[]{:S(2)}) collective-permute-start(bf16[4,208,128]{2,1,0:T(8,128)(2,1)S(1)} %get-tuple-element.70), channel_id=1, source_target_pairs={{0,16},{16,0},{1,17},{17,1},{2,18},{18,2},{3,19},{19,3},{4,20},{20... | collective-permute-start | bytes 638984 | tf_op jit(solution)/shard_map/ppermute | solution.py:381
  36.0 0.5 collective-permute-start.19
  36.4 3.2 %collective-permute-done.11.refs_2_ = bf16[4,208,256]{2,1,0:T(8,128)(2,1)S(1)} collective-permute-done((bf16[4,208,256]{2,1,0:T(8,128)(2,1)S(1)}, bf16[4,208,256]{2,1,0:T(8,128)(2,1)S(1)}, u32[]{:S(2)}, u32[]{:S(2)}) %collective-permute-start.11) | collective-permute-done | bytes 426016 | tf_op jit(solution)/shard_map/ppermute | solution.py:379
  39.7 0.6 shard_map.77
  40.3 1.9 %collective-permute-start.16 = (bf16[2,208,256]{2,1,0:T(8,128)(2,1)S(1)}, bf16[2,208,256]{2,1,0:T(8,128)(2,1)S(1)}, u32[]{:S(2)}, u32[]{:S(2)}) collective-permute-start(bf16[2,208,256]{2,1,0:T(8,128)(2,1)S(1)} %get-tuple-element.68), channel_id=1, source_target_pairs={{0,8},{1,9},{2,10},{3,11},{4,12},{5,13},{6,14},{7,15},{8,0},{9,1},... | collective-permute-start | bytes 638984 | tf_op jit(solution)/shard_map/ppermute | solution.py:379
  42.2 0.4 collective-permute-done.18.refs_3_
  42.6 3.4 %collective-permute-done.19.refs_4_ = bf16[4,208,128]{2,1,0:T(8,128)(2,1)S(1)} collective-permute-done((bf16[4,208,128]{2,1,0:T(8,128)(2,1)S(1)}, bf16[4,208,128]{2,1,0:T(8,128)(2,1)S(1)}, u32[]{:S(2)}, u32[]{:S(2)}) %collective-permute-start.19) | collective-permute-done | bytes 213024 | tf_op jit(solution)/shard_map/ppermute | solution.py:383
  46.1 0.6 shard_map.78
  46.7 1.3 %collective-permute-start.23 = (bf16[1,208,128]{2,1,0:T(8,128)(2,1)S(1)}, bf16[1,208,128]{2,1,0:T(8,128)(2,1)S(1)}, u32[]{:S(2)}, u32[]{:S(2)}) collective-permute-start(bf16[1,208,128]{2,1,0:T(8,128)(2,1)S(1)} %get-tuple-element.77), channel_id=1, source_target_pairs={{0,4},{1,5},{2,6},{3,7},{4,0},{5,1},{6,2},{7,3},{8,12},{9,13},{10,... | collective-permute-start | bytes 159752 | tf_op jit(solution)/shard_map/ppermute | solution.py:379
  48.1 1.8 %collective-permute-start.24 = (bf16[1,208,128]{2,1,0:T(8,128)(2,1)S(1)}, bf16[1,208,128]{2,1,0:T(8,128)(2,1)S(1)}, u32[]{:S(2)}, u32[]{:S(2)}) collective-permute-start(bf16[1,208,128]{2,1,0:T(8,128)(2,1)S(1)} %get-tuple-element.78), channel_id=1, source_target_pairs={{0,8},{1,9},{2,10},{3,11},{4,12},{5,13},{6,14},{7,15},{8,0},{9,1},... | collective-permute-start | bytes 159752 | tf_op jit(solution)/shard_map/ppermute | solution.py:379
  49.9 1.3 %collective-permute-start.25 = (bf16[1,208,128]{2,1,0:T(8,128)(2,1)S(1)}, bf16[1,208,128]{2,1,0:T(8,128)(2,1)S(1)}, u32[]{:S(2)}, u32[]{:S(2)}) collective-permute-start(bf16[1,208,128]{2,1,0:T(8,128)(2,1)S(1)} %get-tuple-element.79), channel_id=1, source_target_pairs={{0,12},{1,13},{2,14},{3,15},{4,8},{5,9},{6,10},{7,11},{8,4},{9,5},... | collective-permute-start | bytes 159752 | tf_op jit(solution)/shard_map/ppermute | solution.py:379
  51.2 3.6 %collective-permute-done.16.refs_2_ = bf16[2,208,256]{2,1,0:T(8,128)(2,1)S(1)} collective-permute-done((bf16[2,208,256]{2,1,0:T(8,128)(2,1)S(1)}, bf16[2,208,256]{2,1,0:T(8,128)(2,1)S(1)}, u32[]{:S(2)}, u32[]{:S(2)}) %collective-permute-start.16) | collective-permute-done | bytes 213024 | tf_op jit(solution)/shard_map/ppermute | solution.py:379
  54.8 0.6 shard_map.79
  55.4 2.2 %collective-permute-start.22 = (bf16[1,80,256]{2,1,0:T(8,128)(2,1)S(1)}, bf16[1,80,256]{2,1,0:T(8,128)(2,1)S(1)}, u32[]{:S(2)}, u32[]{:S(2)}) collective-permute-start(bf16[1,80,256]{2,1,0:T(8,128)(2,1)S(1)} %get-tuple-element.76), channel_id=1, source_target_pairs={{0,2},{1,3},{2,0},{3,1},{4,6},{5,7},{6,4},{7,5},{8,10},{9,11},{10,... | collective-permute-start | bytes 122888 | tf_op jit(solution)/shard_map/ppermute | solution.py:379
  57.5 0.1 collective-permute-start.20
  57.6 1.9 %collective-permute-start.21 = (bf16[1,64,256]{2,1,0:T(8,128)(2,1)S(1)}, bf16[1,64,256]{2,1,0:T(8,128)(2,1)S(1)}, u32[]{:S(2)}, u32[]{:S(2)}) collective-permute-start(bf16[1,64,256]{2,1,0:T(8,128)(2,1)S(1)} %get-tuple-element.75), channel_id=1, source_target_pairs={{0,2},{1,3},{2,0},{3,1},{4,6},{5,7},{6,4},{7,5},{8,10},{9,11},{10,... | collective-permute-start | bytes 98312 | tf_op jit(solution)/shard_map/ppermute | solution.py:379
  59.6 1.9 %collective-permute-done.20.refs_2_ = bf16[1,64,256]{2,1,0:T(8,128)(2,1)S(1)} collective-permute-done((bf16[1,64,256]{2,1,0:T(8,128)(2,1)S(1)}, bf16[1,64,256]{2,1,0:T(8,128)(2,1)S(1)}, u32[]{:S(2)}, u32[]{:S(2)}) %collective-permute-start.20) | collective-permute-done | bytes 32800 | tf_op jit(solution)/shard_map/ppermute | solution.py:379
  61.5 0.4 collective-permute-done.21.refs_3_
  61.8 0.6 shard_map.81
  62.4 1.6 %collective-permute-start.26 = (bf16[208,256]{1,0:T(8,128)(2,1)S(1)}, bf16[208,256]{1,0:T(8,128)(2,1)S(1)}, u32[]{:S(2)}, u32[]{:S(2)}) collective-permute-start(bf16[208,256]{1,0:T(8,128)(2,1)S(1)} %get-tuple-element.81), channel_id=1, source_target_pairs={{0,16},{16,0},{1,17},{17,1},{2,18},{18,2},{3,19},{19,3},{4,20},{20... | collective-permute-start | bytes 319496 | tf_op jit(solution)/shard_map/ppermute | solution.py:381
  64.0 2.1 %shard_map.80 = bf16[4,2,128,1024]{3,2,1,0:T(8,128)(2,1)} custom-call(bf16[2,512,256]{2,1,0:T(8,128)(2,1)S(1)} %get-tuple-element.59.refs_6_.refs_0_, bf16[2,1024,256]{2,1,0:T(8,128)(2,1)S(1)} %copy-done.4, f32[1,208,256]{2,1,0:T(8,128)S(1)} %get-tuple-element.73.refs_2_.refs_1_), custom_call_target="tpu_custom_call" | custom-call | flops 536870912 | bytes 3670016 | tf_op jit(solution)/shard_map/pallas_call | solution.py:360
  66.1 1.1 %collective-permute-done.26.refs_2_ = bf16[208,256]{1,0:T(8,128)(2,1)S(1)} collective-permute-done((bf16[208,256]{1,0:T(8,128)(2,1)S(1)}, bf16[208,256]{1,0:T(8,128)(2,1)S(1)}, u32[]{:S(2)}, u32[]{:S(2)}) %collective-permute-start.26) | collective-permute-done | bytes 106528 | tf_op jit(solution)/shard_map/ppermute | solution.py:381
  67.2 1.3 %shard_map.82 = f32[208,256]{1,0:T(8,128)} custom-call(s32[13]{0:T(128)S(1)} %stack.71.refs_0_, f32[208,256]{1,0:T(8,128)S(1)} %get-tuple-element.80.refs_1_, bf16[208,256]{1,0:T(8,128)(2,1)S(1)} %collective-permute-done.26.refs_2_), custom_call_target="tpu_custom_call" | custom-call | bytes 532532 | tf_op jit(solution)/shard_map/pallas_call | solution.py:360
  (19 shorter events, 0.1 us)
Async XLA Ops:
  1.9 6.0 %collective-permute-start.1 = (bf16[4,16,4,256]{3,2,1,0:T(4,128)(2,1)S(1)}, bf16[4,16,4,256]{3,2,1,0:T(4,128)(2,1)S(1)}, u32[]{:S(2)}, u32[]{:S(2)}) collective-permute-start(bf16[4,16,4,256]{3,2,1,0:T(4,128)(2,1)S(1)} %get-tuple-element.82), channel_id=1, source_target_pairs={{1,3},{3,1},{2,6},{6,2},{7,5},{5,7},{0,4},{4,0},{9,11},{11,9},{10,... | collective-permute-start | bytes 393224 | tf_op jit(solution)/shard_map/ppermute | solution.py:452
  4.9 3.0 %collective-permute-start = (bf16[4,16,4,256]{3,2,1,0:T(4,128)(2,1)S(1)}, bf16[4,16,4,256]{3,2,1,0:T(4,128)(2,1)S(1)}, u32[]{:S(2)}, u32[]{:S(2)}) collective-permute-start(bf16[4,16,4,256]{3,2,1,0:T(4,128)(2,1)S(1)} %get-tuple-element.83), channel_id=1, source_target_pairs={{0,1},{1,0},{3,2},{2,3},{6,7},{7,6},{5,4},{4,5},{8,9},{9,8},{11,10... | collective-permute-start | bytes 393224 | tf_op jit(solution)/shard_map/ppermute | solution.py:452
  4.9 1.2 %copy-start.3 = (bf16[4,16,32,256]{3,2,1,0:T(8,128)(2,1)S(1)}, bf16[4,16,32,256]{3,2,1,0:T(8,128)(2,1)}, u32[]{:S(2)}) copy-start(bf16[4,16,32,256]{3,2,1,0:T(8,128)(2,1)} %refs_0_.1) | copy-start | bytes 3145732
  8.7 7.2 %collective-permute-start.2 = (bf16[144,256]{1,0:T(8,128)(2,1)S(1)}, bf16[144,256]{1,0:T(8,128)(2,1)S(1)}, u32[]{:S(2)}, u32[]{:S(2)}) collective-permute-start(bf16[144,256]{1,0:T(8,128)(2,1)S(1)} %get-tuple-element.42.refs_5_), channel_id=1, source_target_pairs={{0,8},{1,9},{3,11},{2,10},{6,14},{7,15},{5,13},{4,12},{8,0},{9,1},... | collective-permute-start | bytes 221192 | tf_op jit(solution)/shard_map/ppermute | solution.py:452
  11.8 1.7 %copy-start = (bf16[2,3,3,256,256]{4,3,2,1,0:T(8,128)(2,1)S(1)}, bf16[2,3,3,256,256]{4,3,2,1,0:T(8,128)(2,1)}, u32[]{:S(2)}) copy-start(bf16[2,3,3,256,256]{4,3,2,1,0:T(8,128)(2,1)} %refs_6_.2) | copy-start | bytes 7077892
  13.4 2.4 %copy-start.1 = (bf16[2,3,3,256,256]{4,3,2,1,0:T(8,128)(2,1)S(1)}, bf16[2,3,3,256,256]{4,3,2,1,0:T(8,128)(2,1)}, u32[]{:S(2)}) copy-start(bf16[2,3,3,256,256]{4,3,2,1,0:T(8,128)(2,1)} %refs_6_.2) | copy-start | bytes 7077892
  15.8 5.2 %copy-start.5 = (bf16[4,2,8,16,256]{4,3,2,1,0:T(8,128)(2,1)S(1)}, bf16[4,2,8,16,256]{4,3,2,1,0:T(8,128)(2,1)}, u32[]{:S(2)}) copy-start(bf16[4,2,8,16,256]{4,3,2,1,0:T(8,128)(2,1)} %refs_2_.1) | copy-start | bytes 1572868
  17.5 6.2 %collective-permute-start.3 = (bf16[2,2,64,256]{3,2,1,0:T(8,128)(2,1)S(1)}, bf16[2,2,64,256]{3,2,1,0:T(8,128)(2,1)S(1)}, u32[]{:S(2)}, u32[]{:S(2)}) collective-permute-start(bf16[2,2,64,256]{3,2,1,0:T(8,128)(2,1)S(1)} %get-tuple-element.48), channel_id=1, source_target_pairs={{0,2},{1,3},{2,0},{3,1},{4,6},{5,7},{6,4},{7,5},{8,10},{9,11},{10,... | collective-permute-start | bytes 393224 | tf_op jit(solution)/shard_map/ppermute | solution.py:379
  19.1 5.3 %collective-permute-start.4 = (bf16[2,2,64,256]{3,2,1,0:T(8,128)(2,1)S(1)}, bf16[2,2,64,256]{3,2,1,0:T(8,128)(2,1)S(1)}, u32[]{:S(2)}, u32[]{:S(2)}) collective-permute-start(bf16[2,2,64,256]{3,2,1,0:T(8,128)(2,1)S(1)} %get-tuple-element.49), channel_id=1, source_target_pairs={{0,4},{1,5},{2,6},{3,7},{4,0},{5,1},{6,2},{7,3},{8,12},{9,13},{10,... | collective-permute-start | bytes 393224 | tf_op jit(solution)/shard_map/ppermute | solution.py:379
  20.7 5.9 %collective-permute-start.5 = (bf16[2,2,64,256]{3,2,1,0:T(8,128)(2,1)S(1)}, bf16[2,2,64,256]{3,2,1,0:T(8,128)(2,1)S(1)}, u32[]{:S(2)}, u32[]{:S(2)}) collective-permute-start(bf16[2,2,64,256]{3,2,1,0:T(8,128)(2,1)S(1)} %get-tuple-element.50), channel_id=1, source_target_pairs={{0,6},{1,7},{2,4},{3,5},{4,2},{5,3},{6,0},{7,1},{8,14},{9,15},{10,... | collective-permute-start | bytes 393224 | tf_op jit(solution)/shard_map/ppermute | solution.py:379
  23.1 5.1 %copy-start.2 = (bf16[4,2,128,1024]{3,2,1,0:T(8,128)(2,1)S(1)}, bf16[4,2,128,1024]{3,2,1,0:T(8,128)(2,1)}, u32[]{:S(2)}) copy-start(bf16[4,2,128,1024]{3,2,1,0:T(8,128)(2,1)} %refs_6_.3) | copy-start | bytes 6291460
  23.2 3.5 %collective-permute-start.7 = (bf16[2,208,256]{2,1,0:T(8,128)(2,1)S(1)}, bf16[2,208,256]{2,1,0:T(8,128)(2,1)S(1)}, u32[]{:S(2)}, u32[]{:S(2)}) collective-permute-start(bf16[2,208,256]{2,1,0:T(8,128)(2,1)S(1)} %get-tuple-element.54), channel_id=1, source_target_pairs={{0,1},{1,0},{2,3},{3,2},{4,5},{5,4},{6,7},{7,6},{8,9},{9,8},{10,11... | collective-permute-start | bytes 638984 | tf_op jit(solution)/shard_map/ppermute | solution.py:379
  23.2 3.4 %collective-permute-start.8 = (bf16[2,208,256]{2,1,0:T(8,128)(2,1)S(1)}, bf16[2,208,256]{2,1,0:T(8,128)(2,1)S(1)}, u32[]{:S(2)}, u32[]{:S(2)}) collective-permute-start(bf16[2,208,256]{2,1,0:T(8,128)(2,1)S(1)} %get-tuple-element.55), channel_id=1, source_target_pairs={{0,1},{1,0},{2,3},{3,2},{4,5},{5,4},{6,7},{7,6},{8,9},{9,8},{10,11... | collective-permute-start | bytes 638984 | tf_op jit(solution)/shard_map/ppermute | solution.py:379
  23.7 2.9 %collective-permute-start.9 = (bf16[2,208,256]{2,1,0:T(8,128)(2,1)S(1)}, bf16[2,208,256]{2,1,0:T(8,128)(2,1)S(1)}, u32[]{:S(2)}, u32[]{:S(2)}) collective-permute-start(bf16[2,208,256]{2,1,0:T(8,128)(2,1)S(1)} %get-tuple-element.56), channel_id=1, source_target_pairs={{0,1},{1,0},{2,3},{3,2},{4,5},{5,4},{6,7},{7,6},{8,9},{9,8},{10,11... | collective-permute-start | bytes 638984 | tf_op jit(solution)/shard_map/ppermute | solution.py:379
  24.4 2.3 %collective-permute-start.10 = (bf16[2,208,256]{2,1,0:T(8,128)(2,1)S(1)}, bf16[2,208,256]{2,1,0:T(8,128)(2,1)S(1)}, u32[]{:S(2)}, u32[]{:S(2)}) collective-permute-start(bf16[2,208,256]{2,1,0:T(8,128)(2,1)S(1)} %get-tuple-element.57), channel_id=1, source_target_pairs={{0,1},{1,0},{2,3},{3,2},{4,5},{5,4},{6,7},{7,6},{8,9},{9,8},{10,11... | collective-permute-start | bytes 638984 | tf_op jit(solution)/shard_map/ppermute | solution.py:379
  26.5 1.7 %collective-permute-start.6 = (bf16[4,2,64,256]{3,2,1,0:T(8,128)(2,1)S(1)}, bf16[4,2,64,256]{3,2,1,0:T(8,128)(2,1)S(1)}, u32[]{:S(2)}, u32[]{:S(2)}) collective-permute-start(bf16[4,2,64,256]{3,2,1,0:T(8,128)(2,1)S(1)} %shard_map.72), channel_id=1, source_target_pairs={{0,1},{1,0},{2,3},{3,2},{4,5},{5,4},{6,7},{7,6},{8,9},{9,8},{10,11... | collective-permute-start | bytes 786440 | tf_op jit(solution)/shard_map/ppermute | solution.py:379
  27.4 12.3 %collective-permute-start.11 = (bf16[4,208,256]{2,1,0:T(8,128)(2,1)S(1)}, bf16[4,208,256]{2,1,0:T(8,128)(2,1)S(1)}, u32[]{:S(2)}, u32[]{:S(2)}) collective-permute-start(bf16[4,208,256]{2,1,0:T(8,128)(2,1)S(1)} %get-tuple-element.60), channel_id=1, source_target_pairs={{0,4},{1,5},{2,6},{3,7},{4,0},{5,1},{6,2},{7,3},{8,12},{9,13},{10,... | collective-permute-start | bytes 1277960 | tf_op jit(solution)/shard_map/ppermute | solution.py:379
  29.7 1.5 %collective-permute-start.12 = (bf16[2,208,256]{2,1,0:T(8,128)(2,1)S(1)}, bf16[2,208,256]{2,1,0:T(8,128)(2,1)S(1)}, u32[]{:S(2)}, u32[]{:S(2)}) collective-permute-start(bf16[2,208,256]{2,1,0:T(8,128)(2,1)S(1)} %get-tuple-element.62), channel_id=1, source_target_pairs={{0,1},{1,0},{2,3},{3,2},{4,5},{5,4},{6,7},{7,6},{8,9},{9,8},{10,11... | collective-permute-start | bytes 638984 | tf_op jit(solution)/shard_map/ppermute | solution.py:379
  30.0 1.6 %collective-permute-start.13 = (bf16[2,208,256]{2,1,0:T(8,128)(2,1)S(1)}, bf16[2,208,256]{2,1,0:T(8,128)(2,1)S(1)}, u32[]{:S(2)}, u32[]{:S(2)}) collective-permute-start(bf16[2,208,256]{2,1,0:T(8,128)(2,1)S(1)} %get-tuple-element.63), channel_id=1, source_target_pairs={{0,1},{1,0},{2,3},{3,2},{4,5},{5,4},{6,7},{7,6},{8,9},{9,8},{10,11... | collective-permute-start | bytes 638984 | tf_op jit(solution)/shard_map/ppermute | solution.py:379
  30.3 1.6 %collective-permute-start.14 = (bf16[2,208,256]{2,1,0:T(8,128)(2,1)S(1)}, bf16[2,208,256]{2,1,0:T(8,128)(2,1)S(1)}, u32[]{:S(2)}, u32[]{:S(2)}) collective-permute-start(bf16[2,208,256]{2,1,0:T(8,128)(2,1)S(1)} %get-tuple-element.64), channel_id=1, source_target_pairs={{0,1},{1,0},{2,3},{3,2},{4,5},{5,4},{6,7},{7,6},{8,9},{9,8},{10,11... | collective-permute-start | bytes 638984 | tf_op jit(solution)/shard_map/ppermute | solution.py:379
  30.5 1.7 %collective-permute-start.15 = (bf16[2,208,256]{2,1,0:T(8,128)(2,1)S(1)}, bf16[2,208,256]{2,1,0:T(8,128)(2,1)S(1)}, u32[]{:S(2)}, u32[]{:S(2)}) collective-permute-start(bf16[2,208,256]{2,1,0:T(8,128)(2,1)S(1)} %get-tuple-element.65), channel_id=1, source_target_pairs={{0,1},{1,0},{2,3},{3,2},{4,5},{5,4},{6,7},{7,6},{8,9},{9,8},{10,11... | collective-permute-start | bytes 638984 | tf_op jit(solution)/shard_map/ppermute | solution.py:379
  32.9 9.3 %collective-permute-start.17 = (bf16[4,208,128]{2,1,0:T(8,128)(2,1)S(1)}, bf16[4,208,128]{2,1,0:T(8,128)(2,1)S(1)}, u32[]{:S(2)}, u32[]{:S(2)}) collective-permute-start(bf16[4,208,128]{2,1,0:T(8,128)(2,1)S(1)} %get-tuple-element.69), channel_id=1, source_target_pairs={{0,2},{1,3},{2,0},{3,1},{4,6},{5,7},{6,4},{7,5},{8,10},{9,11},{10,... | collective-permute-start | bytes 638984 | tf_op jit(solution)/shard_map/ppermute | solution.py:379
  34.5 8.1 %collective-permute-start.18 = (bf16[4,208,128]{2,1,0:T(8,128)(2,1)S(1)}, bf16[4,208,128]{2,1,0:T(8,128)(2,1)S(1)}, u32[]{:S(2)}, u32[]{:S(2)}) collective-permute-start(bf16[4,208,128]{2,1,0:T(8,128)(2,1)S(1)} %get-tuple-element.70), channel_id=1, source_target_pairs={{0,16},{16,0},{1,17},{17,1},{2,18},{18,2},{3,19},{19,3},{4,20},{20... | collective-permute-start | bytes 638984 | tf_op jit(solution)/shard_map/ppermute | solution.py:381
  36.0 10.1 %collective-permute-start.19 = (bf16[4,208,128]{2,1,0:T(8,128)(2,1)S(1)}, bf16[4,208,128]{2,1,0:T(8,128)(2,1)S(1)}, u32[]{:S(2)}, u32[]{:S(2)}) collective-permute-start(bf16[4,208,128]{2,1,0:T(8,128)(2,1)S(1)} %get-tuple-element.71), channel_id=1, source_target_pairs={{0,18},{1,19},{2,16},{3,17},{4,22},{5,23},{6,20},{7,21},{8,26},{9,... | collective-permute-start | bytes 638984 | tf_op jit(solution)/shard_map/ppermute | solution.py:383
  39.7 24.3 %copy-start.4 = (bf16[2,1024,256]{2,1,0:T(8,128)(2,1)S(1)}, bf16[2,1024,256]{2,1,0:T(8,128)(2,1)}, u32[]{:S(2)}) copy-start(bf16[2,1024,256]{2,1,0:T(8,128)(2,1)} %refs_1_.1) | copy-start | bytes 3145732
  40.3 14.5 %collective-permute-start.16 = (bf16[2,208,256]{2,1,0:T(8,128)(2,1)S(1)}, bf16[2,208,256]{2,1,0:T(8,128)(2,1)S(1)}, u32[]{:S(2)}, u32[]{:S(2)}) collective-permute-start(bf16[2,208,256]{2,1,0:T(8,128)(2,1)S(1)} %get-tuple-element.68), channel_id=1, source_target_pairs={{0,8},{1,9},{2,10},{3,11},{4,12},{5,13},{6,14},{7,15},{8,0},{9,1},... | collective-permute-start | bytes 638984 | tf_op jit(solution)/shard_map/ppermute | solution.py:379
  46.7 10.9 %collective-permute-start.23 = (bf16[1,208,128]{2,1,0:T(8,128)(2,1)S(1)}, bf16[1,208,128]{2,1,0:T(8,128)(2,1)S(1)}, u32[]{:S(2)}, u32[]{:S(2)}) collective-permute-start(bf16[1,208,128]{2,1,0:T(8,128)(2,1)S(1)} %get-tuple-element.77), channel_id=1, source_target_pairs={{0,4},{1,5},{2,6},{3,7},{4,0},{5,1},{6,2},{7,3},{8,12},{9,13},{10,... | collective-permute-start | bytes 159752 | tf_op jit(solution)/shard_map/ppermute | solution.py:379
  48.1 11.5 %collective-permute-start.24 = (bf16[1,208,128]{2,1,0:T(8,128)(2,1)S(1)}, bf16[1,208,128]{2,1,0:T(8,128)(2,1)S(1)}, u32[]{:S(2)}, u32[]{:S(2)}) collective-permute-start(bf16[1,208,128]{2,1,0:T(8,128)(2,1)S(1)} %get-tuple-element.78), channel_id=1, source_target_pairs={{0,8},{1,9},{2,10},{3,11},{4,12},{5,13},{6,14},{7,15},{8,0},{9,1},... | collective-permute-start | bytes 159752 | tf_op jit(solution)/shard_map/ppermute | solution.py:379
  49.9 9.7 %collective-permute-start.25 = (bf16[1,208,128]{2,1,0:T(8,128)(2,1)S(1)}, bf16[1,208,128]{2,1,0:T(8,128)(2,1)S(1)}, u32[]{:S(2)}, u32[]{:S(2)}) collective-permute-start(bf16[1,208,128]{2,1,0:T(8,128)(2,1)S(1)} %get-tuple-element.79), channel_id=1, source_target_pairs={{0,12},{1,13},{2,14},{3,15},{4,8},{5,9},{6,10},{7,11},{8,4},{9,5},... | collective-permute-start | bytes 159752 | tf_op jit(solution)/shard_map/ppermute | solution.py:379
  55.4 6.5 %collective-permute-start.22 = (bf16[1,80,256]{2,1,0:T(8,128)(2,1)S(1)}, bf16[1,80,256]{2,1,0:T(8,128)(2,1)S(1)}, u32[]{:S(2)}, u32[]{:S(2)}) collective-permute-start(bf16[1,80,256]{2,1,0:T(8,128)(2,1)S(1)} %get-tuple-element.76), channel_id=1, source_target_pairs={{0,2},{1,3},{2,0},{3,1},{4,6},{5,7},{6,4},{7,5},{8,10},{9,11},{10,... | collective-permute-start | bytes 122888 | tf_op jit(solution)/shard_map/ppermute | solution.py:379
  57.5 3.9 %collective-permute-start.20 = (bf16[1,64,256]{2,1,0:T(8,128)(2,1)S(1)}, bf16[1,64,256]{2,1,0:T(8,128)(2,1)S(1)}, u32[]{:S(2)}, u32[]{:S(2)}) collective-permute-start(bf16[1,64,256]{2,1,0:T(8,128)(2,1)S(1)} %get-tuple-element.74), channel_id=1, source_target_pairs={{0,2},{1,3},{2,0},{3,1},{4,6},{5,7},{6,4},{7,5},{8,10},{9,11},{10,... | collective-permute-start | bytes 98312 | tf_op jit(solution)/shard_map/ppermute | solution.py:379
  57.6 4.2 %collective-permute-start.21 = (bf16[1,64,256]{2,1,0:T(8,128)(2,1)S(1)}, bf16[1,64,256]{2,1,0:T(8,128)(2,1)S(1)}, u32[]{:S(2)}, u32[]{:S(2)}) collective-permute-start(bf16[1,64,256]{2,1,0:T(8,128)(2,1)S(1)} %get-tuple-element.75), channel_id=1, source_target_pairs={{0,2},{1,3},{2,0},{3,1},{4,6},{5,7},{6,4},{7,5},{8,10},{9,11},{10,... | collective-permute-start | bytes 98312 | tf_op jit(solution)/shard_map/ppermute | solution.py:379
  62.4 4.8 %collective-permute-start.26 = (bf16[208,256]{1,0:T(8,128)(2,1)S(1)}, bf16[208,256]{1,0:T(8,128)(2,1)S(1)}, u32[]{:S(2)}, u32[]{:S(2)}) collective-permute-start(bf16[208,256]{1,0:T(8,128)(2,1)S(1)} %get-tuple-element.81), channel_id=1, source_target_pairs={{0,16},{16,0},{1,17},{17,1},{2,18},{18,2},{3,19},{19,3},{4,20},{20... | collective-permute-start | bytes 319496 | tf_op jit(solution)/shard_map/ppermute | solution.py:381

commit v8 on v7

--- a/solution.py
+++ b/solution.py
@@ -222,7 +222,7 @@
     count, rows = kept.shape[:2]
     size = sent[0].shape[0]
     for j in range(count):
-        p = j >> 1 | (j & 1) * (count >> 1) if turned else j
+        p = (j & ~3 | (j & 1) << 1 | j >> 1 & 1) if turned else j
         kept[p] = full[pl.ds(pl.multiple_of((2 * j + core) * rows, 16), rows), :]
         sent[p // size][p % size] = full[pl.ds(pl.multiple_of((2 * j + 1 - core) * rows, 16), rows), :]
 
@@ -333,17 +333,16 @@
             total = total + (jnp.concatenate(rows, axis=0) if size > 1 else rows[0])
             del ins[:size]
         sums.append(total)
-    wide = jnp.concatenate([sums[1], sums[1]], axis=1)
-    sent[...] = jnp.where(first, sums[0], wide).astype(BF16)
-    kept[...] = jnp.where(first, wide, sums[0])
+    sent[...] = jnp.where(first, sums[0], sums[1]).astype(BF16)
+    kept[...] = jnp.where(first, sums[1], sums[0])
 
 
 def join_kernel(scale, flags, kept, came, out):
-    half = kept.shape[1] // 2
-    first = flags[DP] == 0
-    mine, other = kept[...], came[...].astype(F32)
-    beside = jnp.concatenate([mine[:, :half], other[:, :half]], axis=1)
-    out[...] = jnp.where(first, beside, mine + other) * scale
+    width = kept.shape[1]
+    at = pl.multiple_of(flags[DP] * width, width)
+    out[:, pl.ds(at, width)] = kept[...] * scale
+    at = pl.multiple_of((1 - flags[DP]) * width, width)
+    out[:, pl.ds(at, width)] = came[...].astype(F32) * scale
 
 
 def vmem_call(kernel, out_shape, operands, scratch=(), scalars=1, flops=0, limit=16, after=(), aliases=()):
@@ -389,7 +388,7 @@
         rows, channels = dealt[0].shape[0] // tiles, dealt[0].shape[1]
         pairs = dealt[0].reshape(tiles // 2, 2, rows, channels)
         if turned:
-            pairs = pairs.reshape(tiles // 4, 2, 2, rows, channels).swapaxes(0, 1).reshape(pairs.shape)
+            pairs = pairs.reshape(tiles // 8, 2, 2, 2, rows, channels).swapaxes(1, 2).reshape(pairs.shape)
         kept = lax.dynamic_index_in_dim(pairs, core, 1, keepdims=False)
         sent = lax.dynamic_index_in_dim(pairs, 1 - core, 1, keepdims=False)
         size = sent.shape[0] // pieces
@@ -512,7 +511,7 @@
         scratch=(full, pltpu.VMEM((patches, channels), BF16)),
         flops=conv_flops,
     )
-    (early_parts,), before = deal_rounds([(core_sum(early, position % 2, pieces, True), 2, 1, False, 1)], flags)
+    (early_parts,), before = deal_rounds([(core_sum(early, position % 2, pieces, True), 1, 0, True, 1)], flags)
     proj_flops = 2 * images * tokens * depths * dim * channels
     *terms, token_grad = vmem_call(
         proj_term_kernel,
@@ -525,18 +524,16 @@
     (late_parts,), before = deal_rounds(
         [(core_sum(terms, position % 2, pieces, False), 1, 1, True, 1)], flags, after=(token_grad,)
     )
-    at, early_bits = 2, list(range(3, bits)) + [1]
+    at, early_bits = 2, [2, 1] + list(range(3, bits))
     while at < bits:
         step = min(2, bits - at)
-        if len(early_bits) > 1:
-            (early_parts,), before = deal_rounds([(early_parts, early_bits.pop(0), 1, False, 1)], flags, after=(before,))
-        (late_parts,), before = deal_rounds([(late_parts, at, step, False, 1)], flags, after=(before,))
+        (early_parts,), before = deal_rounds([(early_parts, early_bits.pop(0), 1, False, 1)], flags, after=(before,))
+        (late_parts, early_parts), before = deal_rounds(
+            [(late_parts, at, step, False, 1), (early_parts, early_bits.pop(0), 1, False, 1)], flags, after=(before,)
+        )
         at += step
     while early_bits:
-        bit = early_bits.pop(0)
-        (early_parts,), before = deal_rounds(
-            [(early_parts, bit, 1, False, 3 if bit == 1 else 1)], flags, after=(before,)
-        )
+        (early_parts,), before = deal_rounds([(early_parts, early_bits.pop(0), 1, False, 1)], flags, after=(before,))
     feature_grad = vmem_call(
         feat_grad_kernel,
         sds(images, depths, tokens, dim),
@@ -547,7 +544,7 @@
     )
     sent, kept = vmem_call(
         functools.partial(last_kernel, tuple(len(part) for part in early_parts)),
-        [sds(block_rows, channels), sds(block_rows, channels, dtype=F32)],
+        [sds(block_rows, channels // 2), sds(block_rows, channels // 2, dtype=F32)],
         [flags] + [piece for part in early_parts + late_parts for piece in part],
     )
     other = xor_move(sent, 0, True)

time: 68.7 us -> 67.9 us (0.988)
  starting transfers between devices: 28 us -> 25.8 us
  waiting for transfers between devices: 19.3 us -> 20.7 us
    ppermute x2 -> x3, waiting for transfers between devices: 1.55 us -> 6.59 us  [xor_move(): return lax.ppermute(block, 'dp', [(0, 1), (1, 0)])]
    ppermute x21 -> x19, starting transfers between devices: 18.3 us -> 13.7 us  [xor_move(): return lax.ppermute(block, 'tile', [(t, t ^ apart) for t in range(tiles)])]
    ppermute x21 -> x19, waiting for transfers between devices: 13.2 us -> 8.77 us  [xor_move(): return lax.ppermute(block, 'tile', [(t, t ^ apart) for t in range(tiles)])]
    ppermute x1, starting transfers between devices: 0.46 us -> 2.11 us  [xor_move(): return lax.ppermute(block, ('dp', 'tile'), route)]
    ppermute x1, waiting for transfers between devices: 3.45 us -> 4.27 us  [xor_move(): return lax.ppermute(block, ('dp', 'tile'), route)]
    ppermute x2 -> x3, starting transfers between devices: 3.06 us -> 3.8 us  [xor_move(): return lax.ppermute(block, 'dp', [(0, 1), (1, 0)])]
  transfers between devices with their start and end apart: 27 -> 26, of which waited for: 14 -> 14; matrix products, arithmetic and copies ran while one was open for 0% -> 0% of each run, Pallas kernels for 17% -> 16%
where the time goes in v8:
time: 67.9 us; the launch traced here: 67.7 us
  starting transfers between devices  25.8 us (38%)
  waiting for transfers between devices  20.7 us (30%)
  Pallas kernels  16.1 us (24%)
  local copies, waits for them, and re-layouts  3 us (4%)
  other arithmetic  1.19 us (2%)
  between operations  0.89 us (1%)
    pallas_call x15, Pallas kernels, vmem_call(): pl.pallas_call(run, out_shape=out_shape, in_specs=specs, out_specs=jax.tr...  16.1 us
    ppermute x19, starting transfers between devices, xor_move(): return lax.ppermute(block, 'tile', [(t, t ^ apart) for t in range(tiles)])  13.7 us
    ppermute x19, waiting for transfers between devices, xor_move(): return lax.ppermute(block, 'tile', [(t, t ^ apart) for t in range(tiles)])  8.77 us
    ppermute x3, waiting for transfers between devices, xor_move(): return lax.ppermute(block, 'dp', [(0, 1), (1, 0)])  6.59 us
    ppermute x3, starting transfers between devices, swap(): return lax.ppermute(block, 'tile', tile_route(row_pairs, col_pairs, rows))  6.19 us
    ppermute x1, waiting for transfers between devices, xor_move(): return lax.ppermute(block, ('dp', 'tile'), route)  4.27 us
    ppermute x3, starting transfers between devices, xor_move(): return lax.ppermute(block, 'dp', [(0, 1), (1, 0)])  3.8 us
    unnamed x12, local copies, waits for them, and re-layouts  2.91 us
  transfers between devices with their start and end apart: 26, of which 14 were waited for; matrix products, arithmetic and copies ran while one was open for 0% of the time, Pallas kernels for 16%

profile of v8, /device:TPU:0, one launch (start us, length us, event | category | flops | bytes accessed | tf_op | source)
XLA Modules:
  0.0 67.7 jit_solution(8104574983335535224)
XLA Ops:
  0.7 1.2 %broadcast_select_fusion = (bf16[4,16,4,256]{3,2,1,0:T(4,128)(2,1)S(1)}, bf16[4,16,4,256]{3,2,1,0:T(4,128)(2,1)S(1)}) fusion(pred[]{:T(512)S(6)} %eq.27, bf16[4,16,32,256]{3,2,1,0:T(8,128)(2,1)} %refs_0_.1), kind=kLoop, calls=%fused_computation | loop fusion | flops 131072 | bytes 524289 | tf_op jit(solution)/shard_map/jit(_where)/select_n | solution.py:455
  1.9 3.1 %collective-permute-start.1 = (bf16[4,16,4,256]{3,2,1,0:T(4,128)(2,1)S(1)}, bf16[4,16,4,256]{3,2,1,0:T(4,128)(2,1)S(1)}, u32[]{:S(2)}, u32[]{:S(2)}) collective-permute-start(bf16[4,16,4,256]{3,2,1,0:T(4,128)(2,1)S(1)} %get-tuple-element.82), channel_id=1, source_target_pairs={{1,3},{3,1},{2,6},{6,2},{7,5},{5,7},{0,4},{4,0},{9,11},{11,9},{10,... | collective-permute-start | bytes 393224 | tf_op jit(solution)/shard_map/ppermute | solution.py:451
  4.9 0.0 collective-permute-start
  4.9 1.2 %copy-done.3 = bf16[4,16,32,256]{3,2,1,0:T(8,128)(2,1)S(1)} copy-done((bf16[4,16,32,256]{3,2,1,0:T(8,128)(2,1)S(1)}, bf16[4,16,32,256]{3,2,1,0:T(8,128)(2,1)}, u32[]{:S(2)}) %copy-start.3) | copy-done | bytes 1048600
  6.2 0.5 shard_map.68.refs_1_
  6.7 0.1 stack.71.refs_0_
  6.8 1.1 %collective-permute-done.1.refs_3_ = bf16[4,16,4,256]{3,2,1,0:T(4,128)(2,1)S(1)} collective-permute-done((bf16[4,16,4,256]{3,2,1,0:T(4,128)(2,1)S(1)}, bf16[4,16,4,256]{3,2,1,0:T(4,128)(2,1)S(1)}, u32[]{:S(2)}, u32[]{:S(2)}) %collective-permute-start.1) | collective-permute-done | bytes 131104 | tf_op jit(solution)/shard_map/ppermute | solution.py:451
  7.9 0.8 %shard_map.69 = (bf16[144,256]{1,0:T(8,128)(2,1)S(1)}, f32[4,6,16,256]{3,2,1,0:T(8,128)S(1)}, f32[4,6,2,256]{3,2,1,0:T(2,128)S(1)}) custom-call(s32[13]{0:T(128)S(1)} %stack.71.refs_0_, f32[4,16,24,256]{3,2,1,0:T(8,128)S(1)} %shard_map.68.refs_1_, bf16[4,16,4,256]{3,2,1,0:T(4,128)(2,1)S(1)} %collective-permute-done.refs_2_, ...), custom_call_target="tpu_custom_call" | custom-call | bytes 2351156 | tf_op jit(solution)/shard_map/pallas_call | solution.py:359
  8.7 3.1 %collective-permute-start.2 = (bf16[144,256]{1,0:T(8,128)(2,1)S(1)}, bf16[144,256]{1,0:T(8,128)(2,1)S(1)}, u32[]{:S(2)}, u32[]{:S(2)}) collective-permute-start(bf16[144,256]{1,0:T(8,128)(2,1)S(1)} %get-tuple-element.42.refs_5_), channel_id=1, source_target_pairs={{0,8},{1,9},{3,11},{2,10},{6,14},{7,15},{5,13},{4,12},{8,0},{9,1},... | collective-permute-start | bytes 221192 | tf_op jit(solution)/shard_map/ppermute | solution.py:451
  11.8 1.7 %copy-done = bf16[2,3,3,256,256]{4,3,2,1,0:T(8,128)(2,1)S(1)} copy-done((bf16[2,3,3,256,256]{4,3,2,1,0:T(8,128)(2,1)S(1)}, bf16[2,3,3,256,256]{4,3,2,1,0:T(8,128)(2,1)}, u32[]{:S(2)}) %copy-start) | copy-done | bytes 2359320
  13.4 2.4 %shard_map.70 = (bf16[3,640,256]{2,1,0:T(8,128)(2,1)S(1)}, f32[2,512,256]{2,1,0:T(8,128)S(1)}) custom-call(s32[13]{0:T(128)S(1)} %stack.71.refs_0_, f32[4,16,24,256]{3,2,1,0:T(8,128)S(1)} %shard_map.68.refs_1_, bf16[4,16,4,256]{3,2,1,0:T(4,128)(2,1)S(1)} %collective-permute-done.refs_2_, bf16[4,16,4,256]{3,2,1,0:T(4,128)(2,1)S(1)} %collective-permute-done.1.refs_3_, ...), custom_call_target="tpu_custom_call" | custom-call | flops 1207959552 | bytes 6225972 | tf_op jit(solution)/shard_map/pallas_call | solution.py:359
  15.8 0.0 collective-permute-done.2.refs_1_
  15.8 0.0 copy-start.5
  15.9 1.6 %shard_map.71 = (bf16[2,2,64,256]{3,2,1,0:T(8,128)(2,1)S(1)}, bf16[2,2,64,256]{3,2,1,0:T(8,128)(2,1)S(1)}, bf16[2,2,64,256]{3,2,1,0:T(8,128)(2,1)S(1)}, bf16[2,2...) custom-call(s32[13]{0:T(128)S(1)} %stack.71.refs_0_, ...), custom_call_target="tpu_custom_call", output_to_operand_aliasing={{4}: (4, {})} | custom-call | flops 301989888 | bytes 6414388 | tf_op jit(solution)/shard_map/pallas_call | solution.py:359
  17.5 1.6 %collective-permute-start.3 = (bf16[2,2,64,256]{3,2,1,0:T(8,128)(2,1)S(1)}, bf16[2,2,64,256]{3,2,1,0:T(8,128)(2,1)S(1)}, u32[]{:S(2)}, u32[]{:S(2)}) collective-permute-start(bf16[2,2,64,256]{3,2,1,0:T(8,128)(2,1)S(1)} %get-tuple-element.48), channel_id=1, source_target_pairs={{0,2},{1,3},{2,0},{3,1},{4,6},{5,7},{6,4},{7,5},{8,10},{9,11},{10,... | collective-permute-start | bytes 393224 | tf_op jit(solution)/shard_map/ppermute | solution.py:378
  19.1 1.6 %collective-permute-start.4 = (bf16[2,2,64,256]{3,2,1,0:T(8,128)(2,1)S(1)}, bf16[2,2,64,256]{3,2,1,0:T(8,128)(2,1)S(1)}, u32[]{:S(2)}, u32[]{:S(2)}) collective-permute-start(bf16[2,2,64,256]{3,2,1,0:T(8,128)(2,1)S(1)} %get-tuple-element.49), channel_id=1, source_target_pairs={{0,4},{1,5},{2,6},{3,7},{4,0},{5,1},{6,2},{7,3},{8,12},{9,13},{10,... | collective-permute-start | bytes 393224 | tf_op jit(solution)/shard_map/ppermute | solution.py:378
  20.7 0.4 collective-permute-start.5
  21.1 2.1 %shard_map.73 = (bf16[8,208,256]{2,1,0:T(8,128)(2,1)S(1)}, bf16[2,208,256]{2,1,0:T(8,128)(2,1)S(1)}, bf16[2,208,256]{2,1,0:T(8,128)(2,1)S(1)}, bf16[2,208,256]{2...) custom-call(s32[13]{0:T(128)S(1)} %stack.71.refs_0_, ...), custom_call_target="tpu_custom_call" | custom-call | flops 1207959552 | bytes 3866676 | tf_op jit(solution)/shard_map/pallas_call | solution.py:359
  23.1 0.0 copy-start.2
  23.2 0.1 collective-permute-start.7
  23.2 0.5 collective-permute-start.8
  23.7 0.1 collective-permute-start.9
  23.8 0.5 collective-permute-done.4.refs_2_.refs_3_
  24.4 0.0 collective-permute-start.10
  24.4 2.2 %collective-permute-done.5.refs_3_.refs_4_ = bf16[2,2,64,256]{3,2,1,0:T(8,128)(2,1)S(1)} collective-permute-done((bf16[2,2,64,256]{3,2,1,0:T(8,128)(2,1)S(1)}, bf16[2,2,64,256]{3,2,1,0:T(8,128)(2,1)S(1)}, u32[]{:S(2)}, u32[]{:S(2)}) %collective-permute-start.5) | collective-permute-done | bytes 131104 | tf_op jit(solution)/shard_map/ppermute | solution.py:378
  26.5 0.1 collective-permute-start.6
  26.6 0.0 collective-permute-done.7.refs_2_
  26.6 0.0 collective-permute-done.9.refs_4_
  26.7 0.0 collective-permute-done.10.refs_5_
  26.7 0.7 %shard_map.74 = (f32[8,208,128]{2,1,0:T(8,128)S(1)}, bf16[8,208,128]{2,1,0:T(8,128)(2,1)S(1)}) custom-call(s32[13]{0:T(128)S(1)} %stack.71.refs_0_, bf16[8,208,256]{2,1,0:T(8,128)(2,1)S(1)} %get-tuple-element.53.refs_1_, bf16[2,208,256]{2,1,0:T(8,128)(2,1)S(1)} %collective-permute-done.7.refs_2_, bf16[2,208,256]{2,1,0:T(8,128)(2,1)S(1)} %collective-permute-done.8.refs_3_, ...), custom_call_target="tpu_custom_call" | custom-call | bytes 2981940 | tf_op jit(solution)/shard_map/pallas_call | solution.py:359
  27.4 1.6 %collective-permute-start.18 = (bf16[8,208,128]{2,1,0:T(8,128)(2,1)S(1)}, bf16[8,208,128]{2,1,0:T(8,128)(2,1)S(1)}, u32[]{:S(2)}, u32[]{:S(2)}) collective-permute-start(bf16[8,208,128]{2,1,0:T(8,128)(2,1)S(1)} %get-tuple-element.69), channel_id=1, source_target_pairs={{0,16},{16,0},{1,17},{17,1},{2,18},{18,2},{3,19},{19,3},{4,20},{20... | collective-permute-start | bytes 1277960 | tf_op jit(solution)/shard_map/ppermute | solution.py:380
  29.0 1.5 %shard_map.75 = (bf16[8,208,256]{2,1,0:T(8,128)(2,1)S(1)}, bf16[2,208,256]{2,1,0:T(8,128)(2,1)S(1)}, bf16[2,208,256]{2,1,0:T(8,128)(2,1)S(1)}, bf16[2,208,256]{2...) custom-call(s32[13]{0:T(128)S(1)} %stack.71.refs_0_, ...), custom_call_target="tpu_custom_call" | custom-call | flops 536870912 | bytes 5767220 | tf_op jit(solution)/shard_map/pallas_call | solution.py:359
  30.5 0.3 collective-permute-start.11
  30.7 0.3 collective-permute-start.12
  31.0 0.2 collective-permute-start.13
  31.2 0.3 collective-permute-start.14
  31.5 0.4 collective-permute-done.11.refs_2_
  32.0 0.3 collective-permute-done.12.refs_3_
  32.3 0.3 collective-permute-done.13.refs_4_
  32.6 0.3 collective-permute-done.14.refs_5_
  32.9 0.7 %shard_map.76 = (f32[4,208,128]{2,1,0:T(8,128)S(1)}, bf16[4,208,128]{2,1,0:T(8,128)(2,1)S(1)}, bf16[4,208,128]{2,1,0:T(8,128)(2,1)S(1)}, bf16[4,208,128]{2,1,0:T(8,128)(2,1)S(1)}) custom-call(s32[13]{0:T(128)S(1)} %stack.71.refs_0_, bf16[8,208,256]{2,1,0:T(8,128)(2,1)S(1)} %get-tuple-element.60.refs_1_, ...), custom_call_target="tpu_custom_call" | custom-call | bytes 2768948 | tf_op jit(solution)/shard_map/pallas_call | solution.py:359
  33.6 0.8 %collective-permute-start.15 = (bf16[4,208,128]{2,1,0:T(8,128)(2,1)S(1)}, bf16[4,208,128]{2,1,0:T(8,128)(2,1)S(1)}, u32[]{:S(2)}, u32[]{:S(2)}) collective-permute-start(bf16[4,208,128]{2,1,0:T(8,128)(2,1)S(1)} %get-tuple-element.66), channel_id=1, source_target_pairs={{0,2},{1,3},{2,0},{3,1},{4,6},{5,7},{6,4},{7,5},{8,10},{9,11},{10,... | collective-permute-start | bytes 638984 | tf_op jit(solution)/shard_map/ppermute | solution.py:378
  34.4 0.7 %collective-permute-start.16 = (bf16[4,208,128]{2,1,0:T(8,128)(2,1)S(1)}, bf16[4,208,128]{2,1,0:T(8,128)(2,1)S(1)}, u32[]{:S(2)}, u32[]{:S(2)}) collective-permute-start(bf16[4,208,128]{2,1,0:T(8,128)(2,1)S(1)} %get-tuple-element.67), channel_id=1, source_target_pairs={{0,16},{16,0},{1,17},{17,1},{2,18},{18,2},{3,19},{19,3},{4,20},{20... | collective-permute-start | bytes 638984 | tf_op jit(solution)/shard_map/ppermute | solution.py:380
  35.1 2.1 %collective-permute-start.17 = (bf16[4,208,128]{2,1,0:T(8,128)(2,1)S(1)}, bf16[4,208,128]{2,1,0:T(8,128)(2,1)S(1)}, u32[]{:S(2)}, u32[]{:S(2)}) collective-permute-start(bf16[4,208,128]{2,1,0:T(8,128)(2,1)S(1)} %get-tuple-element.68), channel_id=1, source_target_pairs={{0,18},{1,19},{2,16},{3,17},{4,22},{5,23},{6,20},{7,21},{8,26},{9,... | collective-permute-start | bytes 638984 | tf_op jit(solution)/shard_map/ppermute | solution.py:382
  37.2 2.9 %collective-permute-done.18.refs_2_ = bf16[8,208,128]{2,1,0:T(8,128)(2,1)S(1)} collective-permute-done((bf16[8,208,128]{2,1,0:T(8,128)(2,1)S(1)}, bf16[8,208,128]{2,1,0:T(8,128)(2,1)S(1)}, u32[]{:S(2)}, u32[]{:S(2)}) %collective-permute-start.18) | collective-permute-done | bytes 426016 | tf_op jit(solution)/shard_map/ppermute | solution.py:380
  40.1 0.6 shard_map.77
  40.7 0.8 %collective-permute-start.19 = (bf16[4,208,128]{2,1,0:T(8,128)(2,1)S(1)}, bf16[4,208,128]{2,1,0:T(8,128)(2,1)S(1)}, u32[]{:S(2)}, u32[]{:S(2)}) collective-permute-start(bf16[4,208,128]{2,1,0:T(8,128)(2,1)S(1)} %get-tuple-element.71), channel_id=1, source_target_pairs={{0,4},{1,5},{2,6},{3,7},{4,0},{5,1},{6,2},{7,3},{8,12},{9,13},{10,... | collective-permute-start | bytes 638984 | tf_op jit(solution)/shard_map/ppermute | solution.py:378
  41.5 3.1 %collective-permute-done.16.refs_3_ = bf16[4,208,128]{2,1,0:T(8,128)(2,1)S(1)} collective-permute-done((bf16[4,208,128]{2,1,0:T(8,128)(2,1)S(1)}, bf16[4,208,128]{2,1,0:T(8,128)(2,1)S(1)}, u32[]{:S(2)}, u32[]{:S(2)}) %collective-permute-start.16) | collective-permute-done | bytes 213024 | tf_op jit(solution)/shard_map/ppermute | solution.py:380
  44.7 4.3 %collective-permute-done.17.refs_4_ = bf16[4,208,128]{2,1,0:T(8,128)(2,1)S(1)} collective-permute-done((bf16[4,208,128]{2,1,0:T(8,128)(2,1)S(1)}, bf16[4,208,128]{2,1,0:T(8,128)(2,1)S(1)}, u32[]{:S(2)}, u32[]{:S(2)}) %collective-permute-start.17) | collective-permute-done | bytes 213024 | tf_op jit(solution)/shard_map/ppermute | solution.py:382
  48.9 0.7 %shard_map.78 = (f32[1,208,128]{2,1,0:T(8,128)S(1)}, bf16[1,208,128]{2,1,0:T(8,128)(2,1)S(1)}, bf16[1,208,128]{2,1,0:T(8,128)(2,1)S(1)}, bf16[1,208,128]{2,1,0:T...) custom-call(s32[13]{0:T(128)S(1)} %stack.71.refs_0_, ...), custom_call_target="tpu_custom_call" | custom-call | bytes 2289716 | tf_op jit(solution)/shard_map/pallas_call | solution.py:359
  49.6 1.4 %collective-permute-start.20 = (bf16[2,208,128]{2,1,0:T(8,128)(2,1)S(1)}, bf16[2,208,128]{2,1,0:T(8,128)(2,1)S(1)}, u32[]{:S(2)}, u32[]{:S(2)}) collective-permute-start(bf16[2,208,128]{2,1,0:T(8,128)(2,1)S(1)} %get-tuple-element.73), channel_id=1, source_target_pairs={{0,2},{1,3},{2,0},{3,1},{4,6},{5,7},{6,4},{7,5},{8,10},{9,11},{10,... | collective-permute-start | bytes 319496 | tf_op jit(solution)/shard_map/ppermute | solution.py:378
  51.0 0.7 %collective-permute-start.22 = (bf16[1,208,128]{2,1,0:T(8,128)(2,1)S(1)}, bf16[1,208,128]{2,1,0:T(8,128)(2,1)S(1)}, u32[]{:S(2)}, u32[]{:S(2)}) collective-permute-start(bf16[1,208,128]{2,1,0:T(8,128)(2,1)S(1)} %get-tuple-element.77), channel_id=1, source_target_pairs={{0,4},{1,5},{2,6},{3,7},{4,0},{5,1},{6,2},{7,3},{8,12},{9,13},{10,... | collective-permute-start | bytes 159752 | tf_op jit(solution)/shard_map/ppermute | solution.py:378
  51.8 1.5 %collective-permute-start.23 = (bf16[1,208,128]{2,1,0:T(8,128)(2,1)S(1)}, bf16[1,208,128]{2,1,0:T(8,128)(2,1)S(1)}, u32[]{:S(2)}, u32[]{:S(2)}) collective-permute-start(bf16[1,208,128]{2,1,0:T(8,128)(2,1)S(1)} %get-tuple-element.78), channel_id=1, source_target_pairs={{0,8},{1,9},{2,10},{3,11},{4,12},{5,13},{6,14},{7,15},{8,0},{9,1},... | collective-permute-start | bytes 159752 | tf_op jit(solution)/shard_map/ppermute | solution.py:378
  53.3 2.1 %collective-permute-start.24 = (bf16[1,208,128]{2,1,0:T(8,128)(2,1)S(1)}, bf16[1,208,128]{2,1,0:T(8,128)(2,1)S(1)}, u32[]{:S(2)}, u32[]{:S(2)}) collective-permute-start(bf16[1,208,128]{2,1,0:T(8,128)(2,1)S(1)} %get-tuple-element.79), channel_id=1, source_target_pairs={{0,12},{1,13},{2,14},{3,15},{4,8},{5,9},{6,10},{7,11},{8,4},{9,5},... | collective-permute-start | bytes 159752 | tf_op jit(solution)/shard_map/ppermute | solution.py:378
  55.4 0.6 shard_map.79
  56.0 1.0 %collective-permute-start.21 = (bf16[1,208,128]{2,1,0:T(8,128)(2,1)S(1)}, bf16[1,208,128]{2,1,0:T(8,128)(2,1)S(1)}, u32[]{:S(2)}, u32[]{:S(2)}) collective-permute-start(bf16[1,208,128]{2,1,0:T(8,128)(2,1)S(1)} %get-tuple-element.76), channel_id=1, source_target_pairs={{0,8},{1,9},{2,10},{3,11},{4,12},{5,13},{6,14},{7,15},{8,0},{9,1},... | collective-permute-start | bytes 159752 | tf_op jit(solution)/shard_map/ppermute | solution.py:378
  57.0 1.1 %collective-permute-done.23.refs_5_ = bf16[1,208,128]{2,1,0:T(8,128)(2,1)S(1)} collective-permute-done((bf16[1,208,128]{2,1,0:T(8,128)(2,1)S(1)}, bf16[1,208,128]{2,1,0:T(8,128)(2,1)S(1)}, u32[]{:S(2)}, u32[]{:S(2)}) %collective-permute-start.23) | collective-permute-done | bytes 53280 | tf_op jit(solution)/shard_map/ppermute | solution.py:378
  58.0 1.2 %collective-permute-done.24.refs_6_ = bf16[1,208,128]{2,1,0:T(8,128)(2,1)S(1)} collective-permute-done((bf16[1,208,128]{2,1,0:T(8,128)(2,1)S(1)}, bf16[1,208,128]{2,1,0:T(8,128)(2,1)S(1)}, u32[]{:S(2)}, u32[]{:S(2)}) %collective-permute-start.24) | collective-permute-done | bytes 53280 | tf_op jit(solution)/shard_map/ppermute | solution.py:378
  59.2 2.4 %collective-permute-done.21.refs_2_ = bf16[1,208,128]{2,1,0:T(8,128)(2,1)S(1)} collective-permute-done((bf16[1,208,128]{2,1,0:T(8,128)(2,1)S(1)}, bf16[1,208,128]{2,1,0:T(8,128)(2,1)S(1)}, u32[]{:S(2)}, u32[]{:S(2)}) %collective-permute-start.21) | collective-permute-done | bytes 53280 | tf_op jit(solution)/shard_map/ppermute | solution.py:378
  61.6 0.6 shard_map.81
  62.2 1.6 %collective-permute-start.25 = (bf16[208,128]{1,0:T(8,128)(2,1)S(1)}, bf16[208,128]{1,0:T(8,128)(2,1)S(1)}, u32[]{:S(2)}, u32[]{:S(2)}) collective-permute-start(bf16[208,128]{1,0:T(8,128)(2,1)S(1)} %get-tuple-element.81), channel_id=1, source_target_pairs={{0,16},{16,0},{1,17},{17,1},{2,18},{18,2},{3,19},{19,3},{4,20},{20... | collective-permute-start | bytes 159752 | tf_op jit(solution)/shard_map/ppermute | solution.py:380
  63.8 2.1 %shard_map.80 = bf16[4,2,128,1024]{3,2,1,0:T(8,128)(2,1)} custom-call(bf16[2,512,256]{2,1,0:T(8,128)(2,1)S(1)} %get-tuple-element.59.refs_6_.refs_0_, bf16[2,1024,256]{2,1,0:T(8,128)(2,1)S(1)} %copy-done.4, f32[1,208,128]{2,1,0:T(8,128)S(1)} %get-tuple-element.75.refs_2_.refs_1_), custom_call_target="tpu_custom_call" | custom-call | flops 536870912 | bytes 3670016 | tf_op jit(solution)/shard_map/pallas_call | solution.py:359
  65.9 0.6 collective-permute-done.25.refs_2_
  66.4 1.2 %shard_map.82 = f32[208,256]{1,0:T(8,128)} custom-call(s32[13]{0:T(128)S(1)} %stack.71.refs_0_, f32[208,128]{1,0:T(8,128)S(1)} %get-tuple-element.80.refs_1_, bf16[208,128]{1,0:T(8,128)(2,1)S(1)} %collective-permute-done.25.refs_2_), custom_call_target="tpu_custom_call" | custom-call | bytes 372788 | tf_op jit(solution)/shard_map/pallas_call | solution.py:359
  (17 shorter events, 0.1 us)
Async XLA Ops:
  1.9 6.0 %collective-permute-start.1 = (bf16[4,16,4,256]{3,2,1,0:T(4,128)(2,1)S(1)}, bf16[4,16,4,256]{3,2,1,0:T(4,128)(2,1)S(1)}, u32[]{:S(2)}, u32[]{:S(2)}) collective-permute-start(bf16[4,16,4,256]{3,2,1,0:T(4,128)(2,1)S(1)} %get-tuple-element.82), channel_id=1, source_target_pairs={{1,3},{3,1},{2,6},{6,2},{7,5},{5,7},{0,4},{4,0},{9,11},{11,9},{10,... | collective-permute-start | bytes 393224 | tf_op jit(solution)/shard_map/ppermute | solution.py:451
  4.9 3.0 %collective-permute-start = (bf16[4,16,4,256]{3,2,1,0:T(4,128)(2,1)S(1)}, bf16[4,16,4,256]{3,2,1,0:T(4,128)(2,1)S(1)}, u32[]{:S(2)}, u32[]{:S(2)}) collective-permute-start(bf16[4,16,4,256]{3,2,1,0:T(4,128)(2,1)S(1)} %get-tuple-element.83), channel_id=1, source_target_pairs={{0,1},{1,0},{3,2},{2,3},{6,7},{7,6},{5,4},{4,5},{8,9},{9,8},{11,10... | collective-permute-start | bytes 393224 | tf_op jit(solution)/shard_map/ppermute | solution.py:451
  4.9 1.2 %copy-start.3 = (bf16[4,16,32,256]{3,2,1,0:T(8,128)(2,1)S(1)}, bf16[4,16,32,256]{3,2,1,0:T(8,128)(2,1)}, u32[]{:S(2)}) copy-start(bf16[4,16,32,256]{3,2,1,0:T(8,128)(2,1)} %refs_0_.1) | copy-start | bytes 3145732
  8.7 7.2 %collective-permute-start.2 = (bf16[144,256]{1,0:T(8,128)(2,1)S(1)}, bf16[144,256]{1,0:T(8,128)(2,1)S(1)}, u32[]{:S(2)}, u32[]{:S(2)}) collective-permute-start(bf16[144,256]{1,0:T(8,128)(2,1)S(1)} %get-tuple-element.42.refs_5_), channel_id=1, source_target_pairs={{0,8},{1,9},{3,11},{2,10},{6,14},{7,15},{5,13},{4,12},{8,0},{9,1},... | collective-permute-start | bytes 221192 | tf_op jit(solution)/shard_map/ppermute | solution.py:451
  11.8 1.7 %copy-start = (bf16[2,3,3,256,256]{4,3,2,1,0:T(8,128)(2,1)S(1)}, bf16[2,3,3,256,256]{4,3,2,1,0:T(8,128)(2,1)}, u32[]{:S(2)}) copy-start(bf16[2,3,3,256,256]{4,3,2,1,0:T(8,128)(2,1)} %refs_6_.2) | copy-start | bytes 7077892
  13.4 2.4 %copy-start.1 = (bf16[2,3,3,256,256]{4,3,2,1,0:T(8,128)(2,1)S(1)}, bf16[2,3,3,256,256]{4,3,2,1,0:T(8,128)(2,1)}, u32[]{:S(2)}) copy-start(bf16[2,3,3,256,256]{4,3,2,1,0:T(8,128)(2,1)} %refs_6_.2) | copy-start | bytes 7077892
  15.8 5.2 %copy-start.5 = (bf16[4,2,8,16,256]{4,3,2,1,0:T(8,128)(2,1)S(1)}, bf16[4,2,8,16,256]{4,3,2,1,0:T(8,128)(2,1)}, u32[]{:S(2)}) copy-start(bf16[4,2,8,16,256]{4,3,2,1,0:T(8,128)(2,1)} %refs_2_.1) | copy-start | bytes 1572868
  17.5 6.2 %collective-permute-start.3 = (bf16[2,2,64,256]{3,2,1,0:T(8,128)(2,1)S(1)}, bf16[2,2,64,256]{3,2,1,0:T(8,128)(2,1)S(1)}, u32[]{:S(2)}, u32[]{:S(2)}) collective-permute-start(bf16[2,2,64,256]{3,2,1,0:T(8,128)(2,1)S(1)} %get-tuple-element.48), channel_id=1, source_target_pairs={{0,2},{1,3},{2,0},{3,1},{4,6},{5,7},{6,4},{7,5},{8,10},{9,11},{10,... | collective-permute-start | bytes 393224 | tf_op jit(solution)/shard_map/ppermute | solution.py:378
  19.1 5.3 %collective-permute-start.4 = (bf16[2,2,64,256]{3,2,1,0:T(8,128)(2,1)S(1)}, bf16[2,2,64,256]{3,2,1,0:T(8,128)(2,1)S(1)}, u32[]{:S(2)}, u32[]{:S(2)}) collective-permute-start(bf16[2,2,64,256]{3,2,1,0:T(8,128)(2,1)S(1)} %get-tuple-element.49), channel_id=1, source_target_pairs={{0,4},{1,5},{2,6},{3,7},{4,0},{5,1},{6,2},{7,3},{8,12},{9,13},{10,... | collective-permute-start | bytes 393224 | tf_op jit(solution)/shard_map/ppermute | solution.py:378
  20.7 5.9 %collective-permute-start.5 = (bf16[2,2,64,256]{3,2,1,0:T(8,128)(2,1)S(1)}, bf16[2,2,64,256]{3,2,1,0:T(8,128)(2,1)S(1)}, u32[]{:S(2)}, u32[]{:S(2)}) collective-permute-start(bf16[2,2,64,256]{3,2,1,0:T(8,128)(2,1)S(1)} %get-tuple-element.50), channel_id=1, source_target_pairs={{0,6},{1,7},{2,4},{3,5},{4,2},{5,3},{6,0},{7,1},{8,14},{9,15},{10,... | collective-permute-start | bytes 393224 | tf_op jit(solution)/shard_map/ppermute | solution.py:378
  23.1 5.8 %copy-start.2 = (bf16[4,2,128,1024]{3,2,1,0:T(8,128)(2,1)S(1)}, bf16[4,2,128,1024]{3,2,1,0:T(8,128)(2,1)}, u32[]{:S(2)}) copy-start(bf16[4,2,128,1024]{3,2,1,0:T(8,128)(2,1)} %refs_6_.3) | copy-start | bytes 6291460
  23.2 3.5 %collective-permute-start.7 = (bf16[2,208,256]{2,1,0:T(8,128)(2,1)S(1)}, bf16[2,208,256]{2,1,0:T(8,128)(2,1)S(1)}, u32[]{:S(2)}, u32[]{:S(2)}) collective-permute-start(bf16[2,208,256]{2,1,0:T(8,128)(2,1)S(1)} %get-tuple-element.54), channel_id=1, source_target_pairs={{0,1},{1,0},{2,3},{3,2},{4,5},{5,4},{6,7},{7,6},{8,9},{9,8},{10,11... | collective-permute-start | bytes 638984 | tf_op jit(solution)/shard_map/ppermute | solution.py:378
  23.2 3.4 %collective-permute-start.8 = (bf16[2,208,256]{2,1,0:T(8,128)(2,1)S(1)}, bf16[2,208,256]{2,1,0:T(8,128)(2,1)S(1)}, u32[]{:S(2)}, u32[]{:S(2)}) collective-permute-start(bf16[2,208,256]{2,1,0:T(8,128)(2,1)S(1)} %get-tuple-element.55), channel_id=1, source_target_pairs={{0,1},{1,0},{2,3},{3,2},{4,5},{5,4},{6,7},{7,6},{8,9},{9,8},{10,11... | collective-permute-start | bytes 638984 | tf_op jit(solution)/shard_map/ppermute | solution.py:378
  23.7 2.9 %collective-permute-start.9 = (bf16[2,208,256]{2,1,0:T(8,128)(2,1)S(1)}, bf16[2,208,256]{2,1,0:T(8,128)(2,1)S(1)}, u32[]{:S(2)}, u32[]{:S(2)}) collective-permute-start(bf16[2,208,256]{2,1,0:T(8,128)(2,1)S(1)} %get-tuple-element.56), channel_id=1, source_target_pairs={{0,1},{1,0},{2,3},{3,2},{4,5},{5,4},{6,7},{7,6},{8,9},{9,8},{10,11... | collective-permute-start | bytes 638984 | tf_op jit(solution)/shard_map/ppermute | solution.py:378
  24.4 2.3 %collective-permute-start.10 = (bf16[2,208,256]{2,1,0:T(8,128)(2,1)S(1)}, bf16[2,208,256]{2,1,0:T(8,128)(2,1)S(1)}, u32[]{:S(2)}, u32[]{:S(2)}) collective-permute-start(bf16[2,208,256]{2,1,0:T(8,128)(2,1)S(1)} %get-tuple-element.57), channel_id=1, source_target_pairs={{0,1},{1,0},{2,3},{3,2},{4,5},{5,4},{6,7},{7,6},{8,9},{9,8},{10,11... | collective-permute-start | bytes 638984 | tf_op jit(solution)/shard_map/ppermute | solution.py:378
  26.5 2.4 %collective-permute-start.6 = (bf16[4,2,64,256]{3,2,1,0:T(8,128)(2,1)S(1)}, bf16[4,2,64,256]{3,2,1,0:T(8,128)(2,1)S(1)}, u32[]{:S(2)}, u32[]{:S(2)}) collective-permute-start(bf16[4,2,64,256]{3,2,1,0:T(8,128)(2,1)S(1)} %shard_map.72), channel_id=1, source_target_pairs={{0,1},{1,0},{2,3},{3,2},{4,5},{5,4},{6,7},{7,6},{8,9},{9,8},{10,11... | collective-permute-start | bytes 786440 | tf_op jit(solution)/shard_map/ppermute | solution.py:378
  27.4 12.7 %collective-permute-start.18 = (bf16[8,208,128]{2,1,0:T(8,128)(2,1)S(1)}, bf16[8,208,128]{2,1,0:T(8,128)(2,1)S(1)}, u32[]{:S(2)}, u32[]{:S(2)}) collective-permute-start(bf16[8,208,128]{2,1,0:T(8,128)(2,1)S(1)} %get-tuple-element.69), channel_id=1, source_target_pairs={{0,16},{16,0},{1,17},{17,1},{2,18},{18,2},{3,19},{19,3},{4,20},{20... | collective-permute-start | bytes 1277960 | tf_op jit(solution)/shard_map/ppermute | solution.py:380
  30.5 1.5 %collective-permute-start.11 = (bf16[2,208,256]{2,1,0:T(8,128)(2,1)S(1)}, bf16[2,208,256]{2,1,0:T(8,128)(2,1)S(1)}, u32[]{:S(2)}, u32[]{:S(2)}) collective-permute-start(bf16[2,208,256]{2,1,0:T(8,128)(2,1)S(1)} %get-tuple-element.61), channel_id=1, source_target_pairs={{0,1},{1,0},{2,3},{3,2},{4,5},{5,4},{6,7},{7,6},{8,9},{9,8},{10,11... | collective-permute-start | bytes 638984 | tf_op jit(solution)/shard_map/ppermute | solution.py:378
  30.7 1.6 %collective-permute-start.12 = (bf16[2,208,256]{2,1,0:T(8,128)(2,1)S(1)}, bf16[2,208,256]{2,1,0:T(8,128)(2,1)S(1)}, u32[]{:S(2)}, u32[]{:S(2)}) collective-permute-start(bf16[2,208,256]{2,1,0:T(8,128)(2,1)S(1)} %get-tuple-element.62), channel_id=1, source_target_pairs={{0,1},{1,0},{2,3},{3,2},{4,5},{5,4},{6,7},{7,6},{8,9},{9,8},{10,11... | collective-permute-start | bytes 638984 | tf_op jit(solution)/shard_map/ppermute | solution.py:378
  31.0 1.6 %collective-permute-start.13 = (bf16[2,208,256]{2,1,0:T(8,128)(2,1)S(1)}, bf16[2,208,256]{2,1,0:T(8,128)(2,1)S(1)}, u32[]{:S(2)}, u32[]{:S(2)}) collective-permute-start(bf16[2,208,256]{2,1,0:T(8,128)(2,1)S(1)} %get-tuple-element.63), channel_id=1, source_target_pairs={{0,1},{1,0},{2,3},{3,2},{4,5},{5,4},{6,7},{7,6},{8,9},{9,8},{10,11... | collective-permute-start | bytes 638984 | tf_op jit(solution)/shard_map/ppermute | solution.py:378
  31.2 1.7 %collective-permute-start.14 = (bf16[2,208,256]{2,1,0:T(8,128)(2,1)S(1)}, bf16[2,208,256]{2,1,0:T(8,128)(2,1)S(1)}, u32[]{:S(2)}, u32[]{:S(2)}) collective-permute-start(bf16[2,208,256]{2,1,0:T(8,128)(2,1)S(1)} %get-tuple-element.64), channel_id=1, source_target_pairs={{0,1},{1,0},{2,3},{3,2},{4,5},{5,4},{6,7},{7,6},{8,9},{9,8},{10,11... | collective-permute-start | bytes 638984 | tf_op jit(solution)/shard_map/ppermute | solution.py:378
  33.6 7.9 %collective-permute-start.15 = (bf16[4,208,128]{2,1,0:T(8,128)(2,1)S(1)}, bf16[4,208,128]{2,1,0:T(8,128)(2,1)S(1)}, u32[]{:S(2)}, u32[]{:S(2)}) collective-permute-start(bf16[4,208,128]{2,1,0:T(8,128)(2,1)S(1)} %get-tuple-element.66), channel_id=1, source_target_pairs={{0,2},{1,3},{2,0},{3,1},{4,6},{5,7},{6,4},{7,5},{8,10},{9,11},{10,... | collective-permute-start | bytes 638984 | tf_op jit(solution)/shard_map/ppermute | solution.py:378
  34.4 10.3 %collective-permute-start.16 = (bf16[4,208,128]{2,1,0:T(8,128)(2,1)S(1)}, bf16[4,208,128]{2,1,0:T(8,128)(2,1)S(1)}, u32[]{:S(2)}, u32[]{:S(2)}) collective-permute-start(bf16[4,208,128]{2,1,0:T(8,128)(2,1)S(1)} %get-tuple-element.67), channel_id=1, source_target_pairs={{0,16},{16,0},{1,17},{17,1},{2,18},{18,2},{3,19},{19,3},{4,20},{20... | collective-permute-start | bytes 638984 | tf_op jit(solution)/shard_map/ppermute | solution.py:380
  35.1 13.8 %collective-permute-start.17 = (bf16[4,208,128]{2,1,0:T(8,128)(2,1)S(1)}, bf16[4,208,128]{2,1,0:T(8,128)(2,1)S(1)}, u32[]{:S(2)}, u32[]{:S(2)}) collective-permute-start(bf16[4,208,128]{2,1,0:T(8,128)(2,1)S(1)} %get-tuple-element.68), channel_id=1, source_target_pairs={{0,18},{1,19},{2,16},{3,17},{4,22},{5,23},{6,20},{7,21},{8,26},{9,... | collective-permute-start | bytes 638984 | tf_op jit(solution)/shard_map/ppermute | solution.py:382
  40.1 23.7 %copy-start.4 = (bf16[2,1024,256]{2,1,0:T(8,128)(2,1)S(1)}, bf16[2,1024,256]{2,1,0:T(8,128)(2,1)}, u32[]{:S(2)}) copy-start(bf16[2,1024,256]{2,1,0:T(8,128)(2,1)} %refs_1_.1) | copy-start | bytes 3145732
  40.7 8.2 %collective-permute-start.19 = (bf16[4,208,128]{2,1,0:T(8,128)(2,1)S(1)}, bf16[4,208,128]{2,1,0:T(8,128)(2,1)S(1)}, u32[]{:S(2)}, u32[]{:S(2)}) collective-permute-start(bf16[4,208,128]{2,1,0:T(8,128)(2,1)S(1)} %get-tuple-element.71), channel_id=1, source_target_pairs={{0,4},{1,5},{2,6},{3,7},{4,0},{5,1},{6,2},{7,3},{8,12},{9,13},{10,... | collective-permute-start | bytes 638984 | tf_op jit(solution)/shard_map/ppermute | solution.py:378
  49.6 5.8 %collective-permute-start.20 = (bf16[2,208,128]{2,1,0:T(8,128)(2,1)S(1)}, bf16[2,208,128]{2,1,0:T(8,128)(2,1)S(1)}, u32[]{:S(2)}, u32[]{:S(2)}) collective-permute-start(bf16[2,208,128]{2,1,0:T(8,128)(2,1)S(1)} %get-tuple-element.73), channel_id=1, source_target_pairs={{0,2},{1,3},{2,0},{3,1},{4,6},{5,7},{6,4},{7,5},{8,10},{9,11},{10,... | collective-permute-start | bytes 319496 | tf_op jit(solution)/shard_map/ppermute | solution.py:378
  51.0 6.0 %collective-permute-start.22 = (bf16[1,208,128]{2,1,0:T(8,128)(2,1)S(1)}, bf16[1,208,128]{2,1,0:T(8,128)(2,1)S(1)}, u32[]{:S(2)}, u32[]{:S(2)}) collective-permute-start(bf16[1,208,128]{2,1,0:T(8,128)(2,1)S(1)} %get-tuple-element.77), channel_id=1, source_target_pairs={{0,4},{1,5},{2,6},{3,7},{4,0},{5,1},{6,2},{7,3},{8,12},{9,13},{10,... | collective-permute-start | bytes 159752 | tf_op jit(solution)/shard_map/ppermute | solution.py:378
  51.8 6.3 %collective-permute-start.23 = (bf16[1,208,128]{2,1,0:T(8,128)(2,1)S(1)}, bf16[1,208,128]{2,1,0:T(8,128)(2,1)S(1)}, u32[]{:S(2)}, u32[]{:S(2)}) collective-permute-start(bf16[1,208,128]{2,1,0:T(8,128)(2,1)S(1)} %get-tuple-element.78), channel_id=1, source_target_pairs={{0,8},{1,9},{2,10},{3,11},{4,12},{5,13},{6,14},{7,15},{8,0},{9,1},... | collective-permute-start | bytes 159752 | tf_op jit(solution)/shard_map/ppermute | solution.py:378
  53.3 5.9 %collective-permute-start.24 = (bf16[1,208,128]{2,1,0:T(8,128)(2,1)S(1)}, bf16[1,208,128]{2,1,0:T(8,128)(2,1)S(1)}, u32[]{:S(2)}, u32[]{:S(2)}) collective-permute-start(bf16[1,208,128]{2,1,0:T(8,128)(2,1)S(1)} %get-tuple-element.79), channel_id=1, source_target_pairs={{0,12},{1,13},{2,14},{3,15},{4,8},{5,9},{6,10},{7,11},{8,4},{9,5},... | collective-permute-start | bytes 159752 | tf_op jit(solution)/shard_map/ppermute | solution.py:378
  56.0 5.7 %collective-permute-start.21 = (bf16[1,208,128]{2,1,0:T(8,128)(2,1)S(1)}, bf16[1,208,128]{2,1,0:T(8,128)(2,1)S(1)}, u32[]{:S(2)}, u32[]{:S(2)}) collective-permute-start(bf16[1,208,128]{2,1,0:T(8,128)(2,1)S(1)} %get-tuple-element.76), channel_id=1, source_target_pairs={{0,8},{1,9},{2,10},{3,11},{4,12},{5,13},{6,14},{7,15},{8,0},{9,1},... | collective-permute-start | bytes 159752 | tf_op jit(solution)/shard_map/ppermute | solution.py:378
  62.2 4.2 %collective-permute-start.25 = (bf16[208,128]{1,0:T(8,128)(2,1)S(1)}, bf16[208,128]{1,0:T(8,128)(2,1)S(1)}, u32[]{:S(2)}, u32[]{:S(2)}) collective-permute-start(bf16[208,128]{1,0:T(8,128)(2,1)S(1)} %get-tuple-element.81), channel_id=1, source_target_pairs={{0,16},{16,0},{1,17},{17,1},{2,18},{18,2},{3,19},{19,3},{4,20},{20... | collective-permute-start | bytes 159752 | tf_op jit(solution)/shard_map/ppermute | solution.py:380

commit v9 on v8

--- a/solution.py
+++ b/solution.py
@@ -304,7 +304,8 @@
         mine = 0
         for b in range(bits):
             mine = mine + flags[BITS + at + b] * (1 << b)
-        for n in range(span * (2 if by_columns else 1)):
+        last = span * (2 if by_columns else 1)
+        for n in [0] + list(range(last - 1, 0, -1)):
             across, apart = n // span, n % span
             pieces = outs[: len(heights) if n else 1]
             del outs[: len(pieces)]
@@ -420,7 +421,7 @@
     for _, at, bits, by_columns, heights in plans:
         span = 1 << bits
         parts = [[pieces.pop(0)]]
-        for n in range(1, span * (2 if by_columns else 1)):
+        for n in range(span * (2 if by_columns else 1) - 1, 0, -1):
             parts.append([xor_move(pieces.pop(0), (n % span) << at, n >= span) for _ in heights])
         sums.append(parts)
     return sums, token
@@ -490,7 +491,8 @@
         flops=conv_flops // 4,
         aliases={sides + 3: CHIPS},
     )
-    came = [grads[0]] + [xor_move(grads[chip], 2 * chip, False) for chip in range(1, CHIPS)]
+    came = [xor_move(grads[chip], 2 * chip, False) for chip in range(CHIPS - 1, 0, -1)]
+    came = [grads[0]] + came[::-1]
     to_pass = vmem_call(pass_on_kernel, sds(CHIPS, depths, line, channels), came, scalars=0)
     passed = xor_move(to_pass, 1, False)
 

time: 67.9 us -> 67.2 us (0.990)
    ppermute x1, starting transfers between devices: 2.11 us -> 0.88 us  [xor_move(): return lax.ppermute(block, ('dp', 'tile'), route)]
    ppermute x1, waiting for transfers between devices: 4.27 us -> 3.3 us  [xor_move(): return lax.ppermute(block, ('dp', 'tile'), route)]
    ppermute x3, waiting for transfers between devices: 6.59 us -> 7.48 us  [xor_move(): return lax.ppermute(block, 'dp', [(0, 1), (1, 0)])]
  transfers between devices with their start and end apart: 26 -> 26, of which waited for: 14 -> 13; matrix products, arithmetic and copies ran while one was open for 0% -> 0% of each run, Pallas kernels for 16% -> 17%
where the time goes in v9:
time: 67.2 us; the launch traced here: 67 us
  starting transfers between devices  25.7 us (38%)
  waiting for transfers between devices  20.1 us (30%)
  Pallas kernels  16.1 us (24%)
  local copies, waits for them, and re-layouts  3 us (4%)
  other arithmetic  1.19 us (2%)
  between operations  0.89 us (1%)
    pallas_call x15, Pallas kernels, vmem_call(): pl.pallas_call(run, out_shape=out_shape, in_specs=specs, out_specs=jax.tr...  16.1 us
    ppermute x19, starting transfers between devices, xor_move(): return lax.ppermute(block, 'tile', [(t, t ^ apart) for t in range(tiles)])  14.2 us
    ppermute x19, waiting for transfers between devices, xor_move(): return lax.ppermute(block, 'tile', [(t, t ^ apart) for t in range(tiles)])  8.24 us
    ppermute x3, waiting for transfers between devices, xor_move(): return lax.ppermute(block, 'dp', [(0, 1), (1, 0)])  7.48 us
    ppermute x3, starting transfers between devices, swap(): return lax.ppermute(block, 'tile', tile_route(row_pairs, col_pairs, rows))  6.19 us
    ppermute x3, starting transfers between devices, xor_move(): return lax.ppermute(block, 'dp', [(0, 1), (1, 0)])  4.47 us
    ppermute x1, waiting for transfers between devices, xor_move(): return lax.ppermute(block, ('dp', 'tile'), route)  3.3 us
    unnamed x12, local copies, waits for them, and re-layouts  2.91 us
  transfers between devices with their start and end apart: 26, of which 13 were waited for; matrix products, arithmetic and copies ran while one was open for 0% of the time, Pallas kernels for 17%

profile of v9, /device:TPU:0, one launch (start us, length us, event | category | flops | bytes accessed | tf_op | source)
XLA Modules:
  0.0 67.0 jit_solution(16620084035717417885)
XLA Ops:
  0.7 1.2 %broadcast_select_fusion = (bf16[4,16,4,256]{3,2,1,0:T(4,128)(2,1)S(1)}, bf16[4,16,4,256]{3,2,1,0:T(4,128)(2,1)S(1)}) fusion(pred[]{:T(512)S(6)} %eq.27, bf16[4,16,32,256]{3,2,1,0:T(8,128)(2,1)} %refs_0_.1), kind=kLoop, calls=%fused_computation | loop fusion | flops 131072 | bytes 524289 | tf_op jit(solution)/shard_map/jit(_where)/select_n | solution.py:456
  1.9 3.1 %collective-permute-start.1 = (bf16[4,16,4,256]{3,2,1,0:T(4,128)(2,1)S(1)}, bf16[4,16,4,256]{3,2,1,0:T(4,128)(2,1)S(1)}, u32[]{:S(2)}, u32[]{:S(2)}) collective-permute-start(bf16[4,16,4,256]{3,2,1,0:T(4,128)(2,1)S(1)} %get-tuple-element.82), channel_id=1, source_target_pairs={{1,3},{3,1},{2,6},{6,2},{7,5},{5,7},{0,4},{4,0},{9,11},{11,9},{10,... | collective-permute-start | bytes 393224 | tf_op jit(solution)/shard_map/ppermute | solution.py:452
  4.9 1.2 %copy-done.3 = bf16[4,16,32,256]{3,2,1,0:T(8,128)(2,1)S(1)} copy-done((bf16[4,16,32,256]{3,2,1,0:T(8,128)(2,1)S(1)}, bf16[4,16,32,256]{3,2,1,0:T(8,128)(2,1)}, u32[]{:S(2)}) %copy-start.3) | copy-done | bytes 1048600
  6.2 0.5 shard_map.68.refs_1_
  6.7 0.1 stack.71.refs_0_
  6.8 1.1 %collective-permute-done.1.refs_3_ = bf16[4,16,4,256]{3,2,1,0:T(4,128)(2,1)S(1)} collective-permute-done((bf16[4,16,4,256]{3,2,1,0:T(4,128)(2,1)S(1)}, bf16[4,16,4,256]{3,2,1,0:T(4,128)(2,1)S(1)}, u32[]{:S(2)}, u32[]{:S(2)}) %collective-permute-start.1) | collective-permute-done | bytes 131104 | tf_op jit(solution)/shard_map/ppermute | solution.py:452
  7.9 0.8 %shard_map.69 = (bf16[144,256]{1,0:T(8,128)(2,1)S(1)}, f32[4,6,16,256]{3,2,1,0:T(8,128)S(1)}, f32[4,6,2,256]{3,2,1,0:T(2,128)S(1)}) custom-call(s32[13]{0:T(128)S(1)} %stack.71.refs_0_, f32[4,16,24,256]{3,2,1,0:T(8,128)S(1)} %shard_map.68.refs_1_, bf16[4,16,4,256]{3,2,1,0:T(4,128)(2,1)S(1)} %collective-permute-done.refs_2_, ...), custom_call_target="tpu_custom_call" | custom-call | bytes 2351156 | tf_op jit(solution)/shard_map/pallas_call | solution.py:360
  8.7 3.1 %collective-permute-start.2 = (bf16[144,256]{1,0:T(8,128)(2,1)S(1)}, bf16[144,256]{1,0:T(8,128)(2,1)S(1)}, u32[]{:S(2)}, u32[]{:S(2)}) collective-permute-start(bf16[144,256]{1,0:T(8,128)(2,1)S(1)} %get-tuple-element.42.refs_5_), channel_id=1, source_target_pairs={{0,8},{1,9},{3,11},{2,10},{6,14},{7,15},{5,13},{4,12},{8,0},{9,1},... | collective-permute-start | bytes 221192 | tf_op jit(solution)/shard_map/ppermute | solution.py:452
  11.8 1.7 %copy-done = bf16[2,3,3,256,256]{4,3,2,1,0:T(8,128)(2,1)S(1)} copy-done((bf16[2,3,3,256,256]{4,3,2,1,0:T(8,128)(2,1)S(1)}, bf16[2,3,3,256,256]{4,3,2,1,0:T(8,128)(2,1)}, u32[]{:S(2)}) %copy-start) | copy-done | bytes 2359320
  13.4 2.4 %shard_map.70 = (bf16[3,640,256]{2,1,0:T(8,128)(2,1)S(1)}, f32[2,512,256]{2,1,0:T(8,128)S(1)}) custom-call(s32[13]{0:T(128)S(1)} %stack.71.refs_0_, f32[4,16,24,256]{3,2,1,0:T(8,128)S(1)} %shard_map.68.refs_1_, bf16[4,16,4,256]{3,2,1,0:T(4,128)(2,1)S(1)} %collective-permute-done.refs_2_, bf16[4,16,4,256]{3,2,1,0:T(4,128)(2,1)S(1)} %collective-permute-done.1.refs_3_, ...), custom_call_target="tpu_custom_call" | custom-call | flops 1207959552 | bytes 6225972 | tf_op jit(solution)/shard_map/pallas_call | solution.py:360
  15.8 0.0 collective-permute-done.2.refs_1_
  15.8 0.0 copy-start.5
  15.9 1.6 %shard_map.71 = (bf16[2,2,64,256]{3,2,1,0:T(8,128)(2,1)S(1)}, bf16[2,2,64,256]{3,2,1,0:T(8,128)(2,1)S(1)}, bf16[2,2,64,256]{3,2,1,0:T(8,128)(2,1)S(1)}, bf16[2,2...) custom-call(s32[13]{0:T(128)S(1)} %stack.71.refs_0_, ...), custom_call_target="tpu_custom_call", output_to_operand_aliasing={{4}: (4, {})} | custom-call | flops 301989888 | bytes 6414388 | tf_op jit(solution)/shard_map/pallas_call | solution.py:360
  17.5 1.6 %collective-permute-start.3 = (bf16[2,2,64,256]{3,2,1,0:T(8,128)(2,1)S(1)}, bf16[2,2,64,256]{3,2,1,0:T(8,128)(2,1)S(1)}, u32[]{:S(2)}, u32[]{:S(2)}) collective-permute-start(bf16[2,2,64,256]{3,2,1,0:T(8,128)(2,1)S(1)} %get-tuple-element.48), channel_id=1, source_target_pairs={{0,2},{1,3},{2,0},{3,1},{4,6},{5,7},{6,4},{7,5},{8,10},{9,11},{10,... | collective-permute-start | bytes 393224 | tf_op jit(solution)/shard_map/ppermute | solution.py:379
  19.1 1.6 %collective-permute-start.4 = (bf16[2,2,64,256]{3,2,1,0:T(8,128)(2,1)S(1)}, bf16[2,2,64,256]{3,2,1,0:T(8,128)(2,1)S(1)}, u32[]{:S(2)}, u32[]{:S(2)}) collective-permute-start(bf16[2,2,64,256]{3,2,1,0:T(8,128)(2,1)S(1)} %get-tuple-element.49), channel_id=1, source_target_pairs={{0,4},{1,5},{2,6},{3,7},{4,0},{5,1},{6,2},{7,3},{8,12},{9,13},{10,... | collective-permute-start | bytes 393224 | tf_op jit(solution)/shard_map/ppermute | solution.py:379
  20.7 0.4 collective-permute-start.5
  21.1 2.1 %shard_map.73 = (bf16[8,208,256]{2,1,0:T(8,128)(2,1)S(1)}, bf16[2,208,256]{2,1,0:T(8,128)(2,1)S(1)}, bf16[2,208,256]{2,1,0:T(8,128)(2,1)S(1)}, bf16[2,208,256]{2...) custom-call(s32[13]{0:T(128)S(1)} %stack.71.refs_0_, ...), custom_call_target="tpu_custom_call" | custom-call | flops 1207959552 | bytes 3866676 | tf_op jit(solution)/shard_map/pallas_call | solution.py:360
  23.1 0.0 copy-start.2
  23.2 0.1 collective-permute-start.7
  23.2 0.5 collective-permute-start.8
  23.7 0.1 collective-permute-start.9
  23.8 0.5 collective-permute-done.4.refs_2_.refs_3_
  24.4 0.0 collective-permute-start.10
  24.4 2.2 %collective-permute-done.5.refs_3_.refs_4_ = bf16[2,2,64,256]{3,2,1,0:T(8,128)(2,1)S(1)} collective-permute-done((bf16[2,2,64,256]{3,2,1,0:T(8,128)(2,1)S(1)}, bf16[2,2,64,256]{3,2,1,0:T(8,128)(2,1)S(1)}, u32[]{:S(2)}, u32[]{:S(2)}) %collective-permute-start.5) | collective-permute-done | bytes 131104 | tf_op jit(solution)/shard_map/ppermute | solution.py:379
  26.5 0.1 collective-permute-start.6
  26.6 0.0 collective-permute-done.7.refs_2_
  26.6 0.0 collective-permute-done.9.refs_4_
  26.7 0.0 collective-permute-done.10.refs_5_
  26.7 0.7 %shard_map.74 = (f32[8,208,128]{2,1,0:T(8,128)S(1)}, bf16[8,208,128]{2,1,0:T(8,128)(2,1)S(1)}) custom-call(s32[13]{0:T(128)S(1)} %stack.71.refs_0_, bf16[8,208,256]{2,1,0:T(8,128)(2,1)S(1)} %get-tuple-element.53.refs_1_, bf16[2,208,256]{2,1,0:T(8,128)(2,1)S(1)} %collective-permute-done.7.refs_2_, bf16[2,208,256]{2,1,0:T(8,128)(2,1)S(1)} %collective-permute-done.8.refs_3_, ...), custom_call_target="tpu_custom_call" | custom-call | bytes 2981940 | tf_op jit(solution)/shard_map/pallas_call | solution.py:360
  27.4 1.6 %collective-permute-start.18 = (bf16[8,208,128]{2,1,0:T(8,128)(2,1)S(1)}, bf16[8,208,128]{2,1,0:T(8,128)(2,1)S(1)}, u32[]{:S(2)}, u32[]{:S(2)}) collective-permute-start(bf16[8,208,128]{2,1,0:T(8,128)(2,1)S(1)} %get-tuple-element.69), channel_id=1, source_target_pairs={{0,16},{16,0},{1,17},{17,1},{2,18},{18,2},{3,19},{19,3},{4,20},{20... | collective-permute-start | bytes 1277960 | tf_op jit(solution)/shard_map/ppermute | solution.py:381
  29.0 1.5 %shard_map.75 = (bf16[8,208,256]{2,1,0:T(8,128)(2,1)S(1)}, bf16[2,208,256]{2,1,0:T(8,128)(2,1)S(1)}, bf16[2,208,256]{2,1,0:T(8,128)(2,1)S(1)}, bf16[2,208,256]{2...) custom-call(s32[13]{0:T(128)S(1)} %stack.71.refs_0_, ...), custom_call_target="tpu_custom_call" | custom-call | flops 536870912 | bytes 5767220 | tf_op jit(solution)/shard_map/pallas_call | solution.py:360
  30.5 0.3 collective-permute-start.11
  30.7 0.3 collective-permute-start.12
  31.0 0.2 collective-permute-start.13
  31.2 0.3 collective-permute-start.14
  31.5 0.4 collective-permute-done.11.refs_2_
  32.0 0.3 collective-permute-done.12.refs_3_
  32.3 0.3 collective-permute-done.13.refs_4_
  32.6 0.3 collective-permute-done.14.refs_5_
  32.9 0.7 %shard_map.76 = (f32[4,208,128]{2,1,0:T(8,128)S(1)}, bf16[4,208,128]{2,1,0:T(8,128)(2,1)S(1)}, bf16[4,208,128]{2,1,0:T(8,128)(2,1)S(1)}, bf16[4,208,128]{2,1,0:T(8,128)(2,1)S(1)}) custom-call(s32[13]{0:T(128)S(1)} %stack.71.refs_0_, bf16[8,208,256]{2,1,0:T(8,128)(2,1)S(1)} %get-tuple-element.60.refs_1_, ...), custom_call_target="tpu_custom_call" | custom-call | bytes 2768948 | tf_op jit(solution)/shard_map/pallas_call | solution.py:360
  33.6 0.9 %collective-permute-start.15 = (bf16[4,208,128]{2,1,0:T(8,128)(2,1)S(1)}, bf16[4,208,128]{2,1,0:T(8,128)(2,1)S(1)}, u32[]{:S(2)}, u32[]{:S(2)}) collective-permute-start(bf16[4,208,128]{2,1,0:T(8,128)(2,1)S(1)} %get-tuple-element.66), channel_id=1, source_target_pairs={{0,18},{1,19},{2,16},{3,17},{4,22},{5,23},{6,20},{7,21},{8,26},{9,... | collective-permute-start | bytes 638984 | tf_op jit(solution)/shard_map/ppermute | solution.py:383
  34.5 1.3 %collective-permute-start.16 = (bf16[4,208,128]{2,1,0:T(8,128)(2,1)S(1)}, bf16[4,208,128]{2,1,0:T(8,128)(2,1)S(1)}, u32[]{:S(2)}, u32[]{:S(2)}) collective-permute-start(bf16[4,208,128]{2,1,0:T(8,128)(2,1)S(1)} %get-tuple-element.67), channel_id=1, source_target_pairs={{0,16},{16,0},{1,17},{17,1},{2,18},{18,2},{3,19},{19,3},{4,20},{20... | collective-permute-start | bytes 638984 | tf_op jit(solution)/shard_map/ppermute | solution.py:381
  35.9 1.3 %collective-permute-start.17 = (bf16[4,208,128]{2,1,0:T(8,128)(2,1)S(1)}, bf16[4,208,128]{2,1,0:T(8,128)(2,1)S(1)}, u32[]{:S(2)}, u32[]{:S(2)}) collective-permute-start(bf16[4,208,128]{2,1,0:T(8,128)(2,1)S(1)} %get-tuple-element.68), channel_id=1, source_target_pairs={{0,2},{1,3},{2,0},{3,1},{4,6},{5,7},{6,4},{7,5},{8,10},{9,11},{10,... | collective-permute-start | bytes 638984 | tf_op jit(solution)/shard_map/ppermute | solution.py:379
  37.2 2.9 %collective-permute-done.18.refs_2_ = bf16[8,208,128]{2,1,0:T(8,128)(2,1)S(1)} collective-permute-done((bf16[8,208,128]{2,1,0:T(8,128)(2,1)S(1)}, bf16[8,208,128]{2,1,0:T(8,128)(2,1)S(1)}, u32[]{:S(2)}, u32[]{:S(2)}) %collective-permute-start.18) | collective-permute-done | bytes 426016 | tf_op jit(solution)/shard_map/ppermute | solution.py:381
  40.1 0.6 shard_map.77
  40.7 0.8 %collective-permute-start.19 = (bf16[4,208,128]{2,1,0:T(8,128)(2,1)S(1)}, bf16[4,208,128]{2,1,0:T(8,128)(2,1)S(1)}, u32[]{:S(2)}, u32[]{:S(2)}) collective-permute-start(bf16[4,208,128]{2,1,0:T(8,128)(2,1)S(1)} %get-tuple-element.71), channel_id=1, source_target_pairs={{0,4},{1,5},{2,6},{3,7},{4,0},{5,1},{6,2},{7,3},{8,12},{9,13},{10,... | collective-permute-start | bytes 638984 | tf_op jit(solution)/shard_map/ppermute | solution.py:379
  41.5 3.3 %collective-permute-done.15.refs_2_ = bf16[4,208,128]{2,1,0:T(8,128)(2,1)S(1)} collective-permute-done((bf16[4,208,128]{2,1,0:T(8,128)(2,1)S(1)}, bf16[4,208,128]{2,1,0:T(8,128)(2,1)S(1)}, u32[]{:S(2)}, u32[]{:S(2)}) %collective-permute-start.15) | collective-permute-done | bytes 213024 | tf_op jit(solution)/shard_map/ppermute | solution.py:383
  44.8 4.0 %collective-permute-done.16.refs_3_ = bf16[4,208,128]{2,1,0:T(8,128)(2,1)S(1)} collective-permute-done((bf16[4,208,128]{2,1,0:T(8,128)(2,1)S(1)}, bf16[4,208,128]{2,1,0:T(8,128)(2,1)S(1)}, u32[]{:S(2)}, u32[]{:S(2)}) %collective-permute-start.16) | collective-permute-done | bytes 213024 | tf_op jit(solution)/shard_map/ppermute | solution.py:381
  48.8 0.0 collective-permute-done.17.refs_4_
  48.9 0.0 collective-permute-done.19.refs_6_
  48.9 0.7 %shard_map.78 = (f32[1,208,128]{2,1,0:T(8,128)S(1)}, bf16[1,208,128]{2,1,0:T(8,128)(2,1)S(1)}, bf16[1,208,128]{2,1,0:T(8,128)(2,1)S(1)}, bf16[1,208,128]{2,1,0:T...) custom-call(s32[13]{0:T(128)S(1)} %stack.71.refs_0_, ...), custom_call_target="tpu_custom_call" | custom-call | bytes 2289716 | tf_op jit(solution)/shard_map/pallas_call | solution.py:360
  49.5 0.8 %collective-permute-start.20 = (bf16[2,208,128]{2,1,0:T(8,128)(2,1)S(1)}, bf16[2,208,128]{2,1,0:T(8,128)(2,1)S(1)}, u32[]{:S(2)}, u32[]{:S(2)}) collective-permute-start(bf16[2,208,128]{2,1,0:T(8,128)(2,1)S(1)} %get-tuple-element.73), channel_id=1, source_target_pairs={{0,2},{1,3},{2,0},{3,1},{4,6},{5,7},{6,4},{7,5},{8,10},{9,11},{10,... | collective-permute-start | bytes 319496 | tf_op jit(solution)/shard_map/ppermute | solution.py:379
  50.3 2.5 %collective-permute-start.22 = (bf16[1,208,128]{2,1,0:T(8,128)(2,1)S(1)}, bf16[1,208,128]{2,1,0:T(8,128)(2,1)S(1)}, u32[]{:S(2)}, u32[]{:S(2)}) collective-permute-start(bf16[1,208,128]{2,1,0:T(8,128)(2,1)S(1)} %get-tuple-element.77), channel_id=1, source_target_pairs={{0,12},{1,13},{2,14},{3,15},{4,8},{5,9},{6,10},{7,11},{8,4},{9,5},... | collective-permute-start | bytes 159752 | tf_op jit(solution)/shard_map/ppermute | solution.py:379
  52.8 0.5 collective-permute-start.23
  53.3 1.3 %collective-permute-start.24 = (bf16[1,208,128]{2,1,0:T(8,128)(2,1)S(1)}, bf16[1,208,128]{2,1,0:T(8,128)(2,1)S(1)}, u32[]{:S(2)}, u32[]{:S(2)}) collective-permute-start(bf16[1,208,128]{2,1,0:T(8,128)(2,1)S(1)} %get-tuple-element.79), channel_id=1, source_target_pairs={{0,4},{1,5},{2,6},{3,7},{4,0},{5,1},{6,2},{7,3},{8,12},{9,13},{10,... | collective-permute-start | bytes 159752 | tf_op jit(solution)/shard_map/ppermute | solution.py:379
  54.7 0.6 shard_map.79
  55.3 1.5 %collective-permute-start.21 = (bf16[1,208,128]{2,1,0:T(8,128)(2,1)S(1)}, bf16[1,208,128]{2,1,0:T(8,128)(2,1)S(1)}, u32[]{:S(2)}, u32[]{:S(2)}) collective-permute-start(bf16[1,208,128]{2,1,0:T(8,128)(2,1)S(1)} %get-tuple-element.76), channel_id=1, source_target_pairs={{0,8},{1,9},{2,10},{3,11},{4,12},{5,13},{6,14},{7,15},{8,0},{9,1},... | collective-permute-start | bytes 159752 | tf_op jit(solution)/shard_map/ppermute | solution.py:379
  56.8 2.3 %collective-permute-done.23.refs_5_ = bf16[1,208,128]{2,1,0:T(8,128)(2,1)S(1)} collective-permute-done((bf16[1,208,128]{2,1,0:T(8,128)(2,1)S(1)}, bf16[1,208,128]{2,1,0:T(8,128)(2,1)S(1)}, u32[]{:S(2)}, u32[]{:S(2)}) %collective-permute-start.23) | collective-permute-done | bytes 53280 | tf_op jit(solution)/shard_map/ppermute | solution.py:379
  59.1 1.9 %collective-permute-done.21.refs_2_ = bf16[1,208,128]{2,1,0:T(8,128)(2,1)S(1)} collective-permute-done((bf16[1,208,128]{2,1,0:T(8,128)(2,1)S(1)}, bf16[1,208,128]{2,1,0:T(8,128)(2,1)S(1)}, u32[]{:S(2)}, u32[]{:S(2)}) %collective-permute-start.21) | collective-permute-done | bytes 53280 | tf_op jit(solution)/shard_map/ppermute | solution.py:379
  60.9 0.6 shard_map.81
  61.5 1.6 %collective-permute-start.25 = (bf16[208,128]{1,0:T(8,128)(2,1)S(1)}, bf16[208,128]{1,0:T(8,128)(2,1)S(1)}, u32[]{:S(2)}, u32[]{:S(2)}) collective-permute-start(bf16[208,128]{1,0:T(8,128)(2,1)S(1)} %get-tuple-element.81), channel_id=1, source_target_pairs={{0,16},{16,0},{1,17},{17,1},{2,18},{18,2},{3,19},{19,3},{4,20},{20... | collective-permute-start | bytes 159752 | tf_op jit(solution)/shard_map/ppermute | solution.py:381
  63.1 2.1 %shard_map.80 = bf16[4,2,128,1024]{3,2,1,0:T(8,128)(2,1)} custom-call(bf16[2,512,256]{2,1,0:T(8,128)(2,1)S(1)} %get-tuple-element.59.refs_6_.refs_0_, bf16[2,1024,256]{2,1,0:T(8,128)(2,1)S(1)} %copy-done.4, f32[1,208,128]{2,1,0:T(8,128)S(1)} %get-tuple-element.75.refs_2_.refs_1_), custom_call_target="tpu_custom_call" | custom-call | flops 536870912 | bytes 3670016 | tf_op jit(solution)/shard_map/pallas_call | solution.py:360
  65.2 0.6 collective-permute-done.25.refs_2_
  65.7 1.2 %shard_map.82 = f32[208,256]{1,0:T(8,128)} custom-call(s32[13]{0:T(128)S(1)} %stack.71.refs_0_, f32[208,128]{1,0:T(8,128)S(1)} %get-tuple-element.80.refs_1_, bf16[208,128]{1,0:T(8,128)(2,1)S(1)} %collective-permute-done.25.refs_2_), custom_call_target="tpu_custom_call" | custom-call | bytes 372788 | tf_op jit(solution)/shard_map/pallas_call | solution.py:360
  (17 shorter events, 0.1 us)
Async XLA Ops:
  1.9 6.0 %collective-permute-start.1 = (bf16[4,16,4,256]{3,2,1,0:T(4,128)(2,1)S(1)}, bf16[4,16,4,256]{3,2,1,0:T(4,128)(2,1)S(1)}, u32[]{:S(2)}, u32[]{:S(2)}) collective-permute-start(bf16[4,16,4,256]{3,2,1,0:T(4,128)(2,1)S(1)} %get-tuple-element.82), channel_id=1, source_target_pairs={{1,3},{3,1},{2,6},{6,2},{7,5},{5,7},{0,4},{4,0},{9,11},{11,9},{10,... | collective-permute-start | bytes 393224 | tf_op jit(solution)/shard_map/ppermute | solution.py:452
  4.9 3.0 %collective-permute-start = (bf16[4,16,4,256]{3,2,1,0:T(4,128)(2,1)S(1)}, bf16[4,16,4,256]{3,2,1,0:T(4,128)(2,1)S(1)}, u32[]{:S(2)}, u32[]{:S(2)}) collective-permute-start(bf16[4,16,4,256]{3,2,1,0:T(4,128)(2,1)S(1)} %get-tuple-element.83), channel_id=1, source_target_pairs={{0,1},{1,0},{3,2},{2,3},{6,7},{7,6},{5,4},{4,5},{8,9},{9,8},{11,10... | collective-permute-start | bytes 393224 | tf_op jit(solution)/shard_map/ppermute | solution.py:452
  4.9 1.2 %copy-start.3 = (bf16[4,16,32,256]{3,2,1,0:T(8,128)(2,1)S(1)}, bf16[4,16,32,256]{3,2,1,0:T(8,128)(2,1)}, u32[]{:S(2)}) copy-start(bf16[4,16,32,256]{3,2,1,0:T(8,128)(2,1)} %refs_0_.1) | copy-start | bytes 3145732
  8.7 7.2 %collective-permute-start.2 = (bf16[144,256]{1,0:T(8,128)(2,1)S(1)}, bf16[144,256]{1,0:T(8,128)(2,1)S(1)}, u32[]{:S(2)}, u32[]{:S(2)}) collective-permute-start(bf16[144,256]{1,0:T(8,128)(2,1)S(1)} %get-tuple-element.42.refs_5_), channel_id=1, source_target_pairs={{0,8},{1,9},{3,11},{2,10},{6,14},{7,15},{5,13},{4,12},{8,0},{9,1},... | collective-permute-start | bytes 221192 | tf_op jit(solution)/shard_map/ppermute | solution.py:452
  11.8 1.7 %copy-start = (bf16[2,3,3,256,256]{4,3,2,1,0:T(8,128)(2,1)S(1)}, bf16[2,3,3,256,256]{4,3,2,1,0:T(8,128)(2,1)}, u32[]{:S(2)}) copy-start(bf16[2,3,3,256,256]{4,3,2,1,0:T(8,128)(2,1)} %refs_6_.2) | copy-start | bytes 7077892
  13.4 2.4 %copy-start.1 = (bf16[2,3,3,256,256]{4,3,2,1,0:T(8,128)(2,1)S(1)}, bf16[2,3,3,256,256]{4,3,2,1,0:T(8,128)(2,1)}, u32[]{:S(2)}) copy-start(bf16[2,3,3,256,256]{4,3,2,1,0:T(8,128)(2,1)} %refs_6_.2) | copy-start | bytes 7077892
  15.8 5.2 %copy-start.5 = (bf16[4,2,8,16,256]{4,3,2,1,0:T(8,128)(2,1)S(1)}, bf16[4,2,8,16,256]{4,3,2,1,0:T(8,128)(2,1)}, u32[]{:S(2)}) copy-start(bf16[4,2,8,16,256]{4,3,2,1,0:T(8,128)(2,1)} %refs_2_.1) | copy-start | bytes 1572868
  17.5 6.2 %collective-permute-start.3 = (bf16[2,2,64,256]{3,2,1,0:T(8,128)(2,1)S(1)}, bf16[2,2,64,256]{3,2,1,0:T(8,128)(2,1)S(1)}, u32[]{:S(2)}, u32[]{:S(2)}) collective-permute-start(bf16[2,2,64,256]{3,2,1,0:T(8,128)(2,1)S(1)} %get-tuple-element.48), channel_id=1, source_target_pairs={{0,2},{1,3},{2,0},{3,1},{4,6},{5,7},{6,4},{7,5},{8,10},{9,11},{10,... | collective-permute-start | bytes 393224 | tf_op jit(solution)/shard_map/ppermute | solution.py:379
  19.1 5.3 %collective-permute-start.4 = (bf16[2,2,64,256]{3,2,1,0:T(8,128)(2,1)S(1)}, bf16[2,2,64,256]{3,2,1,0:T(8,128)(2,1)S(1)}, u32[]{:S(2)}, u32[]{:S(2)}) collective-permute-start(bf16[2,2,64,256]{3,2,1,0:T(8,128)(2,1)S(1)} %get-tuple-element.49), channel_id=1, source_target_pairs={{0,4},{1,5},{2,6},{3,7},{4,0},{5,1},{6,2},{7,3},{8,12},{9,13},{10,... | collective-permute-start | bytes 393224 | tf_op jit(solution)/shard_map/ppermute | solution.py:379
  20.7 5.9 %collective-permute-start.5 = (bf16[2,2,64,256]{3,2,1,0:T(8,128)(2,1)S(1)}, bf16[2,2,64,256]{3,2,1,0:T(8,128)(2,1)S(1)}, u32[]{:S(2)}, u32[]{:S(2)}) collective-permute-start(bf16[2,2,64,256]{3,2,1,0:T(8,128)(2,1)S(1)} %get-tuple-element.50), channel_id=1, source_target_pairs={{0,6},{1,7},{2,4},{3,5},{4,2},{5,3},{6,0},{7,1},{8,14},{9,15},{10,... | collective-permute-start | bytes 393224 | tf_op jit(solution)/shard_map/ppermute | solution.py:379
  23.1 5.8 %copy-start.2 = (bf16[4,2,128,1024]{3,2,1,0:T(8,128)(2,1)S(1)}, bf16[4,2,128,1024]{3,2,1,0:T(8,128)(2,1)}, u32[]{:S(2)}) copy-start(bf16[4,2,128,1024]{3,2,1,0:T(8,128)(2,1)} %refs_6_.3) | copy-start | bytes 6291460
  23.2 3.5 %collective-permute-start.7 = (bf16[2,208,256]{2,1,0:T(8,128)(2,1)S(1)}, bf16[2,208,256]{2,1,0:T(8,128)(2,1)S(1)}, u32[]{:S(2)}, u32[]{:S(2)}) collective-permute-start(bf16[2,208,256]{2,1,0:T(8,128)(2,1)S(1)} %get-tuple-element.54), channel_id=1, source_target_pairs={{0,1},{1,0},{2,3},{3,2},{4,5},{5,4},{6,7},{7,6},{8,9},{9,8},{10,11... | collective-permute-start | bytes 638984 | tf_op jit(solution)/shard_map/ppermute | solution.py:379
  23.2 3.4 %collective-permute-start.8 = (bf16[2,208,256]{2,1,0:T(8,128)(2,1)S(1)}, bf16[2,208,256]{2,1,0:T(8,128)(2,1)S(1)}, u32[]{:S(2)}, u32[]{:S(2)}) collective-permute-start(bf16[2,208,256]{2,1,0:T(8,128)(2,1)S(1)} %get-tuple-element.55), channel_id=1, source_target_pairs={{0,1},{1,0},{2,3},{3,2},{4,5},{5,4},{6,7},{7,6},{8,9},{9,8},{10,11... | collective-permute-start | bytes 638984 | tf_op jit(solution)/shard_map/ppermute | solution.py:379
  23.7 2.9 %collective-permute-start.9 = (bf16[2,208,256]{2,1,0:T(8,128)(2,1)S(1)}, bf16[2,208,256]{2,1,0:T(8,128)(2,1)S(1)}, u32[]{:S(2)}, u32[]{:S(2)}) collective-permute-start(bf16[2,208,256]{2,1,0:T(8,128)(2,1)S(1)} %get-tuple-element.56), channel_id=1, source_target_pairs={{0,1},{1,0},{2,3},{3,2},{4,5},{5,4},{6,7},{7,6},{8,9},{9,8},{10,11... | collective-permute-start | bytes 638984 | tf_op jit(solution)/shard_map/ppermute | solution.py:379
  24.4 2.3 %collective-permute-start.10 = (bf16[2,208,256]{2,1,0:T(8,128)(2,1)S(1)}, bf16[2,208,256]{2,1,0:T(8,128)(2,1)S(1)}, u32[]{:S(2)}, u32[]{:S(2)}) collective-permute-start(bf16[2,208,256]{2,1,0:T(8,128)(2,1)S(1)} %get-tuple-element.57), channel_id=1, source_target_pairs={{0,1},{1,0},{2,3},{3,2},{4,5},{5,4},{6,7},{7,6},{8,9},{9,8},{10,11... | collective-permute-start | bytes 638984 | tf_op jit(solution)/shard_map/ppermute | solution.py:379
  26.5 2.4 %collective-permute-start.6 = (bf16[4,2,64,256]{3,2,1,0:T(8,128)(2,1)S(1)}, bf16[4,2,64,256]{3,2,1,0:T(8,128)(2,1)S(1)}, u32[]{:S(2)}, u32[]{:S(2)}) collective-permute-start(bf16[4,2,64,256]{3,2,1,0:T(8,128)(2,1)S(1)} %shard_map.72), channel_id=1, source_target_pairs={{0,1},{1,0},{2,3},{3,2},{4,5},{5,4},{6,7},{7,6},{8,9},{9,8},{10,11... | collective-permute-start | bytes 786440 | tf_op jit(solution)/shard_map/ppermute | solution.py:379
  27.4 12.7 %collective-permute-start.18 = (bf16[8,208,128]{2,1,0:T(8,128)(2,1)S(1)}, bf16[8,208,128]{2,1,0:T(8,128)(2,1)S(1)}, u32[]{:S(2)}, u32[]{:S(2)}) collective-permute-start(bf16[8,208,128]{2,1,0:T(8,128)(2,1)S(1)} %get-tuple-element.69), channel_id=1, source_target_pairs={{0,16},{16,0},{1,17},{17,1},{2,18},{18,2},{3,19},{19,3},{4,20},{20... | collective-permute-start | bytes 1277960 | tf_op jit(solution)/shard_map/ppermute | solution.py:381
  30.5 1.5 %collective-permute-start.11 = (bf16[2,208,256]{2,1,0:T(8,128)(2,1)S(1)}, bf16[2,208,256]{2,1,0:T(8,128)(2,1)S(1)}, u32[]{:S(2)}, u32[]{:S(2)}) collective-permute-start(bf16[2,208,256]{2,1,0:T(8,128)(2,1)S(1)} %get-tuple-element.61), channel_id=1, source_target_pairs={{0,1},{1,0},{2,3},{3,2},{4,5},{5,4},{6,7},{7,6},{8,9},{9,8},{10,11... | collective-permute-start | bytes 638984 | tf_op jit(solution)/shard_map/ppermute | solution.py:379
  30.7 1.6 %collective-permute-start.12 = (bf16[2,208,256]{2,1,0:T(8,128)(2,1)S(1)}, bf16[2,208,256]{2,1,0:T(8,128)(2,1)S(1)}, u32[]{:S(2)}, u32[]{:S(2)}) collective-permute-start(bf16[2,208,256]{2,1,0:T(8,128)(2,1)S(1)} %get-tuple-element.62), channel_id=1, source_target_pairs={{0,1},{1,0},{2,3},{3,2},{4,5},{5,4},{6,7},{7,6},{8,9},{9,8},{10,11... | collective-permute-start | bytes 638984 | tf_op jit(solution)/shard_map/ppermute | solution.py:379
  31.0 1.6 %collective-permute-start.13 = (bf16[2,208,256]{2,1,0:T(8,128)(2,1)S(1)}, bf16[2,208,256]{2,1,0:T(8,128)(2,1)S(1)}, u32[]{:S(2)}, u32[]{:S(2)}) collective-permute-start(bf16[2,208,256]{2,1,0:T(8,128)(2,1)S(1)} %get-tuple-element.63), channel_id=1, source_target_pairs={{0,1},{1,0},{2,3},{3,2},{4,5},{5,4},{6,7},{7,6},{8,9},{9,8},{10,11... | collective-permute-start | bytes 638984 | tf_op jit(solution)/shard_map/ppermute | solution.py:379
  31.2 1.7 %collective-permute-start.14 = (bf16[2,208,256]{2,1,0:T(8,128)(2,1)S(1)}, bf16[2,208,256]{2,1,0:T(8,128)(2,1)S(1)}, u32[]{:S(2)}, u32[]{:S(2)}) collective-permute-start(bf16[2,208,256]{2,1,0:T(8,128)(2,1)S(1)} %get-tuple-element.64), channel_id=1, source_target_pairs={{0,1},{1,0},{2,3},{3,2},{4,5},{5,4},{6,7},{7,6},{8,9},{9,8},{10,11... | collective-permute-start | bytes 638984 | tf_op jit(solution)/shard_map/ppermute | solution.py:379
  33.6 11.2 %collective-permute-start.15 = (bf16[4,208,128]{2,1,0:T(8,128)(2,1)S(1)}, bf16[4,208,128]{2,1,0:T(8,128)(2,1)S(1)}, u32[]{:S(2)}, u32[]{:S(2)}) collective-permute-start(bf16[4,208,128]{2,1,0:T(8,128)(2,1)S(1)} %get-tuple-element.66), channel_id=1, source_target_pairs={{0,18},{1,19},{2,16},{3,17},{4,22},{5,23},{6,20},{7,21},{8,26},{9,... | collective-permute-start | bytes 638984 | tf_op jit(solution)/shard_map/ppermute | solution.py:383
  34.5 14.3 %collective-permute-start.16 = (bf16[4,208,128]{2,1,0:T(8,128)(2,1)S(1)}, bf16[4,208,128]{2,1,0:T(8,128)(2,1)S(1)}, u32[]{:S(2)}, u32[]{:S(2)}) collective-permute-start(bf16[4,208,128]{2,1,0:T(8,128)(2,1)S(1)} %get-tuple-element.67), channel_id=1, source_target_pairs={{0,16},{16,0},{1,17},{17,1},{2,18},{18,2},{3,19},{19,3},{4,20},{20... | collective-permute-start | bytes 638984 | tf_op jit(solution)/shard_map/ppermute | solution.py:381
  35.9 13.0 %collective-permute-start.17 = (bf16[4,208,128]{2,1,0:T(8,128)(2,1)S(1)}, bf16[4,208,128]{2,1,0:T(8,128)(2,1)S(1)}, u32[]{:S(2)}, u32[]{:S(2)}) collective-permute-start(bf16[4,208,128]{2,1,0:T(8,128)(2,1)S(1)} %get-tuple-element.68), channel_id=1, source_target_pairs={{0,2},{1,3},{2,0},{3,1},{4,6},{5,7},{6,4},{7,5},{8,10},{9,11},{10,... | collective-permute-start | bytes 638984 | tf_op jit(solution)/shard_map/ppermute | solution.py:379
  40.1 23.0 %copy-start.4 = (bf16[2,1024,256]{2,1,0:T(8,128)(2,1)S(1)}, bf16[2,1024,256]{2,1,0:T(8,128)(2,1)}, u32[]{:S(2)}) copy-start(bf16[2,1024,256]{2,1,0:T(8,128)(2,1)} %refs_1_.1) | copy-start | bytes 3145732
  40.7 8.1 %collective-permute-start.19 = (bf16[4,208,128]{2,1,0:T(8,128)(2,1)S(1)}, bf16[4,208,128]{2,1,0:T(8,128)(2,1)S(1)}, u32[]{:S(2)}, u32[]{:S(2)}) collective-permute-start(bf16[4,208,128]{2,1,0:T(8,128)(2,1)S(1)} %get-tuple-element.71), channel_id=1, source_target_pairs={{0,4},{1,5},{2,6},{3,7},{4,0},{5,1},{6,2},{7,3},{8,12},{9,13},{10,... | collective-permute-start | bytes 638984 | tf_op jit(solution)/shard_map/ppermute | solution.py:379
  49.5 5.1 %collective-permute-start.20 = (bf16[2,208,128]{2,1,0:T(8,128)(2,1)S(1)}, bf16[2,208,128]{2,1,0:T(8,128)(2,1)S(1)}, u32[]{:S(2)}, u32[]{:S(2)}) collective-permute-start(bf16[2,208,128]{2,1,0:T(8,128)(2,1)S(1)} %get-tuple-element.73), channel_id=1, source_target_pairs={{0,2},{1,3},{2,0},{3,1},{4,6},{5,7},{6,4},{7,5},{8,10},{9,11},{10,... | collective-permute-start | bytes 319496 | tf_op jit(solution)/shard_map/ppermute | solution.py:379
  50.3 6.5 %collective-permute-start.22 = (bf16[1,208,128]{2,1,0:T(8,128)(2,1)S(1)}, bf16[1,208,128]{2,1,0:T(8,128)(2,1)S(1)}, u32[]{:S(2)}, u32[]{:S(2)}) collective-permute-start(bf16[1,208,128]{2,1,0:T(8,128)(2,1)S(1)} %get-tuple-element.77), channel_id=1, source_target_pairs={{0,12},{1,13},{2,14},{3,15},{4,8},{5,9},{6,10},{7,11},{8,4},{9,5},... | collective-permute-start | bytes 159752 | tf_op jit(solution)/shard_map/ppermute | solution.py:379
  52.8 6.2 %collective-permute-start.23 = (bf16[1,208,128]{2,1,0:T(8,128)(2,1)S(1)}, bf16[1,208,128]{2,1,0:T(8,128)(2,1)S(1)}, u32[]{:S(2)}, u32[]{:S(2)}) collective-permute-start(bf16[1,208,128]{2,1,0:T(8,128)(2,1)S(1)} %get-tuple-element.78), channel_id=1, source_target_pairs={{0,8},{1,9},{2,10},{3,11},{4,12},{5,13},{6,14},{7,15},{8,0},{9,1},... | collective-permute-start | bytes 159752 | tf_op jit(solution)/shard_map/ppermute | solution.py:379
  53.3 5.7 %collective-permute-start.24 = (bf16[1,208,128]{2,1,0:T(8,128)(2,1)S(1)}, bf16[1,208,128]{2,1,0:T(8,128)(2,1)S(1)}, u32[]{:S(2)}, u32[]{:S(2)}) collective-permute-start(bf16[1,208,128]{2,1,0:T(8,128)(2,1)S(1)} %get-tuple-element.79), channel_id=1, source_target_pairs={{0,4},{1,5},{2,6},{3,7},{4,0},{5,1},{6,2},{7,3},{8,12},{9,13},{10,... | collective-permute-start | bytes 159752 | tf_op jit(solution)/shard_map/ppermute | solution.py:379
  55.3 5.7 %collective-permute-start.21 = (bf16[1,208,128]{2,1,0:T(8,128)(2,1)S(1)}, bf16[1,208,128]{2,1,0:T(8,128)(2,1)S(1)}, u32[]{:S(2)}, u32[]{:S(2)}) collective-permute-start(bf16[1,208,128]{2,1,0:T(8,128)(2,1)S(1)} %get-tuple-element.76), channel_id=1, source_target_pairs={{0,8},{1,9},{2,10},{3,11},{4,12},{5,13},{6,14},{7,15},{8,0},{9,1},... | collective-permute-start | bytes 159752 | tf_op jit(solution)/shard_map/ppermute | solution.py:379
  61.5 4.2 %collective-permute-start.25 = (bf16[208,128]{1,0:T(8,128)(2,1)S(1)}, bf16[208,128]{1,0:T(8,128)(2,1)S(1)}, u32[]{:S(2)}, u32[]{:S(2)}) collective-permute-start(bf16[208,128]{1,0:T(8,128)(2,1)S(1)} %get-tuple-element.81), channel_id=1, source_target_pairs={{0,16},{16,0},{1,17},{17,1},{2,18},{18,2},{3,19},{19,3},{4,20},{20... | collective-permute-start | bytes 159752 | tf_op jit(solution)/shard_map/ppermute | solution.py:381

commit v10 on v9

--- a/solution.py
+++ b/solution.py
@@ -513,7 +513,7 @@
         scratch=(full, pltpu.VMEM((patches, channels), BF16)),
         flops=conv_flops,
     )
-    (early_parts,), before = deal_rounds([(core_sum(early, position % 2, pieces, True), 1, 0, True, 1)], flags)
+    (early_parts,), before = deal_rounds([(core_sum(early, position % 2, pieces, True), 2, 1, False, 1)], flags)
     proj_flops = 2 * images * tokens * depths * dim * channels
     *terms, token_grad = vmem_call(
         proj_term_kernel,
@@ -526,16 +526,16 @@
     (late_parts,), before = deal_rounds(
         [(core_sum(terms, position % 2, pieces, False), 1, 1, True, 1)], flags, after=(token_grad,)
     )
-    at, early_bits = 2, [2, 1] + list(range(3, bits))
+    at, early_rounds = 2, [(1, 0, True), (1, 1, False)] + [(bit, 1, False) for bit in range(3, bits)]
     while at < bits:
         step = min(2, bits - at)
-        (early_parts,), before = deal_rounds([(early_parts, early_bits.pop(0), 1, False, 1)], flags, after=(before,))
+        (early_parts,), before = deal_rounds([(early_parts, *early_rounds.pop(0), 1)], flags, after=(before,))
         (late_parts, early_parts), before = deal_rounds(
-            [(late_parts, at, step, False, 1), (early_parts, early_bits.pop(0), 1, False, 1)], flags, after=(before,)
+            [(late_parts, at, step, False, 1), (early_parts, *early_rounds.pop(0), 1)], flags, after=(before,)
         )
         at += step
-    while early_bits:
-        (early_parts,), before = deal_rounds([(early_parts, early_bits.pop(0), 1, False, 1)], flags, after=(before,))
+    while early_rounds:
+        (early_parts,), before = deal_rounds([(early_parts, *early_rounds.pop(0), 1)], flags, after=(before,))
     feature_grad = vmem_call(
         feat_grad_kernel,
         sds(images, depths, tokens, dim),

time: 67.2 us -> 68.5 us (1.019)
  waiting for transfers between devices: 20.1 us -> 21.7 us
    ppermute x19, waiting for transfers between devices: 8.24 us -> 11.5 us  [xor_move(): return lax.ppermute(block, 'tile', [(t, t ^ apart) for t in range(tiles)])]
    ppermute x1, waiting for transfers between devices: 3.3 us -> 0.11 us  [xor_move(): return lax.ppermute(block, ('dp', 'tile'), route)]
    ppermute x1, starting transfers between devices: 0.88 us -> 2.52 us  [xor_move(): return lax.ppermute(block, ('dp', 'tile'), route)]
    ppermute x3, waiting for transfers between devices: 7.48 us -> 9.03 us  [xor_move(): return lax.ppermute(block, 'dp', [(0, 1), (1, 0)])]
    ppermute x19, starting transfers between devices: 14.2 us -> 13.1 us  [xor_move(): return lax.ppermute(block, 'tile', [(t, t ^ apart) for t in range(tiles)])]
    ppermute x3, starting transfers between devices: 4.47 us -> 3.66 us  [xor_move(): return lax.ppermute(block, 'dp', [(0, 1), (1, 0)])]
  transfers between devices with their start and end apart: 26 -> 26, of which waited for: 13 -> 14; matrix products, arithmetic and copies ran while one was open for 0% -> 0% of each run, Pallas kernels for 17% -> 16%
where the time goes in v10:
time: 68.5 us; the launch traced here: 68.3 us
  starting transfers between devices  25.4 us (37%)
  waiting for transfers between devices  21.7 us (32%)
  Pallas kernels  16.1 us (24%)
  local copies, waits for them, and re-layouts  3 us (4%)
  other arithmetic  1.19 us (2%)
  between operations  0.9 us (1%)
    pallas_call x15, Pallas kernels, vmem_call(): pl.pallas_call(run, out_shape=out_shape, in_specs=specs, out_specs=jax.tr...  16.1 us
    ppermute x19, starting transfers between devices, xor_move(): return lax.ppermute(block, 'tile', [(t, t ^ apart) for t in range(tiles)])  13.1 us
    ppermute x19, waiting for transfers between devices, xor_move(): return lax.ppermute(block, 'tile', [(t, t ^ apart) for t in range(tiles)])  11.5 us
    ppermute x3, waiting for transfers between devices, xor_move(): return lax.ppermute(block, 'dp', [(0, 1), (1, 0)])  9.03 us
    ppermute x3, starting transfers between devices, swap(): return lax.ppermute(block, 'tile', tile_route(row_pairs, col_pairs, rows))  6.19 us
    ppermute x3, starting transfers between devices, xor_move(): return lax.ppermute(block, 'dp', [(0, 1), (1, 0)])  3.66 us
    unnamed x12, local copies, waits for them, and re-layouts  2.91 us
    ppermute x1, starting transfers between devices, xor_move(): return lax.ppermute(block, ('dp', 'tile'), route)  2.52 us
  transfers between devices with their start and end apart: 26, of which 14 were waited for; matrix products, arithmetic and copies ran while one was open for 0% of the time, Pallas kernels for 16%

profile of v10, /device:TPU:0, one launch (start us, length us, event | category | flops | bytes accessed | tf_op | source)
XLA Modules:
  0.0 68.3 jit_solution(3194007761543959143)
XLA Ops:
  0.7 1.2 %broadcast_select_fusion = (bf16[4,16,4,256]{3,2,1,0:T(4,128)(2,1)S(1)}, bf16[4,16,4,256]{3,2,1,0:T(4,128)(2,1)S(1)}) fusion(pred[]{:T(512)S(6)} %eq.27, bf16[4,16,32,256]{3,2,1,0:T(8,128)(2,1)} %refs_0_.1), kind=kLoop, calls=%fused_computation | loop fusion | flops 131072 | bytes 524289 | tf_op jit(solution)/shard_map/jit(_where)/select_n | solution.py:456
  1.9 3.1 %collective-permute-start.1 = (bf16[4,16,4,256]{3,2,1,0:T(4,128)(2,1)S(1)}, bf16[4,16,4,256]{3,2,1,0:T(4,128)(2,1)S(1)}, u32[]{:S(2)}, u32[]{:S(2)}) collective-permute-start(bf16[4,16,4,256]{3,2,1,0:T(4,128)(2,1)S(1)} %get-tuple-element.82), channel_id=1, source_target_pairs={{1,3},{3,1},{2,6},{6,2},{7,5},{5,7},{0,4},{4,0},{9,11},{11,9},{10,... | collective-permute-start | bytes 393224 | tf_op jit(solution)/shard_map/ppermute | solution.py:452
  4.9 1.2 %copy-done.3 = bf16[4,16,32,256]{3,2,1,0:T(8,128)(2,1)S(1)} copy-done((bf16[4,16,32,256]{3,2,1,0:T(8,128)(2,1)S(1)}, bf16[4,16,32,256]{3,2,1,0:T(8,128)(2,1)}, u32[]{:S(2)}) %copy-start.3) | copy-done | bytes 1048600
  6.2 0.5 shard_map.68.refs_1_
  6.7 0.1 stack.71.refs_0_
  6.8 1.1 %collective-permute-done.1.refs_3_ = bf16[4,16,4,256]{3,2,1,0:T(4,128)(2,1)S(1)} collective-permute-done((bf16[4,16,4,256]{3,2,1,0:T(4,128)(2,1)S(1)}, bf16[4,16,4,256]{3,2,1,0:T(4,128)(2,1)S(1)}, u32[]{:S(2)}, u32[]{:S(2)}) %collective-permute-start.1) | collective-permute-done | bytes 131104 | tf_op jit(solution)/shard_map/ppermute | solution.py:452
  7.9 0.0 collective-permute-done.refs_2_
  7.9 0.8 %shard_map.69 = (bf16[144,256]{1,0:T(8,128)(2,1)S(1)}, f32[4,6,16,256]{3,2,1,0:T(8,128)S(1)}, f32[4,6,2,256]{3,2,1,0:T(2,128)S(1)}) custom-call(s32[13]{0:T(128)S(1)} %stack.71.refs_0_, f32[4,16,24,256]{3,2,1,0:T(8,128)S(1)} %shard_map.68.refs_1_, bf16[4,16,4,256]{3,2,1,0:T(4,128)(2,1)S(1)} %collective-permute-done.refs_2_, ...), custom_call_target="tpu_custom_call" | custom-call | bytes 2351156 | tf_op jit(solution)/shard_map/pallas_call | solution.py:360
  8.7 3.1 %collective-permute-start.2 = (bf16[144,256]{1,0:T(8,128)(2,1)S(1)}, bf16[144,256]{1,0:T(8,128)(2,1)S(1)}, u32[]{:S(2)}, u32[]{:S(2)}) collective-permute-start(bf16[144,256]{1,0:T(8,128)(2,1)S(1)} %get-tuple-element.42.refs_5_), channel_id=1, source_target_pairs={{0,8},{1,9},{3,11},{2,10},{6,14},{7,15},{5,13},{4,12},{8,0},{9,1},... | collective-permute-start | bytes 221192 | tf_op jit(solution)/shard_map/ppermute | solution.py:452
  11.8 1.7 %copy-done = bf16[2,3,3,256,256]{4,3,2,1,0:T(8,128)(2,1)S(1)} copy-done((bf16[2,3,3,256,256]{4,3,2,1,0:T(8,128)(2,1)S(1)}, bf16[2,3,3,256,256]{4,3,2,1,0:T(8,128)(2,1)}, u32[]{:S(2)}) %copy-start) | copy-done | bytes 2359320
  13.4 2.4 %shard_map.70 = (bf16[3,640,256]{2,1,0:T(8,128)(2,1)S(1)}, f32[2,512,256]{2,1,0:T(8,128)S(1)}) custom-call(s32[13]{0:T(128)S(1)} %stack.71.refs_0_, f32[4,16,24,256]{3,2,1,0:T(8,128)S(1)} %shard_map.68.refs_1_, bf16[4,16,4,256]{3,2,1,0:T(4,128)(2,1)S(1)} %collective-permute-done.refs_2_, bf16[4,16,4,256]{3,2,1,0:T(4,128)(2,1)S(1)} %collective-permute-done.1.refs_3_, ...), custom_call_target="tpu_custom_call" | custom-call | flops 1207959552 | bytes 6225972 | tf_op jit(solution)/shard_map/pallas_call | solution.py:360
  15.8 0.0 collective-permute-done.2.refs_1_
  15.8 0.0 copy-start.5
  15.9 1.6 %shard_map.71 = (bf16[2,2,64,256]{3,2,1,0:T(8,128)(2,1)S(1)}, bf16[2,2,64,256]{3,2,1,0:T(8,128)(2,1)S(1)}, bf16[2,2,64,256]{3,2,1,0:T(8,128)(2,1)S(1)}, bf16[2,2...) custom-call(s32[13]{0:T(128)S(1)} %stack.71.refs_0_, ...), custom_call_target="tpu_custom_call", output_to_operand_aliasing={{4}: (4, {})} | custom-call | flops 301989888 | bytes 6414388 | tf_op jit(solution)/shard_map/pallas_call | solution.py:360
  17.5 1.6 %collective-permute-start.3 = (bf16[2,2,64,256]{3,2,1,0:T(8,128)(2,1)S(1)}, bf16[2,2,64,256]{3,2,1,0:T(8,128)(2,1)S(1)}, u32[]{:S(2)}, u32[]{:S(2)}) collective-permute-start(bf16[2,2,64,256]{3,2,1,0:T(8,128)(2,1)S(1)} %get-tuple-element.48), channel_id=1, source_target_pairs={{0,2},{1,3},{2,0},{3,1},{4,6},{5,7},{6,4},{7,5},{8,10},{9,11},{10,... | collective-permute-start | bytes 393224 | tf_op jit(solution)/shard_map/ppermute | solution.py:379
  19.1 1.6 %collective-permute-start.4 = (bf16[2,2,64,256]{3,2,1,0:T(8,128)(2,1)S(1)}, bf16[2,2,64,256]{3,2,1,0:T(8,128)(2,1)S(1)}, u32[]{:S(2)}, u32[]{:S(2)}) collective-permute-start(bf16[2,2,64,256]{3,2,1,0:T(8,128)(2,1)S(1)} %get-tuple-element.49), channel_id=1, source_target_pairs={{0,4},{1,5},{2,6},{3,7},{4,0},{5,1},{6,2},{7,3},{8,12},{9,13},{10,... | collective-permute-start | bytes 393224 | tf_op jit(solution)/shard_map/ppermute | solution.py:379
  20.7 0.4 collective-permute-start.5
  21.1 2.1 %shard_map.73 = (bf16[8,208,256]{2,1,0:T(8,128)(2,1)S(1)}, bf16[2,208,256]{2,1,0:T(8,128)(2,1)S(1)}, bf16[2,208,256]{2,1,0:T(8,128)(2,1)S(1)}, bf16[2,208,256]{2...) custom-call(s32[13]{0:T(128)S(1)} %stack.71.refs_0_, ...), custom_call_target="tpu_custom_call" | custom-call | flops 1207959552 | bytes 3866676 | tf_op jit(solution)/shard_map/pallas_call | solution.py:360
  23.1 0.0 copy-start.2
  23.2 0.1 collective-permute-start.7
  23.2 0.5 collective-permute-start.8
  23.7 0.0 collective-permute-done.3.refs_1_.refs_2_
  23.7 0.1 collective-permute-start.9
  23.8 0.5 collective-permute-done.4.refs_2_.refs_3_
  24.4 2.2 %collective-permute-done.5.refs_3_.refs_4_ = bf16[2,2,64,256]{3,2,1,0:T(8,128)(2,1)S(1)} collective-permute-done((bf16[2,2,64,256]{3,2,1,0:T(8,128)(2,1)S(1)}, bf16[2,2,64,256]{3,2,1,0:T(8,128)(2,1)S(1)}, u32[]{:S(2)}, u32[]{:S(2)}) %collective-permute-start.5) | collective-permute-done | bytes 131104 | tf_op jit(solution)/shard_map/ppermute | solution.py:379
  26.5 0.1 collective-permute-start.6
  26.6 0.0 collective-permute-done.7.refs_2_
  26.6 0.0 collective-permute-done.8.refs_3_
  26.7 0.0 collective-permute-done.10.refs_5_
  26.7 0.7 %shard_map.74 = (f32[4,208,256]{2,1,0:T(8,128)S(1)}, bf16[4,208,256]{2,1,0:T(8,128)(2,1)S(1)}) custom-call(s32[13]{0:T(128)S(1)} %stack.71.refs_0_, bf16[8,208,256]{2,1,0:T(8,128)(2,1)S(1)} %get-tuple-element.53.refs_1_, bf16[2,208,256]{2,1,0:T(8,128)(2,1)S(1)} %collective-permute-done.7.refs_2_, bf16[2,208,256]{2,1,0:T(8,128)(2,1)S(1)} %collective-permute-done.8.refs_3_, ...), custom_call_target="tpu_custom_call" | custom-call | bytes 2981940 | tf_op jit(solution)/shard_map/pallas_call | solution.py:360
  27.4 0.8 %collective-permute-start.18 = (bf16[4,208,256]{2,1,0:T(8,128)(2,1)S(1)}, bf16[4,208,256]{2,1,0:T(8,128)(2,1)S(1)}, u32[]{:S(2)}, u32[]{:S(2)}) collective-permute-start(bf16[4,208,256]{2,1,0:T(8,128)(2,1)S(1)} %get-tuple-element.69), channel_id=1, source_target_pairs={{0,4},{1,5},{2,6},{3,7},{4,0},{5,1},{6,2},{7,3},{8,12},{9,13},{10,... | collective-permute-start | bytes 1277960 | tf_op jit(solution)/shard_map/ppermute | solution.py:379
  28.2 1.5 %shard_map.75 = (bf16[8,208,256]{2,1,0:T(8,128)(2,1)S(1)}, bf16[2,208,256]{2,1,0:T(8,128)(2,1)S(1)}, bf16[2,208,256]{2,1,0:T(8,128)(2,1)S(1)}, bf16[2,208,256]{2...) custom-call(s32[13]{0:T(128)S(1)} %stack.71.refs_0_, ...), custom_call_target="tpu_custom_call" | custom-call | flops 536870912 | bytes 5767220 | tf_op jit(solution)/shard_map/pallas_call | solution.py:360
  29.7 0.3 collective-permute-start.11
  30.0 0.3 collective-permute-start.12
  30.3 0.2 collective-permute-start.13
  30.5 0.3 collective-permute-start.14
  30.8 0.4 collective-permute-done.11.refs_2_
  31.2 0.3 collective-permute-done.12.refs_3_
  31.5 0.3 collective-permute-done.13.refs_4_
  31.8 0.3 collective-permute-done.14.refs_5_
  32.1 0.7 %shard_map.76 = (f32[4,208,128]{2,1,0:T(8,128)S(1)}, bf16[4,208,128]{2,1,0:T(8,128)(2,1)S(1)}, bf16[4,208,128]{2,1,0:T(8,128)(2,1)S(1)}, bf16[4,208,128]{2,1,0:T(8,128)(2,1)S(1)}) custom-call(s32[13]{0:T(128)S(1)} %stack.71.refs_0_, bf16[8,208,256]{2,1,0:T(8,128)(2,1)S(1)} %get-tuple-element.60.refs_1_, ...), custom_call_target="tpu_custom_call" | custom-call | bytes 2768948 | tf_op jit(solution)/shard_map/pallas_call | solution.py:360
  32.9 2.5 %collective-permute-start.15 = (bf16[4,208,128]{2,1,0:T(8,128)(2,1)S(1)}, bf16[4,208,128]{2,1,0:T(8,128)(2,1)S(1)}, u32[]{:S(2)}, u32[]{:S(2)}) collective-permute-start(bf16[4,208,128]{2,1,0:T(8,128)(2,1)S(1)} %get-tuple-element.66), channel_id=1, source_target_pairs={{0,18},{1,19},{2,16},{3,17},{4,22},{5,23},{6,20},{7,21},{8,26},{9,... | collective-permute-start | bytes 638984 | tf_op jit(solution)/shard_map/ppermute | solution.py:383
  35.4 0.5 collective-permute-start.16
  35.9 0.5 collective-permute-start.17
  36.4 3.2 %collective-permute-done.18.refs_2_ = bf16[4,208,256]{2,1,0:T(8,128)(2,1)S(1)} collective-permute-done((bf16[4,208,256]{2,1,0:T(8,128)(2,1)S(1)}, bf16[4,208,256]{2,1,0:T(8,128)(2,1)S(1)}, u32[]{:S(2)}, u32[]{:S(2)}) %collective-permute-start.18) | collective-permute-done | bytes 426016 | tf_op jit(solution)/shard_map/ppermute | solution.py:379
  39.7 0.6 shard_map.77
  40.3 1.6 %collective-permute-start.19 = (bf16[4,208,128]{2,1,0:T(8,128)(2,1)S(1)}, bf16[4,208,128]{2,1,0:T(8,128)(2,1)S(1)}, u32[]{:S(2)}, u32[]{:S(2)}) collective-permute-start(bf16[4,208,128]{2,1,0:T(8,128)(2,1)S(1)} %get-tuple-element.71), channel_id=1, source_target_pairs={{0,16},{16,0},{1,17},{17,1},{2,18},{18,2},{3,19},{19,3},{4,20},{20... | collective-permute-start | bytes 638984 | tf_op jit(solution)/shard_map/ppermute | solution.py:381
  41.9 0.1 collective-permute-done.15.refs_2_
  42.0 4.6 %collective-permute-done.16.refs_3_ = bf16[4,208,128]{2,1,0:T(8,128)(2,1)S(1)} collective-permute-done((bf16[4,208,128]{2,1,0:T(8,128)(2,1)S(1)}, bf16[4,208,128]{2,1,0:T(8,128)(2,1)S(1)}, u32[]{:S(2)}, u32[]{:S(2)}) %collective-permute-start.16) | collective-permute-done | bytes 213024 | tf_op jit(solution)/shard_map/ppermute | solution.py:381
  46.6 3.8 %collective-permute-done.19.refs_6_ = bf16[4,208,128]{2,1,0:T(8,128)(2,1)S(1)} collective-permute-done((bf16[4,208,128]{2,1,0:T(8,128)(2,1)S(1)}, bf16[4,208,128]{2,1,0:T(8,128)(2,1)S(1)}, u32[]{:S(2)}, u32[]{:S(2)}) %collective-permute-start.19) | collective-permute-done | bytes 213024 | tf_op jit(solution)/shard_map/ppermute | solution.py:381
  50.4 0.7 %shard_map.78 = (f32[1,208,128]{2,1,0:T(8,128)S(1)}, bf16[1,208,128]{2,1,0:T(8,128)(2,1)S(1)}, bf16[1,208,128]{2,1,0:T(8,128)(2,1)S(1)}, bf16[1,208,128]{2,1,0:T...) custom-call(s32[13]{0:T(128)S(1)} %stack.71.refs_0_, ...), custom_call_target="tpu_custom_call" | custom-call | bytes 2289716 | tf_op jit(solution)/shard_map/pallas_call | solution.py:360
  51.1 0.6 collective-permute-start.20
  51.7 2.5 %collective-permute-start.22 = (bf16[1,208,128]{2,1,0:T(8,128)(2,1)S(1)}, bf16[1,208,128]{2,1,0:T(8,128)(2,1)S(1)}, u32[]{:S(2)}, u32[]{:S(2)}) collective-permute-start(bf16[1,208,128]{2,1,0:T(8,128)(2,1)S(1)} %get-tuple-element.77), channel_id=1, source_target_pairs={{0,12},{1,13},{2,14},{3,15},{4,8},{5,9},{6,10},{7,11},{8,4},{9,5},... | collective-permute-start | bytes 159752 | tf_op jit(solution)/shard_map/ppermute | solution.py:379
  54.2 0.2 collective-permute-start.23
  54.4 1.6 %collective-permute-start.24 = (bf16[1,208,128]{2,1,0:T(8,128)(2,1)S(1)}, bf16[1,208,128]{2,1,0:T(8,128)(2,1)S(1)}, u32[]{:S(2)}, u32[]{:S(2)}) collective-permute-start(bf16[1,208,128]{2,1,0:T(8,128)(2,1)S(1)} %get-tuple-element.79), channel_id=1, source_target_pairs={{0,4},{1,5},{2,6},{3,7},{4,0},{5,1},{6,2},{7,3},{8,12},{9,13},{10,... | collective-permute-start | bytes 159752 | tf_op jit(solution)/shard_map/ppermute | solution.py:379
  56.1 0.6 shard_map.79
  56.7 1.5 %collective-permute-start.21 = (bf16[1,208,128]{2,1,0:T(8,128)(2,1)S(1)}, bf16[1,208,128]{2,1,0:T(8,128)(2,1)S(1)}, u32[]{:S(2)}, u32[]{:S(2)}) collective-permute-start(bf16[1,208,128]{2,1,0:T(8,128)(2,1)S(1)} %get-tuple-element.76), channel_id=1, source_target_pairs={{0,8},{1,9},{2,10},{3,11},{4,12},{5,13},{6,14},{7,15},{8,0},{9,1},... | collective-permute-start | bytes 159752 | tf_op jit(solution)/shard_map/ppermute | solution.py:379
  58.1 2.4 %collective-permute-done.23.refs_5_ = bf16[1,208,128]{2,1,0:T(8,128)(2,1)S(1)} collective-permute-done((bf16[1,208,128]{2,1,0:T(8,128)(2,1)S(1)}, bf16[1,208,128]{2,1,0:T(8,128)(2,1)S(1)}, u32[]{:S(2)}, u32[]{:S(2)}) %collective-permute-start.23) | collective-permute-done | bytes 53280 | tf_op jit(solution)/shard_map/ppermute | solution.py:379
  60.5 1.8 %collective-permute-done.21.refs_2_ = bf16[1,208,128]{2,1,0:T(8,128)(2,1)S(1)} collective-permute-done((bf16[1,208,128]{2,1,0:T(8,128)(2,1)S(1)}, bf16[1,208,128]{2,1,0:T(8,128)(2,1)S(1)}, u32[]{:S(2)}, u32[]{:S(2)}) %collective-permute-start.21) | collective-permute-done | bytes 53280 | tf_op jit(solution)/shard_map/ppermute | solution.py:379
  62.3 0.6 shard_map.81
  62.9 1.6 %collective-permute-start.25 = (bf16[208,128]{1,0:T(8,128)(2,1)S(1)}, bf16[208,128]{1,0:T(8,128)(2,1)S(1)}, u32[]{:S(2)}, u32[]{:S(2)}) collective-permute-start(bf16[208,128]{1,0:T(8,128)(2,1)S(1)} %get-tuple-element.81), channel_id=1, source_target_pairs={{0,16},{16,0},{1,17},{17,1},{2,18},{18,2},{3,19},{19,3},{4,20},{20... | collective-permute-start | bytes 159752 | tf_op jit(solution)/shard_map/ppermute | solution.py:381
  64.4 2.1 %shard_map.80 = bf16[4,2,128,1024]{3,2,1,0:T(8,128)(2,1)} custom-call(bf16[2,512,256]{2,1,0:T(8,128)(2,1)S(1)} %get-tuple-element.59.refs_6_.refs_0_, bf16[2,1024,256]{2,1,0:T(8,128)(2,1)S(1)} %copy-done.4, f32[1,208,128]{2,1,0:T(8,128)S(1)} %get-tuple-element.75.refs_2_.refs_1_), custom_call_target="tpu_custom_call" | custom-call | flops 536870912 | bytes 3670016 | tf_op jit(solution)/shard_map/pallas_call | solution.py:360
  66.5 0.6 collective-permute-done.25.refs_2_
  67.1 1.2 %shard_map.82 = f32[208,256]{1,0:T(8,128)} custom-call(s32[13]{0:T(128)S(1)} %stack.71.refs_0_, f32[208,128]{1,0:T(8,128)S(1)} %get-tuple-element.80.refs_1_, bf16[208,128]{1,0:T(8,128)(2,1)S(1)} %collective-permute-done.25.refs_2_), custom_call_target="tpu_custom_call" | custom-call | bytes 372788 | tf_op jit(solution)/shard_map/pallas_call | solution.py:360
  (17 shorter events, 0.1 us)
Async XLA Ops:
  1.9 6.0 %collective-permute-start.1 = (bf16[4,16,4,256]{3,2,1,0:T(4,128)(2,1)S(1)}, bf16[4,16,4,256]{3,2,1,0:T(4,128)(2,1)S(1)}, u32[]{:S(2)}, u32[]{:S(2)}) collective-permute-start(bf16[4,16,4,256]{3,2,1,0:T(4,128)(2,1)S(1)} %get-tuple-element.82), channel_id=1, source_target_pairs={{1,3},{3,1},{2,6},{6,2},{7,5},{5,7},{0,4},{4,0},{9,11},{11,9},{10,... | collective-permute-start | bytes 393224 | tf_op jit(solution)/shard_map/ppermute | solution.py:452
  4.9 3.0 %collective-permute-start = (bf16[4,16,4,256]{3,2,1,0:T(4,128)(2,1)S(1)}, bf16[4,16,4,256]{3,2,1,0:T(4,128)(2,1)S(1)}, u32[]{:S(2)}, u32[]{:S(2)}) collective-permute-start(bf16[4,16,4,256]{3,2,1,0:T(4,128)(2,1)S(1)} %get-tuple-element.83), channel_id=1, source_target_pairs={{0,1},{1,0},{3,2},{2,3},{6,7},{7,6},{5,4},{4,5},{8,9},{9,8},{11,10... | collective-permute-start | bytes 393224 | tf_op jit(solution)/shard_map/ppermute | solution.py:452
  4.9 1.2 %copy-start.3 = (bf16[4,16,32,256]{3,2,1,0:T(8,128)(2,1)S(1)}, bf16[4,16,32,256]{3,2,1,0:T(8,128)(2,1)}, u32[]{:S(2)}) copy-start(bf16[4,16,32,256]{3,2,1,0:T(8,128)(2,1)} %refs_0_.1) | copy-start | bytes 3145732
  8.7 7.2 %collective-permute-start.2 = (bf16[144,256]{1,0:T(8,128)(2,1)S(1)}, bf16[144,256]{1,0:T(8,128)(2,1)S(1)}, u32[]{:S(2)}, u32[]{:S(2)}) collective-permute-start(bf16[144,256]{1,0:T(8,128)(2,1)S(1)} %get-tuple-element.42.refs_5_), channel_id=1, source_target_pairs={{0,8},{1,9},{3,11},{2,10},{6,14},{7,15},{5,13},{4,12},{8,0},{9,1},... | collective-permute-start | bytes 221192 | tf_op jit(solution)/shard_map/ppermute | solution.py:452
  11.8 1.7 %copy-start = (bf16[2,3,3,256,256]{4,3,2,1,0:T(8,128)(2,1)S(1)}, bf16[2,3,3,256,256]{4,3,2,1,0:T(8,128)(2,1)}, u32[]{:S(2)}) copy-start(bf16[2,3,3,256,256]{4,3,2,1,0:T(8,128)(2,1)} %refs_6_.2) | copy-start | bytes 7077892
  13.4 2.4 %copy-start.1 = (bf16[2,3,3,256,256]{4,3,2,1,0:T(8,128)(2,1)S(1)}, bf16[2,3,3,256,256]{4,3,2,1,0:T(8,128)(2,1)}, u32[]{:S(2)}) copy-start(bf16[2,3,3,256,256]{4,3,2,1,0:T(8,128)(2,1)} %refs_6_.2) | copy-start | bytes 7077892
  15.8 5.2 %copy-start.5 = (bf16[4,2,8,16,256]{4,3,2,1,0:T(8,128)(2,1)S(1)}, bf16[4,2,8,16,256]{4,3,2,1,0:T(8,128)(2,1)}, u32[]{:S(2)}) copy-start(bf16[4,2,8,16,256]{4,3,2,1,0:T(8,128)(2,1)} %refs_2_.1) | copy-start | bytes 1572868
  17.5 6.2 %collective-permute-start.3 = (bf16[2,2,64,256]{3,2,1,0:T(8,128)(2,1)S(1)}, bf16[2,2,64,256]{3,2,1,0:T(8,128)(2,1)S(1)}, u32[]{:S(2)}, u32[]{:S(2)}) collective-permute-start(bf16[2,2,64,256]{3,2,1,0:T(8,128)(2,1)S(1)} %get-tuple-element.48), channel_id=1, source_target_pairs={{0,2},{1,3},{2,0},{3,1},{4,6},{5,7},{6,4},{7,5},{8,10},{9,11},{10,... | collective-permute-start | bytes 393224 | tf_op jit(solution)/shard_map/ppermute | solution.py:379
  19.1 5.3 %collective-permute-start.4 = (bf16[2,2,64,256]{3,2,1,0:T(8,128)(2,1)S(1)}, bf16[2,2,64,256]{3,2,1,0:T(8,128)(2,1)S(1)}, u32[]{:S(2)}, u32[]{:S(2)}) collective-permute-start(bf16[2,2,64,256]{3,2,1,0:T(8,128)(2,1)S(1)} %get-tuple-element.49), channel_id=1, source_target_pairs={{0,4},{1,5},{2,6},{3,7},{4,0},{5,1},{6,2},{7,3},{8,12},{9,13},{10,... | collective-permute-start | bytes 393224 | tf_op jit(solution)/shard_map/ppermute | solution.py:379
  20.7 5.9 %collective-permute-start.5 = (bf16[2,2,64,256]{3,2,1,0:T(8,128)(2,1)S(1)}, bf16[2,2,64,256]{3,2,1,0:T(8,128)(2,1)S(1)}, u32[]{:S(2)}, u32[]{:S(2)}) collective-permute-start(bf16[2,2,64,256]{3,2,1,0:T(8,128)(2,1)S(1)} %get-tuple-element.50), channel_id=1, source_target_pairs={{0,6},{1,7},{2,4},{3,5},{4,2},{5,3},{6,0},{7,1},{8,14},{9,15},{10,... | collective-permute-start | bytes 393224 | tf_op jit(solution)/shard_map/ppermute | solution.py:379
  23.1 5.1 %copy-start.2 = (bf16[4,2,128,1024]{3,2,1,0:T(8,128)(2,1)S(1)}, bf16[4,2,128,1024]{3,2,1,0:T(8,128)(2,1)}, u32[]{:S(2)}) copy-start(bf16[4,2,128,1024]{3,2,1,0:T(8,128)(2,1)} %refs_6_.3) | copy-start | bytes 6291460
  23.2 3.5 %collective-permute-start.7 = (bf16[2,208,256]{2,1,0:T(8,128)(2,1)S(1)}, bf16[2,208,256]{2,1,0:T(8,128)(2,1)S(1)}, u32[]{:S(2)}, u32[]{:S(2)}) collective-permute-start(bf16[2,208,256]{2,1,0:T(8,128)(2,1)S(1)} %get-tuple-element.54), channel_id=1, source_target_pairs={{0,1},{1,0},{2,3},{3,2},{4,5},{5,4},{6,7},{7,6},{8,9},{9,8},{10,11... | collective-permute-start | bytes 638984 | tf_op jit(solution)/shard_map/ppermute | solution.py:379
  23.2 3.4 %collective-permute-start.8 = (bf16[2,208,256]{2,1,0:T(8,128)(2,1)S(1)}, bf16[2,208,256]{2,1,0:T(8,128)(2,1)S(1)}, u32[]{:S(2)}, u32[]{:S(2)}) collective-permute-start(bf16[2,208,256]{2,1,0:T(8,128)(2,1)S(1)} %get-tuple-element.55), channel_id=1, source_target_pairs={{0,1},{1,0},{2,3},{3,2},{4,5},{5,4},{6,7},{7,6},{8,9},{9,8},{10,11... | collective-permute-start | bytes 638984 | tf_op jit(solution)/shard_map/ppermute | solution.py:379
  23.7 2.9 %collective-permute-start.9 = (bf16[2,208,256]{2,1,0:T(8,128)(2,1)S(1)}, bf16[2,208,256]{2,1,0:T(8,128)(2,1)S(1)}, u32[]{:S(2)}, u32[]{:S(2)}) collective-permute-start(bf16[2,208,256]{2,1,0:T(8,128)(2,1)S(1)} %get-tuple-element.56), channel_id=1, source_target_pairs={{0,1},{1,0},{2,3},{3,2},{4,5},{5,4},{6,7},{7,6},{8,9},{9,8},{10,11... | collective-permute-start | bytes 638984 | tf_op jit(solution)/shard_map/ppermute | solution.py:379
  24.4 2.3 %collective-permute-start.10 = (bf16[2,208,256]{2,1,0:T(8,128)(2,1)S(1)}, bf16[2,208,256]{2,1,0:T(8,128)(2,1)S(1)}, u32[]{:S(2)}, u32[]{:S(2)}) collective-permute-start(bf16[2,208,256]{2,1,0:T(8,128)(2,1)S(1)} %get-tuple-element.57), channel_id=1, source_target_pairs={{0,1},{1,0},{2,3},{3,2},{4,5},{5,4},{6,7},{7,6},{8,9},{9,8},{10,11... | collective-permute-start | bytes 638984 | tf_op jit(solution)/shard_map/ppermute | solution.py:379
  26.5 1.7 %collective-permute-start.6 = (bf16[4,2,64,256]{3,2,1,0:T(8,128)(2,1)S(1)}, bf16[4,2,64,256]{3,2,1,0:T(8,128)(2,1)S(1)}, u32[]{:S(2)}, u32[]{:S(2)}) collective-permute-start(bf16[4,2,64,256]{3,2,1,0:T(8,128)(2,1)S(1)} %shard_map.72), channel_id=1, source_target_pairs={{0,1},{1,0},{2,3},{3,2},{4,5},{5,4},{6,7},{7,6},{8,9},{9,8},{10,11... | collective-permute-start | bytes 786440 | tf_op jit(solution)/shard_map/ppermute | solution.py:379
  27.4 12.3 %collective-permute-start.18 = (bf16[4,208,256]{2,1,0:T(8,128)(2,1)S(1)}, bf16[4,208,256]{2,1,0:T(8,128)(2,1)S(1)}, u32[]{:S(2)}, u32[]{:S(2)}) collective-permute-start(bf16[4,208,256]{2,1,0:T(8,128)(2,1)S(1)} %get-tuple-element.69), channel_id=1, source_target_pairs={{0,4},{1,5},{2,6},{3,7},{4,0},{5,1},{6,2},{7,3},{8,12},{9,13},{10,... | collective-permute-start | bytes 1277960 | tf_op jit(solution)/shard_map/ppermute | solution.py:379
  29.7 1.5 %collective-permute-start.11 = (bf16[2,208,256]{2,1,0:T(8,128)(2,1)S(1)}, bf16[2,208,256]{2,1,0:T(8,128)(2,1)S(1)}, u32[]{:S(2)}, u32[]{:S(2)}) collective-permute-start(bf16[2,208,256]{2,1,0:T(8,128)(2,1)S(1)} %get-tuple-element.61), channel_id=1, source_target_pairs={{0,1},{1,0},{2,3},{3,2},{4,5},{5,4},{6,7},{7,6},{8,9},{9,8},{10,11... | collective-permute-start | bytes 638984 | tf_op jit(solution)/shard_map/ppermute | solution.py:379
  30.0 1.6 %collective-permute-start.12 = (bf16[2,208,256]{2,1,0:T(8,128)(2,1)S(1)}, bf16[2,208,256]{2,1,0:T(8,128)(2,1)S(1)}, u32[]{:S(2)}, u32[]{:S(2)}) collective-permute-start(bf16[2,208,256]{2,1,0:T(8,128)(2,1)S(1)} %get-tuple-element.62), channel_id=1, source_target_pairs={{0,1},{1,0},{2,3},{3,2},{4,5},{5,4},{6,7},{7,6},{8,9},{9,8},{10,11... | collective-permute-start | bytes 638984 | tf_op jit(solution)/shard_map/ppermute | solution.py:379
  30.3 1.6 %collective-permute-start.13 = (bf16[2,208,256]{2,1,0:T(8,128)(2,1)S(1)}, bf16[2,208,256]{2,1,0:T(8,128)(2,1)S(1)}, u32[]{:S(2)}, u32[]{:S(2)}) collective-permute-start(bf16[2,208,256]{2,1,0:T(8,128)(2,1)S(1)} %get-tuple-element.63), channel_id=1, source_target_pairs={{0,1},{1,0},{2,3},{3,2},{4,5},{5,4},{6,7},{7,6},{8,9},{9,8},{10,11... | collective-permute-start | bytes 638984 | tf_op jit(solution)/shard_map/ppermute | solution.py:379
  30.5 1.7 %collective-permute-start.14 = (bf16[2,208,256]{2,1,0:T(8,128)(2,1)S(1)}, bf16[2,208,256]{2,1,0:T(8,128)(2,1)S(1)}, u32[]{:S(2)}, u32[]{:S(2)}) collective-permute-start(bf16[2,208,256]{2,1,0:T(8,128)(2,1)S(1)} %get-tuple-element.64), channel_id=1, source_target_pairs={{0,1},{1,0},{2,3},{3,2},{4,5},{5,4},{6,7},{7,6},{8,9},{9,8},{10,11... | collective-permute-start | bytes 638984 | tf_op jit(solution)/shard_map/ppermute | solution.py:379
  32.9 9.1 %collective-permute-start.15 = (bf16[4,208,128]{2,1,0:T(8,128)(2,1)S(1)}, bf16[4,208,128]{2,1,0:T(8,128)(2,1)S(1)}, u32[]{:S(2)}, u32[]{:S(2)}) collective-permute-start(bf16[4,208,128]{2,1,0:T(8,128)(2,1)S(1)} %get-tuple-element.66), channel_id=1, source_target_pairs={{0,18},{1,19},{2,16},{3,17},{4,22},{5,23},{6,20},{7,21},{8,26},{9,... | collective-permute-start | bytes 638984 | tf_op jit(solution)/shard_map/ppermute | solution.py:383
  35.4 11.2 %collective-permute-start.16 = (bf16[4,208,128]{2,1,0:T(8,128)(2,1)S(1)}, bf16[4,208,128]{2,1,0:T(8,128)(2,1)S(1)}, u32[]{:S(2)}, u32[]{:S(2)}) collective-permute-start(bf16[4,208,128]{2,1,0:T(8,128)(2,1)S(1)} %get-tuple-element.67), channel_id=1, source_target_pairs={{0,16},{16,0},{1,17},{17,1},{2,18},{18,2},{3,19},{19,3},{4,20},{20... | collective-permute-start | bytes 638984 | tf_op jit(solution)/shard_map/ppermute | solution.py:381
  35.9 10.7 %collective-permute-start.17 = (bf16[4,208,128]{2,1,0:T(8,128)(2,1)S(1)}, bf16[4,208,128]{2,1,0:T(8,128)(2,1)S(1)}, u32[]{:S(2)}, u32[]{:S(2)}) collective-permute-start(bf16[4,208,128]{2,1,0:T(8,128)(2,1)S(1)} %get-tuple-element.68), channel_id=1, source_target_pairs={{0,2},{1,3},{2,0},{3,1},{4,6},{5,7},{6,4},{7,5},{8,10},{9,11},{10,... | collective-permute-start | bytes 638984 | tf_op jit(solution)/shard_map/ppermute | solution.py:379
  39.7 24.7 %copy-start.4 = (bf16[2,1024,256]{2,1,0:T(8,128)(2,1)S(1)}, bf16[2,1024,256]{2,1,0:T(8,128)(2,1)}, u32[]{:S(2)}) copy-start(bf16[2,1024,256]{2,1,0:T(8,128)(2,1)} %refs_1_.1) | copy-start | bytes 3145732
  40.3 10.1 %collective-permute-start.19 = (bf16[4,208,128]{2,1,0:T(8,128)(2,1)S(1)}, bf16[4,208,128]{2,1,0:T(8,128)(2,1)S(1)}, u32[]{:S(2)}, u32[]{:S(2)}) collective-permute-start(bf16[4,208,128]{2,1,0:T(8,128)(2,1)S(1)} %get-tuple-element.71), channel_id=1, source_target_pairs={{0,16},{16,0},{1,17},{17,1},{2,18},{18,2},{3,19},{19,3},{4,20},{20... | collective-permute-start | bytes 638984 | tf_op jit(solution)/shard_map/ppermute | solution.py:381
  51.1 5.0 %collective-permute-start.20 = (bf16[2,208,128]{2,1,0:T(8,128)(2,1)S(1)}, bf16[2,208,128]{2,1,0:T(8,128)(2,1)S(1)}, u32[]{:S(2)}, u32[]{:S(2)}) collective-permute-start(bf16[2,208,128]{2,1,0:T(8,128)(2,1)S(1)} %get-tuple-element.73), channel_id=1, source_target_pairs={{0,2},{1,3},{2,0},{3,1},{4,6},{5,7},{6,4},{7,5},{8,10},{9,11},{10,... | collective-permute-start | bytes 319496 | tf_op jit(solution)/shard_map/ppermute | solution.py:379
  51.7 6.4 %collective-permute-start.22 = (bf16[1,208,128]{2,1,0:T(8,128)(2,1)S(1)}, bf16[1,208,128]{2,1,0:T(8,128)(2,1)S(1)}, u32[]{:S(2)}, u32[]{:S(2)}) collective-permute-start(bf16[1,208,128]{2,1,0:T(8,128)(2,1)S(1)} %get-tuple-element.77), channel_id=1, source_target_pairs={{0,12},{1,13},{2,14},{3,15},{4,8},{5,9},{6,10},{7,11},{8,4},{9,5},... | collective-permute-start | bytes 159752 | tf_op jit(solution)/shard_map/ppermute | solution.py:379
  54.2 6.3 %collective-permute-start.23 = (bf16[1,208,128]{2,1,0:T(8,128)(2,1)S(1)}, bf16[1,208,128]{2,1,0:T(8,128)(2,1)S(1)}, u32[]{:S(2)}, u32[]{:S(2)}) collective-permute-start(bf16[1,208,128]{2,1,0:T(8,128)(2,1)S(1)} %get-tuple-element.78), channel_id=1, source_target_pairs={{0,8},{1,9},{2,10},{3,11},{4,12},{5,13},{6,14},{7,15},{8,0},{9,1},... | collective-permute-start | bytes 159752 | tf_op jit(solution)/shard_map/ppermute | solution.py:379
  54.4 6.0 %collective-permute-start.24 = (bf16[1,208,128]{2,1,0:T(8,128)(2,1)S(1)}, bf16[1,208,128]{2,1,0:T(8,128)(2,1)S(1)}, u32[]{:S(2)}, u32[]{:S(2)}) collective-permute-start(bf16[1,208,128]{2,1,0:T(8,128)(2,1)S(1)} %get-tuple-element.79), channel_id=1, source_target_pairs={{0,4},{1,5},{2,6},{3,7},{4,0},{5,1},{6,2},{7,3},{8,12},{9,13},{10,... | collective-permute-start | bytes 159752 | tf_op jit(solution)/shard_map/ppermute | solution.py:379
  56.7 5.6 %collective-permute-start.21 = (bf16[1,208,128]{2,1,0:T(8,128)(2,1)S(1)}, bf16[1,208,128]{2,1,0:T(8,128)(2,1)S(1)}, u32[]{:S(2)}, u32[]{:S(2)}) collective-permute-start(bf16[1,208,128]{2,1,0:T(8,128)(2,1)S(1)} %get-tuple-element.76), channel_id=1, source_target_pairs={{0,8},{1,9},{2,10},{3,11},{4,12},{5,13},{6,14},{7,15},{8,0},{9,1},... | collective-permute-start | bytes 159752 | tf_op jit(solution)/shard_map/ppermute | solution.py:379
  62.9 4.2 %collective-permute-start.25 = (bf16[208,128]{1,0:T(8,128)(2,1)S(1)}, bf16[208,128]{1,0:T(8,128)(2,1)S(1)}, u32[]{:S(2)}, u32[]{:S(2)}) collective-permute-start(bf16[208,128]{1,0:T(8,128)(2,1)S(1)} %get-tuple-element.81), channel_id=1, source_target_pairs={{0,16},{16,0},{1,17},{17,1},{2,18},{18,2},{3,19},{19,3},{4,20},{20... | collective-permute-start | bytes 159752 | tf_op jit(solution)/shard_map/ppermute | solution.py:381

commit v11 on v10

--- a/solution.py
+++ b/solution.py
@@ -287,53 +287,57 @@
         out[:, k] = nt_dot(tokens[k], weight[k]).astype(BF16).reshape(images, count, dim)
 
 
-def take(part, block, at, columns=None):
-    size = part[0].shape[0]
-    return part[block // size][block % size + at, :, slice(None) if columns is None else columns].astype(F32)
-
-
-def round_kernel(jobs, flags, *refs):
-    ins, outs, dp = list(refs[: sum(sum(job[0]) for job in jobs)]), refs, flags[DP]
-    outs = list(refs[len(ins) :])
-    for sizes, at, bits, by_columns, heights in jobs:
-        parts = []
-        for size in sizes:
-            parts.append(ins[:size])
-            del ins[:size]
+def take(part, block, at, columns=slice(None)):
+    pieces, start = part
+    size = pieces[0].shape[0]
+    if len(pieces) > 1:
+        return pieces[block // size][block % size + at, :, columns].astype(F32)
+    return pieces[0][start + block + at, :, columns].astype(F32)
+
+
+def regroup(refs, plan):
+    refs, parts = list(refs), []
+    for size, start in plan:
+        parts.append((refs[:size], start))
+        del refs[:size]
+    return parts, refs
+
+
+def round_kernel(jobs, places, flags, *refs):
+    dp = flags[DP]
+    work = []
+    for plan, at, bits, by_columns in jobs:
+        parts, refs = regroup(refs, plan)
+        work.append((parts, at, bits, by_columns))
+    for j, (parts, at, bits, by_columns) in enumerate(work):
         span = 1 << bits
         mine = 0
         for b in range(bits):
             mine = mine + flags[BITS + at + b] * (1 << b)
-        last = span * (2 if by_columns else 1)
-        for n in [0] + list(range(last - 1, 0, -1)):
+        for n in range(span * (2 if by_columns else 1)):
             across, apart = n // span, n % span
-            pieces = outs[: len(heights) if n else 1]
-            del outs[: len(pieces)]
-            count, _, width = pieces[0].shape
-            columns = None
+            index, start, count, cut = places[j, n]
+            columns, width = slice(None), refs[index].shape[2]
             if by_columns:
                 columns = pl.ds(pl.multiple_of((dp ^ across) * width, width), width)
-            for q in range(count):
+            for q in range(count * cut):
+                out = refs[index + q // count]
                 total = take(parts[0], q * span, mine ^ apart, columns)
                 for other in parts[1:]:
                     total = total + take(other, q * span, mine ^ apart, columns)
-                start = 0
-                for piece in pieces:
-                    piece[q] = total[start : start + piece.shape[1]].astype(piece.dtype)
-                    start += piece.shape[1]
-
-
-def last_kernel(early_parts, flags, *refs):
-    ins, (sent, kept) = list(refs[:-2]), refs[-2:]
+                out[start + q % count] = total.astype(out.dtype)
+
+
+def last_kernel(early_plan, late_plan, flags, *refs):
     first = flags[DP] == 0
     sums = []
-    for sizes in (early_parts, (1,) * (len(ins) - sum(early_parts))):
-        total = 0.0
-        for size in sizes:
-            rows = [piece[0].astype(F32) for piece in ins[:size]]
-            total = total + (jnp.concatenate(rows, axis=0) if size > 1 else rows[0])
-            del ins[:size]
+    for plan in (early_plan, late_plan):
+        parts, refs = regroup(refs, plan)
+        total = take(parts[0], 0, 0)
+        for other in parts[1:]:
+            total = total + take(other, 0, 0)
         sums.append(total)
+    sent, kept = refs
     sent[...] = jnp.where(first, sums[0], sums[1]).astype(BF16)
     kept[...] = jnp.where(first, sums[1], sums[0])
 
@@ -396,34 +400,44 @@
         sent = [sent[n * size : (n + 1) * size] for n in range(pieces)]
     else:
         kept, *sent = dealt
-    return [[kept], [xor_move(piece, 1, False) for piece in sent]]
-
-
-def deal_rounds(jobs, flags, after=()):
-    outs, plans, operands = [], [], [flags]
-    for parts, at, bits, by_columns, cut in jobs:
+    return [([kept], 0), ([xor_move(piece, 1, False) for piece in sent], 0)]
+
+
+def flat(parts):
+    return [piece for pieces, _ in parts for piece in pieces], [(len(pieces), start) for pieces, start in parts]
+
+
+def deal_rounds(jobs, flags, after=(), cut=1):
+    outs, plans, places, moves, operands = [], [], {}, {}, [flags]
+    for j, (parts, at, bits, by_columns) in enumerate(jobs):
         span = 1 << bits
-        count, rows, channels = parts[0][0].shape
-        channels = channels // 2 if by_columns else channels
-        tiles = rows // 16
-        heights = [rows]
-        if rows % 16 == 0 and cut > 1:
-            heights = [16 * (tiles * (n + 1) // cut - tiles * n // cut) for n in range(cut)]
-        for n in range(span * (2 if by_columns else 1)):
+        count, rows, channels = parts[0][0][0].shape
+        count, channels = count // span, channels // 2 if by_columns else channels
+        for n in [0] + list(range(span * (2 if by_columns else 1) - 1, 0, -1)):
+            move = (n % span) << at, n >= span
             if n == 0:
-                outs.append(sds(count // span, rows, channels, dtype=F32))
+                outs.append(sds(count, rows, channels, dtype=F32))
+                places[j, n] = len(outs) - 1, 0, count, 1
+            elif move in moves:
+                index = moves[move]
+                places[j, n] = index, outs[index].shape[0], count, 1
+                outs[index] = sds(outs[index].shape[0] + count, rows, channels)
             else:
-                outs += [sds(count // span, height, channels) for height in heights]
-        plans.append((tuple(len(part) for part in parts), at, bits, by_columns, tuple(heights)))
-        operands += [piece for part in parts for piece in part]
-    pieces = list(vmem_call(functools.partial(round_kernel, plans), outs, operands, after=after))
-    token, sums = pieces[0], []
-    for _, at, bits, by_columns, heights in plans:
-        span = 1 << bits
-        parts = [[pieces.pop(0)]]
-        for n in range(span * (2 if by_columns else 1) - 1, 0, -1):
-            parts.append([xor_move(pieces.pop(0), (n % span) << at, n >= span) for _ in heights])
-        sums.append(parts)
+                moves[move] = len(outs)
+                places[j, n] = len(outs), 0, count // cut, cut
+                outs += [sds(count // cut, rows, channels)] * cut
+        pieces, plan = flat(parts)
+        plans.append((plan, at, bits, by_columns))
+        operands += pieces
+    made = list(vmem_call(functools.partial(round_kernel, plans, places), outs, operands, after=after))
+    token = made[0]
+    for (apart, across), index in moves.items():
+        for n in range(index, index + cut):
+            made[n] = xor_move(made[n], apart, across)
+    sums = []
+    for j in range(len(jobs)):
+        here = [places[key] for key in places if key[0] == j]
+        sums.append([(made[index : index + pieces], start) for index, start, _, pieces in here])
     return sums, token
 
 
@@ -513,7 +527,7 @@
         scratch=(full, pltpu.VMEM((patches, channels), BF16)),
         flops=conv_flops,
     )
-    (early_parts,), before = deal_rounds([(core_sum(early, position % 2, pieces, True), 2, 1, False, 1)], flags)
+    (early_parts,), before = deal_rounds([(core_sum(early, position % 2, pieces, True), 1, 0, True)], flags)
     proj_flops = 2 * images * tokens * depths * dim * channels
     *terms, token_grad = vmem_call(
         proj_term_kernel,
@@ -524,18 +538,20 @@
         after=(before,),
     )
     (late_parts,), before = deal_rounds(
-        [(core_sum(terms, position % 2, pieces, False), 1, 1, True, 1)], flags, after=(token_grad,)
-    )
-    at, early_rounds = 2, [(1, 0, True), (1, 1, False)] + [(bit, 1, False) for bit in range(3, bits)]
+        [(core_sum(terms, position % 2, pieces, False), 1, 1, False)], flags, after=(token_grad,), cut=2
+    )
+    (early_parts,), before = deal_rounds([(early_parts, 2, 1, False)], flags, after=(before,))
+    (late_parts,), before = deal_rounds([(late_parts, 1, 0, True)], flags, after=(before,))
+    (early_parts,), before = deal_rounds([(early_parts, 1, 1, False)], flags, after=(before,))
+    at = 2
     while at < bits:
         step = min(2, bits - at)
-        (early_parts,), before = deal_rounds([(early_parts, *early_rounds.pop(0), 1)], flags, after=(before,))
+        if at > 2 and step == 2:
+            (early_parts,), before = deal_rounds([(early_parts, at, 1, False)], flags, after=(before,))
         (late_parts, early_parts), before = deal_rounds(
-            [(late_parts, at, step, False, 1), (early_parts, *early_rounds.pop(0), 1)], flags, after=(before,)
+            [(late_parts, at, step, False), (early_parts, at + step - 1, 1, False)], flags, after=(before,)
         )
         at += step
-    while early_rounds:
-        (early_parts,), before = deal_rounds([(early_parts, *early_rounds.pop(0), 1)], flags, after=(before,))
     feature_grad = vmem_call(
         feat_grad_kernel,
         sds(images, depths, tokens, dim),
@@ -544,10 +560,12 @@
         flops=proj_flops,
         after=(before,),
     )
+    early_pieces, early_plan = flat(early_parts)
+    late_pieces, late_plan = flat(late_parts)
     sent, kept = vmem_call(
-        functools.partial(last_kernel, tuple(len(part) for part in early_parts)),
+        functools.partial(last_kernel, early_plan, late_plan),
         [sds(block_rows, channels // 2), sds(block_rows, channels // 2, dtype=F32)],
-        [flags] + [piece for part in early_parts + late_parts for piece in part],
+        [flags] + early_pieces + late_pieces,
     )
     other = xor_move(sent, 0, True)
     scale = 1.0 / math.sqrt(images * lax.axis_size("dp") * tokens * tile_count)

time: 68.5 us -> 68.5 us (level)
  starting transfers between devices: 25.4 us -> 21.9 us
  waiting for transfers between devices: 21.7 us -> 24.7 us
    ppermute x19, waiting for transfers between devices: 11.5 us -> 18.1 us  [xor_move(): return lax.ppermute(block, 'tile', [(t, t ^ apart) for t in range(tiles)])]
    ppermute x3, waiting for transfers between devices: 9.03 us -> 5.53 us  [xor_move(): return lax.ppermute(block, 'dp', [(0, 1), (1, 0)])]
    ppermute x1 -> x0, starting transfers between devices: 2.52 us -> none  [xor_move(): return lax.ppermute(block, ('dp', 'tile'), route)]
    pallas_call x15 -> x16, Pallas kernels: 16.1 us -> 16.6 us  [vmem_call(): pl.pallas_call(run, out_shape=out_shape, in_specs=specs, out_specs=jax.tr...]
  transfers between devices with their start and end apart: 26 -> 25, of which waited for: 14 -> 16; matrix products, arithmetic and copies ran while one was open for 0% -> 0% of each run, Pallas kernels for 16% -> 17%
where the time goes in v11:
time: 68.5 us; the launch traced here: 68.3 us
  waiting for transfers between devices  24.7 us (36%)
  starting transfers between devices  21.9 us (32%)
  Pallas kernels  16.6 us (24%)
  local copies, waits for them, and re-layouts  3 us (4%)
  other arithmetic  1.19 us (2%)
  between operations  0.89 us (1%)
    ppermute x19, waiting for transfers between devices, xor_move(): return lax.ppermute(block, 'tile', [(t, t ^ apart) for t in range(tiles)])  18.1 us
    pallas_call x16, Pallas kernels, vmem_call(): pl.pallas_call(run, out_shape=out_shape, in_specs=specs, out_specs=jax.tr...  16.6 us
    ppermute x19, starting transfers between devices, xor_move(): return lax.ppermute(block, 'tile', [(t, t ^ apart) for t in range(tiles)])  12.6 us
    ppermute x3, starting transfers between devices, swap(): return lax.ppermute(block, 'tile', tile_route(row_pairs, col_pairs, rows))  6.19 us
    ppermute x3, waiting for transfers between devices, xor_move(): return lax.ppermute(block, 'dp', [(0, 1), (1, 0)])  5.53 us
    ppermute x3, starting transfers between devices, xor_move(): return lax.ppermute(block, 'dp', [(0, 1), (1, 0)])  3.14 us
    unnamed x12, local copies, waits for them, and re-layouts  2.91 us
  transfers between devices with their start and end apart: 25, of which 16 were waited for; matrix products, arithmetic and copies ran while one was open for 0% of the time, Pallas kernels for 17%

profile of v11, /device:TPU:0, one launch (start us, length us, event | category | flops | bytes accessed | tf_op | source)
XLA Modules:
  0.0 68.3 jit_solution(1899870290508452897)
XLA Ops:
  0.7 1.2 %broadcast_select_fusion = (bf16[4,16,4,256]{3,2,1,0:T(4,128)(2,1)S(1)}, bf16[4,16,4,256]{3,2,1,0:T(4,128)(2,1)S(1)}) fusion(pred[]{:T(512)S(6)} %eq.27, bf16[4,16,32,256]{3,2,1,0:T(8,128)(2,1)} %refs_0_.1), kind=kLoop, calls=%fused_computation | loop fusion | flops 131072 | bytes 524289 | tf_op jit(solution)/shard_map/jit(_where)/select_n | solution.py:470
  1.9 3.1 %collective-permute-start.1 = (bf16[4,16,4,256]{3,2,1,0:T(4,128)(2,1)S(1)}, bf16[4,16,4,256]{3,2,1,0:T(4,128)(2,1)S(1)}, u32[]{:S(2)}, u32[]{:S(2)}) collective-permute-start(bf16[4,16,4,256]{3,2,1,0:T(4,128)(2,1)S(1)} %get-tuple-element.82), channel_id=1, source_target_pairs={{1,3},{3,1},{2,6},{6,2},{7,5},{5,7},{0,4},{4,0},{9,11},{11,9},{10,... | collective-permute-start | bytes 393224 | tf_op jit(solution)/shard_map/ppermute | solution.py:466
  4.9 0.0 collective-permute-start
  4.9 1.2 %copy-done.3 = bf16[4,16,32,256]{3,2,1,0:T(8,128)(2,1)S(1)} copy-done((bf16[4,16,32,256]{3,2,1,0:T(8,128)(2,1)S(1)}, bf16[4,16,32,256]{3,2,1,0:T(8,128)(2,1)}, u32[]{:S(2)}) %copy-start.3) | copy-done | bytes 1048600
  6.2 0.5 shard_map.68.refs_1_
  6.7 0.1 stack.71.refs_0_
  6.8 1.1 %collective-permute-done.1.refs_3_ = bf16[4,16,4,256]{3,2,1,0:T(4,128)(2,1)S(1)} collective-permute-done((bf16[4,16,4,256]{3,2,1,0:T(4,128)(2,1)S(1)}, bf16[4,16,4,256]{3,2,1,0:T(4,128)(2,1)S(1)}, u32[]{:S(2)}, u32[]{:S(2)}) %collective-permute-start.1) | collective-permute-done | bytes 131104 | tf_op jit(solution)/shard_map/ppermute | solution.py:466
  7.9 0.8 %shard_map.69 = (bf16[144,256]{1,0:T(8,128)(2,1)S(1)}, f32[4,6,16,256]{3,2,1,0:T(8,128)S(1)}, f32[4,6,2,256]{3,2,1,0:T(2,128)S(1)}) custom-call(s32[13]{0:T(128)S(1)} %stack.71.refs_0_, f32[4,16,24,256]{3,2,1,0:T(8,128)S(1)} %shard_map.68.refs_1_, bf16[4,16,4,256]{3,2,1,0:T(4,128)(2,1)S(1)} %collective-permute-done.refs_2_, ...), custom_call_target="tpu_custom_call" | custom-call | bytes 2351156 | tf_op jit(solution)/shard_map/pallas_call | solution.py:364
  8.7 3.1 %collective-permute-start.2 = (bf16[144,256]{1,0:T(8,128)(2,1)S(1)}, bf16[144,256]{1,0:T(8,128)(2,1)S(1)}, u32[]{:S(2)}, u32[]{:S(2)}) collective-permute-start(bf16[144,256]{1,0:T(8,128)(2,1)S(1)} %get-tuple-element.42.refs_5_), channel_id=1, source_target_pairs={{0,8},{1,9},{3,11},{2,10},{6,14},{7,15},{5,13},{4,12},{8,0},{9,1},... | collective-permute-start | bytes 221192 | tf_op jit(solution)/shard_map/ppermute | solution.py:466
  11.8 1.7 %copy-done = bf16[2,3,3,256,256]{4,3,2,1,0:T(8,128)(2,1)S(1)} copy-done((bf16[2,3,3,256,256]{4,3,2,1,0:T(8,128)(2,1)S(1)}, bf16[2,3,3,256,256]{4,3,2,1,0:T(8,128)(2,1)}, u32[]{:S(2)}) %copy-start) | copy-done | bytes 2359320
  13.4 2.4 %shard_map.70 = (bf16[3,640,256]{2,1,0:T(8,128)(2,1)S(1)}, f32[2,512,256]{2,1,0:T(8,128)S(1)}) custom-call(s32[13]{0:T(128)S(1)} %stack.71.refs_0_, f32[4,16,24,256]{3,2,1,0:T(8,128)S(1)} %shard_map.68.refs_1_, bf16[4,16,4,256]{3,2,1,0:T(4,128)(2,1)S(1)} %collective-permute-done.refs_2_, bf16[4,16,4,256]{3,2,1,0:T(4,128)(2,1)S(1)} %collective-permute-done.1.refs_3_, ...), custom_call_target="tpu_custom_call" | custom-call | flops 1207959552 | bytes 6225972 | tf_op jit(solution)/shard_map/pallas_call | solution.py:364
  15.8 0.0 copy-start.5
  15.9 1.6 %shard_map.71 = (bf16[2,2,64,256]{3,2,1,0:T(8,128)(2,1)S(1)}, bf16[2,2,64,256]{3,2,1,0:T(8,128)(2,1)S(1)}, bf16[2,2,64,256]{3,2,1,0:T(8,128)(2,1)S(1)}, bf16[2,2...) custom-call(s32[13]{0:T(128)S(1)} %stack.71.refs_0_, ...), custom_call_target="tpu_custom_call", output_to_operand_aliasing={{4}: (4, {})} | custom-call | flops 301989888 | bytes 6414388 | tf_op jit(solution)/shard_map/pallas_call | solution.py:364
  17.5 1.6 %collective-permute-start.3 = (bf16[2,2,64,256]{3,2,1,0:T(8,128)(2,1)S(1)}, bf16[2,2,64,256]{3,2,1,0:T(8,128)(2,1)S(1)}, u32[]{:S(2)}, u32[]{:S(2)}) collective-permute-start(bf16[2,2,64,256]{3,2,1,0:T(8,128)(2,1)S(1)} %get-tuple-element.48), channel_id=1, source_target_pairs={{0,2},{1,3},{2,0},{3,1},{4,6},{5,7},{6,4},{7,5},{8,10},{9,11},{10,... | collective-permute-start | bytes 393224 | tf_op jit(solution)/shard_map/ppermute | solution.py:383
  19.1 1.6 %collective-permute-start.4 = (bf16[2,2,64,256]{3,2,1,0:T(8,128)(2,1)S(1)}, bf16[2,2,64,256]{3,2,1,0:T(8,128)(2,1)S(1)}, u32[]{:S(2)}, u32[]{:S(2)}) collective-permute-start(bf16[2,2,64,256]{3,2,1,0:T(8,128)(2,1)S(1)} %get-tuple-element.49), channel_id=1, source_target_pairs={{0,4},{1,5},{2,6},{3,7},{4,0},{5,1},{6,2},{7,3},{8,12},{9,13},{10,... | collective-permute-start | bytes 393224 | tf_op jit(solution)/shard_map/ppermute | solution.py:383
  20.7 0.4 collective-permute-start.5
  21.1 2.1 %shard_map.73 = (bf16[8,208,256]{2,1,0:T(8,128)(2,1)S(1)}, bf16[2,208,256]{2,1,0:T(8,128)(2,1)S(1)}, bf16[2,208,256]{2,1,0:T(8,128)(2,1)S(1)}, bf16[2,208,256]{2...) custom-call(s32[13]{0:T(128)S(1)} %stack.71.refs_0_, ...), custom_call_target="tpu_custom_call" | custom-call | flops 1207959552 | bytes 3866676 | tf_op jit(solution)/shard_map/pallas_call | solution.py:364
  23.1 0.0 copy-start.2
  23.1 0.1 collective-permute-start.7
  23.2 0.5 collective-permute-start.8
  23.7 0.0 collective-permute-done.3.refs_1_.refs_2_
  23.7 0.1 collective-permute-start.9
  23.8 0.6 collective-permute-done.4.refs_2_.refs_3_
  24.4 0.0 collective-permute-start.10
  24.4 2.2 %collective-permute-done.5.refs_3_.refs_4_ = bf16[2,2,64,256]{3,2,1,0:T(8,128)(2,1)S(1)} collective-permute-done((bf16[2,2,64,256]{3,2,1,0:T(8,128)(2,1)S(1)}, bf16[2,2,64,256]{3,2,1,0:T(8,128)(2,1)S(1)}, u32[]{:S(2)}, u32[]{:S(2)}) %collective-permute-start.5) | collective-permute-done | bytes 131104 | tf_op jit(solution)/shard_map/ppermute | solution.py:383
  26.5 0.1 collective-permute-start.6
  26.6 0.0 collective-permute-done.7.refs_2_
  26.7 0.7 %shard_map.74 = (f32[8,208,128]{2,1,0:T(8,128)S(1)}, bf16[8,208,128]{2,1,0:T(8,128)(2,1)S(1)}) custom-call(s32[13]{0:T(128)S(1)} %stack.71.refs_0_, bf16[8,208,256]{2,1,0:T(8,128)(2,1)S(1)} %get-tuple-element.53.refs_1_, bf16[2,208,256]{2,1,0:T(8,128)(2,1)S(1)} %collective-permute-done.7.refs_2_, bf16[2,208,256]{2,1,0:T(8,128)(2,1)S(1)} %collective-permute-done.8.refs_3_, ...), custom_call_target="tpu_custom_call" | custom-call | bytes 2981940 | tf_op jit(solution)/shard_map/pallas_call | solution.py:364
  27.4 1.6 %collective-permute-start.17 = (bf16[8,208,128]{2,1,0:T(8,128)(2,1)S(1)}, bf16[8,208,128]{2,1,0:T(8,128)(2,1)S(1)}, u32[]{:S(2)}, u32[]{:S(2)}) collective-permute-start(bf16[8,208,128]{2,1,0:T(8,128)(2,1)S(1)} %get-tuple-element.68), channel_id=1, source_target_pairs={{0,16},{16,0},{1,17},{17,1},{2,18},{18,2},{3,19},{19,3},{4,20},{20... | collective-permute-start | bytes 1277960 | tf_op jit(solution)/shard_map/ppermute | solution.py:385
  29.0 1.5 %shard_map.75 = (bf16[8,208,256]{2,1,0:T(8,128)(2,1)S(1)}, bf16[2,208,256]{2,1,0:T(8,128)(2,1)S(1)}, bf16[2,208,256]{2,1,0:T(8,128)(2,1)S(1)}, bf16[2,208,256]{2...) custom-call(s32[13]{0:T(128)S(1)} %stack.71.refs_0_, ...), custom_call_target="tpu_custom_call" | custom-call | flops 536870912 | bytes 5767220 | tf_op jit(solution)/shard_map/pallas_call | solution.py:364
  30.4 0.3 collective-permute-start.11
  30.7 0.3 collective-permute-start.12
  31.0 0.2 collective-permute-start.13
  31.2 0.3 collective-permute-start.14
  31.5 0.4 collective-permute-done.11.refs_2_
  32.0 0.3 collective-permute-done.12.refs_3_
  32.3 0.3 collective-permute-done.13.refs_4_
  32.6 0.3 collective-permute-done.14.refs_5_
  32.9 0.7 %shard_map.76 = (f32[4,208,256]{2,1,0:T(8,128)S(1)}, bf16[2,208,256]{2,1,0:T(8,128)(2,1)S(1)}, bf16[2,208,256]{2,1,0:T(8,128)(2,1)S(1)}) custom-call(s32[13]{0:T(128)S(1)} %stack.71.refs_0_, bf16[8,208,256]{2,1,0:T(8,128)(2,1)S(1)} %get-tuple-element.60.refs_1_, bf16[2,208,256]{2,1,0:T(8,128)(2,1)S(1)} %collective-permute-done.11.refs_2_, ...), custom_call_target="tpu_custom_call" | custom-call | bytes 2981940 | tf_op jit(solution)/shard_map/pallas_call | solution.py:364
  33.6 0.8 %collective-permute-start.15 = (bf16[2,208,256]{2,1,0:T(8,128)(2,1)S(1)}, bf16[2,208,256]{2,1,0:T(8,128)(2,1)S(1)}, u32[]{:S(2)}, u32[]{:S(2)}) collective-permute-start(bf16[2,208,256]{2,1,0:T(8,128)(2,1)S(1)} %get-tuple-element.66), channel_id=1, source_target_pairs={{0,2},{1,3},{2,0},{3,1},{4,6},{5,7},{6,4},{7,5},{8,10},{9,11},{10,... | collective-permute-start | bytes 638984 | tf_op jit(solution)/shard_map/ppermute | solution.py:383
  34.4 1.3 %collective-permute-start.16 = (bf16[2,208,256]{2,1,0:T(8,128)(2,1)S(1)}, bf16[2,208,256]{2,1,0:T(8,128)(2,1)S(1)}, u32[]{:S(2)}, u32[]{:S(2)}) collective-permute-start(bf16[2,208,256]{2,1,0:T(8,128)(2,1)S(1)} %get-tuple-element.67), channel_id=1, source_target_pairs={{0,2},{1,3},{2,0},{3,1},{4,6},{5,7},{6,4},{7,5},{8,10},{9,11},{10,... | collective-permute-start | bytes 638984 | tf_op jit(solution)/shard_map/ppermute | solution.py:383
  35.7 4.0 %collective-permute-done.17.refs_2_ = bf16[8,208,128]{2,1,0:T(8,128)(2,1)S(1)} collective-permute-done((bf16[8,208,128]{2,1,0:T(8,128)(2,1)S(1)}, bf16[8,208,128]{2,1,0:T(8,128)(2,1)S(1)}, u32[]{:S(2)}, u32[]{:S(2)}) %collective-permute-start.17) | collective-permute-done | bytes 426016 | tf_op jit(solution)/shard_map/ppermute | solution.py:385
  39.7 0.6 shard_map.77
  40.3 0.8 %collective-permute-start.19 = (bf16[4,208,128]{2,1,0:T(8,128)(2,1)S(1)}, bf16[4,208,128]{2,1,0:T(8,128)(2,1)S(1)}, u32[]{:S(2)}, u32[]{:S(2)}) collective-permute-start(bf16[4,208,128]{2,1,0:T(8,128)(2,1)S(1)} %get-tuple-element.72), channel_id=1, source_target_pairs={{0,4},{1,5},{2,6},{3,7},{4,0},{5,1},{6,2},{7,3},{8,12},{9,13},{10,... | collective-permute-start | bytes 638984 | tf_op jit(solution)/shard_map/ppermute | solution.py:383
  41.1 0.7 collective-permute-done.15.refs_2_
  41.8 3.8 %collective-permute-done.16.refs_3_ = bf16[2,208,256]{2,1,0:T(8,128)(2,1)S(1)} collective-permute-done((bf16[2,208,256]{2,1,0:T(8,128)(2,1)S(1)}, bf16[2,208,256]{2,1,0:T(8,128)(2,1)S(1)}, u32[]{:S(2)}, u32[]{:S(2)}) %collective-permute-start.16) | collective-permute-done | bytes 213024 | tf_op jit(solution)/shard_map/ppermute | solution.py:383
  45.6 0.6 shard_map.78
  46.3 0.7 %collective-permute-start.18 = (bf16[4,208,128]{2,1,0:T(8,128)(2,1)S(1)}, bf16[4,208,128]{2,1,0:T(8,128)(2,1)S(1)}, u32[]{:S(2)}, u32[]{:S(2)}) collective-permute-start(bf16[4,208,128]{2,1,0:T(8,128)(2,1)S(1)} %get-tuple-element.71), channel_id=1, source_target_pairs={{0,16},{16,0},{1,17},{17,1},{2,18},{18,2},{3,19},{19,3},{4,20},{20... | collective-permute-start | bytes 638984 | tf_op jit(solution)/shard_map/ppermute | solution.py:385
  47.0 0.2 collective-permute-done.19.refs_2_
  47.2 0.6 shard_map.79
  47.8 0.8 %collective-permute-start.20 = (bf16[2,208,128]{2,1,0:T(8,128)(2,1)S(1)}, bf16[2,208,128]{2,1,0:T(8,128)(2,1)S(1)}, u32[]{:S(2)}, u32[]{:S(2)}) collective-permute-start(bf16[2,208,128]{2,1,0:T(8,128)(2,1)S(1)} %get-tuple-element.74), channel_id=1, source_target_pairs={{0,2},{1,3},{2,0},{3,1},{4,6},{5,7},{6,4},{7,5},{8,10},{9,11},{10,... | collective-permute-start | bytes 319496 | tf_op jit(solution)/shard_map/ppermute | solution.py:383
  48.6 4.0 %collective-permute-done.20.refs_4_ = bf16[2,208,128]{2,1,0:T(8,128)(2,1)S(1)} collective-permute-done((bf16[2,208,128]{2,1,0:T(8,128)(2,1)S(1)}, bf16[2,208,128]{2,1,0:T(8,128)(2,1)S(1)}, u32[]{:S(2)}, u32[]{:S(2)}) %collective-permute-start.20) | collective-permute-done | bytes 106528 | tf_op jit(solution)/shard_map/ppermute | solution.py:383
  52.6 0.3 collective-permute-done.18.refs_2_
  52.9 0.6 shard_map.80
  53.5 1.9 %collective-permute-start.21 = (bf16[2,208,128]{2,1,0:T(8,128)(2,1)S(1)}, bf16[2,208,128]{2,1,0:T(8,128)(2,1)S(1)}, u32[]{:S(2)}, u32[]{:S(2)}) collective-permute-start(bf16[2,208,128]{2,1,0:T(8,128)(2,1)S(1)} %get-tuple-element.77), channel_id=1, source_target_pairs={{0,8},{1,9},{2,10},{3,11},{4,12},{5,13},{6,14},{7,15},{8,0},{9,1},... | collective-permute-start | bytes 319496 | tf_op jit(solution)/shard_map/ppermute | solution.py:383
  55.4 1.3 %collective-permute-start.22 = (bf16[1,208,128]{2,1,0:T(8,128)(2,1)S(1)}, bf16[1,208,128]{2,1,0:T(8,128)(2,1)S(1)}, u32[]{:S(2)}, u32[]{:S(2)}) collective-permute-start(bf16[1,208,128]{2,1,0:T(8,128)(2,1)S(1)} %get-tuple-element.78), channel_id=1, source_target_pairs={{0,12},{1,13},{2,14},{3,15},{4,8},{5,9},{6,10},{7,11},{8,4},{9,5},... | collective-permute-start | bytes 159752 | tf_op jit(solution)/shard_map/ppermute | solution.py:383
  56.7 0.4 collective-permute-start.23
  57.0 4.4 %collective-permute-done.22.refs_4_ = bf16[1,208,128]{2,1,0:T(8,128)(2,1)S(1)} collective-permute-done((bf16[1,208,128]{2,1,0:T(8,128)(2,1)S(1)}, bf16[1,208,128]{2,1,0:T(8,128)(2,1)S(1)}, u32[]{:S(2)}, u32[]{:S(2)}) %collective-permute-start.22) | collective-permute-done | bytes 53280 | tf_op jit(solution)/shard_map/ppermute | solution.py:383
  61.5 0.8 %collective-permute-done.23.refs_6_ = bf16[1,208,128]{2,1,0:T(8,128)(2,1)S(1)} collective-permute-done((bf16[1,208,128]{2,1,0:T(8,128)(2,1)S(1)}, bf16[1,208,128]{2,1,0:T(8,128)(2,1)S(1)}, u32[]{:S(2)}, u32[]{:S(2)}) %collective-permute-start.23) | collective-permute-done | bytes 53280 | tf_op jit(solution)/shard_map/ppermute | solution.py:383
  62.3 0.6 shard_map.82
  62.9 0.8 %collective-permute-start.24 = (bf16[208,128]{1,0:T(8,128)(2,1)S(1)}, bf16[208,128]{1,0:T(8,128)(2,1)S(1)}, u32[]{:S(2)}, u32[]{:S(2)}) collective-permute-start(bf16[208,128]{1,0:T(8,128)(2,1)S(1)} %get-tuple-element.81), channel_id=1, source_target_pairs={{0,16},{16,0},{1,17},{17,1},{2,18},{18,2},{3,19},{19,3},{4,20},{20... | collective-permute-start | bytes 159752 | tf_op jit(solution)/shard_map/ppermute | solution.py:385
  63.7 2.1 %shard_map.81 = bf16[4,2,128,1024]{3,2,1,0:T(8,128)(2,1)} custom-call(bf16[2,512,256]{2,1,0:T(8,128)(2,1)S(1)} %get-tuple-element.59.refs_6_.refs_0_, bf16[2,1024,256]{2,1,0:T(8,128)(2,1)S(1)} %copy-done.4, f32[1,208,128]{2,1,0:T(8,128)S(1)} %get-tuple-element.75.refs_2_.refs_3_), custom_call_target="tpu_custom_call" | custom-call | flops 536870912 | bytes 3670016 | tf_op jit(solution)/shard_map/pallas_call | solution.py:364
  65.8 1.3 %collective-permute-done.24.refs_2_ = bf16[208,128]{1,0:T(8,128)(2,1)S(1)} collective-permute-done((bf16[208,128]{1,0:T(8,128)(2,1)S(1)}, bf16[208,128]{1,0:T(8,128)(2,1)S(1)}, u32[]{:S(2)}, u32[]{:S(2)}) %collective-permute-start.24) | collective-permute-done | bytes 53280 | tf_op jit(solution)/shard_map/ppermute | solution.py:385
  67.1 1.2 %shard_map.83 = f32[208,256]{1,0:T(8,128)} custom-call(s32[13]{0:T(128)S(1)} %stack.71.refs_0_, f32[208,128]{1,0:T(8,128)S(1)} %get-tuple-element.80.refs_1_, bf16[208,128]{1,0:T(8,128)(2,1)S(1)} %collective-permute-done.24.refs_2_), custom_call_target="tpu_custom_call" | custom-call | bytes 372788 | tf_op jit(solution)/shard_map/pallas_call | solution.py:364
  (16 shorter events, 0.1 us)
Async XLA Ops:
  1.9 6.0 %collective-permute-start.1 = (bf16[4,16,4,256]{3,2,1,0:T(4,128)(2,1)S(1)}, bf16[4,16,4,256]{3,2,1,0:T(4,128)(2,1)S(1)}, u32[]{:S(2)}, u32[]{:S(2)}) collective-permute-start(bf16[4,16,4,256]{3,2,1,0:T(4,128)(2,1)S(1)} %get-tuple-element.82), channel_id=1, source_target_pairs={{1,3},{3,1},{2,6},{6,2},{7,5},{5,7},{0,4},{4,0},{9,11},{11,9},{10,... | collective-permute-start | bytes 393224 | tf_op jit(solution)/shard_map/ppermute | solution.py:466
  4.9 3.0 %collective-permute-start = (bf16[4,16,4,256]{3,2,1,0:T(4,128)(2,1)S(1)}, bf16[4,16,4,256]{3,2,1,0:T(4,128)(2,1)S(1)}, u32[]{:S(2)}, u32[]{:S(2)}) collective-permute-start(bf16[4,16,4,256]{3,2,1,0:T(4,128)(2,1)S(1)} %get-tuple-element.83), channel_id=1, source_target_pairs={{0,1},{1,0},{3,2},{2,3},{6,7},{7,6},{5,4},{4,5},{8,9},{9,8},{11,10... | collective-permute-start | bytes 393224 | tf_op jit(solution)/shard_map/ppermute | solution.py:466
  4.9 1.2 %copy-start.3 = (bf16[4,16,32,256]{3,2,1,0:T(8,128)(2,1)S(1)}, bf16[4,16,32,256]{3,2,1,0:T(8,128)(2,1)}, u32[]{:S(2)}) copy-start(bf16[4,16,32,256]{3,2,1,0:T(8,128)(2,1)} %refs_0_.1) | copy-start | bytes 3145732
  8.7 7.2 %collective-permute-start.2 = (bf16[144,256]{1,0:T(8,128)(2,1)S(1)}, bf16[144,256]{1,0:T(8,128)(2,1)S(1)}, u32[]{:S(2)}, u32[]{:S(2)}) collective-permute-start(bf16[144,256]{1,0:T(8,128)(2,1)S(1)} %get-tuple-element.42.refs_5_), channel_id=1, source_target_pairs={{0,8},{1,9},{3,11},{2,10},{6,14},{7,15},{5,13},{4,12},{8,0},{9,1},... | collective-permute-start | bytes 221192 | tf_op jit(solution)/shard_map/ppermute | solution.py:466
  11.8 1.7 %copy-start = (bf16[2,3,3,256,256]{4,3,2,1,0:T(8,128)(2,1)S(1)}, bf16[2,3,3,256,256]{4,3,2,1,0:T(8,128)(2,1)}, u32[]{:S(2)}) copy-start(bf16[2,3,3,256,256]{4,3,2,1,0:T(8,128)(2,1)} %refs_6_.2) | copy-start | bytes 7077892
  13.4 2.4 %copy-start.1 = (bf16[2,3,3,256,256]{4,3,2,1,0:T(8,128)(2,1)S(1)}, bf16[2,3,3,256,256]{4,3,2,1,0:T(8,128)(2,1)}, u32[]{:S(2)}) copy-start(bf16[2,3,3,256,256]{4,3,2,1,0:T(8,128)(2,1)} %refs_6_.2) | copy-start | bytes 7077892
  15.8 5.2 %copy-start.5 = (bf16[4,2,8,16,256]{4,3,2,1,0:T(8,128)(2,1)S(1)}, bf16[4,2,8,16,256]{4,3,2,1,0:T(8,128)(2,1)}, u32[]{:S(2)}) copy-start(bf16[4,2,8,16,256]{4,3,2,1,0:T(8,128)(2,1)} %refs_2_.1) | copy-start | bytes 1572868
  17.5 6.2 %collective-permute-start.3 = (bf16[2,2,64,256]{3,2,1,0:T(8,128)(2,1)S(1)}, bf16[2,2,64,256]{3,2,1,0:T(8,128)(2,1)S(1)}, u32[]{:S(2)}, u32[]{:S(2)}) collective-permute-start(bf16[2,2,64,256]{3,2,1,0:T(8,128)(2,1)S(1)} %get-tuple-element.48), channel_id=1, source_target_pairs={{0,2},{1,3},{2,0},{3,1},{4,6},{5,7},{6,4},{7,5},{8,10},{9,11},{10,... | collective-permute-start | bytes 393224 | tf_op jit(solution)/shard_map/ppermute | solution.py:383
  19.1 5.3 %collective-permute-start.4 = (bf16[2,2,64,256]{3,2,1,0:T(8,128)(2,1)S(1)}, bf16[2,2,64,256]{3,2,1,0:T(8,128)(2,1)S(1)}, u32[]{:S(2)}, u32[]{:S(2)}) collective-permute-start(bf16[2,2,64,256]{3,2,1,0:T(8,128)(2,1)S(1)} %get-tuple-element.49), channel_id=1, source_target_pairs={{0,4},{1,5},{2,6},{3,7},{4,0},{5,1},{6,2},{7,3},{8,12},{9,13},{10,... | collective-permute-start | bytes 393224 | tf_op jit(solution)/shard_map/ppermute | solution.py:383
  20.7 5.9 %collective-permute-start.5 = (bf16[2,2,64,256]{3,2,1,0:T(8,128)(2,1)S(1)}, bf16[2,2,64,256]{3,2,1,0:T(8,128)(2,1)S(1)}, u32[]{:S(2)}, u32[]{:S(2)}) collective-permute-start(bf16[2,2,64,256]{3,2,1,0:T(8,128)(2,1)S(1)} %get-tuple-element.50), channel_id=1, source_target_pairs={{0,6},{1,7},{2,4},{3,5},{4,2},{5,3},{6,0},{7,1},{8,14},{9,15},{10,... | collective-permute-start | bytes 393224 | tf_op jit(solution)/shard_map/ppermute | solution.py:383
  23.1 5.8 %copy-start.2 = (bf16[4,2,128,1024]{3,2,1,0:T(8,128)(2,1)S(1)}, bf16[4,2,128,1024]{3,2,1,0:T(8,128)(2,1)}, u32[]{:S(2)}) copy-start(bf16[4,2,128,1024]{3,2,1,0:T(8,128)(2,1)} %refs_6_.3) | copy-start | bytes 6291460
  23.1 3.5 %collective-permute-start.7 = (bf16[2,208,256]{2,1,0:T(8,128)(2,1)S(1)}, bf16[2,208,256]{2,1,0:T(8,128)(2,1)S(1)}, u32[]{:S(2)}, u32[]{:S(2)}) collective-permute-start(bf16[2,208,256]{2,1,0:T(8,128)(2,1)S(1)} %get-tuple-element.54), channel_id=1, source_target_pairs={{0,1},{1,0},{2,3},{3,2},{4,5},{5,4},{6,7},{7,6},{8,9},{9,8},{10,11... | collective-permute-start | bytes 638984 | tf_op jit(solution)/shard_map/ppermute | solution.py:383
  23.2 3.4 %collective-permute-start.8 = (bf16[2,208,256]{2,1,0:T(8,128)(2,1)S(1)}, bf16[2,208,256]{2,1,0:T(8,128)(2,1)S(1)}, u32[]{:S(2)}, u32[]{:S(2)}) collective-permute-start(bf16[2,208,256]{2,1,0:T(8,128)(2,1)S(1)} %get-tuple-element.55), channel_id=1, source_target_pairs={{0,1},{1,0},{2,3},{3,2},{4,5},{5,4},{6,7},{7,6},{8,9},{9,8},{10,11... | collective-permute-start | bytes 638984 | tf_op jit(solution)/shard_map/ppermute | solution.py:383
  23.7 2.9 %collective-permute-start.9 = (bf16[2,208,256]{2,1,0:T(8,128)(2,1)S(1)}, bf16[2,208,256]{2,1,0:T(8,128)(2,1)S(1)}, u32[]{:S(2)}, u32[]{:S(2)}) collective-permute-start(bf16[2,208,256]{2,1,0:T(8,128)(2,1)S(1)} %get-tuple-element.56), channel_id=1, source_target_pairs={{0,1},{1,0},{2,3},{3,2},{4,5},{5,4},{6,7},{7,6},{8,9},{9,8},{10,11... | collective-permute-start | bytes 638984 | tf_op jit(solution)/shard_map/ppermute | solution.py:383
  24.4 2.3 %collective-permute-start.10 = (bf16[2,208,256]{2,1,0:T(8,128)(2,1)S(1)}, bf16[2,208,256]{2,1,0:T(8,128)(2,1)S(1)}, u32[]{:S(2)}, u32[]{:S(2)}) collective-permute-start(bf16[2,208,256]{2,1,0:T(8,128)(2,1)S(1)} %get-tuple-element.57), channel_id=1, source_target_pairs={{0,1},{1,0},{2,3},{3,2},{4,5},{5,4},{6,7},{7,6},{8,9},{9,8},{10,11... | collective-permute-start | bytes 638984 | tf_op jit(solution)/shard_map/ppermute | solution.py:383
  26.5 2.4 %collective-permute-start.6 = (bf16[4,2,64,256]{3,2,1,0:T(8,128)(2,1)S(1)}, bf16[4,2,64,256]{3,2,1,0:T(8,128)(2,1)S(1)}, u32[]{:S(2)}, u32[]{:S(2)}) collective-permute-start(bf16[4,2,64,256]{3,2,1,0:T(8,128)(2,1)S(1)} %shard_map.72), channel_id=1, source_target_pairs={{0,1},{1,0},{2,3},{3,2},{4,5},{5,4},{6,7},{7,6},{8,9},{9,8},{10,11... | collective-permute-start | bytes 786440 | tf_op jit(solution)/shard_map/ppermute | solution.py:383
  27.4 12.3 %collective-permute-start.17 = (bf16[8,208,128]{2,1,0:T(8,128)(2,1)S(1)}, bf16[8,208,128]{2,1,0:T(8,128)(2,1)S(1)}, u32[]{:S(2)}, u32[]{:S(2)}) collective-permute-start(bf16[8,208,128]{2,1,0:T(8,128)(2,1)S(1)} %get-tuple-element.68), channel_id=1, source_target_pairs={{0,16},{16,0},{1,17},{17,1},{2,18},{18,2},{3,19},{19,3},{4,20},{20... | collective-permute-start | bytes 1277960 | tf_op jit(solution)/shard_map/ppermute | solution.py:385
  30.4 1.5 %collective-permute-start.11 = (bf16[2,208,256]{2,1,0:T(8,128)(2,1)S(1)}, bf16[2,208,256]{2,1,0:T(8,128)(2,1)S(1)}, u32[]{:S(2)}, u32[]{:S(2)}) collective-permute-start(bf16[2,208,256]{2,1,0:T(8,128)(2,1)S(1)} %get-tuple-element.61), channel_id=1, source_target_pairs={{0,1},{1,0},{2,3},{3,2},{4,5},{5,4},{6,7},{7,6},{8,9},{9,8},{10,11... | collective-permute-start | bytes 638984 | tf_op jit(solution)/shard_map/ppermute | solution.py:383
  30.7 1.6 %collective-permute-start.12 = (bf16[2,208,256]{2,1,0:T(8,128)(2,1)S(1)}, bf16[2,208,256]{2,1,0:T(8,128)(2,1)S(1)}, u32[]{:S(2)}, u32[]{:S(2)}) collective-permute-start(bf16[2,208,256]{2,1,0:T(8,128)(2,1)S(1)} %get-tuple-element.62), channel_id=1, source_target_pairs={{0,1},{1,0},{2,3},{3,2},{4,5},{5,4},{6,7},{7,6},{8,9},{9,8},{10,11... | collective-permute-start | bytes 638984 | tf_op jit(solution)/shard_map/ppermute | solution.py:383
  31.0 1.6 %collective-permute-start.13 = (bf16[2,208,256]{2,1,0:T(8,128)(2,1)S(1)}, bf16[2,208,256]{2,1,0:T(8,128)(2,1)S(1)}, u32[]{:S(2)}, u32[]{:S(2)}) collective-permute-start(bf16[2,208,256]{2,1,0:T(8,128)(2,1)S(1)} %get-tuple-element.63), channel_id=1, source_target_pairs={{0,1},{1,0},{2,3},{3,2},{4,5},{5,4},{6,7},{7,6},{8,9},{9,8},{10,11... | collective-permute-start | bytes 638984 | tf_op jit(solution)/shard_map/ppermute | solution.py:383
  31.2 1.7 %collective-permute-start.14 = (bf16[2,208,256]{2,1,0:T(8,128)(2,1)S(1)}, bf16[2,208,256]{2,1,0:T(8,128)(2,1)S(1)}, u32[]{:S(2)}, u32[]{:S(2)}) collective-permute-start(bf16[2,208,256]{2,1,0:T(8,128)(2,1)S(1)} %get-tuple-element.64), channel_id=1, source_target_pairs={{0,1},{1,0},{2,3},{3,2},{4,5},{5,4},{6,7},{7,6},{8,9},{9,8},{10,11... | collective-permute-start | bytes 638984 | tf_op jit(solution)/shard_map/ppermute | solution.py:383
  33.6 8.2 %collective-permute-start.15 = (bf16[2,208,256]{2,1,0:T(8,128)(2,1)S(1)}, bf16[2,208,256]{2,1,0:T(8,128)(2,1)S(1)}, u32[]{:S(2)}, u32[]{:S(2)}) collective-permute-start(bf16[2,208,256]{2,1,0:T(8,128)(2,1)S(1)} %get-tuple-element.66), channel_id=1, source_target_pairs={{0,2},{1,3},{2,0},{3,1},{4,6},{5,7},{6,4},{7,5},{8,10},{9,11},{10,... | collective-permute-start | bytes 638984 | tf_op jit(solution)/shard_map/ppermute | solution.py:383
  34.4 11.2 %collective-permute-start.16 = (bf16[2,208,256]{2,1,0:T(8,128)(2,1)S(1)}, bf16[2,208,256]{2,1,0:T(8,128)(2,1)S(1)}, u32[]{:S(2)}, u32[]{:S(2)}) collective-permute-start(bf16[2,208,256]{2,1,0:T(8,128)(2,1)S(1)} %get-tuple-element.67), channel_id=1, source_target_pairs={{0,2},{1,3},{2,0},{3,1},{4,6},{5,7},{6,4},{7,5},{8,10},{9,11},{10,... | collective-permute-start | bytes 638984 | tf_op jit(solution)/shard_map/ppermute | solution.py:383
  40.3 6.9 %collective-permute-start.19 = (bf16[4,208,128]{2,1,0:T(8,128)(2,1)S(1)}, bf16[4,208,128]{2,1,0:T(8,128)(2,1)S(1)}, u32[]{:S(2)}, u32[]{:S(2)}) collective-permute-start(bf16[4,208,128]{2,1,0:T(8,128)(2,1)S(1)} %get-tuple-element.72), channel_id=1, source_target_pairs={{0,4},{1,5},{2,6},{3,7},{4,0},{5,1},{6,2},{7,3},{8,12},{9,13},{10,... | collective-permute-start | bytes 638984 | tf_op jit(solution)/shard_map/ppermute | solution.py:383
  45.6 18.1 %copy-start.4 = (bf16[2,1024,256]{2,1,0:T(8,128)(2,1)S(1)}, bf16[2,1024,256]{2,1,0:T(8,128)(2,1)}, u32[]{:S(2)}) copy-start(bf16[2,1024,256]{2,1,0:T(8,128)(2,1)} %refs_1_.1) | copy-start | bytes 3145732
  46.3 6.6 %collective-permute-start.18 = (bf16[4,208,128]{2,1,0:T(8,128)(2,1)S(1)}, bf16[4,208,128]{2,1,0:T(8,128)(2,1)S(1)}, u32[]{:S(2)}, u32[]{:S(2)}) collective-permute-start(bf16[4,208,128]{2,1,0:T(8,128)(2,1)S(1)} %get-tuple-element.71), channel_id=1, source_target_pairs={{0,16},{16,0},{1,17},{17,1},{2,18},{18,2},{3,19},{19,3},{4,20},{20... | collective-permute-start | bytes 638984 | tf_op jit(solution)/shard_map/ppermute | solution.py:385
  47.8 4.8 %collective-permute-start.20 = (bf16[2,208,128]{2,1,0:T(8,128)(2,1)S(1)}, bf16[2,208,128]{2,1,0:T(8,128)(2,1)S(1)}, u32[]{:S(2)}, u32[]{:S(2)}) collective-permute-start(bf16[2,208,128]{2,1,0:T(8,128)(2,1)S(1)} %get-tuple-element.74), channel_id=1, source_target_pairs={{0,2},{1,3},{2,0},{3,1},{4,6},{5,7},{6,4},{7,5},{8,10},{9,11},{10,... | collective-permute-start | bytes 319496 | tf_op jit(solution)/shard_map/ppermute | solution.py:383
  53.5 8.8 %collective-permute-start.21 = (bf16[2,208,128]{2,1,0:T(8,128)(2,1)S(1)}, bf16[2,208,128]{2,1,0:T(8,128)(2,1)S(1)}, u32[]{:S(2)}, u32[]{:S(2)}) collective-permute-start(bf16[2,208,128]{2,1,0:T(8,128)(2,1)S(1)} %get-tuple-element.77), channel_id=1, source_target_pairs={{0,8},{1,9},{2,10},{3,11},{4,12},{5,13},{6,14},{7,15},{8,0},{9,1},... | collective-permute-start | bytes 319496 | tf_op jit(solution)/shard_map/ppermute | solution.py:383
  55.4 6.1 %collective-permute-start.22 = (bf16[1,208,128]{2,1,0:T(8,128)(2,1)S(1)}, bf16[1,208,128]{2,1,0:T(8,128)(2,1)S(1)}, u32[]{:S(2)}, u32[]{:S(2)}) collective-permute-start(bf16[1,208,128]{2,1,0:T(8,128)(2,1)S(1)} %get-tuple-element.78), channel_id=1, source_target_pairs={{0,12},{1,13},{2,14},{3,15},{4,8},{5,9},{6,10},{7,11},{8,4},{9,5},... | collective-permute-start | bytes 159752 | tf_op jit(solution)/shard_map/ppermute | solution.py:383
  56.7 5.6 %collective-permute-start.23 = (bf16[1,208,128]{2,1,0:T(8,128)(2,1)S(1)}, bf16[1,208,128]{2,1,0:T(8,128)(2,1)S(1)}, u32[]{:S(2)}, u32[]{:S(2)}) collective-permute-start(bf16[1,208,128]{2,1,0:T(8,128)(2,1)S(1)} %get-tuple-element.79), channel_id=1, source_target_pairs={{0,4},{1,5},{2,6},{3,7},{4,0},{5,1},{6,2},{7,3},{8,12},{9,13},{10,... | collective-permute-start | bytes 159752 | tf_op jit(solution)/shard_map/ppermute | solution.py:383
  62.9 4.2 %collective-permute-start.24 = (bf16[208,128]{1,0:T(8,128)(2,1)S(1)}, bf16[208,128]{1,0:T(8,128)(2,1)S(1)}, u32[]{:S(2)}, u32[]{:S(2)}) collective-permute-start(bf16[208,128]{1,0:T(8,128)(2,1)S(1)} %get-tuple-element.81), channel_id=1, source_target_pairs={{0,16},{16,0},{1,17},{17,1},{2,18},{18,2},{3,19},{19,3},{4,20},{20... | collective-permute-start | bytes 159752 | tf_op jit(solution)/shard_map/ppermute | solution.py:385

commit v12 on v11

--- a/solution.py
+++ b/solution.py
@@ -287,12 +287,19 @@
         out[:, k] = nt_dot(tokens[k], weight[k]).astype(BF16).reshape(images, count, dim)
 
 
-def take(part, block, at, columns=slice(None)):
+def take(part, block, at, columns=slice(None), span=1):
     pieces, start = part
     size = pieces[0].shape[0]
-    if len(pieces) > 1:
+    if len(pieces) == 1:
+        return pieces[0][start + block + at, :, columns].astype(F32)
+    if span <= size:
         return pieces[block // size][block % size + at, :, columns].astype(F32)
-    return pieces[0][start + block + at, :, columns].astype(F32)
+    first = block // size
+    inside = at & size - 1
+    value = pieces[first][inside, :, columns].astype(F32)
+    for n in range(1, span // size):
+        value = jnp.where(at >= n * size, pieces[first + n][inside, :, columns].astype(F32), value)
+    return value
 
 
 def regroup(refs, plan):
@@ -322,9 +329,9 @@
                 columns = pl.ds(pl.multiple_of((dp ^ across) * width, width), width)
             for q in range(count * cut):
                 out = refs[index + q // count]
-                total = take(parts[0], q * span, mine ^ apart, columns)
+                total = take(parts[0], q * span, mine ^ apart, columns, span)
                 for other in parts[1:]:
-                    total = total + take(other, q * span, mine ^ apart, columns)
+                    total = total + take(other, q * span, mine ^ apart, columns, span)
                 out[start + q % count] = total.astype(out.dtype)
 
 
@@ -411,7 +418,8 @@
     outs, plans, places, moves, operands = [], [], {}, {}, [flags]
     for j, (parts, at, bits, by_columns) in enumerate(jobs):
         span = 1 << bits
-        count, rows, channels = parts[0][0][0].shape
+        rows, channels = parts[0][0][0].shape[1:]
+        count = min(sum(piece.shape[0] for piece in pieces) for pieces, _ in parts)
         count, channels = count // span, channels // 2 if by_columns else channels
         for n in [0] + list(range(span * (2 if by_columns else 1) - 1, 0, -1)):
             move = (n % span) << at, n >= span
@@ -540,17 +548,22 @@
     (late_parts,), before = deal_rounds(
         [(core_sum(terms, position % 2, pieces, False), 1, 1, False)], flags, after=(token_grad,), cut=2
     )
+    own, came_late = late_parts[0][0][0], late_parts[1][0]
     (early_parts,), before = deal_rounds([(early_parts, 2, 1, False)], flags, after=(before,))
-    (late_parts,), before = deal_rounds([(late_parts, 1, 0, True)], flags, after=(before,))
+    halves = []
+    for n in range(2):
+        half = [([came_late[n]], 0), ([own], n * (own.shape[0] // 2))]
+        waits = (before,) + tuple(halves[0][1][0] if halves else ())
+        (dealt_half,), before = deal_rounds([(half, 1, 0, True)], flags, after=waits)
+        halves.append(dealt_half)
     (early_parts,), before = deal_rounds([(early_parts, 1, 1, False)], flags, after=(before,))
+    late_parts = [([half[n][0][0] for half in halves], 0) for n in range(2)]
     at = 2
     while at < bits:
         step = min(2, bits - at)
-        if at > 2 and step == 2:
-            (early_parts,), before = deal_rounds([(early_parts, at, 1, False)], flags, after=(before,))
-        (late_parts, early_parts), before = deal_rounds(
-            [(late_parts, at, step, False), (early_parts, at + step - 1, 1, False)], flags, after=(before,)
-        )
+        (late_parts,), before = deal_rounds([(late_parts, at, step, False)], flags, after=(before,))
+        for bit in range(max(at, 3), at + step):
+            (early_parts,), before = deal_rounds([(early_parts, bit, 1, False)], flags, after=(before,))
         at += step
     feature_grad = vmem_call(
         feat_grad_kernel,

time: 68.5 us -> 69.6 us (1.016)
  waiting for transfers between devices: 24.7 us -> 20.4 us
  starting transfers between devices: 21.9 us -> 26.1 us
  Pallas kernels: 16.6 us -> 17.8 us
    ppermute x19 -> x20, waiting for transfers between devices: 18.1 us -> 11.2 us  [xor_move(): return lax.ppermute(block, 'tile', [(t, t ^ apart) for t in range(tiles)])]
    ppermute x19 -> x20, starting transfers between devices: 12.6 us -> 15.3 us  [xor_move(): return lax.ppermute(block, 'tile', [(t, t ^ apart) for t in range(tiles)])]
    ppermute x3 -> x4, waiting for transfers between devices: 5.53 us -> 8.04 us  [xor_move(): return lax.ppermute(block, 'dp', [(0, 1), (1, 0)])]
    ppermute x3 -> x4, starting transfers between devices: 3.14 us -> 4.62 us  [xor_move(): return lax.ppermute(block, 'dp', [(0, 1), (1, 0)])]
    pallas_call x16 -> x18, Pallas kernels: 16.6 us -> 17.8 us  [vmem_call(): pl.pallas_call(run, out_shape=out_shape, in_specs=specs, out_specs=jax.tr...]
  transfers between devices with their start and end apart: 25 -> 27, of which waited for: 16 -> 15; matrix products, arithmetic and copies ran while one was open for 0% -> 0% of each run, Pallas kernels for 17% -> 20%
where the time goes in v12:
time: 69.6 us; the launch traced here: 69.4 us
  starting transfers between devices  26.1 us (38%)
  waiting for transfers between devices  20.4 us (29%)
  Pallas kernels  17.8 us (26%)
  local copies, waits for them, and re-layouts  3 us (4%)
  other arithmetic  1.19 us (2%)
  between operations  0.91 us (1%)
    pallas_call x18, Pallas kernels, vmem_call(): pl.pallas_call(run, out_shape=out_shape, in_specs=specs, out_specs=jax.tr...  17.8 us
    ppermute x20, starting transfers between devices, xor_move(): return lax.ppermute(block, 'tile', [(t, t ^ apart) for t in range(tiles)])  15.3 us
    ppermute x20, waiting for transfers between devices, xor_move(): return lax.ppermute(block, 'tile', [(t, t ^ apart) for t in range(tiles)])  11.2 us
    ppermute x4, waiting for transfers between devices, xor_move(): return lax.ppermute(block, 'dp', [(0, 1), (1, 0)])  8.04 us
    ppermute x3, starting transfers between devices, swap(): return lax.ppermute(block, 'tile', tile_route(row_pairs, col_pairs, rows))  6.19 us
    ppermute x4, starting transfers between devices, xor_move(): return lax.ppermute(block, 'dp', [(0, 1), (1, 0)])  4.62 us
    unnamed x12, local copies, waits for them, and re-layouts  2.91 us
  transfers between devices with their start and end apart: 27, of which 15 were waited for; matrix products, arithmetic and copies ran while one was open for 0% of the time, Pallas kernels for 20%

profile of v12, /device:TPU:0, one launch (start us, length us, event | category | flops | bytes accessed | tf_op | source)
XLA Modules:
  0.0 69.4 jit_solution(17094916853843810160)
XLA Ops:
  0.7 1.2 %broadcast_select_fusion = (bf16[4,16,4,256]{3,2,1,0:T(4,128)(2,1)S(1)}, bf16[4,16,4,256]{3,2,1,0:T(4,128)(2,1)S(1)}) fusion(pred[]{:T(512)S(6)} %eq.27, bf16[4,16,32,256]{3,2,1,0:T(8,128)(2,1)} %refs_0_.1), kind=kLoop, calls=%fused_computation | loop fusion | flops 131072 | bytes 524289 | tf_op jit(solution)/shard_map/jit(_where)/select_n | solution.py:478
  1.9 3.1 %collective-permute-start.1 = (bf16[4,16,4,256]{3,2,1,0:T(4,128)(2,1)S(1)}, bf16[4,16,4,256]{3,2,1,0:T(4,128)(2,1)S(1)}, u32[]{:S(2)}, u32[]{:S(2)}) collective-permute-start(bf16[4,16,4,256]{3,2,1,0:T(4,128)(2,1)S(1)} %get-tuple-element.88), channel_id=1, source_target_pairs={{1,3},{3,1},{2,6},{6,2},{7,5},{5,7},{0,4},{4,0},{9,11},{11,9},{10,... | collective-permute-start | bytes 393224 | tf_op jit(solution)/shard_map/ppermute | solution.py:474
  4.9 1.2 %copy-done.3 = bf16[4,16,32,256]{3,2,1,0:T(8,128)(2,1)S(1)} copy-done((bf16[4,16,32,256]{3,2,1,0:T(8,128)(2,1)S(1)}, bf16[4,16,32,256]{3,2,1,0:T(8,128)(2,1)}, u32[]{:S(2)}) %copy-start.3) | copy-done | bytes 1048600
  6.2 0.5 shard_map.68.refs_1_
  6.7 0.1 stack.71.refs_0_
  6.8 1.1 %collective-permute-done.1.refs_3_ = bf16[4,16,4,256]{3,2,1,0:T(4,128)(2,1)S(1)} collective-permute-done((bf16[4,16,4,256]{3,2,1,0:T(4,128)(2,1)S(1)}, bf16[4,16,4,256]{3,2,1,0:T(4,128)(2,1)S(1)}, u32[]{:S(2)}, u32[]{:S(2)}) %collective-permute-start.1) | collective-permute-done | bytes 131104 | tf_op jit(solution)/shard_map/ppermute | solution.py:474
  7.9 0.8 %shard_map.69 = (bf16[144,256]{1,0:T(8,128)(2,1)S(1)}, f32[4,6,16,256]{3,2,1,0:T(8,128)S(1)}, f32[4,6,2,256]{3,2,1,0:T(2,128)S(1)}) custom-call(s32[13]{0:T(128)S(1)} %stack.71.refs_0_, f32[4,16,24,256]{3,2,1,0:T(8,128)S(1)} %shard_map.68.refs_1_, bf16[4,16,4,256]{3,2,1,0:T(4,128)(2,1)S(1)} %collective-permute-done.refs_2_, ...), custom_call_target="tpu_custom_call" | custom-call | bytes 2351156 | tf_op jit(solution)/shard_map/pallas_call | solution.py:371
  8.7 3.1 %collective-permute-start.2 = (bf16[144,256]{1,0:T(8,128)(2,1)S(1)}, bf16[144,256]{1,0:T(8,128)(2,1)S(1)}, u32[]{:S(2)}, u32[]{:S(2)}) collective-permute-start(bf16[144,256]{1,0:T(8,128)(2,1)S(1)} %get-tuple-element.45.refs_5_), channel_id=1, source_target_pairs={{0,8},{1,9},{3,11},{2,10},{6,14},{7,15},{5,13},{4,12},{8,0},{9,1},... | collective-permute-start | bytes 221192 | tf_op jit(solution)/shard_map/ppermute | solution.py:474
  11.8 1.7 %copy-done = bf16[2,3,3,256,256]{4,3,2,1,0:T(8,128)(2,1)S(1)} copy-done((bf16[2,3,3,256,256]{4,3,2,1,0:T(8,128)(2,1)S(1)}, bf16[2,3,3,256,256]{4,3,2,1,0:T(8,128)(2,1)}, u32[]{:S(2)}) %copy-start) | copy-done | bytes 2359320
  13.4 2.4 %shard_map.70 = (bf16[3,640,256]{2,1,0:T(8,128)(2,1)S(1)}, f32[2,512,256]{2,1,0:T(8,128)S(1)}) custom-call(s32[13]{0:T(128)S(1)} %stack.71.refs_0_, f32[4,16,24,256]{3,2,1,0:T(8,128)S(1)} %shard_map.68.refs_1_, bf16[4,16,4,256]{3,2,1,0:T(4,128)(2,1)S(1)} %collective-permute-done.refs_2_, bf16[4,16,4,256]{3,2,1,0:T(4,128)(2,1)S(1)} %collective-permute-done.1.refs_3_, ...), custom_call_target="tpu_custom_call" | custom-call | flops 1207959552 | bytes 6225972 | tf_op jit(solution)/shard_map/pallas_call | solution.py:371
  15.8 0.0 copy-start.5
  15.9 1.6 %shard_map.71 = (bf16[2,2,64,256]{3,2,1,0:T(8,128)(2,1)S(1)}, bf16[2,2,64,256]{3,2,1,0:T(8,128)(2,1)S(1)}, bf16[2,2,64,256]{3,2,1,0:T(8,128)(2,1)S(1)}, bf16[2,2...) custom-call(s32[13]{0:T(128)S(1)} %stack.71.refs_0_, ...), custom_call_target="tpu_custom_call", output_to_operand_aliasing={{4}: (4, {})} | custom-call | flops 301989888 | bytes 6414388 | tf_op jit(solution)/shard_map/pallas_call | solution.py:371
  17.5 1.6 %collective-permute-start.3 = (bf16[2,2,64,256]{3,2,1,0:T(8,128)(2,1)S(1)}, bf16[2,2,64,256]{3,2,1,0:T(8,128)(2,1)S(1)}, u32[]{:S(2)}, u32[]{:S(2)}) collective-permute-start(bf16[2,2,64,256]{3,2,1,0:T(8,128)(2,1)S(1)} %get-tuple-element.51), channel_id=1, source_target_pairs={{0,2},{1,3},{2,0},{3,1},{4,6},{5,7},{6,4},{7,5},{8,10},{9,11},{10,... | collective-permute-start | bytes 393224 | tf_op jit(solution)/shard_map/ppermute | solution.py:390
  19.1 1.6 %collective-permute-start.4 = (bf16[2,2,64,256]{3,2,1,0:T(8,128)(2,1)S(1)}, bf16[2,2,64,256]{3,2,1,0:T(8,128)(2,1)S(1)}, u32[]{:S(2)}, u32[]{:S(2)}) collective-permute-start(bf16[2,2,64,256]{3,2,1,0:T(8,128)(2,1)S(1)} %get-tuple-element.52), channel_id=1, source_target_pairs={{0,4},{1,5},{2,6},{3,7},{4,0},{5,1},{6,2},{7,3},{8,12},{9,13},{10,... | collective-permute-start | bytes 393224 | tf_op jit(solution)/shard_map/ppermute | solution.py:390
  20.7 0.4 collective-permute-start.5
  21.1 2.1 %shard_map.73 = (bf16[8,208,256]{2,1,0:T(8,128)(2,1)S(1)}, bf16[2,208,256]{2,1,0:T(8,128)(2,1)S(1)}, bf16[2,208,256]{2,1,0:T(8,128)(2,1)S(1)}, bf16[2,208,256]{2...) custom-call(s32[13]{0:T(128)S(1)} %stack.71.refs_0_, ...), custom_call_target="tpu_custom_call" | custom-call | flops 1207959552 | bytes 3866676 | tf_op jit(solution)/shard_map/pallas_call | solution.py:371
  23.1 0.0 copy-start.2
  23.1 0.1 collective-permute-start.7
  23.2 0.5 collective-permute-start.8
  23.7 0.1 collective-permute-start.9
  23.8 0.6 collective-permute-done.4.refs_2_.refs_3_
  24.4 2.2 %collective-permute-done.5.refs_3_.refs_4_ = bf16[2,2,64,256]{3,2,1,0:T(8,128)(2,1)S(1)} collective-permute-done((bf16[2,2,64,256]{3,2,1,0:T(8,128)(2,1)S(1)}, bf16[2,2,64,256]{3,2,1,0:T(8,128)(2,1)S(1)}, u32[]{:S(2)}, u32[]{:S(2)}) %collective-permute-start.5) | collective-permute-done | bytes 131104 | tf_op jit(solution)/shard_map/ppermute | solution.py:390
  26.5 0.1 collective-permute-start.6
  26.7 0.7 %shard_map.74 = (f32[8,208,128]{2,1,0:T(8,128)S(1)}, bf16[8,208,128]{2,1,0:T(8,128)(2,1)S(1)}) custom-call(s32[13]{0:T(128)S(1)} %stack.71.refs_0_, bf16[8,208,256]{2,1,0:T(8,128)(2,1)S(1)} %get-tuple-element.56.refs_1_, bf16[2,208,256]{2,1,0:T(8,128)(2,1)S(1)} %collective-permute-done.7.refs_2_, bf16[2,208,256]{2,1,0:T(8,128)(2,1)S(1)} %collective-permute-done.8.refs_3_, ...), custom_call_target="tpu_custom_call" | custom-call | bytes 2981940 | tf_op jit(solution)/shard_map/pallas_call | solution.py:371
  27.4 1.6 %collective-permute-start.11 = (bf16[8,208,128]{2,1,0:T(8,128)(2,1)S(1)}, bf16[8,208,128]{2,1,0:T(8,128)(2,1)S(1)}, u32[]{:S(2)}, u32[]{:S(2)}) collective-permute-start(bf16[8,208,128]{2,1,0:T(8,128)(2,1)S(1)} %get-tuple-element.63), channel_id=1, source_target_pairs={{0,16},{16,0},{1,17},{17,1},{2,18},{18,2},{3,19},{19,3},{4,20},{20... | collective-permute-start | bytes 1277960 | tf_op jit(solution)/shard_map/ppermute | solution.py:392
  29.0 1.5 %shard_map.75 = (bf16[8,208,256]{2,1,0:T(8,128)(2,1)S(1)}, bf16[2,208,256]{2,1,0:T(8,128)(2,1)S(1)}, bf16[2,208,256]{2,1,0:T(8,128)(2,1)S(1)}, bf16[2,208,256]{2...) custom-call(s32[13]{0:T(128)S(1)} %stack.71.refs_0_, ...), custom_call_target="tpu_custom_call" | custom-call | flops 536870912 | bytes 5767220 | tf_op jit(solution)/shard_map/pallas_call | solution.py:371
  30.4 0.3 collective-permute-start.12
  30.7 0.3 collective-permute-start.13
  31.0 0.2 collective-permute-start.14
  31.2 0.3 collective-permute-start.15
  31.5 0.4 collective-permute-done.12.refs_2_
  32.0 0.3 collective-permute-done.13.refs_3_
  32.3 0.3 collective-permute-done.14.refs_4_
  32.6 0.3 collective-permute-done.15.refs_5_
  32.9 0.7 %shard_map.76 = (f32[4,208,256]{2,1,0:T(8,128)S(1)}, bf16[2,208,256]{2,1,0:T(8,128)(2,1)S(1)}, bf16[2,208,256]{2,1,0:T(8,128)(2,1)S(1)}) custom-call(s32[13]{0:T(128)S(1)} %stack.71.refs_0_, bf16[8,208,256]{2,1,0:T(8,128)(2,1)S(1)} %get-tuple-element.64.refs_1_, bf16[2,208,256]{2,1,0:T(8,128)(2,1)S(1)} %collective-permute-done.12.refs_2_, ...), custom_call_target="tpu_custom_call" | custom-call | bytes 2981940 | tf_op jit(solution)/shard_map/pallas_call | solution.py:371
  33.6 0.8 %collective-permute-start.18 = (bf16[2,208,256]{2,1,0:T(8,128)(2,1)S(1)}, bf16[2,208,256]{2,1,0:T(8,128)(2,1)S(1)}, u32[]{:S(2)}, u32[]{:S(2)}) collective-permute-start(bf16[2,208,256]{2,1,0:T(8,128)(2,1)S(1)} %get-tuple-element.73), channel_id=1, source_target_pairs={{0,2},{1,3},{2,0},{3,1},{4,6},{5,7},{6,4},{7,5},{8,10},{9,11},{10,... | collective-permute-start | bytes 638984 | tf_op jit(solution)/shard_map/ppermute | solution.py:390
  34.4 1.3 %collective-permute-start.17 = (bf16[2,208,256]{2,1,0:T(8,128)(2,1)S(1)}, bf16[2,208,256]{2,1,0:T(8,128)(2,1)S(1)}, u32[]{:S(2)}, u32[]{:S(2)}) collective-permute-start(bf16[2,208,256]{2,1,0:T(8,128)(2,1)S(1)} %get-tuple-element.72), channel_id=1, source_target_pairs={{0,2},{1,3},{2,0},{3,1},{4,6},{5,7},{6,4},{7,5},{8,10},{9,11},{10,... | collective-permute-start | bytes 638984 | tf_op jit(solution)/shard_map/ppermute | solution.py:390
  35.7 4.0 %collective-permute-done.11.refs_2_ = bf16[8,208,128]{2,1,0:T(8,128)(2,1)S(1)} collective-permute-done((bf16[8,208,128]{2,1,0:T(8,128)(2,1)S(1)}, bf16[8,208,128]{2,1,0:T(8,128)(2,1)S(1)}, u32[]{:S(2)}, u32[]{:S(2)}) %collective-permute-start.11) | collective-permute-done | bytes 426016 | tf_op jit(solution)/shard_map/ppermute | solution.py:392
  39.7 0.6 shard_map.77
  40.3 0.8 %collective-permute-start.16 = (bf16[4,208,128]{2,1,0:T(8,128)(2,1)S(1)}, bf16[4,208,128]{2,1,0:T(8,128)(2,1)S(1)}, u32[]{:S(2)}, u32[]{:S(2)}) collective-permute-start(bf16[4,208,128]{2,1,0:T(8,128)(2,1)S(1)} %get-tuple-element.71), channel_id=1, source_target_pairs={{0,4},{1,5},{2,6},{3,7},{4,0},{5,1},{6,2},{7,3},{8,12},{9,13},{10,... | collective-permute-start | bytes 638984 | tf_op jit(solution)/shard_map/ppermute | solution.py:390
  41.1 0.7 collective-permute-done.18.refs_1_
  41.8 0.6 shard_map.78
  42.4 0.0 copy-start.4
  42.4 0.9 %collective-permute-start.19 = (bf16[2,208,128]{2,1,0:T(8,128)(2,1)S(1)}, bf16[2,208,128]{2,1,0:T(8,128)(2,1)S(1)}, u32[]{:S(2)}, u32[]{:S(2)}) collective-permute-start(bf16[2,208,128]{2,1,0:T(8,128)(2,1)S(1)} %get-tuple-element.75), channel_id=1, source_target_pairs={{0,16},{16,0},{1,17},{17,1},{2,18},{18,2},{3,19},{19,3},{4,20},{20... | collective-permute-start | bytes 319496 | tf_op jit(solution)/shard_map/ppermute | solution.py:392
  43.3 2.3 %collective-permute-done.17.refs_1_ = bf16[2,208,256]{2,1,0:T(8,128)(2,1)S(1)} collective-permute-done((bf16[2,208,256]{2,1,0:T(8,128)(2,1)S(1)}, bf16[2,208,256]{2,1,0:T(8,128)(2,1)S(1)}, u32[]{:S(2)}, u32[]{:S(2)}) %collective-permute-start.17) | collective-permute-done | bytes 213024 | tf_op jit(solution)/shard_map/ppermute | solution.py:390
  45.6 1.5 %collective-permute-done.19.refs_4_.refs_3_ = bf16[2,208,128]{2,1,0:T(8,128)(2,1)S(1)} collective-permute-done((bf16[2,208,128]{2,1,0:T(8,128)(2,1)S(1)}, bf16[2,208,128]{2,1,0:T(8,128)(2,1)S(1)}, u32[]{:S(2)}, u32[]{:S(2)}) %collective-permute-start.19) | collective-permute-done | bytes 106528 | tf_op jit(solution)/shard_map/ppermute | solution.py:392
  47.2 0.6 shard_map.79
  47.8 0.9 %collective-permute-start.21 = (bf16[2,208,128]{2,1,0:T(8,128)(2,1)S(1)}, bf16[2,208,128]{2,1,0:T(8,128)(2,1)S(1)}, u32[]{:S(2)}, u32[]{:S(2)}) collective-permute-start(bf16[2,208,128]{2,1,0:T(8,128)(2,1)S(1)} %get-tuple-element.79), channel_id=1, source_target_pairs={{0,16},{16,0},{1,17},{17,1},{2,18},{18,2},{3,19},{19,3},{4,20},{20... | collective-permute-start | bytes 319496 | tf_op jit(solution)/shard_map/ppermute | solution.py:392
  48.7 0.6 shard_map.80
  49.2 1.6 %collective-permute-start.20 = (bf16[2,208,128]{2,1,0:T(8,128)(2,1)S(1)}, bf16[2,208,128]{2,1,0:T(8,128)(2,1)S(1)}, u32[]{:S(2)}, u32[]{:S(2)}) collective-permute-start(bf16[2,208,128]{2,1,0:T(8,128)(2,1)S(1)} %get-tuple-element.78), channel_id=1, source_target_pairs={{0,2},{1,3},{2,0},{3,1},{4,6},{5,7},{6,4},{7,5},{8,10},{9,11},{10,... | collective-permute-start | bytes 319496 | tf_op jit(solution)/shard_map/ppermute | solution.py:390
  50.8 1.7 %collective-permute-done.21.refs_4_ = bf16[2,208,128]{2,1,0:T(8,128)(2,1)S(1)} collective-permute-done((bf16[2,208,128]{2,1,0:T(8,128)(2,1)S(1)}, bf16[2,208,128]{2,1,0:T(8,128)(2,1)S(1)}, u32[]{:S(2)}, u32[]{:S(2)}) %collective-permute-start.21) | collective-permute-done | bytes 106528 | tf_op jit(solution)/shard_map/ppermute | solution.py:392
  52.5 0.6 shard_map.81
  53.2 1.9 %collective-permute-start.23 = (bf16[1,208,128]{2,1,0:T(8,128)(2,1)S(1)}, bf16[1,208,128]{2,1,0:T(8,128)(2,1)S(1)}, u32[]{:S(2)}, u32[]{:S(2)}) collective-permute-start(bf16[1,208,128]{2,1,0:T(8,128)(2,1)S(1)} %get-tuple-element.83), channel_id=1, source_target_pairs={{0,12},{1,13},{2,14},{3,15},{4,8},{5,9},{6,10},{7,11},{8,4},{9,5},... | collective-permute-start | bytes 159752 | tf_op jit(solution)/shard_map/ppermute | solution.py:390
  55.1 0.3 collective-permute-start.24
  55.5 2.2 %collective-permute-start.25 = (bf16[1,208,128]{2,1,0:T(8,128)(2,1)S(1)}, bf16[1,208,128]{2,1,0:T(8,128)(2,1)S(1)}, u32[]{:S(2)}, u32[]{:S(2)}) collective-permute-start(bf16[1,208,128]{2,1,0:T(8,128)(2,1)S(1)} %get-tuple-element.85), channel_id=1, source_target_pairs={{0,4},{1,5},{2,6},{3,7},{4,0},{5,1},{6,2},{7,3},{8,12},{9,13},{10,... | collective-permute-start | bytes 159752 | tf_op jit(solution)/shard_map/ppermute | solution.py:390
  57.6 0.6 shard_map.82
  58.2 1.0 %collective-permute-start.22 = (bf16[1,208,128]{2,1,0:T(8,128)(2,1)S(1)}, bf16[1,208,128]{2,1,0:T(8,128)(2,1)S(1)}, u32[]{:S(2)}, u32[]{:S(2)}) collective-permute-start(bf16[1,208,128]{2,1,0:T(8,128)(2,1)S(1)} %get-tuple-element.82), channel_id=1, source_target_pairs={{0,8},{1,9},{2,10},{3,11},{4,12},{5,13},{6,14},{7,15},{8,0},{9,1},... | collective-permute-start | bytes 159752 | tf_op jit(solution)/shard_map/ppermute | solution.py:390
  59.2 1.5 %collective-permute-done.24.refs_5_ = bf16[1,208,128]{2,1,0:T(8,128)(2,1)S(1)} collective-permute-done((bf16[1,208,128]{2,1,0:T(8,128)(2,1)S(1)}, bf16[1,208,128]{2,1,0:T(8,128)(2,1)S(1)}, u32[]{:S(2)}, u32[]{:S(2)}) %collective-permute-start.24) | collective-permute-done | bytes 53280 | tf_op jit(solution)/shard_map/ppermute | solution.py:390
  60.7 2.6 %collective-permute-done.22.refs_2_ = bf16[1,208,128]{2,1,0:T(8,128)(2,1)S(1)} collective-permute-done((bf16[1,208,128]{2,1,0:T(8,128)(2,1)S(1)}, bf16[1,208,128]{2,1,0:T(8,128)(2,1)S(1)}, u32[]{:S(2)}, u32[]{:S(2)}) %collective-permute-start.22) | collective-permute-done | bytes 53280 | tf_op jit(solution)/shard_map/ppermute | solution.py:390
  63.3 0.6 shard_map.84
  63.9 1.3 %collective-permute-start.26 = (bf16[208,128]{1,0:T(8,128)(2,1)S(1)}, bf16[208,128]{1,0:T(8,128)(2,1)S(1)}, u32[]{:S(2)}, u32[]{:S(2)}) collective-permute-start(bf16[208,128]{1,0:T(8,128)(2,1)S(1)} %get-tuple-element.87), channel_id=1, source_target_pairs={{0,16},{16,0},{1,17},{17,1},{2,18},{18,2},{3,19},{19,3},{4,20},{20... | collective-permute-start | bytes 159752 | tf_op jit(solution)/shard_map/ppermute | solution.py:392
  65.2 2.1 %shard_map.83 = bf16[4,2,128,1024]{3,2,1,0:T(8,128)(2,1)} custom-call(bf16[2,512,256]{2,1,0:T(8,128)(2,1)S(1)} %get-tuple-element.62.refs_6_.refs_0_, bf16[2,1024,256]{2,1,0:T(8,128)(2,1)S(1)} %copy-done.4, f32[1,208,128]{2,1,0:T(8,128)S(1)} %get-tuple-element.81.refs_2_.refs_1_), custom_call_target="tpu_custom_call" | custom-call | flops 536870912 | bytes 3670016 | tf_op jit(solution)/shard_map/pallas_call | solution.py:371
  67.3 0.9 %collective-permute-done.26.refs_2_ = bf16[208,128]{1,0:T(8,128)(2,1)S(1)} collective-permute-done((bf16[208,128]{1,0:T(8,128)(2,1)S(1)}, bf16[208,128]{1,0:T(8,128)(2,1)S(1)}, u32[]{:S(2)}, u32[]{:S(2)}) %collective-permute-start.26) | collective-permute-done | bytes 53280 | tf_op jit(solution)/shard_map/ppermute | solution.py:392
  68.1 1.2 %shard_map.85 = f32[208,256]{1,0:T(8,128)} custom-call(s32[13]{0:T(128)S(1)} %stack.71.refs_0_, f32[208,128]{1,0:T(8,128)S(1)} %get-tuple-element.86.refs_1_, bf16[208,128]{1,0:T(8,128)(2,1)S(1)} %collective-permute-done.26.refs_2_), custom_call_target="tpu_custom_call" | custom-call | bytes 372788 | tf_op jit(solution)/shard_map/pallas_call | solution.py:371
  (22 shorter events, 0.1 us)
Async XLA Ops:
  1.9 6.0 %collective-permute-start.1 = (bf16[4,16,4,256]{3,2,1,0:T(4,128)(2,1)S(1)}, bf16[4,16,4,256]{3,2,1,0:T(4,128)(2,1)S(1)}, u32[]{:S(2)}, u32[]{:S(2)}) collective-permute-start(bf16[4,16,4,256]{3,2,1,0:T(4,128)(2,1)S(1)} %get-tuple-element.88), channel_id=1, source_target_pairs={{1,3},{3,1},{2,6},{6,2},{7,5},{5,7},{0,4},{4,0},{9,11},{11,9},{10,... | collective-permute-start | bytes 393224 | tf_op jit(solution)/shard_map/ppermute | solution.py:474
  4.9 3.0 %collective-permute-start = (bf16[4,16,4,256]{3,2,1,0:T(4,128)(2,1)S(1)}, bf16[4,16,4,256]{3,2,1,0:T(4,128)(2,1)S(1)}, u32[]{:S(2)}, u32[]{:S(2)}) collective-permute-start(bf16[4,16,4,256]{3,2,1,0:T(4,128)(2,1)S(1)} %get-tuple-element.89), channel_id=1, source_target_pairs={{0,1},{1,0},{3,2},{2,3},{6,7},{7,6},{5,4},{4,5},{8,9},{9,8},{11,10... | collective-permute-start | bytes 393224 | tf_op jit(solution)/shard_map/ppermute | solution.py:474
  4.9 1.2 %copy-start.3 = (bf16[4,16,32,256]{3,2,1,0:T(8,128)(2,1)S(1)}, bf16[4,16,32,256]{3,2,1,0:T(8,128)(2,1)}, u32[]{:S(2)}) copy-start(bf16[4,16,32,256]{3,2,1,0:T(8,128)(2,1)} %refs_0_.1) | copy-start | bytes 3145732
  8.7 7.2 %collective-permute-start.2 = (bf16[144,256]{1,0:T(8,128)(2,1)S(1)}, bf16[144,256]{1,0:T(8,128)(2,1)S(1)}, u32[]{:S(2)}, u32[]{:S(2)}) collective-permute-start(bf16[144,256]{1,0:T(8,128)(2,1)S(1)} %get-tuple-element.45.refs_5_), channel_id=1, source_target_pairs={{0,8},{1,9},{3,11},{2,10},{6,14},{7,15},{5,13},{4,12},{8,0},{9,1},... | collective-permute-start | bytes 221192 | tf_op jit(solution)/shard_map/ppermute | solution.py:474
  11.8 1.7 %copy-start = (bf16[2,3,3,256,256]{4,3,2,1,0:T(8,128)(2,1)S(1)}, bf16[2,3,3,256,256]{4,3,2,1,0:T(8,128)(2,1)}, u32[]{:S(2)}) copy-start(bf16[2,3,3,256,256]{4,3,2,1,0:T(8,128)(2,1)} %refs_6_.2) | copy-start | bytes 7077892
  13.4 2.4 %copy-start.1 = (bf16[2,3,3,256,256]{4,3,2,1,0:T(8,128)(2,1)S(1)}, bf16[2,3,3,256,256]{4,3,2,1,0:T(8,128)(2,1)}, u32[]{:S(2)}) copy-start(bf16[2,3,3,256,256]{4,3,2,1,0:T(8,128)(2,1)} %refs_6_.2) | copy-start | bytes 7077892
  15.8 5.2 %copy-start.5 = (bf16[4,2,8,16,256]{4,3,2,1,0:T(8,128)(2,1)S(1)}, bf16[4,2,8,16,256]{4,3,2,1,0:T(8,128)(2,1)}, u32[]{:S(2)}) copy-start(bf16[4,2,8,16,256]{4,3,2,1,0:T(8,128)(2,1)} %refs_2_.1) | copy-start | bytes 1572868
  17.5 6.2 %collective-permute-start.3 = (bf16[2,2,64,256]{3,2,1,0:T(8,128)(2,1)S(1)}, bf16[2,2,64,256]{3,2,1,0:T(8,128)(2,1)S(1)}, u32[]{:S(2)}, u32[]{:S(2)}) collective-permute-start(bf16[2,2,64,256]{3,2,1,0:T(8,128)(2,1)S(1)} %get-tuple-element.51), channel_id=1, source_target_pairs={{0,2},{1,3},{2,0},{3,1},{4,6},{5,7},{6,4},{7,5},{8,10},{9,11},{10,... | collective-permute-start | bytes 393224 | tf_op jit(solution)/shard_map/ppermute | solution.py:390
  19.1 5.3 %collective-permute-start.4 = (bf16[2,2,64,256]{3,2,1,0:T(8,128)(2,1)S(1)}, bf16[2,2,64,256]{3,2,1,0:T(8,128)(2,1)S(1)}, u32[]{:S(2)}, u32[]{:S(2)}) collective-permute-start(bf16[2,2,64,256]{3,2,1,0:T(8,128)(2,1)S(1)} %get-tuple-element.52), channel_id=1, source_target_pairs={{0,4},{1,5},{2,6},{3,7},{4,0},{5,1},{6,2},{7,3},{8,12},{9,13},{10,... | collective-permute-start | bytes 393224 | tf_op jit(solution)/shard_map/ppermute | solution.py:390
  20.7 5.9 %collective-permute-start.5 = (bf16[2,2,64,256]{3,2,1,0:T(8,128)(2,1)S(1)}, bf16[2,2,64,256]{3,2,1,0:T(8,128)(2,1)S(1)}, u32[]{:S(2)}, u32[]{:S(2)}) collective-permute-start(bf16[2,2,64,256]{3,2,1,0:T(8,128)(2,1)S(1)} %get-tuple-element.53), channel_id=1, source_target_pairs={{0,6},{1,7},{2,4},{3,5},{4,2},{5,3},{6,0},{7,1},{8,14},{9,15},{10,... | collective-permute-start | bytes 393224 | tf_op jit(solution)/shard_map/ppermute | solution.py:390
  23.1 5.8 %copy-start.2 = (bf16[4,2,128,1024]{3,2,1,0:T(8,128)(2,1)S(1)}, bf16[4,2,128,1024]{3,2,1,0:T(8,128)(2,1)}, u32[]{:S(2)}) copy-start(bf16[4,2,128,1024]{3,2,1,0:T(8,128)(2,1)} %refs_6_.3) | copy-start | bytes 6291460
  23.1 3.5 %collective-permute-start.7 = (bf16[2,208,256]{2,1,0:T(8,128)(2,1)S(1)}, bf16[2,208,256]{2,1,0:T(8,128)(2,1)S(1)}, u32[]{:S(2)}, u32[]{:S(2)}) collective-permute-start(bf16[2,208,256]{2,1,0:T(8,128)(2,1)S(1)} %get-tuple-element.57), channel_id=1, source_target_pairs={{0,1},{1,0},{2,3},{3,2},{4,5},{5,4},{6,7},{7,6},{8,9},{9,8},{10,11... | collective-permute-start | bytes 638984 | tf_op jit(solution)/shard_map/ppermute | solution.py:390
  23.2 3.4 %collective-permute-start.8 = (bf16[2,208,256]{2,1,0:T(8,128)(2,1)S(1)}, bf16[2,208,256]{2,1,0:T(8,128)(2,1)S(1)}, u32[]{:S(2)}, u32[]{:S(2)}) collective-permute-start(bf16[2,208,256]{2,1,0:T(8,128)(2,1)S(1)} %get-tuple-element.58), channel_id=1, source_target_pairs={{0,1},{1,0},{2,3},{3,2},{4,5},{5,4},{6,7},{7,6},{8,9},{9,8},{10,11... | collective-permute-start | bytes 638984 | tf_op jit(solution)/shard_map/ppermute | solution.py:390
  23.7 2.9 %collective-permute-start.9 = (bf16[2,208,256]{2,1,0:T(8,128)(2,1)S(1)}, bf16[2,208,256]{2,1,0:T(8,128)(2,1)S(1)}, u32[]{:S(2)}, u32[]{:S(2)}) collective-permute-start(bf16[2,208,256]{2,1,0:T(8,128)(2,1)S(1)} %get-tuple-element.59), channel_id=1, source_target_pairs={{0,1},{1,0},{2,3},{3,2},{4,5},{5,4},{6,7},{7,6},{8,9},{9,8},{10,11... | collective-permute-start | bytes 638984 | tf_op jit(solution)/shard_map/ppermute | solution.py:390
  24.4 2.3 %collective-permute-start.10 = (bf16[2,208,256]{2,1,0:T(8,128)(2,1)S(1)}, bf16[2,208,256]{2,1,0:T(8,128)(2,1)S(1)}, u32[]{:S(2)}, u32[]{:S(2)}) collective-permute-start(bf16[2,208,256]{2,1,0:T(8,128)(2,1)S(1)} %get-tuple-element.60), channel_id=1, source_target_pairs={{0,1},{1,0},{2,3},{3,2},{4,5},{5,4},{6,7},{7,6},{8,9},{9,8},{10,11... | collective-permute-start | bytes 638984 | tf_op jit(solution)/shard_map/ppermute | solution.py:390
  26.5 2.4 %collective-permute-start.6 = (bf16[4,2,64,256]{3,2,1,0:T(8,128)(2,1)S(1)}, bf16[4,2,64,256]{3,2,1,0:T(8,128)(2,1)S(1)}, u32[]{:S(2)}, u32[]{:S(2)}) collective-permute-start(bf16[4,2,64,256]{3,2,1,0:T(8,128)(2,1)S(1)} %shard_map.72), channel_id=1, source_target_pairs={{0,1},{1,0},{2,3},{3,2},{4,5},{5,4},{6,7},{7,6},{8,9},{9,8},{10,11... | collective-permute-start | bytes 786440 | tf_op jit(solution)/shard_map/ppermute | solution.py:390
  27.4 12.3 %collective-permute-start.11 = (bf16[8,208,128]{2,1,0:T(8,128)(2,1)S(1)}, bf16[8,208,128]{2,1,0:T(8,128)(2,1)S(1)}, u32[]{:S(2)}, u32[]{:S(2)}) collective-permute-start(bf16[8,208,128]{2,1,0:T(8,128)(2,1)S(1)} %get-tuple-element.63), channel_id=1, source_target_pairs={{0,16},{16,0},{1,17},{17,1},{2,18},{18,2},{3,19},{19,3},{4,20},{20... | collective-permute-start | bytes 1277960 | tf_op jit(solution)/shard_map/ppermute | solution.py:392
  30.4 1.5 %collective-permute-start.12 = (bf16[2,208,256]{2,1,0:T(8,128)(2,1)S(1)}, bf16[2,208,256]{2,1,0:T(8,128)(2,1)S(1)}, u32[]{:S(2)}, u32[]{:S(2)}) collective-permute-start(bf16[2,208,256]{2,1,0:T(8,128)(2,1)S(1)} %get-tuple-element.65), channel_id=1, source_target_pairs={{0,1},{1,0},{2,3},{3,2},{4,5},{5,4},{6,7},{7,6},{8,9},{9,8},{10,11... | collective-permute-start | bytes 638984 | tf_op jit(solution)/shard_map/ppermute | solution.py:390
  30.7 1.6 %collective-permute-start.13 = (bf16[2,208,256]{2,1,0:T(8,128)(2,1)S(1)}, bf16[2,208,256]{2,1,0:T(8,128)(2,1)S(1)}, u32[]{:S(2)}, u32[]{:S(2)}) collective-permute-start(bf16[2,208,256]{2,1,0:T(8,128)(2,1)S(1)} %get-tuple-element.66), channel_id=1, source_target_pairs={{0,1},{1,0},{2,3},{3,2},{4,5},{5,4},{6,7},{7,6},{8,9},{9,8},{10,11... | collective-permute-start | bytes 638984 | tf_op jit(solution)/shard_map/ppermute | solution.py:390
  31.0 1.6 %collective-permute-start.14 = (bf16[2,208,256]{2,1,0:T(8,128)(2,1)S(1)}, bf16[2,208,256]{2,1,0:T(8,128)(2,1)S(1)}, u32[]{:S(2)}, u32[]{:S(2)}) collective-permute-start(bf16[2,208,256]{2,1,0:T(8,128)(2,1)S(1)} %get-tuple-element.67), channel_id=1, source_target_pairs={{0,1},{1,0},{2,3},{3,2},{4,5},{5,4},{6,7},{7,6},{8,9},{9,8},{10,11... | collective-permute-start | bytes 638984 | tf_op jit(solution)/shard_map/ppermute | solution.py:390
  31.2 1.7 %collective-permute-start.15 = (bf16[2,208,256]{2,1,0:T(8,128)(2,1)S(1)}, bf16[2,208,256]{2,1,0:T(8,128)(2,1)S(1)}, u32[]{:S(2)}, u32[]{:S(2)}) collective-permute-start(bf16[2,208,256]{2,1,0:T(8,128)(2,1)S(1)} %get-tuple-element.68), channel_id=1, source_target_pairs={{0,1},{1,0},{2,3},{3,2},{4,5},{5,4},{6,7},{7,6},{8,9},{9,8},{10,11... | collective-permute-start | bytes 638984 | tf_op jit(solution)/shard_map/ppermute | solution.py:390
  33.6 8.2 %collective-permute-start.18 = (bf16[2,208,256]{2,1,0:T(8,128)(2,1)S(1)}, bf16[2,208,256]{2,1,0:T(8,128)(2,1)S(1)}, u32[]{:S(2)}, u32[]{:S(2)}) collective-permute-start(bf16[2,208,256]{2,1,0:T(8,128)(2,1)S(1)} %get-tuple-element.73), channel_id=1, source_target_pairs={{0,2},{1,3},{2,0},{3,1},{4,6},{5,7},{6,4},{7,5},{8,10},{9,11},{10,... | collective-permute-start | bytes 638984 | tf_op jit(solution)/shard_map/ppermute | solution.py:390
  34.4 11.2 %collective-permute-start.17 = (bf16[2,208,256]{2,1,0:T(8,128)(2,1)S(1)}, bf16[2,208,256]{2,1,0:T(8,128)(2,1)S(1)}, u32[]{:S(2)}, u32[]{:S(2)}) collective-permute-start(bf16[2,208,256]{2,1,0:T(8,128)(2,1)S(1)} %get-tuple-element.72), channel_id=1, source_target_pairs={{0,2},{1,3},{2,0},{3,1},{4,6},{5,7},{6,4},{7,5},{8,10},{9,11},{10,... | collective-permute-start | bytes 638984 | tf_op jit(solution)/shard_map/ppermute | solution.py:390
  40.3 8.4 %collective-permute-start.16 = (bf16[4,208,128]{2,1,0:T(8,128)(2,1)S(1)}, bf16[4,208,128]{2,1,0:T(8,128)(2,1)S(1)}, u32[]{:S(2)}, u32[]{:S(2)}) collective-permute-start(bf16[4,208,128]{2,1,0:T(8,128)(2,1)S(1)} %get-tuple-element.71), channel_id=1, source_target_pairs={{0,4},{1,5},{2,6},{3,7},{4,0},{5,1},{6,2},{7,3},{8,12},{9,13},{10,... | collective-permute-start | bytes 638984 | tf_op jit(solution)/shard_map/ppermute | solution.py:390
  42.4 22.8 %copy-start.4 = (bf16[2,1024,256]{2,1,0:T(8,128)(2,1)S(1)}, bf16[2,1024,256]{2,1,0:T(8,128)(2,1)}, u32[]{:S(2)}) copy-start(bf16[2,1024,256]{2,1,0:T(8,128)(2,1)} %refs_1_.1) | copy-start | bytes 3145732
  42.4 4.8 %collective-permute-start.19 = (bf16[2,208,128]{2,1,0:T(8,128)(2,1)S(1)}, bf16[2,208,128]{2,1,0:T(8,128)(2,1)S(1)}, u32[]{:S(2)}, u32[]{:S(2)}) collective-permute-start(bf16[2,208,128]{2,1,0:T(8,128)(2,1)S(1)} %get-tuple-element.75), channel_id=1, source_target_pairs={{0,16},{16,0},{1,17},{17,1},{2,18},{18,2},{3,19},{19,3},{4,20},{20... | collective-permute-start | bytes 319496 | tf_op jit(solution)/shard_map/ppermute | solution.py:392
  47.8 4.8 %collective-permute-start.21 = (bf16[2,208,128]{2,1,0:T(8,128)(2,1)S(1)}, bf16[2,208,128]{2,1,0:T(8,128)(2,1)S(1)}, u32[]{:S(2)}, u32[]{:S(2)}) collective-permute-start(bf16[2,208,128]{2,1,0:T(8,128)(2,1)S(1)} %get-tuple-element.79), channel_id=1, source_target_pairs={{0,16},{16,0},{1,17},{17,1},{2,18},{18,2},{3,19},{19,3},{4,20},{20... | collective-permute-start | bytes 319496 | tf_op jit(solution)/shard_map/ppermute | solution.py:392
  49.2 8.4 %collective-permute-start.20 = (bf16[2,208,128]{2,1,0:T(8,128)(2,1)S(1)}, bf16[2,208,128]{2,1,0:T(8,128)(2,1)S(1)}, u32[]{:S(2)}, u32[]{:S(2)}) collective-permute-start(bf16[2,208,128]{2,1,0:T(8,128)(2,1)S(1)} %get-tuple-element.78), channel_id=1, source_target_pairs={{0,2},{1,3},{2,0},{3,1},{4,6},{5,7},{6,4},{7,5},{8,10},{9,11},{10,... | collective-permute-start | bytes 319496 | tf_op jit(solution)/shard_map/ppermute | solution.py:390
  53.2 6.0 %collective-permute-start.23 = (bf16[1,208,128]{2,1,0:T(8,128)(2,1)S(1)}, bf16[1,208,128]{2,1,0:T(8,128)(2,1)S(1)}, u32[]{:S(2)}, u32[]{:S(2)}) collective-permute-start(bf16[1,208,128]{2,1,0:T(8,128)(2,1)S(1)} %get-tuple-element.83), channel_id=1, source_target_pairs={{0,12},{1,13},{2,14},{3,15},{4,8},{5,9},{6,10},{7,11},{8,4},{9,5},... | collective-permute-start | bytes 159752 | tf_op jit(solution)/shard_map/ppermute | solution.py:390
  55.1 5.5 %collective-permute-start.24 = (bf16[1,208,128]{2,1,0:T(8,128)(2,1)S(1)}, bf16[1,208,128]{2,1,0:T(8,128)(2,1)S(1)}, u32[]{:S(2)}, u32[]{:S(2)}) collective-permute-start(bf16[1,208,128]{2,1,0:T(8,128)(2,1)S(1)} %get-tuple-element.84), channel_id=1, source_target_pairs={{0,8},{1,9},{2,10},{3,11},{4,12},{5,13},{6,14},{7,15},{8,0},{9,1},... | collective-permute-start | bytes 159752 | tf_op jit(solution)/shard_map/ppermute | solution.py:390
  55.5 5.2 %collective-permute-start.25 = (bf16[1,208,128]{2,1,0:T(8,128)(2,1)S(1)}, bf16[1,208,128]{2,1,0:T(8,128)(2,1)S(1)}, u32[]{:S(2)}, u32[]{:S(2)}) collective-permute-start(bf16[1,208,128]{2,1,0:T(8,128)(2,1)S(1)} %get-tuple-element.85), channel_id=1, source_target_pairs={{0,4},{1,5},{2,6},{3,7},{4,0},{5,1},{6,2},{7,3},{8,12},{9,13},{10,... | collective-permute-start | bytes 159752 | tf_op jit(solution)/shard_map/ppermute | solution.py:390
  58.2 5.1 %collective-permute-start.22 = (bf16[1,208,128]{2,1,0:T(8,128)(2,1)S(1)}, bf16[1,208,128]{2,1,0:T(8,128)(2,1)S(1)}, u32[]{:S(2)}, u32[]{:S(2)}) collective-permute-start(bf16[1,208,128]{2,1,0:T(8,128)(2,1)S(1)} %get-tuple-element.82), channel_id=1, source_target_pairs={{0,8},{1,9},{2,10},{3,11},{4,12},{5,13},{6,14},{7,15},{8,0},{9,1},... | collective-permute-start | bytes 159752 | tf_op jit(solution)/shard_map/ppermute | solution.py:390
  63.9 4.2 %collective-permute-start.26 = (bf16[208,128]{1,0:T(8,128)(2,1)S(1)}, bf16[208,128]{1,0:T(8,128)(2,1)S(1)}, u32[]{:S(2)}, u32[]{:S(2)}) collective-permute-start(bf16[208,128]{1,0:T(8,128)(2,1)S(1)} %get-tuple-element.87), channel_id=1, source_target_pairs={{0,16},{16,0},{1,17},{17,1},{2,18},{18,2},{3,19},{19,3},{4,20},{20... | collective-permute-start | bytes 159752 | tf_op jit(solution)/shard_map/ppermute | solution.py:392

commit v13 on v9

--- a/solution.py
+++ b/solution.py
@@ -99,30 +99,45 @@
         window[v, pl.ds(at, width), :] = pooled[pl.ds(LEFT + 1 - v, width), :].astype(BF16)
 
 
-def row_pack_kernel(has_second, flags, centre, col_a, col_b, *refs):
+def facing(group):
+    above = [group[0], 0.75 * (group[0] + group[1]) + 0.25 * group[2]]
+    below = [0.25 * group[3] + 0.75 * (group[4] + group[5]), group[5]]
+    return above, below
+
+
+def row_pack_kernel(flags, centre, *outs):
+    images, height2, width = centre.shape[0], centre.shape[1], centre.shape[2] - 8
+    row_odd = flags[ROW_ODD] == 1
+    for i in range(images):
+        above, below = facing([centre[i, r, :width, :] for r in (0, 1, 2, height2 - 3, height2 - 2, height2 - 1)])
+        for second, out in enumerate(outs):
+            for n in range(2):
+                odd, even = (below[n], above[n]) if second else (above[n], below[n])
+                at = (2 * i + n) * width
+                out[at : at + width, :] = jnp.where(row_odd, odd, even).astype(BF16)
+
+
+def corner_pack_kernel(has_second, flags, centre, col_a, col_b, *refs):
     outs, (cells_out, beside_out, ends) = refs[: 2 if has_second else 1], refs[-3:]
     images, height2, width = centre.shape[0], centre.shape[1], centre.shape[2] - 8
     row_odd = flags[ROW_ODD] == 1
     lines = [0, 1, 2, height2 - 3, height2 - 2, height2 - 1]
     for i in range(images):
         cells, beside = pool_columns(flags, centre, col_a, col_b, i, lines)
+        added = []
         for n in range(6):
             cells_out[i, n] = cells[n]
             beside_out[i, n] = beside[n]
-        for group, is_end in ((cells, False), (beside, True)):
-            above = [group[0], 0.75 * (group[0] + group[1]) + 0.25 * group[2]]
-            below = [0.25 * group[3] + 0.75 * (group[4] + group[5]), group[5]]
-            for second in range(len(outs)):
-                for n in range(2):
-                    odd, even = (below[n], above[n]) if second else (above[n], below[n])
-                    value = jnp.where(row_odd, odd, even)
-                    if is_end:
-                        ends[second, (2 * i + n) * 2 : (2 * i + n) * 2 + 2, :] = value
-                    else:
-                        at = (2 * i + n) * width
-                        outs[second][at : at + width, :] = value.astype(BF16)
+            more = cells[n] - centre[i, lines[n], :width, :]
+            added.append(jnp.concatenate([more[:1], more[width - 1 :], beside[n]], axis=0))
+        above, below = facing(added)
+        for second in range(len(outs)):
+            for n in range(2):
+                odd, even = (below[n], above[n]) if second else (above[n], below[n])
+                at = (2 * i + n) * 4
+                ends[second, at : at + 4, :] = jnp.where(row_odd, odd, even)
     for second in range(len(outs)):
-        outs[second][2 * images * width :, :] = ends[second].astype(BF16)
+        outs[second][...] = ends[second].astype(BF16)
 
 
 def main_kernel(flags, centre, col_a, col_b, weight, window, acc, pooled):
@@ -160,26 +175,28 @@
 
 def edge_kernel(has_second, flags, *refs):
     sides = 2 if has_second else 1
-    rows, (cells, beside, _, acc, weight) = refs[:sides], refs[sides : sides + 5]
-    *grads, window, pooled, ends, total = refs[sides + 5 :]
+    rows, corners, (cells, beside, _, acc, weight) = refs[:sides], refs[sides : 2 * sides], refs[2 * sides : 2 * sides + 5]
+    *grads, window, pooled, ends, total = refs[2 * sides + 5 :]
     images, width = cells.shape[0], cells.shape[2]
     depths, count = acc.shape[:2]
     line = images * width
     height = count // line
     row_odd, top, bottom = flags[ROW_ODD] == 1, flags[TOP] == 1, flags[BOTTOM] == 1
     for n in range(sides):
-        ends[n] = rows[n][2 * line :, :].astype(F32)
+        ends[n] = corners[n][...].astype(F32)
     pooled[...] = jnp.zeros_like(pooled)
+    cell = lax.broadcasted_iota(jnp.int32, (width, cells.shape[3]), 0)
     for i in range(images):
         for_rows = []
         for is_end, own in ((False, cells), (True, beside)):
             def came(from_above, n):
                 def of(ref_at):
+                    end, at = (2 * i + n) * 4, (2 * i + n) * width
                     if is_end:
-                        at = (2 * i + n) * 2
-                        return ends[ref_at, at : at + 2, :]
-                    at = (2 * i + n) * width
-                    return rows[ref_at][at : at + width, :].astype(F32)
+                        return ends[ref_at, end + 2 : end + 4, :]
+                    more = jnp.where(cell == 0, ends[ref_at, end : end + 1, :], 0.0)
+                    more = jnp.where(cell == width - 1, ends[ref_at, end + 1 : end + 2, :], more)
+                    return rows[ref_at][at : at + width, :].astype(F32) + more
 
                 first = of(0)
                 second = of(1) if has_second else jnp.zeros_like(first)
@@ -462,14 +479,16 @@
         scratch=(pltpu.VMEM((channels // 128, height2, LEFT + width2 + 8, 128), F32),),
         scalars=0,
     )
-    *row_out, cells, beside = vmem_call(
-        functools.partial(row_pack_kernel, has_second),
-        [sds(2 * images * (width + 2), channels)] * sides
+    row_out = vmem_call(row_pack_kernel, [sds(2 * line, channels)] * sides, (flags, centre))
+    came_rows = [swap(row_out[n], paired(rows, n), None) for n in range(sides)]
+    *corner_out, cells, beside = vmem_call(
+        functools.partial(corner_pack_kernel, has_second),
+        [sds(8 * images, channels)] * sides
         + [sds(images, 6, width, channels, dtype=F32), sds(images, 6, 2, channels, dtype=F32)],
         (flags, centre, col_a, col_b),
-        scratch=(pltpu.VMEM((sides, 4 * images, channels), F32),),
-    )
-    came_rows = [swap(row_out[n], paired(rows, n), None) for n in range(sides)]
+        scratch=(pltpu.VMEM((sides, 8 * images, channels), F32),),
+    )
+    came_rows += [swap(corner_out[n], paired(rows, n), None) for n in range(sides)]
     conv_flops = 2 * patches * depths * 9 * channels * channels
     window, acc = vmem_call(
         main_kernel,
@@ -477,7 +496,7 @@
         (flags, centre, col_a, col_b, conv_weight),
         scratch=(pltpu.VMEM((height, LEFT + width + 8, channels), F32),),
         flops=conv_flops,
-        after=(row_out[0],),
+        after=(corner_out[0],),
     )
     *grads, window = vmem_call(
         functools.partial(edge_kernel, has_second),
@@ -485,11 +504,11 @@
         [flags] + came_rows + [cells, beside, window, acc, conv_weight],
         scratch=(
             pltpu.VMEM((4, LEFT + width + 8, channels), F32),
-            pltpu.VMEM((sides, 4 * images, channels), F32),
+            pltpu.VMEM((sides, 8 * images, channels), F32),
             pltpu.VMEM((patches, channels), F32),
         ),
         flops=conv_flops // 4,
-        aliases={sides + 3: CHIPS},
+        aliases={2 * sides + 3: CHIPS},
     )
     came = [xor_move(grads[chip], 2 * chip, False) for chip in range(CHIPS - 1, 0, -1)]
     came = [grads[0]] + came[::-1]

time: 67.2 us -> 66.7 us (level)
  local copies, waits for them, and re-layouts: 3 us -> 1.34 us
  starting transfers between devices: 25.7 us -> 26.8 us
    unnamed x12 -> x10, local copies, waits for them, and re-layouts: 2.91 us -> 1.24 us
    ppermute x1, starting transfers between devices: 0.88 us -> 1.58 us  [xor_move(): return lax.ppermute(block, ('dp', 'tile'), route)]
    ppermute x3, waiting for transfers between devices: 7.48 us -> 6.79 us  [xor_move(): return lax.ppermute(block, 'dp', [(0, 1), (1, 0)])]
    pallas_call x15 -> x16, Pallas kernels: 16.1 us -> 16.6 us  [vmem_call(): pl.pallas_call(run, out_shape=out_shape, in_specs=specs, out_specs=jax.tr...]
    ppermute x3 -> x4, starting transfers between devices: 6.19 us -> 6.71 us  [swap(): return lax.ppermute(block, 'tile', tile_route(row_pairs, col_pairs, rows))]
  transfers between devices with their start and end apart: 26 -> 27, of which waited for: 13 -> 14; matrix products, arithmetic and copies ran while one was open for 0% -> 0% of each run, Pallas kernels for 17% -> 19%
where the time goes in v13:
time: 66.7 us; the launch traced here: 66.5 us
  starting transfers between devices  26.8 us (40%)
  waiting for transfers between devices  19.7 us (30%)
  Pallas kernels  16.6 us (25%)
  local copies, waits for them, and re-layouts  1.34 us (2%)
  other arithmetic  1.19 us (2%)
  between operations  0.88 us (1%)
    pallas_call x16, Pallas kernels, vmem_call(): pl.pallas_call(run, out_shape=out_shape, in_specs=specs, out_specs=jax.tr...  16.6 us
    ppermute x19, starting transfers between devices, xor_move(): return lax.ppermute(block, 'tile', [(t, t ^ apart) for t in range(tiles)])  14.1 us
    ppermute x19, waiting for transfers between devices, xor_move(): return lax.ppermute(block, 'tile', [(t, t ^ apart) for t in range(tiles)])  7.99 us
    ppermute x3, waiting for transfers between devices, xor_move(): return lax.ppermute(block, 'dp', [(0, 1), (1, 0)])  6.79 us
    ppermute x4, starting transfers between devices, swap(): return lax.ppermute(block, 'tile', tile_route(row_pairs, col_pairs, rows))  6.71 us
    ppermute x3, starting transfers between devices, xor_move(): return lax.ppermute(block, 'dp', [(0, 1), (1, 0)])  4.47 us
    ppermute x1, waiting for transfers between devices, xor_move(): return lax.ppermute(block, ('dp', 'tile'), route)  3.57 us
    ppermute x1, starting transfers between devices, xor_move(): return lax.ppermute(block, ('dp', 'tile'), route)  1.58 us
  transfers between devices with their start and end apart: 27, of which 14 were waited for; matrix products, arithmetic and copies ran while one was open for 0% of the time, Pallas kernels for 19%

profile of v13, /device:TPU:0, one launch (start us, length us, event | category | flops | bytes accessed | tf_op | source)
XLA Modules:
  0.0 66.5 jit_solution(4005303510763289971)
XLA Ops:
  0.7 1.2 %broadcast_select_fusion = (bf16[4,16,4,256]{3,2,1,0:T(4,128)(2,1)S(1)}, bf16[4,16,4,256]{3,2,1,0:T(4,128)(2,1)S(1)}) fusion(pred[]{:T(512)S(6)} %eq.27, bf16[4,16,32,256]{3,2,1,0:T(8,128)(2,1)} %refs_0_.1), kind=kLoop, calls=%fused_computation | loop fusion | flops 131072 | bytes 524289 | tf_op jit(solution)/shard_map/jit(_where)/select_n | solution.py:473
  1.9 3.1 %collective-permute-start.2 = (bf16[4,16,4,256]{3,2,1,0:T(4,128)(2,1)S(1)}, bf16[4,16,4,256]{3,2,1,0:T(4,128)(2,1)S(1)}, u32[]{:S(2)}, u32[]{:S(2)}) collective-permute-start(bf16[4,16,4,256]{3,2,1,0:T(4,128)(2,1)S(1)} %get-tuple-element.82), channel_id=1, source_target_pairs={{1,3},{3,1},{2,6},{6,2},{7,5},{5,7},{0,4},{4,0},{9,11},{11,9},{10,... | collective-permute-start | bytes 393224 | tf_op jit(solution)/shard_map/ppermute | solution.py:469
  4.9 0.0 collective-permute-start.1
  4.9 1.2 %copy-done.2 = bf16[4,16,32,256]{3,2,1,0:T(8,128)(2,1)S(1)} copy-done((bf16[4,16,32,256]{3,2,1,0:T(8,128)(2,1)S(1)}, bf16[4,16,32,256]{3,2,1,0:T(8,128)(2,1)}, u32[]{:S(2)}) %copy-start.2) | copy-done | bytes 1048600
  6.2 0.5 shard_map.68.refs_1_
  6.7 0.1 stack.71.refs_0_
  6.8 0.0 copy-start
  6.8 0.6 shard_map.69
  7.4 2.7 %collective-permute-start = (bf16[128,256]{1,0:T(8,128)(2,1)S(1)}, bf16[128,256]{1,0:T(8,128)(2,1)S(1)}, u32[]{:S(2)}, u32[]{:S(2)}) collective-permute-start(bf16[128,256]{1,0:T(8,128)(2,1)S(1)} %shard_map.69), channel_id=1, source_target_pairs={{0,8},{1,9},{3,11},{2,10},{6,14},{7,15},{5,13},{4,12},{8,0},{9,1},... | collective-permute-start | bytes 196616 | tf_op jit(solution)/shard_map/ppermute | solution.py:469
  10.0 0.0 collective-permute-done.2.refs_3_
  10.0 0.8 %shard_map.70 = (bf16[32,256]{1,0:T(8,128)(2,1)S(1)}, f32[4,6,16,256]{3,2,1,0:T(8,128)S(1)}, f32[4,6,2,256]{3,2,1,0:T(2,128)S(1)}) custom-call(s32[13]{0:T(128)S(1)} %stack.71.refs_0_, f32[4,16,24,256]{3,2,1,0:T(8,128)S(1)} %shard_map.68.refs_1_, bf16[4,16,4,256]{3,2,1,0:T(4,128)(2,1)S(1)} %collective-permute-done.1.refs_2_, ...), custom_call_target="tpu_custom_call" | custom-call | bytes 2293812 | tf_op jit(solution)/shard_map/pallas_call | solution.py:377
  10.8 1.0 %collective-permute-start.3 = (bf16[32,256]{1,0:T(8,128)(2,1)S(1)}, bf16[32,256]{1,0:T(8,128)(2,1)S(1)}, u32[]{:S(2)}, u32[]{:S(2)}) collective-permute-start(bf16[32,256]{1,0:T(8,128)(2,1)S(1)} %get-tuple-element.42.refs_5_), channel_id=1, source_target_pairs={{0,8},{1,9},{3,11},{2,10},{6,14},{7,15},{5,13},{4,12},{8,0},{9,1},... | collective-permute-start | bytes 49160 | tf_op jit(solution)/shard_map/ppermute | solution.py:469
  11.8 2.4 %shard_map.71 = (bf16[3,640,256]{2,1,0:T(8,128)(2,1)S(1)}, f32[2,512,256]{2,1,0:T(8,128)S(1)}) custom-call(s32[13]{0:T(128)S(1)} %stack.71.refs_0_, f32[4,16,24,256]{3,2,1,0:T(8,128)S(1)} %shard_map.68.refs_1_, bf16[4,16,4,256]{3,2,1,0:T(4,128)(2,1)S(1)} %collective-permute-done.1.refs_2_, bf16[4,16,4,256]{3,2,1,0:T(4,128)(2,1)S(1)} %collective-permute-done.2.refs_3_, ...), custom_call_target="tpu_custom_call" | custom-call | flops 1207959552 | bytes 6225972 | tf_op jit(solution)/shard_map/pallas_call | solution.py:377
  14.2 0.1 collective-permute-done.refs_1_
  14.2 1.3 %collective-permute-done.3.refs_2_ = bf16[32,256]{1,0:T(8,128)(2,1)S(1)} collective-permute-done((bf16[32,256]{1,0:T(8,128)(2,1)S(1)}, bf16[32,256]{1,0:T(8,128)(2,1)S(1)}, u32[]{:S(2)}, u32[]{:S(2)}) %collective-permute-start.3) | collective-permute-done | bytes 16416 | tf_op jit(solution)/shard_map/ppermute | solution.py:469
  15.5 1.6 %shard_map.72 = (bf16[2,2,64,256]{3,2,1,0:T(8,128)(2,1)S(1)}, bf16[2,2,64,256]{3,2,1,0:T(8,128)(2,1)S(1)}, bf16[2,2,64,256]{3,2,1,0:T(8,128)(2,1)S(1)}, bf16[2,2...) custom-call(s32[13]{0:T(128)S(1)} %stack.71.refs_0_, ...), custom_call_target="tpu_custom_call", output_to_operand_aliasing={{4}: (5, {})} | custom-call | flops 301989888 | bytes 6422580 | tf_op jit(solution)/shard_map/pallas_call | solution.py:377
  17.1 1.6 %collective-permute-start.4 = (bf16[2,2,64,256]{3,2,1,0:T(8,128)(2,1)S(1)}, bf16[2,2,64,256]{3,2,1,0:T(8,128)(2,1)S(1)}, u32[]{:S(2)}, u32[]{:S(2)}) collective-permute-start(bf16[2,2,64,256]{3,2,1,0:T(8,128)(2,1)S(1)} %get-tuple-element.48), channel_id=1, source_target_pairs={{0,2},{1,3},{2,0},{3,1},{4,6},{5,7},{6,4},{7,5},{8,10},{9,11},{10,... | collective-permute-start | bytes 393224 | tf_op jit(solution)/shard_map/ppermute | solution.py:396
  18.8 0.4 collective-permute-start.5
  19.2 1.5 %collective-permute-start.6 = (bf16[2,2,64,256]{3,2,1,0:T(8,128)(2,1)S(1)}, bf16[2,2,64,256]{3,2,1,0:T(8,128)(2,1)S(1)}, u32[]{:S(2)}, u32[]{:S(2)}) collective-permute-start(bf16[2,2,64,256]{3,2,1,0:T(8,128)(2,1)S(1)} %get-tuple-element.50), channel_id=1, source_target_pairs={{0,6},{1,7},{2,4},{3,5},{4,2},{5,3},{6,0},{7,1},{8,14},{9,15},{10,... | collective-permute-start | bytes 393224 | tf_op jit(solution)/shard_map/ppermute | solution.py:396
  20.7 2.1 %shard_map.74 = (bf16[8,208,256]{2,1,0:T(8,128)(2,1)S(1)}, bf16[2,208,256]{2,1,0:T(8,128)(2,1)S(1)}, bf16[2,208,256]{2,1,0:T(8,128)(2,1)S(1)}, bf16[2,208,256]{2...) custom-call(s32[13]{0:T(128)S(1)} %stack.71.refs_0_, ...), custom_call_target="tpu_custom_call" | custom-call | flops 1207959552 | bytes 3866676 | tf_op jit(solution)/shard_map/pallas_call | solution.py:377
  22.8 0.0 copy-start.1
  22.8 0.1 collective-permute-start.8
  22.9 0.5 collective-permute-start.9
  23.4 0.0 collective-permute-done.4.refs_1_.refs_2_
  23.4 0.1 collective-permute-start.10
  23.4 0.9 %collective-permute-done.5.refs_2_.refs_3_ = bf16[2,2,64,256]{3,2,1,0:T(8,128)(2,1)S(1)} collective-permute-done((bf16[2,2,64,256]{3,2,1,0:T(8,128)(2,1)S(1)}, bf16[2,2,64,256]{3,2,1,0:T(8,128)(2,1)S(1)}, u32[]{:S(2)}, u32[]{:S(2)}) %collective-permute-start.5) | collective-permute-done | bytes 131104 | tf_op jit(solution)/shard_map/ppermute | solution.py:396
  24.4 1.5 %collective-permute-done.6.refs_3_.refs_4_ = bf16[2,2,64,256]{3,2,1,0:T(8,128)(2,1)S(1)} collective-permute-done((bf16[2,2,64,256]{3,2,1,0:T(8,128)(2,1)S(1)}, bf16[2,2,64,256]{3,2,1,0:T(8,128)(2,1)S(1)}, u32[]{:S(2)}, u32[]{:S(2)}) %collective-permute-start.6) | collective-permute-done | bytes 131104 | tf_op jit(solution)/shard_map/ppermute | solution.py:396
  25.9 0.1 collective-permute-start.7
  26.0 0.0 collective-permute-done.8.refs_2_
  26.0 0.0 collective-permute-done.10.refs_4_
  26.0 0.0 collective-permute-done.11.refs_5_
  26.0 0.7 %shard_map.75 = (f32[8,208,128]{2,1,0:T(8,128)S(1)}, bf16[8,208,128]{2,1,0:T(8,128)(2,1)S(1)}) custom-call(s32[13]{0:T(128)S(1)} %stack.71.refs_0_, bf16[8,208,256]{2,1,0:T(8,128)(2,1)S(1)} %get-tuple-element.53.refs_1_, bf16[2,208,256]{2,1,0:T(8,128)(2,1)S(1)} %collective-permute-done.8.refs_2_, bf16[2,208,256]{2,1,0:T(8,128)(2,1)S(1)} %collective-permute-done.9.refs_3_, ...), custom_call_target="tpu_custom_call" | custom-call | bytes 2981940 | tf_op jit(solution)/shard_map/pallas_call | solution.py:377
  26.7 1.6 %collective-permute-start.19 = (bf16[8,208,128]{2,1,0:T(8,128)(2,1)S(1)}, bf16[8,208,128]{2,1,0:T(8,128)(2,1)S(1)}, u32[]{:S(2)}, u32[]{:S(2)}) collective-permute-start(bf16[8,208,128]{2,1,0:T(8,128)(2,1)S(1)} %get-tuple-element.69), channel_id=1, source_target_pairs={{0,16},{16,0},{1,17},{17,1},{2,18},{18,2},{3,19},{19,3},{4,20},{20... | collective-permute-start | bytes 1277960 | tf_op jit(solution)/shard_map/ppermute | solution.py:398
  28.3 1.5 %shard_map.76 = (bf16[8,208,256]{2,1,0:T(8,128)(2,1)S(1)}, bf16[2,208,256]{2,1,0:T(8,128)(2,1)S(1)}, bf16[2,208,256]{2,1,0:T(8,128)(2,1)S(1)}, bf16[2,208,256]{2...) custom-call(s32[13]{0:T(128)S(1)} %stack.71.refs_0_, ...), custom_call_target="tpu_custom_call" | custom-call | flops 536870912 | bytes 5767220 | tf_op jit(solution)/shard_map/pallas_call | solution.py:377
  29.8 0.3 collective-permute-start.12
  30.0 0.3 collective-permute-start.13
  30.4 0.2 collective-permute-start.14
  30.6 0.3 collective-permute-start.15
  30.9 0.4 collective-permute-done.12.refs_2_
  31.3 0.3 collective-permute-done.13.refs_3_
  31.6 0.3 collective-permute-done.14.refs_4_
  31.9 0.3 collective-permute-done.15.refs_5_
  32.2 0.7 %shard_map.77 = (f32[4,208,128]{2,1,0:T(8,128)S(1)}, bf16[4,208,128]{2,1,0:T(8,128)(2,1)S(1)}, bf16[4,208,128]{2,1,0:T(8,128)(2,1)S(1)}, bf16[4,208,128]{2,1,0:T(8,128)(2,1)S(1)}) custom-call(s32[13]{0:T(128)S(1)} %stack.71.refs_0_, bf16[8,208,256]{2,1,0:T(8,128)(2,1)S(1)} %get-tuple-element.60.refs_1_, ...), custom_call_target="tpu_custom_call" | custom-call | bytes 2768948 | tf_op jit(solution)/shard_map/pallas_call | solution.py:377
  33.0 1.6 %collective-permute-start.16 = (bf16[4,208,128]{2,1,0:T(8,128)(2,1)S(1)}, bf16[4,208,128]{2,1,0:T(8,128)(2,1)S(1)}, u32[]{:S(2)}, u32[]{:S(2)}) collective-permute-start(bf16[4,208,128]{2,1,0:T(8,128)(2,1)S(1)} %get-tuple-element.66), channel_id=1, source_target_pairs={{0,18},{1,19},{2,16},{3,17},{4,22},{5,23},{6,20},{7,21},{8,26},{9,... | collective-permute-start | bytes 638984 | tf_op jit(solution)/shard_map/ppermute | solution.py:400
  34.5 1.4 %collective-permute-start.17 = (bf16[4,208,128]{2,1,0:T(8,128)(2,1)S(1)}, bf16[4,208,128]{2,1,0:T(8,128)(2,1)S(1)}, u32[]{:S(2)}, u32[]{:S(2)}) collective-permute-start(bf16[4,208,128]{2,1,0:T(8,128)(2,1)S(1)} %get-tuple-element.67), channel_id=1, source_target_pairs={{0,16},{16,0},{1,17},{17,1},{2,18},{18,2},{3,19},{19,3},{4,20},{20... | collective-permute-start | bytes 638984 | tf_op jit(solution)/shard_map/ppermute | solution.py:398
  35.9 0.6 collective-permute-start.18
  36.5 2.9 %collective-permute-done.19.refs_2_ = bf16[8,208,128]{2,1,0:T(8,128)(2,1)S(1)} collective-permute-done((bf16[8,208,128]{2,1,0:T(8,128)(2,1)S(1)}, bf16[8,208,128]{2,1,0:T(8,128)(2,1)S(1)}, u32[]{:S(2)}, u32[]{:S(2)}) %collective-permute-start.19) | collective-permute-done | bytes 426016 | tf_op jit(solution)/shard_map/ppermute | solution.py:398
  39.4 0.6 shard_map.78
  40.1 1.2 %collective-permute-start.20 = (bf16[4,208,128]{2,1,0:T(8,128)(2,1)S(1)}, bf16[4,208,128]{2,1,0:T(8,128)(2,1)S(1)}, u32[]{:S(2)}, u32[]{:S(2)}) collective-permute-start(bf16[4,208,128]{2,1,0:T(8,128)(2,1)S(1)} %get-tuple-element.71), channel_id=1, source_target_pairs={{0,4},{1,5},{2,6},{3,7},{4,0},{5,1},{6,2},{7,3},{8,12},{9,13},{10,... | collective-permute-start | bytes 638984 | tf_op jit(solution)/shard_map/ppermute | solution.py:396
  41.3 3.6 %collective-permute-done.16.refs_2_ = bf16[4,208,128]{2,1,0:T(8,128)(2,1)S(1)} collective-permute-done((bf16[4,208,128]{2,1,0:T(8,128)(2,1)S(1)}, bf16[4,208,128]{2,1,0:T(8,128)(2,1)S(1)}, u32[]{:S(2)}, u32[]{:S(2)}) %collective-permute-start.16) | collective-permute-done | bytes 213024 | tf_op jit(solution)/shard_map/ppermute | solution.py:400
  44.9 3.3 %collective-permute-done.17.refs_3_ = bf16[4,208,128]{2,1,0:T(8,128)(2,1)S(1)} collective-permute-done((bf16[4,208,128]{2,1,0:T(8,128)(2,1)S(1)}, bf16[4,208,128]{2,1,0:T(8,128)(2,1)S(1)}, u32[]{:S(2)}, u32[]{:S(2)}) %collective-permute-start.17) | collective-permute-done | bytes 213024 | tf_op jit(solution)/shard_map/ppermute | solution.py:398
  48.2 0.7 %shard_map.79 = (f32[1,208,128]{2,1,0:T(8,128)S(1)}, bf16[1,208,128]{2,1,0:T(8,128)(2,1)S(1)}, bf16[1,208,128]{2,1,0:T(8,128)(2,1)S(1)}, bf16[1,208,128]{2,1,0:T...) custom-call(s32[13]{0:T(128)S(1)} %stack.71.refs_0_, ...), custom_call_target="tpu_custom_call" | custom-call | bytes 2289716 | tf_op jit(solution)/shard_map/pallas_call | solution.py:377
  48.9 1.5 %collective-permute-start.21 = (bf16[2,208,128]{2,1,0:T(8,128)(2,1)S(1)}, bf16[2,208,128]{2,1,0:T(8,128)(2,1)S(1)}, u32[]{:S(2)}, u32[]{:S(2)}) collective-permute-start(bf16[2,208,128]{2,1,0:T(8,128)(2,1)S(1)} %get-tuple-element.73), channel_id=1, source_target_pairs={{0,2},{1,3},{2,0},{3,1},{4,6},{5,7},{6,4},{7,5},{8,10},{9,11},{10,... | collective-permute-start | bytes 319496 | tf_op jit(solution)/shard_map/ppermute | solution.py:396
  50.3 2.4 %collective-permute-start.23 = (bf16[1,208,128]{2,1,0:T(8,128)(2,1)S(1)}, bf16[1,208,128]{2,1,0:T(8,128)(2,1)S(1)}, u32[]{:S(2)}, u32[]{:S(2)}) collective-permute-start(bf16[1,208,128]{2,1,0:T(8,128)(2,1)S(1)} %get-tuple-element.77), channel_id=1, source_target_pairs={{0,12},{1,13},{2,14},{3,15},{4,8},{5,9},{6,10},{7,11},{8,4},{9,5},... | collective-permute-start | bytes 159752 | tf_op jit(solution)/shard_map/ppermute | solution.py:396
  52.7 2.0 %collective-permute-start.25 = (bf16[1,208,128]{2,1,0:T(8,128)(2,1)S(1)}, bf16[1,208,128]{2,1,0:T(8,128)(2,1)S(1)}, u32[]{:S(2)}, u32[]{:S(2)}) collective-permute-start(bf16[1,208,128]{2,1,0:T(8,128)(2,1)S(1)} %get-tuple-element.79), channel_id=1, source_target_pairs={{0,4},{1,5},{2,6},{3,7},{4,0},{5,1},{6,2},{7,3},{8,12},{9,13},{10,... | collective-permute-start | bytes 159752 | tf_op jit(solution)/shard_map/ppermute | solution.py:396
  54.7 0.6 shard_map.80
  55.3 1.0 %collective-permute-start.22 = (bf16[1,208,128]{2,1,0:T(8,128)(2,1)S(1)}, bf16[1,208,128]{2,1,0:T(8,128)(2,1)S(1)}, u32[]{:S(2)}, u32[]{:S(2)}) collective-permute-start(bf16[1,208,128]{2,1,0:T(8,128)(2,1)S(1)} %get-tuple-element.76), channel_id=1, source_target_pairs={{0,8},{1,9},{2,10},{3,11},{4,12},{5,13},{6,14},{7,15},{8,0},{9,1},... | collective-permute-start | bytes 159752 | tf_op jit(solution)/shard_map/ppermute | solution.py:396
  56.3 2.5 %collective-permute-done.24.refs_5_ = bf16[1,208,128]{2,1,0:T(8,128)(2,1)S(1)} collective-permute-done((bf16[1,208,128]{2,1,0:T(8,128)(2,1)S(1)}, bf16[1,208,128]{2,1,0:T(8,128)(2,1)S(1)}, u32[]{:S(2)}, u32[]{:S(2)}) %collective-permute-start.24) | collective-permute-done | bytes 53280 | tf_op jit(solution)/shard_map/ppermute | solution.py:396
  58.8 1.7 %collective-permute-done.22.refs_2_ = bf16[1,208,128]{2,1,0:T(8,128)(2,1)S(1)} collective-permute-done((bf16[1,208,128]{2,1,0:T(8,128)(2,1)S(1)}, bf16[1,208,128]{2,1,0:T(8,128)(2,1)S(1)}, u32[]{:S(2)}, u32[]{:S(2)}) %collective-permute-start.22) | collective-permute-done | bytes 53280 | tf_op jit(solution)/shard_map/ppermute | solution.py:396
  60.5 0.6 shard_map.82
  61.1 1.6 %collective-permute-start.26 = (bf16[208,128]{1,0:T(8,128)(2,1)S(1)}, bf16[208,128]{1,0:T(8,128)(2,1)S(1)}, u32[]{:S(2)}, u32[]{:S(2)}) collective-permute-start(bf16[208,128]{1,0:T(8,128)(2,1)S(1)} %get-tuple-element.81), channel_id=1, source_target_pairs={{0,16},{16,0},{1,17},{17,1},{2,18},{18,2},{3,19},{19,3},{4,20},{20... | collective-permute-start | bytes 159752 | tf_op jit(solution)/shard_map/ppermute | solution.py:398
  62.7 2.1 %shard_map.81 = bf16[4,2,128,1024]{3,2,1,0:T(8,128)(2,1)} custom-call(bf16[2,512,256]{2,1,0:T(8,128)(2,1)S(1)} %get-tuple-element.59.refs_6_.refs_0_, bf16[2,1024,256]{2,1,0:T(8,128)(2,1)S(1)} %copy-done.3, f32[1,208,128]{2,1,0:T(8,128)S(1)} %get-tuple-element.75.refs_2_.refs_1_), custom_call_target="tpu_custom_call" | custom-call | flops 536870912 | bytes 3670016 | tf_op jit(solution)/shard_map/pallas_call | solution.py:377
  64.7 0.6 collective-permute-done.26.refs_2_
  65.3 1.2 %shard_map.83 = f32[208,256]{1,0:T(8,128)} custom-call(s32[13]{0:T(128)S(1)} %stack.71.refs_0_, f32[208,128]{1,0:T(8,128)S(1)} %get-tuple-element.80.refs_1_, bf16[208,128]{1,0:T(8,128)(2,1)S(1)} %collective-permute-done.26.refs_2_), custom_call_target="tpu_custom_call" | custom-call | bytes 372788 | tf_op jit(solution)/shard_map/pallas_call | solution.py:377
  (18 shorter events, 0.1 us)
Async XLA Ops:
  1.9 8.2 %collective-permute-start.2 = (bf16[4,16,4,256]{3,2,1,0:T(4,128)(2,1)S(1)}, bf16[4,16,4,256]{3,2,1,0:T(4,128)(2,1)S(1)}, u32[]{:S(2)}, u32[]{:S(2)}) collective-permute-start(bf16[4,16,4,256]{3,2,1,0:T(4,128)(2,1)S(1)} %get-tuple-element.82), channel_id=1, source_target_pairs={{1,3},{3,1},{2,6},{6,2},{7,5},{5,7},{0,4},{4,0},{9,11},{11,9},{10,... | collective-permute-start | bytes 393224 | tf_op jit(solution)/shard_map/ppermute | solution.py:469
  4.9 5.1 %collective-permute-start.1 = (bf16[4,16,4,256]{3,2,1,0:T(4,128)(2,1)S(1)}, bf16[4,16,4,256]{3,2,1,0:T(4,128)(2,1)S(1)}, u32[]{:S(2)}, u32[]{:S(2)}) collective-permute-start(bf16[4,16,4,256]{3,2,1,0:T(4,128)(2,1)S(1)} %get-tuple-element.83), channel_id=1, source_target_pairs={{0,1},{1,0},{3,2},{2,3},{6,7},{7,6},{5,4},{4,5},{8,9},{9,8},{11,10... | collective-permute-start | bytes 393224 | tf_op jit(solution)/shard_map/ppermute | solution.py:469
  4.9 1.2 %copy-start.2 = (bf16[4,16,32,256]{3,2,1,0:T(8,128)(2,1)S(1)}, bf16[4,16,32,256]{3,2,1,0:T(8,128)(2,1)}, u32[]{:S(2)}) copy-start(bf16[4,16,32,256]{3,2,1,0:T(8,128)(2,1)} %refs_0_.1) | copy-start | bytes 3145732
  6.8 5.0 %copy-start = (bf16[2,3,3,256,256]{4,3,2,1,0:T(8,128)(2,1)S(1)}, bf16[2,3,3,256,256]{4,3,2,1,0:T(8,128)(2,1)}, u32[]{:S(2)}) copy-start(bf16[2,3,3,256,256]{4,3,2,1,0:T(8,128)(2,1)} %refs_7_.1) | copy-start | bytes 7077892
  7.4 6.9 %collective-permute-start = (bf16[128,256]{1,0:T(8,128)(2,1)S(1)}, bf16[128,256]{1,0:T(8,128)(2,1)S(1)}, u32[]{:S(2)}, u32[]{:S(2)}) collective-permute-start(bf16[128,256]{1,0:T(8,128)(2,1)S(1)} %shard_map.69), channel_id=1, source_target_pairs={{0,8},{1,9},{3,11},{2,10},{6,14},{7,15},{5,13},{4,12},{8,0},{9,1},... | collective-permute-start | bytes 196616 | tf_op jit(solution)/shard_map/ppermute | solution.py:469
  10.8 4.7 %collective-permute-start.3 = (bf16[32,256]{1,0:T(8,128)(2,1)S(1)}, bf16[32,256]{1,0:T(8,128)(2,1)S(1)}, u32[]{:S(2)}, u32[]{:S(2)}) collective-permute-start(bf16[32,256]{1,0:T(8,128)(2,1)S(1)} %get-tuple-element.42.refs_5_), channel_id=1, source_target_pairs={{0,8},{1,9},{3,11},{2,10},{6,14},{7,15},{5,13},{4,12},{8,0},{9,1},... | collective-permute-start | bytes 49160 | tf_op jit(solution)/shard_map/ppermute | solution.py:469
  15.5 5.2 %copy-start.4 = (bf16[4,2,8,16,256]{4,3,2,1,0:T(8,128)(2,1)S(1)}, bf16[4,2,8,16,256]{4,3,2,1,0:T(8,128)(2,1)}, u32[]{:S(2)}) copy-start(bf16[4,2,8,16,256]{4,3,2,1,0:T(8,128)(2,1)} %refs_2_.1) | copy-start | bytes 1572868
  17.1 6.2 %collective-permute-start.4 = (bf16[2,2,64,256]{3,2,1,0:T(8,128)(2,1)S(1)}, bf16[2,2,64,256]{3,2,1,0:T(8,128)(2,1)S(1)}, u32[]{:S(2)}, u32[]{:S(2)}) collective-permute-start(bf16[2,2,64,256]{3,2,1,0:T(8,128)(2,1)S(1)} %get-tuple-element.48), channel_id=1, source_target_pairs={{0,2},{1,3},{2,0},{3,1},{4,6},{5,7},{6,4},{7,5},{8,10},{9,11},{10,... | collective-permute-start | bytes 393224 | tf_op jit(solution)/shard_map/ppermute | solution.py:396
  18.8 5.6 %collective-permute-start.5 = (bf16[2,2,64,256]{3,2,1,0:T(8,128)(2,1)S(1)}, bf16[2,2,64,256]{3,2,1,0:T(8,128)(2,1)S(1)}, u32[]{:S(2)}, u32[]{:S(2)}) collective-permute-start(bf16[2,2,64,256]{3,2,1,0:T(8,128)(2,1)S(1)} %get-tuple-element.49), channel_id=1, source_target_pairs={{0,4},{1,5},{2,6},{3,7},{4,0},{5,1},{6,2},{7,3},{8,12},{9,13},{10,... | collective-permute-start | bytes 393224 | tf_op jit(solution)/shard_map/ppermute | solution.py:396
  19.2 6.7 %collective-permute-start.6 = (bf16[2,2,64,256]{3,2,1,0:T(8,128)(2,1)S(1)}, bf16[2,2,64,256]{3,2,1,0:T(8,128)(2,1)S(1)}, u32[]{:S(2)}, u32[]{:S(2)}) collective-permute-start(bf16[2,2,64,256]{3,2,1,0:T(8,128)(2,1)S(1)} %get-tuple-element.50), channel_id=1, source_target_pairs={{0,6},{1,7},{2,4},{3,5},{4,2},{5,3},{6,0},{7,1},{8,14},{9,15},{10,... | collective-permute-start | bytes 393224 | tf_op jit(solution)/shard_map/ppermute | solution.py:396
  22.8 5.5 %copy-start.1 = (bf16[4,2,128,1024]{3,2,1,0:T(8,128)(2,1)S(1)}, bf16[4,2,128,1024]{3,2,1,0:T(8,128)(2,1)}, u32[]{:S(2)}) copy-start(bf16[4,2,128,1024]{3,2,1,0:T(8,128)(2,1)} %refs_6_.1) | copy-start | bytes 6291460
  22.8 3.2 %collective-permute-start.8 = (bf16[2,208,256]{2,1,0:T(8,128)(2,1)S(1)}, bf16[2,208,256]{2,1,0:T(8,128)(2,1)S(1)}, u32[]{:S(2)}, u32[]{:S(2)}) collective-permute-start(bf16[2,208,256]{2,1,0:T(8,128)(2,1)S(1)} %get-tuple-element.54), channel_id=1, source_target_pairs={{0,1},{1,0},{2,3},{3,2},{4,5},{5,4},{6,7},{7,6},{8,9},{9,8},{10,11... | collective-permute-start | bytes 638984 | tf_op jit(solution)/shard_map/ppermute | solution.py:396
  22.9 3.1 %collective-permute-start.9 = (bf16[2,208,256]{2,1,0:T(8,128)(2,1)S(1)}, bf16[2,208,256]{2,1,0:T(8,128)(2,1)S(1)}, u32[]{:S(2)}, u32[]{:S(2)}) collective-permute-start(bf16[2,208,256]{2,1,0:T(8,128)(2,1)S(1)} %get-tuple-element.55), channel_id=1, source_target_pairs={{0,1},{1,0},{2,3},{3,2},{4,5},{5,4},{6,7},{7,6},{8,9},{9,8},{10,11... | collective-permute-start | bytes 638984 | tf_op jit(solution)/shard_map/ppermute | solution.py:396
  23.4 2.6 %collective-permute-start.10 = (bf16[2,208,256]{2,1,0:T(8,128)(2,1)S(1)}, bf16[2,208,256]{2,1,0:T(8,128)(2,1)S(1)}, u32[]{:S(2)}, u32[]{:S(2)}) collective-permute-start(bf16[2,208,256]{2,1,0:T(8,128)(2,1)S(1)} %get-tuple-element.56), channel_id=1, source_target_pairs={{0,1},{1,0},{2,3},{3,2},{4,5},{5,4},{6,7},{7,6},{8,9},{9,8},{10,11... | collective-permute-start | bytes 638984 | tf_op jit(solution)/shard_map/ppermute | solution.py:396
  24.4 1.6 %collective-permute-start.11 = (bf16[2,208,256]{2,1,0:T(8,128)(2,1)S(1)}, bf16[2,208,256]{2,1,0:T(8,128)(2,1)S(1)}, u32[]{:S(2)}, u32[]{:S(2)}) collective-permute-start(bf16[2,208,256]{2,1,0:T(8,128)(2,1)S(1)} %get-tuple-element.57), channel_id=1, source_target_pairs={{0,1},{1,0},{2,3},{3,2},{4,5},{5,4},{6,7},{7,6},{8,9},{9,8},{10,11... | collective-permute-start | bytes 638984 | tf_op jit(solution)/shard_map/ppermute | solution.py:396
  25.9 2.4 %collective-permute-start.7 = (bf16[4,2,64,256]{3,2,1,0:T(8,128)(2,1)S(1)}, bf16[4,2,64,256]{3,2,1,0:T(8,128)(2,1)S(1)}, u32[]{:S(2)}, u32[]{:S(2)}) collective-permute-start(bf16[4,2,64,256]{3,2,1,0:T(8,128)(2,1)S(1)} %shard_map.73), channel_id=1, source_target_pairs={{0,1},{1,0},{2,3},{3,2},{4,5},{5,4},{6,7},{7,6},{8,9},{9,8},{10,11... | collective-permute-start | bytes 786440 | tf_op jit(solution)/shard_map/ppermute | solution.py:396
  26.7 12.7 %collective-permute-start.19 = (bf16[8,208,128]{2,1,0:T(8,128)(2,1)S(1)}, bf16[8,208,128]{2,1,0:T(8,128)(2,1)S(1)}, u32[]{:S(2)}, u32[]{:S(2)}) collective-permute-start(bf16[8,208,128]{2,1,0:T(8,128)(2,1)S(1)} %get-tuple-element.69), channel_id=1, source_target_pairs={{0,16},{16,0},{1,17},{17,1},{2,18},{18,2},{3,19},{19,3},{4,20},{20... | collective-permute-start | bytes 1277960 | tf_op jit(solution)/shard_map/ppermute | solution.py:398
  29.8 1.5 %collective-permute-start.12 = (bf16[2,208,256]{2,1,0:T(8,128)(2,1)S(1)}, bf16[2,208,256]{2,1,0:T(8,128)(2,1)S(1)}, u32[]{:S(2)}, u32[]{:S(2)}) collective-permute-start(bf16[2,208,256]{2,1,0:T(8,128)(2,1)S(1)} %get-tuple-element.61), channel_id=1, source_target_pairs={{0,1},{1,0},{2,3},{3,2},{4,5},{5,4},{6,7},{7,6},{8,9},{9,8},{10,11... | collective-permute-start | bytes 638984 | tf_op jit(solution)/shard_map/ppermute | solution.py:396
  30.0 1.6 %collective-permute-start.13 = (bf16[2,208,256]{2,1,0:T(8,128)(2,1)S(1)}, bf16[2,208,256]{2,1,0:T(8,128)(2,1)S(1)}, u32[]{:S(2)}, u32[]{:S(2)}) collective-permute-start(bf16[2,208,256]{2,1,0:T(8,128)(2,1)S(1)} %get-tuple-element.62), channel_id=1, source_target_pairs={{0,1},{1,0},{2,3},{3,2},{4,5},{5,4},{6,7},{7,6},{8,9},{9,8},{10,11... | collective-permute-start | bytes 638984 | tf_op jit(solution)/shard_map/ppermute | solution.py:396
  30.4 1.6 %collective-permute-start.14 = (bf16[2,208,256]{2,1,0:T(8,128)(2,1)S(1)}, bf16[2,208,256]{2,1,0:T(8,128)(2,1)S(1)}, u32[]{:S(2)}, u32[]{:S(2)}) collective-permute-start(bf16[2,208,256]{2,1,0:T(8,128)(2,1)S(1)} %get-tuple-element.63), channel_id=1, source_target_pairs={{0,1},{1,0},{2,3},{3,2},{4,5},{5,4},{6,7},{7,6},{8,9},{9,8},{10,11... | collective-permute-start | bytes 638984 | tf_op jit(solution)/shard_map/ppermute | solution.py:396
  30.6 1.7 %collective-permute-start.15 = (bf16[2,208,256]{2,1,0:T(8,128)(2,1)S(1)}, bf16[2,208,256]{2,1,0:T(8,128)(2,1)S(1)}, u32[]{:S(2)}, u32[]{:S(2)}) collective-permute-start(bf16[2,208,256]{2,1,0:T(8,128)(2,1)S(1)} %get-tuple-element.64), channel_id=1, source_target_pairs={{0,1},{1,0},{2,3},{3,2},{4,5},{5,4},{6,7},{7,6},{8,9},{9,8},{10,11... | collective-permute-start | bytes 638984 | tf_op jit(solution)/shard_map/ppermute | solution.py:396
  33.0 11.9 %collective-permute-start.16 = (bf16[4,208,128]{2,1,0:T(8,128)(2,1)S(1)}, bf16[4,208,128]{2,1,0:T(8,128)(2,1)S(1)}, u32[]{:S(2)}, u32[]{:S(2)}) collective-permute-start(bf16[4,208,128]{2,1,0:T(8,128)(2,1)S(1)} %get-tuple-element.66), channel_id=1, source_target_pairs={{0,18},{1,19},{2,16},{3,17},{4,22},{5,23},{6,20},{7,21},{8,26},{9,... | collective-permute-start | bytes 638984 | tf_op jit(solution)/shard_map/ppermute | solution.py:400
  34.5 13.6 %collective-permute-start.17 = (bf16[4,208,128]{2,1,0:T(8,128)(2,1)S(1)}, bf16[4,208,128]{2,1,0:T(8,128)(2,1)S(1)}, u32[]{:S(2)}, u32[]{:S(2)}) collective-permute-start(bf16[4,208,128]{2,1,0:T(8,128)(2,1)S(1)} %get-tuple-element.67), channel_id=1, source_target_pairs={{0,16},{16,0},{1,17},{17,1},{2,18},{18,2},{3,19},{19,3},{4,20},{20... | collective-permute-start | bytes 638984 | tf_op jit(solution)/shard_map/ppermute | solution.py:398
  35.9 12.3 %collective-permute-start.18 = (bf16[4,208,128]{2,1,0:T(8,128)(2,1)S(1)}, bf16[4,208,128]{2,1,0:T(8,128)(2,1)S(1)}, u32[]{:S(2)}, u32[]{:S(2)}) collective-permute-start(bf16[4,208,128]{2,1,0:T(8,128)(2,1)S(1)} %get-tuple-element.68), channel_id=1, source_target_pairs={{0,2},{1,3},{2,0},{3,1},{4,6},{5,7},{6,4},{7,5},{8,10},{9,11},{10,... | collective-permute-start | bytes 638984 | tf_op jit(solution)/shard_map/ppermute | solution.py:396
  39.4 23.2 %copy-start.3 = (bf16[2,1024,256]{2,1,0:T(8,128)(2,1)S(1)}, bf16[2,1024,256]{2,1,0:T(8,128)(2,1)}, u32[]{:S(2)}) copy-start(bf16[2,1024,256]{2,1,0:T(8,128)(2,1)} %refs_1_.1) | copy-start | bytes 3145732
  40.1 8.1 %collective-permute-start.20 = (bf16[4,208,128]{2,1,0:T(8,128)(2,1)S(1)}, bf16[4,208,128]{2,1,0:T(8,128)(2,1)S(1)}, u32[]{:S(2)}, u32[]{:S(2)}) collective-permute-start(bf16[4,208,128]{2,1,0:T(8,128)(2,1)S(1)} %get-tuple-element.71), channel_id=1, source_target_pairs={{0,4},{1,5},{2,6},{3,7},{4,0},{5,1},{6,2},{7,3},{8,12},{9,13},{10,... | collective-permute-start | bytes 638984 | tf_op jit(solution)/shard_map/ppermute | solution.py:396
  48.9 5.9 %collective-permute-start.21 = (bf16[2,208,128]{2,1,0:T(8,128)(2,1)S(1)}, bf16[2,208,128]{2,1,0:T(8,128)(2,1)S(1)}, u32[]{:S(2)}, u32[]{:S(2)}) collective-permute-start(bf16[2,208,128]{2,1,0:T(8,128)(2,1)S(1)} %get-tuple-element.73), channel_id=1, source_target_pairs={{0,2},{1,3},{2,0},{3,1},{4,6},{5,7},{6,4},{7,5},{8,10},{9,11},{10,... | collective-permute-start | bytes 319496 | tf_op jit(solution)/shard_map/ppermute | solution.py:396
  50.3 6.0 %collective-permute-start.23 = (bf16[1,208,128]{2,1,0:T(8,128)(2,1)S(1)}, bf16[1,208,128]{2,1,0:T(8,128)(2,1)S(1)}, u32[]{:S(2)}, u32[]{:S(2)}) collective-permute-start(bf16[1,208,128]{2,1,0:T(8,128)(2,1)S(1)} %get-tuple-element.77), channel_id=1, source_target_pairs={{0,12},{1,13},{2,14},{3,15},{4,8},{5,9},{6,10},{7,11},{8,4},{9,5},... | collective-permute-start | bytes 159752 | tf_op jit(solution)/shard_map/ppermute | solution.py:396
  52.7 6.0 %collective-permute-start.24 = (bf16[1,208,128]{2,1,0:T(8,128)(2,1)S(1)}, bf16[1,208,128]{2,1,0:T(8,128)(2,1)S(1)}, u32[]{:S(2)}, u32[]{:S(2)}) collective-permute-start(bf16[1,208,128]{2,1,0:T(8,128)(2,1)S(1)} %get-tuple-element.78), channel_id=1, source_target_pairs={{0,8},{1,9},{2,10},{3,11},{4,12},{5,13},{6,14},{7,15},{8,0},{9,1},... | collective-permute-start | bytes 159752 | tf_op jit(solution)/shard_map/ppermute | solution.py:396
  52.7 6.0 %collective-permute-start.25 = (bf16[1,208,128]{2,1,0:T(8,128)(2,1)S(1)}, bf16[1,208,128]{2,1,0:T(8,128)(2,1)S(1)}, u32[]{:S(2)}, u32[]{:S(2)}) collective-permute-start(bf16[1,208,128]{2,1,0:T(8,128)(2,1)S(1)} %get-tuple-element.79), channel_id=1, source_target_pairs={{0,4},{1,5},{2,6},{3,7},{4,0},{5,1},{6,2},{7,3},{8,12},{9,13},{10,... | collective-permute-start | bytes 159752 | tf_op jit(solution)/shard_map/ppermute | solution.py:396
  55.3 5.2 %collective-permute-start.22 = (bf16[1,208,128]{2,1,0:T(8,128)(2,1)S(1)}, bf16[1,208,128]{2,1,0:T(8,128)(2,1)S(1)}, u32[]{:S(2)}, u32[]{:S(2)}) collective-permute-start(bf16[1,208,128]{2,1,0:T(8,128)(2,1)S(1)} %get-tuple-element.76), channel_id=1, source_target_pairs={{0,8},{1,9},{2,10},{3,11},{4,12},{5,13},{6,14},{7,15},{8,0},{9,1},... | collective-permute-start | bytes 159752 | tf_op jit(solution)/shard_map/ppermute | solution.py:396
  61.1 4.2 %collective-permute-start.26 = (bf16[208,128]{1,0:T(8,128)(2,1)S(1)}, bf16[208,128]{1,0:T(8,128)(2,1)S(1)}, u32[]{:S(2)}, u32[]{:S(2)}) collective-permute-start(bf16[208,128]{1,0:T(8,128)(2,1)S(1)} %get-tuple-element.81), channel_id=1, source_target_pairs={{0,16},{16,0},{1,17},{17,1},{2,18},{18,2},{3,19},{19,3},{4,20},{20... | collective-permute-start | bytes 159752 | tf_op jit(solution)/shard_map/ppermute | solution.py:398

commit v14 on v13

--- a/solution.py
+++ b/solution.py
@@ -46,7 +46,15 @@
     return lax.dot_general(left, right, (((1,), (1,)), ((), ())), preferred_element_type=F32)
 
 
-def centre_kernel(cot, pooled, wide):
+def facing(group):
+    above = [group[0], 0.75 * (group[0] + group[1]) + 0.25 * group[2]]
+    below = [0.25 * group[3] + 0.75 * (group[4] + group[5]), group[5]]
+    return above, below
+
+
+def centre_kernel(flags, cot, pooled, *refs):
+    outs, wide = refs[:-1], refs[-1]
+    row_odd = flags[ROW_ODD] == 1
     images, height2, width2, channels = cot.shape
     width = width2 // 2
     wide[...] = jnp.zeros_like(wide)
@@ -62,6 +70,12 @@
             for h in range(channels // 128):
                 taps = [wide[h, r, pl.ds(LEFT - 1 + n, width, stride=2), :] for n in range(4)]
                 pooled[i, r, :width, h * 128 : (h + 1) * 128] = 0.75 * (taps[1] + taps[2]) + 0.25 * (taps[0] + taps[3])
+        above, below = facing([pooled[i, r, :width, :] for r in (0, 1, 2, height2 - 3, height2 - 2, height2 - 1)])
+        for second, out in enumerate(outs):
+            for n in range(2):
+                odd, even = (below[n], above[n]) if second else (above[n], below[n])
+                at = pl.multiple_of((2 * i + n) * width, width)
+                out[pl.ds(at, width), :] = jnp.where(row_odd, odd, even).astype(BF16)
         return carry
 
     lax.fori_loop(0, images, per_image, 0)
@@ -97,24 +111,6 @@
     pooled[LEFT + width : LEFT + width + 1, :] = beside[1:]
     for v in range(3):
         window[v, pl.ds(at, width), :] = pooled[pl.ds(LEFT + 1 - v, width), :].astype(BF16)
-
-
-def facing(group):
-    above = [group[0], 0.75 * (group[0] + group[1]) + 0.25 * group[2]]
-    below = [0.25 * group[3] + 0.75 * (group[4] + group[5]), group[5]]
-    return above, below
-
-
-def row_pack_kernel(flags, centre, *outs):
-    images, height2, width = centre.shape[0], centre.shape[1], centre.shape[2] - 8
-    row_odd = flags[ROW_ODD] == 1
-    for i in range(images):
-        above, below = facing([centre[i, r, :width, :] for r in (0, 1, 2, height2 - 3, height2 - 2, height2 - 1)])
-        for second, out in enumerate(outs):
-            for n in range(2):
-                odd, even = (below[n], above[n]) if second else (above[n], below[n])
-                at = (2 * i + n) * width
-                out[at : at + width, :] = jnp.where(row_odd, odd, even).astype(BF16)
 
 
 def corner_pack_kernel(has_second, flags, centre, col_a, col_b, *refs):
@@ -472,14 +468,12 @@
     around = paired(TILE_COLS, 1) + [(0, TILE_COLS - 1), (TILE_COLS - 1, 0)]
     col_b = swap(jnp.where(col % 2 == 1, high, low), None, around)
     col_a = swap(jnp.where(col % 2 == 1, low, high), None, paired(TILE_COLS, 0))
-    centre = vmem_call(
+    centre, *row_out = vmem_call(
         centre_kernel,
-        sds(images, height2, width + 8, channels, dtype=F32),
-        (cotangent,),
+        [sds(images, height2, width + 8, channels, dtype=F32)] + [sds(2 * line, channels)] * sides,
+        (flags, cotangent),
         scratch=(pltpu.VMEM((channels // 128, height2, LEFT + width2 + 8, 128), F32),),
-        scalars=0,
-    )
-    row_out = vmem_call(row_pack_kernel, [sds(2 * line, channels)] * sides, (flags, centre))
+    )
     came_rows = [swap(row_out[n], paired(rows, n), None) for n in range(sides)]
     *corner_out, cells, beside = vmem_call(
         functools.partial(corner_pack_kernel, has_second),

time: 66.7 us -> 66.8 us (level)
    pallas_call x16 -> x15, Pallas kernels: 16.6 us -> 16.6 us  [vmem_call(): pl.pallas_call(run, out_shape=out_shape, in_specs=specs, out_specs=jax.tr...]
  transfers between devices with their start and end apart: 27 -> 27, of which waited for: 14 -> 13; matrix products, arithmetic and copies ran while one was open for 0% -> 0% of each run, Pallas kernels for 19% -> 19%
where the time goes in v14:
time: 66.8 us; the launch traced here: 66.6 us
  starting transfers between devices  26.9 us (40%)
  waiting for transfers between devices  19.6 us (29%)
  Pallas kernels  16.6 us (25%)
  other arithmetic  1.34 us (2%)
  local copies, waits for them, and re-layouts  1.33 us (2%)
  between operations  0.85 us (1%)
    pallas_call x15, Pallas kernels, vmem_call(): pl.pallas_call(run, out_shape=out_shape, in_specs=specs, out_specs=jax.tr...  16.6 us
    ppermute x19, starting transfers between devices, xor_move(): return lax.ppermute(block, 'tile', [(t, t ^ apart) for t in range(tiles)])  14.1 us
    ppermute x19, waiting for transfers between devices, xor_move(): return lax.ppermute(block, 'tile', [(t, t ^ apart) for t in range(tiles)])  7.98 us
    ppermute x3, waiting for transfers between devices, xor_move(): return lax.ppermute(block, 'dp', [(0, 1), (1, 0)])  6.78 us
    ppermute x4, starting transfers between devices, swap(): return lax.ppermute(block, 'tile', tile_route(row_pairs, col_pairs, rows))  6.77 us
    ppermute x3, starting transfers between devices, xor_move(): return lax.ppermute(block, 'dp', [(0, 1), (1, 0)])  4.46 us
    ppermute x1, waiting for transfers between devices, xor_move(): return lax.ppermute(block, ('dp', 'tile'), route)  3.57 us
    ppermute x1, starting transfers between devices, xor_move(): return lax.ppermute(block, ('dp', 'tile'), route)  1.58 us
  transfers between devices with their start and end apart: 27, of which 13 were waited for; matrix products, arithmetic and copies ran while one was open for 0% of the time, Pallas kernels for 19%

profile of v14, /device:TPU:0, one launch (start us, length us, event | category | flops | bytes accessed | tf_op | source)
XLA Modules:
  0.0 66.6 jit_solution(13253935707538040568)
XLA Ops:
  0.7 1.3 %broadcast_select_fusion = (bf16[4,16,4,256]{3,2,1,0:T(4,128)(2,1)S(1)}, bf16[4,16,4,256]{3,2,1,0:T(4,128)(2,1)S(1)}) fusion(pred[]{:T(512)S(6)} %eq.27, bf16[4,16,32,256]{3,2,1,0:T(8,128)(2,1)} %refs_1_.2), kind=kLoop, calls=%fused_computation | loop fusion | flops 131072 | bytes 524289 | tf_op jit(solution)/shard_map/jit(_where)/select_n | solution.py:469
  2.0 3.1 %collective-permute-start.2 = (bf16[4,16,4,256]{3,2,1,0:T(4,128)(2,1)S(1)}, bf16[4,16,4,256]{3,2,1,0:T(4,128)(2,1)S(1)}, u32[]{:S(2)}, u32[]{:S(2)}) collective-permute-start(bf16[4,16,4,256]{3,2,1,0:T(4,128)(2,1)S(1)} %get-tuple-element.86), channel_id=1, source_target_pairs={{1,3},{3,1},{2,6},{6,2},{7,5},{5,7},{0,4},{4,0},{9,11},{11,9},{10,... | collective-permute-start | bytes 393224 | tf_op jit(solution)/shard_map/ppermute | solution.py:465
  5.1 0.1 stack.71.refs_0_
  5.2 0.0 copy-start.2
  5.2 1.2 %copy-done.2 = bf16[4,16,32,256]{3,2,1,0:T(8,128)(2,1)S(1)} copy-done((bf16[4,16,32,256]{3,2,1,0:T(8,128)(2,1)S(1)}, bf16[4,16,32,256]{3,2,1,0:T(8,128)(2,1)}, u32[]{:S(2)}) %copy-start.2) | copy-done | bytes 1048600
  6.4 1.0 %shard_map.68 = (f32[4,16,24,256]{3,2,1,0:T(8,128)S(1)}, bf16[128,256]{1,0:T(8,128)(2,1)S(1)}) custom-call(s32[13]{0:T(128)S(1)} %stack.71.refs_0_, bf16[4,16,32,256]{3,2,1,0:T(8,128)(2,1)S(1)} %copy-done.2), custom_call_target="tpu_custom_call" | custom-call | bytes 2687028 | tf_op jit(solution)/shard_map/pallas_call | solution.py:373
  7.5 2.7 %collective-permute-start = (bf16[128,256]{1,0:T(8,128)(2,1)S(1)}, bf16[128,256]{1,0:T(8,128)(2,1)S(1)}, u32[]{:S(2)}, u32[]{:S(2)}) collective-permute-start(bf16[128,256]{1,0:T(8,128)(2,1)S(1)} %get-tuple-element.44), channel_id=1, source_target_pairs={{0,8},{1,9},{3,11},{2,10},{6,14},{7,15},{5,13},{4,12},{8,0},{9,1},... | collective-permute-start | bytes 196616 | tf_op jit(solution)/shard_map/ppermute | solution.py:465
  10.1 0.0 collective-permute-done.2.refs_3_
  10.1 0.0 collective-permute-done.1.refs_2_
  10.1 0.8 %shard_map.69 = (bf16[32,256]{1,0:T(8,128)(2,1)S(1)}, f32[4,6,16,256]{3,2,1,0:T(8,128)S(1)}, f32[4,6,2,256]{3,2,1,0:T(2,128)S(1)}) custom-call(s32[13]{0:T(128)S(1)} %stack.71.refs_0_, f32[4,16,24,256]{3,2,1,0:T(8,128)S(1)} %get-tuple-element.45.refs_1_, bf16[4,16,4,256]{3,2,1,0:T(4,128)(2,1)S(1)} %collective-permute-done.1.refs_2_, ...), custom_call_target="tpu_custom_call" | custom-call | bytes 2293812 | tf_op jit(solution)/shard_map/pallas_call | solution.py:373
  10.9 1.0 %collective-permute-start.3 = (bf16[32,256]{1,0:T(8,128)(2,1)S(1)}, bf16[32,256]{1,0:T(8,128)(2,1)S(1)}, u32[]{:S(2)}, u32[]{:S(2)}) collective-permute-start(bf16[32,256]{1,0:T(8,128)(2,1)S(1)} %get-tuple-element.46.refs_5_), channel_id=1, source_target_pairs={{0,8},{1,9},{3,11},{2,10},{6,14},{7,15},{5,13},{4,12},{8,0},{9,1},... | collective-permute-start | bytes 49160 | tf_op jit(solution)/shard_map/ppermute | solution.py:465
  11.9 2.4 %shard_map.70 = (bf16[3,640,256]{2,1,0:T(8,128)(2,1)S(1)}, f32[2,512,256]{2,1,0:T(8,128)S(1)}) custom-call(s32[13]{0:T(128)S(1)} %stack.71.refs_0_, f32[4,16,24,256]{3,2,1,0:T(8,128)S(1)} %get-tuple-element.45.refs_1_, bf16[4,16,4,256]{3,2,1,0:T(4,128)(2,1)S(1)} %collective-permute-done.1.refs_2_, ...), custom_call_target="tpu_custom_call" | custom-call | flops 1207959552 | bytes 6225972 | tf_op jit(solution)/shard_map/pallas_call | solution.py:373
  14.3 0.0 collective-permute-done.refs_1_
  14.3 1.3 %collective-permute-done.3.refs_2_ = bf16[32,256]{1,0:T(8,128)(2,1)S(1)} collective-permute-done((bf16[32,256]{1,0:T(8,128)(2,1)S(1)}, bf16[32,256]{1,0:T(8,128)(2,1)S(1)}, u32[]{:S(2)}, u32[]{:S(2)}) %collective-permute-start.3) | collective-permute-done | bytes 16416 | tf_op jit(solution)/shard_map/ppermute | solution.py:465
  15.6 1.6 %shard_map.71 = (bf16[2,2,64,256]{3,2,1,0:T(8,128)(2,1)S(1)}, bf16[2,2,64,256]{3,2,1,0:T(8,128)(2,1)S(1)}, bf16[2,2,64,256]{3,2,1,0:T(8,128)(2,1)S(1)}, bf16[2,2...) custom-call(s32[13]{0:T(128)S(1)} %stack.71.refs_0_, ...), custom_call_target="tpu_custom_call", output_to_operand_aliasing={{4}: (5, {})} | custom-call | flops 301989888 | bytes 6422580 | tf_op jit(solution)/shard_map/pallas_call | solution.py:373
  17.2 1.6 %collective-permute-start.4 = (bf16[2,2,64,256]{3,2,1,0:T(8,128)(2,1)S(1)}, bf16[2,2,64,256]{3,2,1,0:T(8,128)(2,1)S(1)}, u32[]{:S(2)}, u32[]{:S(2)}) collective-permute-start(bf16[2,2,64,256]{3,2,1,0:T(8,128)(2,1)S(1)} %get-tuple-element.52), channel_id=1, source_target_pairs={{0,2},{1,3},{2,0},{3,1},{4,6},{5,7},{6,4},{7,5},{8,10},{9,11},{10,... | collective-permute-start | bytes 393224 | tf_op jit(solution)/shard_map/ppermute | solution.py:392
  18.9 0.4 collective-permute-start.5
  19.3 1.5 %collective-permute-start.6 = (bf16[2,2,64,256]{3,2,1,0:T(8,128)(2,1)S(1)}, bf16[2,2,64,256]{3,2,1,0:T(8,128)(2,1)S(1)}, u32[]{:S(2)}, u32[]{:S(2)}) collective-permute-start(bf16[2,2,64,256]{3,2,1,0:T(8,128)(2,1)S(1)} %get-tuple-element.54), channel_id=1, source_target_pairs={{0,6},{1,7},{2,4},{3,5},{4,2},{5,3},{6,0},{7,1},{8,14},{9,15},{10,... | collective-permute-start | bytes 393224 | tf_op jit(solution)/shard_map/ppermute | solution.py:392
  20.8 2.1 %shard_map.73 = (bf16[8,208,256]{2,1,0:T(8,128)(2,1)S(1)}, bf16[2,208,256]{2,1,0:T(8,128)(2,1)S(1)}, bf16[2,208,256]{2,1,0:T(8,128)(2,1)S(1)}, bf16[2,208,256]{2...) custom-call(s32[13]{0:T(128)S(1)} %stack.71.refs_0_, ...), custom_call_target="tpu_custom_call" | custom-call | flops 1207959552 | bytes 3866676 | tf_op jit(solution)/shard_map/pallas_call | solution.py:373
  22.9 0.0 copy-start.1
  22.9 0.1 collective-permute-start.8
  23.0 0.5 collective-permute-start.9
  23.5 0.0 collective-permute-done.4.refs_1_.refs_2_
  23.5 0.1 collective-permute-start.10
  23.5 0.9 %collective-permute-done.5.refs_2_.refs_3_ = bf16[2,2,64,256]{3,2,1,0:T(8,128)(2,1)S(1)} collective-permute-done((bf16[2,2,64,256]{3,2,1,0:T(8,128)(2,1)S(1)}, bf16[2,2,64,256]{3,2,1,0:T(8,128)(2,1)S(1)}, u32[]{:S(2)}, u32[]{:S(2)}) %collective-permute-start.5) | collective-permute-done | bytes 131104 | tf_op jit(solution)/shard_map/ppermute | solution.py:392
  24.5 0.0 collective-permute-start.11
  24.5 1.5 %collective-permute-done.6.refs_3_.refs_4_ = bf16[2,2,64,256]{3,2,1,0:T(8,128)(2,1)S(1)} collective-permute-done((bf16[2,2,64,256]{3,2,1,0:T(8,128)(2,1)S(1)}, bf16[2,2,64,256]{3,2,1,0:T(8,128)(2,1)S(1)}, u32[]{:S(2)}, u32[]{:S(2)}) %collective-permute-start.6) | collective-permute-done | bytes 131104 | tf_op jit(solution)/shard_map/ppermute | solution.py:392
  26.0 0.1 collective-permute-start.7
  26.1 0.0 collective-permute-done.8.refs_2_
  26.1 0.0 collective-permute-done.10.refs_4_
  26.1 0.0 collective-permute-done.11.refs_5_
  26.1 0.7 %shard_map.74 = (f32[8,208,128]{2,1,0:T(8,128)S(1)}, bf16[8,208,128]{2,1,0:T(8,128)(2,1)S(1)}) custom-call(s32[13]{0:T(128)S(1)} %stack.71.refs_0_, bf16[8,208,256]{2,1,0:T(8,128)(2,1)S(1)} %get-tuple-element.57.refs_1_, bf16[2,208,256]{2,1,0:T(8,128)(2,1)S(1)} %collective-permute-done.8.refs_2_, bf16[2,208,256]{2,1,0:T(8,128)(2,1)S(1)} %collective-permute-done.9.refs_3_, ...), custom_call_target="tpu_custom_call" | custom-call | bytes 2981940 | tf_op jit(solution)/shard_map/pallas_call | solution.py:373
  26.8 1.6 %collective-permute-start.19 = (bf16[8,208,128]{2,1,0:T(8,128)(2,1)S(1)}, bf16[8,208,128]{2,1,0:T(8,128)(2,1)S(1)}, u32[]{:S(2)}, u32[]{:S(2)}) collective-permute-start(bf16[8,208,128]{2,1,0:T(8,128)(2,1)S(1)} %get-tuple-element.73), channel_id=1, source_target_pairs={{0,16},{16,0},{1,17},{17,1},{2,18},{18,2},{3,19},{19,3},{4,20},{20... | collective-permute-start | bytes 1277960 | tf_op jit(solution)/shard_map/ppermute | solution.py:394
  28.4 1.5 %shard_map.75 = (bf16[8,208,256]{2,1,0:T(8,128)(2,1)S(1)}, bf16[2,208,256]{2,1,0:T(8,128)(2,1)S(1)}, bf16[2,208,256]{2,1,0:T(8,128)(2,1)S(1)}, bf16[2,208,256]{2...) custom-call(s32[13]{0:T(128)S(1)} %stack.71.refs_0_, ...), custom_call_target="tpu_custom_call" | custom-call | flops 536870912 | bytes 5767220 | tf_op jit(solution)/shard_map/pallas_call | solution.py:373
  29.9 0.3 collective-permute-start.12
  30.1 0.3 collective-permute-start.13
  30.5 0.2 collective-permute-start.14
  30.7 0.3 collective-permute-start.15
  31.0 0.4 collective-permute-done.12.refs_2_
  31.4 0.3 collective-permute-done.13.refs_3_
  31.7 0.3 collective-permute-done.14.refs_4_
  32.0 0.3 collective-permute-done.15.refs_5_
  32.3 0.7 %shard_map.76 = (f32[4,208,128]{2,1,0:T(8,128)S(1)}, bf16[4,208,128]{2,1,0:T(8,128)(2,1)S(1)}, bf16[4,208,128]{2,1,0:T(8,128)(2,1)S(1)}, bf16[4,208,128]{2,1,0:T(8,128)(2,1)S(1)}) custom-call(s32[13]{0:T(128)S(1)} %stack.71.refs_0_, bf16[8,208,256]{2,1,0:T(8,128)(2,1)S(1)} %get-tuple-element.64.refs_1_, ...), custom_call_target="tpu_custom_call" | custom-call | bytes 2768948 | tf_op jit(solution)/shard_map/pallas_call | solution.py:373
  33.1 1.6 %collective-permute-start.16 = (bf16[4,208,128]{2,1,0:T(8,128)(2,1)S(1)}, bf16[4,208,128]{2,1,0:T(8,128)(2,1)S(1)}, u32[]{:S(2)}, u32[]{:S(2)}) collective-permute-start(bf16[4,208,128]{2,1,0:T(8,128)(2,1)S(1)} %get-tuple-element.70), channel_id=1, source_target_pairs={{0,18},{1,19},{2,16},{3,17},{4,22},{5,23},{6,20},{7,21},{8,26},{9,... | collective-permute-start | bytes 638984 | tf_op jit(solution)/shard_map/ppermute | solution.py:396
  34.6 1.3 %collective-permute-start.17 = (bf16[4,208,128]{2,1,0:T(8,128)(2,1)S(1)}, bf16[4,208,128]{2,1,0:T(8,128)(2,1)S(1)}, u32[]{:S(2)}, u32[]{:S(2)}) collective-permute-start(bf16[4,208,128]{2,1,0:T(8,128)(2,1)S(1)} %get-tuple-element.71), channel_id=1, source_target_pairs={{0,16},{16,0},{1,17},{17,1},{2,18},{18,2},{3,19},{19,3},{4,20},{20... | collective-permute-start | bytes 638984 | tf_op jit(solution)/shard_map/ppermute | solution.py:394
  36.0 0.6 collective-permute-start.18
  36.6 2.9 %collective-permute-done.19.refs_2_ = bf16[8,208,128]{2,1,0:T(8,128)(2,1)S(1)} collective-permute-done((bf16[8,208,128]{2,1,0:T(8,128)(2,1)S(1)}, bf16[8,208,128]{2,1,0:T(8,128)(2,1)S(1)}, u32[]{:S(2)}, u32[]{:S(2)}) %collective-permute-start.19) | collective-permute-done | bytes 426016 | tf_op jit(solution)/shard_map/ppermute | solution.py:394
  39.5 0.6 shard_map.77
  40.2 1.2 %collective-permute-start.20 = (bf16[4,208,128]{2,1,0:T(8,128)(2,1)S(1)}, bf16[4,208,128]{2,1,0:T(8,128)(2,1)S(1)}, u32[]{:S(2)}, u32[]{:S(2)}) collective-permute-start(bf16[4,208,128]{2,1,0:T(8,128)(2,1)S(1)} %get-tuple-element.75), channel_id=1, source_target_pairs={{0,4},{1,5},{2,6},{3,7},{4,0},{5,1},{6,2},{7,3},{8,12},{9,13},{10,... | collective-permute-start | bytes 638984 | tf_op jit(solution)/shard_map/ppermute | solution.py:392
  41.4 3.6 %collective-permute-done.16.refs_2_ = bf16[4,208,128]{2,1,0:T(8,128)(2,1)S(1)} collective-permute-done((bf16[4,208,128]{2,1,0:T(8,128)(2,1)S(1)}, bf16[4,208,128]{2,1,0:T(8,128)(2,1)S(1)}, u32[]{:S(2)}, u32[]{:S(2)}) %collective-permute-start.16) | collective-permute-done | bytes 213024 | tf_op jit(solution)/shard_map/ppermute | solution.py:396
  45.0 3.3 %collective-permute-done.17.refs_3_ = bf16[4,208,128]{2,1,0:T(8,128)(2,1)S(1)} collective-permute-done((bf16[4,208,128]{2,1,0:T(8,128)(2,1)S(1)}, bf16[4,208,128]{2,1,0:T(8,128)(2,1)S(1)}, u32[]{:S(2)}, u32[]{:S(2)}) %collective-permute-start.17) | collective-permute-done | bytes 213024 | tf_op jit(solution)/shard_map/ppermute | solution.py:394
  48.3 0.7 %shard_map.78 = (f32[1,208,128]{2,1,0:T(8,128)S(1)}, bf16[1,208,128]{2,1,0:T(8,128)(2,1)S(1)}, bf16[1,208,128]{2,1,0:T(8,128)(2,1)S(1)}, bf16[1,208,128]{2,1,0:T...) custom-call(s32[13]{0:T(128)S(1)} %stack.71.refs_0_, ...), custom_call_target="tpu_custom_call" | custom-call | bytes 2289716 | tf_op jit(solution)/shard_map/pallas_call | solution.py:373
  49.0 1.5 %collective-permute-start.21 = (bf16[2,208,128]{2,1,0:T(8,128)(2,1)S(1)}, bf16[2,208,128]{2,1,0:T(8,128)(2,1)S(1)}, u32[]{:S(2)}, u32[]{:S(2)}) collective-permute-start(bf16[2,208,128]{2,1,0:T(8,128)(2,1)S(1)} %get-tuple-element.77), channel_id=1, source_target_pairs={{0,2},{1,3},{2,0},{3,1},{4,6},{5,7},{6,4},{7,5},{8,10},{9,11},{10,... | collective-permute-start | bytes 319496 | tf_op jit(solution)/shard_map/ppermute | solution.py:392
  50.4 2.4 %collective-permute-start.23 = (bf16[1,208,128]{2,1,0:T(8,128)(2,1)S(1)}, bf16[1,208,128]{2,1,0:T(8,128)(2,1)S(1)}, u32[]{:S(2)}, u32[]{:S(2)}) collective-permute-start(bf16[1,208,128]{2,1,0:T(8,128)(2,1)S(1)} %get-tuple-element.81), channel_id=1, source_target_pairs={{0,12},{1,13},{2,14},{3,15},{4,8},{5,9},{6,10},{7,11},{8,4},{9,5},... | collective-permute-start | bytes 159752 | tf_op jit(solution)/shard_map/ppermute | solution.py:392
  52.8 2.0 %collective-permute-start.25 = (bf16[1,208,128]{2,1,0:T(8,128)(2,1)S(1)}, bf16[1,208,128]{2,1,0:T(8,128)(2,1)S(1)}, u32[]{:S(2)}, u32[]{:S(2)}) collective-permute-start(bf16[1,208,128]{2,1,0:T(8,128)(2,1)S(1)} %get-tuple-element.83), channel_id=1, source_target_pairs={{0,4},{1,5},{2,6},{3,7},{4,0},{5,1},{6,2},{7,3},{8,12},{9,13},{10,... | collective-permute-start | bytes 159752 | tf_op jit(solution)/shard_map/ppermute | solution.py:392
  54.8 0.6 shard_map.79
  55.4 1.0 %collective-permute-start.22 = (bf16[1,208,128]{2,1,0:T(8,128)(2,1)S(1)}, bf16[1,208,128]{2,1,0:T(8,128)(2,1)S(1)}, u32[]{:S(2)}, u32[]{:S(2)}) collective-permute-start(bf16[1,208,128]{2,1,0:T(8,128)(2,1)S(1)} %get-tuple-element.80), channel_id=1, source_target_pairs={{0,8},{1,9},{2,10},{3,11},{4,12},{5,13},{6,14},{7,15},{8,0},{9,1},... | collective-permute-start | bytes 159752 | tf_op jit(solution)/shard_map/ppermute | solution.py:392
  56.4 2.4 %collective-permute-done.24.refs_5_ = bf16[1,208,128]{2,1,0:T(8,128)(2,1)S(1)} collective-permute-done((bf16[1,208,128]{2,1,0:T(8,128)(2,1)S(1)}, bf16[1,208,128]{2,1,0:T(8,128)(2,1)S(1)}, u32[]{:S(2)}, u32[]{:S(2)}) %collective-permute-start.24) | collective-permute-done | bytes 53280 | tf_op jit(solution)/shard_map/ppermute | solution.py:392
  58.9 1.7 %collective-permute-done.22.refs_2_ = bf16[1,208,128]{2,1,0:T(8,128)(2,1)S(1)} collective-permute-done((bf16[1,208,128]{2,1,0:T(8,128)(2,1)S(1)}, bf16[1,208,128]{2,1,0:T(8,128)(2,1)S(1)}, u32[]{:S(2)}, u32[]{:S(2)}) %collective-permute-start.22) | collective-permute-done | bytes 53280 | tf_op jit(solution)/shard_map/ppermute | solution.py:392
  60.6 0.6 shard_map.81
  61.2 1.6 %collective-permute-start.26 = (bf16[208,128]{1,0:T(8,128)(2,1)S(1)}, bf16[208,128]{1,0:T(8,128)(2,1)S(1)}, u32[]{:S(2)}, u32[]{:S(2)}) collective-permute-start(bf16[208,128]{1,0:T(8,128)(2,1)S(1)} %get-tuple-element.85), channel_id=1, source_target_pairs={{0,16},{16,0},{1,17},{17,1},{2,18},{18,2},{3,19},{19,3},{4,20},{20... | collective-permute-start | bytes 159752 | tf_op jit(solution)/shard_map/ppermute | solution.py:394
  62.8 2.1 %shard_map.80 = bf16[4,2,128,1024]{3,2,1,0:T(8,128)(2,1)} custom-call(bf16[2,512,256]{2,1,0:T(8,128)(2,1)S(1)} %get-tuple-element.63.refs_6_.refs_0_, bf16[2,1024,256]{2,1,0:T(8,128)(2,1)S(1)} %copy-done.3, f32[1,208,128]{2,1,0:T(8,128)S(1)} %get-tuple-element.79.refs_2_.refs_1_), custom_call_target="tpu_custom_call" | custom-call | flops 536870912 | bytes 3670016 | tf_op jit(solution)/shard_map/pallas_call | solution.py:373
  64.8 0.6 collective-permute-done.26.refs_2_
  65.4 1.2 %shard_map.82 = f32[208,256]{1,0:T(8,128)} custom-call(s32[13]{0:T(128)S(1)} %stack.71.refs_0_, f32[208,128]{1,0:T(8,128)S(1)} %get-tuple-element.84.refs_1_, bf16[208,128]{1,0:T(8,128)(2,1)S(1)} %collective-permute-done.26.refs_2_), custom_call_target="tpu_custom_call" | custom-call | bytes 372788 | tf_op jit(solution)/shard_map/pallas_call | solution.py:373
  (17 shorter events, 0.1 us)
Async XLA Ops:
  0.6 11.3 %copy-start = (bf16[2,3,3,256,256]{4,3,2,1,0:T(8,128)(2,1)S(1)}, bf16[2,3,3,256,256]{4,3,2,1,0:T(8,128)(2,1)}, u32[]{:S(2)}) copy-start(bf16[2,3,3,256,256]{4,3,2,1,0:T(8,128)(2,1)} %refs_7_.1) | copy-start | bytes 7077892
  2.0 8.1 %collective-permute-start.2 = (bf16[4,16,4,256]{3,2,1,0:T(4,128)(2,1)S(1)}, bf16[4,16,4,256]{3,2,1,0:T(4,128)(2,1)S(1)}, u32[]{:S(2)}, u32[]{:S(2)}) collective-permute-start(bf16[4,16,4,256]{3,2,1,0:T(4,128)(2,1)S(1)} %get-tuple-element.86), channel_id=1, source_target_pairs={{1,3},{3,1},{2,6},{6,2},{7,5},{5,7},{0,4},{4,0},{9,11},{11,9},{10,... | collective-permute-start | bytes 393224 | tf_op jit(solution)/shard_map/ppermute | solution.py:465
  5.1 5.0 %collective-permute-start.1 = (bf16[4,16,4,256]{3,2,1,0:T(4,128)(2,1)S(1)}, bf16[4,16,4,256]{3,2,1,0:T(4,128)(2,1)S(1)}, u32[]{:S(2)}, u32[]{:S(2)}) collective-permute-start(bf16[4,16,4,256]{3,2,1,0:T(4,128)(2,1)S(1)} %get-tuple-element.87), channel_id=1, source_target_pairs={{0,1},{1,0},{3,2},{2,3},{6,7},{7,6},{5,4},{4,5},{8,9},{9,8},{11,10... | collective-permute-start | bytes 393224 | tf_op jit(solution)/shard_map/ppermute | solution.py:465
  5.2 1.2 %copy-start.2 = (bf16[4,16,32,256]{3,2,1,0:T(8,128)(2,1)S(1)}, bf16[4,16,32,256]{3,2,1,0:T(8,128)(2,1)}, u32[]{:S(2)}) copy-start(bf16[4,16,32,256]{3,2,1,0:T(8,128)(2,1)} %refs_1_.2) | copy-start | bytes 3145732
  7.5 6.9 %collective-permute-start = (bf16[128,256]{1,0:T(8,128)(2,1)S(1)}, bf16[128,256]{1,0:T(8,128)(2,1)S(1)}, u32[]{:S(2)}, u32[]{:S(2)}) collective-permute-start(bf16[128,256]{1,0:T(8,128)(2,1)S(1)} %get-tuple-element.44), channel_id=1, source_target_pairs={{0,8},{1,9},{3,11},{2,10},{6,14},{7,15},{5,13},{4,12},{8,0},{9,1},... | collective-permute-start | bytes 196616 | tf_op jit(solution)/shard_map/ppermute | solution.py:465
  10.9 4.7 %collective-permute-start.3 = (bf16[32,256]{1,0:T(8,128)(2,1)S(1)}, bf16[32,256]{1,0:T(8,128)(2,1)S(1)}, u32[]{:S(2)}, u32[]{:S(2)}) collective-permute-start(bf16[32,256]{1,0:T(8,128)(2,1)S(1)} %get-tuple-element.46.refs_5_), channel_id=1, source_target_pairs={{0,8},{1,9},{3,11},{2,10},{6,14},{7,15},{5,13},{4,12},{8,0},{9,1},... | collective-permute-start | bytes 49160 | tf_op jit(solution)/shard_map/ppermute | solution.py:465
  15.6 5.2 %copy-start.4 = (bf16[4,2,8,16,256]{4,3,2,1,0:T(8,128)(2,1)S(1)}, bf16[4,2,8,16,256]{4,3,2,1,0:T(8,128)(2,1)}, u32[]{:S(2)}) copy-start(bf16[4,2,8,16,256]{4,3,2,1,0:T(8,128)(2,1)} %refs_2_.1) | copy-start | bytes 1572868
  17.2 6.2 %collective-permute-start.4 = (bf16[2,2,64,256]{3,2,1,0:T(8,128)(2,1)S(1)}, bf16[2,2,64,256]{3,2,1,0:T(8,128)(2,1)S(1)}, u32[]{:S(2)}, u32[]{:S(2)}) collective-permute-start(bf16[2,2,64,256]{3,2,1,0:T(8,128)(2,1)S(1)} %get-tuple-element.52), channel_id=1, source_target_pairs={{0,2},{1,3},{2,0},{3,1},{4,6},{5,7},{6,4},{7,5},{8,10},{9,11},{10,... | collective-permute-start | bytes 393224 | tf_op jit(solution)/shard_map/ppermute | solution.py:392
  18.9 5.6 %collective-permute-start.5 = (bf16[2,2,64,256]{3,2,1,0:T(8,128)(2,1)S(1)}, bf16[2,2,64,256]{3,2,1,0:T(8,128)(2,1)S(1)}, u32[]{:S(2)}, u32[]{:S(2)}) collective-permute-start(bf16[2,2,64,256]{3,2,1,0:T(8,128)(2,1)S(1)} %get-tuple-element.53), channel_id=1, source_target_pairs={{0,4},{1,5},{2,6},{3,7},{4,0},{5,1},{6,2},{7,3},{8,12},{9,13},{10,... | collective-permute-start | bytes 393224 | tf_op jit(solution)/shard_map/ppermute | solution.py:392
  19.3 6.7 %collective-permute-start.6 = (bf16[2,2,64,256]{3,2,1,0:T(8,128)(2,1)S(1)}, bf16[2,2,64,256]{3,2,1,0:T(8,128)(2,1)S(1)}, u32[]{:S(2)}, u32[]{:S(2)}) collective-permute-start(bf16[2,2,64,256]{3,2,1,0:T(8,128)(2,1)S(1)} %get-tuple-element.54), channel_id=1, source_target_pairs={{0,6},{1,7},{2,4},{3,5},{4,2},{5,3},{6,0},{7,1},{8,14},{9,15},{10,... | collective-permute-start | bytes 393224 | tf_op jit(solution)/shard_map/ppermute | solution.py:392
  22.9 5.5 %copy-start.1 = (bf16[4,2,128,1024]{3,2,1,0:T(8,128)(2,1)S(1)}, bf16[4,2,128,1024]{3,2,1,0:T(8,128)(2,1)}, u32[]{:S(2)}) copy-start(bf16[4,2,128,1024]{3,2,1,0:T(8,128)(2,1)} %refs_6_.1) | copy-start | bytes 6291460
  22.9 3.2 %collective-permute-start.8 = (bf16[2,208,256]{2,1,0:T(8,128)(2,1)S(1)}, bf16[2,208,256]{2,1,0:T(8,128)(2,1)S(1)}, u32[]{:S(2)}, u32[]{:S(2)}) collective-permute-start(bf16[2,208,256]{2,1,0:T(8,128)(2,1)S(1)} %get-tuple-element.58), channel_id=1, source_target_pairs={{0,1},{1,0},{2,3},{3,2},{4,5},{5,4},{6,7},{7,6},{8,9},{9,8},{10,11... | collective-permute-start | bytes 638984 | tf_op jit(solution)/shard_map/ppermute | solution.py:392
  23.0 3.1 %collective-permute-start.9 = (bf16[2,208,256]{2,1,0:T(8,128)(2,1)S(1)}, bf16[2,208,256]{2,1,0:T(8,128)(2,1)S(1)}, u32[]{:S(2)}, u32[]{:S(2)}) collective-permute-start(bf16[2,208,256]{2,1,0:T(8,128)(2,1)S(1)} %get-tuple-element.59), channel_id=1, source_target_pairs={{0,1},{1,0},{2,3},{3,2},{4,5},{5,4},{6,7},{7,6},{8,9},{9,8},{10,11... | collective-permute-start | bytes 638984 | tf_op jit(solution)/shard_map/ppermute | solution.py:392
  23.5 2.6 %collective-permute-start.10 = (bf16[2,208,256]{2,1,0:T(8,128)(2,1)S(1)}, bf16[2,208,256]{2,1,0:T(8,128)(2,1)S(1)}, u32[]{:S(2)}, u32[]{:S(2)}) collective-permute-start(bf16[2,208,256]{2,1,0:T(8,128)(2,1)S(1)} %get-tuple-element.60), channel_id=1, source_target_pairs={{0,1},{1,0},{2,3},{3,2},{4,5},{5,4},{6,7},{7,6},{8,9},{9,8},{10,11... | collective-permute-start | bytes 638984 | tf_op jit(solution)/shard_map/ppermute | solution.py:392
  24.5 1.6 %collective-permute-start.11 = (bf16[2,208,256]{2,1,0:T(8,128)(2,1)S(1)}, bf16[2,208,256]{2,1,0:T(8,128)(2,1)S(1)}, u32[]{:S(2)}, u32[]{:S(2)}) collective-permute-start(bf16[2,208,256]{2,1,0:T(8,128)(2,1)S(1)} %get-tuple-element.61), channel_id=1, source_target_pairs={{0,1},{1,0},{2,3},{3,2},{4,5},{5,4},{6,7},{7,6},{8,9},{9,8},{10,11... | collective-permute-start | bytes 638984 | tf_op jit(solution)/shard_map/ppermute | solution.py:392
  26.0 2.4 %collective-permute-start.7 = (bf16[4,2,64,256]{3,2,1,0:T(8,128)(2,1)S(1)}, bf16[4,2,64,256]{3,2,1,0:T(8,128)(2,1)S(1)}, u32[]{:S(2)}, u32[]{:S(2)}) collective-permute-start(bf16[4,2,64,256]{3,2,1,0:T(8,128)(2,1)S(1)} %shard_map.72), channel_id=1, source_target_pairs={{0,1},{1,0},{2,3},{3,2},{4,5},{5,4},{6,7},{7,6},{8,9},{9,8},{10,11... | collective-permute-start | bytes 786440 | tf_op jit(solution)/shard_map/ppermute | solution.py:392
  26.8 12.7 %collective-permute-start.19 = (bf16[8,208,128]{2,1,0:T(8,128)(2,1)S(1)}, bf16[8,208,128]{2,1,0:T(8,128)(2,1)S(1)}, u32[]{:S(2)}, u32[]{:S(2)}) collective-permute-start(bf16[8,208,128]{2,1,0:T(8,128)(2,1)S(1)} %get-tuple-element.73), channel_id=1, source_target_pairs={{0,16},{16,0},{1,17},{17,1},{2,18},{18,2},{3,19},{19,3},{4,20},{20... | collective-permute-start | bytes 1277960 | tf_op jit(solution)/shard_map/ppermute | solution.py:394
  29.9 1.5 %collective-permute-start.12 = (bf16[2,208,256]{2,1,0:T(8,128)(2,1)S(1)}, bf16[2,208,256]{2,1,0:T(8,128)(2,1)S(1)}, u32[]{:S(2)}, u32[]{:S(2)}) collective-permute-start(bf16[2,208,256]{2,1,0:T(8,128)(2,1)S(1)} %get-tuple-element.65), channel_id=1, source_target_pairs={{0,1},{1,0},{2,3},{3,2},{4,5},{5,4},{6,7},{7,6},{8,9},{9,8},{10,11... | collective-permute-start | bytes 638984 | tf_op jit(solution)/shard_map/ppermute | solution.py:392
  30.1 1.6 %collective-permute-start.13 = (bf16[2,208,256]{2,1,0:T(8,128)(2,1)S(1)}, bf16[2,208,256]{2,1,0:T(8,128)(2,1)S(1)}, u32[]{:S(2)}, u32[]{:S(2)}) collective-permute-start(bf16[2,208,256]{2,1,0:T(8,128)(2,1)S(1)} %get-tuple-element.66), channel_id=1, source_target_pairs={{0,1},{1,0},{2,3},{3,2},{4,5},{5,4},{6,7},{7,6},{8,9},{9,8},{10,11... | collective-permute-start | bytes 638984 | tf_op jit(solution)/shard_map/ppermute | solution.py:392
  30.5 1.6 %collective-permute-start.14 = (bf16[2,208,256]{2,1,0:T(8,128)(2,1)S(1)}, bf16[2,208,256]{2,1,0:T(8,128)(2,1)S(1)}, u32[]{:S(2)}, u32[]{:S(2)}) collective-permute-start(bf16[2,208,256]{2,1,0:T(8,128)(2,1)S(1)} %get-tuple-element.67), channel_id=1, source_target_pairs={{0,1},{1,0},{2,3},{3,2},{4,5},{5,4},{6,7},{7,6},{8,9},{9,8},{10,11... | collective-permute-start | bytes 638984 | tf_op jit(solution)/shard_map/ppermute | solution.py:392
  30.7 1.7 %collective-permute-start.15 = (bf16[2,208,256]{2,1,0:T(8,128)(2,1)S(1)}, bf16[2,208,256]{2,1,0:T(8,128)(2,1)S(1)}, u32[]{:S(2)}, u32[]{:S(2)}) collective-permute-start(bf16[2,208,256]{2,1,0:T(8,128)(2,1)S(1)} %get-tuple-element.68), channel_id=1, source_target_pairs={{0,1},{1,0},{2,3},{3,2},{4,5},{5,4},{6,7},{7,6},{8,9},{9,8},{10,11... | collective-permute-start | bytes 638984 | tf_op jit(solution)/shard_map/ppermute | solution.py:392
  33.1 11.9 %collective-permute-start.16 = (bf16[4,208,128]{2,1,0:T(8,128)(2,1)S(1)}, bf16[4,208,128]{2,1,0:T(8,128)(2,1)S(1)}, u32[]{:S(2)}, u32[]{:S(2)}) collective-permute-start(bf16[4,208,128]{2,1,0:T(8,128)(2,1)S(1)} %get-tuple-element.70), channel_id=1, source_target_pairs={{0,18},{1,19},{2,16},{3,17},{4,22},{5,23},{6,20},{7,21},{8,26},{9,... | collective-permute-start | bytes 638984 | tf_op jit(solution)/shard_map/ppermute | solution.py:396
  34.6 13.6 %collective-permute-start.17 = (bf16[4,208,128]{2,1,0:T(8,128)(2,1)S(1)}, bf16[4,208,128]{2,1,0:T(8,128)(2,1)S(1)}, u32[]{:S(2)}, u32[]{:S(2)}) collective-permute-start(bf16[4,208,128]{2,1,0:T(8,128)(2,1)S(1)} %get-tuple-element.71), channel_id=1, source_target_pairs={{0,16},{16,0},{1,17},{17,1},{2,18},{18,2},{3,19},{19,3},{4,20},{20... | collective-permute-start | bytes 638984 | tf_op jit(solution)/shard_map/ppermute | solution.py:394
  36.0 12.3 %collective-permute-start.18 = (bf16[4,208,128]{2,1,0:T(8,128)(2,1)S(1)}, bf16[4,208,128]{2,1,0:T(8,128)(2,1)S(1)}, u32[]{:S(2)}, u32[]{:S(2)}) collective-permute-start(bf16[4,208,128]{2,1,0:T(8,128)(2,1)S(1)} %get-tuple-element.72), channel_id=1, source_target_pairs={{0,2},{1,3},{2,0},{3,1},{4,6},{5,7},{6,4},{7,5},{8,10},{9,11},{10,... | collective-permute-start | bytes 638984 | tf_op jit(solution)/shard_map/ppermute | solution.py:392
  39.5 23.2 %copy-start.3 = (bf16[2,1024,256]{2,1,0:T(8,128)(2,1)S(1)}, bf16[2,1024,256]{2,1,0:T(8,128)(2,1)}, u32[]{:S(2)}) copy-start(bf16[2,1024,256]{2,1,0:T(8,128)(2,1)} %refs_1_.3) | copy-start | bytes 3145732
  40.2 8.1 %collective-permute-start.20 = (bf16[4,208,128]{2,1,0:T(8,128)(2,1)S(1)}, bf16[4,208,128]{2,1,0:T(8,128)(2,1)S(1)}, u32[]{:S(2)}, u32[]{:S(2)}) collective-permute-start(bf16[4,208,128]{2,1,0:T(8,128)(2,1)S(1)} %get-tuple-element.75), channel_id=1, source_target_pairs={{0,4},{1,5},{2,6},{3,7},{4,0},{5,1},{6,2},{7,3},{8,12},{9,13},{10,... | collective-permute-start | bytes 638984 | tf_op jit(solution)/shard_map/ppermute | solution.py:392
  49.0 5.9 %collective-permute-start.21 = (bf16[2,208,128]{2,1,0:T(8,128)(2,1)S(1)}, bf16[2,208,128]{2,1,0:T(8,128)(2,1)S(1)}, u32[]{:S(2)}, u32[]{:S(2)}) collective-permute-start(bf16[2,208,128]{2,1,0:T(8,128)(2,1)S(1)} %get-tuple-element.77), channel_id=1, source_target_pairs={{0,2},{1,3},{2,0},{3,1},{4,6},{5,7},{6,4},{7,5},{8,10},{9,11},{10,... | collective-permute-start | bytes 319496 | tf_op jit(solution)/shard_map/ppermute | solution.py:392
  50.4 6.0 %collective-permute-start.23 = (bf16[1,208,128]{2,1,0:T(8,128)(2,1)S(1)}, bf16[1,208,128]{2,1,0:T(8,128)(2,1)S(1)}, u32[]{:S(2)}, u32[]{:S(2)}) collective-permute-start(bf16[1,208,128]{2,1,0:T(8,128)(2,1)S(1)} %get-tuple-element.81), channel_id=1, source_target_pairs={{0,12},{1,13},{2,14},{3,15},{4,8},{5,9},{6,10},{7,11},{8,4},{9,5},... | collective-permute-start | bytes 159752 | tf_op jit(solution)/shard_map/ppermute | solution.py:392
  52.8 6.0 %collective-permute-start.24 = (bf16[1,208,128]{2,1,0:T(8,128)(2,1)S(1)}, bf16[1,208,128]{2,1,0:T(8,128)(2,1)S(1)}, u32[]{:S(2)}, u32[]{:S(2)}) collective-permute-start(bf16[1,208,128]{2,1,0:T(8,128)(2,1)S(1)} %get-tuple-element.82), channel_id=1, source_target_pairs={{0,8},{1,9},{2,10},{3,11},{4,12},{5,13},{6,14},{7,15},{8,0},{9,1},... | collective-permute-start | bytes 159752 | tf_op jit(solution)/shard_map/ppermute | solution.py:392
  52.8 6.0 %collective-permute-start.25 = (bf16[1,208,128]{2,1,0:T(8,128)(2,1)S(1)}, bf16[1,208,128]{2,1,0:T(8,128)(2,1)S(1)}, u32[]{:S(2)}, u32[]{:S(2)}) collective-permute-start(bf16[1,208,128]{2,1,0:T(8,128)(2,1)S(1)} %get-tuple-element.83), channel_id=1, source_target_pairs={{0,4},{1,5},{2,6},{3,7},{4,0},{5,1},{6,2},{7,3},{8,12},{9,13},{10,... | collective-permute-start | bytes 159752 | tf_op jit(solution)/shard_map/ppermute | solution.py:392
  55.4 5.2 %collective-permute-start.22 = (bf16[1,208,128]{2,1,0:T(8,128)(2,1)S(1)}, bf16[1,208,128]{2,1,0:T(8,128)(2,1)S(1)}, u32[]{:S(2)}, u32[]{:S(2)}) collective-permute-start(bf16[1,208,128]{2,1,0:T(8,128)(2,1)S(1)} %get-tuple-element.80), channel_id=1, source_target_pairs={{0,8},{1,9},{2,10},{3,11},{4,12},{5,13},{6,14},{7,15},{8,0},{9,1},... | collective-permute-start | bytes 159752 | tf_op jit(solution)/shard_map/ppermute | solution.py:392
  61.2 4.2 %collective-permute-start.26 = (bf16[208,128]{1,0:T(8,128)(2,1)S(1)}, bf16[208,128]{1,0:T(8,128)(2,1)S(1)}, u32[]{:S(2)}, u32[]{:S(2)}) collective-permute-start(bf16[208,128]{1,0:T(8,128)(2,1)S(1)} %get-tuple-element.85), channel_id=1, source_target_pairs={{0,16},{16,0},{1,17},{17,1},{2,18},{18,2},{3,19},{19,3},{4,20},{20... | collective-permute-start | bytes 159752 | tf_op jit(solution)/shard_map/ppermute | solution.py:394

commit v15 on v13

--- a/solution.py
+++ b/solution.py
@@ -67,26 +67,31 @@
     lax.fori_loop(0, images, per_image, 0)
 
 
+def column_ends(flags, centre, col_a, col_b, i, r):
+    width = centre.shape[2] - 8
+    col_odd, left, right = flags[COL_ODD] == 1, flags[LEFT_END] == 1, flags[RIGHT_END] == 1
+    own_first, own_last = centre[i, r, width : width + 1, :], centre[i, r, width + 1 : width + 2, :]
+    one, two = col_a[i, r].astype(F32), col_b[i, r].astype(F32)
+    before, after = jnp.where(col_odd, one, two), jnp.where(col_odd, two, one)
+    first = 0.75 * (before[2:3] + before[3:4]) + 0.25 * (before[1:2] + own_first)
+    last = 0.75 * (after[0:1] + after[1:2]) + 0.25 * (own_last + after[2:3])
+    return (
+        0.25 * jnp.where(left, own_first, before[3:4]),
+        0.25 * jnp.where(right, own_last, after[0:1]),
+        jnp.where(left, 0.0, first),
+        jnp.where(right, 0.0, last),
+    )
+
+
 def pool_columns(flags, centre, col_a, col_b, i, lines):
     width, channels = centre.shape[2] - 8, centre.shape[3]
-    col_odd, left, right = flags[COL_ODD] == 1, flags[LEFT_END] == 1, flags[RIGHT_END] == 1
     cell = lax.broadcasted_iota(jnp.int32, (width, channels), 0)
     is_first, is_last = cell == 0, cell == width - 1
     cells, beside = [], []
     for r in lines:
-        own_first, own_last = centre[i, r, width : width + 1, :], centre[i, r, width + 1 : width + 2, :]
-        one, two = col_a[i, r].astype(F32), col_b[i, r].astype(F32)
-        before, after = jnp.where(col_odd, one, two), jnp.where(col_odd, two, one)
-        near_before = jnp.where(left, own_first, before[3:4])
-        near_after = jnp.where(right, own_last, after[0:1])
-        cells.append(
-            centre[i, r, :width, :] + 0.25 * (jnp.where(is_first, near_before, 0.0) + jnp.where(is_last, near_after, 0.0))
-        )
-        first = 0.75 * (before[2:3] + before[3:4]) + 0.25 * (before[1:2] + own_first)
-        last = 0.75 * (after[0:1] + after[1:2]) + 0.25 * (own_last + after[2:3])
-        beside.append(
-            jnp.concatenate([jnp.where(left, 0.0, first), jnp.where(right, 0.0, last)], axis=0)
-        )
+        to_first, to_last, first, last = column_ends(flags, centre, col_a, col_b, i, r)
+        cells.append(centre[i, r, :width, :] + (jnp.where(is_first, to_first, 0.0) + jnp.where(is_last, to_last, 0.0)))
+        beside.append(jnp.concatenate([first, last], axis=0))
     return cells, beside
 
 
@@ -117,20 +122,15 @@
                 out[at : at + width, :] = jnp.where(row_odd, odd, even).astype(BF16)
 
 
-def corner_pack_kernel(has_second, flags, centre, col_a, col_b, *refs):
-    outs, (cells_out, beside_out, ends) = refs[: 2 if has_second else 1], refs[-3:]
-    images, height2, width = centre.shape[0], centre.shape[1], centre.shape[2] - 8
+def corner_pack_kernel(flags, centre, col_a, col_b, *refs):
+    outs, ends = refs[:-1], refs[-1]
+    images, height2 = centre.shape[:2]
     row_odd = flags[ROW_ODD] == 1
-    lines = [0, 1, 2, height2 - 3, height2 - 2, height2 - 1]
     for i in range(images):
-        cells, beside = pool_columns(flags, centre, col_a, col_b, i, lines)
-        added = []
-        for n in range(6):
-            cells_out[i, n] = cells[n]
-            beside_out[i, n] = beside[n]
-            more = cells[n] - centre[i, lines[n], :width, :]
-            added.append(jnp.concatenate([more[:1], more[width - 1 :], beside[n]], axis=0))
-        above, below = facing(added)
+        lines = (0, 1, 2, height2 - 3, height2 - 2, height2 - 1)
+        above, below = facing(
+            [jnp.concatenate(column_ends(flags, centre, col_a, col_b, i, r), axis=0) for r in lines]
+        )
         for second in range(len(outs)):
             for n in range(2):
                 odd, even = (below[n], above[n]) if second else (above[n], below[n])
@@ -140,15 +140,18 @@
         outs[second][...] = ends[second].astype(BF16)
 
 
-def main_kernel(flags, centre, col_a, col_b, weight, window, acc, pooled):
+def main_kernel(flags, centre, col_a, col_b, weight, window, acc, cells_out, beside_out, pooled):
     images, height2, width, channels = centre.shape[0], centre.shape[1], centre.shape[2] - 8, centre.shape[3]
     height, depths = height2 // 2, weight.shape[0]
     pooled[...] = jnp.zeros_like(pooled)
 
     def per_image(i, carry):
-        cells, beside = pool_columns(flags, centre, col_a, col_b, i, range(1, height2 - 1))
+        cells, beside = pool_columns(flags, centre, col_a, col_b, i, range(height2))
+        for n, r in enumerate((0, 1, 2, height2 - 3, height2 - 2, height2 - 1)):
+            cells_out[i, n] = cells[r]
+            beside_out[i, n] = beside[r]
         for p in range(1, height - 1):
-            at = 2 * p - 2
+            at = 2 * p - 1
             both = [
                 0.75 * (group[at + 1] + group[at + 2]) + 0.25 * (group[at] + group[at + 3])
                 for group in (cells, beside)
@@ -481,18 +484,22 @@
     )
     row_out = vmem_call(row_pack_kernel, [sds(2 * line, channels)] * sides, (flags, centre))
     came_rows = [swap(row_out[n], paired(rows, n), None) for n in range(sides)]
-    *corner_out, cells, beside = vmem_call(
-        functools.partial(corner_pack_kernel, has_second),
-        [sds(8 * images, channels)] * sides
-        + [sds(images, 6, width, channels, dtype=F32), sds(images, 6, 2, channels, dtype=F32)],
+    corner_out = vmem_call(
+        corner_pack_kernel,
+        [sds(8 * images, channels)] * sides,
         (flags, centre, col_a, col_b),
         scratch=(pltpu.VMEM((sides, 8 * images, channels), F32),),
     )
     came_rows += [swap(corner_out[n], paired(rows, n), None) for n in range(sides)]
     conv_flops = 2 * patches * depths * 9 * channels * channels
-    window, acc = vmem_call(
+    window, acc, cells, beside = vmem_call(
         main_kernel,
-        [sds(3, (height + 2) * line, channels), sds(depths, patches, channels, dtype=F32)],
+        [
+            sds(3, (height + 2) * line, channels),
+            sds(depths, patches, channels, dtype=F32),
+            sds(images, 6, width, channels, dtype=F32),
+            sds(images, 6, 2, channels, dtype=F32),
+        ],
         (flags, centre, col_a, col_b, conv_weight),
         scratch=(pltpu.VMEM((height, LEFT + width + 8, channels), F32),),
         flops=conv_flops,

time: 66.7 us -> 66.6 us (level)
  no operation moved by 1% of the time
where the time goes in v15:
time: 66.6 us; the launch traced here: 66.5 us
  starting transfers between devices  26.9 us (40%)
  waiting for transfers between devices  19.6 us (29%)
  Pallas kernels  16.6 us (25%)
  local copies, waits for them, and re-layouts  1.34 us (2%)
  other arithmetic  1.19 us (2%)
  between operations  0.88 us (1%)
    pallas_call x16, Pallas kernels, vmem_call(): pl.pallas_call(run, out_shape=out_shape, in_specs=specs, out_specs=jax.tr...  16.6 us
    ppermute x19, starting transfers between devices, xor_move(): return lax.ppermute(block, 'tile', [(t, t ^ apart) for t in range(tiles)])  14.1 us
    ppermute x19, waiting for transfers between devices, xor_move(): return lax.ppermute(block, 'tile', [(t, t ^ apart) for t in range(tiles)])  7.93 us
    ppermute x3, waiting for transfers between devices, xor_move(): return lax.ppermute(block, 'dp', [(0, 1), (1, 0)])  6.78 us
    ppermute x4, starting transfers between devices, swap(): return lax.ppermute(block, 'tile', tile_route(row_pairs, col_pairs, rows))  6.71 us
    ppermute x3, starting transfers between devices, xor_move(): return lax.ppermute(block, 'dp', [(0, 1), (1, 0)])  4.47 us
    ppermute x1, waiting for transfers between devices, xor_move(): return lax.ppermute(block, ('dp', 'tile'), route)  3.57 us
    ppermute x1, starting transfers between devices, xor_move(): return lax.ppermute(block, ('dp', 'tile'), route)  1.58 us
  transfers between devices with their start and end apart: 27, of which 14 were waited for; matrix products, arithmetic and copies ran while one was open for 0% of the time, Pallas kernels for 19%

profile of v15, /device:TPU:0, one launch (start us, length us, event | category | flops | bytes accessed | tf_op | source)
XLA Modules:
  0.0 66.5 jit_solution(7311124238639086625)
XLA Ops:
  0.7 1.2 %broadcast_select_fusion = (bf16[4,16,4,256]{3,2,1,0:T(4,128)(2,1)S(1)}, bf16[4,16,4,256]{3,2,1,0:T(4,128)(2,1)S(1)}) fusion(pred[]{:T(512)S(6)} %eq.27, bf16[4,16,32,256]{3,2,1,0:T(8,128)(2,1)} %refs_0_.1), kind=kLoop, calls=%fused_computation | loop fusion | flops 131072 | bytes 524289 | tf_op jit(solution)/shard_map/jit(_where)/select_n | solution.py:476
  1.9 3.1 %collective-permute-start.2 = (bf16[4,16,4,256]{3,2,1,0:T(4,128)(2,1)S(1)}, bf16[4,16,4,256]{3,2,1,0:T(4,128)(2,1)S(1)}, u32[]{:S(2)}, u32[]{:S(2)}) collective-permute-start(bf16[4,16,4,256]{3,2,1,0:T(4,128)(2,1)S(1)} %get-tuple-element.80), channel_id=1, source_target_pairs={{1,3},{3,1},{2,6},{6,2},{7,5},{5,7},{0,4},{4,0},{9,11},{11,9},{10,... | collective-permute-start | bytes 393224 | tf_op jit(solution)/shard_map/ppermute | solution.py:472
  4.9 0.0 collective-permute-start.1
  4.9 1.2 %copy-done.2 = bf16[4,16,32,256]{3,2,1,0:T(8,128)(2,1)S(1)} copy-done((bf16[4,16,32,256]{3,2,1,0:T(8,128)(2,1)S(1)}, bf16[4,16,32,256]{3,2,1,0:T(8,128)(2,1)}, u32[]{:S(2)}) %copy-start.2) | copy-done | bytes 1048600
  6.2 0.5 shard_map.68.refs_1_
  6.7 0.1 stack.71.refs_0_
  6.8 0.0 copy-start
  6.8 0.6 shard_map.69
  7.4 2.7 %collective-permute-start = (bf16[128,256]{1,0:T(8,128)(2,1)S(1)}, bf16[128,256]{1,0:T(8,128)(2,1)S(1)}, u32[]{:S(2)}, u32[]{:S(2)}) collective-permute-start(bf16[128,256]{1,0:T(8,128)(2,1)S(1)} %shard_map.69), channel_id=1, source_target_pairs={{0,8},{1,9},{3,11},{2,10},{6,14},{7,15},{5,13},{4,12},{8,0},{9,1},... | collective-permute-start | bytes 196616 | tf_op jit(solution)/shard_map/ppermute | solution.py:472
  10.0 0.0 collective-permute-done.2.refs_3_
  10.0 0.0 collective-permute-done.1.refs_2_
  10.0 0.7 %shard_map.70.refs_5_ = bf16[32,256]{1,0:T(8,128)(2,1)S(1)} custom-call(s32[13]{0:T(128)S(1)} %stack.71.refs_0_, f32[4,16,24,256]{3,2,1,0:T(8,128)S(1)} %shard_map.68.refs_1_, bf16[4,16,4,256]{3,2,1,0:T(4,128)(2,1)S(1)} %collective-permute-done.1.refs_2_, bf16[4,16,4,256]{3,2,1,0:T(4,128)(2,1)S(1)} %collective-permute-done.2.refs_3_), custom_call_target="tpu_custom_call" | custom-call | bytes 1851444 | tf_op jit(solution)/shard_map/pallas_call | solution.py:380
  10.7 1.0 %collective-permute-start.3 = (bf16[32,256]{1,0:T(8,128)(2,1)S(1)}, bf16[32,256]{1,0:T(8,128)(2,1)S(1)}, u32[]{:S(2)}, u32[]{:S(2)}) collective-permute-start(bf16[32,256]{1,0:T(8,128)(2,1)S(1)} %shard_map.70.refs_5_), channel_id=1, source_target_pairs={{0,8},{1,9},{3,11},{2,10},{6,14},{7,15},{5,13},{4,12},{8,0},{9,1},... | collective-permute-start | bytes 49160 | tf_op jit(solution)/shard_map/ppermute | solution.py:472
  11.7 2.4 %shard_map.71 = (bf16[3,640,256]{2,1,0:T(8,128)(2,1)S(1)}, f32[2,512,256]{2,1,0:T(8,128)S(1)}, f32[4,6,16,256]{3,2,1,0:T(8,128)S(1)}, f32[4,6,2,256]{3,2,1,0:T(2,128)S(1)}) custom-call(s32[13]{0:T(128)S(1)} %stack.71.refs_0_, f32[4,16,24,256]{3,2,1,0:T(8,128)S(1)} %shard_map.68.refs_1_, bf16[4,16,4,256]{3,2,1,0:T(4,128)(2,1)S(1)} %collective-permute-done.1.refs_2_, ...), custom_call_target="tpu_custom_call" | custom-call | flops 1207959552 | bytes 6668340 | tf_op jit(solution)/shard_map/pallas_call | solution.py:380
  14.2 0.1 collective-permute-done.refs_1_
  14.2 1.2 %collective-permute-done.3.refs_2_ = bf16[32,256]{1,0:T(8,128)(2,1)S(1)} collective-permute-done((bf16[32,256]{1,0:T(8,128)(2,1)S(1)}, bf16[32,256]{1,0:T(8,128)(2,1)S(1)}, u32[]{:S(2)}, u32[]{:S(2)}) %collective-permute-start.3) | collective-permute-done | bytes 16416 | tf_op jit(solution)/shard_map/ppermute | solution.py:472
  15.4 1.6 %shard_map.72 = (bf16[2,2,64,256]{3,2,1,0:T(8,128)(2,1)S(1)}, bf16[2,2,64,256]{3,2,1,0:T(8,128)(2,1)S(1)}, bf16[2,2,64,256]{3,2,1,0:T(8,128)(2,1)S(1)}, bf16[2,2...) custom-call(s32[13]{0:T(128)S(1)} %stack.71.refs_0_, ...), custom_call_target="tpu_custom_call", output_to_operand_aliasing={{4}: (5, {})} | custom-call | flops 301989888 | bytes 6422580 | tf_op jit(solution)/shard_map/pallas_call | solution.py:380
  17.1 1.6 %collective-permute-start.4 = (bf16[2,2,64,256]{3,2,1,0:T(8,128)(2,1)S(1)}, bf16[2,2,64,256]{3,2,1,0:T(8,128)(2,1)S(1)}, u32[]{:S(2)}, u32[]{:S(2)}) collective-permute-start(bf16[2,2,64,256]{3,2,1,0:T(8,128)(2,1)S(1)} %get-tuple-element.46), channel_id=1, source_target_pairs={{0,2},{1,3},{2,0},{3,1},{4,6},{5,7},{6,4},{7,5},{8,10},{9,11},{10,... | collective-permute-start | bytes 393224 | tf_op jit(solution)/shard_map/ppermute | solution.py:399
  18.7 0.4 collective-permute-start.5
  19.1 1.5 %collective-permute-start.6 = (bf16[2,2,64,256]{3,2,1,0:T(8,128)(2,1)S(1)}, bf16[2,2,64,256]{3,2,1,0:T(8,128)(2,1)S(1)}, u32[]{:S(2)}, u32[]{:S(2)}) collective-permute-start(bf16[2,2,64,256]{3,2,1,0:T(8,128)(2,1)S(1)} %get-tuple-element.48), channel_id=1, source_target_pairs={{0,6},{1,7},{2,4},{3,5},{4,2},{5,3},{6,0},{7,1},{8,14},{9,15},{10,... | collective-permute-start | bytes 393224 | tf_op jit(solution)/shard_map/ppermute | solution.py:399
  20.6 2.1 %shard_map.74 = (bf16[8,208,256]{2,1,0:T(8,128)(2,1)S(1)}, bf16[2,208,256]{2,1,0:T(8,128)(2,1)S(1)}, bf16[2,208,256]{2,1,0:T(8,128)(2,1)S(1)}, bf16[2,208,256]{2...) custom-call(s32[13]{0:T(128)S(1)} %stack.71.refs_0_, ...), custom_call_target="tpu_custom_call" | custom-call | flops 1207959552 | bytes 3866676 | tf_op jit(solution)/shard_map/pallas_call | solution.py:380
  22.7 0.0 copy-start.1
  22.7 0.1 collective-permute-start.8
  22.8 0.5 collective-permute-start.9
  23.3 0.0 collective-permute-done.4.refs_1_.refs_2_
  23.3 0.1 collective-permute-start.10
  23.4 0.9 %collective-permute-done.5.refs_2_.refs_3_ = bf16[2,2,64,256]{3,2,1,0:T(8,128)(2,1)S(1)} collective-permute-done((bf16[2,2,64,256]{3,2,1,0:T(8,128)(2,1)S(1)}, bf16[2,2,64,256]{3,2,1,0:T(8,128)(2,1)S(1)}, u32[]{:S(2)}, u32[]{:S(2)}) %collective-permute-start.5) | collective-permute-done | bytes 131104 | tf_op jit(solution)/shard_map/ppermute | solution.py:399
  24.3 0.0 collective-permute-start.11
  24.3 1.5 %collective-permute-done.6.refs_3_.refs_4_ = bf16[2,2,64,256]{3,2,1,0:T(8,128)(2,1)S(1)} collective-permute-done((bf16[2,2,64,256]{3,2,1,0:T(8,128)(2,1)S(1)}, bf16[2,2,64,256]{3,2,1,0:T(8,128)(2,1)S(1)}, u32[]{:S(2)}, u32[]{:S(2)}) %collective-permute-start.6) | collective-permute-done | bytes 131104 | tf_op jit(solution)/shard_map/ppermute | solution.py:399
  25.8 0.1 collective-permute-start.7
  25.9 0.0 collective-permute-done.8.refs_2_
  25.9 0.7 %shard_map.75 = (f32[8,208,128]{2,1,0:T(8,128)S(1)}, bf16[8,208,128]{2,1,0:T(8,128)(2,1)S(1)}) custom-call(s32[13]{0:T(128)S(1)} %stack.71.refs_0_, bf16[8,208,256]{2,1,0:T(8,128)(2,1)S(1)} %get-tuple-element.51.refs_1_, bf16[2,208,256]{2,1,0:T(8,128)(2,1)S(1)} %collective-permute-done.8.refs_2_, bf16[2,208,256]{2,1,0:T(8,128)(2,1)S(1)} %collective-permute-done.9.refs_3_, ...), custom_call_target="tpu_custom_call" | custom-call | bytes 2981940 | tf_op jit(solution)/shard_map/pallas_call | solution.py:380
  26.7 1.6 %collective-permute-start.19 = (bf16[8,208,128]{2,1,0:T(8,128)(2,1)S(1)}, bf16[8,208,128]{2,1,0:T(8,128)(2,1)S(1)}, u32[]{:S(2)}, u32[]{:S(2)}) collective-permute-start(bf16[8,208,128]{2,1,0:T(8,128)(2,1)S(1)} %get-tuple-element.67), channel_id=1, source_target_pairs={{0,16},{16,0},{1,17},{17,1},{2,18},{18,2},{3,19},{19,3},{4,20},{20... | collective-permute-start | bytes 1277960 | tf_op jit(solution)/shard_map/ppermute | solution.py:401
  28.2 1.5 %shard_map.76 = (bf16[8,208,256]{2,1,0:T(8,128)(2,1)S(1)}, bf16[2,208,256]{2,1,0:T(8,128)(2,1)S(1)}, bf16[2,208,256]{2,1,0:T(8,128)(2,1)S(1)}, bf16[2,208,256]{2...) custom-call(s32[13]{0:T(128)S(1)} %stack.71.refs_0_, ...), custom_call_target="tpu_custom_call" | custom-call | flops 536870912 | bytes 5767220 | tf_op jit(solution)/shard_map/pallas_call | solution.py:380
  29.7 0.3 collective-permute-start.12
  30.0 0.3 collective-permute-start.13
  30.3 0.2 collective-permute-start.14
  30.5 0.3 collective-permute-start.15
  30.8 0.4 collective-permute-done.12.refs_2_
  31.2 0.3 collective-permute-done.13.refs_3_
  31.5 0.3 collective-permute-done.14.refs_4_
  31.9 0.3 collective-permute-done.15.refs_5_
  32.2 0.7 %shard_map.77 = (f32[4,208,128]{2,1,0:T(8,128)S(1)}, bf16[4,208,128]{2,1,0:T(8,128)(2,1)S(1)}, bf16[4,208,128]{2,1,0:T(8,128)(2,1)S(1)}, bf16[4,208,128]{2,1,0:T(8,128)(2,1)S(1)}) custom-call(s32[13]{0:T(128)S(1)} %stack.71.refs_0_, bf16[8,208,256]{2,1,0:T(8,128)(2,1)S(1)} %get-tuple-element.58.refs_1_, ...), custom_call_target="tpu_custom_call" | custom-call | bytes 2768948 | tf_op jit(solution)/shard_map/pallas_call | solution.py:380
  32.9 1.6 %collective-permute-start.16 = (bf16[4,208,128]{2,1,0:T(8,128)(2,1)S(1)}, bf16[4,208,128]{2,1,0:T(8,128)(2,1)S(1)}, u32[]{:S(2)}, u32[]{:S(2)}) collective-permute-start(bf16[4,208,128]{2,1,0:T(8,128)(2,1)S(1)} %get-tuple-element.64), channel_id=1, source_target_pairs={{0,18},{1,19},{2,16},{3,17},{4,22},{5,23},{6,20},{7,21},{8,26},{9,... | collective-permute-start | bytes 638984 | tf_op jit(solution)/shard_map/ppermute | solution.py:403
  34.5 1.4 %collective-permute-start.17 = (bf16[4,208,128]{2,1,0:T(8,128)(2,1)S(1)}, bf16[4,208,128]{2,1,0:T(8,128)(2,1)S(1)}, u32[]{:S(2)}, u32[]{:S(2)}) collective-permute-start(bf16[4,208,128]{2,1,0:T(8,128)(2,1)S(1)} %get-tuple-element.65), channel_id=1, source_target_pairs={{0,16},{16,0},{1,17},{17,1},{2,18},{18,2},{3,19},{19,3},{4,20},{20... | collective-permute-start | bytes 638984 | tf_op jit(solution)/shard_map/ppermute | solution.py:401
  35.8 0.6 collective-permute-start.18
  36.5 2.9 %collective-permute-done.19.refs_2_ = bf16[8,208,128]{2,1,0:T(8,128)(2,1)S(1)} collective-permute-done((bf16[8,208,128]{2,1,0:T(8,128)(2,1)S(1)}, bf16[8,208,128]{2,1,0:T(8,128)(2,1)S(1)}, u32[]{:S(2)}, u32[]{:S(2)}) %collective-permute-start.19) | collective-permute-done | bytes 426016 | tf_op jit(solution)/shard_map/ppermute | solution.py:401
  39.4 0.6 shard_map.78
  40.0 1.2 %collective-permute-start.20 = (bf16[4,208,128]{2,1,0:T(8,128)(2,1)S(1)}, bf16[4,208,128]{2,1,0:T(8,128)(2,1)S(1)}, u32[]{:S(2)}, u32[]{:S(2)}) collective-permute-start(bf16[4,208,128]{2,1,0:T(8,128)(2,1)S(1)} %get-tuple-element.69), channel_id=1, source_target_pairs={{0,4},{1,5},{2,6},{3,7},{4,0},{5,1},{6,2},{7,3},{8,12},{9,13},{10,... | collective-permute-start | bytes 638984 | tf_op jit(solution)/shard_map/ppermute | solution.py:399
  41.2 3.6 %collective-permute-done.16.refs_2_ = bf16[4,208,128]{2,1,0:T(8,128)(2,1)S(1)} collective-permute-done((bf16[4,208,128]{2,1,0:T(8,128)(2,1)S(1)}, bf16[4,208,128]{2,1,0:T(8,128)(2,1)S(1)}, u32[]{:S(2)}, u32[]{:S(2)}) %collective-permute-start.16) | collective-permute-done | bytes 213024 | tf_op jit(solution)/shard_map/ppermute | solution.py:403
  44.8 3.3 %collective-permute-done.17.refs_3_ = bf16[4,208,128]{2,1,0:T(8,128)(2,1)S(1)} collective-permute-done((bf16[4,208,128]{2,1,0:T(8,128)(2,1)S(1)}, bf16[4,208,128]{2,1,0:T(8,128)(2,1)S(1)}, u32[]{:S(2)}, u32[]{:S(2)}) %collective-permute-start.17) | collective-permute-done | bytes 213024 | tf_op jit(solution)/shard_map/ppermute | solution.py:401
  48.1 0.7 %shard_map.79 = (f32[1,208,128]{2,1,0:T(8,128)S(1)}, bf16[1,208,128]{2,1,0:T(8,128)(2,1)S(1)}, bf16[1,208,128]{2,1,0:T(8,128)(2,1)S(1)}, bf16[1,208,128]{2,1,0:T...) custom-call(s32[13]{0:T(128)S(1)} %stack.71.refs_0_, ...), custom_call_target="tpu_custom_call" | custom-call | bytes 2289716 | tf_op jit(solution)/shard_map/pallas_call | solution.py:380
  48.8 1.5 %collective-permute-start.21 = (bf16[2,208,128]{2,1,0:T(8,128)(2,1)S(1)}, bf16[2,208,128]{2,1,0:T(8,128)(2,1)S(1)}, u32[]{:S(2)}, u32[]{:S(2)}) collective-permute-start(bf16[2,208,128]{2,1,0:T(8,128)(2,1)S(1)} %get-tuple-element.71), channel_id=1, source_target_pairs={{0,2},{1,3},{2,0},{3,1},{4,6},{5,7},{6,4},{7,5},{8,10},{9,11},{10,... | collective-permute-start | bytes 319496 | tf_op jit(solution)/shard_map/ppermute | solution.py:399
  50.3 2.5 %collective-permute-start.23 = (bf16[1,208,128]{2,1,0:T(8,128)(2,1)S(1)}, bf16[1,208,128]{2,1,0:T(8,128)(2,1)S(1)}, u32[]{:S(2)}, u32[]{:S(2)}) collective-permute-start(bf16[1,208,128]{2,1,0:T(8,128)(2,1)S(1)} %get-tuple-element.75), channel_id=1, source_target_pairs={{0,12},{1,13},{2,14},{3,15},{4,8},{5,9},{6,10},{7,11},{8,4},{9,5},... | collective-permute-start | bytes 159752 | tf_op jit(solution)/shard_map/ppermute | solution.py:399
  52.7 1.9 %collective-permute-start.25 = (bf16[1,208,128]{2,1,0:T(8,128)(2,1)S(1)}, bf16[1,208,128]{2,1,0:T(8,128)(2,1)S(1)}, u32[]{:S(2)}, u32[]{:S(2)}) collective-permute-start(bf16[1,208,128]{2,1,0:T(8,128)(2,1)S(1)} %get-tuple-element.77), channel_id=1, source_target_pairs={{0,4},{1,5},{2,6},{3,7},{4,0},{5,1},{6,2},{7,3},{8,12},{9,13},{10,... | collective-permute-start | bytes 159752 | tf_op jit(solution)/shard_map/ppermute | solution.py:399
  54.7 0.6 shard_map.80
  55.2 1.1 %collective-permute-start.22 = (bf16[1,208,128]{2,1,0:T(8,128)(2,1)S(1)}, bf16[1,208,128]{2,1,0:T(8,128)(2,1)S(1)}, u32[]{:S(2)}, u32[]{:S(2)}) collective-permute-start(bf16[1,208,128]{2,1,0:T(8,128)(2,1)S(1)} %get-tuple-element.74), channel_id=1, source_target_pairs={{0,8},{1,9},{2,10},{3,11},{4,12},{5,13},{6,14},{7,15},{8,0},{9,1},... | collective-permute-start | bytes 159752 | tf_op jit(solution)/shard_map/ppermute | solution.py:399
  56.3 2.5 %collective-permute-done.24.refs_5_ = bf16[1,208,128]{2,1,0:T(8,128)(2,1)S(1)} collective-permute-done((bf16[1,208,128]{2,1,0:T(8,128)(2,1)S(1)}, bf16[1,208,128]{2,1,0:T(8,128)(2,1)S(1)}, u32[]{:S(2)}, u32[]{:S(2)}) %collective-permute-start.24) | collective-permute-done | bytes 53280 | tf_op jit(solution)/shard_map/ppermute | solution.py:399
  58.8 1.7 %collective-permute-done.22.refs_2_ = bf16[1,208,128]{2,1,0:T(8,128)(2,1)S(1)} collective-permute-done((bf16[1,208,128]{2,1,0:T(8,128)(2,1)S(1)}, bf16[1,208,128]{2,1,0:T(8,128)(2,1)S(1)}, u32[]{:S(2)}, u32[]{:S(2)}) %collective-permute-start.22) | collective-permute-done | bytes 53280 | tf_op jit(solution)/shard_map/ppermute | solution.py:399
  60.4 0.6 shard_map.82
  61.0 1.6 %collective-permute-start.26 = (bf16[208,128]{1,0:T(8,128)(2,1)S(1)}, bf16[208,128]{1,0:T(8,128)(2,1)S(1)}, u32[]{:S(2)}, u32[]{:S(2)}) collective-permute-start(bf16[208,128]{1,0:T(8,128)(2,1)S(1)} %get-tuple-element.79), channel_id=1, source_target_pairs={{0,16},{16,0},{1,17},{17,1},{2,18},{18,2},{3,19},{19,3},{4,20},{20... | collective-permute-start | bytes 159752 | tf_op jit(solution)/shard_map/ppermute | solution.py:401
  62.6 2.1 %shard_map.81 = bf16[4,2,128,1024]{3,2,1,0:T(8,128)(2,1)} custom-call(bf16[2,512,256]{2,1,0:T(8,128)(2,1)S(1)} %get-tuple-element.57.refs_6_.refs_0_, bf16[2,1024,256]{2,1,0:T(8,128)(2,1)S(1)} %copy-done.3, f32[1,208,128]{2,1,0:T(8,128)S(1)} %get-tuple-element.73.refs_2_.refs_1_), custom_call_target="tpu_custom_call" | custom-call | flops 536870912 | bytes 3670016 | tf_op jit(solution)/shard_map/pallas_call | solution.py:380
  64.7 0.6 collective-permute-done.26.refs_2_
  65.2 1.2 %shard_map.83 = f32[208,256]{1,0:T(8,128)} custom-call(s32[13]{0:T(128)S(1)} %stack.71.refs_0_, f32[208,128]{1,0:T(8,128)S(1)} %get-tuple-element.78.refs_1_, bf16[208,128]{1,0:T(8,128)(2,1)S(1)} %collective-permute-done.26.refs_2_), custom_call_target="tpu_custom_call" | custom-call | bytes 372788 | tf_op jit(solution)/shard_map/pallas_call | solution.py:380
  (18 shorter events, 0.1 us)
Async XLA Ops:
  1.9 8.2 %collective-permute-start.2 = (bf16[4,16,4,256]{3,2,1,0:T(4,128)(2,1)S(1)}, bf16[4,16,4,256]{3,2,1,0:T(4,128)(2,1)S(1)}, u32[]{:S(2)}, u32[]{:S(2)}) collective-permute-start(bf16[4,16,4,256]{3,2,1,0:T(4,128)(2,1)S(1)} %get-tuple-element.80), channel_id=1, source_target_pairs={{1,3},{3,1},{2,6},{6,2},{7,5},{5,7},{0,4},{4,0},{9,11},{11,9},{10,... | collective-permute-start | bytes 393224 | tf_op jit(solution)/shard_map/ppermute | solution.py:472
  4.9 5.1 %collective-permute-start.1 = (bf16[4,16,4,256]{3,2,1,0:T(4,128)(2,1)S(1)}, bf16[4,16,4,256]{3,2,1,0:T(4,128)(2,1)S(1)}, u32[]{:S(2)}, u32[]{:S(2)}) collective-permute-start(bf16[4,16,4,256]{3,2,1,0:T(4,128)(2,1)S(1)} %get-tuple-element.81), channel_id=1, source_target_pairs={{0,1},{1,0},{3,2},{2,3},{6,7},{7,6},{5,4},{4,5},{8,9},{9,8},{11,10... | collective-permute-start | bytes 393224 | tf_op jit(solution)/shard_map/ppermute | solution.py:472
  4.9 1.2 %copy-start.2 = (bf16[4,16,32,256]{3,2,1,0:T(8,128)(2,1)S(1)}, bf16[4,16,32,256]{3,2,1,0:T(8,128)(2,1)}, u32[]{:S(2)}) copy-start(bf16[4,16,32,256]{3,2,1,0:T(8,128)(2,1)} %refs_0_.1) | copy-start | bytes 3145732
  6.8 4.9 %copy-start = (bf16[2,3,3,256,256]{4,3,2,1,0:T(8,128)(2,1)S(1)}, bf16[2,3,3,256,256]{4,3,2,1,0:T(8,128)(2,1)}, u32[]{:S(2)}) copy-start(bf16[2,3,3,256,256]{4,3,2,1,0:T(8,128)(2,1)} %refs_7_.1) | copy-start | bytes 7077892
  7.4 6.9 %collective-permute-start = (bf16[128,256]{1,0:T(8,128)(2,1)S(1)}, bf16[128,256]{1,0:T(8,128)(2,1)S(1)}, u32[]{:S(2)}, u32[]{:S(2)}) collective-permute-start(bf16[128,256]{1,0:T(8,128)(2,1)S(1)} %shard_map.69), channel_id=1, source_target_pairs={{0,8},{1,9},{3,11},{2,10},{6,14},{7,15},{5,13},{4,12},{8,0},{9,1},... | collective-permute-start | bytes 196616 | tf_op jit(solution)/shard_map/ppermute | solution.py:472
  10.7 4.7 %collective-permute-start.3 = (bf16[32,256]{1,0:T(8,128)(2,1)S(1)}, bf16[32,256]{1,0:T(8,128)(2,1)S(1)}, u32[]{:S(2)}, u32[]{:S(2)}) collective-permute-start(bf16[32,256]{1,0:T(8,128)(2,1)S(1)} %shard_map.70.refs_5_), channel_id=1, source_target_pairs={{0,8},{1,9},{3,11},{2,10},{6,14},{7,15},{5,13},{4,12},{8,0},{9,1},... | collective-permute-start | bytes 49160 | tf_op jit(solution)/shard_map/ppermute | solution.py:472
  15.4 5.2 %copy-start.4 = (bf16[4,2,8,16,256]{4,3,2,1,0:T(8,128)(2,1)S(1)}, bf16[4,2,8,16,256]{4,3,2,1,0:T(8,128)(2,1)}, u32[]{:S(2)}) copy-start(bf16[4,2,8,16,256]{4,3,2,1,0:T(8,128)(2,1)} %refs_2_.1) | copy-start | bytes 1572868
  17.1 6.2 %collective-permute-start.4 = (bf16[2,2,64,256]{3,2,1,0:T(8,128)(2,1)S(1)}, bf16[2,2,64,256]{3,2,1,0:T(8,128)(2,1)S(1)}, u32[]{:S(2)}, u32[]{:S(2)}) collective-permute-start(bf16[2,2,64,256]{3,2,1,0:T(8,128)(2,1)S(1)} %get-tuple-element.46), channel_id=1, source_target_pairs={{0,2},{1,3},{2,0},{3,1},{4,6},{5,7},{6,4},{7,5},{8,10},{9,11},{10,... | collective-permute-start | bytes 393224 | tf_op jit(solution)/shard_map/ppermute | solution.py:399
  18.7 5.6 %collective-permute-start.5 = (bf16[2,2,64,256]{3,2,1,0:T(8,128)(2,1)S(1)}, bf16[2,2,64,256]{3,2,1,0:T(8,128)(2,1)S(1)}, u32[]{:S(2)}, u32[]{:S(2)}) collective-permute-start(bf16[2,2,64,256]{3,2,1,0:T(8,128)(2,1)S(1)} %get-tuple-element.47), channel_id=1, source_target_pairs={{0,4},{1,5},{2,6},{3,7},{4,0},{5,1},{6,2},{7,3},{8,12},{9,13},{10,... | collective-permute-start | bytes 393224 | tf_op jit(solution)/shard_map/ppermute | solution.py:399
  19.1 6.7 %collective-permute-start.6 = (bf16[2,2,64,256]{3,2,1,0:T(8,128)(2,1)S(1)}, bf16[2,2,64,256]{3,2,1,0:T(8,128)(2,1)S(1)}, u32[]{:S(2)}, u32[]{:S(2)}) collective-permute-start(bf16[2,2,64,256]{3,2,1,0:T(8,128)(2,1)S(1)} %get-tuple-element.48), channel_id=1, source_target_pairs={{0,6},{1,7},{2,4},{3,5},{4,2},{5,3},{6,0},{7,1},{8,14},{9,15},{10,... | collective-permute-start | bytes 393224 | tf_op jit(solution)/shard_map/ppermute | solution.py:399
  22.7 5.5 %copy-start.1 = (bf16[4,2,128,1024]{3,2,1,0:T(8,128)(2,1)S(1)}, bf16[4,2,128,1024]{3,2,1,0:T(8,128)(2,1)}, u32[]{:S(2)}) copy-start(bf16[4,2,128,1024]{3,2,1,0:T(8,128)(2,1)} %refs_6_.1) | copy-start | bytes 6291460
  22.7 3.2 %collective-permute-start.8 = (bf16[2,208,256]{2,1,0:T(8,128)(2,1)S(1)}, bf16[2,208,256]{2,1,0:T(8,128)(2,1)S(1)}, u32[]{:S(2)}, u32[]{:S(2)}) collective-permute-start(bf16[2,208,256]{2,1,0:T(8,128)(2,1)S(1)} %get-tuple-element.52), channel_id=1, source_target_pairs={{0,1},{1,0},{2,3},{3,2},{4,5},{5,4},{6,7},{7,6},{8,9},{9,8},{10,11... | collective-permute-start | bytes 638984 | tf_op jit(solution)/shard_map/ppermute | solution.py:399
  22.8 3.1 %collective-permute-start.9 = (bf16[2,208,256]{2,1,0:T(8,128)(2,1)S(1)}, bf16[2,208,256]{2,1,0:T(8,128)(2,1)S(1)}, u32[]{:S(2)}, u32[]{:S(2)}) collective-permute-start(bf16[2,208,256]{2,1,0:T(8,128)(2,1)S(1)} %get-tuple-element.53), channel_id=1, source_target_pairs={{0,1},{1,0},{2,3},{3,2},{4,5},{5,4},{6,7},{7,6},{8,9},{9,8},{10,11... | collective-permute-start | bytes 638984 | tf_op jit(solution)/shard_map/ppermute | solution.py:399
  23.3 2.6 %collective-permute-start.10 = (bf16[2,208,256]{2,1,0:T(8,128)(2,1)S(1)}, bf16[2,208,256]{2,1,0:T(8,128)(2,1)S(1)}, u32[]{:S(2)}, u32[]{:S(2)}) collective-permute-start(bf16[2,208,256]{2,1,0:T(8,128)(2,1)S(1)} %get-tuple-element.54), channel_id=1, source_target_pairs={{0,1},{1,0},{2,3},{3,2},{4,5},{5,4},{6,7},{7,6},{8,9},{9,8},{10,11... | collective-permute-start | bytes 638984 | tf_op jit(solution)/shard_map/ppermute | solution.py:399
  24.3 1.6 %collective-permute-start.11 = (bf16[2,208,256]{2,1,0:T(8,128)(2,1)S(1)}, bf16[2,208,256]{2,1,0:T(8,128)(2,1)S(1)}, u32[]{:S(2)}, u32[]{:S(2)}) collective-permute-start(bf16[2,208,256]{2,1,0:T(8,128)(2,1)S(1)} %get-tuple-element.55), channel_id=1, source_target_pairs={{0,1},{1,0},{2,3},{3,2},{4,5},{5,4},{6,7},{7,6},{8,9},{9,8},{10,11... | collective-permute-start | bytes 638984 | tf_op jit(solution)/shard_map/ppermute | solution.py:399
  25.8 2.4 %collective-permute-start.7 = (bf16[4,2,64,256]{3,2,1,0:T(8,128)(2,1)S(1)}, bf16[4,2,64,256]{3,2,1,0:T(8,128)(2,1)S(1)}, u32[]{:S(2)}, u32[]{:S(2)}) collective-permute-start(bf16[4,2,64,256]{3,2,1,0:T(8,128)(2,1)S(1)} %shard_map.73), channel_id=1, source_target_pairs={{0,1},{1,0},{2,3},{3,2},{4,5},{5,4},{6,7},{7,6},{8,9},{9,8},{10,11... | collective-permute-start | bytes 786440 | tf_op jit(solution)/shard_map/ppermute | solution.py:399
  26.7 12.7 %collective-permute-start.19 = (bf16[8,208,128]{2,1,0:T(8,128)(2,1)S(1)}, bf16[8,208,128]{2,1,0:T(8,128)(2,1)S(1)}, u32[]{:S(2)}, u32[]{:S(2)}) collective-permute-start(bf16[8,208,128]{2,1,0:T(8,128)(2,1)S(1)} %get-tuple-element.67), channel_id=1, source_target_pairs={{0,16},{16,0},{1,17},{17,1},{2,18},{18,2},{3,19},{19,3},{4,20},{20... | collective-permute-start | bytes 1277960 | tf_op jit(solution)/shard_map/ppermute | solution.py:401
  29.7 1.5 %collective-permute-start.12 = (bf16[2,208,256]{2,1,0:T(8,128)(2,1)S(1)}, bf16[2,208,256]{2,1,0:T(8,128)(2,1)S(1)}, u32[]{:S(2)}, u32[]{:S(2)}) collective-permute-start(bf16[2,208,256]{2,1,0:T(8,128)(2,1)S(1)} %get-tuple-element.59), channel_id=1, source_target_pairs={{0,1},{1,0},{2,3},{3,2},{4,5},{5,4},{6,7},{7,6},{8,9},{9,8},{10,11... | collective-permute-start | bytes 638984 | tf_op jit(solution)/shard_map/ppermute | solution.py:399
  30.0 1.6 %collective-permute-start.13 = (bf16[2,208,256]{2,1,0:T(8,128)(2,1)S(1)}, bf16[2,208,256]{2,1,0:T(8,128)(2,1)S(1)}, u32[]{:S(2)}, u32[]{:S(2)}) collective-permute-start(bf16[2,208,256]{2,1,0:T(8,128)(2,1)S(1)} %get-tuple-element.60), channel_id=1, source_target_pairs={{0,1},{1,0},{2,3},{3,2},{4,5},{5,4},{6,7},{7,6},{8,9},{9,8},{10,11... | collective-permute-start | bytes 638984 | tf_op jit(solution)/shard_map/ppermute | solution.py:399
  30.3 1.6 %collective-permute-start.14 = (bf16[2,208,256]{2,1,0:T(8,128)(2,1)S(1)}, bf16[2,208,256]{2,1,0:T(8,128)(2,1)S(1)}, u32[]{:S(2)}, u32[]{:S(2)}) collective-permute-start(bf16[2,208,256]{2,1,0:T(8,128)(2,1)S(1)} %get-tuple-element.61), channel_id=1, source_target_pairs={{0,1},{1,0},{2,3},{3,2},{4,5},{5,4},{6,7},{7,6},{8,9},{9,8},{10,11... | collective-permute-start | bytes 638984 | tf_op jit(solution)/shard_map/ppermute | solution.py:399
  30.5 1.7 %collective-permute-start.15 = (bf16[2,208,256]{2,1,0:T(8,128)(2,1)S(1)}, bf16[2,208,256]{2,1,0:T(8,128)(2,1)S(1)}, u32[]{:S(2)}, u32[]{:S(2)}) collective-permute-start(bf16[2,208,256]{2,1,0:T(8,128)(2,1)S(1)} %get-tuple-element.62), channel_id=1, source_target_pairs={{0,1},{1,0},{2,3},{3,2},{4,5},{5,4},{6,7},{7,6},{8,9},{9,8},{10,11... | collective-permute-start | bytes 638984 | tf_op jit(solution)/shard_map/ppermute | solution.py:399
  32.9 11.9 %collective-permute-start.16 = (bf16[4,208,128]{2,1,0:T(8,128)(2,1)S(1)}, bf16[4,208,128]{2,1,0:T(8,128)(2,1)S(1)}, u32[]{:S(2)}, u32[]{:S(2)}) collective-permute-start(bf16[4,208,128]{2,1,0:T(8,128)(2,1)S(1)} %get-tuple-element.64), channel_id=1, source_target_pairs={{0,18},{1,19},{2,16},{3,17},{4,22},{5,23},{6,20},{7,21},{8,26},{9,... | collective-permute-start | bytes 638984 | tf_op jit(solution)/shard_map/ppermute | solution.py:403
  34.5 13.6 %collective-permute-start.17 = (bf16[4,208,128]{2,1,0:T(8,128)(2,1)S(1)}, bf16[4,208,128]{2,1,0:T(8,128)(2,1)S(1)}, u32[]{:S(2)}, u32[]{:S(2)}) collective-permute-start(bf16[4,208,128]{2,1,0:T(8,128)(2,1)S(1)} %get-tuple-element.65), channel_id=1, source_target_pairs={{0,16},{16,0},{1,17},{17,1},{2,18},{18,2},{3,19},{19,3},{4,20},{20... | collective-permute-start | bytes 638984 | tf_op jit(solution)/shard_map/ppermute | solution.py:401
  35.8 12.3 %collective-permute-start.18 = (bf16[4,208,128]{2,1,0:T(8,128)(2,1)S(1)}, bf16[4,208,128]{2,1,0:T(8,128)(2,1)S(1)}, u32[]{:S(2)}, u32[]{:S(2)}) collective-permute-start(bf16[4,208,128]{2,1,0:T(8,128)(2,1)S(1)} %get-tuple-element.66), channel_id=1, source_target_pairs={{0,2},{1,3},{2,0},{3,1},{4,6},{5,7},{6,4},{7,5},{8,10},{9,11},{10,... | collective-permute-start | bytes 638984 | tf_op jit(solution)/shard_map/ppermute | solution.py:399
  39.4 23.2 %copy-start.3 = (bf16[2,1024,256]{2,1,0:T(8,128)(2,1)S(1)}, bf16[2,1024,256]{2,1,0:T(8,128)(2,1)}, u32[]{:S(2)}) copy-start(bf16[2,1024,256]{2,1,0:T(8,128)(2,1)} %refs_1_.1) | copy-start | bytes 3145732
  40.0 8.1 %collective-permute-start.20 = (bf16[4,208,128]{2,1,0:T(8,128)(2,1)S(1)}, bf16[4,208,128]{2,1,0:T(8,128)(2,1)S(1)}, u32[]{:S(2)}, u32[]{:S(2)}) collective-permute-start(bf16[4,208,128]{2,1,0:T(8,128)(2,1)S(1)} %get-tuple-element.69), channel_id=1, source_target_pairs={{0,4},{1,5},{2,6},{3,7},{4,0},{5,1},{6,2},{7,3},{8,12},{9,13},{10,... | collective-permute-start | bytes 638984 | tf_op jit(solution)/shard_map/ppermute | solution.py:399
  48.8 5.9 %collective-permute-start.21 = (bf16[2,208,128]{2,1,0:T(8,128)(2,1)S(1)}, bf16[2,208,128]{2,1,0:T(8,128)(2,1)S(1)}, u32[]{:S(2)}, u32[]{:S(2)}) collective-permute-start(bf16[2,208,128]{2,1,0:T(8,128)(2,1)S(1)} %get-tuple-element.71), channel_id=1, source_target_pairs={{0,2},{1,3},{2,0},{3,1},{4,6},{5,7},{6,4},{7,5},{8,10},{9,11},{10,... | collective-permute-start | bytes 319496 | tf_op jit(solution)/shard_map/ppermute | solution.py:399
  50.3 6.0 %collective-permute-start.23 = (bf16[1,208,128]{2,1,0:T(8,128)(2,1)S(1)}, bf16[1,208,128]{2,1,0:T(8,128)(2,1)S(1)}, u32[]{:S(2)}, u32[]{:S(2)}) collective-permute-start(bf16[1,208,128]{2,1,0:T(8,128)(2,1)S(1)} %get-tuple-element.75), channel_id=1, source_target_pairs={{0,12},{1,13},{2,14},{3,15},{4,8},{5,9},{6,10},{7,11},{8,4},{9,5},... | collective-permute-start | bytes 159752 | tf_op jit(solution)/shard_map/ppermute | solution.py:399
  52.7 6.1 %collective-permute-start.24 = (bf16[1,208,128]{2,1,0:T(8,128)(2,1)S(1)}, bf16[1,208,128]{2,1,0:T(8,128)(2,1)S(1)}, u32[]{:S(2)}, u32[]{:S(2)}) collective-permute-start(bf16[1,208,128]{2,1,0:T(8,128)(2,1)S(1)} %get-tuple-element.76), channel_id=1, source_target_pairs={{0,8},{1,9},{2,10},{3,11},{4,12},{5,13},{6,14},{7,15},{8,0},{9,1},... | collective-permute-start | bytes 159752 | tf_op jit(solution)/shard_map/ppermute | solution.py:399
  52.7 6.1 %collective-permute-start.25 = (bf16[1,208,128]{2,1,0:T(8,128)(2,1)S(1)}, bf16[1,208,128]{2,1,0:T(8,128)(2,1)S(1)}, u32[]{:S(2)}, u32[]{:S(2)}) collective-permute-start(bf16[1,208,128]{2,1,0:T(8,128)(2,1)S(1)} %get-tuple-element.77), channel_id=1, source_target_pairs={{0,4},{1,5},{2,6},{3,7},{4,0},{5,1},{6,2},{7,3},{8,12},{9,13},{10,... | collective-permute-start | bytes 159752 | tf_op jit(solution)/shard_map/ppermute | solution.py:399
  55.2 5.2 %collective-permute-start.22 = (bf16[1,208,128]{2,1,0:T(8,128)(2,1)S(1)}, bf16[1,208,128]{2,1,0:T(8,128)(2,1)S(1)}, u32[]{:S(2)}, u32[]{:S(2)}) collective-permute-start(bf16[1,208,128]{2,1,0:T(8,128)(2,1)S(1)} %get-tuple-element.74), channel_id=1, source_target_pairs={{0,8},{1,9},{2,10},{3,11},{4,12},{5,13},{6,14},{7,15},{8,0},{9,1},... | collective-permute-start | bytes 159752 | tf_op jit(solution)/shard_map/ppermute | solution.py:399
  61.0 4.2 %collective-permute-start.26 = (bf16[208,128]{1,0:T(8,128)(2,1)S(1)}, bf16[208,128]{1,0:T(8,128)(2,1)S(1)}, u32[]{:S(2)}, u32[]{:S(2)}) collective-permute-start(bf16[208,128]{1,0:T(8,128)(2,1)S(1)} %get-tuple-element.79), channel_id=1, source_target_pairs={{0,16},{16,0},{1,17},{17,1},{2,18},{18,2},{3,19},{19,3},{4,20},{20... | collective-permute-start | bytes 159752 | tf_op jit(solution)/shard_map/ppermute | solution.py:401

commit v16 on v15

--- a/solution.py
+++ b/solution.py
@@ -325,7 +325,7 @@
         for b in range(bits):
             mine = mine + flags[BITS + at + b] * (1 << b)
         last = span * (2 if by_columns else 1)
-        for n in [0] + list(range(last - 1, 0, -1)):
+        for n in [0] + (list(range(last - 1, 0, -1)) if by_columns else list(range(1, last))):
             across, apart = n // span, n % span
             pieces = outs[: len(heights) if n else 1]
             del outs[: len(pieces)]
@@ -441,7 +441,8 @@
     for _, at, bits, by_columns, heights in plans:
         span = 1 << bits
         parts = [[pieces.pop(0)]]
-        for n in range(span * (2 if by_columns else 1) - 1, 0, -1):
+        order = range(2 * span - 1, 0, -1) if by_columns else range(1, span)
+        for n in order:
             parts.append([xor_move(pieces.pop(0), (n % span) << at, n >= span) for _ in heights])
         sums.append(parts)
     return sums, token

time: 66.6 us -> 67 us (level)
  transfers between devices with their start and end apart: 27 -> 27, of which waited for: 14 -> 15; matrix products, arithmetic and copies ran while one was open for 0% -> 0% of each run, Pallas kernels for 19% -> 19%
where the time goes in v16:
time: 67 us; the launch traced here: 66.8 us
  starting transfers between devices  26.6 us (40%)
  waiting for transfers between devices  20.2 us (30%)
  Pallas kernels  16.6 us (25%)
  local copies, waits for them, and re-layouts  1.34 us (2%)
  other arithmetic  1.19 us (2%)
  between operations  0.88 us (1%)
    pallas_call x16, Pallas kernels, vmem_call(): pl.pallas_call(run, out_shape=out_shape, in_specs=specs, out_specs=jax.tr...  16.6 us
    ppermute x19, starting transfers between devices, xor_move(): return lax.ppermute(block, 'tile', [(t, t ^ apart) for t in range(tiles)])  13.8 us
    ppermute x19, waiting for transfers between devices, xor_move(): return lax.ppermute(block, 'tile', [(t, t ^ apart) for t in range(tiles)])  8.57 us
    ppermute x3, waiting for transfers between devices, xor_move(): return lax.ppermute(block, 'dp', [(0, 1), (1, 0)])  6.78 us
    ppermute x4, starting transfers between devices, swap(): return lax.ppermute(block, 'tile', tile_route(row_pairs, col_pairs, rows))  6.71 us
    ppermute x3, starting transfers between devices, xor_move(): return lax.ppermute(block, 'dp', [(0, 1), (1, 0)])  4.47 us
    ppermute x1, waiting for transfers between devices, xor_move(): return lax.ppermute(block, ('dp', 'tile'), route)  3.57 us
    ppermute x1, starting transfers between devices, xor_move(): return lax.ppermute(block, ('dp', 'tile'), route)  1.58 us
  transfers between devices with their start and end apart: 27, of which 15 were waited for; matrix products, arithmetic and copies ran while one was open for 0% of the time, Pallas kernels for 19%

profile of v16, /device:TPU:0, one launch (start us, length us, event | category | flops | bytes accessed | tf_op | source)
XLA Modules:
  0.0 66.8 jit_solution(2645324170886567007)
XLA Ops:
  0.7 1.2 %broadcast_select_fusion = (bf16[4,16,4,256]{3,2,1,0:T(4,128)(2,1)S(1)}, bf16[4,16,4,256]{3,2,1,0:T(4,128)(2,1)S(1)}) fusion(pred[]{:T(512)S(6)} %eq.27, bf16[4,16,32,256]{3,2,1,0:T(8,128)(2,1)} %refs_0_.1), kind=kLoop, calls=%fused_computation | loop fusion | flops 131072 | bytes 524289 | tf_op jit(solution)/shard_map/jit(_where)/select_n | solution.py:477
  1.9 3.1 %collective-permute-start.2 = (bf16[4,16,4,256]{3,2,1,0:T(4,128)(2,1)S(1)}, bf16[4,16,4,256]{3,2,1,0:T(4,128)(2,1)S(1)}, u32[]{:S(2)}, u32[]{:S(2)}) collective-permute-start(bf16[4,16,4,256]{3,2,1,0:T(4,128)(2,1)S(1)} %get-tuple-element.80), channel_id=1, source_target_pairs={{1,3},{3,1},{2,6},{6,2},{7,5},{5,7},{0,4},{4,0},{9,11},{11,9},{10,... | collective-permute-start | bytes 393224 | tf_op jit(solution)/shard_map/ppermute | solution.py:473
  4.9 0.0 collective-permute-start.1
  4.9 1.2 %copy-done.2 = bf16[4,16,32,256]{3,2,1,0:T(8,128)(2,1)S(1)} copy-done((bf16[4,16,32,256]{3,2,1,0:T(8,128)(2,1)S(1)}, bf16[4,16,32,256]{3,2,1,0:T(8,128)(2,1)}, u32[]{:S(2)}) %copy-start.2) | copy-done | bytes 1048600
  6.2 0.5 shard_map.68.refs_1_
  6.7 0.1 stack.71.refs_0_
  6.8 0.0 copy-start
  6.8 0.6 shard_map.69
  7.4 2.7 %collective-permute-start = (bf16[128,256]{1,0:T(8,128)(2,1)S(1)}, bf16[128,256]{1,0:T(8,128)(2,1)S(1)}, u32[]{:S(2)}, u32[]{:S(2)}) collective-permute-start(bf16[128,256]{1,0:T(8,128)(2,1)S(1)} %shard_map.69), channel_id=1, source_target_pairs={{0,8},{1,9},{3,11},{2,10},{6,14},{7,15},{5,13},{4,12},{8,0},{9,1},... | collective-permute-start | bytes 196616 | tf_op jit(solution)/shard_map/ppermute | solution.py:473
  10.0 0.0 collective-permute-done.2.refs_3_
  10.0 0.0 collective-permute-done.1.refs_2_
  10.0 0.7 %shard_map.70.refs_5_ = bf16[32,256]{1,0:T(8,128)(2,1)S(1)} custom-call(s32[13]{0:T(128)S(1)} %stack.71.refs_0_, f32[4,16,24,256]{3,2,1,0:T(8,128)S(1)} %shard_map.68.refs_1_, bf16[4,16,4,256]{3,2,1,0:T(4,128)(2,1)S(1)} %collective-permute-done.1.refs_2_, bf16[4,16,4,256]{3,2,1,0:T(4,128)(2,1)S(1)} %collective-permute-done.2.refs_3_), custom_call_target="tpu_custom_call" | custom-call | bytes 1851444 | tf_op jit(solution)/shard_map/pallas_call | solution.py:380
  10.7 1.0 %collective-permute-start.3 = (bf16[32,256]{1,0:T(8,128)(2,1)S(1)}, bf16[32,256]{1,0:T(8,128)(2,1)S(1)}, u32[]{:S(2)}, u32[]{:S(2)}) collective-permute-start(bf16[32,256]{1,0:T(8,128)(2,1)S(1)} %shard_map.70.refs_5_), channel_id=1, source_target_pairs={{0,8},{1,9},{3,11},{2,10},{6,14},{7,15},{5,13},{4,12},{8,0},{9,1},... | collective-permute-start | bytes 49160 | tf_op jit(solution)/shard_map/ppermute | solution.py:473
  11.7 2.4 %shard_map.71 = (bf16[3,640,256]{2,1,0:T(8,128)(2,1)S(1)}, f32[2,512,256]{2,1,0:T(8,128)S(1)}, f32[4,6,16,256]{3,2,1,0:T(8,128)S(1)}, f32[4,6,2,256]{3,2,1,0:T(2,128)S(1)}) custom-call(s32[13]{0:T(128)S(1)} %stack.71.refs_0_, f32[4,16,24,256]{3,2,1,0:T(8,128)S(1)} %shard_map.68.refs_1_, bf16[4,16,4,256]{3,2,1,0:T(4,128)(2,1)S(1)} %collective-permute-done.1.refs_2_, ...), custom_call_target="tpu_custom_call" | custom-call | flops 1207959552 | bytes 6668340 | tf_op jit(solution)/shard_map/pallas_call | solution.py:380
  14.2 0.1 collective-permute-done.refs_1_
  14.2 1.2 %collective-permute-done.3.refs_2_ = bf16[32,256]{1,0:T(8,128)(2,1)S(1)} collective-permute-done((bf16[32,256]{1,0:T(8,128)(2,1)S(1)}, bf16[32,256]{1,0:T(8,128)(2,1)S(1)}, u32[]{:S(2)}, u32[]{:S(2)}) %collective-permute-start.3) | collective-permute-done | bytes 16416 | tf_op jit(solution)/shard_map/ppermute | solution.py:473
  15.4 1.6 %shard_map.72 = (bf16[2,2,64,256]{3,2,1,0:T(8,128)(2,1)S(1)}, bf16[2,2,64,256]{3,2,1,0:T(8,128)(2,1)S(1)}, bf16[2,2,64,256]{3,2,1,0:T(8,128)(2,1)S(1)}, bf16[2,2...) custom-call(s32[13]{0:T(128)S(1)} %stack.71.refs_0_, ...), custom_call_target="tpu_custom_call", output_to_operand_aliasing={{4}: (5, {})} | custom-call | flops 301989888 | bytes 6422580 | tf_op jit(solution)/shard_map/pallas_call | solution.py:380
  17.1 1.6 %collective-permute-start.4 = (bf16[2,2,64,256]{3,2,1,0:T(8,128)(2,1)S(1)}, bf16[2,2,64,256]{3,2,1,0:T(8,128)(2,1)S(1)}, u32[]{:S(2)}, u32[]{:S(2)}) collective-permute-start(bf16[2,2,64,256]{3,2,1,0:T(8,128)(2,1)S(1)} %get-tuple-element.46), channel_id=1, source_target_pairs={{0,2},{1,3},{2,0},{3,1},{4,6},{5,7},{6,4},{7,5},{8,10},{9,11},{10,... | collective-permute-start | bytes 393224 | tf_op jit(solution)/shard_map/ppermute | solution.py:399
  18.7 0.4 collective-permute-start.5
  19.1 1.5 %collective-permute-start.6 = (bf16[2,2,64,256]{3,2,1,0:T(8,128)(2,1)S(1)}, bf16[2,2,64,256]{3,2,1,0:T(8,128)(2,1)S(1)}, u32[]{:S(2)}, u32[]{:S(2)}) collective-permute-start(bf16[2,2,64,256]{3,2,1,0:T(8,128)(2,1)S(1)} %get-tuple-element.48), channel_id=1, source_target_pairs={{0,6},{1,7},{2,4},{3,5},{4,2},{5,3},{6,0},{7,1},{8,14},{9,15},{10,... | collective-permute-start | bytes 393224 | tf_op jit(solution)/shard_map/ppermute | solution.py:399
  20.6 2.1 %shard_map.74 = (bf16[8,208,256]{2,1,0:T(8,128)(2,1)S(1)}, bf16[2,208,256]{2,1,0:T(8,128)(2,1)S(1)}, bf16[2,208,256]{2,1,0:T(8,128)(2,1)S(1)}, bf16[2,208,256]{2...) custom-call(s32[13]{0:T(128)S(1)} %stack.71.refs_0_, ...), custom_call_target="tpu_custom_call" | custom-call | flops 1207959552 | bytes 3866676 | tf_op jit(solution)/shard_map/pallas_call | solution.py:380
  22.7 0.0 copy-start.1
  22.7 0.1 collective-permute-start.8
  22.8 0.5 collective-permute-start.9
  23.3 0.0 collective-permute-done.4.refs_1_.refs_2_
  23.3 0.1 collective-permute-start.10
  23.4 0.9 %collective-permute-done.5.refs_2_.refs_3_ = bf16[2,2,64,256]{3,2,1,0:T(8,128)(2,1)S(1)} collective-permute-done((bf16[2,2,64,256]{3,2,1,0:T(8,128)(2,1)S(1)}, bf16[2,2,64,256]{3,2,1,0:T(8,128)(2,1)S(1)}, u32[]{:S(2)}, u32[]{:S(2)}) %collective-permute-start.5) | collective-permute-done | bytes 131104 | tf_op jit(solution)/shard_map/ppermute | solution.py:399
  24.3 1.5 %collective-permute-done.6.refs_3_.refs_4_ = bf16[2,2,64,256]{3,2,1,0:T(8,128)(2,1)S(1)} collective-permute-done((bf16[2,2,64,256]{3,2,1,0:T(8,128)(2,1)S(1)}, bf16[2,2,64,256]{3,2,1,0:T(8,128)(2,1)S(1)}, u32[]{:S(2)}, u32[]{:S(2)}) %collective-permute-start.6) | collective-permute-done | bytes 131104 | tf_op jit(solution)/shard_map/ppermute | solution.py:399
  25.8 0.1 collective-permute-start.7
  25.9 0.7 %shard_map.75 = (f32[8,208,128]{2,1,0:T(8,128)S(1)}, bf16[8,208,128]{2,1,0:T(8,128)(2,1)S(1)}) custom-call(s32[13]{0:T(128)S(1)} %stack.71.refs_0_, bf16[8,208,256]{2,1,0:T(8,128)(2,1)S(1)} %get-tuple-element.51.refs_1_, bf16[2,208,256]{2,1,0:T(8,128)(2,1)S(1)} %collective-permute-done.8.refs_2_, bf16[2,208,256]{2,1,0:T(8,128)(2,1)S(1)} %collective-permute-done.9.refs_3_, ...), custom_call_target="tpu_custom_call" | custom-call | bytes 2981940 | tf_op jit(solution)/shard_map/pallas_call | solution.py:380
  26.7 1.6 %collective-permute-start.19 = (bf16[8,208,128]{2,1,0:T(8,128)(2,1)S(1)}, bf16[8,208,128]{2,1,0:T(8,128)(2,1)S(1)}, u32[]{:S(2)}, u32[]{:S(2)}) collective-permute-start(bf16[8,208,128]{2,1,0:T(8,128)(2,1)S(1)} %get-tuple-element.67), channel_id=1, source_target_pairs={{0,16},{16,0},{1,17},{17,1},{2,18},{18,2},{3,19},{19,3},{4,20},{20... | collective-permute-start | bytes 1277960 | tf_op jit(solution)/shard_map/ppermute | solution.py:401
  28.2 1.5 %shard_map.76 = (bf16[8,208,256]{2,1,0:T(8,128)(2,1)S(1)}, bf16[2,208,256]{2,1,0:T(8,128)(2,1)S(1)}, bf16[2,208,256]{2,1,0:T(8,128)(2,1)S(1)}, bf16[2,208,256]{2...) custom-call(s32[13]{0:T(128)S(1)} %stack.71.refs_0_, ...), custom_call_target="tpu_custom_call" | custom-call | flops 536870912 | bytes 5767220 | tf_op jit(solution)/shard_map/pallas_call | solution.py:380
  29.7 0.3 collective-permute-start.12
  30.0 0.3 collective-permute-start.13
  30.3 0.2 collective-permute-start.14
  30.5 0.3 collective-permute-start.15
  30.8 0.4 collective-permute-done.12.refs_2_
  31.2 0.3 collective-permute-done.13.refs_3_
  31.5 0.3 collective-permute-done.14.refs_4_
  31.9 0.3 collective-permute-done.15.refs_5_
  32.2 0.7 %shard_map.77 = (f32[4,208,128]{2,1,0:T(8,128)S(1)}, bf16[4,208,128]{2,1,0:T(8,128)(2,1)S(1)}, bf16[4,208,128]{2,1,0:T(8,128)(2,1)S(1)}, bf16[4,208,128]{2,1,0:T(8,128)(2,1)S(1)}) custom-call(s32[13]{0:T(128)S(1)} %stack.71.refs_0_, bf16[8,208,256]{2,1,0:T(8,128)(2,1)S(1)} %get-tuple-element.58.refs_1_, ...), custom_call_target="tpu_custom_call" | custom-call | bytes 2768948 | tf_op jit(solution)/shard_map/pallas_call | solution.py:380
  32.9 1.6 %collective-permute-start.16 = (bf16[4,208,128]{2,1,0:T(8,128)(2,1)S(1)}, bf16[4,208,128]{2,1,0:T(8,128)(2,1)S(1)}, u32[]{:S(2)}, u32[]{:S(2)}) collective-permute-start(bf16[4,208,128]{2,1,0:T(8,128)(2,1)S(1)} %get-tuple-element.64), channel_id=1, source_target_pairs={{0,18},{1,19},{2,16},{3,17},{4,22},{5,23},{6,20},{7,21},{8,26},{9,... | collective-permute-start | bytes 638984 | tf_op jit(solution)/shard_map/ppermute | solution.py:403
  34.5 1.4 %collective-permute-start.17 = (bf16[4,208,128]{2,1,0:T(8,128)(2,1)S(1)}, bf16[4,208,128]{2,1,0:T(8,128)(2,1)S(1)}, u32[]{:S(2)}, u32[]{:S(2)}) collective-permute-start(bf16[4,208,128]{2,1,0:T(8,128)(2,1)S(1)} %get-tuple-element.65), channel_id=1, source_target_pairs={{0,16},{16,0},{1,17},{17,1},{2,18},{18,2},{3,19},{19,3},{4,20},{20... | collective-permute-start | bytes 638984 | tf_op jit(solution)/shard_map/ppermute | solution.py:401
  35.8 0.6 collective-permute-start.18
  36.5 2.9 %collective-permute-done.19.refs_2_ = bf16[8,208,128]{2,1,0:T(8,128)(2,1)S(1)} collective-permute-done((bf16[8,208,128]{2,1,0:T(8,128)(2,1)S(1)}, bf16[8,208,128]{2,1,0:T(8,128)(2,1)S(1)}, u32[]{:S(2)}, u32[]{:S(2)}) %collective-permute-start.19) | collective-permute-done | bytes 426016 | tf_op jit(solution)/shard_map/ppermute | solution.py:401
  39.4 0.6 shard_map.78
  40.0 1.2 %collective-permute-start.20 = (bf16[4,208,128]{2,1,0:T(8,128)(2,1)S(1)}, bf16[4,208,128]{2,1,0:T(8,128)(2,1)S(1)}, u32[]{:S(2)}, u32[]{:S(2)}) collective-permute-start(bf16[4,208,128]{2,1,0:T(8,128)(2,1)S(1)} %get-tuple-element.69), channel_id=1, source_target_pairs={{0,4},{1,5},{2,6},{3,7},{4,0},{5,1},{6,2},{7,3},{8,12},{9,13},{10,... | collective-permute-start | bytes 638984 | tf_op jit(solution)/shard_map/ppermute | solution.py:399
  41.2 3.6 %collective-permute-done.16.refs_2_ = bf16[4,208,128]{2,1,0:T(8,128)(2,1)S(1)} collective-permute-done((bf16[4,208,128]{2,1,0:T(8,128)(2,1)S(1)}, bf16[4,208,128]{2,1,0:T(8,128)(2,1)S(1)}, u32[]{:S(2)}, u32[]{:S(2)}) %collective-permute-start.16) | collective-permute-done | bytes 213024 | tf_op jit(solution)/shard_map/ppermute | solution.py:403
  44.8 3.3 %collective-permute-done.17.refs_3_ = bf16[4,208,128]{2,1,0:T(8,128)(2,1)S(1)} collective-permute-done((bf16[4,208,128]{2,1,0:T(8,128)(2,1)S(1)}, bf16[4,208,128]{2,1,0:T(8,128)(2,1)S(1)}, u32[]{:S(2)}, u32[]{:S(2)}) %collective-permute-start.17) | collective-permute-done | bytes 213024 | tf_op jit(solution)/shard_map/ppermute | solution.py:401
  48.1 0.7 %shard_map.79 = (f32[1,208,128]{2,1,0:T(8,128)S(1)}, bf16[1,208,128]{2,1,0:T(8,128)(2,1)S(1)}, bf16[1,208,128]{2,1,0:T(8,128)(2,1)S(1)}, bf16[1,208,128]{2,1,0:T...) custom-call(s32[13]{0:T(128)S(1)} %stack.71.refs_0_, ...), custom_call_target="tpu_custom_call" | custom-call | bytes 2289716 | tf_op jit(solution)/shard_map/pallas_call | solution.py:380
  48.8 1.5 %collective-permute-start.21 = (bf16[2,208,128]{2,1,0:T(8,128)(2,1)S(1)}, bf16[2,208,128]{2,1,0:T(8,128)(2,1)S(1)}, u32[]{:S(2)}, u32[]{:S(2)}) collective-permute-start(bf16[2,208,128]{2,1,0:T(8,128)(2,1)S(1)} %get-tuple-element.71), channel_id=1, source_target_pairs={{0,2},{1,3},{2,0},{3,1},{4,6},{5,7},{6,4},{7,5},{8,10},{9,11},{10,... | collective-permute-start | bytes 319496 | tf_op jit(solution)/shard_map/ppermute | solution.py:399
  50.3 0.4 collective-permute-start.23
  50.7 2.6 %collective-permute-start.24 = (bf16[1,208,128]{2,1,0:T(8,128)(2,1)S(1)}, bf16[1,208,128]{2,1,0:T(8,128)(2,1)S(1)}, u32[]{:S(2)}, u32[]{:S(2)}) collective-permute-start(bf16[1,208,128]{2,1,0:T(8,128)(2,1)S(1)} %get-tuple-element.76), channel_id=1, source_target_pairs={{0,8},{1,9},{2,10},{3,11},{4,12},{5,13},{6,14},{7,15},{8,0},{9,1},... | collective-permute-start | bytes 159752 | tf_op jit(solution)/shard_map/ppermute | solution.py:399
  53.3 1.4 %collective-permute-start.25 = (bf16[1,208,128]{2,1,0:T(8,128)(2,1)S(1)}, bf16[1,208,128]{2,1,0:T(8,128)(2,1)S(1)}, u32[]{:S(2)}, u32[]{:S(2)}) collective-permute-start(bf16[1,208,128]{2,1,0:T(8,128)(2,1)S(1)} %get-tuple-element.77), channel_id=1, source_target_pairs={{0,12},{1,13},{2,14},{3,15},{4,8},{5,9},{6,10},{7,11},{8,4},{9,5},... | collective-permute-start | bytes 159752 | tf_op jit(solution)/shard_map/ppermute | solution.py:399
  54.7 0.6 shard_map.80
  55.2 0.7 %collective-permute-start.22 = (bf16[1,208,128]{2,1,0:T(8,128)(2,1)S(1)}, bf16[1,208,128]{2,1,0:T(8,128)(2,1)S(1)}, u32[]{:S(2)}, u32[]{:S(2)}) collective-permute-start(bf16[1,208,128]{2,1,0:T(8,128)(2,1)S(1)} %get-tuple-element.74), channel_id=1, source_target_pairs={{0,8},{1,9},{2,10},{3,11},{4,12},{5,13},{6,14},{7,15},{8,0},{9,1},... | collective-permute-start | bytes 159752 | tf_op jit(solution)/shard_map/ppermute | solution.py:399
  56.0 0.1 collective-permute-done.24.refs_5_
  56.1 3.2 %collective-permute-done.25.refs_6_ = bf16[1,208,128]{2,1,0:T(8,128)(2,1)S(1)} collective-permute-done((bf16[1,208,128]{2,1,0:T(8,128)(2,1)S(1)}, bf16[1,208,128]{2,1,0:T(8,128)(2,1)S(1)}, u32[]{:S(2)}, u32[]{:S(2)}) %collective-permute-start.25) | collective-permute-done | bytes 53280 | tf_op jit(solution)/shard_map/ppermute | solution.py:399
  59.3 1.4 %collective-permute-done.22.refs_2_ = bf16[1,208,128]{2,1,0:T(8,128)(2,1)S(1)} collective-permute-done((bf16[1,208,128]{2,1,0:T(8,128)(2,1)S(1)}, bf16[1,208,128]{2,1,0:T(8,128)(2,1)S(1)}, u32[]{:S(2)}, u32[]{:S(2)}) %collective-permute-start.22) | collective-permute-done | bytes 53280 | tf_op jit(solution)/shard_map/ppermute | solution.py:399
  60.8 0.6 shard_map.82
  61.4 1.6 %collective-permute-start.26 = (bf16[208,128]{1,0:T(8,128)(2,1)S(1)}, bf16[208,128]{1,0:T(8,128)(2,1)S(1)}, u32[]{:S(2)}, u32[]{:S(2)}) collective-permute-start(bf16[208,128]{1,0:T(8,128)(2,1)S(1)} %get-tuple-element.79), channel_id=1, source_target_pairs={{0,16},{16,0},{1,17},{17,1},{2,18},{18,2},{3,19},{19,3},{4,20},{20... | collective-permute-start | bytes 159752 | tf_op jit(solution)/shard_map/ppermute | solution.py:401
  62.9 2.1 %shard_map.81 = bf16[4,2,128,1024]{3,2,1,0:T(8,128)(2,1)} custom-call(bf16[2,512,256]{2,1,0:T(8,128)(2,1)S(1)} %get-tuple-element.57.refs_6_.refs_0_, bf16[2,1024,256]{2,1,0:T(8,128)(2,1)S(1)} %copy-done.3, f32[1,208,128]{2,1,0:T(8,128)S(1)} %get-tuple-element.73.refs_2_.refs_1_), custom_call_target="tpu_custom_call" | custom-call | flops 536870912 | bytes 3670016 | tf_op jit(solution)/shard_map/pallas_call | solution.py:380
  65.0 0.6 collective-permute-done.26.refs_2_
  65.6 1.2 %shard_map.83 = f32[208,256]{1,0:T(8,128)} custom-call(s32[13]{0:T(128)S(1)} %stack.71.refs_0_, f32[208,128]{1,0:T(8,128)S(1)} %get-tuple-element.78.refs_1_, bf16[208,128]{1,0:T(8,128)(2,1)S(1)} %collective-permute-done.26.refs_2_), custom_call_target="tpu_custom_call" | custom-call | bytes 372788 | tf_op jit(solution)/shard_map/pallas_call | solution.py:380
  (18 shorter events, 0.1 us)
Async XLA Ops:
  1.9 8.2 %collective-permute-start.2 = (bf16[4,16,4,256]{3,2,1,0:T(4,128)(2,1)S(1)}, bf16[4,16,4,256]{3,2,1,0:T(4,128)(2,1)S(1)}, u32[]{:S(2)}, u32[]{:S(2)}) collective-permute-start(bf16[4,16,4,256]{3,2,1,0:T(4,128)(2,1)S(1)} %get-tuple-element.80), channel_id=1, source_target_pairs={{1,3},{3,1},{2,6},{6,2},{7,5},{5,7},{0,4},{4,0},{9,11},{11,9},{10,... | collective-permute-start | bytes 393224 | tf_op jit(solution)/shard_map/ppermute | solution.py:473
  4.9 5.1 %collective-permute-start.1 = (bf16[4,16,4,256]{3,2,1,0:T(4,128)(2,1)S(1)}, bf16[4,16,4,256]{3,2,1,0:T(4,128)(2,1)S(1)}, u32[]{:S(2)}, u32[]{:S(2)}) collective-permute-start(bf16[4,16,4,256]{3,2,1,0:T(4,128)(2,1)S(1)} %get-tuple-element.81), channel_id=1, source_target_pairs={{0,1},{1,0},{3,2},{2,3},{6,7},{7,6},{5,4},{4,5},{8,9},{9,8},{11,10... | collective-permute-start | bytes 393224 | tf_op jit(solution)/shard_map/ppermute | solution.py:473
  4.9 1.2 %copy-start.2 = (bf16[4,16,32,256]{3,2,1,0:T(8,128)(2,1)S(1)}, bf16[4,16,32,256]{3,2,1,0:T(8,128)(2,1)}, u32[]{:S(2)}) copy-start(bf16[4,16,32,256]{3,2,1,0:T(8,128)(2,1)} %refs_0_.1) | copy-start | bytes 3145732
  6.8 4.9 %copy-start = (bf16[2,3,3,256,256]{4,3,2,1,0:T(8,128)(2,1)S(1)}, bf16[2,3,3,256,256]{4,3,2,1,0:T(8,128)(2,1)}, u32[]{:S(2)}) copy-start(bf16[2,3,3,256,256]{4,3,2,1,0:T(8,128)(2,1)} %refs_7_.1) | copy-start | bytes 7077892
  7.4 6.9 %collective-permute-start = (bf16[128,256]{1,0:T(8,128)(2,1)S(1)}, bf16[128,256]{1,0:T(8,128)(2,1)S(1)}, u32[]{:S(2)}, u32[]{:S(2)}) collective-permute-start(bf16[128,256]{1,0:T(8,128)(2,1)S(1)} %shard_map.69), channel_id=1, source_target_pairs={{0,8},{1,9},{3,11},{2,10},{6,14},{7,15},{5,13},{4,12},{8,0},{9,1},... | collective-permute-start | bytes 196616 | tf_op jit(solution)/shard_map/ppermute | solution.py:473
  10.7 4.7 %collective-permute-start.3 = (bf16[32,256]{1,0:T(8,128)(2,1)S(1)}, bf16[32,256]{1,0:T(8,128)(2,1)S(1)}, u32[]{:S(2)}, u32[]{:S(2)}) collective-permute-start(bf16[32,256]{1,0:T(8,128)(2,1)S(1)} %shard_map.70.refs_5_), channel_id=1, source_target_pairs={{0,8},{1,9},{3,11},{2,10},{6,14},{7,15},{5,13},{4,12},{8,0},{9,1},... | collective-permute-start | bytes 49160 | tf_op jit(solution)/shard_map/ppermute | solution.py:473
  15.4 5.2 %copy-start.4 = (bf16[4,2,8,16,256]{4,3,2,1,0:T(8,128)(2,1)S(1)}, bf16[4,2,8,16,256]{4,3,2,1,0:T(8,128)(2,1)}, u32[]{:S(2)}) copy-start(bf16[4,2,8,16,256]{4,3,2,1,0:T(8,128)(2,1)} %refs_2_.1) | copy-start | bytes 1572868
  17.1 6.2 %collective-permute-start.4 = (bf16[2,2,64,256]{3,2,1,0:T(8,128)(2,1)S(1)}, bf16[2,2,64,256]{3,2,1,0:T(8,128)(2,1)S(1)}, u32[]{:S(2)}, u32[]{:S(2)}) collective-permute-start(bf16[2,2,64,256]{3,2,1,0:T(8,128)(2,1)S(1)} %get-tuple-element.46), channel_id=1, source_target_pairs={{0,2},{1,3},{2,0},{3,1},{4,6},{5,7},{6,4},{7,5},{8,10},{9,11},{10,... | collective-permute-start | bytes 393224 | tf_op jit(solution)/shard_map/ppermute | solution.py:399
  18.7 5.6 %collective-permute-start.5 = (bf16[2,2,64,256]{3,2,1,0:T(8,128)(2,1)S(1)}, bf16[2,2,64,256]{3,2,1,0:T(8,128)(2,1)S(1)}, u32[]{:S(2)}, u32[]{:S(2)}) collective-permute-start(bf16[2,2,64,256]{3,2,1,0:T(8,128)(2,1)S(1)} %get-tuple-element.47), channel_id=1, source_target_pairs={{0,4},{1,5},{2,6},{3,7},{4,0},{5,1},{6,2},{7,3},{8,12},{9,13},{10,... | collective-permute-start | bytes 393224 | tf_op jit(solution)/shard_map/ppermute | solution.py:399
  19.1 6.7 %collective-permute-start.6 = (bf16[2,2,64,256]{3,2,1,0:T(8,128)(2,1)S(1)}, bf16[2,2,64,256]{3,2,1,0:T(8,128)(2,1)S(1)}, u32[]{:S(2)}, u32[]{:S(2)}) collective-permute-start(bf16[2,2,64,256]{3,2,1,0:T(8,128)(2,1)S(1)} %get-tuple-element.48), channel_id=1, source_target_pairs={{0,6},{1,7},{2,4},{3,5},{4,2},{5,3},{6,0},{7,1},{8,14},{9,15},{10,... | collective-permute-start | bytes 393224 | tf_op jit(solution)/shard_map/ppermute | solution.py:399
  22.7 5.5 %copy-start.1 = (bf16[4,2,128,1024]{3,2,1,0:T(8,128)(2,1)S(1)}, bf16[4,2,128,1024]{3,2,1,0:T(8,128)(2,1)}, u32[]{:S(2)}) copy-start(bf16[4,2,128,1024]{3,2,1,0:T(8,128)(2,1)} %refs_6_.1) | copy-start | bytes 6291460
  22.7 3.2 %collective-permute-start.8 = (bf16[2,208,256]{2,1,0:T(8,128)(2,1)S(1)}, bf16[2,208,256]{2,1,0:T(8,128)(2,1)S(1)}, u32[]{:S(2)}, u32[]{:S(2)}) collective-permute-start(bf16[2,208,256]{2,1,0:T(8,128)(2,1)S(1)} %get-tuple-element.52), channel_id=1, source_target_pairs={{0,1},{1,0},{2,3},{3,2},{4,5},{5,4},{6,7},{7,6},{8,9},{9,8},{10,11... | collective-permute-start | bytes 638984 | tf_op jit(solution)/shard_map/ppermute | solution.py:399
  22.8 3.1 %collective-permute-start.9 = (bf16[2,208,256]{2,1,0:T(8,128)(2,1)S(1)}, bf16[2,208,256]{2,1,0:T(8,128)(2,1)S(1)}, u32[]{:S(2)}, u32[]{:S(2)}) collective-permute-start(bf16[2,208,256]{2,1,0:T(8,128)(2,1)S(1)} %get-tuple-element.53), channel_id=1, source_target_pairs={{0,1},{1,0},{2,3},{3,2},{4,5},{5,4},{6,7},{7,6},{8,9},{9,8},{10,11... | collective-permute-start | bytes 638984 | tf_op jit(solution)/shard_map/ppermute | solution.py:399
  23.3 2.6 %collective-permute-start.10 = (bf16[2,208,256]{2,1,0:T(8,128)(2,1)S(1)}, bf16[2,208,256]{2,1,0:T(8,128)(2,1)S(1)}, u32[]{:S(2)}, u32[]{:S(2)}) collective-permute-start(bf16[2,208,256]{2,1,0:T(8,128)(2,1)S(1)} %get-tuple-element.54), channel_id=1, source_target_pairs={{0,1},{1,0},{2,3},{3,2},{4,5},{5,4},{6,7},{7,6},{8,9},{9,8},{10,11... | collective-permute-start | bytes 638984 | tf_op jit(solution)/shard_map/ppermute | solution.py:399
  24.3 1.6 %collective-permute-start.11 = (bf16[2,208,256]{2,1,0:T(8,128)(2,1)S(1)}, bf16[2,208,256]{2,1,0:T(8,128)(2,1)S(1)}, u32[]{:S(2)}, u32[]{:S(2)}) collective-permute-start(bf16[2,208,256]{2,1,0:T(8,128)(2,1)S(1)} %get-tuple-element.55), channel_id=1, source_target_pairs={{0,1},{1,0},{2,3},{3,2},{4,5},{5,4},{6,7},{7,6},{8,9},{9,8},{10,11... | collective-permute-start | bytes 638984 | tf_op jit(solution)/shard_map/ppermute | solution.py:399
  25.8 2.4 %collective-permute-start.7 = (bf16[4,2,64,256]{3,2,1,0:T(8,128)(2,1)S(1)}, bf16[4,2,64,256]{3,2,1,0:T(8,128)(2,1)S(1)}, u32[]{:S(2)}, u32[]{:S(2)}) collective-permute-start(bf16[4,2,64,256]{3,2,1,0:T(8,128)(2,1)S(1)} %shard_map.73), channel_id=1, source_target_pairs={{0,1},{1,0},{2,3},{3,2},{4,5},{5,4},{6,7},{7,6},{8,9},{9,8},{10,11... | collective-permute-start | bytes 786440 | tf_op jit(solution)/shard_map/ppermute | solution.py:399
  26.7 12.7 %collective-permute-start.19 = (bf16[8,208,128]{2,1,0:T(8,128)(2,1)S(1)}, bf16[8,208,128]{2,1,0:T(8,128)(2,1)S(1)}, u32[]{:S(2)}, u32[]{:S(2)}) collective-permute-start(bf16[8,208,128]{2,1,0:T(8,128)(2,1)S(1)} %get-tuple-element.67), channel_id=1, source_target_pairs={{0,16},{16,0},{1,17},{17,1},{2,18},{18,2},{3,19},{19,3},{4,20},{20... | collective-permute-start | bytes 1277960 | tf_op jit(solution)/shard_map/ppermute | solution.py:401
  29.7 1.5 %collective-permute-start.12 = (bf16[2,208,256]{2,1,0:T(8,128)(2,1)S(1)}, bf16[2,208,256]{2,1,0:T(8,128)(2,1)S(1)}, u32[]{:S(2)}, u32[]{:S(2)}) collective-permute-start(bf16[2,208,256]{2,1,0:T(8,128)(2,1)S(1)} %get-tuple-element.59), channel_id=1, source_target_pairs={{0,1},{1,0},{2,3},{3,2},{4,5},{5,4},{6,7},{7,6},{8,9},{9,8},{10,11... | collective-permute-start | bytes 638984 | tf_op jit(solution)/shard_map/ppermute | solution.py:399
  30.0 1.6 %collective-permute-start.13 = (bf16[2,208,256]{2,1,0:T(8,128)(2,1)S(1)}, bf16[2,208,256]{2,1,0:T(8,128)(2,1)S(1)}, u32[]{:S(2)}, u32[]{:S(2)}) collective-permute-start(bf16[2,208,256]{2,1,0:T(8,128)(2,1)S(1)} %get-tuple-element.60), channel_id=1, source_target_pairs={{0,1},{1,0},{2,3},{3,2},{4,5},{5,4},{6,7},{7,6},{8,9},{9,8},{10,11... | collective-permute-start | bytes 638984 | tf_op jit(solution)/shard_map/ppermute | solution.py:399
  30.3 1.6 %collective-permute-start.14 = (bf16[2,208,256]{2,1,0:T(8,128)(2,1)S(1)}, bf16[2,208,256]{2,1,0:T(8,128)(2,1)S(1)}, u32[]{:S(2)}, u32[]{:S(2)}) collective-permute-start(bf16[2,208,256]{2,1,0:T(8,128)(2,1)S(1)} %get-tuple-element.61), channel_id=1, source_target_pairs={{0,1},{1,0},{2,3},{3,2},{4,5},{5,4},{6,7},{7,6},{8,9},{9,8},{10,11... | collective-permute-start | bytes 638984 | tf_op jit(solution)/shard_map/ppermute | solution.py:399
  30.5 1.7 %collective-permute-start.15 = (bf16[2,208,256]{2,1,0:T(8,128)(2,1)S(1)}, bf16[2,208,256]{2,1,0:T(8,128)(2,1)S(1)}, u32[]{:S(2)}, u32[]{:S(2)}) collective-permute-start(bf16[2,208,256]{2,1,0:T(8,128)(2,1)S(1)} %get-tuple-element.62), channel_id=1, source_target_pairs={{0,1},{1,0},{2,3},{3,2},{4,5},{5,4},{6,7},{7,6},{8,9},{9,8},{10,11... | collective-permute-start | bytes 638984 | tf_op jit(solution)/shard_map/ppermute | solution.py:399
  32.9 11.9 %collective-permute-start.16 = (bf16[4,208,128]{2,1,0:T(8,128)(2,1)S(1)}, bf16[4,208,128]{2,1,0:T(8,128)(2,1)S(1)}, u32[]{:S(2)}, u32[]{:S(2)}) collective-permute-start(bf16[4,208,128]{2,1,0:T(8,128)(2,1)S(1)} %get-tuple-element.64), channel_id=1, source_target_pairs={{0,18},{1,19},{2,16},{3,17},{4,22},{5,23},{6,20},{7,21},{8,26},{9,... | collective-permute-start | bytes 638984 | tf_op jit(solution)/shard_map/ppermute | solution.py:403
  34.5 13.6 %collective-permute-start.17 = (bf16[4,208,128]{2,1,0:T(8,128)(2,1)S(1)}, bf16[4,208,128]{2,1,0:T(8,128)(2,1)S(1)}, u32[]{:S(2)}, u32[]{:S(2)}) collective-permute-start(bf16[4,208,128]{2,1,0:T(8,128)(2,1)S(1)} %get-tuple-element.65), channel_id=1, source_target_pairs={{0,16},{16,0},{1,17},{17,1},{2,18},{18,2},{3,19},{19,3},{4,20},{20... | collective-permute-start | bytes 638984 | tf_op jit(solution)/shard_map/ppermute | solution.py:401
  35.8 12.3 %collective-permute-start.18 = (bf16[4,208,128]{2,1,0:T(8,128)(2,1)S(1)}, bf16[4,208,128]{2,1,0:T(8,128)(2,1)S(1)}, u32[]{:S(2)}, u32[]{:S(2)}) collective-permute-start(bf16[4,208,128]{2,1,0:T(8,128)(2,1)S(1)} %get-tuple-element.66), channel_id=1, source_target_pairs={{0,2},{1,3},{2,0},{3,1},{4,6},{5,7},{6,4},{7,5},{8,10},{9,11},{10,... | collective-permute-start | bytes 638984 | tf_op jit(solution)/shard_map/ppermute | solution.py:399
  39.4 23.6 %copy-start.3 = (bf16[2,1024,256]{2,1,0:T(8,128)(2,1)S(1)}, bf16[2,1024,256]{2,1,0:T(8,128)(2,1)}, u32[]{:S(2)}) copy-start(bf16[2,1024,256]{2,1,0:T(8,128)(2,1)} %refs_1_.1) | copy-start | bytes 3145732
  40.0 8.1 %collective-permute-start.20 = (bf16[4,208,128]{2,1,0:T(8,128)(2,1)S(1)}, bf16[4,208,128]{2,1,0:T(8,128)(2,1)S(1)}, u32[]{:S(2)}, u32[]{:S(2)}) collective-permute-start(bf16[4,208,128]{2,1,0:T(8,128)(2,1)S(1)} %get-tuple-element.69), channel_id=1, source_target_pairs={{0,4},{1,5},{2,6},{3,7},{4,0},{5,1},{6,2},{7,3},{8,12},{9,13},{10,... | collective-permute-start | bytes 638984 | tf_op jit(solution)/shard_map/ppermute | solution.py:399
  48.8 5.9 %collective-permute-start.21 = (bf16[2,208,128]{2,1,0:T(8,128)(2,1)S(1)}, bf16[2,208,128]{2,1,0:T(8,128)(2,1)S(1)}, u32[]{:S(2)}, u32[]{:S(2)}) collective-permute-start(bf16[2,208,128]{2,1,0:T(8,128)(2,1)S(1)} %get-tuple-element.71), channel_id=1, source_target_pairs={{0,2},{1,3},{2,0},{3,1},{4,6},{5,7},{6,4},{7,5},{8,10},{9,11},{10,... | collective-permute-start | bytes 319496 | tf_op jit(solution)/shard_map/ppermute | solution.py:399
  50.3 5.7 %collective-permute-start.23 = (bf16[1,208,128]{2,1,0:T(8,128)(2,1)S(1)}, bf16[1,208,128]{2,1,0:T(8,128)(2,1)S(1)}, u32[]{:S(2)}, u32[]{:S(2)}) collective-permute-start(bf16[1,208,128]{2,1,0:T(8,128)(2,1)S(1)} %get-tuple-element.75), channel_id=1, source_target_pairs={{0,4},{1,5},{2,6},{3,7},{4,0},{5,1},{6,2},{7,3},{8,12},{9,13},{10,... | collective-permute-start | bytes 159752 | tf_op jit(solution)/shard_map/ppermute | solution.py:399
  50.7 5.4 %collective-permute-start.24 = (bf16[1,208,128]{2,1,0:T(8,128)(2,1)S(1)}, bf16[1,208,128]{2,1,0:T(8,128)(2,1)S(1)}, u32[]{:S(2)}, u32[]{:S(2)}) collective-permute-start(bf16[1,208,128]{2,1,0:T(8,128)(2,1)S(1)} %get-tuple-element.76), channel_id=1, source_target_pairs={{0,8},{1,9},{2,10},{3,11},{4,12},{5,13},{6,14},{7,15},{8,0},{9,1},... | collective-permute-start | bytes 159752 | tf_op jit(solution)/shard_map/ppermute | solution.py:399
  53.3 6.0 %collective-permute-start.25 = (bf16[1,208,128]{2,1,0:T(8,128)(2,1)S(1)}, bf16[1,208,128]{2,1,0:T(8,128)(2,1)S(1)}, u32[]{:S(2)}, u32[]{:S(2)}) collective-permute-start(bf16[1,208,128]{2,1,0:T(8,128)(2,1)S(1)} %get-tuple-element.77), channel_id=1, source_target_pairs={{0,12},{1,13},{2,14},{3,15},{4,8},{5,9},{6,10},{7,11},{8,4},{9,5},... | collective-permute-start | bytes 159752 | tf_op jit(solution)/shard_map/ppermute | solution.py:399
  55.2 5.5 %collective-permute-start.22 = (bf16[1,208,128]{2,1,0:T(8,128)(2,1)S(1)}, bf16[1,208,128]{2,1,0:T(8,128)(2,1)S(1)}, u32[]{:S(2)}, u32[]{:S(2)}) collective-permute-start(bf16[1,208,128]{2,1,0:T(8,128)(2,1)S(1)} %get-tuple-element.74), channel_id=1, source_target_pairs={{0,8},{1,9},{2,10},{3,11},{4,12},{5,13},{6,14},{7,15},{8,0},{9,1},... | collective-permute-start | bytes 159752 | tf_op jit(solution)/shard_map/ppermute | solution.py:399
  61.4 4.2 %collective-permute-start.26 = (bf16[208,128]{1,0:T(8,128)(2,1)S(1)}, bf16[208,128]{1,0:T(8,128)(2,1)S(1)}, u32[]{:S(2)}, u32[]{:S(2)}) collective-permute-start(bf16[208,128]{1,0:T(8,128)(2,1)S(1)} %get-tuple-element.79), channel_id=1, source_target_pairs={{0,16},{16,0},{1,17},{17,1},{2,18},{18,2},{3,19},{19,3},{4,20},{20... | collective-permute-start | bytes 159752 | tf_op jit(solution)/shard_map/ppermute | solution.py:401
